TPU v7x, 32 devices: a whole 2x2x4 slice. The times are simulated.
32 devices in a mesh: region: 16 (over z, y, x), split: 2 (over core).
Axes of the slice: x: 2, y: 2, z: 4, core: 2. Of those that a mesh axis runs over, the one named last changes fastest.
Arguments:
- vectors: float32 [18432, 256], P(('region', 'split'))
- hessian: bfloat16 [96, 12, 192, 192], P(('region', 'split')), may hold values from -0.125 to 0.125
- block_cols: int32 [96, 12], P(('region', 'split')), may hold values from 0 to 17, as said below
- live_blocks: int32 [96], P(('region', 'split')), may hold values from 6 to 12, as said below
- halo_lists: int32 [16, 2, 6], P('region'), may hold values from 0 to 5, as said below
- bounds: float32 [2], replicated, as said below
Outputs:
- basis: float32 [18432, 256], P(('region', 'split'))
- projected: float32 [256, 256], replicated
Inputs may be any that keep to these rules, and one draw needn't show every extreme that they name: `block_cols`: in each row the entries are distinct and entry 0 is the row's own block within its region; values below 6 name blocks of the row's region, 6 + j the j-th block received from the lower region, 12 + j the j-th from the upper region. `live_blocks`: the first block row of every region has all 12 blocks intact. `halo_lists`: each list holds distinct block indices within the region. bounds[0] < 0 < bounds[1].
All inputs are finite; a program needn't handle non-finite values.
Results may differ from a plain program's by a relative error of at most 0.0005.
The roundings to bfloat16 on the way count: a program that leaves them out, or rounds other values in their place, can miss the bound.
Values may be sent and summed in bfloat16 or wider, within the bound.
No kernel may reach another device: no remote copies, remote signals or barrier semaphores. Data moves between devices by JAX's collectives and lax.ppermute only.
A program may use at most 64 MiB of HBM per device.

v0:
```python
import jax
import jax.numpy as jnp
from jax import lax
from jax.sharding import PartitionSpec as P


def shifted(value, axis, steps):
    count = lax.axis_size(axis)
    pairs = [(source, (source + steps) % count) for source in range(count)]
    return lax.ppermute(value, axis, pairs)


def apply_blocks(operand, hessian, block_cols, live_blocks, halo_lists):
    row_blocks = hessian.shape[0]
    block_size = hessian.shape[2]
    mode_count = operand.shape[1]
    shard_blocks = operand.reshape(row_blocks, block_size, mode_count)
    region = lax.all_gather(shard_blocks, "split", axis=0, tiled=True)
    send_lower = region[halo_lists[0, 0]]
    send_upper = region[halo_lists[0, 1]]
    share_width = mode_count // lax.axis_size("split")
    share_start = lax.axis_index("split") * share_width
    lower_share = lax.dynamic_slice_in_dim(send_lower, share_start, share_width, 2)
    upper_share = lax.dynamic_slice_in_dim(send_upper, share_start, share_width, 2)
    got_lower = shifted(upper_share, "region", 1)
    got_upper = shifted(lower_share, "region", -1)
    from_lower, from_upper = (
        lax.all_gather(got_lower, "split", axis=2, tiled=True),
        lax.all_gather(got_upper, "split", axis=2, tiled=True),
    )
    candidates = jnp.concatenate([region, from_lower, from_upper], 0)
    picked = candidates[block_cols]
    used_mask = lax.broadcasted_iota(jnp.int32, block_cols.shape, 1) < live_blocks[:, None]
    picked = jnp.where(used_mask[:, :, None, None], picked, jnp.zeros((), jnp.bfloat16))
    product = jnp.einsum("rkij,rkjm->rim", hessian, picked, preferred_element_type=jnp.float32)
    return product.reshape(row_blocks * block_size, mode_count)


def local(vectors, hessian, block_cols, live_blocks, halo_lists, bounds):
    centre = 0.5 * (bounds[0] + bounds[1])
    half_width = 0.5 * (bounds[1] - bounds[0])
    first = apply_blocks(vectors.astype(jnp.bfloat16), hessian, block_cols, live_blocks, halo_lists)
    filtered_one = (first - centre * vectors) / half_width
    second = apply_blocks(
        filtered_one.astype(jnp.bfloat16), hessian, block_cols, live_blocks, halo_lists
    )
    filtered_two = 2.0 * (second - centre * filtered_one) / half_width - vectors
    image = apply_blocks(
        filtered_two.astype(jnp.bfloat16), hessian, block_cols, live_blocks, halo_lists
    )
    total_rows = vectors.shape[0] * lax.axis_size("region") * lax.axis_size("split")
    contract = (((0,), (0,)), ((), ()))
    gram_part = lax.dot_general(
        filtered_two, filtered_two, contract, precision=lax.Precision.HIGHEST
    )
    cross_part = lax.dot_general(filtered_two, image, contract, precision=lax.Precision.HIGHEST)
    gram, cross = lax.psum((gram_part, cross_part), ("region", "split"))
    gram = gram / total_rows
    cross = cross / total_rows
    lower = jnp.linalg.cholesky(gram)
    basis = jax.scipy.linalg.solve_triangular(lower, filtered_two.T, lower=True).T
    partial_left = jax.scipy.linalg.solve_triangular(lower, cross, lower=True)
    projected = jax.scipy.linalg.solve_triangular(lower, partial_left.T, lower=True).T
    return (basis, projected)


def solution(mesh):
    placed = (
        P(("region", "split"), None),
        P(("region", "split"), None, None, None),
        P(("region", "split"), None),
        P(("region", "split")),
        P("region", None, None),
        P(),
    )
    return jax.shard_map(
        local,
        mesh=mesh,
        in_specs=placed,
        out_specs=(P(("region", "split"), None), P()),
        check_vma=False,
    )
```

profile of v0, /device:TPU:1, one launch (start us, length us, event | category | flops | bytes accessed | tf_op | source)
XLA Modules:
  0.0 357.3 jit_solution(2259500133869670541)
XLA Ops:
  12.7 2.5 gather_fusion
  19.2 2.5 gather_fusion.1
  23.4 4.0 %collective-permute-start.1 = (bf16[6,192,128]{2,1,0:T(8,128)(2,1)}, bf16[6,192,128]{2,1,0:T(8,128)(2,1)}, u32[]{:S(2)}, u32[]{:S(2)}) collective-permute-start(bf16[6,192,128]{2,1,0:T(8,128)(2,1)} %constant_dynamic-slice_fusion.5), channel_id=1, source_target_pairs={{0,30},{2,0},{4,2},{6,4},{8,6},{10,8},{12,10},{14,12},{16,14},{18,... | collective-permute-start | bytes 884744 | tf_op jit(solution)/shard_map/ppermute | solution.py:10
  32.7 2.7 all_gather.28
  37.8 2.5 pad_maximum_fusion
  40.3 4.3 %gather_fusion.2 = bf16[36,192,256]{2,1,0:T(8,128)(2,1)} fusion(bf16[18,192,256]{2,1,0:T(8,128)(2,1)} %pad_maximum_fusion, s32[1024]{0:T(1024)S(1)} %pad_clamp_fusion), kind=kCustom, calls=%fused_computation.2 | custom fusion | bytes 7078032 | tf_op jit(solution)/shard_map/gather | solution.py:32
  44.6 3.0 fusion.4
  50.8 2.5 gather_fusion.3
  55.4 2.5 gather_fusion.4
  58.9 4.7 %collective-permute-start.3 = (bf16[6,192,128]{2,1,0:T(8,128)(2,1)S(1)}, bf16[6,192,128]{2,1,0:T(8,128)(2,1)S(1)}, u32[]{:S(2)}, u32[]{:S(2)}) collective-permute-start(bf16[6,192,128]{2,1,0:T(8,128)(2,1)S(1)} %constant_dynamic-slice_fusion.3), channel_id=1, source_target_pairs={{0,30},{2,0},{4,2},{6,4},{8,6},{10,8},{12,10},{14,12},{16,14},{18,... | collective-permute-start | bytes 884744 | tf_op jit(solution)/shard_map/ppermute | solution.py:10
  63.5 3.6 collective-permute-done.2
  67.1 3.4 all_gather.31
  71.7 3.0 all_gather.32
  77.3 4.3 %gather_fusion.5 = bf16[36,192,256]{2,1,0:T(8,128)(2,1)} fusion(bf16[18,192,256]{2,1,0:T(8,128)(2,1)} %pad_maximum_fusion.1, s32[1024]{0:T(1024)S(1)} %pad_clamp_fusion), kind=kCustom, calls=%fused_computation.5 | custom fusion | bytes 7078032 | tf_op jit(solution)/shard_map/gather | solution.py:32
  81.5 3.1 fusion.2
  88.0 2.5 gather_fusion.6
  90.5 2.5 gather_fusion.7
  95.1 5.1 %collective-permute-start.5 = (bf16[6,192,128]{2,1,0:T(8,128)(2,1)S(1)}, bf16[6,192,128]{2,1,0:T(8,128)(2,1)S(1)}, u32[]{:S(2)}, u32[]{:S(2)}) collective-permute-start(bf16[6,192,128]{2,1,0:T(8,128)(2,1)S(1)} %constant_dynamic-slice_fusion.1), channel_id=1, source_target_pairs={{0,30},{2,0},{4,2},{6,4},{8,6},{10,8},{12,10},{14,12},{16,14},{18,... | collective-permute-start | bytes 884744 | tf_op jit(solution)/shard_map/ppermute | solution.py:10
  100.2 3.3 fusion.42
  103.4 3.0 collective-permute-done.4
  106.4 3.0 all_gather.34
  110.2 3.2 all_gather.35
  114.8 4.3 %gather_fusion.8 = bf16[36,192,256]{2,1,0:T(8,128)(2,1)} fusion(bf16[18,192,256]{2,1,0:T(8,128)(2,1)} %pad_maximum_fusion.2, s32[1024]{0:T(1024)S(1)} %pad_clamp_fusion), kind=kCustom, calls=%fused_computation.8 | custom fusion | bytes 7078032 | tf_op jit(solution)/shard_map/gather | solution.py:32
  119.1 3.0 fusion
  124.2 126.8 %all-reduce.4.cloned.1.call-done = (f32[256,256]{0,1:T(8,128)}, f32[256,256]{0,1:T(8,128)}) async-done(((f32[256,256]{0,1:T(8,128)}, f32[256,256]{0,1:T(8,128)}), (f32[256,256]{0,1:T(8,128)}, f32[256,256]{0,1:T(8,128)})) %all-reduce.4.cloned.1.call-update) | async-done | bytes 524304 | tf_op jit(solution)/shard_map/psum | solution.py:57
  256.8 13.2 %cholesky.50 = f32[128,128]{1,0:T(8,128)} custom-call(f32[128,128]{1,0:T(8,128)} %cholesky.118), custom_call_target="Cholesky" | custom-call | tf_op jit(solution)/shard_map/jit(cholesky)/cholesky | solution.py:60
  273.0 11.3 %custom-call.18 = f32[1,128,128]{1,2,0:T(8,128)} custom-call(f32[1,128,128]{2,1,0:T(8,128)} %get-tuple-element.48), custom_call_target="InvertDiagBlocksLowerTriangular" | custom-call | tf_op jit(solution)/shard_map/jit(cholesky)/cholesky | solution.py:60
  287.7 13.4 %cholesky.105 = f32[128,128]{1,0:T(8,128)} custom-call(f32[128,128]{1,0:T(8,128)} %convolution_subtract_fusion.3), custom_call_target="Cholesky" | custom-call | tf_op jit(solution)/shard_map/jit(cholesky)/cholesky | solution.py:60
  306.9 6.9 %while.5 = (s32[]{:T(128)}, f32[256,256]{1,0:T(8,128)}, s32[2,2]{1,0:T(2,128)S(1)}, f32[2,128,128]{2,1,0:T(8,128)}, s32[]{:T(128)}) while((s32[]{:T(128)}, f32[256,256]{1,0:T(8,128)}, s32[2,2]{1,0:T(2,128)S(1)}, f32[2,128,128]{2,1,0:T(8,128)}, s32[]{:T(128)}) %tuple.40), condition=%wide.while_cond.1, body=%wide.while_body.1.sunk | while | flops 2 | bytes 132705 | solution.py:61
  307.5 2.9 bitcast_dynamic-update-slice_fusion.2
  311.0 2.8 bitcast_dynamic-update-slice_fusion.2
  313.9 21.1 %custom-call.19 = f32[2,128,128]{1,2,0:T(8,128)} custom-call(f32[2,128,128]{2,1,0:T(8,128)} %get-tuple-element.18), custom_call_target="InvertDiagBlocksLowerTriangular" | custom-call | tf_op jit(solution)/shard_map/jit(_solve_triangular)/triangular_solve | solution.py:61
  (85 shorter events, 69.5 us)
Async XLA Ops:
  7.2 37.4 %copy-start = (bf16[3,12,192,192]{3,2,1,0:T(8,128)(2,1)S(1)}, bf16[3,12,192,192]{3,2,1,0:T(8,128)(2,1)}, u32[]{:S(2)}) copy-start(bf16[3,12,192,192]{3,2,1,0:T(8,128)(2,1)} %param.9) | copy-start | bytes 7962628
  7.2 20.2 %copy-start.8 = (s32[3,12]{1,0:T(4,128)S(1)}, s32[3,12]{1,0:T(4,128)}, u32[]{:S(2)}) copy-start(s32[3,12]{1,0:T(4,128)} %param.10) | copy-start | bytes 436
  7.2 243.8 %all-reduce.4.cloned.1.call-start = ((), (), s32[]{:S(2)}) async-start(), calls=%async_computation | async-start | bytes 1048576 | tf_op jit(solution)/shard_map/psum | solution.py:57
  16.9 15.8 %collective-permute-start = (bf16[6,192,128]{2,1,0:T(8,128)(2,1)}, bf16[6,192,128]{2,1,0:T(8,128)(2,1)}, u32[]{:S(2)}, u32[]{:S(2)}) collective-permute-start(bf16[6,192,128]{2,1,0:T(8,128)(2,1)} %constant_dynamic-slice_fusion.6), channel_id=1, source_target_pairs={{0,2},{2,4},{4,6},{6,8},{8,10},{10,12},{12,14},{14,16},{16,18},{18... | collective-permute-start | bytes 884744 | tf_op jit(solution)/shard_map/ppermute | solution.py:10
  23.4 12.0 %collective-permute-start.1 = (bf16[6,192,128]{2,1,0:T(8,128)(2,1)}, bf16[6,192,128]{2,1,0:T(8,128)(2,1)}, u32[]{:S(2)}, u32[]{:S(2)}) collective-permute-start(bf16[6,192,128]{2,1,0:T(8,128)(2,1)} %constant_dynamic-slice_fusion.5), channel_id=1, source_target_pairs={{0,30},{2,0},{4,2},{6,4},{8,6},{10,8},{12,10},{14,12},{16,14},{18,... | collective-permute-start | bytes 884744 | tf_op jit(solution)/shard_map/ppermute | solution.py:10
  40.3 4.3 %copy-start.9 = (pred[3,12]{1,0:T(4,128)(4,1)S(1)}, pred[3,12]{1,0:T(4,128)(4,1)}, u32[]{:S(2)}) copy-start(pred[3,12]{1,0:T(4,128)(4,1)} %iota_compare_fusion.3) | copy-start | bytes 112
  44.6 3.1 copy-start.3
  47.6 0.8 copy-start.5
  55.0 12.1 %collective-permute-start.2 = (bf16[6,192,128]{2,1,0:T(8,128)(2,1)}, bf16[6,192,128]{2,1,0:T(8,128)(2,1)}, u32[]{:S(2)}, u32[]{:S(2)}) collective-permute-start(bf16[6,192,128]{2,1,0:T(8,128)(2,1)} %constant_dynamic-slice_fusion.4), channel_id=1, source_target_pairs={{0,2},{2,4},{4,6},{6,8},{8,10},{10,12},{12,14},{14,16},{16,18},{18... | collective-permute-start | bytes 884744 | tf_op jit(solution)/shard_map/ppermute | solution.py:10
  58.9 12.9 %collective-permute-start.3 = (bf16[6,192,128]{2,1,0:T(8,128)(2,1)S(1)}, bf16[6,192,128]{2,1,0:T(8,128)(2,1)S(1)}, u32[]{:S(2)}, u32[]{:S(2)}) collective-permute-start(bf16[6,192,128]{2,1,0:T(8,128)(2,1)S(1)} %constant_dynamic-slice_fusion.3), channel_id=1, source_target_pairs={{0,30},{2,0},{4,2},{6,4},{8,6},{10,8},{12,10},{14,12},{16,14},{18,... | collective-permute-start | bytes 884744 | tf_op jit(solution)/shard_map/ppermute | solution.py:10
  81.5 3.1 copy-start.4
  81.5 3.1 copy-start.6
  93.0 20.4 %copy-start.2 = (bf16[6,192,256]{2,1,0:T(8,128)(2,1)S(1)}, bf16[6,192,256]{2,1,0:T(8,128)(2,1)}, u32[]{:S(2)}) copy-start(bf16[6,192,256]{2,1,0:T(8,128)(2,1)} %all_gather.33) | copy-start | bytes 1769476
  94.0 12.4 %collective-permute-start.4 = (bf16[6,192,128]{2,1,0:T(8,128)(2,1)S(1)}, bf16[6,192,128]{2,1,0:T(8,128)(2,1)S(1)}, u32[]{:S(2)}, u32[]{:S(2)}) collective-permute-start(bf16[6,192,128]{2,1,0:T(8,128)(2,1)S(1)} %constant_dynamic-slice_fusion.2), channel_id=1, source_target_pairs={{0,2},{2,4},{4,6},{6,8},{8,10},{10,12},{12,14},{14,16},{16,18},{18... | collective-permute-start | bytes 884744 | tf_op jit(solution)/shard_map/ppermute | solution.py:10
  95.1 15.1 %collective-permute-start.5 = (bf16[6,192,128]{2,1,0:T(8,128)(2,1)S(1)}, bf16[6,192,128]{2,1,0:T(8,128)(2,1)S(1)}, u32[]{:S(2)}, u32[]{:S(2)}) collective-permute-start(bf16[6,192,128]{2,1,0:T(8,128)(2,1)S(1)} %constant_dynamic-slice_fusion.1), channel_id=1, source_target_pairs={{0,30},{2,0},{4,2},{6,4},{8,6},{10,8},{12,10},{14,12},{16,14},{18,... | collective-permute-start | bytes 884744 | tf_op jit(solution)/shard_map/ppermute | solution.py:10
  119.1 3.0 copy-start.1
  255.5 0.7 copy-start.7
Sparse Core Ops, SparseCore 0:
  124.3 126.6 all-reduce.3
where the time goes:
time: 361 us; the launch traced here: 357 us
  waiting for transfers between devices  135 us (37%)
  other arithmetic  82.1 us (23%)
  local copies, waits for them, and re-layouts  51.3 us (14%)
  matrix products  28.9 us (8%)
  blocking collectives  24.9 us (7%)
  between operations  18.1 us (5%)
  starting transfers between devices  16.6 us (5%)
    psum x1, waiting for transfers between devices, local(): gram, cross = lax.psum((gram_part, cross_part), ('region', 'split'))  127 us
    another operation x7, other arithmetic, local(): lower = jnp.linalg.cholesky(gram)  42.1 us
    another operation x3, other arithmetic, local(): jax.scipy.linalg.solve_triangular(lower, filtered_two.T, lower=True)  22.8 us
    ppermute x6, starting transfers between devices, shifted(): return lax.ppermute(value, axis, pairs)  16.6 us
    gather x3, local copies, waits for them, and re-layouts, apply_blocks(): picked = candidates[block_cols]  12.8 us
    dot_general x3, matrix products, apply_blocks(): jnp.einsum('rkij,rkjm->rim', hessian, picked, preferred_element_type=jnp....  9.13 us
    all_gather x3, blocking collectives, apply_blocks(): lax.all_gather(got_lower, 'split', axis=2, tiled=True)  9.12 us
    all_gather x3, blocking collectives, apply_blocks(): lax.all_gather(got_upper, 'split', axis=2, tiled=True)  8.7 us
  transfers between devices with their start and end apart: 7, of which 5 were waited for; matrix products, arithmetic and copies ran while one was open for 4% of the time, Pallas kernels for 0%

commit v1 on v0

v1 whole, which is shorter than its diff:
```python
import functools
import jax
import jax.numpy as jnp
from jax import lax
from jax.experimental import pallas as pl
from jax.experimental.pallas import tpu as pltpu
from jax.sharding import PartitionSpec as P

AXES = ("region", "split")
VMEM = pl.BlockSpec(memory_space=pltpu.VMEM)
SMEM = pl.BlockSpec(memory_space=pltpu.SMEM)
EXACT = lax.Precision.HIGHEST
NN = (((1,), (0,)), ((), ()))
NT = (((1,), (1,)), ((), ()))
TN = (((0,), (0,)), ((), ()))
VMEM_LIMIT = 48 * 1024 * 1024
GROUP = 8
TILE = 128


def shifted(value, axis, steps):
    count = lax.axis_size(axis)
    pairs = [(source, (source + steps) % count) for source in range(count)]
    return lax.ppermute(value, axis, pairs)


def exact_dot(left, right, dims=NN):
    return lax.dot_general(left, right, dims, precision=EXACT, preferred_element_type=jnp.float32)


def kernel_call(body, out_shape, in_specs, flops, bytes_accessed):
    return pl.pallas_call(
        body,
        out_shape=out_shape,
        in_specs=in_specs,
        out_specs=jax.tree.map(lambda _: VMEM, out_shape),
        compiler_params=pltpu.CompilerParams(vmem_limit_bytes=VMEM_LIMIT),
        cost_estimate=pl.CostEstimate(flops=flops, bytes_accessed=bytes_accessed, transcendentals=0),
    )


def candidate_dot(slots_ref, hessian_ref, first_slot, index, block):
    rows, _, size, _ = hessian_ref.shape
    parts = []
    for row in range(rows):
        slot = slots_ref[row, first_slot + index]
        live = jnp.where(slot >= 0, 1.0, 0.0).astype(jnp.float32)
        stored = hessian_ref[row, jnp.maximum(slot, 0)]
        parts.append(stored * jnp.broadcast_to(live, (size, size)).astype(jnp.bfloat16))
    return jnp.dot(jnp.concatenate(parts, 0), block, preferred_element_type=jnp.float32)


def accumulate(slots_ref, hessian_ref, first_slot, operand_ref, total):
    size = hessian_ref.shape[2]
    for index in range(operand_ref.shape[0] // size):
        block = operand_ref[index * size : (index + 1) * size, :]
        term = candidate_dot(slots_ref, hessian_ref, first_slot, index, block)
        total = term if total is None else total + term
    return total


def local_body(slots_ref, hessian_ref, region_ref, out_ref):
    out_ref[...] = accumulate(slots_ref, hessian_ref, 0, region_ref, None)


def halo_total(slots_ref, hessian_ref, lower_ref, upper_ref, local_ref):
    size = hessian_ref.shape[2]
    halo = lower_ref.shape[0] // size
    own = slots_ref.shape[1] - 2 * halo
    total = accumulate(slots_ref, hessian_ref, own, lower_ref, local_ref[...])
    return accumulate(slots_ref, hessian_ref, own + halo, upper_ref, total)


def first_body(slots_ref, bounds_ref, hessian_ref, lower_ref, upper_ref, local_ref, vectors_ref, one_ref, cast_ref):
    centre = 0.5 * (bounds_ref[0] + bounds_ref[1])
    half = 0.5 * (bounds_ref[1] - bounds_ref[0])
    total = halo_total(slots_ref, hessian_ref, lower_ref, upper_ref, local_ref)
    one = (total - centre * vectors_ref[...]) / half
    one_ref[...] = one
    cast_ref[...] = one.astype(jnp.bfloat16)


def second_body(slots_ref, bounds_ref, hessian_ref, lower_ref, upper_ref, local_ref, one_ref, vectors_ref, two_ref, cast_ref):
    centre = 0.5 * (bounds_ref[0] + bounds_ref[1])
    half = 0.5 * (bounds_ref[1] - bounds_ref[0])
    total = halo_total(slots_ref, hessian_ref, lower_ref, upper_ref, local_ref)
    two = 2.0 * (total - centre * one_ref[...]) / half - vectors_ref[...]
    two_ref[...] = two
    cast_ref[...] = two.astype(jnp.bfloat16)


def third_body(slots_ref, hessian_ref, lower_ref, upper_ref, local_ref, two_ref, sums_ref):
    modes = two_ref.shape[1]
    image = halo_total(slots_ref, hessian_ref, lower_ref, upper_ref, local_ref)
    two = two_ref[...]
    sums_ref[:modes, :] = exact_dot(two, two, TN)
    sums_ref[modes:, :] = exact_dot(two, image, TN)


def over_lanes(value, lane):
    return jnp.broadcast_to(value[:, lane : lane + 1], value.shape)


def over_rows(value, row):
    return jnp.broadcast_to(value[row : row + 1, :], value.shape)


def tile_inverse(tile):
    count = tile.shape[0] // GROUP
    rows = [tile[index * GROUP : (index + 1) * GROUP, :] for index in range(count)]
    sub = lax.broadcasted_iota(jnp.int32, rows[0].shape, 0)
    lane = lax.broadcasted_iota(jnp.int32, rows[0].shape, 1)
    done = []
    for step in range(count):
        start = step * GROUP
        pivot_cols = [over_lanes(rows[step], start + col) for col in range(GROUP)]
        factors = {
            below: [over_lanes(rows[below], start + col) for col in range(GROUP)]
            for below in range(step + 1, count)
        }
        inside = (lane >= start) & (lane < start + GROUP)
        forward = jnp.where(inside, jnp.where(lane - start == sub, 1.0, 0.0), rows[step])
        solved = forward
        for pivot in range(GROUP):
            here = sub == pivot
            value = over_rows(pivot_cols[pivot], pivot)
            inverse = 1.0 / value
            ratio = pivot_cols[pivot] * inverse
            row = over_rows(forward, pivot)
            forward = jnp.where(
                here, row * lax.rsqrt(value), jnp.where(sub > pivot, forward - ratio * row, forward)
            )
            solved = jnp.where(here, row * inverse, solved - ratio * row)
            for col in range(pivot + 1, GROUP):
                top = over_rows(pivot_cols[col], pivot)
                pivot_cols[col] = jnp.where(here, top * inverse, pivot_cols[col] - ratio * top)
        done.append(jnp.where(lane < start + GROUP, forward, 0.0))
        solved_rows = [over_rows(solved, pivot) for pivot in range(GROUP)]
        for below in range(step + 1, count):
            terms = [factors[below][col] * solved_rows[col] for col in range(GROUP)]
            while len(terms) > 1:
                terms = [terms[at] + terms[at + 1] for at in range(0, len(terms), 2)]
            rows[below] = jnp.where(inside, 0.0, rows[below]) - terms[0]
    return jnp.concatenate(done, 0)


def factor_inverse(gram):
    count = gram.shape[0] // TILE

    def part(row, col):
        return gram[row * TILE : (row + 1) * TILE, col * TILE : (col + 1) * TILE]

    rest = {(row, col): part(row, col) for row in range(count) for col in range(row + 1)}
    lower = {}
    inverse = {}
    for at in range(count):
        inverse[at, at] = tile_inverse(rest[at, at])
        for row in range(at + 1, count):
            lower[row, at] = exact_dot(rest[row, at], inverse[at, at], NT)
        for row in range(at + 1, count):
            for col in range(at + 1, row + 1):
                rest[row, col] = rest[row, col] - exact_dot(lower[row, at], lower[col, at], NT)
        for col in range(at):
            mixed = exact_dot(lower[at, col], inverse[col, col])
            for mid in range(col + 1, at):
                mixed = mixed + exact_dot(lower[at, mid], inverse[mid, col])
            inverse[at, col] = -exact_dot(inverse[at, at], mixed)
    zero = jnp.zeros((TILE, TILE), jnp.float32)
    return jnp.concatenate(
        [
            jnp.concatenate([inverse[row, col] if col <= row else zero for col in range(count)], 1)
            for row in range(count)
        ],
        0,
    )


def finish_body(total_rows, sums_ref, two_ref, basis_ref, projected_ref):
    modes = two_ref.shape[1]
    inverse = factor_inverse(sums_ref[:modes, :] / total_rows)
    basis_ref[...] = exact_dot(two_ref[...], inverse, NT)
    left = exact_dot(inverse, sums_ref[modes:, :] / total_rows)
    projected_ref[...] = exact_dot(left, inverse, NT)


def summed(part):
    count = lax.axis_size(AXES)
    pieces = part.reshape(count, part.shape[0] // count, part.shape[1])
    mine = jnp.sum(lax.all_to_all(pieces, AXES, 0, 0), axis=0)
    every = jnp.broadcast_to(mine[None], pieces.shape)
    return lax.all_to_all(every, AXES, 0, 0).reshape(part.shape)


def local(vectors, hessian, block_cols, live_blocks, halo_lists, bounds):
    row_blocks, stored, size, _ = hessian.shape
    rows, modes = vectors.shape
    splits = lax.axis_size("split")
    region_blocks = row_blocks * splits
    halo_blocks = halo_lists.shape[2]
    whole = halo_blocks == region_blocks
    total_rows = rows * lax.axis_size(AXES)

    def halos(operand, region):
        if whole:
            return shifted(operand, "region", 1), shifted(operand, "region", -1), 0
        width = modes // splits
        start = lax.axis_index("split") * width
        blocks = region.reshape(region_blocks, size, modes)
        share = lambda listed: lax.dynamic_slice_in_dim(blocks[listed], start, width, 2).reshape(-1, width)
        lower = shifted(share(halo_lists[0, 1]), "region", 1)
        upper = shifted(share(halo_lists[0, 0]), "region", -1)
        return lower, upper, 1

    def exchange(operand):
        region = lax.all_gather(operand, "split", axis=0, tiled=True)
        lower, upper, axis = halos(operand, region)
        gather = lambda value: lax.all_gather(value, "split", axis=axis, tiled=True)
        return region, lower, upper, gather

    if whole:
        lower_order = shifted(halo_lists[0, 1], "region", 1)
        upper_order = shifted(halo_lists[0, 0], "region", -1)
    else:
        lower_order = upper_order = jnp.arange(halo_blocks, dtype=jnp.int32)
    places = jnp.concatenate(
        [
            jnp.arange(region_blocks, dtype=jnp.int32),
            region_blocks + lower_order,
            region_blocks + halo_blocks + upper_order,
        ]
    )
    place = places[block_cols]
    candidates = region_blocks + 2 * halo_blocks
    order = jnp.arange(stored, dtype=jnp.int32)[None, None, :]
    meets = place[:, None, :] == jnp.arange(candidates, dtype=jnp.int32)[None, :, None]
    meets = meets & (order < live_blocks[:, None, None])
    slots = jnp.max(jnp.where(meets, order, -1), axis=2)

    wide = jax.ShapeDtypeStruct((rows, modes), jnp.float32)
    narrow = jax.ShapeDtypeStruct((rows, modes), jnp.bfloat16)
    work = 2 * rows * size * modes
    traffic = hessian.size * 2 + 3 * rows * modes * 4

    def local_part(region):
        call = kernel_call(local_body, wide, [SMEM, VMEM, VMEM], work * region_blocks, traffic)
        return call(slots, hessian, region)

    def step(body, outs, operand, scalars, extra):
        region, lower, upper, gather = exchange(operand)
        partial = local_part(region)
        specs = [SMEM] * (1 + len(scalars)) + [VMEM] * (4 + len(extra))
        call = kernel_call(body, outs, specs, work * 2 * halo_blocks, traffic)
        return call(slots, *scalars, hessian, gather(lower), gather(upper), partial, *extra)

    one, one_cast = step(first_body, (wide, narrow), vectors.astype(jnp.bfloat16), (bounds,), (vectors,))
    two, two_cast = step(second_body, (wide, narrow), one_cast, (bounds,), (one, vectors))
    pair = jax.ShapeDtypeStruct((2 * modes, modes), jnp.float32)
    sums = summed(step(third_body, pair, two_cast, (), (two,)))
    square = jax.ShapeDtypeStruct((modes, modes), jnp.float32)
    call = kernel_call(
        functools.partial(finish_body, float(total_rows)), (wide, square), [VMEM, VMEM], 8 * rows * modes * modes, traffic
    )
    return call(sums, two)


def solution(mesh):
    placed = (
        P(("region", "split"), None),
        P(("region", "split"), None, None, None),
        P(("region", "split"), None),
        P(("region", "split")),
        P("region", None, None),
        P(),
    )
    return jax.shard_map(
        local,
        mesh=mesh,
        in_specs=placed,
        out_specs=(P(("region", "split"), None), P()),
        check_vma=False,
    )
```

time: 361 us -> 132 us (0.37)
  waiting for transfers between devices: 135 us -> 9.6 us
  other arithmetic: 82.1 us -> 4.85 us
  local copies, waits for them, and re-layouts: 51.3 us -> 3.43 us
  blocking collectives: 24.9 us -> 67.4 us
  matrix products: 28.9 us -> 0 us
  Pallas kernels: 0 us -> 27.5 us
  between operations: 18.1 us -> 0.75 us
    psum x1 -> x0, waiting for transfers between devices: 127 us -> none  [local(): gram, cross = lax.psum((gram_part, cross_part), ('region', 'split'))]
    another operation x10 -> x0, other arithmetic: 64.9 us -> none  [the longest x7 42.1 us: local(): lower = jnp.linalg.cholesky(gram)]
    all_to_all x0 -> x2, blocking collectives: none -> 39.4 us  [the longest x1 21 us: summed(): mine = jnp.sum(lax.all_to_all(pieces, AXES, 0, 0), axis=0)]
    pallas_call x0 -> x7, Pallas kernels: none -> 27.5 us  [the longest x1 12.2 us: local(): return call(sums, two)]
    gather x9 -> x2, local copies, waits for them, and re-layouts: 27.7 us -> 0.86 us  [local(): place = places[block_cols]]
    another operation x11 -> x0, matrix products: 14.5 us -> none  [the longest x3 4.02 us: local(): jax.scipy.linalg.solve_triangular(lower, filtered_two.T, lower=True)]
    dot_general x5 -> x0, matrix products: 14.4 us -> none  [the longest x3 9.13 us: apply_blocks(): jnp.einsum('rkij,rkjm->rim', hessian, picked, preferred_element_type=jnp....]
    another operation x9 -> x0, local copies, waits for them, and re-layouts: 9.17 us -> none
  transfers between devices with their start and end apart: 7 -> 8, of which waited for: 5 -> 4; matrix products, arithmetic and copies ran while one was open for 4% -> 4% of each run, Pallas kernels for 0% -> 3%
where the time goes in v1:
time: 132 us; the launch traced here: 131 us
  blocking collectives  67.4 us (51%)
  Pallas kernels  27.5 us (21%)
  starting transfers between devices  17.4 us (13%)
  waiting for transfers between devices  9.6 us (7%)
  other arithmetic  4.85 us (4%)
  local copies, waits for them, and re-layouts  3.43 us (3%)
    all_to_all x1, blocking collectives, summed(): mine = jnp.sum(lax.all_to_all(pieces, AXES, 0, 0), axis=0)  21 us
    all_to_all x1, blocking collectives, summed(): return lax.all_to_all(every, AXES, 0, 0).reshape(part.shape)  18.4 us
    all_gather x6, blocking collectives, exchange(): gather = lambda value: lax.all_gather(value, 'split', axis=axis, tiled=True)  17.7 us
    ppermute x8, starting transfers between devices, shifted(): return lax.ppermute(value, axis, pairs)  17.4 us
    pallas_call x1, Pallas kernels, local(): return call(sums, two)  12.2 us
    pallas_call x3, Pallas kernels, step(): call(slots, *scalars, hessian, gather(lower), gather(upper), partial, *ex...  11.8 us
    all_gather x3, blocking collectives, exchange(): region = lax.all_gather(operand, 'split', axis=0, tiled=True)  10.2 us
    ppermute x8, waiting for transfers between devices, shifted(): return lax.ppermute(value, axis, pairs)  9.6 us
  transfers between devices with their start and end apart: 8, of which 4 were waited for; matrix products, arithmetic and copies ran while one was open for 4% of the time, Pallas kernels for 3%

profile of v1, /device:TPU:1, one launch (start us, length us, event | category | flops | bytes accessed | tf_op | source)
XLA Modules:
  0.0 131.0 jit_solution(18238725282071720278)
XLA Ops:
  0.6 2.0 %convert_element_type.3 = bf16[576,256]{1,0:T(8,128)(2,1)} convert(f32[576,256]{1,0:T(8,128)} %vectors_ref.3) | non-fusion elementwise | flops 147456 | bytes 884736 | tf_op jit(solution)/shard_map/convert_element_type | solution.py:255
  2.6 6.0 %collective-permute-start.3 = (bf16[576,256]{1,0:T(8,128)(2,1)}, bf16[576,256]{1,0:T(8,128)(2,1)}, u32[]{:S(2)}, u32[]{:S(2)}) collective-permute-start(bf16[576,256]{1,0:T(8,128)(2,1)} %convert_element_type.3), channel_id=1, source_target_pairs={{0,30},{2,0},{4,2},{6,4},{8,6},{10,8},{12,10},{14,12},{16,14},{18,... | collective-permute-start | bytes 884744 | tf_op jit(solution)/shard_map/ppermute | solution.py:24
  8.6 1.3 slice_bitcast_fusion.1
  9.9 5.1 %collective-permute-start.1 = (s32[6]{0:T(128)}, s32[6]{0:T(128)}, u32[]{:S(2)}, u32[]{:S(2)}) collective-permute-start(s32[6]{0:T(128)} %get-tuple-element.11), channel_id=1, source_target_pairs={{0,30},{2,0},{4,2},{6,4},{8,6},{10,8},{12,10},{14,12},{16,14},{18,... | collective-permute-start | bytes 80 | tf_op jit(solution)/shard_map/ppermute | solution.py:24
  15.0 5.2 %all_gather.29.region_ref = bf16[1152,256]{1,0:T(8,128)(2,1)} all-gather(bf16[576,256]{1,0:T(8,128)(2,1)} %convert_element_type.3), channel_id=1, replica_groups=mesh['region'=16,'split'=2] {'split'}, dimensions={0}, use_global_device_ids=true | all-gather | bytes 884736 | tf_op jit(solution)/shard_map/all_gather | solution.py:215
  20.2 0.7 iota_compare_fusion.1
  20.9 0.7 compare_select_fusion
  23.1 0.8 gather_fusion
  24.0 1.1 copy-done.4
  25.2 1.2 shard_map.77.local_ref
  26.4 2.4 %all_gather.28.upper_ref = bf16[1152,256]{1,0:T(8,128)(2,1)S(1)} all-gather(bf16[576,256]{1,0:T(8,128)(2,1)} %collective-permute-done.3), channel_id=1, replica_groups=mesh['region'=16,'split'=2] {'split'}, dimensions={0}, use_global_device_ids=true | all-gather | bytes 884736 | tf_op jit(solution)/shard_map/all_gather | solution.py:217
  28.8 2.4 %all_gather.27.lower_ref = bf16[1152,256]{1,0:T(8,128)(2,1)S(1)} all-gather(bf16[576,256]{1,0:T(8,128)(2,1)} %collective-permute-done.2), channel_id=1, replica_groups=mesh['region'=16,'split'=2] {'split'}, dimensions={0}, use_global_device_ids=true | all-gather | bytes 884736 | tf_op jit(solution)/shard_map/all_gather | solution.py:217
  31.2 3.2 %shard_map.78 = (f32[576,256]{1,0:T(8,128)S(1)}, bf16[576,256]{1,0:T(8,128)(2,1)S(1)}) custom-call(s32[3,18]{1,0:T(4,128)S(1)} %select_reduce_fusion.slots_ref, f32[2]{0:T(128)S(1)} %copy-done.5, bf16[3,12,192,192]{3,2,1,0:T(8,128)(2,1)} %hessian_ref.11, bf16[1152,256]{1,0:T(8,128)(2,1)S(1)} %all_gather.27.lower_ref, ...), custom_call_target="tpu_custom_call" | custom-call | flops 679477248 | bytes 4423680 | tf_op jit(solution)/shard_map/pallas_call | solution.py:253
  34.5 2.7 %collective-permute-start.5 = (bf16[576,256]{1,0:T(8,128)(2,1)S(1)}, bf16[576,256]{1,0:T(8,128)(2,1)S(1)}, u32[]{:S(2)}, u32[]{:S(2)}) collective-permute-start(bf16[576,256]{1,0:T(8,128)(2,1)S(1)} %get-tuple-element.6), channel_id=1, source_target_pairs={{0,30},{2,0},{4,2},{6,4},{8,6},{10,8},{12,10},{14,12},{16,14},{18,... | collective-permute-start | bytes 884744 | tf_op jit(solution)/shard_map/ppermute | solution.py:24
  37.2 2.5 %all_gather.32.region_ref = bf16[1152,256]{1,0:T(8,128)(2,1)S(1)} all-gather(bf16[576,256]{1,0:T(8,128)(2,1)S(1)} %get-tuple-element.6), channel_id=1, replica_groups=mesh['region'=16,'split'=2] {'split'}, dimensions={0}, use_global_device_ids=true | all-gather | bytes 884736 | tf_op jit(solution)/shard_map/all_gather | solution.py:215
  39.7 1.2 shard_map.79.local_ref
  40.8 2.3 %collective-permute-done.5 = bf16[576,256]{1,0:T(8,128)(2,1)S(1)} collective-permute-done((bf16[576,256]{1,0:T(8,128)(2,1)S(1)}, bf16[576,256]{1,0:T(8,128)(2,1)S(1)}, u32[]{:S(2)}, u32[]{:S(2)}) %collective-permute-start.5) | collective-permute-done | bytes 294944 | tf_op jit(solution)/shard_map/ppermute | solution.py:24
  43.2 3.4 %all_gather.31.upper_ref = bf16[1152,256]{1,0:T(8,128)(2,1)S(1)} all-gather(bf16[576,256]{1,0:T(8,128)(2,1)S(1)} %collective-permute-done.5), channel_id=1, replica_groups=mesh['region'=16,'split'=2] {'split'}, dimensions={0}, use_global_device_ids=true | all-gather | bytes 884736 | tf_op jit(solution)/shard_map/all_gather | solution.py:217
  46.6 2.1 %collective-permute-done.4 = bf16[576,256]{1,0:T(8,128)(2,1)S(1)} collective-permute-done((bf16[576,256]{1,0:T(8,128)(2,1)S(1)}, bf16[576,256]{1,0:T(8,128)(2,1)S(1)}, u32[]{:S(2)}, u32[]{:S(2)}) %collective-permute-start.4) | collective-permute-done | bytes 294944 | tf_op jit(solution)/shard_map/ppermute | solution.py:24
  48.6 3.4 %all_gather.30.lower_ref = bf16[1152,256]{1,0:T(8,128)(2,1)S(1)} all-gather(bf16[576,256]{1,0:T(8,128)(2,1)S(1)} %collective-permute-done.4), channel_id=1, replica_groups=mesh['region'=16,'split'=2] {'split'}, dimensions={0}, use_global_device_ids=true | all-gather | bytes 884736 | tf_op jit(solution)/shard_map/all_gather | solution.py:217
  52.0 3.3 %shard_map.80 = (f32[576,256]{1,0:T(8,128)S(1)}, bf16[576,256]{1,0:T(8,128)(2,1)S(1)}) custom-call(s32[3,18]{1,0:T(4,128)S(1)} %select_reduce_fusion.slots_ref, f32[2]{0:T(128)S(1)} %copy-done.5, bf16[3,12,192,192]{3,2,1,0:T(8,128)(2,1)} %hessian_ref.11, bf16[1152,256]{1,0:T(8,128)(2,1)S(1)} %all_gather.30.lower_ref, ...), custom_call_target="tpu_custom_call" | custom-call | flops 679477248 | bytes 4423680 | tf_op jit(solution)/shard_map/pallas_call | solution.py:253
  55.3 3.7 %collective-permute-start.7 = (bf16[576,256]{1,0:T(8,128)(2,1)S(1)}, bf16[576,256]{1,0:T(8,128)(2,1)S(1)}, u32[]{:S(2)}, u32[]{:S(2)}) collective-permute-start(bf16[576,256]{1,0:T(8,128)(2,1)S(1)} %get-tuple-element.8), channel_id=1, source_target_pairs={{0,30},{2,0},{4,2},{6,4},{8,6},{10,8},{12,10},{14,12},{16,14},{18,... | collective-permute-start | bytes 884744 | tf_op jit(solution)/shard_map/ppermute | solution.py:24
  58.9 2.5 %all_gather.35.region_ref = bf16[1152,256]{1,0:T(8,128)(2,1)S(1)} all-gather(bf16[576,256]{1,0:T(8,128)(2,1)S(1)} %get-tuple-element.8), channel_id=1, replica_groups=mesh['region'=16,'split'=2] {'split'}, dimensions={0}, use_global_device_ids=true | all-gather | bytes 884736 | tf_op jit(solution)/shard_map/all_gather | solution.py:215
  61.5 1.2 shard_map.81.local_ref
  62.6 2.3 %collective-permute-done.7 = bf16[576,256]{1,0:T(8,128)(2,1)S(1)} collective-permute-done((bf16[576,256]{1,0:T(8,128)(2,1)S(1)}, bf16[576,256]{1,0:T(8,128)(2,1)S(1)}, u32[]{:S(2)}, u32[]{:S(2)}) %collective-permute-start.7) | collective-permute-done | bytes 294944 | tf_op jit(solution)/shard_map/ppermute | solution.py:24
  65.0 3.0 %all_gather.34.upper_ref = bf16[1152,256]{1,0:T(8,128)(2,1)S(1)} all-gather(bf16[576,256]{1,0:T(8,128)(2,1)S(1)} %collective-permute-done.7), channel_id=1, replica_groups=mesh['region'=16,'split'=2] {'split'}, dimensions={0}, use_global_device_ids=true | all-gather | bytes 884736 | tf_op jit(solution)/shard_map/all_gather | solution.py:217
  68.0 2.8 %collective-permute-done.6 = bf16[576,256]{1,0:T(8,128)(2,1)S(1)} collective-permute-done((bf16[576,256]{1,0:T(8,128)(2,1)S(1)}, bf16[576,256]{1,0:T(8,128)(2,1)S(1)}, u32[]{:S(2)}, u32[]{:S(2)}) %collective-permute-start.6) | collective-permute-done | bytes 294944 | tf_op jit(solution)/shard_map/ppermute | solution.py:24
  70.8 3.1 %all_gather.33.lower_ref = bf16[1152,256]{1,0:T(8,128)(2,1)S(1)} all-gather(bf16[576,256]{1,0:T(8,128)(2,1)S(1)} %collective-permute-done.6), channel_id=1, replica_groups=mesh['region'=16,'split'=2] {'split'}, dimensions={0}, use_global_device_ids=true | all-gather | bytes 884736 | tf_op jit(solution)/shard_map/all_gather | solution.py:217
  73.9 5.3 %shard_map.82 = f32[512,256]{1,0:T(8,128)S(1)} custom-call(s32[3,18]{1,0:T(4,128)S(1)} %select_reduce_fusion.slots_ref, bf16[3,12,192,192]{3,2,1,0:T(8,128)(2,1)} %hessian_ref.11, bf16[1152,256]{1,0:T(8,128)(2,1)S(1)} %all_gather.33.lower_ref, bf16[1152,256]{1,0:T(8,128)(2,1)S(1)} %all_gather.34.upper_ref, f32[576,256]{1,0:T(8,128)S(1)} %shard_map.81.local_ref, ...), custom_call_target="tpu_custom_call" | custom-call | flops 679477248 | bytes 4423680 | tf_op jit(solution)/shard_map/pallas_call | solution.py:253
  79.2 21.0 %all_to_all.10 = f32[32,16,256]{2,1,0:T(8,128)S(1)} all-to-all(f32[32,16,256]{2,1,0:T(8,128)S(1)} %bitcast.6), channel_id=1, replica_groups=mesh['region'=16,'split'=2] {'region','split'}, dimensions={0} | all-to-all | bytes 1048576 | tf_op jit(solution)/shard_map/all_to_all | solution.py:189
  100.3 18.4 %all_to_all.11 = f32[32,16,256]{2,1,0:T(8,128)S(1)} all-to-all(f32[32,16,256]{2,1,0:T(8,128)S(1)} %broadcast_in_dim.28), channel_id=1, replica_groups=mesh['region'=16,'split'=2] {'region','split'}, dimensions={0} | all-to-all | bytes 1048576 | tf_op jit(solution)/shard_map/all_to_all | solution.py:191
  118.8 12.2 %shard_map.83 = (f32[576,256]{1,0:T(8,128)}, f32[256,256]{1,0:T(8,128)}) custom-call(f32[512,256]{1,0:T(8,128)S(1)} %bitcast.7, f32[576,256]{1,0:T(8,128)S(1)} %get-tuple-element.9.two_ref), custom_call_target="tpu_custom_call" | custom-call | flops 301989888 | bytes 4423680 | tf_op jit(solution)/shard_map/pallas_call | solution.py:263
  (29 shorter events, 1.7 us)
Async XLA Ops:
  0.6 23.4 %copy-start = (bf16[3,12,192,192]{3,2,1,0:T(8,128)(2,1)S(1)}, bf16[3,12,192,192]{3,2,1,0:T(8,128)(2,1)}, u32[]{:S(2)}) copy-start(bf16[3,12,192,192]{3,2,1,0:T(8,128)(2,1)} %hessian_ref.11) | copy-start | bytes 7962628
  2.6 23.7 %collective-permute-start.3 = (bf16[576,256]{1,0:T(8,128)(2,1)}, bf16[576,256]{1,0:T(8,128)(2,1)}, u32[]{:S(2)}, u32[]{:S(2)}) collective-permute-start(bf16[576,256]{1,0:T(8,128)(2,1)} %convert_element_type.3), channel_id=1, source_target_pairs={{0,30},{2,0},{4,2},{6,4},{8,6},{10,8},{12,10},{14,12},{16,14},{18,... | collective-permute-start | bytes 884744 | tf_op jit(solution)/shard_map/ppermute | solution.py:24
  8.6 20.2 %collective-permute-start.2 = (bf16[576,256]{1,0:T(8,128)(2,1)}, bf16[576,256]{1,0:T(8,128)(2,1)}, u32[]{:S(2)}, u32[]{:S(2)}) collective-permute-start(bf16[576,256]{1,0:T(8,128)(2,1)} %convert_element_type.3), channel_id=1, source_target_pairs={{0,2},{2,4},{4,6},{6,8},{8,10},{10,12},{12,14},{14,16},{16,18},{18... | collective-permute-start | bytes 884744 | tf_op jit(solution)/shard_map/ppermute | solution.py:24
  9.9 11.8 %collective-permute-start = (s32[6]{0:T(128)}, s32[6]{0:T(128)}, u32[]{:S(2)}, u32[]{:S(2)}) collective-permute-start(s32[6]{0:T(128)} %get-tuple-element.10), channel_id=1, source_target_pairs={{0,2},{2,4},{4,6},{6,8},{8,10},{10,12},{12,14},{14,16},{16,18},{18... | collective-permute-start | bytes 80 | tf_op jit(solution)/shard_map/ppermute | solution.py:24
  9.9 12.4 %collective-permute-start.1 = (s32[6]{0:T(128)}, s32[6]{0:T(128)}, u32[]{:S(2)}, u32[]{:S(2)}) collective-permute-start(s32[6]{0:T(128)} %get-tuple-element.11), channel_id=1, source_target_pairs={{0,30},{2,0},{4,2},{6,4},{8,6},{10,8},{12,10},{14,12},{16,14},{18,... | collective-permute-start | bytes 80 | tf_op jit(solution)/shard_map/ppermute | solution.py:24
  23.8 7.4 %copy-start.5 = (f32[2]{0:T(128)S(1)}, f32[2]{0:T(128)}, u32[]{:S(2)}) copy-start(f32[2]{0:T(128)} %bounds_ref.3) | copy-start | bytes 28
  23.9 7.3 %copy-start.3 = (f32[576,256]{1,0:T(8,128)S(1)}, f32[576,256]{1,0:T(8,128)}, u32[]{:S(2)}) copy-start(f32[576,256]{1,0:T(8,128)} %vectors_ref.3) | copy-start | bytes 1769476
  24.0 1.1 copy-start.4
  31.2 8.4 %copy-start.1 = (bf16[3,12,192,192]{3,2,1,0:T(8,128)(2,1)S(1)}, bf16[3,12,192,192]{3,2,1,0:T(8,128)(2,1)}, u32[]{:S(2)}) copy-start(bf16[3,12,192,192]{3,2,1,0:T(8,128)(2,1)} %hessian_ref.11) | copy-start | bytes 7962628
  34.5 8.7 %collective-permute-start.5 = (bf16[576,256]{1,0:T(8,128)(2,1)S(1)}, bf16[576,256]{1,0:T(8,128)(2,1)S(1)}, u32[]{:S(2)}, u32[]{:S(2)}) collective-permute-start(bf16[576,256]{1,0:T(8,128)(2,1)S(1)} %get-tuple-element.6), channel_id=1, source_target_pairs={{0,30},{2,0},{4,2},{6,4},{8,6},{10,8},{12,10},{14,12},{16,14},{18,... | collective-permute-start | bytes 884744 | tf_op jit(solution)/shard_map/ppermute | solution.py:24
  37.2 11.5 %collective-permute-start.4 = (bf16[576,256]{1,0:T(8,128)(2,1)S(1)}, bf16[576,256]{1,0:T(8,128)(2,1)S(1)}, u32[]{:S(2)}, u32[]{:S(2)}) collective-permute-start(bf16[576,256]{1,0:T(8,128)(2,1)S(1)} %get-tuple-element.6), channel_id=1, source_target_pairs={{0,2},{2,4},{4,6},{6,8},{8,10},{10,12},{12,14},{14,16},{16,18},{18... | collective-permute-start | bytes 884744 | tf_op jit(solution)/shard_map/ppermute | solution.py:24
  52.0 9.4 %copy-start.2 = (bf16[3,12,192,192]{3,2,1,0:T(8,128)(2,1)S(1)}, bf16[3,12,192,192]{3,2,1,0:T(8,128)(2,1)}, u32[]{:S(2)}) copy-start(bf16[3,12,192,192]{3,2,1,0:T(8,128)(2,1)} %hessian_ref.11) | copy-start | bytes 7962628
  55.3 9.7 %collective-permute-start.7 = (bf16[576,256]{1,0:T(8,128)(2,1)S(1)}, bf16[576,256]{1,0:T(8,128)(2,1)S(1)}, u32[]{:S(2)}, u32[]{:S(2)}) collective-permute-start(bf16[576,256]{1,0:T(8,128)(2,1)S(1)} %get-tuple-element.8), channel_id=1, source_target_pairs={{0,30},{2,0},{4,2},{6,4},{8,6},{10,8},{12,10},{14,12},{16,14},{18,... | collective-permute-start | bytes 884744 | tf_op jit(solution)/shard_map/ppermute | solution.py:24
  58.9 11.9 %collective-permute-start.6 = (bf16[576,256]{1,0:T(8,128)(2,1)S(1)}, bf16[576,256]{1,0:T(8,128)(2,1)S(1)}, u32[]{:S(2)}, u32[]{:S(2)}) collective-permute-start(bf16[576,256]{1,0:T(8,128)(2,1)S(1)} %get-tuple-element.8), channel_id=1, source_target_pairs={{0,2},{2,4},{4,6},{6,8},{8,10},{10,12},{12,14},{14,16},{16,18},{18... | collective-permute-start | bytes 884744 | tf_op jit(solution)/shard_map/ppermute | solution.py:24

commit v2 on v1

--- a/solution.py
+++ b/solution.py
@@ -16,6 +16,7 @@
 VMEM_LIMIT = 48 * 1024 * 1024
 GROUP = 8
 TILE = 128
+LIST_ROWS = 16
 
 
 def shifted(value, axis, steps):
@@ -52,8 +53,11 @@
 
 def accumulate(slots_ref, hessian_ref, first_slot, operand_ref, total):
     size = hessian_ref.shape[2]
-    for index in range(operand_ref.shape[0] // size):
-        block = operand_ref[index * size : (index + 1) * size, :]
+    shards, shard_rows, _ = operand_ref.shape
+    each = shard_rows // size
+    for index in range(shards * each):
+        start = index % each * size
+        block = operand_ref[index // each, start : start + size, :]
         term = candidate_dot(slots_ref, hessian_ref, first_slot, index, block)
         total = term if total is None else total + term
     return total
@@ -65,10 +69,9 @@
 
 def halo_total(slots_ref, hessian_ref, lower_ref, upper_ref, local_ref):
     size = hessian_ref.shape[2]
-    halo = lower_ref.shape[0] // size
-    own = slots_ref.shape[1] - 2 * halo
-    total = accumulate(slots_ref, hessian_ref, own, lower_ref, local_ref[...])
-    return accumulate(slots_ref, hessian_ref, own + halo, upper_ref, total)
+    halo = lower_ref.shape[0] * (lower_ref.shape[1] // size)
+    total = accumulate(slots_ref, hessian_ref, 0, lower_ref, local_ref[...])
+    return accumulate(slots_ref, hessian_ref, halo, upper_ref, total)
 
 
 def first_body(slots_ref, bounds_ref, hessian_ref, lower_ref, upper_ref, local_ref, vectors_ref, one_ref, cast_ref):
@@ -183,12 +186,33 @@
     projected_ref[...] = exact_dot(left, inverse, NT)
 
 
+def region_groups():
+    count = lax.axis_size("region")
+    near = 1
+    while near * near < count:
+        near *= 2
+    if count % near:
+        near = count
+    minor = [[first + at for at in range(near)] for first in range(0, count, near)]
+    major = [[at + first for first in range(0, count, near)] for at in range(near)]
+    return [groups for groups in (minor, major) if len(groups[0]) > 1]
+
+
 def summed(part):
-    count = lax.axis_size(AXES)
-    pieces = part.reshape(count, part.shape[0] // count, part.shape[1])
-    mine = jnp.sum(lax.all_to_all(pieces, AXES, 0, 0), axis=0)
-    every = jnp.broadcast_to(mine[None], pieces.shape)
-    return lax.all_to_all(every, AXES, 0, 0).reshape(part.shape)
+    width = part.shape[1]
+    stages = [("split", None, lax.axis_size("split"))]
+    stages += [("region", groups, len(groups[0])) for groups in region_groups()]
+    value = part
+    for axis, groups, count in stages:
+        pieces = value.reshape(count, value.shape[0] // count, width)
+        value = jnp.sum(lax.all_to_all(pieces, axis, 0, 0, axis_index_groups=groups), axis=0)
+    for axis, groups, count in reversed(stages):
+        if groups is None:
+            value = lax.all_gather(value, axis, axis=0, tiled=True)
+        else:
+            every = jnp.broadcast_to(value[None], (count,) + value.shape)
+            value = lax.all_to_all(every, axis, 0, 0, axis_index_groups=groups).reshape(-1, width)
+    return value
 
 
 def local(vectors, hessian, block_cols, live_blocks, halo_lists, bounds):
@@ -197,44 +221,50 @@
     splits = lax.axis_size("split")
     region_blocks = row_blocks * splits
     halo_blocks = halo_lists.shape[2]
-    whole = halo_blocks == region_blocks
+    whole = halo_blocks == region_blocks and region_blocks <= 256
     total_rows = rows * lax.axis_size(AXES)
 
     def halos(operand, region):
         if whole:
-            return shifted(operand, "region", 1), shifted(operand, "region", -1), 0
+            return shifted(operand, "region", 1), shifted(operand, "region", -1)
         width = modes // splits
         start = lax.axis_index("split") * width
-        blocks = region.reshape(region_blocks, size, modes)
+        blocks = region[:, :rows].reshape(region_blocks, size, modes)
         share = lambda listed: lax.dynamic_slice_in_dim(blocks[listed], start, width, 2).reshape(-1, width)
         lower = shifted(share(halo_lists[0, 1]), "region", 1)
         upper = shifted(share(halo_lists[0, 0]), "region", -1)
-        return lower, upper, 1
-
-    def exchange(operand):
-        region = lax.all_gather(operand, "split", axis=0, tiled=True)
-        lower, upper, axis = halos(operand, region)
-        gather = lambda value: lax.all_gather(value, "split", axis=axis, tiled=True)
-        return region, lower, upper, gather
-
+        return lower, upper
+
+    def gather(value):
+        if whole:
+            return lax.all_gather(value, "split", axis=0)
+        return lax.all_gather(value, "split", axis=1, tiled=True)[None]
+
+    listed = jnp.pad(halo_lists[0], ((0, LIST_ROWS - 2), (0, modes - halo_blocks)))
+    first = vectors.astype(jnp.bfloat16)
     if whole:
-        lower_order = shifted(halo_lists[0, 1], "region", 1)
-        upper_order = shifted(halo_lists[0, 0], "region", -1)
+        first = jnp.concatenate([first, listed.astype(jnp.bfloat16)], 0)
+    first_region = lax.all_gather(first, "split", axis=0)
+    first_lower, first_upper = halos(first, first_region)
+    if whole:
+        lower_order = first_lower[rows + 1, :halo_blocks].astype(jnp.int32)
+        upper_order = first_upper[rows, :halo_blocks].astype(jnp.int32)
     else:
         lower_order = upper_order = jnp.arange(halo_blocks, dtype=jnp.int32)
-    places = jnp.concatenate(
-        [
-            jnp.arange(region_blocks, dtype=jnp.int32),
-            region_blocks + lower_order,
-            region_blocks + halo_blocks + upper_order,
-        ]
-    )
-    place = places[block_cols]
-    candidates = region_blocks + 2 * halo_blocks
+    near_places = jnp.arange(region_blocks, dtype=jnp.int32)
+    lower_places = region_blocks + lower_order
+    upper_places = region_blocks + halo_blocks + upper_order
+
     order = jnp.arange(stored, dtype=jnp.int32)[None, None, :]
-    meets = place[:, None, :] == jnp.arange(candidates, dtype=jnp.int32)[None, :, None]
-    meets = meets & (order < live_blocks[:, None, None])
-    slots = jnp.max(jnp.where(meets, order, -1), axis=2)
+    live = order < live_blocks[:, None, None]
+
+    def slots_of(place, first_place, count):
+        meets = place[:, None, :] == first_place + jnp.arange(count, dtype=jnp.int32)[None, :, None]
+        return jnp.max(jnp.where(meets & live, order, -1), axis=2)
+
+    near_slots = slots_of(block_cols, 0, region_blocks)
+    places = jnp.concatenate([near_places, lower_places, upper_places])
+    far_slots = slots_of(places[block_cols], region_blocks, 2 * halo_blocks)
 
     wide = jax.ShapeDtypeStruct((rows, modes), jnp.float32)
     narrow = jax.ShapeDtypeStruct((rows, modes), jnp.bfloat16)
@@ -243,19 +273,22 @@
 
     def local_part(region):
         call = kernel_call(local_body, wide, [SMEM, VMEM, VMEM], work * region_blocks, traffic)
-        return call(slots, hessian, region)
-
-    def step(body, outs, operand, scalars, extra):
-        region, lower, upper, gather = exchange(operand)
+        return call(near_slots, hessian, region)
+
+    def step(body, outs, region, lower, upper, scalars, extra):
         partial = local_part(region)
         specs = [SMEM] * (1 + len(scalars)) + [VMEM] * (4 + len(extra))
         call = kernel_call(body, outs, specs, work * 2 * halo_blocks, traffic)
-        return call(slots, *scalars, hessian, gather(lower), gather(upper), partial, *extra)
-
-    one, one_cast = step(first_body, (wide, narrow), vectors.astype(jnp.bfloat16), (bounds,), (vectors,))
-    two, two_cast = step(second_body, (wide, narrow), one_cast, (bounds,), (one, vectors))
+        return call(far_slots, *scalars, hessian, gather(lower), gather(upper), partial, *extra)
+
+    def later(body, outs, operand, scalars, extra):
+        region = lax.all_gather(operand, "split", axis=0)
+        return step(body, outs, region, *halos(operand, region), scalars, extra)
+
+    one, one_cast = step(first_body, (wide, narrow), first_region, first_lower, first_upper, (bounds,), (vectors,))
+    two, two_cast = later(second_body, (wide, narrow), one_cast, (bounds,), (one, vectors))
     pair = jax.ShapeDtypeStruct((2 * modes, modes), jnp.float32)
-    sums = summed(step(third_body, pair, two_cast, (), (two,)))
+    sums = summed(later(third_body, pair, two_cast, (), (two,)))
     square = jax.ShapeDtypeStruct((modes, modes), jnp.float32)
     call = kernel_call(
         functools.partial(finish_body, float(total_rows)), (wide, square), [VMEM, VMEM], 8 * rows * modes * modes, traffic

time: 132 us -> 131 us (level)
  starting transfers between devices: 17.4 us -> 12.6 us
  waiting for transfers between devices: 9.6 us -> 12.7 us
  blocking collectives: 67.4 us -> 69.2 us
    all_gather x9 -> x10, blocking collectives: 27.9 us -> 34.1 us  [the longest x6 18.5 us: gather(): return lax.all_gather(value, 'split', axis=0)]
    ppermute x8 -> x6, starting transfers between devices: 17.4 us -> 12.6 us  [shifted(): return lax.ppermute(value, axis, pairs)]
    all_to_all x2 -> x5, blocking collectives: 39.4 us -> 35.2 us  [the longest x3 21.2 us: summed(): lax.all_to_all(pieces, axis, 0, 0, axis_index_groups=groups)]
    ppermute x8 -> x6, waiting for transfers between devices: 9.6 us -> 12.7 us  [shifted(): return lax.ppermute(value, axis, pairs)]
  transfers between devices with their start and end apart: 8 -> 6, of which waited for: 4 -> 5; matrix products, arithmetic and copies ran while one was open for 4% -> 2% of each run, Pallas kernels for 3% -> 3%
where the time goes in v2:
time: 131 us; the launch traced here: 130 us
  blocking collectives  69.2 us (53%)
  Pallas kernels  27.5 us (21%)
  waiting for transfers between devices  12.7 us (10%)
  starting transfers between devices  12.6 us (10%)
  other arithmetic  4.42 us (3%)
  local copies, waits for them, and re-layouts  2.99 us (2%)
    all_to_all x3, blocking collectives, summed(): lax.all_to_all(pieces, axis, 0, 0, axis_index_groups=groups)  21.2 us
    all_gather x6, blocking collectives, gather(): return lax.all_gather(value, 'split', axis=0)  18.5 us
    all_to_all x2, blocking collectives, summed(): lax.all_to_all(every, axis, 0, 0, axis_index_groups=groups)  13.9 us
    ppermute x6, waiting for transfers between devices, shifted(): return lax.ppermute(value, axis, pairs)  12.7 us
    ppermute x6, starting transfers between devices, shifted(): return lax.ppermute(value, axis, pairs)  12.6 us
    pallas_call x1, Pallas kernels, local(): return call(sums, two)  12.2 us
    pallas_call x3, Pallas kernels, step(): call(far_slots, *scalars, hessian, gather(lower), gather(upper), partial,...  11.8 us
    all_gather x1, blocking collectives, summed(): value = lax.all_gather(value, axis, axis=0, tiled=True)  7.76 us
  transfers between devices with their start and end apart: 6, of which 5 were waited for; matrix products, arithmetic and copies ran while one was open for 2% of the time, Pallas kernels for 3%

profile of v2, /device:TPU:1, one launch (start us, length us, event | category | flops | bytes accessed | tf_op | source)
XLA Modules:
  0.0 130.3 jit_solution(3220579951709547643)
XLA Ops:
  1.3 1.1 convert_element_type.12
  2.4 6.1 %collective-permute-start.1 = (bf16[592,256]{1,0:T(8,128)(2,1)S(1)}, bf16[592,256]{1,0:T(8,128)(2,1)S(1)}, u32[]{:S(2)}, u32[]{:S(2)}) collective-permute-start(bf16[592,256]{1,0:T(8,128)(2,1)S(1)} %fusion.1), channel_id=1, source_target_pairs={{0,30},{2,0},{4,2},{6,4},{8,6},{10,8},{12,10},{14,12},{16,14},{18,... | collective-permute-start | bytes 909320 | tf_op jit(solution)/shard_map/ppermute | solution.py:25
  8.5 2.8 %all-gather.2 = bf16[1184,256]{1,0:T(8,128)(2,1)S(1)} all-gather(bf16[592,256]{1,0:T(8,128)(2,1)S(1)} %fusion.1), channel_id=4, replica_groups=mesh['region'=16,'split'=2] {'split'}, dimensions={0}, use_global_device_ids=true | all-gather | bytes 909312 | tf_op jit(solution)/shard_map/all_gather | solution.py:247
  13.7 2.0 %copy-done = bf16[3,12,192,192]{3,2,1,0:T(8,128)(2,1)S(1)} copy-done((bf16[3,12,192,192]{3,2,1,0:T(8,128)(2,1)S(1)}, bf16[3,12,192,192]{3,2,1,0:T(8,128)(2,1)}, u32[]{:S(2)}) %copy-start) | copy-done | bytes 2654232
  15.7 1.2 shard_map.77.local_ref
  16.9 2.9 %collective-permute-done = bf16[592,256]{1,0:T(8,128)(2,1)S(1)} collective-permute-done((bf16[592,256]{1,0:T(8,128)(2,1)S(1)}, bf16[592,256]{1,0:T(8,128)(2,1)S(1)}, u32[]{:S(2)}, u32[]{:S(2)}) %collective-permute-start) | collective-permute-done | bytes 303136 | tf_op jit(solution)/shard_map/ppermute | solution.py:25
  21.0 3.7 %all-gather.1 = bf16[1184,256]{1,0:T(8,128)(2,1)S(1)} all-gather(bf16[592,256]{1,0:T(8,128)(2,1)S(1)} %collective-permute-done.1), channel_id=3, replica_groups=mesh['region'=16,'split'=2] {'split'}, dimensions={0}, use_global_device_ids=true | all-gather | bytes 909312 | tf_op jit(solution)/shard_map/all_gather | solution.py:240
  24.8 2.2 %all-gather = bf16[1184,256]{1,0:T(8,128)(2,1)S(1)} all-gather(bf16[592,256]{1,0:T(8,128)(2,1)S(1)} %collective-permute-done), channel_id=2, replica_groups=mesh['region'=16,'split'=2] {'split'}, dimensions={0}, use_global_device_ids=true | all-gather | bytes 909312 | tf_op jit(solution)/shard_map/all_gather | solution.py:240
  27.0 3.2 %shard_map.78 = (f32[576,256]{1,0:T(8,128)S(1)}, bf16[576,256]{1,0:T(8,128)(2,1)S(1)}) custom-call(s32[3,12]{1,0:T(4,128)S(1)} %select_reduce_fusion.slots_ref, f32[2]{0:T(128)S(1)} %copy-done.4, bf16[3,12,192,192]{3,2,1,0:T(8,128)(2,1)} %hessian_ref.11, bf16[2,592,256]{2,1,0:T(8,128)(2,1)S(1)} %bitcast.21, bf16[2,592,256]{2,1,0:T(8,128)(2,1)S(1)} %bitcast.20, ...), custom_call_target="tpu_custom_call" | custom-call | flops 679477248 | bytes 4423680 | tf_op jit(solution)/shard_map/pallas_call | solution.py:282
  30.2 2.9 %collective-permute-start.3 = (bf16[576,256]{1,0:T(8,128)(2,1)S(1)}, bf16[576,256]{1,0:T(8,128)(2,1)S(1)}, u32[]{:S(2)}, u32[]{:S(2)}) collective-permute-start(bf16[576,256]{1,0:T(8,128)(2,1)S(1)} %get-tuple-element.6), channel_id=1, source_target_pairs={{0,30},{2,0},{4,2},{6,4},{8,6},{10,8},{12,10},{14,12},{16,14},{18,... | collective-permute-start | bytes 884744 | tf_op jit(solution)/shard_map/ppermute | solution.py:25
  33.1 2.5 %all-gather.5 = bf16[1152,256]{1,0:T(8,128)(2,1)S(1)} all-gather(bf16[576,256]{1,0:T(8,128)(2,1)S(1)} %get-tuple-element.6), channel_id=7, replica_groups=mesh['region'=16,'split'=2] {'split'}, dimensions={0}, use_global_device_ids=true | all-gather | bytes 884736 | tf_op jit(solution)/shard_map/all_gather | solution.py:285
  35.6 1.2 shard_map.79.local_ref
  36.8 2.3 %collective-permute-done.3 = bf16[576,256]{1,0:T(8,128)(2,1)S(1)} collective-permute-done((bf16[576,256]{1,0:T(8,128)(2,1)S(1)}, bf16[576,256]{1,0:T(8,128)(2,1)S(1)}, u32[]{:S(2)}, u32[]{:S(2)}) %collective-permute-start.3) | collective-permute-done | bytes 294944 | tf_op jit(solution)/shard_map/ppermute | solution.py:25
  39.2 3.2 %all-gather.4 = bf16[1152,256]{1,0:T(8,128)(2,1)S(1)} all-gather(bf16[576,256]{1,0:T(8,128)(2,1)S(1)} %collective-permute-done.3), channel_id=6, replica_groups=mesh['region'=16,'split'=2] {'split'}, dimensions={0}, use_global_device_ids=true | all-gather | bytes 884736 | tf_op jit(solution)/shard_map/all_gather | solution.py:240
  42.4 2.3 %collective-permute-done.2 = bf16[576,256]{1,0:T(8,128)(2,1)S(1)} collective-permute-done((bf16[576,256]{1,0:T(8,128)(2,1)S(1)}, bf16[576,256]{1,0:T(8,128)(2,1)S(1)}, u32[]{:S(2)}, u32[]{:S(2)}) %collective-permute-start.2) | collective-permute-done | bytes 294944 | tf_op jit(solution)/shard_map/ppermute | solution.py:25
  44.6 3.4 %all-gather.3 = bf16[1152,256]{1,0:T(8,128)(2,1)S(1)} all-gather(bf16[576,256]{1,0:T(8,128)(2,1)S(1)} %collective-permute-done.2), channel_id=5, replica_groups=mesh['region'=16,'split'=2] {'split'}, dimensions={0}, use_global_device_ids=true | all-gather | bytes 884736 | tf_op jit(solution)/shard_map/all_gather | solution.py:240
  48.0 3.3 %shard_map.80 = (f32[576,256]{1,0:T(8,128)S(1)}, bf16[576,256]{1,0:T(8,128)(2,1)S(1)}) custom-call(s32[3,12]{1,0:T(4,128)S(1)} %select_reduce_fusion.slots_ref, f32[2]{0:T(128)S(1)} %copy-done.4, bf16[3,12,192,192]{3,2,1,0:T(8,128)(2,1)} %hessian_ref.11, bf16[2,576,256]{2,1,0:T(8,128)(2,1)S(1)} %bitcast.25, bf16[2,576,256]{2,1,0:T(8,128)(2,1)S(1)} %bitcast.23, ...), custom_call_target="tpu_custom_call" | custom-call | flops 679477248 | bytes 4423680 | tf_op jit(solution)/shard_map/pallas_call | solution.py:282
  51.3 3.6 %collective-permute-start.5 = (bf16[576,256]{1,0:T(8,128)(2,1)S(1)}, bf16[576,256]{1,0:T(8,128)(2,1)S(1)}, u32[]{:S(2)}, u32[]{:S(2)}) collective-permute-start(bf16[576,256]{1,0:T(8,128)(2,1)S(1)} %get-tuple-element.8), channel_id=1, source_target_pairs={{0,30},{2,0},{4,2},{6,4},{8,6},{10,8},{12,10},{14,12},{16,14},{18,... | collective-permute-start | bytes 884744 | tf_op jit(solution)/shard_map/ppermute | solution.py:25
  54.9 2.5 %all-gather.8 = bf16[1152,256]{1,0:T(8,128)(2,1)S(1)} all-gather(bf16[576,256]{1,0:T(8,128)(2,1)S(1)} %get-tuple-element.8), channel_id=10, replica_groups=mesh['region'=16,'split'=2] {'split'}, dimensions={0}, use_global_device_ids=true | all-gather | bytes 884736 | tf_op jit(solution)/shard_map/all_gather | solution.py:285
  57.4 1.2 shard_map.81.local_ref
  58.6 2.3 %collective-permute-done.5 = bf16[576,256]{1,0:T(8,128)(2,1)S(1)} collective-permute-done((bf16[576,256]{1,0:T(8,128)(2,1)S(1)}, bf16[576,256]{1,0:T(8,128)(2,1)S(1)}, u32[]{:S(2)}, u32[]{:S(2)}) %collective-permute-start.5) | collective-permute-done | bytes 294944 | tf_op jit(solution)/shard_map/ppermute | solution.py:25
  60.9 3.0 %all-gather.7 = bf16[1152,256]{1,0:T(8,128)(2,1)S(1)} all-gather(bf16[576,256]{1,0:T(8,128)(2,1)S(1)} %collective-permute-done.5), channel_id=9, replica_groups=mesh['region'=16,'split'=2] {'split'}, dimensions={0}, use_global_device_ids=true | all-gather | bytes 884736 | tf_op jit(solution)/shard_map/all_gather | solution.py:240
  64.0 2.9 %collective-permute-done.4 = bf16[576,256]{1,0:T(8,128)(2,1)S(1)} collective-permute-done((bf16[576,256]{1,0:T(8,128)(2,1)S(1)}, bf16[576,256]{1,0:T(8,128)(2,1)S(1)}, u32[]{:S(2)}, u32[]{:S(2)}) %collective-permute-start.4) | collective-permute-done | bytes 294944 | tf_op jit(solution)/shard_map/ppermute | solution.py:25
  66.8 2.9 %all-gather.6 = bf16[1152,256]{1,0:T(8,128)(2,1)S(1)} all-gather(bf16[576,256]{1,0:T(8,128)(2,1)S(1)} %collective-permute-done.4), channel_id=8, replica_groups=mesh['region'=16,'split'=2] {'split'}, dimensions={0}, use_global_device_ids=true | all-gather | bytes 884736 | tf_op jit(solution)/shard_map/all_gather | solution.py:240
  69.8 5.3 %shard_map.82 = f32[512,256]{1,0:T(8,128)S(1)} custom-call(s32[3,12]{1,0:T(4,128)S(1)} %select_reduce_fusion.slots_ref, bf16[3,12,192,192]{3,2,1,0:T(8,128)(2,1)} %hessian_ref.11, bf16[2,576,256]{2,1,0:T(8,128)(2,1)S(1)} %bitcast.26, bf16[2,576,256]{2,1,0:T(8,128)(2,1)S(1)} %bitcast.24, f32[576,256]{1,0:T(8,128)S(1)} %shard_map.81.local_ref, ...), custom_call_target="tpu_custom_call" | custom-call | flops 679477248 | bytes 4423680 | tf_op jit(solution)/shard_map/pallas_call | solution.py:282
  75.0 4.2 %all_to_all.25 = f32[2,256,256]{2,1,0:T(8,128)S(1)} all-to-all(f32[2,256,256]{2,1,0:T(8,128)S(1)} %bitcast.29), channel_id=1, replica_groups=mesh['region'=16,'split'=2] {'split'}, dimensions={0} | all-to-all | bytes 1048576 | tf_op jit(solution)/shard_map/all_to_all | solution.py:208
  79.2 7.3 %all_to_all.26 = f32[4,64,256]{2,1,0:T(8,128)S(1)} all-to-all(f32[4,64,256]{2,1,0:T(8,128)S(1)} %bitcast.31), channel_id=1, replica_groups={{0,2,4,6},{8,10,12,14},{16,18,20,22},{24,26,28,30},{1,3,5,7},{9,11,13,1..., dimensions={0} | all-to-all | bytes 524288 | tf_op jit(solution)/shard_map/all_to_all | solution.py:208
  86.5 9.8 %all_to_all.27 = f32[4,16,256]{2,1,0:T(8,128)S(1)} all-to-all(f32[4,16,256]{2,1,0:T(8,128)S(1)} %bitcast.32), channel_id=1, replica_groups={{0,8,16,24},{2,10,18,26},{4,12,20,28},{6,14,22,30},{1,9,17,25},{3,11,19..., dimensions={0} | all-to-all | bytes 131072 | tf_op jit(solution)/shard_map/all_to_all | solution.py:208
  96.4 7.0 %all_to_all.28 = f32[4,16,256]{2,1,0:T(8,128)S(1)} all-to-all(f32[4,16,256]{2,1,0:T(8,128)S(1)} %broadcast_in_dim.51), channel_id=1, replica_groups={{0,8,16,24},{2,10,18,26},{4,12,20,28},{6,14,22,30},{1,9,17,25},{3,11,19..., dimensions={0} | all-to-all | bytes 131072 | tf_op jit(solution)/shard_map/all_to_all | solution.py:214
  103.4 7.0 %all_to_all.29 = f32[4,64,256]{2,1,0:T(8,128)S(1)} all-to-all(f32[4,64,256]{2,1,0:T(8,128)S(1)} %broadcast_in_dim.53), channel_id=1, replica_groups={{0,2,4,6},{8,10,12,14},{16,18,20,22},{24,26,28,30},{1,3,5,7},{9,11,13,1..., dimensions={0} | all-to-all | bytes 524288 | tf_op jit(solution)/shard_map/all_to_all | solution.py:214
  110.3 7.8 %all_gather.75.sums_ref = f32[512,256]{1,0:T(8,128)S(1)} all-gather(f32[256,256]{1,0:T(8,128)S(1)} %bitcast.30), channel_id=1, replica_groups=mesh['region'=16,'split'=2] {'split'}, dimensions={0}, use_global_device_ids=true | all-gather | bytes 786432 | tf_op jit(solution)/shard_map/all_gather | solution.py:211
  118.1 12.2 %shard_map.83 = (f32[576,256]{1,0:T(8,128)}, f32[256,256]{1,0:T(8,128)}) custom-call(f32[512,256]{1,0:T(8,128)S(1)} %all_gather.75.sums_ref, f32[576,256]{1,0:T(8,128)S(1)} %get-tuple-element.9.two_ref), custom_call_target="tpu_custom_call" | custom-call | flops 301989888 | bytes 4423680 | tf_op jit(solution)/shard_map/pallas_call | solution.py:296
  (33 shorter events, 4.3 us)
Async XLA Ops:
  2.4 14.4 %collective-permute-start.1 = (bf16[592,256]{1,0:T(8,128)(2,1)S(1)}, bf16[592,256]{1,0:T(8,128)(2,1)S(1)}, u32[]{:S(2)}, u32[]{:S(2)}) collective-permute-start(bf16[592,256]{1,0:T(8,128)(2,1)S(1)} %fusion.1), channel_id=1, source_target_pairs={{0,30},{2,0},{4,2},{6,4},{8,6},{10,8},{12,10},{14,12},{16,14},{18,... | collective-permute-start | bytes 909320 | tf_op jit(solution)/shard_map/ppermute | solution.py:25
  8.5 11.3 %collective-permute-start = (bf16[592,256]{1,0:T(8,128)(2,1)S(1)}, bf16[592,256]{1,0:T(8,128)(2,1)S(1)}, u32[]{:S(2)}, u32[]{:S(2)}) collective-permute-start(bf16[592,256]{1,0:T(8,128)(2,1)S(1)} %fusion.1), channel_id=1, source_target_pairs={{0,2},{2,4},{4,6},{6,8},{8,10},{10,12},{12,14},{14,16},{16,18},{18... | collective-permute-start | bytes 909320 | tf_op jit(solution)/shard_map/ppermute | solution.py:25
  13.7 2.0 %copy-start = (bf16[3,12,192,192]{3,2,1,0:T(8,128)(2,1)S(1)}, bf16[3,12,192,192]{3,2,1,0:T(8,128)(2,1)}, u32[]{:S(2)}) copy-start(bf16[3,12,192,192]{3,2,1,0:T(8,128)(2,1)} %hessian_ref.11) | copy-start | bytes 7962628
  15.7 11.3 %copy-start.3 = (f32[576,256]{1,0:T(8,128)S(1)}, f32[576,256]{1,0:T(8,128)}, u32[]{:S(2)}) copy-start(f32[576,256]{1,0:T(8,128)} %vectors_ref.3) | copy-start | bytes 1769476
  15.7 11.3 %copy-start.4 = (f32[2]{0:T(128)S(1)}, f32[2]{0:T(128)}, u32[]{:S(2)}) copy-start(f32[2]{0:T(128)} %bounds_ref.3) | copy-start | bytes 28
  27.0 8.7 %copy-start.1 = (bf16[3,12,192,192]{3,2,1,0:T(8,128)(2,1)S(1)}, bf16[3,12,192,192]{3,2,1,0:T(8,128)(2,1)}, u32[]{:S(2)}) copy-start(bf16[3,12,192,192]{3,2,1,0:T(8,128)(2,1)} %hessian_ref.11) | copy-start | bytes 7962628
  30.2 8.9 %collective-permute-start.3 = (bf16[576,256]{1,0:T(8,128)(2,1)S(1)}, bf16[576,256]{1,0:T(8,128)(2,1)S(1)}, u32[]{:S(2)}, u32[]{:S(2)}) collective-permute-start(bf16[576,256]{1,0:T(8,128)(2,1)S(1)} %get-tuple-element.6), channel_id=1, source_target_pairs={{0,30},{2,0},{4,2},{6,4},{8,6},{10,8},{12,10},{14,12},{16,14},{18,... | collective-permute-start | bytes 884744 | tf_op jit(solution)/shard_map/ppermute | solution.py:25
  33.1 11.5 %collective-permute-start.2 = (bf16[576,256]{1,0:T(8,128)(2,1)S(1)}, bf16[576,256]{1,0:T(8,128)(2,1)S(1)}, u32[]{:S(2)}, u32[]{:S(2)}) collective-permute-start(bf16[576,256]{1,0:T(8,128)(2,1)S(1)} %get-tuple-element.6), channel_id=1, source_target_pairs={{0,2},{2,4},{4,6},{6,8},{8,10},{10,12},{12,14},{14,16},{16,18},{18... | collective-permute-start | bytes 884744 | tf_op jit(solution)/shard_map/ppermute | solution.py:25
  48.0 9.4 %copy-start.2 = (bf16[3,12,192,192]{3,2,1,0:T(8,128)(2,1)S(1)}, bf16[3,12,192,192]{3,2,1,0:T(8,128)(2,1)}, u32[]{:S(2)}) copy-start(bf16[3,12,192,192]{3,2,1,0:T(8,128)(2,1)} %hessian_ref.11) | copy-start | bytes 7962628
  51.3 9.6 %collective-permute-start.5 = (bf16[576,256]{1,0:T(8,128)(2,1)S(1)}, bf16[576,256]{1,0:T(8,128)(2,1)S(1)}, u32[]{:S(2)}, u32[]{:S(2)}) collective-permute-start(bf16[576,256]{1,0:T(8,128)(2,1)S(1)} %get-tuple-element.8), channel_id=1, source_target_pairs={{0,30},{2,0},{4,2},{6,4},{8,6},{10,8},{12,10},{14,12},{16,14},{18,... | collective-permute-start | bytes 884744 | tf_op jit(solution)/shard_map/ppermute | solution.py:25
  54.9 11.9 %collective-permute-start.4 = (bf16[576,256]{1,0:T(8,128)(2,1)S(1)}, bf16[576,256]{1,0:T(8,128)(2,1)S(1)}, u32[]{:S(2)}, u32[]{:S(2)}) collective-permute-start(bf16[576,256]{1,0:T(8,128)(2,1)S(1)} %get-tuple-element.8), channel_id=1, source_target_pairs={{0,2},{2,4},{4,6},{6,8},{8,10},{10,12},{12,14},{14,16},{16,18},{18... | collective-permute-start | bytes 884744 | tf_op jit(solution)/shard_map/ppermute | solution.py:25

commit v3 on v2

--- a/solution.py
+++ b/solution.py
@@ -13,7 +13,6 @@
 NN = (((1,), (0,)), ((), ()))
 NT = (((1,), (1,)), ((), ()))
 TN = (((0,), (0,)), ((), ()))
-VMEM_LIMIT = 48 * 1024 * 1024
 GROUP = 8
 TILE = 128
 LIST_ROWS = 16
@@ -29,13 +28,13 @@
     return lax.dot_general(left, right, dims, precision=EXACT, preferred_element_type=jnp.float32)
 
 
-def kernel_call(body, out_shape, in_specs, flops, bytes_accessed):
+def kernel_call(body, out_shape, in_specs, flops, bytes_accessed, vmem=20):
     return pl.pallas_call(
         body,
         out_shape=out_shape,
         in_specs=in_specs,
         out_specs=jax.tree.map(lambda _: VMEM, out_shape),
-        compiler_params=pltpu.CompilerParams(vmem_limit_bytes=VMEM_LIMIT),
+        compiler_params=pltpu.CompilerParams(vmem_limit_bytes=vmem * 1024 * 1024),
         cost_estimate=pl.CostEstimate(flops=flops, bytes_accessed=bytes_accessed, transcendentals=0),
     )
 
@@ -67,34 +66,31 @@
     out_ref[...] = accumulate(slots_ref, hessian_ref, 0, region_ref, None)
 
 
-def halo_total(slots_ref, hessian_ref, lower_ref, upper_ref, local_ref):
-    size = hessian_ref.shape[2]
-    halo = lower_ref.shape[0] * (lower_ref.shape[1] // size)
-    total = accumulate(slots_ref, hessian_ref, 0, lower_ref, local_ref[...])
-    return accumulate(slots_ref, hessian_ref, halo, upper_ref, total)
-
-
-def first_body(slots_ref, bounds_ref, hessian_ref, lower_ref, upper_ref, local_ref, vectors_ref, one_ref, cast_ref):
+def lower_body(slots_ref, hessian_ref, lower_ref, local_ref, out_ref):
+    out_ref[...] = accumulate(slots_ref, hessian_ref, 0, lower_ref, local_ref[...])
+
+
+def first_body(slots_ref, bounds_ref, hessian_ref, upper_ref, partial_ref, vectors_ref, one_ref, cast_ref):
     centre = 0.5 * (bounds_ref[0] + bounds_ref[1])
     half = 0.5 * (bounds_ref[1] - bounds_ref[0])
-    total = halo_total(slots_ref, hessian_ref, lower_ref, upper_ref, local_ref)
+    total = accumulate(slots_ref, hessian_ref, 0, upper_ref, partial_ref[...])
     one = (total - centre * vectors_ref[...]) / half
     one_ref[...] = one
     cast_ref[...] = one.astype(jnp.bfloat16)
 
 
-def second_body(slots_ref, bounds_ref, hessian_ref, lower_ref, upper_ref, local_ref, one_ref, vectors_ref, two_ref, cast_ref):
+def second_body(slots_ref, bounds_ref, hessian_ref, upper_ref, partial_ref, one_ref, vectors_ref, two_ref, cast_ref):
     centre = 0.5 * (bounds_ref[0] + bounds_ref[1])
     half = 0.5 * (bounds_ref[1] - bounds_ref[0])
-    total = halo_total(slots_ref, hessian_ref, lower_ref, upper_ref, local_ref)
+    total = accumulate(slots_ref, hessian_ref, 0, upper_ref, partial_ref[...])
     two = 2.0 * (total - centre * one_ref[...]) / half - vectors_ref[...]
     two_ref[...] = two
     cast_ref[...] = two.astype(jnp.bfloat16)
 
 
-def third_body(slots_ref, hessian_ref, lower_ref, upper_ref, local_ref, two_ref, sums_ref):
+def third_body(slots_ref, hessian_ref, upper_ref, partial_ref, two_ref, sums_ref):
     modes = two_ref.shape[1]
-    image = halo_total(slots_ref, hessian_ref, lower_ref, upper_ref, local_ref)
+    image = accumulate(slots_ref, hessian_ref, 0, upper_ref, partial_ref[...])
     two = two_ref[...]
     sums_ref[:modes, :] = exact_dot(two, two, TN)
     sums_ref[modes:, :] = exact_dot(two, image, TN)
@@ -207,11 +203,7 @@
         pieces = value.reshape(count, value.shape[0] // count, width)
         value = jnp.sum(lax.all_to_all(pieces, axis, 0, 0, axis_index_groups=groups), axis=0)
     for axis, groups, count in reversed(stages):
-        if groups is None:
-            value = lax.all_gather(value, axis, axis=0, tiled=True)
-        else:
-            every = jnp.broadcast_to(value[None], (count,) + value.shape)
-            value = lax.all_to_all(every, axis, 0, 0, axis_index_groups=groups).reshape(-1, width)
+        value = lax.all_gather(value, axis, axis=0, tiled=True, axis_index_groups=groups)
     return value
 
 
@@ -251,10 +243,6 @@
         upper_order = first_upper[rows, :halo_blocks].astype(jnp.int32)
     else:
         lower_order = upper_order = jnp.arange(halo_blocks, dtype=jnp.int32)
-    near_places = jnp.arange(region_blocks, dtype=jnp.int32)
-    lower_places = region_blocks + lower_order
-    upper_places = region_blocks + halo_blocks + upper_order
-
     order = jnp.arange(stored, dtype=jnp.int32)[None, None, :]
     live = order < live_blocks[:, None, None]
 
@@ -262,9 +250,14 @@
         meets = place[:, None, :] == first_place + jnp.arange(count, dtype=jnp.int32)[None, :, None]
         return jnp.max(jnp.where(meets & live, order, -1), axis=2)
 
+    def halo_slots(first_place, listed_order):
+        inside = (block_cols >= first_place) & (block_cols < first_place + halo_blocks)
+        place = listed_order[jnp.clip(block_cols - first_place, 0, halo_blocks - 1)]
+        return slots_of(jnp.where(inside, place, -1), 0, halo_blocks)
+
     near_slots = slots_of(block_cols, 0, region_blocks)
-    places = jnp.concatenate([near_places, lower_places, upper_places])
-    far_slots = slots_of(places[block_cols], region_blocks, 2 * halo_blocks)
+    lower_slots = halo_slots(region_blocks, lower_order)
+    upper_slots = halo_slots(region_blocks + halo_blocks, upper_order)
 
     wide = jax.ShapeDtypeStruct((rows, modes), jnp.float32)
     narrow = jax.ShapeDtypeStruct((rows, modes), jnp.bfloat16)
@@ -277,9 +270,11 @@
 
     def step(body, outs, region, lower, upper, scalars, extra):
         partial = local_part(region)
-        specs = [SMEM] * (1 + len(scalars)) + [VMEM] * (4 + len(extra))
-        call = kernel_call(body, outs, specs, work * 2 * halo_blocks, traffic)
-        return call(far_slots, *scalars, hessian, gather(lower), gather(upper), partial, *extra)
+        call = kernel_call(lower_body, wide, [SMEM] + [VMEM] * 3, work * halo_blocks, traffic)
+        partial = call(lower_slots, hessian, gather(lower), partial)
+        specs = [SMEM] * (1 + len(scalars)) + [VMEM] * (3 + len(extra))
+        call = kernel_call(body, outs, specs, work * halo_blocks, traffic)
+        return call(upper_slots, *scalars, hessian, gather(upper), partial, *extra)
 
     def later(body, outs, operand, scalars, extra):
         region = lax.all_gather(operand, "split", axis=0)

time: 131 us -> 140 us (1.069)
  blocking collectives: 69.2 us -> 74.5 us
  other arithmetic: 4.42 us -> 8.15 us
  starting transfers between devices: 12.6 us -> 16.3 us
  Pallas kernels: 27.5 us -> 24.1 us
    all_gather x1 -> x3, blocking collectives: 7.76 us -> 27 us  [summed(): lax.all_gather(value, axis, axis=0, tiled=True, axis_index_groups=groups)]
    all_to_all x2 -> x0, blocking collectives: 13.9 us -> none  [summed(): lax.all_to_all(every, axis, 0, 0, axis_index_groups=groups)]
    ppermute x6, starting transfers between devices: 12.6 us -> 16.3 us  [shifted(): return lax.ppermute(value, axis, pairs)]
    pallas_call x3 -> x6, Pallas kernels: 11.8 us -> 8.38 us  [the longest x3 4.85 us: step(): return call(upper_slots, *scalars, hessian, gather(upper), partial, *extra)]
    all_gather x1, blocking collectives: 2.81 us -> 4.67 us  [local(): first_region = lax.all_gather(first, 'split', axis=0)]
    gather x2 -> x4, local copies, waits for them, and re-layouts: 0.86 us -> 2.42 us  [halo_slots(): place = listed_order[jnp.clip(block_cols - first_place, 0, halo_blocks - 1)]]
    all_gather x6, blocking collectives: 18.5 us -> 17.1 us  [gather(): return lax.all_gather(value, 'split', axis=0)]
  transfers between devices with their start and end apart: 6 -> 6, of which waited for: 5 -> 3; matrix products, arithmetic and copies ran while one was open for 2% -> 4% of each run, Pallas kernels for 3% -> 3%
where the time goes in v3:
time: 140 us; the launch traced here: 139 us
  blocking collectives  74.5 us (53%)
  Pallas kernels  24.1 us (17%)
  starting transfers between devices  16.3 us (12%)
  waiting for transfers between devices  11.6 us (8%)
  other arithmetic  8.15 us (6%)
  local copies, waits for them, and re-layouts  3.68 us (3%)
    all_gather x3, blocking collectives, summed(): lax.all_gather(value, axis, axis=0, tiled=True, axis_index_groups=groups)  27 us
    all_to_all x3, blocking collectives, summed(): lax.all_to_all(pieces, axis, 0, 0, axis_index_groups=groups)  20.2 us
    all_gather x6, blocking collectives, gather(): return lax.all_gather(value, 'split', axis=0)  17.1 us
    ppermute x6, starting transfers between devices, shifted(): return lax.ppermute(value, axis, pairs)  16.3 us
    pallas_call x1, Pallas kernels, local(): return call(sums, two)  12.2 us
    ppermute x6, waiting for transfers between devices, shifted(): return lax.ppermute(value, axis, pairs)  11.6 us
    all_gather x2, blocking collectives, later(): region = lax.all_gather(operand, 'split', axis=0)  5.55 us
    pallas_call x3, Pallas kernels, step(): return call(upper_slots, *scalars, hessian, gather(upper), partial, *extra)  4.85 us
  transfers between devices with their start and end apart: 6, of which 3 were waited for; matrix products, arithmetic and copies ran while one was open for 4% of the time, Pallas kernels for 3%

profile of v3, /device:TPU:1, one launch (start us, length us, event | category | flops | bytes accessed | tf_op | source)
XLA Modules:
  0.0 139.1 jit_solution(13050339227772839643)
XLA Ops:
  0.7 1.2 convert_element_type.16
  3.3 6.0 %collective-permute-start = (bf16[592,256]{1,0:T(8,128)(2,1)}, bf16[592,256]{1,0:T(8,128)(2,1)}, u32[]{:S(2)}, u32[]{:S(2)}) collective-permute-start(bf16[592,256]{1,0:T(8,128)(2,1)} %fusion.1), channel_id=1, source_target_pairs={{0,30},{2,0},{4,2},{6,4},{8,6},{10,8},{12,10},{14,12},{16,14},{18,... | collective-permute-start | bytes 909320 | tf_op jit(solution)/shard_map/ppermute | solution.py:24
  9.4 4.7 %all-gather.2 = bf16[1184,256]{1,0:T(8,128)(2,1)} all-gather(bf16[592,256]{1,0:T(8,128)(2,1)} %fusion.1), channel_id=4, replica_groups=mesh['region'=16,'split'=2] {'split'}, dimensions={0}, use_global_device_ids=true | all-gather | bytes 909312 | tf_op jit(solution)/shard_map/all_gather | solution.py:239
  15.5 1.2 iota_compare_fusion.4
  19.0 2.0 %collective-permute-done.1 = bf16[592,256]{1,0:T(8,128)(2,1)} collective-permute-done((bf16[592,256]{1,0:T(8,128)(2,1)}, bf16[592,256]{1,0:T(8,128)(2,1)}, u32[]{:S(2)}, u32[]{:S(2)}) %collective-permute-start.1) | collective-permute-done | bytes 303136 | tf_op jit(solution)/shard_map/ppermute | solution.py:24
  25.2 1.2 shard_map.77.local_ref
  26.4 4.1 %all-gather.1 = bf16[1184,256]{1,0:T(8,128)(2,1)S(1)} all-gather(bf16[592,256]{1,0:T(8,128)(2,1)} %collective-permute-done.1), channel_id=3, replica_groups=mesh['region'=16,'split'=2] {'split'}, dimensions={0}, use_global_device_ids=true | all-gather | bytes 909312 | tf_op jit(solution)/shard_map/all_gather | solution.py:232
  30.5 1.2 shard_map.78.partial_ref
  31.6 2.5 %all-gather = bf16[1184,256]{1,0:T(8,128)(2,1)S(1)} all-gather(bf16[592,256]{1,0:T(8,128)(2,1)} %collective-permute-done), channel_id=2, replica_groups=mesh['region'=16,'split'=2] {'split'}, dimensions={0}, use_global_device_ids=true | all-gather | bytes 909312 | tf_op jit(solution)/shard_map/all_gather | solution.py:232
  34.1 1.2 shard_map.79
  36.1 4.3 %collective-permute-start.2 = (bf16[576,256]{1,0:T(8,128)(2,1)S(1)}, bf16[576,256]{1,0:T(8,128)(2,1)S(1)}, u32[]{:S(2)}, u32[]{:S(2)}) collective-permute-start(bf16[576,256]{1,0:T(8,128)(2,1)S(1)} %get-tuple-element.6), channel_id=1, source_target_pairs={{0,30},{2,0},{4,2},{6,4},{8,6},{10,8},{12,10},{14,12},{16,14},{18,... | collective-permute-start | bytes 884744 | tf_op jit(solution)/shard_map/ppermute | solution.py:24
  40.4 2.8 %all-gather.5 = bf16[1152,256]{1,0:T(8,128)(2,1)S(1)} all-gather(bf16[576,256]{1,0:T(8,128)(2,1)S(1)} %get-tuple-element.6), channel_id=7, replica_groups=mesh['region'=16,'split'=2] {'split'}, dimensions={0}, use_global_device_ids=true | all-gather | bytes 884736 | tf_op jit(solution)/shard_map/all_gather | solution.py:280
  44.4 4.1 %collective-permute-done.3 = bf16[576,256]{1,0:T(8,128)(2,1)S(1)} collective-permute-done((bf16[576,256]{1,0:T(8,128)(2,1)S(1)}, bf16[576,256]{1,0:T(8,128)(2,1)S(1)}, u32[]{:S(2)}, u32[]{:S(2)}) %collective-permute-start.3) | collective-permute-done | bytes 294944 | tf_op jit(solution)/shard_map/ppermute | solution.py:24
  48.4 3.0 %all-gather.4 = bf16[1152,256]{1,0:T(8,128)(2,1)S(1)} all-gather(bf16[576,256]{1,0:T(8,128)(2,1)S(1)} %collective-permute-done.3), channel_id=6, replica_groups=mesh['region'=16,'split'=2] {'split'}, dimensions={0}, use_global_device_ids=true | all-gather | bytes 884736 | tf_op jit(solution)/shard_map/all_gather | solution.py:232
  51.5 1.2 shard_map.81.partial_ref
  52.7 2.2 %all-gather.3 = bf16[1152,256]{1,0:T(8,128)(2,1)S(1)} all-gather(bf16[576,256]{1,0:T(8,128)(2,1)S(1)} %collective-permute-done.2), channel_id=5, replica_groups=mesh['region'=16,'split'=2] {'split'}, dimensions={0}, use_global_device_ids=true | all-gather | bytes 884736 | tf_op jit(solution)/shard_map/all_gather | solution.py:232
  54.9 1.2 shard_map.82
  56.1 2.3 %collective-permute-start.5 = (bf16[576,256]{1,0:T(8,128)(2,1)S(1)}, bf16[576,256]{1,0:T(8,128)(2,1)S(1)}, u32[]{:S(2)}, u32[]{:S(2)}) collective-permute-start(bf16[576,256]{1,0:T(8,128)(2,1)S(1)} %get-tuple-element.8), channel_id=1, source_target_pairs={{0,2},{2,4},{4,6},{6,8},{8,10},{10,12},{12,14},{14,16},{16,18},{18... | collective-permute-start | bytes 884744 | tf_op jit(solution)/shard_map/ppermute | solution.py:24
  58.4 2.9 %collective-permute-start.4 = (bf16[576,256]{1,0:T(8,128)(2,1)S(1)}, bf16[576,256]{1,0:T(8,128)(2,1)S(1)}, u32[]{:S(2)}, u32[]{:S(2)}) collective-permute-start(bf16[576,256]{1,0:T(8,128)(2,1)S(1)} %get-tuple-element.8), channel_id=1, source_target_pairs={{0,30},{2,0},{4,2},{6,4},{8,6},{10,8},{12,10},{14,12},{16,14},{18,... | collective-permute-start | bytes 884744 | tf_op jit(solution)/shard_map/ppermute | solution.py:24
  61.2 2.8 %all-gather.8 = bf16[1152,256]{1,0:T(8,128)(2,1)S(1)} all-gather(bf16[576,256]{1,0:T(8,128)(2,1)S(1)} %get-tuple-element.8), channel_id=10, replica_groups=mesh['region'=16,'split'=2] {'split'}, dimensions={0}, use_global_device_ids=true | all-gather | bytes 884736 | tf_op jit(solution)/shard_map/all_gather | solution.py:280
  64.0 1.2 shard_map.83.local_ref
  65.2 5.5 %collective-permute-done.5 = bf16[576,256]{1,0:T(8,128)(2,1)S(1)} collective-permute-done((bf16[576,256]{1,0:T(8,128)(2,1)S(1)}, bf16[576,256]{1,0:T(8,128)(2,1)S(1)}, u32[]{:S(2)}, u32[]{:S(2)}) %collective-permute-start.5) | collective-permute-done | bytes 294944 | tf_op jit(solution)/shard_map/ppermute | solution.py:24
  70.7 3.0 %all-gather.7 = bf16[1152,256]{1,0:T(8,128)(2,1)S(1)} all-gather(bf16[576,256]{1,0:T(8,128)(2,1)S(1)} %collective-permute-done.5), channel_id=9, replica_groups=mesh['region'=16,'split'=2] {'split'}, dimensions={0}, use_global_device_ids=true | all-gather | bytes 884736 | tf_op jit(solution)/shard_map/all_gather | solution.py:232
  75.0 2.2 %all-gather.6 = bf16[1152,256]{1,0:T(8,128)(2,1)S(1)} all-gather(bf16[576,256]{1,0:T(8,128)(2,1)S(1)} %collective-permute-done.4), channel_id=8, replica_groups=mesh['region'=16,'split'=2] {'split'}, dimensions={0}, use_global_device_ids=true | all-gather | bytes 884736 | tf_op jit(solution)/shard_map/all_gather | solution.py:232
  77.2 2.5 %shard_map.85 = f32[512,256]{1,0:T(8,128)S(1)} custom-call(s32[3,6]{1,0:T(4,128)S(1)} %get-tuple-element.12.slots_ref, bf16[3,12,192,192]{3,2,1,0:T(8,128)(2,1)S(1)} %copy-done, bf16[2,576,256]{2,1,0:T(8,128)(2,1)S(1)} %bitcast.30, f32[576,256]{1,0:T(8,128)S(1)} %shard_map.84.partial_ref, f32[576,256]{1,0:T(8,128)S(1)} %get-tuple-element.9.two_ref), custom_call_target="tpu_custom_call" | custom-call | flops 339738624 | bytes 4423680 | tf_op jit(solution)/shard_map/pallas_call | solution.py:277
  79.7 4.3 %all_to_all.15 = f32[2,256,256]{2,1,0:T(8,128)S(1)} all-to-all(f32[2,256,256]{2,1,0:T(8,128)S(1)} %bitcast.33), channel_id=1, replica_groups=mesh['region'=16,'split'=2] {'split'}, dimensions={0} | all-to-all | bytes 1048576 | tf_op jit(solution)/shard_map/all_to_all | solution.py:204
  84.0 7.9 %all_to_all.16 = f32[4,64,256]{2,1,0:T(8,128)S(1)} all-to-all(f32[4,64,256]{2,1,0:T(8,128)S(1)} %bitcast.34), channel_id=1, replica_groups={{0,2,4,6},{8,10,12,14},{16,18,20,22},{24,26,28,30},{1,3,5,7},{9,11,13,1..., dimensions={0} | all-to-all | bytes 524288 | tf_op jit(solution)/shard_map/all_to_all | solution.py:204
  91.9 8.0 %all_to_all.17 = f32[4,16,256]{2,1,0:T(8,128)S(1)} all-to-all(f32[4,16,256]{2,1,0:T(8,128)S(1)} %bitcast.35), channel_id=1, replica_groups={{0,8,16,24},{2,10,18,26},{4,12,20,28},{6,14,22,30},{1,9,17,25},{3,11,19..., dimensions={0} | all-to-all | bytes 131072 | tf_op jit(solution)/shard_map/all_to_all | solution.py:204
  99.9 10.3 %all_gather.81 = f32[64,256]{1,0:T(8,128)S(1)} all-gather(f32[16,256]{1,0:T(8,128)S(1)} %reduce_sum.29), channel_id=1, replica_groups={{0,8,16,24},{2,10,18,26},{4,12,20,28},{6,14,22,30},{1,9,17,25},{3,11,19..., dimensions={0}, use_global_device_ids=true | all-gather | bytes 81920 | tf_op jit(solution)/shard_map/all_gather | solution.py:206
  110.2 7.4 %all_gather.82 = f32[256,256]{1,0:T(8,128)S(1)} all-gather(f32[64,256]{1,0:T(8,128)S(1)} %all_gather.81), channel_id=1, replica_groups={{0,2,4,6},{8,10,12,14},{16,18,20,22},{24,26,28,30},{1,3,5,7},{9,11,13,1..., dimensions={0}, use_global_device_ids=true | all-gather | bytes 327680 | tf_op jit(solution)/shard_map/all_gather | solution.py:206
  117.6 9.3 %all_gather.83.sums_ref = f32[512,256]{1,0:T(8,128)S(1)} all-gather(f32[256,256]{1,0:T(8,128)S(1)} %all_gather.82), channel_id=1, replica_groups=mesh['region'=16,'split'=2] {'split'}, dimensions={0}, use_global_device_ids=true | all-gather | bytes 786432 | tf_op jit(solution)/shard_map/all_gather | solution.py:206
  126.9 12.2 %shard_map.86 = (f32[576,256]{1,0:T(8,128)}, f32[256,256]{1,0:T(8,128)}) custom-call(f32[512,256]{1,0:T(8,128)S(1)} %all_gather.83.sums_ref, f32[576,256]{1,0:T(8,128)S(1)} %copy-done.4), custom_call_target="tpu_custom_call" | custom-call | flops 301989888 | bytes 4423680 | tf_op jit(solution)/shard_map/pallas_call | solution.py:291
  (39 shorter events, 12.5 us)
Async XLA Ops:
  0.6 21.9 %copy-start.6 = (s32[3,12]{1,0:T(4,128)S(1)}, s32[3,12]{1,0:T(4,128)}, u32[]{:S(2)}) copy-start(s32[3,12]{1,0:T(4,128)} %param.8) | copy-start | bytes 436
  0.6 23.5 %copy-start = (bf16[3,12,192,192]{3,2,1,0:T(8,128)(2,1)S(1)}, bf16[3,12,192,192]{3,2,1,0:T(8,128)(2,1)}, u32[]{:S(2)}) copy-start(bf16[3,12,192,192]{3,2,1,0:T(8,128)(2,1)} %hessian_ref.17) | copy-start | bytes 7962628
  3.3 13.4 %collective-permute-start = (bf16[592,256]{1,0:T(8,128)(2,1)}, bf16[592,256]{1,0:T(8,128)(2,1)}, u32[]{:S(2)}, u32[]{:S(2)}) collective-permute-start(bf16[592,256]{1,0:T(8,128)(2,1)} %fusion.1), channel_id=1, source_target_pairs={{0,30},{2,0},{4,2},{6,4},{8,6},{10,8},{12,10},{14,12},{16,14},{18,... | collective-permute-start | bytes 909320 | tf_op jit(solution)/shard_map/ppermute | solution.py:24
  9.4 11.6 %collective-permute-start.1 = (bf16[592,256]{1,0:T(8,128)(2,1)}, bf16[592,256]{1,0:T(8,128)(2,1)}, u32[]{:S(2)}, u32[]{:S(2)}) collective-permute-start(bf16[592,256]{1,0:T(8,128)(2,1)} %fusion.1), channel_id=1, source_target_pairs={{0,2},{2,4},{4,6},{6,8},{8,10},{10,12},{12,14},{14,16},{16,18},{18... | collective-permute-start | bytes 909320 | tf_op jit(solution)/shard_map/ppermute | solution.py:24
  24.1 1.1 copy-start.2
  26.4 7.7 %copy-start.1 = (f32[576,256]{1,0:T(8,128)S(1)}, f32[576,256]{1,0:T(8,128)}, u32[]{:S(2)}) copy-start(f32[576,256]{1,0:T(8,128)} %vectors_ref.3) | copy-start | bytes 1769476
  26.4 7.7 %copy-start.5 = (f32[2]{0:T(128)S(1)}, f32[2]{0:T(128)}, u32[]{:S(2)}) copy-start(f32[2]{0:T(128)} %bounds_ref.3) | copy-start | bytes 28
  35.3 13.1 %collective-permute-start.3 = (bf16[576,256]{1,0:T(8,128)(2,1)S(1)}, bf16[576,256]{1,0:T(8,128)(2,1)S(1)}, u32[]{:S(2)}, u32[]{:S(2)}) collective-permute-start(bf16[576,256]{1,0:T(8,128)(2,1)S(1)} %get-tuple-element.6), channel_id=1, source_target_pairs={{0,2},{2,4},{4,6},{6,8},{8,10},{10,12},{12,14},{14,16},{16,18},{18... | collective-permute-start | bytes 884744 | tf_op jit(solution)/shard_map/ppermute | solution.py:24
  36.1 16.6 %collective-permute-start.2 = (bf16[576,256]{1,0:T(8,128)(2,1)S(1)}, bf16[576,256]{1,0:T(8,128)(2,1)S(1)}, u32[]{:S(2)}, u32[]{:S(2)}) collective-permute-start(bf16[576,256]{1,0:T(8,128)(2,1)S(1)} %get-tuple-element.6), channel_id=1, source_target_pairs={{0,30},{2,0},{4,2},{6,4},{8,6},{10,8},{12,10},{14,12},{16,14},{18,... | collective-permute-start | bytes 884744 | tf_op jit(solution)/shard_map/ppermute | solution.py:24
  56.1 21.1 %copy-start.3 = (f32[576,256]{1,0:T(8,128)}, f32[576,256]{1,0:T(8,128)S(1)}, u32[]{:S(2)}) copy-start(f32[576,256]{1,0:T(8,128)S(1)} %get-tuple-element.9.two_ref) | copy-start | bytes 1769476
  56.1 14.6 %collective-permute-start.5 = (bf16[576,256]{1,0:T(8,128)(2,1)S(1)}, bf16[576,256]{1,0:T(8,128)(2,1)S(1)}, u32[]{:S(2)}, u32[]{:S(2)}) collective-permute-start(bf16[576,256]{1,0:T(8,128)(2,1)S(1)} %get-tuple-element.8), channel_id=1, source_target_pairs={{0,2},{2,4},{4,6},{6,8},{8,10},{10,12},{12,14},{14,16},{16,18},{18... | collective-permute-start | bytes 884744 | tf_op jit(solution)/shard_map/ppermute | solution.py:24
  58.4 16.6 %collective-permute-start.4 = (bf16[576,256]{1,0:T(8,128)(2,1)S(1)}, bf16[576,256]{1,0:T(8,128)(2,1)S(1)}, u32[]{:S(2)}, u32[]{:S(2)}) collective-permute-start(bf16[576,256]{1,0:T(8,128)(2,1)S(1)} %get-tuple-element.8), channel_id=1, source_target_pairs={{0,30},{2,0},{4,2},{6,4},{8,6},{10,8},{12,10},{14,12},{16,14},{18,... | collective-permute-start | bytes 884744 | tf_op jit(solution)/shard_map/ppermute | solution.py:24
  79.7 47.3 %copy-start.4 = (f32[576,256]{1,0:T(8,128)S(1)}, f32[576,256]{1,0:T(8,128)}, u32[]{:S(2)}) copy-start(f32[576,256]{1,0:T(8,128)} %copy-done.3) | copy-start | bytes 1769476

commit v4 on v3

v4 whole, which is shorter than its diff:
```python
import functools
import jax
import jax.numpy as jnp
from jax import lax
from jax.experimental import pallas as pl
from jax.experimental.pallas import tpu as pltpu
from jax.sharding import PartitionSpec as P

AXES = ("region", "split")
VMEM = pl.BlockSpec(memory_space=pltpu.VMEM)
SMEM = pl.BlockSpec(memory_space=pltpu.SMEM)
EXACT = lax.Precision.HIGHEST
NN = (((1,), (0,)), ((), ()))
NT = (((1,), (1,)), ((), ()))
TN = (((0,), (0,)), ((), ()))
GROUP = 8
TILE = 128
VMEM_LIMIT = 20 * 1024 * 1024
LIST_ROWS = 16
PIECES = 4


def shifted(value, axis, steps):
    count = lax.axis_size(axis)
    pairs = [(source, (source + steps) % count) for source in range(count)]
    return lax.ppermute(value, axis, pairs)


def exact_dot(left, right, dims=NN):
    return lax.dot_general(left, right, dims, precision=EXACT, preferred_element_type=jnp.float32)


def kernel_call(body, out_shape, in_specs, flops, bytes_accessed, slots=None):
    return pl.pallas_call(
        body,
        out_shape=out_shape,
        in_specs=in_specs,
        out_specs=jax.tree.map(lambda _: VMEM, out_shape),
        scratch_shapes=[] if slots is None else [pltpu.SMEM(slots, jnp.int32)],
        compiler_params=pltpu.CompilerParams(vmem_limit_bytes=VMEM_LIMIT),
        cost_estimate=pl.CostEstimate(flops=flops, bytes_accessed=bytes_accessed, transcendentals=0),
    )


def fill_slots(slots_ref, cols_ref, live_ref, first, place_of):
    rows, stored = cols_ref.shape
    count = slots_ref.shape[1]
    for row in range(rows):
        for index in range(count):
            slots_ref[row, index] = -1
        for at in range(stored):
            name = cols_ref[row, at] - first

            @pl.when((name >= 0) & (name < count) & (at < live_ref[row]))
            def _():
                slots_ref[row, place_of(name)] = at


def accumulate(slots_ref, hessian_ref, operand_ref, total):
    rows, _, size, _ = hessian_ref.shape
    shards, shard_rows, _ = operand_ref.shape
    each = shard_rows // size
    for index in range(shards * each):
        start = index % each * size
        block = operand_ref[index // each, start : start + size, :]
        parts = []
        for row in range(rows):
            slot = slots_ref[row, index]
            live = jnp.where(slot >= 0, 1.0, 0.0).astype(jnp.float32)
            stored = hessian_ref[row, jnp.maximum(slot, 0)]
            parts.append(stored * jnp.broadcast_to(live, (size, size)).astype(jnp.bfloat16))
        term = jnp.dot(jnp.concatenate(parts, 0), block, preferred_element_type=jnp.float32)
        total = term if total is None else total + term
    return total


def local_body(cols_ref, live_ref, hessian_ref, region_ref, out_ref, slots_ref):
    fill_slots(slots_ref, cols_ref, live_ref, 0, lambda name: name)
    out_ref[...] = accumulate(slots_ref, hessian_ref, region_ref, None)


def lower_body(first, cols_ref, live_ref, list_ref, hessian_ref, lower_ref, local_ref, out_ref, slots_ref):
    fill_slots(slots_ref, cols_ref, live_ref, first, lambda name: list_ref[name])
    out_ref[...] = accumulate(slots_ref, hessian_ref, lower_ref, local_ref[...])


def upper_total(first, cols_ref, live_ref, list_ref, hessian_ref, upper_ref, partial_ref, slots_ref):
    fill_slots(slots_ref, cols_ref, live_ref, first, lambda name: list_ref[name])
    return accumulate(slots_ref, hessian_ref, upper_ref, partial_ref[...])


def interval(bounds_ref):
    return 0.5 * (bounds_ref[0] + bounds_ref[1]), 0.5 * (bounds_ref[1] - bounds_ref[0])


def first_body(first, cols_ref, live_ref, list_ref, bounds_ref, hessian_ref, upper_ref, partial_ref, vectors_ref, one_ref, cast_ref, slots_ref):
    centre, half = interval(bounds_ref)
    total = upper_total(first, cols_ref, live_ref, list_ref, hessian_ref, upper_ref, partial_ref, slots_ref)
    one = (total - centre * vectors_ref[...]) / half
    one_ref[...] = one
    cast_ref[...] = one.astype(jnp.bfloat16)


def second_body(first, cols_ref, live_ref, list_ref, bounds_ref, hessian_ref, upper_ref, partial_ref, one_ref, vectors_ref, two_ref, cast_ref, slots_ref):
    centre, half = interval(bounds_ref)
    total = upper_total(first, cols_ref, live_ref, list_ref, hessian_ref, upper_ref, partial_ref, slots_ref)
    two = 2.0 * (total - centre * one_ref[...]) / half - vectors_ref[...]
    two_ref[...] = two
    cast_ref[...] = two.astype(jnp.bfloat16)


def place_rows(number_ref, piece, rows):
    return pl.ds(pl.multiple_of((piece ^ number_ref[0]) * rows, GROUP), rows)


def scatter_pieces(number_ref, out_ref, value):
    rows = out_ref.shape[0] // PIECES
    for piece in range(PIECES):
        out_ref[place_rows(number_ref, piece, rows), :] = value[piece * rows : (piece + 1) * rows, :]


def ordered_pieces(number_ref, in_ref):
    rows = in_ref.shape[0] // PIECES
    return jnp.concatenate([in_ref[place_rows(number_ref, piece, rows), :] for piece in range(PIECES)], 0)


def lower_tiles(count):
    return [(row, col) for row in range(count) for col in range(row + 1)]


def gram_body(number_ref, two_ref, out_ref):
    two = two_ref[...]
    cols = [two[:, at * TILE : (at + 1) * TILE] for at in range(two.shape[1] // TILE)]
    tiles = [exact_dot(cols[row], cols[col], TN) for row, col in lower_tiles(len(cols))]
    scatter_pieces(number_ref, out_ref, jnp.concatenate(tiles, 0))


def third_body(first, cols_ref, live_ref, list_ref, number_ref, hessian_ref, upper_ref, partial_ref, two_ref, out_ref, slots_ref):
    image = upper_total(first, cols_ref, live_ref, list_ref, hessian_ref, upper_ref, partial_ref, slots_ref)
    scatter_pieces(number_ref, out_ref, exact_dot(two_ref[...], image, TN))


def over_lanes(value, lane):
    return jnp.broadcast_to(value[:, lane : lane + 1], value.shape)


def over_rows(value, row):
    return jnp.broadcast_to(value[row : row + 1, :], value.shape)


def tile_inverse(tile):
    count = tile.shape[0] // GROUP
    rows = [tile[index * GROUP : (index + 1) * GROUP, :] for index in range(count)]
    sub = lax.broadcasted_iota(jnp.int32, rows[0].shape, 0)
    lane = lax.broadcasted_iota(jnp.int32, rows[0].shape, 1)
    done = []
    for step in range(count):
        start = step * GROUP
        pivot_cols = [over_lanes(rows[step], start + col) for col in range(GROUP)]
        factors = {
            below: [over_lanes(rows[below], start + col) for col in range(GROUP)]
            for below in range(step + 1, count)
        }
        inside = (lane >= start) & (lane < start + GROUP)
        forward = jnp.where(inside, jnp.where(lane - start == sub, 1.0, 0.0), rows[step])
        solved = forward
        for pivot in range(GROUP):
            here = sub == pivot
            value = over_rows(pivot_cols[pivot], pivot)
            inverse = 1.0 / value
            ratio = pivot_cols[pivot] * inverse
            row = over_rows(forward, pivot)
            forward = jnp.where(
                here, row * lax.rsqrt(value), jnp.where(sub > pivot, forward - ratio * row, forward)
            )
            solved = jnp.where(here, row * inverse, solved - ratio * row)
            for col in range(pivot + 1, GROUP):
                top = over_rows(pivot_cols[col], pivot)
                pivot_cols[col] = jnp.where(here, top * inverse, pivot_cols[col] - ratio * top)
        done.append(jnp.where(lane < start + GROUP, forward, 0.0))
        solved_rows = [over_rows(solved, pivot) for pivot in range(GROUP)]
        for below in range(step + 1, count):
            terms = [factors[below][col] * solved_rows[col] for col in range(GROUP)]
            while len(terms) > 1:
                terms = [terms[at] + terms[at + 1] for at in range(0, len(terms), 2)]
            rows[below] = jnp.where(inside, 0.0, rows[below]) - terms[0]
    return jnp.concatenate(done, 0)


def factor_inverse(tiles, count):
    rest = {at: tiles[index * TILE : (index + 1) * TILE] for index, at in enumerate(lower_tiles(count))}
    lower = {}
    inverse = {}
    for at in range(count):
        inverse[at, at] = tile_inverse(rest[at, at])
        for row in range(at + 1, count):
            lower[row, at] = exact_dot(rest[row, at], inverse[at, at], NT)
        for row in range(at + 1, count):
            for col in range(at + 1, row + 1):
                rest[row, col] = rest[row, col] - exact_dot(lower[row, at], lower[col, at], NT)
        for col in range(at):
            mixed = exact_dot(lower[at, col], inverse[col, col])
            for mid in range(col + 1, at):
                mixed = mixed + exact_dot(lower[at, mid], inverse[mid, col])
            inverse[at, col] = -exact_dot(inverse[at, at], mixed)
    zero = jnp.zeros((TILE, TILE), jnp.float32)
    return jnp.concatenate(
        [
            jnp.concatenate([inverse[row, col] if col <= row else zero for col in range(count)], 1)
            for row in range(count)
        ],
        0,
    )


def basis_body(total_rows, number_ref, gram_ref, two_ref, basis_ref, inverse_ref):
    tiles = ordered_pieces(number_ref, gram_ref) / total_rows
    inverse = factor_inverse(tiles, two_ref.shape[1] // TILE)
    inverse_ref[...] = inverse
    basis_ref[...] = exact_dot(two_ref[...], inverse, NT)


def projected_body(total_rows, number_ref, cross_ref, inverse_ref, projected_ref):
    cross = ordered_pieces(number_ref, cross_ref) / total_rows
    projected_ref[...] = exact_dot(exact_dot(inverse_ref[...], cross), inverse_ref[...], NT)


def partner_value(value, axis, bit):
    return lax.ppermute(value, axis, [(at, at ^ bit) for at in range(lax.axis_size(axis))])


def halving_bits():
    bits = []
    for axis in ("split", "region"):
        size = lax.axis_size(axis)
        bits.append([(axis, 1 << at) for at in range(size.bit_length() - 1)])
    halved = [bits[0][0], bits[1][0]]
    return halved, bits[1][1:] + bits[0][1:]


def device_number():
    halved, _ = halving_bits()
    number = 0
    for axis, bit in halved:
        number = number * 2 + (lax.axis_index(axis) // bit) % 2
    return number.astype(jnp.int32).reshape(1)


def summed(value):
    halved, doubled = halving_bits()
    for axis, bit in halved:
        half = value.shape[0] // 2
        value = value[:half] + partner_value(value[half:], axis, bit)
    for axis, bit in doubled:
        value = value + partner_value(value, axis, bit)
    for axis, bit in reversed(halved):
        value = jnp.concatenate([value, partner_value(value, axis, bit)], 0)
    return value


def local(vectors, hessian, block_cols, live_blocks, halo_lists, bounds):
    row_blocks, stored, size, _ = hessian.shape
    rows, modes = vectors.shape
    splits = lax.axis_size("split")
    region_blocks = row_blocks * splits
    halo_blocks = halo_lists.shape[2]
    whole = halo_blocks == region_blocks and region_blocks <= 256
    total_rows = rows * lax.axis_size(AXES)

    def halos(operand, region):
        if whole:
            return shifted(operand, "region", 1), shifted(operand, "region", -1)
        width = modes // splits
        start = lax.axis_index("split") * width
        blocks = region[:, :rows].reshape(region_blocks, size, modes)
        share = lambda listed: lax.dynamic_slice_in_dim(blocks[listed], start, width, 2).reshape(-1, width)
        lower = shifted(share(halo_lists[0, 1]), "region", 1)
        upper = shifted(share(halo_lists[0, 0]), "region", -1)
        return lower, upper

    def gather(value):
        if whole:
            return lax.all_gather(value, "split", axis=0)
        return lax.all_gather(value, "split", axis=1, tiled=True)[None]

    listed = jnp.pad(halo_lists[0], ((0, LIST_ROWS - 2), (0, modes - halo_blocks)))
    first = vectors.astype(jnp.bfloat16)
    if whole:
        first = jnp.concatenate([first, listed.astype(jnp.bfloat16)], 0)
    first_region = lax.all_gather(first, "split", axis=0)
    first_lower, first_upper = halos(first, first_region)
    if whole:
        lower_order = first_lower[rows + 1, :halo_blocks].astype(jnp.int32)
        upper_order = first_upper[rows, :halo_blocks].astype(jnp.int32)
    else:
        lower_order = upper_order = jnp.arange(halo_blocks, dtype=jnp.int32)
    wide = jax.ShapeDtypeStruct((rows, modes), jnp.float32)
    narrow = jax.ShapeDtypeStruct((rows, modes), jnp.bfloat16)
    square = jax.ShapeDtypeStruct((modes, modes), jnp.float32)
    tile_rows = len(lower_tiles(modes // TILE)) * TILE
    work = 2 * rows * size * modes
    square_work = 2 * rows * modes * modes
    traffic = hessian.size * 2 + 3 * rows * modes * 4
    number = device_number()
    halo_slots = (row_blocks, halo_blocks)
    upper_first = region_blocks + halo_blocks

    def step(body, outs, region, lower, upper, scalars, extra):
        slots = (row_blocks, region_blocks)
        call = kernel_call(local_body, wide, [SMEM] * 2 + [VMEM] * 2, work * region_blocks, traffic, slots)
        partial = call(block_cols, live_blocks, hessian, region)
        body_of = functools.partial(lower_body, region_blocks)
        call = kernel_call(body_of, wide, [SMEM] * 3 + [VMEM] * 3, work * halo_blocks, traffic, halo_slots)
        partial = call(block_cols, live_blocks, lower_order, hessian, gather(lower), partial)
        specs = [SMEM] * (3 + len(scalars)) + [VMEM] * (3 + len(extra))
        call = kernel_call(functools.partial(body, upper_first), outs, specs, work * halo_blocks, traffic, halo_slots)
        return call(block_cols, live_blocks, upper_order, *scalars, hessian, gather(upper), partial, *extra)

    def later(body, outs, operand, scalars, extra):
        region = lax.all_gather(operand, "split", axis=0)
        return step(body, outs, region, *halos(operand, region), scalars, extra)

    one, one_cast = step(first_body, (wide, narrow), first_region, first_lower, first_upper, (bounds,), (vectors,))
    two, two_cast = later(second_body, (wide, narrow), one_cast, (bounds,), (one, vectors))
    packed = jax.ShapeDtypeStruct((tile_rows, TILE), jnp.float32)
    gram = summed(kernel_call(gram_body, packed, [SMEM, VMEM], square_work, traffic)(number, two))
    cross = summed(later(third_body, square, two_cast, (number,), (two,)))
    body_of = functools.partial(basis_body, float(total_rows))
    call = kernel_call(body_of, (wide, square), [SMEM] + [VMEM] * 2, 160 * square_work, traffic)
    basis, inverse = call(number, gram, two)
    body_of = functools.partial(projected_body, float(total_rows))
    call = kernel_call(body_of, square, [SMEM] + [VMEM] * 2, 2 * square_work, traffic)
    return basis, call(number, cross, inverse)


def solution(mesh):
    placed = (
        P(("region", "split"), None),
        P(("region", "split"), None, None, None),
        P(("region", "split"), None),
        P(("region", "split")),
        P("region", None, None),
        P(),
    )
    return jax.shard_map(
        local,
        mesh=mesh,
        in_specs=placed,
        out_specs=(P(("region", "split"), None), P()),
        check_vma=False,
    )
```

time: 140 us -> 119 us (0.85)
  blocking collectives: 74.5 us -> 27.5 us
  starting transfers between devices: 16.3 us -> 40.8 us
  other arithmetic: 8.15 us -> 1.97 us
  Pallas kernels: 24.1 us -> 28.9 us
  waiting for transfers between devices: 11.6 us -> 14.5 us
    all_gather x3 -> x0, blocking collectives: 27 us -> none  [summed(): lax.all_gather(value, axis, axis=0, tiled=True, axis_index_groups=groups)]
    ppermute x0 -> x14, starting transfers between devices: none -> 24.4 us  [partner_value(): lax.ppermute(value, axis, [(at, at ^ bit) for at in range(lax.axis_size(a...]
    all_to_all x3 -> x0, blocking collectives: 20.2 us -> none  [summed(): lax.all_to_all(pieces, axis, 0, 0, axis_index_groups=groups)]
    ppermute x0 -> x14, waiting for transfers between devices: none -> 6.81 us  [partner_value(): lax.ppermute(value, axis, [(at, at ^ bit) for at in range(lax.axis_size(a...]
    pallas_call x10 -> x12, Pallas kernels: 24.1 us -> 28.9 us  [the longest x1 11.7 us: local(): basis, inverse = call(number, gram, two)]
    ppermute x6, waiting for transfers between devices: 11.6 us -> 7.65 us  [shifted(): return lax.ppermute(value, axis, pairs)]
    unnamed x14 -> x24, local copies, waits for them, and re-layouts: 1.1 us -> 4.2 us
    gather x4 -> x0, local copies, waits for them, and re-layouts: 2.42 us -> none  [halo_slots(): place = listed_order[jnp.clip(block_cols - first_place, 0, halo_blocks - 1)]]
  transfers between devices with their start and end apart: 6 -> 20, of which waited for: 3 -> 9; matrix products, arithmetic and copies ran while one was open for 4% -> 0% of each run, Pallas kernels for 3% -> 20%
where the time goes in v4:
time: 119 us
  starting transfers between devices  40.8 us (34%)
  Pallas kernels  28.9 us (24%)
  blocking collectives  27.5 us (23%)
  waiting for transfers between devices  14.5 us (12%)
  local copies, waits for them, and re-layouts  4.23 us (4%)
  other arithmetic  1.97 us (2%)
    ppermute x14, starting transfers between devices, partner_value(): lax.ppermute(value, axis, [(at, at ^ bit) for at in range(lax.axis_size(a...  24.4 us
    all_gather x6, blocking collectives, gather(): return lax.all_gather(value, 'split', axis=0)  19.4 us
    ppermute x6, starting transfers between devices, shifted(): return lax.ppermute(value, axis, pairs)  16.3 us
    pallas_call x1, Pallas kernels, local(): basis, inverse = call(number, gram, two)  11.7 us
    ppermute x6, waiting for transfers between devices, shifted(): return lax.ppermute(value, axis, pairs)  7.65 us
    ppermute x14, waiting for transfers between devices, partner_value(): lax.ppermute(value, axis, [(at, at ^ bit) for at in range(lax.axis_size(a...  6.81 us
    pallas_call x3, Pallas kernels, step(): call(block_cols, live_blocks, upper_order, *scalars, hessian, gather(uppe...  6.43 us
    all_gather x2, blocking collectives, later(): region = lax.all_gather(operand, 'split', axis=0)  5.2 us
  transfers between devices with their start and end apart: 20, of which 9 were waited for; matrix products, arithmetic and copies ran while one was open for 0% of the time, Pallas kernels for 20%

profile of v4, /device:TPU:1, one launch (start us, length us, event | category | flops | bytes accessed | tf_op | source)
XLA Modules:
  0.0 118.7 jit_solution(17550238415933795955)
XLA Ops:
  2.4 2.1 %collective-permute-start.1 = (bf16[592,256]{1,0:T(8,128)(2,1)S(1)}, bf16[592,256]{1,0:T(8,128)(2,1)S(1)}, u32[]{:S(2)}, u32[]{:S(2)}) collective-permute-start(bf16[592,256]{1,0:T(8,128)(2,1)S(1)} %fusion.1), channel_id=1, source_target_pairs={{0,2},{2,4},{4,6},{6,8},{8,10},{10,12},{12,14},{14,16},{16,18},{18... | collective-permute-start | bytes 909320 | tf_op jit(solution)/shard_map/ppermute | solution.py:26
  4.5 4.1 %collective-permute-start = (bf16[592,256]{1,0:T(8,128)(2,1)S(1)}, bf16[592,256]{1,0:T(8,128)(2,1)S(1)}, u32[]{:S(2)}, u32[]{:S(2)}) collective-permute-start(bf16[592,256]{1,0:T(8,128)(2,1)S(1)} %fusion.1), channel_id=1, source_target_pairs={{0,30},{2,0},{4,2},{6,4},{8,6},{10,8},{12,10},{14,12},{16,14},{18,... | collective-permute-start | bytes 909320 | tf_op jit(solution)/shard_map/ppermute | solution.py:26
  8.6 2.8 %all-gather.2 = bf16[1184,256]{1,0:T(8,128)(2,1)S(1)} all-gather(bf16[592,256]{1,0:T(8,128)(2,1)S(1)} %fusion.1), channel_id=4, replica_groups=mesh['region'=16,'split'=2] {'split'}, dimensions={0}, use_global_device_ids=true | all-gather | bytes 909312 | tf_op jit(solution)/shard_map/all_gather | solution.py:290
  11.4 2.0 %copy-done = bf16[3,12,192,192]{3,2,1,0:T(8,128)(2,1)S(1)} copy-done((bf16[3,12,192,192]{3,2,1,0:T(8,128)(2,1)S(1)}, bf16[3,12,192,192]{3,2,1,0:T(8,128)(2,1)}, u32[]{:S(2)}) %copy-start) | copy-done | bytes 2654232
  16.9 3.4 %all-gather.1 = bf16[1184,256]{1,0:T(8,128)(2,1)S(1)} all-gather(bf16[592,256]{1,0:T(8,128)(2,1)S(1)} %collective-permute-done.1), channel_id=3, replica_groups=mesh['region'=16,'split'=2] {'split'}, dimensions={0}, use_global_device_ids=true | all-gather | bytes 909312 | tf_op jit(solution)/shard_map/all_gather | solution.py:283
  21.7 2.4 %all-gather = bf16[1184,256]{1,0:T(8,128)(2,1)S(1)} all-gather(bf16[592,256]{1,0:T(8,128)(2,1)S(1)} %collective-permute-done), channel_id=2, replica_groups=mesh['region'=16,'split'=2] {'split'}, dimensions={0}, use_global_device_ids=true | all-gather | bytes 909312 | tf_op jit(solution)/shard_map/all_gather | solution.py:283
  24.1 2.1 %shard_map.79 = (f32[576,256]{1,0:T(8,128)S(1)}, bf16[576,256]{1,0:T(8,128)(2,1)}) custom-call(s32[3,12]{1,0:T(4,128)S(1)} %copy-done.6, s32[3]{0:T(128)S(1)} %copy-done.8, s32[6]{0:T(128)S(1)} %fusion.3.list_ref, f32[2]{0:T(128)S(1)} %copy-done.10, bf16[3,12,192,192]{3,2,1,0:T(8,128)(2,1)S(1)} %copy-done, bf16[2,592,256]{2,1,0:T(8,128)(2,1)S(1)} %bitcast.23, ...), custom_call_target="tpu_custom_call" | custom-call | flops 339738624 | bytes 4423680 | tf_op jit(solution)/shard_map/pallas_call | solution.py:317
  27.0 2.2 %collective-permute-start.3 = (bf16[576,256]{1,0:T(8,128)(2,1)}, bf16[576,256]{1,0:T(8,128)(2,1)}, u32[]{:S(2)}, u32[]{:S(2)}) collective-permute-start(bf16[576,256]{1,0:T(8,128)(2,1)} %get-tuple-element.8), channel_id=1, source_target_pairs={{0,2},{2,4},{4,6},{6,8},{8,10},{10,12},{12,14},{14,16},{16,18},{18... | collective-permute-start | bytes 884744 | tf_op jit(solution)/shard_map/ppermute | solution.py:26
  29.2 2.9 %collective-permute-start.2 = (bf16[576,256]{1,0:T(8,128)(2,1)}, bf16[576,256]{1,0:T(8,128)(2,1)S(1)}, u32[]{:S(2)}, u32[]{:S(2)}) collective-permute-start(bf16[576,256]{1,0:T(8,128)(2,1)} %get-tuple-element.8), channel_id=1, source_target_pairs={{0,30},{2,0},{4,2},{6,4},{8,6},{10,8},{12,10},{14,12},{16,14},{18,... | collective-permute-start | bytes 884744 | tf_op jit(solution)/shard_map/ppermute | solution.py:26
  32.1 3.0 %all-gather.5 = bf16[1152,256]{1,0:T(8,128)(2,1)S(1)} all-gather(bf16[576,256]{1,0:T(8,128)(2,1)} %get-tuple-element.8), channel_id=7, replica_groups=mesh['region'=16,'split'=2] {'split'}, dimensions={0}, use_global_device_ids=true | all-gather | bytes 884736 | tf_op jit(solution)/shard_map/all_gather | solution.py:320
  36.4 5.5 %collective-permute-done.3 = bf16[576,256]{1,0:T(8,128)(2,1)} collective-permute-done((bf16[576,256]{1,0:T(8,128)(2,1)}, bf16[576,256]{1,0:T(8,128)(2,1)}, u32[]{:S(2)}, u32[]{:S(2)}) %collective-permute-start.3) | collective-permute-done | bytes 294944 | tf_op jit(solution)/shard_map/ppermute | solution.py:26
  41.9 3.3 %all-gather.4 = bf16[1152,256]{1,0:T(8,128)(2,1)S(1)} all-gather(bf16[576,256]{1,0:T(8,128)(2,1)} %collective-permute-done.3), channel_id=6, replica_groups=mesh['region'=16,'split'=2] {'split'}, dimensions={0}, use_global_device_ids=true | all-gather | bytes 884736 | tf_op jit(solution)/shard_map/all_gather | solution.py:283
  46.5 2.2 %all-gather.3 = bf16[1152,256]{1,0:T(8,128)(2,1)S(1)} all-gather(bf16[576,256]{1,0:T(8,128)(2,1)S(1)} %collective-permute-done.2), channel_id=5, replica_groups=mesh['region'=16,'split'=2] {'split'}, dimensions={0}, use_global_device_ids=true | all-gather | bytes 884736 | tf_op jit(solution)/shard_map/all_gather | solution.py:283
  50.1 2.3 %collective-permute-start.12 = (bf16[576,256]{1,0:T(8,128)(2,1)S(1)}, bf16[576,256]{1,0:T(8,128)(2,1)S(1)}, u32[]{:S(2)}, u32[]{:S(2)}) collective-permute-start(bf16[576,256]{1,0:T(8,128)(2,1)S(1)} %get-tuple-element.12), channel_id=1, source_target_pairs={{0,2},{2,4},{4,6},{6,8},{8,10},{10,12},{12,14},{14,16},{16,18},{18... | collective-permute-start | bytes 884744 | tf_op jit(solution)/shard_map/ppermute | solution.py:26
  54.1 2.2 %all-gather.8 = bf16[1152,256]{1,0:T(8,128)(2,1)S(1)} all-gather(bf16[576,256]{1,0:T(8,128)(2,1)S(1)} %get-tuple-element.12), channel_id=10, replica_groups=mesh['region'=16,'split'=2] {'split'}, dimensions={0}, use_global_device_ids=true | all-gather | bytes 884736 | tf_op jit(solution)/shard_map/all_gather | solution.py:320
  56.3 2.9 %collective-permute-start.11 = (bf16[576,256]{1,0:T(8,128)(2,1)S(1)}, bf16[576,256]{1,0:T(8,128)(2,1)S(1)}, u32[]{:S(2)}, u32[]{:S(2)}) collective-permute-start(bf16[576,256]{1,0:T(8,128)(2,1)S(1)} %get-tuple-element.12), channel_id=1, source_target_pairs={{0,30},{2,0},{4,2},{6,4},{8,6},{10,8},{12,10},{14,12},{16,14},{18,... | collective-permute-start | bytes 884744 | tf_op jit(solution)/shard_map/ppermute | solution.py:26
  62.0 5.8 %all-gather.7 = bf16[1152,256]{1,0:T(8,128)(2,1)S(1)} all-gather(bf16[576,256]{1,0:T(8,128)(2,1)S(1)} %collective-permute-done.12), channel_id=9, replica_groups=mesh['region'=16,'split'=2] {'split'}, dimensions={0}, use_global_device_ids=true | all-gather | bytes 884736 | tf_op jit(solution)/shard_map/all_gather | solution.py:283
  67.8 2.4 %all-gather.6 = bf16[1152,256]{1,0:T(8,128)(2,1)S(1)} all-gather(bf16[576,256]{1,0:T(8,128)(2,1)S(1)} %collective-permute-done.11), channel_id=8, replica_groups=mesh['region'=16,'split'=2] {'split'}, dimensions={0}, use_global_device_ids=true | all-gather | bytes 884736 | tf_op jit(solution)/shard_map/all_gather | solution.py:283
  71.6 3.0 %shard_map.87 = f32[256,256]{1,0:T(8,128)S(1)} custom-call(s32[3,12]{1,0:T(4,128)S(1)} %copy-done.7, s32[3]{0:T(128)S(1)} %copy-done.9, s32[6]{0:T(128)S(1)} %fusion.3.list_ref, s32[1]{0:T(128)} %bitcast.number_ref, bf16[3,12,192,192]{3,2,1,0:T(8,128)(2,1)S(1)} %copy-done.1, bf16[2,576,256]{2,1,0:T(8,128)(2,1)S(1)} %bitcast.26, ...), custom_call_target="tpu_custom_call" | custom-call | flops 339738624 | bytes 4423680 | tf_op jit(solution)/shard_map/pallas_call | solution.py:317
  75.0 1.7 %collective-permute-start.6 = (f32[96,128]{1,0:T(8,128)S(1)}, f32[96,128]{1,0:T(8,128)S(1)}, u32[]{:S(2)}, u32[]{:S(2)}) collective-permute-start(f32[96,128]{1,0:T(8,128)S(1)} %slice_add_fusion.3), channel_id=1, source_target_pairs={{0,4},{2,6},{4,0},{6,2},{8,12},{10,14},{12,8},{14,10},{16,20},{18,... | collective-permute-start | bytes 147464 | tf_op jit(solution)/shard_map/ppermute | solution.py:229
  76.7 1.6 %collective-permute-start.14 = (f32[64,256]{1,0:T(8,128)S(1)}, f32[64,256]{1,0:T(8,128)S(1)}, u32[]{:S(2)}, u32[]{:S(2)}) collective-permute-start(f32[64,256]{1,0:T(8,128)S(1)} %slice.49), channel_id=1, source_target_pairs={{0,2},{2,0},{4,6},{6,4},{8,10},{10,8},{12,14},{14,12},{16,18},{18,... | collective-permute-start | bytes 196616 | tf_op jit(solution)/shard_map/ppermute | solution.py:229
  79.7 1.9 %collective-permute-done.7 = f32[96,128]{1,0:T(8,128)S(1)} collective-permute-done((f32[96,128]{1,0:T(8,128)S(1)}, f32[96,128]{1,0:T(8,128)S(1)}, u32[]{:S(2)}, u32[]{:S(2)}) %collective-permute-start.7) | collective-permute-done | bytes 49184 | tf_op jit(solution)/shard_map/ppermute | solution.py:229
  81.7 2.1 %collective-permute-start.8 = (f32[96,128]{1,0:T(8,128)S(1)}, f32[96,128]{1,0:T(8,128)S(1)}, u32[]{:S(2)}, u32[]{:S(2)}) collective-permute-start(f32[96,128]{1,0:T(8,128)S(1)} %add.50), channel_id=1, source_target_pairs={{0,16},{2,18},{4,20},{6,22},{8,24},{10,26},{12,28},{14,30},{16,0},... | collective-permute-start | bytes 147464 | tf_op jit(solution)/shard_map/ppermute | solution.py:229
  85.6 1.7 %collective-permute-start.9 = (f32[96,128]{1,0:T(8,128)S(1)}, f32[96,128]{1,0:T(8,128)S(1)}, u32[]{:S(2)}, u32[]{:S(2)}) collective-permute-start(f32[96,128]{1,0:T(8,128)S(1)} %add.51), channel_id=1, source_target_pairs={{0,2},{2,0},{4,6},{6,4},{8,10},{10,8},{12,14},{14,12},{16,18},{18,... | collective-permute-start | bytes 147464 | tf_op jit(solution)/shard_map/ppermute | solution.py:229
  88.8 4.5 %collective-permute-start.10 = (f32[192,128]{1,0:T(8,128)S(1)}, f32[192,128]{1,0:T(8,128)S(1)}, u32[]{:S(2)}, u32[]{:S(2)}) collective-permute-start(f32[192,128]{1,0:T(8,128)S(1)} %pad_maximum_fusion.3), channel_id=1, source_target_pairs={{0,1},{1,0},{2,3},{3,2},{4,5},{5,4},{6,7},{7,6},{8,9},{9,8},{10,11... | collective-permute-start | bytes 294920 | tf_op jit(solution)/shard_map/ppermute | solution.py:229
  93.3 2.6 %collective-permute-start.17 = (f32[64,256]{1,0:T(8,128)S(1)}, f32[64,256]{1,0:T(8,128)S(1)}, u32[]{:S(2)}, u32[]{:S(2)}) collective-permute-start(f32[64,256]{1,0:T(8,128)S(1)} %add.55), channel_id=1, source_target_pairs={{0,16},{2,18},{4,20},{6,22},{8,24},{10,26},{12,28},{14,30},{16,0},... | collective-permute-start | bytes 196616 | tf_op jit(solution)/shard_map/ppermute | solution.py:229
  95.9 1.7 %collective-permute-done.17 = f32[64,256]{1,0:T(8,128)S(1)} collective-permute-done((f32[64,256]{1,0:T(8,128)S(1)}, f32[64,256]{1,0:T(8,128)S(1)}, u32[]{:S(2)}, u32[]{:S(2)}) %collective-permute-start.17) | collective-permute-done | bytes 65568 | tf_op jit(solution)/shard_map/ppermute | solution.py:229
  97.6 1.8 %collective-permute-start.18 = (f32[64,256]{1,0:T(8,128)S(1)}, f32[64,256]{1,0:T(8,128)S(1)}, u32[]{:S(2)}, u32[]{:S(2)}) collective-permute-start(f32[64,256]{1,0:T(8,128)S(1)} %add.56), channel_id=1, source_target_pairs={{0,2},{2,0},{4,6},{6,4},{8,10},{10,8},{12,14},{14,12},{16,18},{18,... | collective-permute-start | bytes 196616 | tf_op jit(solution)/shard_map/ppermute | solution.py:229
  99.4 1.6 %collective-permute-done.18 = f32[64,256]{1,0:T(8,128)S(1)} collective-permute-done((f32[64,256]{1,0:T(8,128)S(1)}, f32[64,256]{1,0:T(8,128)S(1)}, u32[]{:S(2)}, u32[]{:S(2)}) %collective-permute-start.18) | collective-permute-done | bytes 65568 | tf_op jit(solution)/shard_map/ppermute | solution.py:229
  101.1 4.1 %collective-permute-start.19 = (f32[128,256]{1,0:T(8,128)S(1)}, f32[128,256]{1,0:T(8,128)S(1)}, u32[]{:S(2)}, u32[]{:S(2)}) collective-permute-start(f32[128,256]{1,0:T(8,128)S(1)} %pad_maximum_fusion.2), channel_id=1, source_target_pairs={{0,1},{1,0},{2,3},{3,2},{4,5},{5,4},{6,7},{7,6},{8,9},{9,8},{10,11... | collective-permute-start | bytes 393224 | tf_op jit(solution)/shard_map/ppermute | solution.py:229
  105.2 11.7 %shard_map.84 = (f32[576,256]{1,0:T(8,128)}, f32[256,256]{1,0:T(8,128)S(1)}) custom-call(s32[1]{0:T(128)} %bitcast.number_ref, f32[384,128]{1,0:T(8,128)S(1)} %pad_maximum_fusion.1.gram_ref, f32[576,256]{1,0:T(8,128)S(1)} %get-tuple-element.10.two_ref), custom_call_target="tpu_custom_call" | custom-call | flops 12079595520 | bytes 4423680 | tf_op jit(solution)/shard_map/pallas_call | solution.py:330
  116.9 1.7 %shard_map.88 = f32[256,256]{1,0:T(8,128)} custom-call(s32[1]{0:T(128)} %bitcast.number_ref, f32[256,256]{1,0:T(8,128)S(1)} %pad_maximum_fusion.cross_ref, f32[256,256]{1,0:T(8,128)S(1)} %get-tuple-element.13.inverse_ref), custom_call_target="tpu_custom_call" | custom-call | flops 150994944 | bytes 4423680 | tf_op jit(solution)/shard_map/pallas_call | solution.py:333
  (76 shorter events, 22.7 us)
Async XLA Ops:
  2.4 14.4 %collective-permute-start.1 = (bf16[592,256]{1,0:T(8,128)(2,1)S(1)}, bf16[592,256]{1,0:T(8,128)(2,1)S(1)}, u32[]{:S(2)}, u32[]{:S(2)}) collective-permute-start(bf16[592,256]{1,0:T(8,128)(2,1)S(1)} %fusion.1), channel_id=1, source_target_pairs={{0,2},{2,4},{4,6},{6,8},{8,10},{10,12},{12,14},{14,16},{16,18},{18... | collective-permute-start | bytes 909320 | tf_op jit(solution)/shard_map/ppermute | solution.py:26
  4.5 17.1 %collective-permute-start = (bf16[592,256]{1,0:T(8,128)(2,1)S(1)}, bf16[592,256]{1,0:T(8,128)(2,1)S(1)}, u32[]{:S(2)}, u32[]{:S(2)}) collective-permute-start(bf16[592,256]{1,0:T(8,128)(2,1)S(1)} %fusion.1), channel_id=1, source_target_pairs={{0,30},{2,0},{4,2},{6,4},{8,6},{10,8},{12,10},{14,12},{16,14},{18,... | collective-permute-start | bytes 909320 | tf_op jit(solution)/shard_map/ppermute | solution.py:26
  11.4 2.0 %copy-start = (bf16[3,12,192,192]{3,2,1,0:T(8,128)(2,1)S(1)}, bf16[3,12,192,192]{3,2,1,0:T(8,128)(2,1)}, u32[]{:S(2)}) copy-start(bf16[3,12,192,192]{3,2,1,0:T(8,128)(2,1)} %hessian_ref.17) | copy-start | bytes 7962628
  13.4 0.7 copy-start.6
  14.1 0.7 copy-start.8
  16.0 8.1 %copy-start.2 = (f32[576,256]{1,0:T(8,128)S(1)}, f32[576,256]{1,0:T(8,128)}, u32[]{:S(2)}) copy-start(f32[576,256]{1,0:T(8,128)} %vectors_ref.3) | copy-start | bytes 1769476
  16.1 8.0 %copy-start.10 = (f32[2]{0:T(128)S(1)}, f32[2]{0:T(128)}, u32[]{:S(2)}) copy-start(f32[2]{0:T(128)} %bounds_ref.3) | copy-start | bytes 28
  21.7 13.4 %copy-start.1 = (bf16[3,12,192,192]{3,2,1,0:T(8,128)(2,1)S(1)}, bf16[3,12,192,192]{3,2,1,0:T(8,128)(2,1)}, u32[]{:S(2)}) copy-start(bf16[3,12,192,192]{3,2,1,0:T(8,128)(2,1)} %hessian_ref.17) | copy-start | bytes 7962628
  21.7 13.3 %copy-start.7 = (s32[3,12]{1,0:T(4,128)S(1)}, s32[3,12]{1,0:T(4,128)}, u32[]{:S(2)}) copy-start(s32[3,12]{1,0:T(4,128)} %cols_ref.17) | copy-start | bytes 436
  21.7 13.3 %copy-start.9 = (s32[3]{0:T(128)S(1)}, s32[3]{0:T(128)}, u32[]{:S(2)}) copy-start(s32[3]{0:T(128)} %live_ref.17) | copy-start | bytes 40
  26.2 0.8 copy-start.4
  27.0 14.9 %collective-permute-start.3 = (bf16[576,256]{1,0:T(8,128)(2,1)}, bf16[576,256]{1,0:T(8,128)(2,1)}, u32[]{:S(2)}, u32[]{:S(2)}) collective-permute-start(bf16[576,256]{1,0:T(8,128)(2,1)} %get-tuple-element.8), channel_id=1, source_target_pairs={{0,2},{2,4},{4,6},{6,8},{8,10},{10,12},{12,14},{14,16},{16,18},{18... | collective-permute-start | bytes 884744 | tf_op jit(solution)/shard_map/ppermute | solution.py:26
  29.2 17.3 %collective-permute-start.2 = (bf16[576,256]{1,0:T(8,128)(2,1)}, bf16[576,256]{1,0:T(8,128)(2,1)S(1)}, u32[]{:S(2)}, u32[]{:S(2)}) collective-permute-start(bf16[576,256]{1,0:T(8,128)(2,1)} %get-tuple-element.8), channel_id=1, source_target_pairs={{0,30},{2,0},{4,2},{6,4},{8,6},{10,8},{12,10},{14,12},{16,14},{18,... | collective-permute-start | bytes 884744 | tf_op jit(solution)/shard_map/ppermute | solution.py:26
  36.4 12.4 %copy-start.3 = (f32[576,256]{1,0:T(8,128)S(1)}, f32[576,256]{1,0:T(8,128)}, u32[]{:S(2)}) copy-start(f32[576,256]{1,0:T(8,128)} %vectors_ref.3) | copy-start | bytes 1769476
  36.4 12.3 %copy-start.5 = (f32[576,256]{1,0:T(8,128)S(1)}, f32[576,256]{1,0:T(8,128)}, u32[]{:S(2)}) copy-start(f32[576,256]{1,0:T(8,128)} %copy-done.4) | copy-start | bytes 1769476
  36.4 12.3 %copy-start.11 = (f32[2]{0:T(128)S(1)}, f32[2]{0:T(128)}, u32[]{:S(2)}) copy-start(f32[2]{0:T(128)} %bounds_ref.3) | copy-start | bytes 28
  50.1 11.9 %collective-permute-start.12 = (bf16[576,256]{1,0:T(8,128)(2,1)S(1)}, bf16[576,256]{1,0:T(8,128)(2,1)S(1)}, u32[]{:S(2)}, u32[]{:S(2)}) collective-permute-start(bf16[576,256]{1,0:T(8,128)(2,1)S(1)} %get-tuple-element.12), channel_id=1, source_target_pairs={{0,2},{2,4},{4,6},{6,8},{8,10},{10,12},{12,14},{14,16},{16,18},{18... | collective-permute-start | bytes 884744 | tf_op jit(solution)/shard_map/ppermute | solution.py:26
  53.4 7.1 %collective-permute-start.4 = (f32[192,128]{1,0:T(8,128)S(1)}, f32[192,128]{1,0:T(8,128)S(1)}, u32[]{:S(2)}, u32[]{:S(2)}) collective-permute-start(f32[192,128]{1,0:T(8,128)S(1)} %slice.43), channel_id=1, source_target_pairs={{0,1},{1,0},{2,3},{3,2},{4,5},{5,4},{6,7},{7,6},{8,9},{9,8},{10,11... | collective-permute-start | bytes 294920 | tf_op jit(solution)/shard_map/ppermute | solution.py:229
  56.3 11.5 %collective-permute-start.11 = (bf16[576,256]{1,0:T(8,128)(2,1)S(1)}, bf16[576,256]{1,0:T(8,128)(2,1)S(1)}, u32[]{:S(2)}, u32[]{:S(2)}) collective-permute-start(bf16[576,256]{1,0:T(8,128)(2,1)S(1)} %get-tuple-element.12), channel_id=1, source_target_pairs={{0,30},{2,0},{4,2},{6,4},{8,6},{10,8},{12,10},{14,12},{16,14},{18,... | collective-permute-start | bytes 884744 | tf_op jit(solution)/shard_map/ppermute | solution.py:26
  60.5 14.4 %collective-permute-start.5 = (f32[96,128]{1,0:T(8,128)S(1)}, f32[96,128]{1,0:T(8,128)S(1)}, u32[]{:S(2)}, u32[]{:S(2)}) collective-permute-start(f32[96,128]{1,0:T(8,128)S(1)} %slice.45), channel_id=1, source_target_pairs={{0,2},{2,0},{4,6},{6,4},{8,10},{10,8},{12,14},{14,12},{16,18},{18,... | collective-permute-start | bytes 147464 | tf_op jit(solution)/shard_map/ppermute | solution.py:229
  74.5 2.2 %collective-permute-start.13 = (f32[128,256]{1,0:T(8,128)S(1)}, f32[128,256]{1,0:T(8,128)S(1)}, u32[]{:S(2)}, u32[]{:S(2)}) collective-permute-start(f32[128,256]{1,0:T(8,128)S(1)} %slice.47), channel_id=1, source_target_pairs={{0,1},{1,0},{2,3},{3,2},{4,5},{5,4},{6,7},{7,6},{8,9},{9,8},{10,11... | collective-permute-start | bytes 393224 | tf_op jit(solution)/shard_map/ppermute | solution.py:229
  75.0 3.7 %collective-permute-start.6 = (f32[96,128]{1,0:T(8,128)S(1)}, f32[96,128]{1,0:T(8,128)S(1)}, u32[]{:S(2)}, u32[]{:S(2)}) collective-permute-start(f32[96,128]{1,0:T(8,128)S(1)} %slice_add_fusion.3), channel_id=1, source_target_pairs={{0,4},{2,6},{4,0},{6,2},{8,12},{10,14},{12,8},{14,10},{16,20},{18,... | collective-permute-start | bytes 147464 | tf_op jit(solution)/shard_map/ppermute | solution.py:229
  76.7 7.0 %collective-permute-start.14 = (f32[64,256]{1,0:T(8,128)S(1)}, f32[64,256]{1,0:T(8,128)S(1)}, u32[]{:S(2)}, u32[]{:S(2)}) collective-permute-start(f32[64,256]{1,0:T(8,128)S(1)} %slice.49), channel_id=1, source_target_pairs={{0,2},{2,0},{4,6},{6,4},{8,10},{10,8},{12,14},{14,12},{16,18},{18,... | collective-permute-start | bytes 196616 | tf_op jit(solution)/shard_map/ppermute | solution.py:229
  78.7 3.0 %collective-permute-start.7 = (f32[96,128]{1,0:T(8,128)S(1)}, f32[96,128]{1,0:T(8,128)S(1)}, u32[]{:S(2)}, u32[]{:S(2)}) collective-permute-start(f32[96,128]{1,0:T(8,128)S(1)} %add.49), channel_id=1, source_target_pairs={{0,8},{2,10},{4,12},{6,14},{8,0},{10,2},{12,4},{14,6},{16,24},{18,... | collective-permute-start | bytes 147464 | tf_op jit(solution)/shard_map/ppermute | solution.py:229
  81.7 3.9 %collective-permute-start.8 = (f32[96,128]{1,0:T(8,128)S(1)}, f32[96,128]{1,0:T(8,128)S(1)}, u32[]{:S(2)}, u32[]{:S(2)}) collective-permute-start(f32[96,128]{1,0:T(8,128)S(1)} %add.50), channel_id=1, source_target_pairs={{0,16},{2,18},{4,20},{6,22},{8,24},{10,26},{12,28},{14,30},{16,0},... | collective-permute-start | bytes 147464 | tf_op jit(solution)/shard_map/ppermute | solution.py:229
  83.8 3.5 %collective-permute-start.15 = (f32[64,256]{1,0:T(8,128)S(1)}, f32[64,256]{1,0:T(8,128)S(1)}, u32[]{:S(2)}, u32[]{:S(2)}) collective-permute-start(f32[64,256]{1,0:T(8,128)S(1)} %slice_add_fusion.2), channel_id=1, source_target_pairs={{0,4},{2,6},{4,0},{6,2},{8,12},{10,14},{12,8},{14,10},{16,20},{18,... | collective-permute-start | bytes 196616 | tf_op jit(solution)/shard_map/ppermute | solution.py:229
  85.6 3.2 %collective-permute-start.9 = (f32[96,128]{1,0:T(8,128)S(1)}, f32[96,128]{1,0:T(8,128)S(1)}, u32[]{:S(2)}, u32[]{:S(2)}) collective-permute-start(f32[96,128]{1,0:T(8,128)S(1)} %add.51), channel_id=1, source_target_pairs={{0,2},{2,0},{4,6},{6,4},{8,10},{10,8},{12,14},{14,12},{16,18},{18,... | collective-permute-start | bytes 147464 | tf_op jit(solution)/shard_map/ppermute | solution.py:229
  87.3 6.0 %collective-permute-start.16 = (f32[64,256]{1,0:T(8,128)S(1)}, f32[64,256]{1,0:T(8,128)S(1)}, u32[]{:S(2)}, u32[]{:S(2)}) collective-permute-start(f32[64,256]{1,0:T(8,128)S(1)} %add.54), channel_id=1, source_target_pairs={{0,8},{2,10},{4,12},{6,14},{8,0},{10,2},{12,4},{14,6},{16,24},{18,... | collective-permute-start | bytes 196616 | tf_op jit(solution)/shard_map/ppermute | solution.py:229
  88.8 10.6 %collective-permute-start.10 = (f32[192,128]{1,0:T(8,128)S(1)}, f32[192,128]{1,0:T(8,128)S(1)}, u32[]{:S(2)}, u32[]{:S(2)}) collective-permute-start(f32[192,128]{1,0:T(8,128)S(1)} %pad_maximum_fusion.3), channel_id=1, source_target_pairs={{0,1},{1,0},{2,3},{3,2},{4,5},{5,4},{6,7},{7,6},{8,9},{9,8},{10,11... | collective-permute-start | bytes 294920 | tf_op jit(solution)/shard_map/ppermute | solution.py:229
  93.3 4.3 %collective-permute-start.17 = (f32[64,256]{1,0:T(8,128)S(1)}, f32[64,256]{1,0:T(8,128)S(1)}, u32[]{:S(2)}, u32[]{:S(2)}) collective-permute-start(f32[64,256]{1,0:T(8,128)S(1)} %add.55), channel_id=1, source_target_pairs={{0,16},{2,18},{4,20},{6,22},{8,24},{10,26},{12,28},{14,30},{16,0},... | collective-permute-start | bytes 196616 | tf_op jit(solution)/shard_map/ppermute | solution.py:229
  97.6 3.5 %collective-permute-start.18 = (f32[64,256]{1,0:T(8,128)S(1)}, f32[64,256]{1,0:T(8,128)S(1)}, u32[]{:S(2)}, u32[]{:S(2)}) collective-permute-start(f32[64,256]{1,0:T(8,128)S(1)} %add.56), channel_id=1, source_target_pairs={{0,2},{2,0},{4,6},{6,4},{8,10},{10,8},{12,14},{14,12},{16,18},{18,... | collective-permute-start | bytes 196616 | tf_op jit(solution)/shard_map/ppermute | solution.py:229
  101.1 15.8 %collective-permute-start.19 = (f32[128,256]{1,0:T(8,128)S(1)}, f32[128,256]{1,0:T(8,128)S(1)}, u32[]{:S(2)}, u32[]{:S(2)}) collective-permute-start(f32[128,256]{1,0:T(8,128)S(1)} %pad_maximum_fusion.2), channel_id=1, source_target_pairs={{0,1},{1,0},{2,3},{3,2},{4,5},{5,4},{6,7},{7,6},{8,9},{9,8},{10,11... | collective-permute-start | bytes 393224 | tf_op jit(solution)/shard_map/ppermute | solution.py:229

commit v5 on v4

v5 whole, which is shorter than its diff:
```python
import functools
import jax
import jax.numpy as jnp
from jax import lax
from jax.experimental import pallas as pl
from jax.experimental.pallas import tpu as pltpu
from jax.sharding import PartitionSpec as P

AXES = ("region", "split")
VMEM = pl.BlockSpec(memory_space=pltpu.VMEM)
SMEM = pl.BlockSpec(memory_space=pltpu.SMEM)
EXACT = lax.Precision.HIGHEST
NN = (((1,), (0,)), ((), ()))
NT = (((1,), (1,)), ((), ()))
TN = (((0,), (0,)), ((), ()))
GROUP = 8
TILE = 128
VMEM_LIMIT = 20 * 1024 * 1024
LIST_ROWS = 16
PIECES = 4
EARLY = 2


def shifted(value, axis, steps):
    count = lax.axis_size(axis)
    pairs = [(source, (source + steps) % count) for source in range(count)]
    return lax.ppermute(value, axis, pairs)


def exact_dot(left, right, dims=NN):
    return lax.dot_general(left, right, dims, precision=EXACT, preferred_element_type=jnp.float32)


def kernel_call(body, out_shape, in_specs, flops, bytes_accessed, slots=None):
    return pl.pallas_call(
        body,
        out_shape=out_shape,
        in_specs=in_specs,
        out_specs=jax.tree.map(lambda _: VMEM, out_shape),
        scratch_shapes=[] if slots is None else [pltpu.SMEM(slots, jnp.int32)],
        compiler_params=pltpu.CompilerParams(vmem_limit_bytes=VMEM_LIMIT),
        cost_estimate=pl.CostEstimate(flops=flops, bytes_accessed=bytes_accessed, transcendentals=0),
    )


def fill_slots(slots_ref, cols_ref, live_ref, first, place_of):
    rows, stored = cols_ref.shape
    count = slots_ref.shape[1]
    for row in range(rows):
        for index in range(count):
            slots_ref[row, index] = -1
        for at in range(stored):
            name = cols_ref[row, at] - first

            @pl.when((name >= 0) & (name < count) & (at < live_ref[row]))
            def _():
                slots_ref[row, place_of(name)] = at


def accumulate(slots_ref, hessian_ref, operand_ref, base, total):
    rows, _, size, _ = hessian_ref.shape
    shards, shard_rows, _ = operand_ref.shape
    each = shard_rows // size
    for index in range(shards * each):
        start = index % each * size
        block = operand_ref[index // each, start : start + size, :]
        parts = []
        for row in range(rows):
            slot = slots_ref[row, base + index]
            live = jnp.where(slot >= 0, 1.0, 0.0).astype(jnp.float32)
            stored = hessian_ref[row, jnp.maximum(slot, 0)]
            parts.append(stored * jnp.broadcast_to(live, (size, size)).astype(jnp.bfloat16))
        term = jnp.dot(jnp.concatenate(parts, 0), block, preferred_element_type=jnp.float32)
        total = term if total is None else total + term
    return total


def near_body(count, *refs):
    cols_ref, live_ref, bases_ref, hessian_ref = refs[:4]
    operands, (out_ref, slots_ref) = refs[4:-2], refs[-2:]
    fill_slots(slots_ref, cols_ref, live_ref, 0, lambda name: name)
    total = None
    for at, operand_ref in enumerate(operands):
        total = accumulate(slots_ref, hessian_ref, operand_ref, bases_ref[at], total)
    out_ref[...] = total


def halo_total(first, which, cols_ref, live_ref, lists_ref, bases_ref, hessian_ref, lower_ref, upper_ref, total_ref, slots_ref):
    halo = lists_ref.shape[1]
    fill_slots(slots_ref, cols_ref, live_ref, first, lambda name: list_place(lists_ref, name))
    total = accumulate(slots_ref, hessian_ref, lower_ref, bases_ref[which], total_ref[...])
    return accumulate(slots_ref, hessian_ref, upper_ref, halo + bases_ref[which], total)


def list_place(lists_ref, name):
    halo = lists_ref.shape[1]
    side = jnp.where(name >= halo, 1, 0).astype(jnp.int32)
    return side * halo + lists_ref[side, name - side * halo]


def middle_body(first, which, *refs):
    out_ref, slots_ref = refs[-2:]
    out_ref[...] = halo_total(first, which, *refs[:-2], slots_ref)


def interval(bounds_ref):
    return 0.5 * (bounds_ref[0] + bounds_ref[1]), 0.5 * (bounds_ref[1] - bounds_ref[0])


def first_body(first, which, *refs):
    *operands, bounds_ref, vectors_ref, one_ref, cast_ref, slots_ref = refs
    centre, half = interval(bounds_ref)
    total = halo_total(first, which, *operands, slots_ref)
    one = (total - centre * vectors_ref[...]) / half
    one_ref[...] = one
    cast_ref[...] = one.astype(jnp.bfloat16)


def second_body(first, which, *refs):
    *operands, bounds_ref, one_ref, vectors_ref, two_ref, cast_ref, slots_ref = refs
    centre, half = interval(bounds_ref)
    total = halo_total(first, which, *operands, slots_ref)
    two = 2.0 * (total - centre * one_ref[...]) / half - vectors_ref[...]
    two_ref[...] = two
    cast_ref[...] = two.astype(jnp.bfloat16)


def place_rows(number_ref, piece, rows):
    return pl.ds(pl.multiple_of((piece ^ number_ref[0]) * rows, GROUP), rows)


def scatter_pieces(number_ref, out_ref, value):
    rows = out_ref.shape[0] // PIECES
    for piece in range(PIECES):
        out_ref[place_rows(number_ref, piece, rows), :] = value[piece * rows : (piece + 1) * rows, :]


def ordered_pieces(number_ref, in_ref):
    rows = in_ref.shape[0] // PIECES
    return jnp.concatenate([in_ref[place_rows(number_ref, piece, rows), :] for piece in range(PIECES)], 0)


def lower_tiles(count):
    return [(row, col) for row in range(count) for col in range(row + 1)]


def gram_body(number_ref, two_ref, out_ref):
    two = two_ref[...]
    cols = [two[:, at * TILE : (at + 1) * TILE] for at in range(two.shape[1] // TILE)]
    tiles = [exact_dot(cols[row], cols[col], TN) for row, col in lower_tiles(len(cols))]
    scatter_pieces(number_ref, out_ref, jnp.concatenate(tiles, 0))


def third_body(first, which, *refs):
    *operands, number_ref, two_ref, out_ref, slots_ref = refs
    image = halo_total(first, which, *operands, slots_ref)
    scatter_pieces(number_ref, out_ref, exact_dot(two_ref[...], image, TN))


def over_lanes(value, lane):
    return jnp.broadcast_to(value[:, lane : lane + 1], value.shape)


def over_rows(value, row):
    return jnp.broadcast_to(value[row : row + 1, :], value.shape)


def eliminate(tile, first, last):
    count = tile.shape[0] // GROUP
    rows = [tile[index * GROUP : (index + 1) * GROUP, :] for index in range(count)]
    sub = lax.broadcasted_iota(jnp.int32, rows[0].shape, 0)
    lane = lax.broadcasted_iota(jnp.int32, rows[0].shape, 1)
    for step in range(first, last):
        start = step * GROUP
        pivot_cols = [over_lanes(rows[step], start + col) for col in range(GROUP)]
        factors = {
            below: [over_lanes(rows[below], start + col) for col in range(GROUP)]
            for below in range(step + 1, count)
        }
        inside = (lane >= start) & (lane < start + GROUP)
        forward = jnp.where(inside, jnp.where(lane - start == sub, 1.0, 0.0), rows[step])
        solved = forward
        for pivot in range(GROUP):
            here = sub == pivot
            value = over_rows(pivot_cols[pivot], pivot)
            inverse = 1.0 / value
            ratio = pivot_cols[pivot] * inverse
            row = over_rows(forward, pivot)
            forward = jnp.where(
                here, row * lax.rsqrt(value), jnp.where(sub > pivot, forward - ratio * row, forward)
            )
            solved = jnp.where(here, row * inverse, solved - ratio * row)
            for col in range(pivot + 1, GROUP):
                top = over_rows(pivot_cols[col], pivot)
                pivot_cols[col] = jnp.where(here, top * inverse, pivot_cols[col] - ratio * top)
        rows[step] = jnp.where(lane < start + GROUP, forward, 0.0)
        solved_rows = [over_rows(solved, pivot) for pivot in range(GROUP)]
        for below in range(step + 1, count):
            terms = [factors[below][col] * solved_rows[col] for col in range(GROUP)]
            while len(terms) > 1:
                terms = [terms[at] + terms[at + 1] for at in range(0, len(terms), 2)]
            rows[below] = jnp.where(inside, 0.0, rows[below]) - terms[0]
    return jnp.concatenate(rows, 0)


def unpack_body(total_rows, number_ref, gram_ref, *tile_refs):
    tiles = ordered_pieces(number_ref, gram_ref) / total_rows
    for at, tile_ref in enumerate(tile_refs):
        tile_ref[...] = tiles[at * TILE : (at + 1) * TILE, :]


def eliminate_body(first, last, tile_ref, out_ref):
    out_ref[...] = eliminate(tile_ref[...], first, last)


def update_body(at, count, *refs):
    inputs = refs[: len(refs) // 2]
    outputs = refs[len(refs) // 2 :]
    names = [name for name in lower_tiles(count) if name[1] >= at]
    tiles = {name: ref[...] for name, ref in zip(names, inputs)}
    column = {row: exact_dot(tiles[row, at], tiles[at, at], NT) for row in range(at + 1, count)}
    for (row, col), out_ref in zip(names, outputs):
        if row == at:
            out_ref[...] = tiles[row, col]
        elif col == at:
            out_ref[...] = column[row]
        else:
            out_ref[...] = tiles[row, col] - exact_dot(column[row], column[col], NT)


def basis_body(count, *refs):
    *tile_refs, two_ref, basis_ref, inverse_ref = refs
    tiles = {name: ref[...] for name, ref in zip(lower_tiles(count), tile_refs)}
    inverse = {}
    for row in range(count):
        inverse[row, row] = tiles[row, row]
        for col in range(row):
            mixed = exact_dot(tiles[row, col], inverse[col, col])
            for mid in range(col + 1, row):
                mixed = mixed + exact_dot(tiles[row, mid], inverse[mid, col])
            inverse[row, col] = -exact_dot(tiles[row, row], mixed)
    zero = jnp.zeros((TILE, TILE), jnp.float32)
    whole = jnp.concatenate(
        [
            jnp.concatenate([inverse[row, col] if col <= row else zero for col in range(count)], 1)
            for row in range(count)
        ],
        0,
    )
    inverse_ref[...] = whole
    basis_ref[...] = exact_dot(two_ref[...], whole, NT)


def projected_body(total_rows, number_ref, cross_ref, inverse_ref, projected_ref):
    cross = ordered_pieces(number_ref, cross_ref) / total_rows
    projected_ref[...] = exact_dot(exact_dot(inverse_ref[...], cross), inverse_ref[...], NT)


def factor_stages(total_rows, count, number, two):
    rows, modes = two.shape
    tile = jax.ShapeDtypeStruct((TILE, TILE), jnp.float32)
    names = lower_tiles(count)
    work = 4 * 10 ** 9

    def unpack(gram):
        body = functools.partial(unpack_body, total_rows)
        return kernel_call(body, (tile,) * len(names), [SMEM, VMEM], work // 8, gram.size)(number, gram)

    def elimination(at, first, last):
        def stage(tiles):
            place = names.index((at, at))
            call = kernel_call(functools.partial(eliminate_body, first, last), tile, [VMEM], work // 2, TILE * TILE)
            return tiles[:place] + (call(tiles[place]),) + tiles[place + 1 :]

        return stage

    def update(at):
        def stage(tiles):
            picked = [index for index, name in enumerate(names) if name[1] >= at]
            body = functools.partial(update_body, at, count)
            call = kernel_call(body, (tile,) * len(picked), [VMEM] * len(picked), work // 4, TILE * TILE)
            new = call(*[tiles[index] for index in picked])
            return tuple(new[picked.index(index)] if index in picked else old for index, old in enumerate(tiles))

        return stage

    def finish(tiles):
        outs = (jax.ShapeDtypeStruct((rows, modes), jnp.float32), jax.ShapeDtypeStruct((modes, modes), jnp.float32))
        body = functools.partial(basis_body, count)
        return kernel_call(body, outs, [VMEM] * (len(names) + 1), work // 2, rows * modes)(*tiles, two)

    groups = TILE // GROUP
    cuts = [0, groups // 4, groups // 2 + 1, groups]
    stages = [unpack]
    for at in range(count):
        stages += [elimination(at, first, last) for first, last in zip(cuts, cuts[1:])]
        if at + 1 < count:
            stages.append(update(at))
    return stages + [finish]


def tied(left, right):
    return lax.optimization_barrier((left, right))


def partner_value(value, axis, bit):
    return lax.ppermute(value, axis, [(at, at ^ bit) for at in range(lax.axis_size(axis))])


def halving_bits():
    bits = []
    for axis in ("split", "region"):
        size = lax.axis_size(axis)
        bits.append([(axis, 1 << at) for at in range(size.bit_length() - 1)])
    cores, regions = bits
    return [cores[0], regions[1]], cores[1:] + regions[2:] + regions[:1]


def device_number():
    halved, _ = halving_bits()
    number = 0
    for axis, bit in halved:
        number = number * 2 + (lax.axis_index(axis) // bit) % 2
    return number.astype(jnp.int32).reshape(1)


def sum_steps():
    halved, doubled = halving_bits()

    def halving(axis, bit):
        send = lambda value: partner_value(value[value.shape[0] // 2 :], axis, bit)
        return send, lambda value, got: value[: value.shape[0] // 2] + got

    def doubling(axis, bit):
        return lambda value: partner_value(value, axis, bit), lambda value, got: value + got

    def joining(axis, bit):
        send = lambda value: partner_value(value, axis, bit)
        return send, lambda value, got: jnp.concatenate([value, got], 0)

    steps = [halving(axis, bit) for axis, bit in halved]
    steps += [doubling(axis, bit) for axis, bit in doubled]
    return steps + [joining(axis, bit) for axis, bit in reversed(halved)]


def run_steps(value, steps):
    for send, join in steps:
        value = join(value, send(value))
    return value


def run_beside(value, steps, state, stages):
    stages = list(stages)
    for index, (send, join) in enumerate(steps):
        value, state = tied(value, state)
        got = send(value)
        due = -(-len(stages) // (len(steps) - index))
        for _ in range(due):
            state = stages.pop(0)(state)
        if due:
            got, state = tied(got, state)
        value = join(value, got)
    return value, state


def local(vectors, hessian, block_cols, live_blocks, halo_lists, bounds):
    row_blocks, stored, size, _ = hessian.shape
    rows, modes = vectors.shape
    splits = lax.axis_size("split")
    region_blocks = row_blocks * splits
    halo_blocks = halo_lists.shape[2]
    whole = halo_blocks == region_blocks and region_blocks <= 256
    total_rows = rows * lax.axis_size(AXES)

    paired = whole and splits == 2
    core = lax.axis_index("split").astype(jnp.int32)
    swapped = lambda value: lax.ppermute(value, "split", [(0, 1), (1, 0)])
    near_first = [core * row_blocks, (1 - core) * row_blocks] if paired else [0]
    bases = jnp.stack(near_first).astype(jnp.int32) if paired else jnp.zeros((1,), jnp.int32)

    def sent(operand, region):
        if whole:
            return operand, operand
        width = modes // splits
        start = core * width
        blocks = region[:, :rows].reshape(region_blocks, size, modes)
        share = lambda listed: lax.dynamic_slice_in_dim(blocks[listed], start, width, 2).reshape(-1, width)
        return share(halo_lists[0, 1]), share(halo_lists[0, 0])

    def gathered(value):
        if paired:
            return [value[None], swapped(value)[None]]
        if whole:
            return [lax.all_gather(value, "split", axis=0)]
        return [lax.all_gather(value, "split", axis=1, tiled=True)[None]]

    listed = jnp.pad(halo_lists[0], ((0, LIST_ROWS - 2), (0, modes - halo_blocks)))
    first = vectors.astype(jnp.bfloat16)
    if whole:
        first = jnp.concatenate([first, listed.astype(jnp.bfloat16)], 0)

    def near_parts(operand):
        if paired:
            return [operand[None], swapped(operand)[None]]
        return [lax.all_gather(operand, "split", axis=0)]

    def exchange(operand, hold=lambda value: value):
        near = near_parts(operand)
        up, down = sent(operand, near[0])
        lower = shifted(up, "region", 1)
        return near, lower, shifted(hold(down), "region", -1)

    first_near, first_lower, first_upper = exchange(first)
    if whole:
        orders = [first_lower[rows + 1, :halo_blocks], first_upper[rows, :halo_blocks]]
        lists = jnp.stack(orders).astype(jnp.int32)
    else:
        lists = jnp.broadcast_to(jnp.arange(halo_blocks, dtype=jnp.int32), (2, halo_blocks))

    wide = jax.ShapeDtypeStruct((rows, modes), jnp.float32)
    narrow = jax.ShapeDtypeStruct((rows, modes), jnp.bfloat16)
    square = jax.ShapeDtypeStruct((modes, modes), jnp.float32)
    tile_rows = len(lower_tiles(modes // TILE)) * TILE
    work = 2 * rows * size * modes
    square_work = 2 * rows * modes * modes
    traffic = hessian.size * 2 + 3 * rows * modes * 4
    number = device_number()
    halo_slots = (row_blocks, 2 * halo_blocks)

    def step(body, outs, near, lower, upper, scalars, extra):
        call = kernel_call(
            functools.partial(near_body, region_blocks),
            wide,
            [SMEM] * 3 + [VMEM] * (1 + len(near)),
            work * region_blocks,
            traffic,
            (row_blocks, region_blocks),
        )
        total = call(block_cols, live_blocks, bases, hessian, *near)
        pairs = list(zip(gathered(lower), gathered(upper)))
        for which, pair in enumerate(pairs):
            last = which == len(pairs) - 1
            given = (block_cols, live_blocks, lists, bases, hessian, *pair, total) + ((*scalars, *extra) if last else ())
            specs = [SMEM] * 4 + [VMEM] * 4 + ([SMEM] * len(scalars) + [VMEM] * len(extra) if last else [])
            body_of = functools.partial(body if last else middle_body, region_blocks, which)
            cost = 2 * work * halo_blocks // len(pairs)
            total = kernel_call(body_of, outs if last else wide, specs, cost, traffic, halo_slots)(*given)
        return total

    one, one_cast = step(first_body, (wide, narrow), first_near, first_lower, first_upper, (bounds,), (vectors,))
    two, two_cast = step(second_body, (wide, narrow), *exchange(one_cast), (bounds,), (one, vectors))

    steps = sum_steps()
    packed = jax.ShapeDtypeStruct((tile_rows, TILE), jnp.float32)
    gram = kernel_call(gram_body, packed, [SMEM, VMEM], square_work, traffic)(number, two)
    gram = run_steps(gram, steps[:EARLY])

    def hold(value):
        nonlocal gram
        value, gram = tied(value, gram)
        return value

    third = exchange(two_cast, hold)
    gram = run_steps(gram, steps[EARLY:])
    cross = step(third_body, square, *third, (number,), (two,))
    stages = factor_stages(float(total_rows), modes // TILE, number, two)
    cross, (basis, inverse) = run_beside(cross, steps, gram, stages)
    body_of = functools.partial(projected_body, float(total_rows))
    call = kernel_call(body_of, square, [SMEM] + [VMEM] * 2, 2 * square_work, traffic)
    return basis, call(number, cross, inverse)


def solution(mesh):
    placed = (
        P(("region", "split"), None),
        P(("region", "split"), None, None, None),
        P(("region", "split"), None),
        P(("region", "split")),
        P("region", None, None),
        P(),
    )
    return jax.shard_map(
        local,
        mesh=mesh,
        in_specs=placed,
        out_specs=(P(("region", "split"), None), P()),
        check_vma=False,
    )
```

time: 119 us -> 123 us (1.034)
  blocking collectives: 27.5 us -> 0 us
  waiting for transfers between devices: 14.5 us -> 35.3 us
  starting transfers between devices: 40.8 us -> 46.3 us
  Pallas kernels: 28.9 us -> 32 us
  local copies, waits for them, and re-layouts: 4.23 us -> 5.58 us
    all_gather x9 -> x0, blocking collectives: 27.5 us -> none  [the longest x6 19.4 us: gather(): return lax.all_gather(value, 'split', axis=0)]
    ppermute x0 -> x9, starting transfers between devices: none -> 15.3 us  [local(): swapped = lambda value: lax.ppermute(value, 'split', [(0, 1), (1, 0)])]
    ppermute x6, waiting for transfers between devices: 7.65 us -> 19 us  [shifted(): return lax.ppermute(value, axis, pairs)]
    ppermute x14, waiting for transfers between devices: 6.81 us -> 16.4 us  [partner_value(): lax.ppermute(value, axis, [(at, at ^ bit) for at in range(lax.axis_size(a...]
    ppermute x14, starting transfers between devices: 24.4 us -> 16.1 us  [partner_value(): lax.ppermute(value, axis, [(at, at ^ bit) for at in range(lax.axis_size(a...]
    pallas_call x10 -> x18, Pallas kernels: 26.1 us -> 29.2 us  [the longest x6 13.5 us: step(): kernel_call(body_of, outs if last else wide, specs, cost, traffic, halo_s...]
    ppermute x6, starting transfers between devices: 16.3 us -> 14.9 us  [shifted(): return lax.ppermute(value, axis, pairs)]
    slice x4 -> x6, local copies, waits for them, and re-layouts: 0.03 us -> 1.38 us  [the longest x1 0.68 us: local(): first_lower[rows + 1, :halo_blocks]]
  transfers between devices with their start and end apart: 20 -> 29, of which waited for: 9 -> 13; matrix products, arithmetic and copies ran while one was open for 0% -> 1% of each run, Pallas kernels for 20% -> 17%
where the time goes in v5:
time: 123 us; the launch traced here: 122 us
  starting transfers between devices  46.3 us (38%)
  waiting for transfers between devices  35.3 us (29%)
  Pallas kernels  32 us (26%)
  local copies, waits for them, and re-layouts  5.58 us (5%)
  other arithmetic  2.06 us (2%)
    ppermute x6, waiting for transfers between devices, shifted(): return lax.ppermute(value, axis, pairs)  19 us
    ppermute x14, waiting for transfers between devices, partner_value(): lax.ppermute(value, axis, [(at, at ^ bit) for at in range(lax.axis_size(a...  16.4 us
    ppermute x14, starting transfers between devices, partner_value(): lax.ppermute(value, axis, [(at, at ^ bit) for at in range(lax.axis_size(a...  16.1 us
    ppermute x9, starting transfers between devices, local(): swapped = lambda value: lax.ppermute(value, 'split', [(0, 1), (1, 0)])  15.3 us
    ppermute x6, starting transfers between devices, shifted(): return lax.ppermute(value, axis, pairs)  14.9 us
    pallas_call x6, Pallas kernels, step(): kernel_call(body_of, outs if last else wide, specs, cost, traffic, halo_s...  13.5 us
    pallas_call x6, Pallas kernels, stage(): return tiles[:place] + (call(tiles[place]),) + tiles[place + 1:]  8.78 us
    pallas_call x3, Pallas kernels, step(): total = call(block_cols, live_blocks, bases, hessian, *near)  4.41 us
  transfers between devices with their start and end apart: 29, of which 13 were waited for; matrix products, arithmetic and copies ran while one was open for 1% of the time, Pallas kernels for 17%

profile of v5, /device:TPU:1, one launch (start us, length us, event | category | flops | bytes accessed | tf_op | source)
XLA Modules:
  0.0 122.4 jit_solution(15547365092820253556)
XLA Ops:
  2.5 2.1 %collective-permute-start = (bf16[592,256]{1,0:T(8,128)(2,1)S(1)}, bf16[592,256]{1,0:T(8,128)(2,1)}, u32[]{:S(2)}, u32[]{:S(2)}) collective-permute-start(bf16[592,256]{1,0:T(8,128)(2,1)S(1)} %get-tuple-element.137), channel_id=1, source_target_pairs={{0,2},{2,4},{4,6},{6,8},{8,10},{10,12},{12,14},{14,16},{16,18},{18... | collective-permute-start | bytes 909320 | tf_op jit(solution)/shard_map/ppermute | solution.py:27
  4.6 4.1 %collective-permute-start.1 = (bf16[592,256]{1,0:T(8,128)(2,1)S(1)}, bf16[592,256]{1,0:T(8,128)(2,1)}, u32[]{:S(2)}, u32[]{:S(2)}) collective-permute-start(bf16[592,256]{1,0:T(8,128)(2,1)S(1)} %get-tuple-element.137), channel_id=1, source_target_pairs={{0,30},{2,0},{4,2},{6,4},{8,6},{10,8},{12,10},{14,12},{16,14},{18,... | collective-permute-start | bytes 909320 | tf_op jit(solution)/shard_map/ppermute | solution.py:27
  9.6 7.3 %collective-permute-done = bf16[592,256]{1,0:T(8,128)(2,1)} collective-permute-done((bf16[592,256]{1,0:T(8,128)(2,1)S(1)}, bf16[592,256]{1,0:T(8,128)(2,1)}, u32[]{:S(2)}, u32[]{:S(2)}) %collective-permute-start) | collective-permute-done | bytes 303136 | tf_op jit(solution)/shard_map/ppermute | solution.py:27
  16.9 1.5 %collective-permute-start.2 = (bf16[592,256]{1,0:T(8,128)(2,1)}, bf16[592,256]{1,0:T(8,128)(2,1)}, u32[]{:S(2)}, u32[]{:S(2)}) collective-permute-start(bf16[592,256]{1,0:T(8,128)(2,1)} %collective-permute-done), channel_id=1, source_target_pairs={{0,1},{1,0},{2,3},{3,2},{4,5},{5,4},{6,7},{7,6},{8,9},{9,8},{10,11... | collective-permute-start | bytes 909320 | tf_op jit(solution)/shard_map/ppermute | solution.py:377
  19.0 1.5 %collective-permute-start.3 = (bf16[592,256]{1,0:T(8,128)(2,1)}, bf16[592,256]{1,0:T(8,128)(2,1)}, u32[]{:S(2)}, u32[]{:S(2)}) collective-permute-start(bf16[592,256]{1,0:T(8,128)(2,1)} %collective-permute-done.1), channel_id=1, source_target_pairs={{0,1},{1,0},{2,3},{3,2},{4,5},{5,4},{6,7},{7,6},{8,9},{9,8},{10,11... | collective-permute-start | bytes 909320 | tf_op jit(solution)/shard_map/ppermute | solution.py:377
  21.9 2.0 %copy-done = bf16[3,12,192,192]{3,2,1,0:T(8,128)(2,1)S(1)} copy-done((bf16[3,12,192,192]{3,2,1,0:T(8,128)(2,1)S(1)}, bf16[3,12,192,192]{3,2,1,0:T(8,128)(2,1)}, u32[]{:S(2)}) %copy-start) | copy-done | bytes 2654232
  26.6 2.0 %shard_map.78.refs_7_ = f32[576,256]{1,0:T(8,128)S(1)} custom-call(s32[3,12]{1,0:T(4,128)S(1)} %copy-done.6, s32[3]{0:T(128)S(1)} %copy-done.8, s32[2,6]{1,0:T(2,128)S(1)} %maximum_convert_fusion.refs_2_, s32[2]{0:T(128)S(1)} %pad_add_fusion.refs_2_.refs_3_, bf16[3,12,192,192]{3,2,1,0:T(8,128)(2,1)S(1)} %copy-done, bf16[1,592,256]{2,1,0:T(8,128)(2,1)} %bitcast.5.refs_5_, ...), custom_call_target="tpu_custom_call" | custom-call | flops 339738624 | bytes 4423680 | tf_op jit(solution)/shard_map/pallas_call | solution.py:447
  28.7 2.8 %shard_map.79 = (f32[576,256]{1,0:T(8,128)S(1)}, bf16[576,256]{1,0:T(8,128)(2,1)}) custom-call(s32[3,12]{1,0:T(4,128)S(1)} %copy-done.6, s32[3]{0:T(128)S(1)} %copy-done.8, s32[2,6]{1,0:T(2,128)S(1)} %maximum_convert_fusion.refs_2_, s32[2]{0:T(128)S(1)} %pad_add_fusion.refs_2_.refs_3_, bf16[3,12,192,192]{3,2,1,0:T(8,128)(2,1)S(1)} %copy-done, ...), custom_call_target="tpu_custom_call" | custom-call | flops 339738624 | bytes 4423680 | tf_op jit(solution)/shard_map/pallas_call | solution.py:447
  32.4 3.0 %collective-permute-start.7 = (bf16[576,256]{1,0:T(8,128)(2,1)}, bf16[576,256]{1,0:T(8,128)(2,1)}, u32[]{:S(2)}, u32[]{:S(2)}) collective-permute-start(bf16[576,256]{1,0:T(8,128)(2,1)} %get-tuple-element.69), channel_id=1, source_target_pairs={{0,30},{2,0},{4,2},{6,4},{8,6},{10,8},{12,10},{14,12},{16,14},{18,... | collective-permute-start | bytes 884744 | tf_op jit(solution)/shard_map/ppermute | solution.py:27
  35.7 6.4 %collective-permute-done.7 = bf16[576,256]{1,0:T(8,128)(2,1)} collective-permute-done((bf16[576,256]{1,0:T(8,128)(2,1)}, bf16[576,256]{1,0:T(8,128)(2,1)}, u32[]{:S(2)}, u32[]{:S(2)}) %collective-permute-start.7) | collective-permute-done | bytes 294944 | tf_op jit(solution)/shard_map/ppermute | solution.py:27
  43.0 4.7 %collective-permute-done.5 = bf16[576,256]{1,0:T(8,128)(2,1)} collective-permute-done((bf16[576,256]{1,0:T(8,128)(2,1)}, bf16[576,256]{1,0:T(8,128)(2,1)}, u32[]{:S(2)}, u32[]{:S(2)}) %collective-permute-start.5) | collective-permute-done | bytes 294944 | tf_op jit(solution)/shard_map/ppermute | solution.py:27
  48.9 1.8 %shard_map.80.refs_7_ = f32[576,256]{1,0:T(8,128)S(1)} custom-call(s32[3,12]{1,0:T(4,128)S(1)} %copy-done.7, s32[3]{0:T(128)S(1)} %copy-done.9, s32[2]{0:T(128)S(1)} %pad_add_fusion.refs_2_.refs_3_, bf16[3,12,192,192]{3,2,1,0:T(8,128)(2,1)S(1)} %copy-done.1, bf16[1,576,256]{2,1,0:T(8,128)(2,1)} %bitcast.13.refs_4_, bf16[1,576,256]{2,1,0:T(8,128)(2,1)} %bitcast.14.refs_5_), custom_call_target="tpu_custom_call" | custom-call | flops 339738624 | bytes 4423680 | tf_op jit(solution)/shard_map/pallas_call | solution.py:439
  50.7 2.1 %shard_map.81.refs_7_ = f32[576,256]{1,0:T(8,128)S(1)} custom-call(s32[3,12]{1,0:T(4,128)S(1)} %copy-done.7, s32[3]{0:T(128)S(1)} %copy-done.9, s32[2,6]{1,0:T(2,128)S(1)} %maximum_convert_fusion.refs_2_, s32[2]{0:T(128)S(1)} %pad_add_fusion.refs_2_.refs_3_, bf16[3,12,192,192]{3,2,1,0:T(8,128)(2,1)S(1)} %copy-done.1, bf16[1,576,256]{2,1,0:T(8,128)(2,1)} %bitcast.11.refs_5_, ...), custom_call_target="tpu_custom_call" | custom-call | flops 339738624 | bytes 4423680 | tf_op jit(solution)/shard_map/pallas_call | solution.py:447
  52.9 2.0 %shard_map.82 = (f32[576,256]{1,0:T(8,128)S(1)}, bf16[576,256]{1,0:T(8,128)(2,1)S(1)}) custom-call(s32[3,12]{1,0:T(4,128)S(1)} %copy-done.7, s32[3]{0:T(128)S(1)} %copy-done.9, s32[2,6]{1,0:T(2,128)S(1)} %maximum_convert_fusion.refs_2_, s32[2]{0:T(128)S(1)} %pad_add_fusion.refs_2_.refs_3_, bf16[3,12,192,192]{3,2,1,0:T(8,128)(2,1)S(1)} %copy-done.1, ...), custom_call_target="tpu_custom_call" | custom-call | flops 339738624 | bytes 4423680 | tf_op jit(solution)/shard_map/pallas_call | solution.py:447
  60.3 5.0 %collective-permute-start.14 = (bf16[576,256]{1,0:T(8,128)(2,1)S(1)}, bf16[576,256]{1,0:T(8,128)(2,1)S(1)}, u32[]{:S(2)}, u32[]{:S(2)}) collective-permute-start(bf16[576,256]{1,0:T(8,128)(2,1)S(1)} %get-tuple-element.73), channel_id=1, source_target_pairs={{0,30},{2,0},{4,2},{6,4},{8,6},{10,8},{12,10},{14,12},{16,14},{18,... | collective-permute-start | bytes 884744 | tf_op jit(solution)/shard_map/ppermute | solution.py:27
  65.3 6.0 %collective-permute-done.17 = f32[96,128]{1,0:T(8,128)S(1)} collective-permute-done((f32[96,128]{1,0:T(8,128)S(1)}, f32[96,128]{1,0:T(8,128)S(1)}, u32[]{:S(2)}, u32[]{:S(2)}) %collective-permute-start.17) | collective-permute-done | bytes 49184 | tf_op jit(solution)/shard_map/ppermute | solution.py:307
  71.3 4.4 %collective-permute-start.16 = (bf16[576,256]{1,0:T(8,128)(2,1)S(1)}, bf16[576,256]{1,0:T(8,128)(2,1)S(1)}, u32[]{:S(2)}, u32[]{:S(2)}) collective-permute-start(bf16[576,256]{1,0:T(8,128)(2,1)S(1)} %get-tuple-element.73), channel_id=1, source_target_pairs={{0,1},{1,0},{2,3},{3,2},{4,5},{5,4},{6,7},{7,6},{8,9},{9,8},{10,11... | collective-permute-start | bytes 884744 | tf_op jit(solution)/shard_map/ppermute | solution.py:377
  75.8 2.9 %collective-permute-done.19 = f32[96,128]{1,0:T(8,128)S(1)} collective-permute-done((f32[96,128]{1,0:T(8,128)S(1)}, f32[96,128]{1,0:T(8,128)S(1)}, u32[]{:S(2)}, u32[]{:S(2)}) %collective-permute-start.19) | collective-permute-done | bytes 49184 | tf_op jit(solution)/shard_map/ppermute | solution.py:307
  78.9 4.5 %collective-permute-start.11 = (bf16[576,256]{1,0:T(8,128)(2,1)S(1)}, bf16[576,256]{1,0:T(8,128)(2,1)S(1)}, u32[]{:S(2)}, u32[]{:S(2)}) collective-permute-start(bf16[576,256]{1,0:T(8,128)(2,1)S(1)} %collective-permute-done.10), channel_id=1, source_target_pairs={{0,1},{1,0},{2,3},{3,2},{4,5},{5,4},{6,7},{7,6},{8,9},{9,8},{10,11... | collective-permute-start | bytes 884744 | tf_op jit(solution)/shard_map/ppermute | solution.py:377
  83.5 4.0 %collective-permute-start.21 = (f32[192,128]{1,0:T(8,128)S(1)}, f32[192,128]{1,0:T(8,128)S(1)}, u32[]{:S(2)}, u32[]{:S(2)}) collective-permute-start(f32[192,128]{1,0:T(8,128)S(1)} %pad_maximum_fusion.3), channel_id=1, source_target_pairs={{0,1},{1,0},{2,3},{3,2},{4,5},{5,4},{6,7},{7,6},{8,9},{9,8},{10,11... | collective-permute-start | bytes 294920 | tf_op jit(solution)/shard_map/ppermute | solution.py:307
  88.8 1.5 %shard_map.85.refs_7_ = f32[576,256]{1,0:T(8,128)S(1)} custom-call(s32[3,12]{1,0:T(4,128)S(1)} %copy-done.7, s32[3]{0:T(128)S(1)} %copy-done.9, s32[2,6]{1,0:T(2,128)S(1)} %maximum_convert_fusion.refs_2_, s32[2]{0:T(128)S(1)} %pad_add_fusion.refs_2_.refs_3_, bf16[3,12,192,192]{3,2,1,0:T(8,128)(2,1)S(1)} %copy-done.1, bf16[1,576,256]{2,1,0:T(8,128)(2,1)S(1)} %bitcast.26, ...), custom_call_target="tpu_custom_call" | custom-call | flops 339738624 | bytes 4423680 | tf_op jit(solution)/shard_map/pallas_call | solution.py:447
  90.3 3.1 %shard_map.86 = f32[256,256]{1,0:T(8,128)S(1)} custom-call(s32[3,12]{1,0:T(4,128)S(1)} %copy-done.7, s32[3]{0:T(128)S(1)} %copy-done.9, s32[2,6]{1,0:T(2,128)S(1)} %maximum_convert_fusion.refs_2_, s32[2]{0:T(128)S(1)} %pad_add_fusion.refs_2_.refs_3_, bf16[3,12,192,192]{3,2,1,0:T(8,128)(2,1)S(1)} %copy-done.1, bf16[1,576,256]{2,1,0:T(8,128)(2,1)S(1)} %bitcast.29, ...), custom_call_target="tpu_custom_call" | custom-call | flops 339738624 | bytes 4423680 | tf_op jit(solution)/shard_map/pallas_call | solution.py:447
  93.6 1.5 %shard_map.88.tile_ref = f32[128,128]{1,0:T(8,128)S(1)} custom-call(f32[128,128]{1,0:T(8,128)S(1)} %get-tuple-element.77.tile_ref), custom_call_target="tpu_custom_call" | custom-call | flops 2000000000 | bytes 16384 | tf_op jit(solution)/shard_map/pallas_call | solution.py:273
  96.4 1.7 %shard_map.90.refs_0_ = f32[128,128]{1,0:T(8,128)S(1)} custom-call(f32[128,128]{1,0:T(8,128)S(1)} %shard_map.89.tile_ref), custom_call_target="tpu_custom_call" | custom-call | flops 2000000000 | bytes 16384 | tf_op jit(solution)/shard_map/pallas_call | solution.py:273
  98.3 2.3 %collective-permute-start.24 = (f32[64,256]{1,0:T(8,128)S(1)}, f32[64,256]{1,0:T(8,128)S(1)}, u32[]{:S(2)}, u32[]{:S(2)}) collective-permute-start(f32[64,256]{1,0:T(8,128)S(1)} %slice_add_fusion.2), channel_id=1, source_target_pairs={{0,8},{2,10},{4,12},{6,14},{8,0},{10,2},{12,4},{14,6},{16,24},{18,... | collective-permute-start | bytes 196616 | tf_op jit(solution)/shard_map/ppermute | solution.py:307
  103.0 1.5 %shard_map.92.tile_ref = f32[128,128]{1,0:T(8,128)S(1)} custom-call(f32[128,128]{1,0:T(8,128)S(1)} %get-tuple-element.106.tile_ref), custom_call_target="tpu_custom_call" | custom-call | flops 2000000000 | bytes 16384 | tf_op jit(solution)/shard_map/pallas_call | solution.py:273
  104.5 1.9 %collective-permute-done.25 = f32[64,256]{1,0:T(8,128)S(1)} collective-permute-done((f32[64,256]{1,0:T(8,128)S(1)}, f32[64,256]{1,0:T(8,128)S(1)}, u32[]{:S(2)}, u32[]{:S(2)}) %collective-permute-start.25) | collective-permute-done | bytes 65568 | tf_op jit(solution)/shard_map/ppermute | solution.py:307
  107.7 1.9 %collective-permute-done.26 = f32[64,256]{1,0:T(8,128)S(1)} collective-permute-done((f32[64,256]{1,0:T(8,128)S(1)}, f32[64,256]{1,0:T(8,128)S(1)}, u32[]{:S(2)}, u32[]{:S(2)}) %collective-permute-start.26) | collective-permute-done | bytes 65568 | tf_op jit(solution)/shard_map/ppermute | solution.py:307
  110.9 1.7 %shard_map.94.refs_2_ = f32[128,128]{1,0:T(8,128)S(1)} custom-call(f32[128,128]{1,0:T(8,128)S(1)} %shard_map.93.tile_ref), custom_call_target="tpu_custom_call" | custom-call | flops 2000000000 | bytes 16384 | tf_op jit(solution)/shard_map/pallas_call | solution.py:273
  112.8 6.0 %collective-permute-start.28 = (f32[128,256]{1,0:T(8,128)S(1)}, f32[128,256]{1,0:T(8,128)S(1)}, u32[]{:S(2)}, u32[]{:S(2)}) collective-permute-start(f32[128,256]{1,0:T(8,128)S(1)} %pad_maximum_fusion.2), channel_id=1, source_target_pairs={{0,1},{1,0},{2,3},{3,2},{4,5},{5,4},{6,7},{7,6},{8,9},{9,8},{10,11... | collective-permute-start | bytes 393224 | tf_op jit(solution)/shard_map/ppermute | solution.py:307
  118.8 1.9 %shard_map.95 = (f32[576,256]{1,0:T(8,128)}, f32[256,256]{1,0:T(8,128)S(1)}) custom-call(f32[128,128]{1,0:T(8,128)S(1)} %get-tuple-element.128.refs_0_, f32[128,128]{1,0:T(8,128)S(1)} %get-tuple-element.129.refs_1_, f32[128,128]{1,0:T(8,128)S(1)} %shard_map.94.refs_2_, f32[576,256]{1,0:T(8,128)S(1)} %get-tuple-element.72.two_ref.refs_9_.refs_3_), custom_call_target="tpu_custom_call" | custom-call | flops 2000000000 | bytes 147456 | tf_op jit(solution)/shard_map/pallas_call | solution.py:290
  120.7 1.7 %shard_map.96 = f32[256,256]{1,0:T(8,128)} custom-call(s32[1]{0:T(128)} %bitcast.16.number_ref.refs_8_, f32[256,256]{1,0:T(8,128)S(1)} %pad_maximum_fusion.cross_ref, f32[256,256]{1,0:T(8,128)S(1)} %get-tuple-element.135.inverse_ref), custom_call_target="tpu_custom_call" | custom-call | flops 150994944 | bytes 4423680 | tf_op jit(solution)/shard_map/pallas_call | solution.py:470
  (95 shorter events, 24.6 us)
Async XLA Ops:
  2.5 14.4 %collective-permute-start = (bf16[592,256]{1,0:T(8,128)(2,1)S(1)}, bf16[592,256]{1,0:T(8,128)(2,1)}, u32[]{:S(2)}, u32[]{:S(2)}) collective-permute-start(bf16[592,256]{1,0:T(8,128)(2,1)S(1)} %get-tuple-element.137), channel_id=1, source_target_pairs={{0,2},{2,4},{4,6},{6,8},{8,10},{10,12},{12,14},{14,16},{16,18},{18... | collective-permute-start | bytes 909320 | tf_op jit(solution)/shard_map/ppermute | solution.py:27
  4.6 14.4 %collective-permute-start.1 = (bf16[592,256]{1,0:T(8,128)(2,1)S(1)}, bf16[592,256]{1,0:T(8,128)(2,1)}, u32[]{:S(2)}, u32[]{:S(2)}) collective-permute-start(bf16[592,256]{1,0:T(8,128)(2,1)S(1)} %get-tuple-element.137), channel_id=1, source_target_pairs={{0,30},{2,0},{4,2},{6,4},{8,6},{10,8},{12,10},{14,12},{16,14},{18,... | collective-permute-start | bytes 909320 | tf_op jit(solution)/shard_map/ppermute | solution.py:27
  8.6 13.3 %collective-permute-start.4 = (bf16[592,256]{1,0:T(8,128)(2,1)S(1)}, bf16[592,256]{1,0:T(8,128)(2,1)S(1)}, u32[]{:S(2)}, u32[]{:S(2)}) collective-permute-start(bf16[592,256]{1,0:T(8,128)(2,1)S(1)} %get-tuple-element.137), channel_id=1, source_target_pairs={{0,1},{1,0},{2,3},{3,2},{4,5},{5,4},{6,7},{7,6},{8,9},{9,8},{10,11... | collective-permute-start | bytes 909320 | tf_op jit(solution)/shard_map/ppermute | solution.py:377
  16.9 11.8 %collective-permute-start.2 = (bf16[592,256]{1,0:T(8,128)(2,1)}, bf16[592,256]{1,0:T(8,128)(2,1)}, u32[]{:S(2)}, u32[]{:S(2)}) collective-permute-start(bf16[592,256]{1,0:T(8,128)(2,1)} %collective-permute-done), channel_id=1, source_target_pairs={{0,1},{1,0},{2,3},{3,2},{4,5},{5,4},{6,7},{7,6},{8,9},{9,8},{10,11... | collective-permute-start | bytes 909320 | tf_op jit(solution)/shard_map/ppermute | solution.py:377
  19.0 9.8 %collective-permute-start.3 = (bf16[592,256]{1,0:T(8,128)(2,1)}, bf16[592,256]{1,0:T(8,128)(2,1)}, u32[]{:S(2)}, u32[]{:S(2)}) collective-permute-start(bf16[592,256]{1,0:T(8,128)(2,1)} %collective-permute-done.1), channel_id=1, source_target_pairs={{0,1},{1,0},{2,3},{3,2},{4,5},{5,4},{6,7},{7,6},{8,9},{9,8},{10,11... | collective-permute-start | bytes 909320 | tf_op jit(solution)/shard_map/ppermute | solution.py:377
  28.7 20.2 %copy-start.1 = (bf16[3,12,192,192]{3,2,1,0:T(8,128)(2,1)S(1)}, bf16[3,12,192,192]{3,2,1,0:T(8,128)(2,1)}, u32[]{:S(2)}) copy-start(bf16[3,12,192,192]{3,2,1,0:T(8,128)(2,1)} %refs_4_.11) | copy-start | bytes 7962628
  28.7 20.2 %copy-start.7 = (s32[3,12]{1,0:T(4,128)S(1)}, s32[3,12]{1,0:T(4,128)}, u32[]{:S(2)}) copy-start(s32[3,12]{1,0:T(4,128)} %refs_0_.17) | copy-start | bytes 436
  28.7 20.2 %copy-start.9 = (s32[3]{0:T(128)S(1)}, s32[3]{0:T(128)}, u32[]{:S(2)}) copy-start(s32[3]{0:T(128)} %refs_1_.17) | copy-start | bytes 40
  32.4 9.8 %collective-permute-start.7 = (bf16[576,256]{1,0:T(8,128)(2,1)}, bf16[576,256]{1,0:T(8,128)(2,1)}, u32[]{:S(2)}, u32[]{:S(2)}) collective-permute-start(bf16[576,256]{1,0:T(8,128)(2,1)} %get-tuple-element.69), channel_id=1, source_target_pairs={{0,30},{2,0},{4,2},{6,4},{8,6},{10,8},{12,10},{14,12},{16,14},{18,... | collective-permute-start | bytes 884744 | tf_op jit(solution)/shard_map/ppermute | solution.py:27
  35.4 12.2 %collective-permute-start.5 = (bf16[576,256]{1,0:T(8,128)(2,1)}, bf16[576,256]{1,0:T(8,128)(2,1)}, u32[]{:S(2)}, u32[]{:S(2)}) collective-permute-start(bf16[576,256]{1,0:T(8,128)(2,1)} %get-tuple-element.69), channel_id=1, source_target_pairs={{0,2},{2,4},{4,6},{6,8},{8,10},{10,12},{12,14},{14,16},{16,18},{18... | collective-permute-start | bytes 884744 | tf_op jit(solution)/shard_map/ppermute | solution.py:27
  35.4 13.4 %collective-permute-start.9 = (bf16[576,256]{1,0:T(8,128)(2,1)}, bf16[576,256]{1,0:T(8,128)(2,1)}, u32[]{:S(2)}, u32[]{:S(2)}) collective-permute-start(bf16[576,256]{1,0:T(8,128)(2,1)} %get-tuple-element.69), channel_id=1, source_target_pairs={{0,1},{1,0},{2,3},{3,2},{4,5},{5,4},{6,7},{7,6},{8,9},{9,8},{10,11... | collective-permute-start | bytes 884744 | tf_op jit(solution)/shard_map/ppermute | solution.py:377
  42.2 10.6 %collective-permute-start.8 = (bf16[576,256]{1,0:T(8,128)(2,1)}, bf16[576,256]{1,0:T(8,128)(2,1)}, u32[]{:S(2)}, u32[]{:S(2)}) collective-permute-start(bf16[576,256]{1,0:T(8,128)(2,1)} %collective-permute-done.7), channel_id=1, source_target_pairs={{0,1},{1,0},{2,3},{3,2},{4,5},{5,4},{6,7},{7,6},{8,9},{9,8},{10,11... | collective-permute-start | bytes 884744 | tf_op jit(solution)/shard_map/ppermute | solution.py:377
  47.7 5.2 %collective-permute-start.6 = (bf16[576,256]{1,0:T(8,128)(2,1)}, bf16[576,256]{1,0:T(8,128)(2,1)}, u32[]{:S(2)}, u32[]{:S(2)}) collective-permute-start(bf16[576,256]{1,0:T(8,128)(2,1)} %collective-permute-done.5), channel_id=1, source_target_pairs={{0,1},{1,0},{2,3},{3,2},{4,5},{5,4},{6,7},{7,6},{8,9},{9,8},{10,11... | collective-permute-start | bytes 884744 | tf_op jit(solution)/shard_map/ppermute | solution.py:377
  55.9 1.4 %collective-permute-start.12 = (f32[192,128]{1,0:T(8,128)S(1)}, f32[192,128]{1,0:T(8,128)S(1)}, u32[]{:S(2)}, u32[]{:S(2)}) collective-permute-start(f32[192,128]{1,0:T(8,128)S(1)} %slice.43), channel_id=1, source_target_pairs={{0,1},{1,0},{2,3},{3,2},{4,5},{5,4},{6,7},{7,6},{8,9},{9,8},{10,11... | collective-permute-start | bytes 294920 | tf_op jit(solution)/shard_map/ppermute | solution.py:307
  57.3 3.0 %collective-permute-start.13 = (f32[96,128]{1,0:T(8,128)S(1)}, f32[96,128]{1,0:T(8,128)S(1)}, u32[]{:S(2)}, u32[]{:S(2)}) collective-permute-start(f32[96,128]{1,0:T(8,128)S(1)} %slice.45), channel_id=1, source_target_pairs={{0,4},{2,6},{4,0},{6,2},{8,12},{10,14},{12,8},{14,10},{16,20},{18,... | collective-permute-start | bytes 147464 | tf_op jit(solution)/shard_map/ppermute | solution.py:307
  58.6 20.3 %collective-permute-start.10 = (bf16[576,256]{1,0:T(8,128)(2,1)S(1)}, bf16[576,256]{1,0:T(8,128)(2,1)S(1)}, u32[]{:S(2)}, u32[]{:S(2)}) collective-permute-start(bf16[576,256]{1,0:T(8,128)(2,1)S(1)} %get-tuple-element.73), channel_id=1, source_target_pairs={{0,2},{2,4},{4,6},{6,8},{8,10},{10,12},{12,14},{14,16},{16,18},{18... | collective-permute-start | bytes 884744 | tf_op jit(solution)/shard_map/ppermute | solution.py:27
  60.3 23.1 %collective-permute-start.14 = (bf16[576,256]{1,0:T(8,128)(2,1)S(1)}, bf16[576,256]{1,0:T(8,128)(2,1)S(1)}, u32[]{:S(2)}, u32[]{:S(2)}) collective-permute-start(bf16[576,256]{1,0:T(8,128)(2,1)S(1)} %get-tuple-element.73), channel_id=1, source_target_pairs={{0,30},{2,0},{4,2},{6,4},{8,6},{10,8},{12,10},{14,12},{16,14},{18,... | collective-permute-start | bytes 884744 | tf_op jit(solution)/shard_map/ppermute | solution.py:27
  65.3 6.0 %collective-permute-start.17 = (f32[96,128]{1,0:T(8,128)S(1)}, f32[96,128]{1,0:T(8,128)S(1)}, u32[]{:S(2)}, u32[]{:S(2)}) collective-permute-start(f32[96,128]{1,0:T(8,128)S(1)} %slice_add_fusion.3), channel_id=1, source_target_pairs={{0,8},{2,10},{4,12},{6,14},{8,0},{10,2},{12,4},{14,6},{16,24},{18,... | collective-permute-start | bytes 147464 | tf_op jit(solution)/shard_map/ppermute | solution.py:307
  71.3 4.4 %collective-permute-start.18 = (f32[96,128]{1,0:T(8,128)S(1)}, f32[96,128]{1,0:T(8,128)S(1)}, u32[]{:S(2)}, u32[]{:S(2)}) collective-permute-start(f32[96,128]{1,0:T(8,128)S(1)} %add.49), channel_id=1, source_target_pairs={{0,16},{2,18},{4,20},{6,22},{8,24},{10,26},{12,28},{14,30},{16,0},... | collective-permute-start | bytes 147464 | tf_op jit(solution)/shard_map/ppermute | solution.py:307
  71.3 16.1 %collective-permute-start.16 = (bf16[576,256]{1,0:T(8,128)(2,1)S(1)}, bf16[576,256]{1,0:T(8,128)(2,1)S(1)}, u32[]{:S(2)}, u32[]{:S(2)}) collective-permute-start(bf16[576,256]{1,0:T(8,128)(2,1)S(1)} %get-tuple-element.73), channel_id=1, source_target_pairs={{0,1},{1,0},{2,3},{3,2},{4,5},{5,4},{6,7},{7,6},{8,9},{9,8},{10,11... | collective-permute-start | bytes 884744 | tf_op jit(solution)/shard_map/ppermute | solution.py:377
  75.7 3.0 %collective-permute-start.19 = (f32[96,128]{1,0:T(8,128)S(1)}, f32[96,128]{1,0:T(8,128)S(1)}, u32[]{:S(2)}, u32[]{:S(2)}) collective-permute-start(f32[96,128]{1,0:T(8,128)S(1)} %add.50), channel_id=1, source_target_pairs={{0,2},{2,0},{4,6},{6,4},{8,10},{10,8},{12,14},{14,12},{16,18},{18,... | collective-permute-start | bytes 147464 | tf_op jit(solution)/shard_map/ppermute | solution.py:307
  78.7 4.7 %collective-permute-start.20 = (f32[96,128]{1,0:T(8,128)S(1)}, f32[96,128]{1,0:T(8,128)S(1)}, u32[]{:S(2)}, u32[]{:S(2)}) collective-permute-start(f32[96,128]{1,0:T(8,128)S(1)} %add.51), channel_id=1, source_target_pairs={{0,4},{2,6},{4,0},{6,2},{8,12},{10,14},{12,8},{14,10},{16,20},{18,... | collective-permute-start | bytes 147464 | tf_op jit(solution)/shard_map/ppermute | solution.py:307
  78.9 11.4 %collective-permute-start.11 = (bf16[576,256]{1,0:T(8,128)(2,1)S(1)}, bf16[576,256]{1,0:T(8,128)(2,1)S(1)}, u32[]{:S(2)}, u32[]{:S(2)}) collective-permute-start(bf16[576,256]{1,0:T(8,128)(2,1)S(1)} %collective-permute-done.10), channel_id=1, source_target_pairs={{0,1},{1,0},{2,3},{3,2},{4,5},{5,4},{6,7},{7,6},{8,9},{9,8},{10,11... | collective-permute-start | bytes 884744 | tf_op jit(solution)/shard_map/ppermute | solution.py:377
  83.4 6.9 %collective-permute-start.15 = (bf16[576,256]{1,0:T(8,128)(2,1)S(1)}, bf16[576,256]{1,0:T(8,128)(2,1)S(1)}, u32[]{:S(2)}, u32[]{:S(2)}) collective-permute-start(bf16[576,256]{1,0:T(8,128)(2,1)S(1)} %collective-permute-done.14), channel_id=1, source_target_pairs={{0,1},{1,0},{2,3},{3,2},{4,5},{5,4},{6,7},{7,6},{8,9},{9,8},{10,11... | collective-permute-start | bytes 884744 | tf_op jit(solution)/shard_map/ppermute | solution.py:377
  83.5 6.8 %collective-permute-start.21 = (f32[192,128]{1,0:T(8,128)S(1)}, f32[192,128]{1,0:T(8,128)S(1)}, u32[]{:S(2)}, u32[]{:S(2)}) collective-permute-start(f32[192,128]{1,0:T(8,128)S(1)} %pad_maximum_fusion.3), channel_id=1, source_target_pairs={{0,1},{1,0},{2,3},{3,2},{4,5},{5,4},{6,7},{7,6},{8,9},{9,8},{10,11... | collective-permute-start | bytes 294920 | tf_op jit(solution)/shard_map/ppermute | solution.py:307
  93.5 1.6 %collective-permute-start.22 = (f32[128,256]{1,0:T(8,128)S(1)}, f32[128,256]{1,0:T(8,128)S(1)}, u32[]{:S(2)}, u32[]{:S(2)}) collective-permute-start(f32[128,256]{1,0:T(8,128)S(1)} %slice.37), channel_id=1, source_target_pairs={{0,1},{1,0},{2,3},{3,2},{4,5},{5,4},{6,7},{7,6},{8,9},{9,8},{10,11... | collective-permute-start | bytes 393224 | tf_op jit(solution)/shard_map/ppermute | solution.py:307
  95.1 3.2 %collective-permute-start.23 = (f32[64,256]{1,0:T(8,128)S(1)}, f32[64,256]{1,0:T(8,128)S(1)}, u32[]{:S(2)}, u32[]{:S(2)}) collective-permute-start(f32[64,256]{1,0:T(8,128)S(1)} %slice.39), channel_id=1, source_target_pairs={{0,4},{2,6},{4,0},{6,2},{8,12},{10,14},{12,8},{14,10},{16,20},{18,... | collective-permute-start | bytes 196616 | tf_op jit(solution)/shard_map/ppermute | solution.py:307
  98.3 4.0 %collective-permute-start.24 = (f32[64,256]{1,0:T(8,128)S(1)}, f32[64,256]{1,0:T(8,128)S(1)}, u32[]{:S(2)}, u32[]{:S(2)}) collective-permute-start(f32[64,256]{1,0:T(8,128)S(1)} %slice_add_fusion.2), channel_id=1, source_target_pairs={{0,8},{2,10},{4,12},{6,14},{8,0},{10,2},{12,4},{14,6},{16,24},{18,... | collective-permute-start | bytes 196616 | tf_op jit(solution)/shard_map/ppermute | solution.py:307
  102.3 4.1 %collective-permute-start.25 = (f32[64,256]{1,0:T(8,128)S(1)}, f32[64,256]{1,0:T(8,128)S(1)}, u32[]{:S(2)}, u32[]{:S(2)}) collective-permute-start(f32[64,256]{1,0:T(8,128)S(1)} %add.54), channel_id=1, source_target_pairs={{0,16},{2,18},{4,20},{6,22},{8,24},{10,26},{12,28},{14,30},{16,0},... | collective-permute-start | bytes 196616 | tf_op jit(solution)/shard_map/ppermute | solution.py:307
  106.4 3.2 %collective-permute-start.26 = (f32[64,256]{1,0:T(8,128)S(1)}, f32[64,256]{1,0:T(8,128)S(1)}, u32[]{:S(2)}, u32[]{:S(2)}) collective-permute-start(f32[64,256]{1,0:T(8,128)S(1)} %add.55), channel_id=1, source_target_pairs={{0,2},{2,0},{4,6},{6,4},{8,10},{10,8},{12,14},{14,12},{16,18},{18,... | collective-permute-start | bytes 196616 | tf_op jit(solution)/shard_map/ppermute | solution.py:307
  109.6 3.2 %collective-permute-start.27 = (f32[64,256]{1,0:T(8,128)S(1)}, f32[64,256]{1,0:T(8,128)S(1)}, u32[]{:S(2)}, u32[]{:S(2)}) collective-permute-start(f32[64,256]{1,0:T(8,128)S(1)} %add.56), channel_id=1, source_target_pairs={{0,4},{2,6},{4,0},{6,2},{8,12},{10,14},{12,8},{14,10},{16,20},{18,... | collective-permute-start | bytes 196616 | tf_op jit(solution)/shard_map/ppermute | solution.py:307
  112.8 7.8 %collective-permute-start.28 = (f32[128,256]{1,0:T(8,128)S(1)}, f32[128,256]{1,0:T(8,128)S(1)}, u32[]{:S(2)}, u32[]{:S(2)}) collective-permute-start(f32[128,256]{1,0:T(8,128)S(1)} %pad_maximum_fusion.2), channel_id=1, source_target_pairs={{0,1},{1,0},{2,3},{3,2},{4,5},{5,4},{6,7},{7,6},{8,9},{9,8},{10,11... | collective-permute-start | bytes 393224 | tf_op jit(solution)/shard_map/ppermute | solution.py:307
  (9 other events, 14.8 us)

commit v6 on v5

--- a/solution.py
+++ b/solution.py
@@ -18,7 +18,6 @@
 VMEM_LIMIT = 20 * 1024 * 1024
 LIST_ROWS = 16
 PIECES = 4
-EARLY = 2
 
 
 def shifted(value, axis, steps):
@@ -45,16 +44,14 @@
 
 def fill_slots(slots_ref, cols_ref, live_ref, first, place_of):
     rows, stored = cols_ref.shape
-    count = slots_ref.shape[1]
+    count = slots_ref.shape[1] - 1
     for row in range(rows):
         for index in range(count):
             slots_ref[row, index] = -1
         for at in range(stored):
             name = cols_ref[row, at] - first
-
-            @pl.when((name >= 0) & (name < count) & (at < live_ref[row]))
-            def _():
-                slots_ref[row, place_of(name)] = at
+            inside = (name >= 0) & (name < count) & (at < live_ref[row])
+            slots_ref[row, jnp.where(inside, place_of(jnp.clip(name, 0, count - 1)), count)] = at
 
 
 def accumulate(slots_ref, hessian_ref, operand_ref, base, total):
@@ -324,42 +321,42 @@
     return number.astype(jnp.int32).reshape(1)
 
 
-def sum_steps():
-    halved, doubled = halving_bits()
-
-    def halving(axis, bit):
-        send = lambda value: partner_value(value[value.shape[0] // 2 :], axis, bit)
-        return send, lambda value, got: value[: value.shape[0] // 2] + got
-
-    def doubling(axis, bit):
-        return lambda value: partner_value(value, axis, bit), lambda value, got: value + got
-
-    def joining(axis, bit):
-        send = lambda value: partner_value(value, axis, bit)
-        return send, lambda value, got: jnp.concatenate([value, got], 0)
-
-    steps = [halving(axis, bit) for axis, bit in halved]
-    steps += [doubling(axis, bit) for axis, bit in doubled]
-    return steps + [joining(axis, bit) for axis, bit in reversed(halved)]
-
-
-def run_steps(value, steps):
-    for send, join in steps:
-        value = join(value, send(value))
-    return value
+def halving(axis, bit):
+    def step(value):
+        half = value.shape[0] // 2
+        got = partner_value(value[half:], axis, bit)
+        return lambda: value[:half] + got
+
+    return step
+
+
+def doubling(axis, bit):
+    def step(value):
+        got = partner_value(value, axis, bit)
+        return lambda: value + got
+
+    return step
+
+
+def joining(axis, bit):
+    def step(value):
+        got = partner_value(value, axis, bit)
+        return lambda: jnp.concatenate([value, got], 0)
+
+    return step
 
 
 def run_beside(value, steps, state, stages):
     stages = list(stages)
-    for index, (send, join) in enumerate(steps):
+    for index, step in enumerate(steps):
         value, state = tied(value, state)
-        got = send(value)
+        join = step(value)
         due = -(-len(stages) // (len(steps) - index))
         for _ in range(due):
             state = stages.pop(0)(state)
+        value = join()
         if due:
-            got, state = tied(got, state)
-        value = join(value, got)
+            value, state = tied(value, state)
     return value, state
 
 
@@ -404,11 +401,10 @@
             return [operand[None], swapped(operand)[None]]
         return [lax.all_gather(operand, "split", axis=0)]
 
-    def exchange(operand, hold=lambda value: value):
+    def exchange(operand):
         near = near_parts(operand)
         up, down = sent(operand, near[0])
-        lower = shifted(up, "region", 1)
-        return near, lower, shifted(hold(down), "region", -1)
+        return near, shifted(up, "region", 1), shifted(down, "region", -1)
 
     first_near, first_lower, first_upper = exchange(first)
     if whole:
@@ -425,7 +421,7 @@
     square_work = 2 * rows * modes * modes
     traffic = hessian.size * 2 + 3 * rows * modes * 4
     number = device_number()
-    halo_slots = (row_blocks, 2 * halo_blocks)
+    halo_slots = (row_blocks, 2 * halo_blocks + 1)
 
     def step(body, outs, near, lower, upper, scalars, extra):
         call = kernel_call(
@@ -434,9 +430,10 @@
             [SMEM] * 3 + [VMEM] * (1 + len(near)),
             work * region_blocks,
             traffic,
-            (row_blocks, region_blocks),
+            (row_blocks, region_blocks + 1),
         )
         total = call(block_cols, live_blocks, bases, hessian, *near)
+        lower, upper, total = lax.optimization_barrier((lower, upper, total))
         pairs = list(zip(gathered(lower), gathered(upper)))
         for which, pair in enumerate(pairs):
             last = which == len(pairs) - 1
@@ -450,20 +447,28 @@
     one, one_cast = step(first_body, (wide, narrow), first_near, first_lower, first_upper, (bounds,), (vectors,))
     two, two_cast = step(second_body, (wide, narrow), *exchange(one_cast), (bounds,), (one, vectors))
 
-    steps = sum_steps()
+    (cores, across), doubled = halving_bits()
+    *between, near_chip = doubled
     packed = jax.ShapeDtypeStruct((tile_rows, TILE), jnp.float32)
+    third = exchange(two_cast)
     gram = kernel_call(gram_body, packed, [SMEM, VMEM], square_work, traffic)(number, two)
-    gram = run_steps(gram, steps[:EARLY])
-
-    def hold(value):
-        nonlocal gram
-        value, gram = tied(value, gram)
-        return value
-
-    third = exchange(two_cast, hold)
-    gram = run_steps(gram, steps[EARLY:])
+    for step_of in [halving(*cores), halving(*across)] + [doubling(*bit) for bit in between]:
+        gram = step_of(gram)()
     cross = step(third_body, square, *third, (number,), (two,))
+    cross = halving(*cores)(cross)()
+
+    fold = modes // TILE
+    cut = gram.shape[0] // fold
+    folded = jnp.concatenate([gram[at * cut : (at + 1) * cut] for at in range(fold)], 1)
+    flat = lambda value: [value[:, at * TILE : (at + 1) * TILE] for at in range(fold)]
+    both = doubling(*near_chip)(jnp.concatenate([folded, cross], 0))()
+    half = cut + cross.shape[0] // 2
+    got = partner_value(jnp.concatenate([both[:cut], both[half:]], 0), *across)
+    gram = jnp.concatenate(flat(both[:cut]) + flat(got[:cut]), 0)
+    cross = both[cut:half] + got[cut:]
+    gram = joining(*cores)(gram)()
     stages = factor_stages(float(total_rows), modes // TILE, number, two)
+    steps = [doubling(*bit) for bit in between] + [joining(*across), joining(*cores)]
     cross, (basis, inverse) = run_beside(cross, steps, gram, stages)
     body_of = functools.partial(projected_body, float(total_rows))
     call = kernel_call(body_of, square, [SMEM] + [VMEM] * 2, 2 * square_work, traffic)

time: 123 us -> 121 us (0.984)
  starting transfers between devices: 46.3 us -> 29 us
  waiting for transfers between devices: 35.3 us -> 52 us
  Pallas kernels: 32 us -> 29.9 us
  local copies, waits for them, and re-layouts: 5.58 us -> 6.83 us
    ppermute x9, starting transfers between devices: 15.3 us -> 4.1 us  [local(): swapped = lambda value: lax.ppermute(value, 'split', [(0, 1), (1, 0)])]
    ppermute x6, waiting for transfers between devices: 19 us -> 27.4 us  [shifted(): return lax.ppermute(value, axis, pairs)]
    ppermute x14 -> x12, waiting for transfers between devices: 16.4 us -> 24.5 us  [partner_value(): lax.ppermute(value, axis, [(at, at ^ bit) for at in range(lax.axis_size(a...]
    ppermute x14 -> x12, starting transfers between devices: 16.1 us -> 11.9 us  [partner_value(): lax.ppermute(value, axis, [(at, at ^ bit) for at in range(lax.axis_size(a...]
    unnamed x24 -> x30, local copies, waits for them, and re-layouts: 4.2 us -> 6.76 us
    ppermute x6, starting transfers between devices: 14.9 us -> 13.1 us  [shifted(): return lax.ppermute(value, axis, pairs)]
    pallas_call x6, Pallas kernels: 13.5 us -> 11.7 us  [step(): kernel_call(body_of, outs if last else wide, specs, cost, traffic, halo_s...]
  transfers between devices with their start and end apart: 29 -> 27, of which waited for: 13 -> 16; matrix products, arithmetic and copies ran while one was open for 1% -> 0% of each run, Pallas kernels for 17% -> 12%
where the time goes in v6:
time: 121 us
  waiting for transfers between devices  52 us (43%)
  Pallas kernels  29.9 us (25%)
  starting transfers between devices  29 us (24%)
  local copies, waits for them, and re-layouts  6.83 us (6%)
  other arithmetic  2.07 us (2%)
    ppermute x6, waiting for transfers between devices, shifted(): return lax.ppermute(value, axis, pairs)  27.4 us
    ppermute x12, waiting for transfers between devices, partner_value(): lax.ppermute(value, axis, [(at, at ^ bit) for at in range(lax.axis_size(a...  24.5 us
    ppermute x6, starting transfers between devices, shifted(): return lax.ppermute(value, axis, pairs)  13.1 us
    ppermute x12, starting transfers between devices, partner_value(): lax.ppermute(value, axis, [(at, at ^ bit) for at in range(lax.axis_size(a...  11.9 us
    pallas_call x6, Pallas kernels, step(): kernel_call(body_of, outs if last else wide, specs, cost, traffic, halo_s...  11.7 us
    pallas_call x6, Pallas kernels, stage(): return tiles[:place] + (call(tiles[place]),) + tiles[place + 1:]  8.78 us
    unnamed x30, local copies, waits for them, and re-layouts  6.76 us
    ppermute x9, starting transfers between devices, local(): swapped = lambda value: lax.ppermute(value, 'split', [(0, 1), (1, 0)])  4.1 us
  transfers between devices with their start and end apart: 27, of which 16 were waited for; matrix products, arithmetic and copies ran while one was open for 0% of the time, Pallas kernels for 12%

profile of v6, /device:TPU:1, one launch (start us, length us, event | category | flops | bytes accessed | tf_op | source)
XLA Modules:
  0.0 120.9 jit_solution(7975201076928929435)
XLA Ops:
  2.6 6.7 %collective-permute-start.1 = (bf16[592,256]{1,0:T(8,128)(2,1)S(1)}, bf16[592,256]{1,0:T(8,128)(2,1)S(1)}, u32[]{:S(2)}, u32[]{:S(2)}) collective-permute-start(bf16[592,256]{1,0:T(8,128)(2,1)S(1)} %get-tuple-element.79), channel_id=1, source_target_pairs={{0,30},{2,0},{4,2},{6,4},{8,6},{10,8},{12,10},{14,12},{16,14},{18,... | collective-permute-start | bytes 909320 | tf_op jit(solution)/shard_map/ppermute | solution.py:26
  9.3 2.0 %copy-done = bf16[3,12,192,192]{3,2,1,0:T(8,128)(2,1)S(1)} copy-done((bf16[3,12,192,192]{3,2,1,0:T(8,128)(2,1)S(1)}, bf16[3,12,192,192]{3,2,1,0:T(8,128)(2,1)}, u32[]{:S(2)}) %copy-start) | copy-done | bytes 2654232
  14.0 1.7 %collective-permute-done.1 = bf16[592,256]{1,0:T(8,128)(2,1)S(1)} collective-permute-done((bf16[592,256]{1,0:T(8,128)(2,1)S(1)}, bf16[592,256]{1,0:T(8,128)(2,1)S(1)}, u32[]{:S(2)}, u32[]{:S(2)}) %collective-permute-start.1) | collective-permute-done | bytes 303136 | tf_op jit(solution)/shard_map/ppermute | solution.py:26
  15.8 5.5 %collective-permute-done = bf16[592,256]{1,0:T(8,128)(2,1)S(1)} collective-permute-done((bf16[592,256]{1,0:T(8,128)(2,1)S(1)}, bf16[592,256]{1,0:T(8,128)(2,1)S(1)}, u32[]{:S(2)}, u32[]{:S(2)}) %collective-permute-start) | collective-permute-done | bytes 303136 | tf_op jit(solution)/shard_map/ppermute | solution.py:26
  22.5 1.5 %shard_map.78.refs_7_ = f32[576,256]{1,0:T(8,128)S(1)} custom-call(s32[3,12]{1,0:T(4,128)S(1)} %copy-done.8, s32[3]{0:T(128)S(1)} %copy-done.10, s32[2,6]{1,0:T(2,128)S(1)} %maximum_convert_fusion.refs_2_, s32[2]{0:T(128)S(1)} %pad_add_fusion.refs_2_.refs_3_, bf16[3,12,192,192]{3,2,1,0:T(8,128)(2,1)S(1)} %copy-done, bf16[1,592,256]{2,1,0:T(8,128)(2,1)S(1)} %bitcast.25, ...), custom_call_target="tpu_custom_call" | custom-call | flops 339738624 | bytes 4423680 | tf_op jit(solution)/shard_map/pallas_call | solution.py:444
  24.1 1.5 %shard_map.79 = (f32[576,256]{1,0:T(8,128)S(1)}, bf16[576,256]{1,0:T(8,128)(2,1)S(1)}) custom-call(s32[3,12]{1,0:T(4,128)S(1)} %copy-done.8, s32[3]{0:T(128)S(1)} %copy-done.10, s32[2,6]{1,0:T(2,128)S(1)} %maximum_convert_fusion.refs_2_, s32[2]{0:T(128)S(1)} %pad_add_fusion.refs_2_.refs_3_, bf16[3,12,192,192]{3,2,1,0:T(8,128)(2,1)S(1)} %copy-done, ...), custom_call_target="tpu_custom_call" | custom-call | flops 339738624 | bytes 4423680 | tf_op jit(solution)/shard_map/pallas_call | solution.py:444
  26.9 2.8 %collective-permute-start.6 = (bf16[576,256]{1,0:T(8,128)(2,1)S(1)}, bf16[576,256]{1,0:T(8,128)(2,1)}, u32[]{:S(2)}, u32[]{:S(2)}) collective-permute-start(bf16[576,256]{1,0:T(8,128)(2,1)S(1)} %get-tuple-element.43), channel_id=1, source_target_pairs={{0,30},{2,0},{4,2},{6,4},{8,6},{10,8},{12,10},{14,12},{16,14},{18,... | collective-permute-start | bytes 884744 | tf_op jit(solution)/shard_map/ppermute | solution.py:26
  31.9 4.2 %collective-permute-done.6 = bf16[576,256]{1,0:T(8,128)(2,1)} collective-permute-done((bf16[576,256]{1,0:T(8,128)(2,1)S(1)}, bf16[576,256]{1,0:T(8,128)(2,1)}, u32[]{:S(2)}, u32[]{:S(2)}) %collective-permute-start.6) | collective-permute-done | bytes 294944 | tf_op jit(solution)/shard_map/ppermute | solution.py:26
  36.1 5.6 %collective-permute-done.5 = bf16[576,256]{1,0:T(8,128)(2,1)} collective-permute-done((bf16[576,256]{1,0:T(8,128)(2,1)S(1)}, bf16[576,256]{1,0:T(8,128)(2,1)}, u32[]{:S(2)}, u32[]{:S(2)}) %collective-permute-start.5) | collective-permute-done | bytes 294944 | tf_op jit(solution)/shard_map/ppermute | solution.py:26
  44.0 2.0 %shard_map.81.refs_7_ = f32[576,256]{1,0:T(8,128)S(1)} custom-call(s32[3,12]{1,0:T(4,128)S(1)} %copy-done.9, s32[3]{0:T(128)S(1)} %copy-done.11, s32[2,6]{1,0:T(2,128)S(1)} %maximum_convert_fusion.refs_2_, s32[2]{0:T(128)S(1)} %pad_add_fusion.refs_2_.refs_3_, bf16[3,12,192,192]{3,2,1,0:T(8,128)(2,1)S(1)} %copy-done.1, bf16[1,576,256]{2,1,0:T(8,128)(2,1)} %bitcast.14.refs_5_, ...), custom_call_target="tpu_custom_call" | custom-call | flops 339738624 | bytes 4423680 | tf_op jit(solution)/shard_map/pallas_call | solution.py:444
  46.8 2.0 %shard_map.82 = (f32[576,256]{1,0:T(8,128)S(1)}, bf16[576,256]{1,0:T(8,128)(2,1)S(1)}) custom-call(s32[3,12]{1,0:T(4,128)S(1)} %copy-done.9, s32[3]{0:T(128)S(1)} %copy-done.11, s32[2,6]{1,0:T(2,128)S(1)} %maximum_convert_fusion.refs_2_, s32[2]{0:T(128)S(1)} %pad_add_fusion.refs_2_.refs_3_, bf16[3,12,192,192]{3,2,1,0:T(8,128)(2,1)S(1)} %copy-done.1, ...), custom_call_target="tpu_custom_call" | custom-call | flops 339738624 | bytes 4423680 | tf_op jit(solution)/shard_map/pallas_call | solution.py:444
  50.5 3.6 %collective-permute-start.15 = (bf16[576,256]{1,0:T(8,128)(2,1)S(1)}, bf16[576,256]{1,0:T(8,128)(2,1)S(1)}, u32[]{:S(2)}, u32[]{:S(2)}) collective-permute-start(bf16[576,256]{1,0:T(8,128)(2,1)S(1)} %get-tuple-element.49), channel_id=1, source_target_pairs={{0,30},{2,0},{4,2},{6,4},{8,6},{10,8},{12,10},{14,12},{16,14},{18,... | collective-permute-start | bytes 884744 | tf_op jit(solution)/shard_map/ppermute | solution.py:26
  55.5 4.5 %collective-permute-done.15 = bf16[576,256]{1,0:T(8,128)(2,1)S(1)} collective-permute-done((bf16[576,256]{1,0:T(8,128)(2,1)S(1)}, bf16[576,256]{1,0:T(8,128)(2,1)S(1)}, u32[]{:S(2)}, u32[]{:S(2)}) %collective-permute-start.15) | collective-permute-done | bytes 294944 | tf_op jit(solution)/shard_map/ppermute | solution.py:26
  60.0 6.0 %collective-permute-done.14 = bf16[576,256]{1,0:T(8,128)(2,1)S(1)} collective-permute-done((bf16[576,256]{1,0:T(8,128)(2,1)S(1)}, bf16[576,256]{1,0:T(8,128)(2,1)S(1)}, u32[]{:S(2)}, u32[]{:S(2)}) %collective-permute-start.14) | collective-permute-done | bytes 294944 | tf_op jit(solution)/shard_map/ppermute | solution.py:26
  67.2 2.9 %collective-permute-done.12 = f32[96,128]{1,0:T(8,128)S(1)} collective-permute-done((f32[96,128]{1,0:T(8,128)S(1)}, f32[96,128]{1,0:T(8,128)S(1)}, u32[]{:S(2)}, u32[]{:S(2)}) %collective-permute-start.12) | collective-permute-done | bytes 49184 | tf_op jit(solution)/shard_map/ppermute | solution.py:304
  70.2 4.1 %collective-permute-done.13 = f32[96,128]{1,0:T(8,128)S(1)} collective-permute-done((f32[96,128]{1,0:T(8,128)S(1)}, f32[96,128]{1,0:T(8,128)S(1)}, u32[]{:S(2)}, u32[]{:S(2)}) %collective-permute-start.13) | collective-permute-done | bytes 49184 | tf_op jit(solution)/shard_map/ppermute | solution.py:304
  74.2 1.5 %shard_map.85.refs_7_ = f32[576,256]{1,0:T(8,128)S(1)} custom-call(s32[3,12]{1,0:T(4,128)S(1)} %copy-done.9, s32[3]{0:T(128)S(1)} %copy-done.11, s32[2,6]{1,0:T(2,128)S(1)} %maximum_convert_fusion.refs_2_, s32[2]{0:T(128)S(1)} %pad_add_fusion.refs_2_.refs_3_, bf16[3,12,192,192]{3,2,1,0:T(8,128)(2,1)S(1)} %copy-done.1, bf16[1,576,256]{2,1,0:T(8,128)(2,1)S(1)} %bitcast.30, ...), custom_call_target="tpu_custom_call" | custom-call | flops 339738624 | bytes 4423680 | tf_op jit(solution)/shard_map/pallas_call | solution.py:444
  75.8 3.1 %shard_map.86 = f32[256,256]{1,0:T(8,128)S(1)} custom-call(s32[3,12]{1,0:T(4,128)S(1)} %copy-done.9, s32[3]{0:T(128)S(1)} %copy-done.11, s32[2,6]{1,0:T(2,128)S(1)} %maximum_convert_fusion.refs_2_, s32[2]{0:T(128)S(1)} %pad_add_fusion.refs_2_.refs_3_, bf16[3,12,192,192]{3,2,1,0:T(8,128)(2,1)S(1)} %copy-done.1, bf16[1,576,256]{2,1,0:T(8,128)(2,1)S(1)} %bitcast.32, ...), custom_call_target="tpu_custom_call" | custom-call | flops 339738624 | bytes 4423680 | tf_op jit(solution)/shard_map/pallas_call | solution.py:444
  78.9 2.6 %collective-permute-start.19 = (f32[128,256]{1,0:T(8,128)S(1)}, f32[128,256]{1,0:T(8,128)S(1)}, u32[]{:S(2)}, u32[]{:S(2)}) collective-permute-start(f32[128,256]{1,0:T(8,128)S(1)} %slice.87), channel_id=1, source_target_pairs={{0,1},{1,0},{2,3},{3,2},{4,5},{5,4},{6,7},{7,6},{8,9},{9,8},{10,11... | collective-permute-start | bytes 393224 | tf_op jit(solution)/shard_map/ppermute | solution.py:304
  82.6 2.2 %collective-permute-start.20 = (f32[176,256]{1,0:T(8,128)S(1)}, f32[176,256]{1,0:T(8,128)S(1)}, u32[]{:S(2)}, u32[]{:S(2)}) collective-permute-start(f32[176,256]{1,0:T(8,128)S(1)} %pad_maximum_fusion.1), channel_id=1, source_target_pairs={{0,2},{2,0},{4,6},{6,4},{8,10},{10,8},{12,14},{14,12},{16,18},{18,... | collective-permute-start | bytes 540680 | tf_op jit(solution)/shard_map/ppermute | solution.py:304
  84.8 4.6 %collective-permute-done.20 = f32[176,256]{1,0:T(8,128)S(1)} collective-permute-done((f32[176,256]{1,0:T(8,128)S(1)}, f32[176,256]{1,0:T(8,128)S(1)}, u32[]{:S(2)}, u32[]{:S(2)}) %collective-permute-start.20) | collective-permute-done | bytes 180256 | tf_op jit(solution)/shard_map/ppermute | solution.py:304
  89.6 3.6 %collective-permute-done.21 = f32[112,256]{1,0:T(8,128)S(1)} collective-permute-done((f32[112,256]{1,0:T(8,128)S(1)}, f32[112,256]{1,0:T(8,128)S(1)}, u32[]{:S(2)}, u32[]{:S(2)}) %collective-permute-start.21) | collective-permute-done | bytes 114720 | tf_op jit(solution)/shard_map/ppermute | solution.py:304
  93.2 2.1 %collective-permute-start.22 = (f32[192,128]{1,0:T(8,128)S(1)}, f32[192,128]{1,0:T(8,128)S(1)}, u32[]{:S(2)}, u32[]{:S(2)}) collective-permute-start(f32[192,128]{1,0:T(8,128)S(1)} %pad_maximum_fusion.4), channel_id=1, source_target_pairs={{0,1},{1,0},{2,3},{3,2},{4,5},{5,4},{6,7},{7,6},{8,9},{9,8},{10,11... | collective-permute-start | bytes 294920 | tf_op jit(solution)/shard_map/ppermute | solution.py:304
  96.3 1.5 %shard_map.88.tile_ref = f32[128,128]{1,0:T(8,128)S(1)} custom-call(f32[128,128]{1,0:T(8,128)S(1)} %get-tuple-element.55.tile_ref), custom_call_target="tpu_custom_call" | custom-call | flops 2000000000 | bytes 16384 | tf_op jit(solution)/shard_map/pallas_call | solution.py:270
  99.1 1.8 %collective-permute-done.23 = f32[64,256]{1,0:T(8,128)S(1)} collective-permute-done((f32[64,256]{1,0:T(8,128)S(1)}, f32[64,256]{1,0:T(8,128)S(1)}, u32[]{:S(2)}, u32[]{:S(2)}) %collective-permute-start.23) | collective-permute-done | bytes 65568 | tf_op jit(solution)/shard_map/ppermute | solution.py:304
  100.9 1.7 %shard_map.90.refs_0_ = f32[128,128]{1,0:T(8,128)S(1)} custom-call(f32[128,128]{1,0:T(8,128)S(1)} %shard_map.89.tile_ref), custom_call_target="tpu_custom_call" | custom-call | flops 2000000000 | bytes 16384 | tf_op jit(solution)/shard_map/pallas_call | solution.py:270
  103.8 3.6 %collective-permute-done.24 = f32[64,256]{1,0:T(8,128)S(1)} collective-permute-done((f32[64,256]{1,0:T(8,128)S(1)}, f32[64,256]{1,0:T(8,128)S(1)}, u32[]{:S(2)}, u32[]{:S(2)}) %collective-permute-start.24) | collective-permute-done | bytes 65568 | tf_op jit(solution)/shard_map/ppermute | solution.py:304
  110.2 1.8 %collective-permute-done.25 = f32[64,256]{1,0:T(8,128)S(1)} collective-permute-done((f32[64,256]{1,0:T(8,128)S(1)}, f32[64,256]{1,0:T(8,128)S(1)}, u32[]{:S(2)}, u32[]{:S(2)}) %collective-permute-start.25) | collective-permute-done | bytes 65568 | tf_op jit(solution)/shard_map/ppermute | solution.py:304
  112.1 1.7 %shard_map.94.refs_2_ = f32[128,128]{1,0:T(8,128)S(1)} custom-call(f32[128,128]{1,0:T(8,128)S(1)} %shard_map.93.tile_ref), custom_call_target="tpu_custom_call" | custom-call | flops 2000000000 | bytes 16384 | tf_op jit(solution)/shard_map/pallas_call | solution.py:270
  113.8 3.5 %collective-permute-start.26 = (f32[128,256]{1,0:T(8,128)S(1)}, f32[128,256]{1,0:T(8,128)S(1)}, u32[]{:S(2)}, u32[]{:S(2)}) collective-permute-start(f32[128,256]{1,0:T(8,128)S(1)} %pad_maximum_fusion.2), channel_id=1, source_target_pairs={{0,1},{1,0},{2,3},{3,2},{4,5},{5,4},{6,7},{7,6},{8,9},{9,8},{10,11... | collective-permute-start | bytes 393224 | tf_op jit(solution)/shard_map/ppermute | solution.py:304
  117.3 1.9 %shard_map.95 = (f32[576,256]{1,0:T(8,128)}, f32[256,256]{1,0:T(8,128)S(1)}) custom-call(f32[128,128]{1,0:T(8,128)S(1)} %get-tuple-element.70.refs_0_, f32[128,128]{1,0:T(8,128)S(1)} %get-tuple-element.71.refs_1_, f32[128,128]{1,0:T(8,128)S(1)} %shard_map.94.refs_2_, f32[576,256]{1,0:T(8,128)S(1)} %get-tuple-element.48.two_ref.refs_9_.refs_3_), custom_call_target="tpu_custom_call" | custom-call | flops 2000000000 | bytes 147456 | tf_op jit(solution)/shard_map/pallas_call | solution.py:287
  119.2 1.7 %shard_map.96 = f32[256,256]{1,0:T(8,128)} custom-call(s32[1]{0:T(128)} %bitcast.number_ref.refs_8_, f32[256,256]{1,0:T(8,128)S(1)} %pad_maximum_fusion.cross_ref, f32[256,256]{1,0:T(8,128)S(1)} %get-tuple-element.77.inverse_ref), custom_call_target="tpu_custom_call" | custom-call | flops 150994944 | bytes 4423680 | tf_op jit(solution)/shard_map/pallas_call | solution.py:475
  (102 shorter events, 24.3 us)
Async XLA Ops:
  2.5 6.9 %collective-permute-start.2 = (bf16[592,256]{1,0:T(8,128)(2,1)S(1)}, bf16[592,256]{1,0:T(8,128)(2,1)S(1)}, u32[]{:S(2)}, u32[]{:S(2)}) collective-permute-start(bf16[592,256]{1,0:T(8,128)(2,1)S(1)} %get-tuple-element.79), channel_id=1, source_target_pairs={{0,1},{1,0},{2,3},{3,2},{4,5},{5,4},{6,7},{7,6},{8,9},{9,8},{10,11... | collective-permute-start | bytes 909320 | tf_op jit(solution)/shard_map/ppermute | solution.py:374
  2.6 13.2 %collective-permute-start.1 = (bf16[592,256]{1,0:T(8,128)(2,1)S(1)}, bf16[592,256]{1,0:T(8,128)(2,1)S(1)}, u32[]{:S(2)}, u32[]{:S(2)}) collective-permute-start(bf16[592,256]{1,0:T(8,128)(2,1)S(1)} %get-tuple-element.79), channel_id=1, source_target_pairs={{0,30},{2,0},{4,2},{6,4},{8,6},{10,8},{12,10},{14,12},{16,14},{18,... | collective-permute-start | bytes 909320 | tf_op jit(solution)/shard_map/ppermute | solution.py:26
  9.2 12.0 %collective-permute-start = (bf16[592,256]{1,0:T(8,128)(2,1)S(1)}, bf16[592,256]{1,0:T(8,128)(2,1)S(1)}, u32[]{:S(2)}, u32[]{:S(2)}) collective-permute-start(bf16[592,256]{1,0:T(8,128)(2,1)S(1)} %get-tuple-element.79), channel_id=1, source_target_pairs={{0,2},{2,4},{4,6},{6,8},{8,10},{10,12},{12,14},{14,16},{16,18},{18... | collective-permute-start | bytes 909320 | tf_op jit(solution)/shard_map/ppermute | solution.py:26
  14.0 10.1 %copy-start.2 = (f32[576,256]{1,0:T(8,128)S(1)}, f32[576,256]{1,0:T(8,128)}, u32[]{:S(2)}) copy-start(f32[576,256]{1,0:T(8,128)} %refs_10_.1) | copy-start | bytes 1769476
  14.0 10.1 %copy-start.12 = (f32[2]{0:T(128)S(1)}, f32[2]{0:T(128)}, u32[]{:S(2)}) copy-start(f32[2]{0:T(128)} %refs_8_.3) | copy-start | bytes 28
  21.3 2.7 %collective-permute-start.3 = (bf16[592,256]{1,0:T(8,128)(2,1)S(1)}, bf16[592,256]{1,0:T(8,128)(2,1)S(1)}, u32[]{:S(2)}, u32[]{:S(2)}) collective-permute-start(bf16[592,256]{1,0:T(8,128)(2,1)S(1)} %collective-permute-done), channel_id=1, source_target_pairs={{0,1},{1,0},{2,3},{3,2},{4,5},{5,4},{6,7},{7,6},{8,9},{9,8},{10,11... | collective-permute-start | bytes 909320 | tf_op jit(solution)/shard_map/ppermute | solution.py:374
  22.4 1.7 %collective-permute-start.4 = (bf16[592,256]{1,0:T(8,128)(2,1)S(1)}, bf16[592,256]{1,0:T(8,128)(2,1)S(1)}, u32[]{:S(2)}, u32[]{:S(2)}) collective-permute-start(bf16[592,256]{1,0:T(8,128)(2,1)S(1)} %collective-permute-done.1), channel_id=1, source_target_pairs={{0,1},{1,0},{2,3},{3,2},{4,5},{5,4},{6,7},{7,6},{8,9},{9,8},{10,11... | collective-permute-start | bytes 909320 | tf_op jit(solution)/shard_map/ppermute | solution.py:374
  26.4 16.4 %copy-start.1 = (bf16[3,12,192,192]{3,2,1,0:T(8,128)(2,1)S(1)}, bf16[3,12,192,192]{3,2,1,0:T(8,128)(2,1)}, u32[]{:S(2)}) copy-start(bf16[3,12,192,192]{3,2,1,0:T(8,128)(2,1)} %refs_4_.11) | copy-start | bytes 7962628
  26.4 16.4 %copy-start.9 = (s32[3,12]{1,0:T(4,128)S(1)}, s32[3,12]{1,0:T(4,128)}, u32[]{:S(2)}) copy-start(s32[3,12]{1,0:T(4,128)} %refs_0_.17) | copy-start | bytes 436
  26.4 16.4 %copy-start.11 = (s32[3]{0:T(128)S(1)}, s32[3]{0:T(128)}, u32[]{:S(2)}) copy-start(s32[3]{0:T(128)} %refs_1_.17) | copy-start | bytes 40
  26.4 3.3 %collective-permute-start.7 = (bf16[576,256]{1,0:T(8,128)(2,1)S(1)}, bf16[576,256]{1,0:T(8,128)(2,1)S(1)}, u32[]{:S(2)}, u32[]{:S(2)}) collective-permute-start(bf16[576,256]{1,0:T(8,128)(2,1)S(1)} %get-tuple-element.43), channel_id=1, source_target_pairs={{0,1},{1,0},{2,3},{3,2},{4,5},{5,4},{6,7},{7,6},{8,9},{9,8},{10,11... | collective-permute-start | bytes 884744 | tf_op jit(solution)/shard_map/ppermute | solution.py:374
  26.9 9.2 %collective-permute-start.6 = (bf16[576,256]{1,0:T(8,128)(2,1)S(1)}, bf16[576,256]{1,0:T(8,128)(2,1)}, u32[]{:S(2)}, u32[]{:S(2)}) collective-permute-start(bf16[576,256]{1,0:T(8,128)(2,1)S(1)} %get-tuple-element.43), channel_id=1, source_target_pairs={{0,30},{2,0},{4,2},{6,4},{8,6},{10,8},{12,10},{14,12},{16,14},{18,... | collective-permute-start | bytes 884744 | tf_op jit(solution)/shard_map/ppermute | solution.py:26
  29.7 12.0 %collective-permute-start.5 = (bf16[576,256]{1,0:T(8,128)(2,1)S(1)}, bf16[576,256]{1,0:T(8,128)(2,1)}, u32[]{:S(2)}, u32[]{:S(2)}) collective-permute-start(bf16[576,256]{1,0:T(8,128)(2,1)S(1)} %get-tuple-element.43), channel_id=1, source_target_pairs={{0,2},{2,4},{4,6},{6,8},{8,10},{10,12},{12,14},{14,16},{16,18},{18... | collective-permute-start | bytes 884744 | tf_op jit(solution)/shard_map/ppermute | solution.py:26
  41.7 4.4 %collective-permute-start.8 = (bf16[576,256]{1,0:T(8,128)(2,1)}, bf16[576,256]{1,0:T(8,128)(2,1)}, u32[]{:S(2)}, u32[]{:S(2)}) collective-permute-start(bf16[576,256]{1,0:T(8,128)(2,1)} %collective-permute-done.5), channel_id=1, source_target_pairs={{0,1},{1,0},{2,3},{3,2},{4,5},{5,4},{6,7},{7,6},{8,9},{9,8},{10,11... | collective-permute-start | bytes 884744 | tf_op jit(solution)/shard_map/ppermute | solution.py:374
  42.9 3.2 %collective-permute-start.9 = (bf16[576,256]{1,0:T(8,128)(2,1)}, bf16[576,256]{1,0:T(8,128)(2,1)}, u32[]{:S(2)}, u32[]{:S(2)}) collective-permute-start(bf16[576,256]{1,0:T(8,128)(2,1)} %collective-permute-done.6), channel_id=1, source_target_pairs={{0,1},{1,0},{2,3},{3,2},{4,5},{5,4},{6,7},{7,6},{8,9},{9,8},{10,11... | collective-permute-start | bytes 884744 | tf_op jit(solution)/shard_map/ppermute | solution.py:374
  49.8 4.2 %collective-permute-start.10 = (f32[192,128]{1,0:T(8,128)S(1)}, f32[192,128]{1,0:T(8,128)S(1)}, u32[]{:S(2)}, u32[]{:S(2)}) collective-permute-start(f32[192,128]{1,0:T(8,128)S(1)} %slice.81), channel_id=1, source_target_pairs={{0,1},{1,0},{2,3},{3,2},{4,5},{5,4},{6,7},{7,6},{8,9},{9,8},{10,11... | collective-permute-start | bytes 294920 | tf_op jit(solution)/shard_map/ppermute | solution.py:304
  50.4 3.8 %collective-permute-start.16 = (bf16[576,256]{1,0:T(8,128)(2,1)S(1)}, bf16[576,256]{1,0:T(8,128)(2,1)S(1)}, u32[]{:S(2)}, u32[]{:S(2)}) collective-permute-start(bf16[576,256]{1,0:T(8,128)(2,1)S(1)} %get-tuple-element.49), channel_id=1, source_target_pairs={{0,1},{1,0},{2,3},{3,2},{4,5},{5,4},{6,7},{7,6},{8,9},{9,8},{10,11... | collective-permute-start | bytes 884744 | tf_op jit(solution)/shard_map/ppermute | solution.py:374
  50.5 9.5 %collective-permute-start.15 = (bf16[576,256]{1,0:T(8,128)(2,1)S(1)}, bf16[576,256]{1,0:T(8,128)(2,1)S(1)}, u32[]{:S(2)}, u32[]{:S(2)}) collective-permute-start(bf16[576,256]{1,0:T(8,128)(2,1)S(1)} %get-tuple-element.49), channel_id=1, source_target_pairs={{0,30},{2,0},{4,2},{6,4},{8,6},{10,8},{12,10},{14,12},{16,14},{18,... | collective-permute-start | bytes 884744 | tf_op jit(solution)/shard_map/ppermute | solution.py:26
  54.0 11.9 %collective-permute-start.14 = (bf16[576,256]{1,0:T(8,128)(2,1)S(1)}, bf16[576,256]{1,0:T(8,128)(2,1)S(1)}, u32[]{:S(2)}, u32[]{:S(2)}) collective-permute-start(bf16[576,256]{1,0:T(8,128)(2,1)S(1)} %get-tuple-element.49), channel_id=1, source_target_pairs={{0,2},{2,4},{4,6},{6,8},{8,10},{10,12},{12,14},{14,16},{16,18},{18... | collective-permute-start | bytes 884744 | tf_op jit(solution)/shard_map/ppermute | solution.py:26
  54.1 13.0 %collective-permute-start.11 = (f32[96,128]{1,0:T(8,128)S(1)}, f32[96,128]{1,0:T(8,128)S(1)}, u32[]{:S(2)}, u32[]{:S(2)}) collective-permute-start(f32[96,128]{1,0:T(8,128)S(1)} %slice.83), channel_id=1, source_target_pairs={{0,4},{2,6},{4,0},{6,2},{8,12},{10,14},{12,8},{14,10},{16,20},{18,... | collective-permute-start | bytes 147464 | tf_op jit(solution)/shard_map/ppermute | solution.py:304
  66.0 9.8 %collective-permute-start.17 = (bf16[576,256]{1,0:T(8,128)(2,1)S(1)}, bf16[576,256]{1,0:T(8,128)(2,1)S(1)}, u32[]{:S(2)}, u32[]{:S(2)}) collective-permute-start(bf16[576,256]{1,0:T(8,128)(2,1)S(1)} %collective-permute-done.14), channel_id=1, source_target_pairs={{0,1},{1,0},{2,3},{3,2},{4,5},{5,4},{6,7},{7,6},{8,9},{9,8},{10,11... | collective-permute-start | bytes 884744 | tf_op jit(solution)/shard_map/ppermute | solution.py:374
  67.1 8.7 %collective-permute-start.18 = (bf16[576,256]{1,0:T(8,128)(2,1)S(1)}, bf16[576,256]{1,0:T(8,128)(2,1)S(1)}, u32[]{:S(2)}, u32[]{:S(2)}) collective-permute-start(bf16[576,256]{1,0:T(8,128)(2,1)S(1)} %collective-permute-done.15), channel_id=1, source_target_pairs={{0,1},{1,0},{2,3},{3,2},{4,5},{5,4},{6,7},{7,6},{8,9},{9,8},{10,11... | collective-permute-start | bytes 884744 | tf_op jit(solution)/shard_map/ppermute | solution.py:374
  67.1 3.0 %collective-permute-start.12 = (f32[96,128]{1,0:T(8,128)S(1)}, f32[96,128]{1,0:T(8,128)S(1)}, u32[]{:S(2)}, u32[]{:S(2)}) collective-permute-start(f32[96,128]{1,0:T(8,128)S(1)} %slice_add_fusion.3), channel_id=1, source_target_pairs={{0,8},{2,10},{4,12},{6,14},{8,0},{10,2},{12,4},{14,6},{16,24},{18,... | collective-permute-start | bytes 147464 | tf_op jit(solution)/shard_map/ppermute | solution.py:304
  70.1 4.1 %collective-permute-start.13 = (f32[96,128]{1,0:T(8,128)S(1)}, f32[96,128]{1,0:T(8,128)S(1)}, u32[]{:S(2)}, u32[]{:S(2)}) collective-permute-start(f32[96,128]{1,0:T(8,128)S(1)} %add.46), channel_id=1, source_target_pairs={{0,16},{2,18},{4,20},{6,22},{8,24},{10,26},{12,28},{14,30},{16,0},... | collective-permute-start | bytes 147464 | tf_op jit(solution)/shard_map/ppermute | solution.py:304
  78.9 3.6 %collective-permute-start.19 = (f32[128,256]{1,0:T(8,128)S(1)}, f32[128,256]{1,0:T(8,128)S(1)}, u32[]{:S(2)}, u32[]{:S(2)}) collective-permute-start(f32[128,256]{1,0:T(8,128)S(1)} %slice.87), channel_id=1, source_target_pairs={{0,1},{1,0},{2,3},{3,2},{4,5},{5,4},{6,7},{7,6},{8,9},{9,8},{10,11... | collective-permute-start | bytes 393224 | tf_op jit(solution)/shard_map/ppermute | solution.py:304
  82.6 6.8 %collective-permute-start.20 = (f32[176,256]{1,0:T(8,128)S(1)}, f32[176,256]{1,0:T(8,128)S(1)}, u32[]{:S(2)}, u32[]{:S(2)}) collective-permute-start(f32[176,256]{1,0:T(8,128)S(1)} %pad_maximum_fusion.1), channel_id=1, source_target_pairs={{0,2},{2,0},{4,6},{6,4},{8,10},{10,8},{12,14},{14,12},{16,18},{18,... | collective-permute-start | bytes 540680 | tf_op jit(solution)/shard_map/ppermute | solution.py:304
  89.5 3.7 %collective-permute-start.21 = (f32[112,256]{1,0:T(8,128)S(1)}, f32[112,256]{1,0:T(8,128)S(1)}, u32[]{:S(2)}, u32[]{:S(2)}) collective-permute-start(f32[112,256]{1,0:T(8,128)S(1)} %pad_maximum_fusion.3), channel_id=1, source_target_pairs={{0,4},{2,6},{4,0},{6,2},{8,12},{10,14},{12,8},{14,10},{16,20},{18,... | collective-permute-start | bytes 344072 | tf_op jit(solution)/shard_map/ppermute | solution.py:304
  93.2 3.0 %collective-permute-start.22 = (f32[192,128]{1,0:T(8,128)S(1)}, f32[192,128]{1,0:T(8,128)S(1)}, u32[]{:S(2)}, u32[]{:S(2)}) collective-permute-start(f32[192,128]{1,0:T(8,128)S(1)} %pad_maximum_fusion.4), channel_id=1, source_target_pairs={{0,1},{1,0},{2,3},{3,2},{4,5},{5,4},{6,7},{7,6},{8,9},{9,8},{10,11... | collective-permute-start | bytes 294920 | tf_op jit(solution)/shard_map/ppermute | solution.py:304
  97.7 3.2 %collective-permute-start.23 = (f32[64,256]{1,0:T(8,128)S(1)}, f32[64,256]{1,0:T(8,128)S(1)}, u32[]{:S(2)}, u32[]{:S(2)}) collective-permute-start(f32[64,256]{1,0:T(8,128)S(1)} %slice_add_fusion.2), channel_id=1, source_target_pairs={{0,8},{2,10},{4,12},{6,14},{8,0},{10,2},{12,4},{14,6},{16,24},{18,... | collective-permute-start | bytes 196616 | tf_op jit(solution)/shard_map/ppermute | solution.py:304
  102.6 4.8 %collective-permute-start.24 = (f32[64,256]{1,0:T(8,128)S(1)}, f32[64,256]{1,0:T(8,128)S(1)}, u32[]{:S(2)}, u32[]{:S(2)}) collective-permute-start(f32[64,256]{1,0:T(8,128)S(1)} %add.51), channel_id=1, source_target_pairs={{0,16},{2,18},{4,20},{6,22},{8,24},{10,26},{12,28},{14,30},{16,0},... | collective-permute-start | bytes 196616 | tf_op jit(solution)/shard_map/ppermute | solution.py:304
  108.9 3.2 %collective-permute-start.25 = (f32[64,256]{1,0:T(8,128)S(1)}, f32[64,256]{1,0:T(8,128)S(1)}, u32[]{:S(2)}, u32[]{:S(2)}) collective-permute-start(f32[64,256]{1,0:T(8,128)S(1)} %add.52), channel_id=1, source_target_pairs={{0,4},{2,6},{4,0},{6,2},{8,12},{10,14},{12,8},{14,10},{16,20},{18,... | collective-permute-start | bytes 196616 | tf_op jit(solution)/shard_map/ppermute | solution.py:304
  113.8 5.4 %collective-permute-start.26 = (f32[128,256]{1,0:T(8,128)S(1)}, f32[128,256]{1,0:T(8,128)S(1)}, u32[]{:S(2)}, u32[]{:S(2)}) collective-permute-start(f32[128,256]{1,0:T(8,128)S(1)} %pad_maximum_fusion.2), channel_id=1, source_target_pairs={{0,1},{1,0},{2,3},{3,2},{4,5},{5,4},{6,7},{7,6},{8,9},{9,8},{10,11... | collective-permute-start | bytes 393224 | tf_op jit(solution)/shard_map/ppermute | solution.py:304
  (9 other events, 12.1 us)

commit v7 on v6

--- a/solution.py
+++ b/solution.py
@@ -15,7 +15,7 @@
 TN = (((0,), (0,)), ((), ()))
 GROUP = 8
 TILE = 128
-VMEM_LIMIT = 20 * 1024 * 1024
+VMEM_LIMIT = 12 * 1024 * 1024
 LIST_ROWS = 16
 PIECES = 4
 
@@ -38,7 +38,7 @@
         out_specs=jax.tree.map(lambda _: VMEM, out_shape),
         scratch_shapes=[] if slots is None else [pltpu.SMEM(slots, jnp.int32)],
         compiler_params=pltpu.CompilerParams(vmem_limit_bytes=VMEM_LIMIT),
-        cost_estimate=pl.CostEstimate(flops=flops, bytes_accessed=bytes_accessed, transcendentals=0),
+        cost_estimate=pl.CostEstimate(flops=flops // 16, bytes_accessed=bytes_accessed // 16, transcendentals=0),
     )
 
 
@@ -304,17 +304,11 @@
     return lax.ppermute(value, axis, [(at, at ^ bit) for at in range(lax.axis_size(axis))])
 
 
-def halving_bits():
-    bits = []
-    for axis in ("split", "region"):
-        size = lax.axis_size(axis)
-        bits.append([(axis, 1 << at) for at in range(size.bit_length() - 1)])
-    cores, regions = bits
-    return [cores[0], regions[1]], cores[1:] + regions[2:] + regions[:1]
-
-
-def device_number():
-    halved, _ = halving_bits()
+def axis_bits(axis):
+    return [(axis, 1 << at) for at in range(lax.axis_size(axis).bit_length() - 1)]
+
+
+def device_number(halved):
     number = 0
     for axis, bit in halved:
         number = number * 2 + (lax.axis_index(axis) // bit) % 2
@@ -420,20 +414,23 @@
     work = 2 * rows * size * modes
     square_work = 2 * rows * modes * modes
     traffic = hessian.size * 2 + 3 * rows * modes * 4
-    number = device_number()
+    cores, *other_cores = axis_bits("split")
+    near, across, *far = axis_bits("region")
+    between = other_cores + far
+    gram_number, cross_number = device_number([cores, across]), device_number([cores, near])
     halo_slots = (row_blocks, 2 * halo_blocks + 1)
 
-    def step(body, outs, near, lower, upper, scalars, extra):
+    def step(body, outs, own, lower, upper, scalars, extra, beside=()):
         call = kernel_call(
             functools.partial(near_body, region_blocks),
             wide,
-            [SMEM] * 3 + [VMEM] * (1 + len(near)),
+            [SMEM] * 3 + [VMEM] * (1 + len(own)),
             work * region_blocks,
             traffic,
             (row_blocks, region_blocks + 1),
         )
-        total = call(block_cols, live_blocks, bases, hessian, *near)
-        lower, upper, total = lax.optimization_barrier((lower, upper, total))
+        total = call(block_cols, live_blocks, bases, hessian, *own)
+        lower, upper, total, beside = lax.optimization_barrier((lower, upper, total, beside))
         pairs = list(zip(gathered(lower), gathered(upper)))
         for which, pair in enumerate(pairs):
             last = which == len(pairs) - 1
@@ -442,37 +439,35 @@
             body_of = functools.partial(body if last else middle_body, region_blocks, which)
             cost = 2 * work * halo_blocks // len(pairs)
             total = kernel_call(body_of, outs if last else wide, specs, cost, traffic, halo_slots)(*given)
-        return total
+        return (total, beside) if beside else total
 
     one, one_cast = step(first_body, (wide, narrow), first_near, first_lower, first_upper, (bounds,), (vectors,))
     two, two_cast = step(second_body, (wide, narrow), *exchange(one_cast), (bounds,), (one, vectors))
 
-    (cores, across), doubled = halving_bits()
-    *between, near_chip = doubled
     packed = jax.ShapeDtypeStruct((tile_rows, TILE), jnp.float32)
     third = exchange(two_cast)
-    gram = kernel_call(gram_body, packed, [SMEM, VMEM], square_work, traffic)(number, two)
+    gram = kernel_call(gram_body, packed, [SMEM, VMEM], square_work, traffic)(gram_number, two)
     for step_of in [halving(*cores), halving(*across)] + [doubling(*bit) for bit in between]:
         gram = step_of(gram)()
-    cross = step(third_body, square, *third, (number,), (two,))
+    cross, (gram,) = step(third_body, square, *third, (cross_number,), (two,), (gram,))
     cross = halving(*cores)(cross)()
 
     fold = modes // TILE
     cut = gram.shape[0] // fold
     folded = jnp.concatenate([gram[at * cut : (at + 1) * cut] for at in range(fold)], 1)
     flat = lambda value: [value[:, at * TILE : (at + 1) * TILE] for at in range(fold)]
-    both = doubling(*near_chip)(jnp.concatenate([folded, cross], 0))()
-    half = cut + cross.shape[0] // 2
-    got = partner_value(jnp.concatenate([both[:cut], both[half:]], 0), *across)
-    gram = jnp.concatenate(flat(both[:cut]) + flat(got[:cut]), 0)
-    cross = both[cut:half] + got[cut:]
-    gram = joining(*cores)(gram)()
-    stages = factor_stages(float(total_rows), modes // TILE, number, two)
-    steps = [doubling(*bit) for bit in between] + [joining(*across), joining(*cores)]
+    half = cross.shape[0] // 2
+    got = partner_value(jnp.concatenate([folded, cross[half:]], 0), *near)
+    both = jnp.concatenate([folded, cross[:half]], 0) + got
+    got = partner_value(both, *across)
+    gram = joining(*cores)(jnp.concatenate(flat(both[:cut]) + flat(got[:cut]), 0))()
+    cross = both[cut:] + got[cut:]
+    stages = factor_stages(float(total_rows), modes // TILE, gram_number, two)
+    steps = [doubling(*bit) for bit in between] + [joining(*near), joining(*cores)]
     cross, (basis, inverse) = run_beside(cross, steps, gram, stages)
     body_of = functools.partial(projected_body, float(total_rows))
     call = kernel_call(body_of, square, [SMEM] + [VMEM] * 2, 2 * square_work, traffic)
-    return basis, call(number, cross, inverse)
+    return basis, call(cross_number, cross, inverse)
 
 
 def solution(mesh):

time: 121 us -> 116 us (0.959)
  waiting for transfers between devices: 52 us -> 38.2 us
  starting transfers between devices: 29 us -> 33.4 us
  local copies, waits for them, and re-layouts: 6.83 us -> 9.61 us
    ppermute x6, waiting for transfers between devices: 27.4 us -> 15.1 us  [shifted(): return lax.ppermute(value, axis, pairs)]
    ppermute x6, starting transfers between devices: 13.1 us -> 16.8 us  [shifted(): return lax.ppermute(value, axis, pairs)]
    unnamed x30 -> x40, local copies, waits for them, and re-layouts: 6.76 us -> 9.54 us
    ppermute x9, starting transfers between devices: 4.1 us -> 5.66 us  [local(): swapped = lambda value: lax.ppermute(value, 'split', [(0, 1), (1, 0)])]
    ppermute x12, waiting for transfers between devices: 24.5 us -> 22.9 us  [partner_value(): lax.ppermute(value, axis, [(at, at ^ bit) for at in range(lax.axis_size(a...]
  transfers between devices with their start and end apart: 27 -> 27, of which waited for: 16 -> 14; matrix products, arithmetic and copies ran while one was open for 0% -> 1% of each run, Pallas kernels for 12% -> 18%
where the time goes in v7:
time: 116 us
  waiting for transfers between devices  38.2 us (33%)
  starting transfers between devices  33.4 us (29%)
  Pallas kernels  30.9 us (27%)
  local copies, waits for them, and re-layouts  9.61 us (8%)
  other arithmetic  2.67 us (2%)
    ppermute x12, waiting for transfers between devices, partner_value(): lax.ppermute(value, axis, [(at, at ^ bit) for at in range(lax.axis_size(a...  22.9 us
    ppermute x6, starting transfers between devices, shifted(): return lax.ppermute(value, axis, pairs)  16.8 us
    ppermute x6, waiting for transfers between devices, shifted(): return lax.ppermute(value, axis, pairs)  15.1 us
    pallas_call x6, Pallas kernels, step(): kernel_call(body_of, outs if last else wide, specs, cost, traffic, halo_s...  12.7 us
    ppermute x12, starting transfers between devices, partner_value(): lax.ppermute(value, axis, [(at, at ^ bit) for at in range(lax.axis_size(a...  10.9 us
    unnamed x40, local copies, waits for them, and re-layouts  9.54 us
    pallas_call x6, Pallas kernels, stage(): return tiles[:place] + (call(tiles[place]),) + tiles[place + 1:]  8.78 us
    ppermute x9, starting transfers between devices, local(): swapped = lambda value: lax.ppermute(value, 'split', [(0, 1), (1, 0)])  5.66 us
  transfers between devices with their start and end apart: 27, of which 14 were waited for; matrix products, arithmetic and copies ran while one was open for 1% of the time, Pallas kernels for 18%

profile of v7, /device:TPU:1, one launch (start us, length us, event | category | flops | bytes accessed | tf_op | source)
XLA Modules:
  0.0 115.8 jit_solution(13429577236547718729)
XLA Ops:
  2.6 2.7 %collective-permute-start = (bf16[592,256]{1,0:T(8,128)(2,1)S(1)}, bf16[592,256]{1,0:T(8,128)(2,1)S(1)}, u32[]{:S(2)}, u32[]{:S(2)}) collective-permute-start(bf16[592,256]{1,0:T(8,128)(2,1)S(1)} %get-tuple-element.81), channel_id=1, source_target_pairs={{0,2},{2,4},{4,6},{6,8},{8,10},{10,12},{12,14},{14,16},{16,18},{18... | collective-permute-start | bytes 909320 | tf_op jit(solution)/shard_map/ppermute | solution.py:26
  5.2 4.0 %collective-permute-start.1 = (bf16[592,256]{1,0:T(8,128)(2,1)S(1)}, bf16[592,256]{1,0:T(8,128)(2,1)S(1)}, u32[]{:S(2)}, u32[]{:S(2)}) collective-permute-start(bf16[592,256]{1,0:T(8,128)(2,1)S(1)} %get-tuple-element.81), channel_id=1, source_target_pairs={{0,30},{2,0},{4,2},{6,4},{8,6},{10,8},{12,10},{14,12},{16,14},{18,... | collective-permute-start | bytes 909320 | tf_op jit(solution)/shard_map/ppermute | solution.py:26
  9.3 2.0 %copy-done = bf16[3,12,192,192]{3,2,1,0:T(8,128)(2,1)S(1)} copy-done((bf16[3,12,192,192]{3,2,1,0:T(8,128)(2,1)S(1)}, bf16[3,12,192,192]{3,2,1,0:T(8,128)(2,1)}, u32[]{:S(2)}) %copy-start) | copy-done | bytes 2654232
  12.7 1.4 %shard_map.77.refs_7_ = f32[576,256]{1,0:T(8,128)S(1)} custom-call(s32[3,12]{1,0:T(4,128)S(1)} %copy-done.12, s32[3]{0:T(128)S(1)} %copy-done.14, s32[2]{0:T(128)S(1)} %pad_add_fusion.refs_2_.refs_3_, bf16[3,12,192,192]{3,2,1,0:T(8,128)(2,1)S(1)} %copy-done, bf16[1,592,256]{2,1,0:T(8,128)(2,1)S(1)} %get-tuple-element.80.refs_4_, ...), custom_call_target="tpu_custom_call" | custom-call | flops 21233664 | bytes 276480 | tf_op jit(solution)/shard_map/pallas_call | solution.py:432
  14.1 4.2 %collective-permute-done = bf16[592,256]{1,0:T(8,128)(2,1)S(1)} collective-permute-done((bf16[592,256]{1,0:T(8,128)(2,1)S(1)}, bf16[592,256]{1,0:T(8,128)(2,1)S(1)}, u32[]{:S(2)}, u32[]{:S(2)}) %collective-permute-start) | collective-permute-done | bytes 303136 | tf_op jit(solution)/shard_map/ppermute | solution.py:26
  18.3 1.9 %collective-permute-done.1 = bf16[592,256]{1,0:T(8,128)(2,1)S(1)} collective-permute-done((bf16[592,256]{1,0:T(8,128)(2,1)S(1)}, bf16[592,256]{1,0:T(8,128)(2,1)S(1)}, u32[]{:S(2)}, u32[]{:S(2)}) %collective-permute-start.1) | collective-permute-done | bytes 303136 | tf_op jit(solution)/shard_map/ppermute | solution.py:26
  21.1 1.5 %shard_map.78.refs_7_ = f32[576,256]{1,0:T(8,128)S(1)} custom-call(s32[3,12]{1,0:T(4,128)S(1)} %copy-done.12, s32[3]{0:T(128)S(1)} %copy-done.14, s32[2,6]{1,0:T(2,128)S(1)} %maximum_convert_fusion.refs_2_, s32[2]{0:T(128)S(1)} %pad_add_fusion.refs_2_.refs_3_, bf16[3,12,192,192]{3,2,1,0:T(8,128)(2,1)S(1)} %copy-done, bf16[1,592,256]{2,1,0:T(8,128)(2,1)S(1)} %bitcast.25, ...), custom_call_target="tpu_custom_call" | custom-call | flops 21233664 | bytes 276480 | tf_op jit(solution)/shard_map/pallas_call | solution.py:441
  22.7 1.5 %shard_map.79 = (f32[576,256]{1,0:T(8,128)S(1)}, bf16[576,256]{1,0:T(8,128)(2,1)S(1)}) custom-call(s32[3,12]{1,0:T(4,128)S(1)} %copy-done.12, s32[3]{0:T(128)S(1)} %copy-done.14, s32[2,6]{1,0:T(2,128)S(1)} %maximum_convert_fusion.refs_2_, s32[2]{0:T(128)S(1)} %pad_add_fusion.refs_2_.refs_3_, bf16[3,12,192,192]{3,2,1,0:T(8,128)(2,1)S(1)} %copy-done, ...), custom_call_target="tpu_custom_call" | custom-call | flops 21233664 | bytes 276480 | tf_op jit(solution)/shard_map/pallas_call | solution.py:441
  26.8 3.9 %collective-permute-start.6 = (bf16[576,256]{1,0:T(8,128)(2,1)S(1)}, bf16[576,256]{1,0:T(8,128)(2,1)}, u32[]{:S(2)}, u32[]{:S(2)}) collective-permute-start(bf16[576,256]{1,0:T(8,128)(2,1)S(1)} %get-tuple-element.44), channel_id=1, source_target_pairs={{0,30},{2,0},{4,2},{6,4},{8,6},{10,8},{12,10},{14,12},{16,14},{18,... | collective-permute-start | bytes 884744 | tf_op jit(solution)/shard_map/ppermute | solution.py:26
  32.8 6.7 %collective-permute-done.5 = bf16[576,256]{1,0:T(8,128)(2,1)} collective-permute-done((bf16[576,256]{1,0:T(8,128)(2,1)S(1)}, bf16[576,256]{1,0:T(8,128)(2,1)}, u32[]{:S(2)}, u32[]{:S(2)}) %collective-permute-start.5) | collective-permute-done | bytes 294944 | tf_op jit(solution)/shard_map/ppermute | solution.py:26
  39.5 2.3 %collective-permute-done.6 = bf16[576,256]{1,0:T(8,128)(2,1)} collective-permute-done((bf16[576,256]{1,0:T(8,128)(2,1)S(1)}, bf16[576,256]{1,0:T(8,128)(2,1)}, u32[]{:S(2)}, u32[]{:S(2)}) %collective-permute-start.6) | collective-permute-done | bytes 294944 | tf_op jit(solution)/shard_map/ppermute | solution.py:26
  43.8 2.0 %shard_map.81.refs_7_ = f32[576,256]{1,0:T(8,128)S(1)} custom-call(s32[3,12]{1,0:T(4,128)S(1)} %copy-done.13, s32[3]{0:T(128)S(1)} %copy-done.15, s32[2,6]{1,0:T(2,128)S(1)} %maximum_convert_fusion.refs_2_, s32[2]{0:T(128)S(1)} %pad_add_fusion.refs_2_.refs_3_, bf16[3,12,192,192]{3,2,1,0:T(8,128)(2,1)S(1)} %copy-done.1, ...), custom_call_target="tpu_custom_call" | custom-call | flops 21233664 | bytes 276480 | tf_op jit(solution)/shard_map/pallas_call | solution.py:441
  46.5 2.0 %shard_map.82 = (f32[576,256]{1,0:T(8,128)S(1)}, bf16[576,256]{1,0:T(8,128)(2,1)S(1)}) custom-call(s32[3,12]{1,0:T(4,128)S(1)} %copy-done.13, s32[3]{0:T(128)S(1)} %copy-done.15, s32[2,6]{1,0:T(2,128)S(1)} %maximum_convert_fusion.refs_2_, s32[2]{0:T(128)S(1)} %pad_add_fusion.refs_2_.refs_3_, bf16[3,12,192,192]{3,2,1,0:T(8,128)(2,1)S(1)} %copy-done.1, ...), custom_call_target="tpu_custom_call" | custom-call | flops 21233664 | bytes 276480 | tf_op jit(solution)/shard_map/pallas_call | solution.py:441
  53.6 5.1 %collective-permute-start.11 = (bf16[576,256]{1,0:T(8,128)(2,1)S(1)}, bf16[576,256]{1,0:T(8,128)(2,1)}, u32[]{:S(2)}, u32[]{:S(2)}) collective-permute-start(bf16[576,256]{1,0:T(8,128)(2,1)S(1)} %get-tuple-element.49), channel_id=1, source_target_pairs={{0,30},{2,0},{4,2},{6,4},{8,6},{10,8},{12,10},{14,12},{16,14},{18,... | collective-permute-start | bytes 884744 | tf_op jit(solution)/shard_map/ppermute | solution.py:26
  58.8 7.3 %collective-permute-done.15 = f32[96,128]{1,0:T(8,128)S(1)} collective-permute-done((f32[96,128]{1,0:T(8,128)S(1)}, f32[96,128]{1,0:T(8,128)S(1)}, u32[]{:S(2)}, u32[]{:S(2)}) %collective-permute-start.15) | collective-permute-done | bytes 49184 | tf_op jit(solution)/shard_map/ppermute | solution.py:304
  66.1 1.4 %collective-permute-start.16 = (f32[96,128]{1,0:T(8,128)S(1)}, f32[96,128]{1,0:T(8,128)S(1)}, u32[]{:S(2)}, u32[]{:S(2)}) collective-permute-start(f32[96,128]{1,0:T(8,128)S(1)} %add.54), channel_id=1, source_target_pairs={{0,16},{2,18},{4,20},{6,22},{8,24},{10,26},{12,28},{14,30},{16,0},... | collective-permute-start | bytes 147464 | tf_op jit(solution)/shard_map/ppermute | solution.py:304
  67.6 2.5 %collective-permute-done.16 = f32[96,128]{1,0:T(8,128)S(1)} collective-permute-done((f32[96,128]{1,0:T(8,128)S(1)}, f32[96,128]{1,0:T(8,128)S(1)}, u32[]{:S(2)}, u32[]{:S(2)}) %collective-permute-start.16) | collective-permute-done | bytes 49184 | tf_op jit(solution)/shard_map/ppermute | solution.py:304
  72.9 2.7 %collective-permute-start.17 = (bf16[576,256]{1,0:T(8,128)(2,1)}, bf16[576,256]{1,0:T(8,128)(2,1)}, u32[]{:S(2)}, u32[]{:S(2)}) collective-permute-start(bf16[576,256]{1,0:T(8,128)(2,1)} %collective-permute-done.10), channel_id=1, source_target_pairs={{0,1},{1,0},{2,3},{3,2},{4,5},{5,4},{6,7},{7,6},{8,9},{9,8},{10,11... | collective-permute-start | bytes 884744 | tf_op jit(solution)/shard_map/ppermute | solution.py:368
  76.7 2.0 %shard_map.85.refs_7_ = f32[576,256]{1,0:T(8,128)S(1)} custom-call(s32[3,12]{1,0:T(4,128)S(1)} %copy-done.13, s32[3]{0:T(128)S(1)} %copy-done.15, s32[2,6]{1,0:T(2,128)S(1)} %maximum_convert_fusion.refs_2_, s32[2]{0:T(128)S(1)} %pad_add_fusion.refs_2_.refs_3_, bf16[3,12,192,192]{3,2,1,0:T(8,128)(2,1)S(1)} %copy-done.1, ...), custom_call_target="tpu_custom_call" | custom-call | flops 21233664 | bytes 276480 | tf_op jit(solution)/shard_map/pallas_call | solution.py:441
  78.8 3.6 %shard_map.86 = f32[256,256]{1,0:T(8,128)S(1)} custom-call(s32[3,12]{1,0:T(4,128)S(1)} %copy-done.13, s32[3]{0:T(128)S(1)} %copy-done.15, s32[2,6]{1,0:T(2,128)S(1)} %maximum_convert_fusion.refs_2_, s32[2]{0:T(128)S(1)} %pad_add_fusion.refs_2_.refs_3_, bf16[3,12,192,192]{3,2,1,0:T(8,128)(2,1)S(1)} %copy-done.1, bf16[1,576,256]{2,1,0:T(8,128)(2,1)} %bitcast.18.refs_5_, ...), custom_call_target="tpu_custom_call" | custom-call | flops 21233664 | bytes 276480 | tf_op jit(solution)/shard_map/pallas_call | solution.py:441
  84.0 4.4 %collective-permute-done.20 = f32[112,256]{1,0:T(8,128)S(1)} collective-permute-done((f32[112,256]{1,0:T(8,128)S(1)}, f32[112,256]{1,0:T(8,128)S(1)}, u32[]{:S(2)}, u32[]{:S(2)}) %collective-permute-start.20) | collective-permute-done | bytes 114720 | tf_op jit(solution)/shard_map/ppermute | solution.py:304
  88.5 3.6 %collective-permute-done.21 = f32[112,256]{1,0:T(8,128)S(1)} collective-permute-done((f32[112,256]{1,0:T(8,128)S(1)}, f32[112,256]{1,0:T(8,128)S(1)}, u32[]{:S(2)}, u32[]{:S(2)}) %collective-permute-start.21) | collective-permute-done | bytes 114720 | tf_op jit(solution)/shard_map/ppermute | solution.py:304
  92.1 2.4 %collective-permute-start.22 = (f32[192,128]{1,0:T(8,128)S(1)}, f32[192,128]{1,0:T(8,128)S(1)}, u32[]{:S(2)}, u32[]{:S(2)}) collective-permute-start(f32[192,128]{1,0:T(8,128)S(1)} %pad_maximum_fusion.3), channel_id=1, source_target_pairs={{0,1},{1,0},{2,3},{3,2},{4,5},{5,4},{6,7},{7,6},{8,9},{9,8},{10,11... | collective-permute-start | bytes 294920 | tf_op jit(solution)/shard_map/ppermute | solution.py:304
  95.5 1.6 %collective-permute-start.23 = (f32[64,256]{1,0:T(8,128)S(1)}, f32[64,256]{1,0:T(8,128)S(1)}, u32[]{:S(2)}, u32[]{:S(2)}) collective-permute-start(f32[64,256]{1,0:T(8,128)S(1)} %slice_add_fusion.2), channel_id=1, source_target_pairs={{0,8},{2,10},{4,12},{6,14},{8,0},{10,2},{12,4},{14,6},{16,24},{18,... | collective-permute-start | bytes 196616 | tf_op jit(solution)/shard_map/ppermute | solution.py:304
  97.1 1.5 %shard_map.88.tile_ref = f32[128,128]{1,0:T(8,128)S(1)} custom-call(f32[128,128]{1,0:T(8,128)S(1)} %get-tuple-element.57.tile_ref), custom_call_target="tpu_custom_call" | custom-call | flops 125000000 | bytes 1024 | tf_op jit(solution)/shard_map/pallas_call | solution.py:270
  100.9 1.7 %shard_map.90.refs_0_ = f32[128,128]{1,0:T(8,128)S(1)} custom-call(f32[128,128]{1,0:T(8,128)S(1)} %shard_map.89.tile_ref), custom_call_target="tpu_custom_call" | custom-call | flops 125000000 | bytes 1024 | tf_op jit(solution)/shard_map/pallas_call | solution.py:270
  103.3 1.9 %collective-permute-done.24 = f32[64,256]{1,0:T(8,128)S(1)} collective-permute-done((f32[64,256]{1,0:T(8,128)S(1)}, f32[64,256]{1,0:T(8,128)S(1)}, u32[]{:S(2)}, u32[]{:S(2)}) %collective-permute-start.24) | collective-permute-done | bytes 65568 | tf_op jit(solution)/shard_map/ppermute | solution.py:304
  105.3 1.5 %shard_map.92.tile_ref = f32[128,128]{1,0:T(8,128)S(1)} custom-call(f32[128,128]{1,0:T(8,128)S(1)} %get-tuple-element.70.tile_ref), custom_call_target="tpu_custom_call" | custom-call | flops 125000000 | bytes 1024 | tf_op jit(solution)/shard_map/pallas_call | solution.py:270
  108.4 2.0 %collective-permute-start.26 = (f32[128,256]{1,0:T(8,128)S(1)}, f32[128,256]{1,0:T(8,128)S(1)}, u32[]{:S(2)}, u32[]{:S(2)}) collective-permute-start(f32[128,256]{1,0:T(8,128)S(1)} %pad_maximum_fusion.1), channel_id=1, source_target_pairs={{0,1},{1,0},{2,3},{3,2},{4,5},{5,4},{6,7},{7,6},{8,9},{9,8},{10,11... | collective-permute-start | bytes 393224 | tf_op jit(solution)/shard_map/ppermute | solution.py:304
  110.4 1.7 %shard_map.94.refs_2_ = f32[128,128]{1,0:T(8,128)S(1)} custom-call(f32[128,128]{1,0:T(8,128)S(1)} %shard_map.93.tile_ref), custom_call_target="tpu_custom_call" | custom-call | flops 125000000 | bytes 1024 | tf_op jit(solution)/shard_map/pallas_call | solution.py:270
  112.1 1.9 %shard_map.95 = (f32[576,256]{1,0:T(8,128)}, f32[256,256]{1,0:T(8,128)S(1)}) custom-call(f32[128,128]{1,0:T(8,128)S(1)} %get-tuple-element.72.refs_0_, f32[128,128]{1,0:T(8,128)S(1)} %get-tuple-element.73.refs_1_, f32[128,128]{1,0:T(8,128)S(1)} %shard_map.94.refs_2_, f32[576,256]{1,0:T(8,128)S(1)} %copy-done.3), custom_call_target="tpu_custom_call" | custom-call | flops 125000000 | bytes 9216 | tf_op jit(solution)/shard_map/pallas_call | solution.py:287
  114.0 1.7 %shard_map.96 = f32[256,256]{1,0:T(8,128)} custom-call(s32[1]{0:T(128)} %bitcast.22.refs_8_.number_ref, f32[256,256]{1,0:T(8,128)S(1)} %pad_maximum_fusion.cross_ref, f32[256,256]{1,0:T(8,128)S(1)} %get-tuple-element.79.inverse_ref), custom_call_target="tpu_custom_call" | custom-call | flops 9437184 | bytes 276480 | tf_op jit(solution)/shard_map/pallas_call | solution.py:470
  (110 shorter events, 28.2 us)
Async XLA Ops:
  2.5 6.9 %collective-permute-start.2 = (bf16[592,256]{1,0:T(8,128)(2,1)S(1)}, bf16[592,256]{1,0:T(8,128)(2,1)S(1)}, u32[]{:S(2)}, u32[]{:S(2)}) collective-permute-start(bf16[592,256]{1,0:T(8,128)(2,1)S(1)} %get-tuple-element.81), channel_id=1, source_target_pairs={{0,1},{1,0},{2,3},{3,2},{4,5},{5,4},{6,7},{7,6},{8,9},{9,8},{10,11... | collective-permute-start | bytes 909320 | tf_op jit(solution)/shard_map/ppermute | solution.py:368
  2.6 15.7 %collective-permute-start = (bf16[592,256]{1,0:T(8,128)(2,1)S(1)}, bf16[592,256]{1,0:T(8,128)(2,1)S(1)}, u32[]{:S(2)}, u32[]{:S(2)}) collective-permute-start(bf16[592,256]{1,0:T(8,128)(2,1)S(1)} %get-tuple-element.81), channel_id=1, source_target_pairs={{0,2},{2,4},{4,6},{6,8},{8,10},{10,12},{12,14},{14,16},{16,18},{18... | collective-permute-start | bytes 909320 | tf_op jit(solution)/shard_map/ppermute | solution.py:26
  5.2 15.0 %collective-permute-start.1 = (bf16[592,256]{1,0:T(8,128)(2,1)S(1)}, bf16[592,256]{1,0:T(8,128)(2,1)S(1)}, u32[]{:S(2)}, u32[]{:S(2)}) collective-permute-start(bf16[592,256]{1,0:T(8,128)(2,1)S(1)} %get-tuple-element.81), channel_id=1, source_target_pairs={{0,30},{2,0},{4,2},{6,4},{8,6},{10,8},{12,10},{14,12},{16,14},{18,... | collective-permute-start | bytes 909320 | tf_op jit(solution)/shard_map/ppermute | solution.py:26
  14.0 8.7 %copy-start.4 = (f32[576,256]{1,0:T(8,128)S(1)}, f32[576,256]{1,0:T(8,128)}, u32[]{:S(2)}) copy-start(f32[576,256]{1,0:T(8,128)} %refs_10_.1) | copy-start | bytes 1769476
  14.0 8.7 %copy-start.16 = (f32[2]{0:T(128)S(1)}, f32[2]{0:T(128)}, u32[]{:S(2)}) copy-start(f32[2]{0:T(128)} %refs_8_.3) | copy-start | bytes 28
  20.2 2.4 %collective-permute-start.3 = (bf16[592,256]{1,0:T(8,128)(2,1)S(1)}, bf16[592,256]{1,0:T(8,128)(2,1)S(1)}, u32[]{:S(2)}, u32[]{:S(2)}) collective-permute-start(bf16[592,256]{1,0:T(8,128)(2,1)S(1)} %collective-permute-done), channel_id=1, source_target_pairs={{0,1},{1,0},{2,3},{3,2},{4,5},{5,4},{6,7},{7,6},{8,9},{9,8},{10,11... | collective-permute-start | bytes 909320 | tf_op jit(solution)/shard_map/ppermute | solution.py:368
  21.1 1.7 %collective-permute-start.4 = (bf16[592,256]{1,0:T(8,128)(2,1)S(1)}, bf16[592,256]{1,0:T(8,128)(2,1)S(1)}, u32[]{:S(2)}, u32[]{:S(2)}) collective-permute-start(bf16[592,256]{1,0:T(8,128)(2,1)S(1)} %collective-permute-done.1), channel_id=1, source_target_pairs={{0,1},{1,0},{2,3},{3,2},{4,5},{5,4},{6,7},{7,6},{8,9},{9,8},{10,11... | collective-permute-start | bytes 909320 | tf_op jit(solution)/shard_map/ppermute | solution.py:368
  25.1 17.5 %copy-start.1 = (bf16[3,12,192,192]{3,2,1,0:T(8,128)(2,1)S(1)}, bf16[3,12,192,192]{3,2,1,0:T(8,128)(2,1)}, u32[]{:S(2)}) copy-start(bf16[3,12,192,192]{3,2,1,0:T(8,128)(2,1)} %refs_4_.11) | copy-start | bytes 7962628
  25.1 17.5 %copy-start.13 = (s32[3,12]{1,0:T(4,128)S(1)}, s32[3,12]{1,0:T(4,128)}, u32[]{:S(2)}) copy-start(s32[3,12]{1,0:T(4,128)} %refs_0_.17) | copy-start | bytes 436
  25.1 17.5 %copy-start.15 = (s32[3]{0:T(128)S(1)}, s32[3]{0:T(128)}, u32[]{:S(2)}) copy-start(s32[3]{0:T(128)} %refs_1_.17) | copy-start | bytes 40
  25.1 5.5 %collective-permute-start.7 = (bf16[576,256]{1,0:T(8,128)(2,1)S(1)}, bf16[576,256]{1,0:T(8,128)(2,1)S(1)}, u32[]{:S(2)}, u32[]{:S(2)}) collective-permute-start(bf16[576,256]{1,0:T(8,128)(2,1)S(1)} %get-tuple-element.44), channel_id=1, source_target_pairs={{0,1},{1,0},{2,3},{3,2},{4,5},{5,4},{6,7},{7,6},{8,9},{9,8},{10,11... | collective-permute-start | bytes 884744 | tf_op jit(solution)/shard_map/ppermute | solution.py:368
  25.6 13.9 %collective-permute-start.5 = (bf16[576,256]{1,0:T(8,128)(2,1)S(1)}, bf16[576,256]{1,0:T(8,128)(2,1)}, u32[]{:S(2)}, u32[]{:S(2)}) collective-permute-start(bf16[576,256]{1,0:T(8,128)(2,1)S(1)} %get-tuple-element.44), channel_id=1, source_target_pairs={{0,2},{2,4},{4,6},{6,8},{8,10},{10,12},{12,14},{14,16},{16,18},{18... | collective-permute-start | bytes 884744 | tf_op jit(solution)/shard_map/ppermute | solution.py:26
  26.8 15.0 %collective-permute-start.6 = (bf16[576,256]{1,0:T(8,128)(2,1)S(1)}, bf16[576,256]{1,0:T(8,128)(2,1)}, u32[]{:S(2)}, u32[]{:S(2)}) collective-permute-start(bf16[576,256]{1,0:T(8,128)(2,1)S(1)} %get-tuple-element.44), channel_id=1, source_target_pairs={{0,30},{2,0},{4,2},{6,4},{8,6},{10,8},{12,10},{14,12},{16,14},{18,... | collective-permute-start | bytes 884744 | tf_op jit(solution)/shard_map/ppermute | solution.py:26
  41.8 4.1 %collective-permute-start.8 = (bf16[576,256]{1,0:T(8,128)(2,1)}, bf16[576,256]{1,0:T(8,128)(2,1)}, u32[]{:S(2)}, u32[]{:S(2)}) collective-permute-start(bf16[576,256]{1,0:T(8,128)(2,1)} %collective-permute-done.5), channel_id=1, source_target_pairs={{0,1},{1,0},{2,3},{3,2},{4,5},{5,4},{6,7},{7,6},{8,9},{9,8},{10,11... | collective-permute-start | bytes 884744 | tf_op jit(solution)/shard_map/ppermute | solution.py:368
  42.6 3.2 %collective-permute-start.9 = (bf16[576,256]{1,0:T(8,128)(2,1)}, bf16[576,256]{1,0:T(8,128)(2,1)}, u32[]{:S(2)}, u32[]{:S(2)}) collective-permute-start(bf16[576,256]{1,0:T(8,128)(2,1)} %collective-permute-done.6), channel_id=1, source_target_pairs={{0,1},{1,0},{2,3},{3,2},{4,5},{5,4},{6,7},{7,6},{8,9},{9,8},{10,11... | collective-permute-start | bytes 884744 | tf_op jit(solution)/shard_map/ppermute | solution.py:368
  50.4 1.5 %collective-permute-start.13 = (f32[192,128]{1,0:T(8,128)S(1)}, f32[192,128]{1,0:T(8,128)S(1)}, u32[]{:S(2)}, u32[]{:S(2)}) collective-permute-start(f32[192,128]{1,0:T(8,128)S(1)} %slice.81), channel_id=1, source_target_pairs={{0,1},{1,0},{2,3},{3,2},{4,5},{5,4},{6,7},{7,6},{8,9},{9,8},{10,11... | collective-permute-start | bytes 294920 | tf_op jit(solution)/shard_map/ppermute | solution.py:304
  52.0 6.7 %collective-permute-start.14 = (f32[96,128]{1,0:T(8,128)S(1)}, f32[96,128]{1,0:T(8,128)S(1)}, u32[]{:S(2)}, u32[]{:S(2)}) collective-permute-start(f32[96,128]{1,0:T(8,128)S(1)} %slice.83), channel_id=1, source_target_pairs={{0,4},{2,6},{4,0},{6,2},{8,12},{10,14},{12,8},{14,10},{16,20},{18,... | collective-permute-start | bytes 147464 | tf_op jit(solution)/shard_map/ppermute | solution.py:304
  53.0 17.7 %collective-permute-start.12 = (bf16[576,256]{1,0:T(8,128)(2,1)S(1)}, bf16[576,256]{1,0:T(8,128)(2,1)S(1)}, u32[]{:S(2)}, u32[]{:S(2)}) collective-permute-start(bf16[576,256]{1,0:T(8,128)(2,1)S(1)} %get-tuple-element.49), channel_id=1, source_target_pairs={{0,1},{1,0},{2,3},{3,2},{4,5},{5,4},{6,7},{7,6},{8,9},{9,8},{10,11... | collective-permute-start | bytes 884744 | tf_op jit(solution)/shard_map/ppermute | solution.py:368
  53.6 19.2 %collective-permute-start.10 = (bf16[576,256]{1,0:T(8,128)(2,1)S(1)}, bf16[576,256]{1,0:T(8,128)(2,1)}, u32[]{:S(2)}, u32[]{:S(2)}) collective-permute-start(bf16[576,256]{1,0:T(8,128)(2,1)S(1)} %get-tuple-element.49), channel_id=1, source_target_pairs={{0,2},{2,4},{4,6},{6,8},{8,10},{10,12},{12,14},{14,16},{16,18},{18... | collective-permute-start | bytes 884744 | tf_op jit(solution)/shard_map/ppermute | solution.py:26
  53.6 19.2 %collective-permute-start.11 = (bf16[576,256]{1,0:T(8,128)(2,1)S(1)}, bf16[576,256]{1,0:T(8,128)(2,1)}, u32[]{:S(2)}, u32[]{:S(2)}) collective-permute-start(bf16[576,256]{1,0:T(8,128)(2,1)S(1)} %get-tuple-element.49), channel_id=1, source_target_pairs={{0,30},{2,0},{4,2},{6,4},{8,6},{10,8},{12,10},{14,12},{16,14},{18,... | collective-permute-start | bytes 884744 | tf_op jit(solution)/shard_map/ppermute | solution.py:26
  58.7 7.4 %collective-permute-start.15 = (f32[96,128]{1,0:T(8,128)S(1)}, f32[96,128]{1,0:T(8,128)S(1)}, u32[]{:S(2)}, u32[]{:S(2)}) collective-permute-start(f32[96,128]{1,0:T(8,128)S(1)} %slice_add_fusion.3), channel_id=1, source_target_pairs={{0,8},{2,10},{4,12},{6,14},{8,0},{10,2},{12,4},{14,6},{16,24},{18,... | collective-permute-start | bytes 147464 | tf_op jit(solution)/shard_map/ppermute | solution.py:304
  66.1 3.9 %collective-permute-start.16 = (f32[96,128]{1,0:T(8,128)S(1)}, f32[96,128]{1,0:T(8,128)S(1)}, u32[]{:S(2)}, u32[]{:S(2)}) collective-permute-start(f32[96,128]{1,0:T(8,128)S(1)} %add.54), channel_id=1, source_target_pairs={{0,16},{2,18},{4,20},{6,22},{8,24},{10,26},{12,28},{14,30},{16,0},... | collective-permute-start | bytes 147464 | tf_op jit(solution)/shard_map/ppermute | solution.py:304
  72.9 5.9 %collective-permute-start.17 = (bf16[576,256]{1,0:T(8,128)(2,1)}, bf16[576,256]{1,0:T(8,128)(2,1)}, u32[]{:S(2)}, u32[]{:S(2)}) collective-permute-start(bf16[576,256]{1,0:T(8,128)(2,1)} %collective-permute-done.10), channel_id=1, source_target_pairs={{0,1},{1,0},{2,3},{3,2},{4,5},{5,4},{6,7},{7,6},{8,9},{9,8},{10,11... | collective-permute-start | bytes 884744 | tf_op jit(solution)/shard_map/ppermute | solution.py:368
  75.5 3.2 %collective-permute-start.18 = (bf16[576,256]{1,0:T(8,128)(2,1)}, bf16[576,256]{1,0:T(8,128)(2,1)}, u32[]{:S(2)}, u32[]{:S(2)}) collective-permute-start(bf16[576,256]{1,0:T(8,128)(2,1)} %collective-permute-done.11), channel_id=1, source_target_pairs={{0,1},{1,0},{2,3},{3,2},{4,5},{5,4},{6,7},{7,6},{8,9},{9,8},{10,11... | collective-permute-start | bytes 884744 | tf_op jit(solution)/shard_map/ppermute | solution.py:368
  82.4 1.5 %collective-permute-start.19 = (f32[128,256]{1,0:T(8,128)S(1)}, f32[128,256]{1,0:T(8,128)S(1)}, u32[]{:S(2)}, u32[]{:S(2)}) collective-permute-start(f32[128,256]{1,0:T(8,128)S(1)} %slice.85), channel_id=1, source_target_pairs={{0,1},{1,0},{2,3},{3,2},{4,5},{5,4},{6,7},{7,6},{8,9},{9,8},{10,11... | collective-permute-start | bytes 393224 | tf_op jit(solution)/shard_map/ppermute | solution.py:304
  83.9 4.4 %collective-permute-start.20 = (f32[112,256]{1,0:T(8,128)S(1)}, f32[112,256]{1,0:T(8,128)S(1)}, u32[]{:S(2)}, u32[]{:S(2)}) collective-permute-start(f32[112,256]{1,0:T(8,128)S(1)} %fusion.2), channel_id=1, source_target_pairs={{0,2},{2,0},{4,6},{6,4},{8,10},{10,8},{12,14},{14,12},{16,18},{18,... | collective-permute-start | bytes 344072 | tf_op jit(solution)/shard_map/ppermute | solution.py:304
  88.4 3.7 %collective-permute-start.21 = (f32[112,256]{1,0:T(8,128)S(1)}, f32[112,256]{1,0:T(8,128)S(1)}, u32[]{:S(2)}, u32[]{:S(2)}) collective-permute-start(f32[112,256]{1,0:T(8,128)S(1)} %maximum_add_fusion), channel_id=1, source_target_pairs={{0,4},{2,6},{4,0},{6,2},{8,12},{10,14},{12,8},{14,10},{16,20},{18,... | collective-permute-start | bytes 344072 | tf_op jit(solution)/shard_map/ppermute | solution.py:304
  92.1 3.3 %collective-permute-start.22 = (f32[192,128]{1,0:T(8,128)S(1)}, f32[192,128]{1,0:T(8,128)S(1)}, u32[]{:S(2)}, u32[]{:S(2)}) collective-permute-start(f32[192,128]{1,0:T(8,128)S(1)} %pad_maximum_fusion.3), channel_id=1, source_target_pairs={{0,1},{1,0},{2,3},{3,2},{4,5},{5,4},{6,7},{7,6},{8,9},{9,8},{10,11... | collective-permute-start | bytes 294920 | tf_op jit(solution)/shard_map/ppermute | solution.py:304
  95.5 4.3 %collective-permute-start.23 = (f32[64,256]{1,0:T(8,128)S(1)}, f32[64,256]{1,0:T(8,128)S(1)}, u32[]{:S(2)}, u32[]{:S(2)}) collective-permute-start(f32[64,256]{1,0:T(8,128)S(1)} %slice_add_fusion.2), channel_id=1, source_target_pairs={{0,8},{2,10},{4,12},{6,14},{8,0},{10,2},{12,4},{14,6},{16,24},{18,... | collective-permute-start | bytes 196616 | tf_op jit(solution)/shard_map/ppermute | solution.py:304
  99.8 5.4 %collective-permute-start.24 = (f32[64,256]{1,0:T(8,128)S(1)}, f32[64,256]{1,0:T(8,128)S(1)}, u32[]{:S(2)}, u32[]{:S(2)}) collective-permute-start(f32[64,256]{1,0:T(8,128)S(1)} %add.61), channel_id=1, source_target_pairs={{0,16},{2,18},{4,20},{6,22},{8,24},{10,26},{12,28},{14,30},{16,0},... | collective-permute-start | bytes 196616 | tf_op jit(solution)/shard_map/ppermute | solution.py:304
  105.2 3.2 %collective-permute-start.25 = (f32[64,256]{1,0:T(8,128)S(1)}, f32[64,256]{1,0:T(8,128)S(1)}, u32[]{:S(2)}, u32[]{:S(2)}) collective-permute-start(f32[64,256]{1,0:T(8,128)S(1)} %add.62), channel_id=1, source_target_pairs={{0,2},{2,0},{4,6},{6,4},{8,10},{10,8},{12,14},{14,12},{16,18},{18,... | collective-permute-start | bytes 196616 | tf_op jit(solution)/shard_map/ppermute | solution.py:304
  108.4 5.6 %collective-permute-start.26 = (f32[128,256]{1,0:T(8,128)S(1)}, f32[128,256]{1,0:T(8,128)S(1)}, u32[]{:S(2)}, u32[]{:S(2)}) collective-permute-start(f32[128,256]{1,0:T(8,128)S(1)} %pad_maximum_fusion.1), channel_id=1, source_target_pairs={{0,1},{1,0},{2,3},{3,2},{4,5},{5,4},{6,7},{7,6},{8,9},{9,8},{10,11... | collective-permute-start | bytes 393224 | tf_op jit(solution)/shard_map/ppermute | solution.py:304
  (14 other events, 22.2 us)

commit v8 on v7

--- a/solution.py
+++ b/solution.py
@@ -18,6 +18,7 @@
 VMEM_LIMIT = 12 * 1024 * 1024
 LIST_ROWS = 16
 PIECES = 4
+CHUNKS = 2
 
 
 def shifted(value, axis, steps):
@@ -30,37 +31,50 @@
     return lax.dot_general(left, right, dims, precision=EXACT, preferred_element_type=jnp.float32)
 
 
-def kernel_call(body, out_shape, in_specs, flops, bytes_accessed, slots=None):
-    return pl.pallas_call(
+def kernel_call(body, outs, in_specs, flops, bytes_accessed, slots=None):
+    pinned = lambda out: out[1] if isinstance(out, tuple) else pltpu.VMEM(out.shape, out.dtype)
+    call = pl.pallas_call(
         body,
-        out_shape=out_shape,
+        out_shape=[pinned(out) for out in outs],
         in_specs=in_specs,
-        out_specs=jax.tree.map(lambda _: VMEM, out_shape),
+        out_specs=[VMEM for _ in outs],
         scratch_shapes=[] if slots is None else [pltpu.SMEM(slots, jnp.int32)],
         compiler_params=pltpu.CompilerParams(vmem_limit_bytes=VMEM_LIMIT),
         cost_estimate=pl.CostEstimate(flops=flops // 16, bytes_accessed=bytes_accessed // 16, transcendentals=0),
     )
 
-
-def fill_slots(slots_ref, cols_ref, live_ref, first, place_of):
+    def run(*operands):
+        placed = [
+            pltpu.with_memory_space_constraint(value, pltpu.VMEM) if spec is VMEM else value
+            for spec, value in zip(in_specs, operands)
+        ]
+        return call(*placed)
+
+    return run
+
+
+def fill_slots(slots_ref, cols_ref, live_ref, sections):
     rows, stored = cols_ref.shape
-    count = slots_ref.shape[1] - 1
+    unused = slots_ref.shape[1] - 1
     for row in range(rows):
-        for index in range(count):
+        for index in range(unused):
             slots_ref[row, index] = -1
         for at in range(stored):
-            name = cols_ref[row, at] - first
-            inside = (name >= 0) & (name < count) & (at < live_ref[row])
-            slots_ref[row, jnp.where(inside, place_of(jnp.clip(name, 0, count - 1)), count)] = at
-
-
-def accumulate(slots_ref, hessian_ref, operand_ref, base, total):
+            place = unused
+            for first, count, column, column_of in sections:
+                name = cols_ref[row, at] - first
+                inside = (name >= 0) & (name < count) & (at < live_ref[row])
+                place = jnp.where(inside, column + column_of(jnp.clip(name, 0, count - 1)), place)
+            slots_ref[row, place] = at
+
+
+def accumulate(slots_ref, hessian_ref, chunk_refs, base, total):
     rows, _, size, _ = hessian_ref.shape
-    shards, shard_rows, _ = operand_ref.shape
+    shards, shard_rows, _ = chunk_refs[0].shape
     each = shard_rows // size
     for index in range(shards * each):
         start = index % each * size
-        block = operand_ref[index // each, start : start + size, :]
+        block = jnp.concatenate([ref[index // each, start : start + size, :] for ref in chunk_refs], 1)
         parts = []
         for row in range(rows):
             slot = slots_ref[row, base + index]
@@ -72,54 +86,62 @@
     return total
 
 
-def near_body(count, *refs):
-    cols_ref, live_ref, bases_ref, hessian_ref = refs[:4]
-    operands, (out_ref, slots_ref) = refs[4:-2], refs[-2:]
-    fill_slots(slots_ref, cols_ref, live_ref, 0, lambda name: name)
+def near_body(region, halo, chunks, *refs):
+    cols_ref, live_ref, list_ref, places_ref, hessian_ref = refs[:5]
+    operands, (out_ref, slots_ref) = refs[5:-2], refs[-2:]
+    groups = [operands[at : at + chunks] for at in range(0, len(operands), chunks)]
+    sections = [(0, region, 0, lambda name: name)]
+    if len(groups) > 2:
+        sections.append((places_ref[2], halo, region, lambda name: list_ref[name]))
+    fill_slots(slots_ref, cols_ref, live_ref, sections)
     total = None
-    for at, operand_ref in enumerate(operands):
-        total = accumulate(slots_ref, hessian_ref, operand_ref, bases_ref[at], total)
+    for at, group in enumerate(groups):
+        total = accumulate(slots_ref, hessian_ref, group, places_ref[at % 2] + at // 2 * region, total)
     out_ref[...] = total
 
 
-def halo_total(first, which, cols_ref, live_ref, lists_ref, bases_ref, hessian_ref, lower_ref, upper_ref, total_ref, slots_ref):
-    halo = lists_ref.shape[1]
-    fill_slots(slots_ref, cols_ref, live_ref, first, lambda name: list_place(lists_ref, name))
-    total = accumulate(slots_ref, hessian_ref, lower_ref, bases_ref[which], total_ref[...])
-    return accumulate(slots_ref, hessian_ref, upper_ref, halo + bases_ref[which], total)
-
-
-def list_place(lists_ref, name):
-    halo = lists_ref.shape[1]
-    side = jnp.where(name >= halo, 1, 0).astype(jnp.int32)
-    return side * halo + lists_ref[side, name - side * halo]
-
-
-def middle_body(first, which, *refs):
-    out_ref, slots_ref = refs[-2:]
-    out_ref[...] = halo_total(first, which, *refs[:-2], slots_ref)
+def halo_total(halo, chunks, which, cols_ref, live_ref, list_ref, places_ref, hessian_ref, *rest):
+    *group, total_ref, slots_ref = rest
+    fill_slots(slots_ref, cols_ref, live_ref, [(places_ref[3], halo, 0, lambda name: list_ref[name])])
+    return accumulate(slots_ref, hessian_ref, group, places_ref[which], total_ref[...])
+
+
+def split_refs(refs, chunks, extra):
+    cut = 5 + chunks + 1
+    return refs[:cut], refs[cut : cut + extra], refs[cut + extra : -1], refs[-1]
+
+
+def middle_body(halo, chunks, which, *refs):
+    common, _, (out_ref,), slots_ref = split_refs(refs, chunks, 0)
+    out_ref[...] = halo_total(halo, chunks, which, *common, slots_ref)
 
 
 def interval(bounds_ref):
     return 0.5 * (bounds_ref[0] + bounds_ref[1]), 0.5 * (bounds_ref[1] - bounds_ref[0])
 
 
-def first_body(first, which, *refs):
-    *operands, bounds_ref, vectors_ref, one_ref, cast_ref, slots_ref = refs
+def store_cast(value, cast_refs):
+    width = value.shape[1] // len(cast_refs)
+    for at, cast_ref in enumerate(cast_refs):
+        cast_ref[...] = value[:, at * width : (at + 1) * width].astype(jnp.bfloat16)
+
+
+def first_body(halo, chunks, which, *refs):
+    common, (bounds_ref, vectors_ref), (one_ref, *cast_refs), slots_ref = split_refs(refs, chunks, 2)
     centre, half = interval(bounds_ref)
-    total = halo_total(first, which, *operands, slots_ref)
+    total = halo_total(halo, chunks, which, *common, slots_ref)
     one = (total - centre * vectors_ref[...]) / half
     one_ref[...] = one
-    cast_ref[...] = one.astype(jnp.bfloat16)
-
-
-def second_body(first, which, *refs):
-    *operands, bounds_ref, one_ref, vectors_ref, two_ref, cast_ref, slots_ref = refs
+    store_cast(one, cast_refs)
+
+
+def second_body(halo, chunks, which, *refs):
+    common, (bounds_ref, one_ref, vectors_ref), (two_ref, *cast_refs), slots_ref = split_refs(refs, chunks, 3)
     centre, half = interval(bounds_ref)
-    total = halo_total(first, which, *operands, slots_ref)
+    total = halo_total(halo, chunks, which, *common, slots_ref)
     two = 2.0 * (total - centre * one_ref[...]) / half - vectors_ref[...]
     two_ref[...] = two
-    cast_ref[...] = two.astype(jnp.bfloat16)
+    store_cast(two, cast_refs)
 
 
 def place_rows(number_ref, piece, rows):
@@ -148,9 +170,9 @@
     scatter_pieces(number_ref, out_ref, jnp.concatenate(tiles, 0))
 
 
-def third_body(first, which, *refs):
-    *operands, number_ref, two_ref, out_ref, slots_ref = refs
-    image = halo_total(first, which, *operands, slots_ref)
+def third_body(halo, chunks, which, *refs):
+    common, (number_ref, two_ref), (out_ref,), slots_ref = split_refs(refs, chunks, 2)
+    image = halo_total(halo, chunks, which, *common, slots_ref)
     scatter_pieces(number_ref, out_ref, exact_dot(two_ref[...], image, TN))
 
 
@@ -261,13 +283,13 @@
 
     def unpack(gram):
         body = functools.partial(unpack_body, total_rows)
-        return kernel_call(body, (tile,) * len(names), [SMEM, VMEM], work // 8, gram.size)(number, gram)
+        return tuple(kernel_call(body, [tile] * len(names), [SMEM, VMEM], work // 8, gram.size)(number, gram))
 
     def elimination(at, first, last):
         def stage(tiles):
             place = names.index((at, at))
-            call = kernel_call(functools.partial(eliminate_body, first, last), tile, [VMEM], work // 2, TILE * TILE)
-            return tiles[:place] + (call(tiles[place]),) + tiles[place + 1 :]
+            call = kernel_call(functools.partial(eliminate_body, first, last), [tile], [VMEM], work // 2, TILE * TILE)
+            return tiles[:place] + tuple(call(tiles[place])) + tiles[place + 1 :]
 
         return stage
 
@@ -275,16 +297,16 @@
         def stage(tiles):
             picked = [index for index, name in enumerate(names) if name[1] >= at]
             body = functools.partial(update_body, at, count)
-            call = kernel_call(body, (tile,) * len(picked), [VMEM] * len(picked), work // 4, TILE * TILE)
+            call = kernel_call(body, [tile] * len(picked), [VMEM] * len(picked), work // 4, TILE * TILE)
             new = call(*[tiles[index] for index in picked])
             return tuple(new[picked.index(index)] if index in picked else old for index, old in enumerate(tiles))
 
         return stage
 
     def finish(tiles):
-        outs = (jax.ShapeDtypeStruct((rows, modes), jnp.float32), jax.ShapeDtypeStruct((modes, modes), jnp.float32))
+        outs = [(None, jax.ShapeDtypeStruct((rows, modes), jnp.float32)), jax.ShapeDtypeStruct((modes, modes), jnp.float32)]
         body = functools.partial(basis_body, count)
-        return kernel_call(body, outs, [VMEM] * (len(names) + 1), work // 2, rows * modes)(*tiles, two)
+        return tuple(kernel_call(body, outs, [VMEM] * (len(names) + 1), work // 2, rows * modes)(*tiles, two))
 
     groups = TILE // GROUP
     cuts = [0, groups // 4, groups // 2 + 1, groups]
@@ -357,117 +379,137 @@
 def local(vectors, hessian, block_cols, live_blocks, halo_lists, bounds):
     row_blocks, stored, size, _ = hessian.shape
     rows, modes = vectors.shape
-    splits = lax.axis_size("split")
+    splits, regions = lax.axis_size("split"), lax.axis_size("region")
     region_blocks = row_blocks * splits
     halo_blocks = halo_lists.shape[2]
-    whole = halo_blocks == region_blocks and region_blocks <= 256
-    total_rows = rows * lax.axis_size(AXES)
-
-    paired = whole and splits == 2
+    total_rows = float(rows * splits * regions)
+    relayed = halo_blocks == region_blocks <= 256 and splits == 2 and regions % 2 == 0
+    chunks = CHUNKS if relayed else 1
+    width = modes // chunks
     core = lax.axis_index("split").astype(jnp.int32)
-    swapped = lambda value: lax.ppermute(value, "split", [(0, 1), (1, 0)])
-    near_first = [core * row_blocks, (1 - core) * row_blocks] if paired else [0]
-    bases = jnp.stack(near_first).astype(jnp.int32) if paired else jnp.zeros((1,), jnp.int32)
-
-    def sent(operand, region):
-        if whole:
-            return operand, operand
-        width = modes // splits
-        start = core * width
-        blocks = region[:, :rows].reshape(region_blocks, size, modes)
-        share = lambda listed: lax.dynamic_slice_in_dim(blocks[listed], start, width, 2).reshape(-1, width)
-        return share(halo_lists[0, 1]), share(halo_lists[0, 0])
-
-    def gathered(value):
-        if paired:
-            return [value[None], swapped(value)[None]]
-        if whole:
-            return [lax.all_gather(value, "split", axis=0)]
-        return [lax.all_gather(value, "split", axis=1, tiled=True)[None]]
-
-    listed = jnp.pad(halo_lists[0], ((0, LIST_ROWS - 2), (0, modes - halo_blocks)))
-    first = vectors.astype(jnp.bfloat16)
-    if whole:
-        first = jnp.concatenate([first, listed.astype(jnp.bfloat16)], 0)
-
-    def near_parts(operand):
-        if paired:
-            return [operand[None], swapped(operand)[None]]
-        return [lax.all_gather(operand, "split", axis=0)]
-
-    def exchange(operand):
-        near = near_parts(operand)
-        up, down = sent(operand, near[0])
-        return near, shifted(up, "region", 1), shifted(down, "region", -1)
-
-    first_near, first_lower, first_upper = exchange(first)
-    if whole:
-        orders = [first_lower[rows + 1, :halo_blocks], first_upper[rows, :halo_blocks]]
-        lists = jnp.stack(orders).astype(jnp.int32)
-    else:
-        lists = jnp.broadcast_to(jnp.arange(halo_blocks, dtype=jnp.int32), (2, halo_blocks))
-
-    wide = jax.ShapeDtypeStruct((rows, modes), jnp.float32)
-    narrow = jax.ShapeDtypeStruct((rows, modes), jnp.bfloat16)
-    square = jax.ShapeDtypeStruct((modes, modes), jnp.float32)
-    tile_rows = len(lower_tiles(modes // TILE)) * TILE
-    work = 2 * rows * size * modes
-    square_work = 2 * rows * modes * modes
-    traffic = hessian.size * 2 + 3 * rows * modes * 4
+    odd = (lax.axis_index("region") % 2).astype(jnp.int32)
+
     cores, *other_cores = axis_bits("split")
     near, across, *far = axis_bits("region")
     between = other_cores + far
     gram_number, cross_number = device_number([cores, across]), device_number([cores, near])
-    halo_slots = (row_blocks, 2 * halo_blocks + 1)
-
-    def step(body, outs, own, lower, upper, scalars, extra, beside=()):
+
+    wide = jax.ShapeDtypeStruct((rows, modes), jnp.float32)
+    casts = [jax.ShapeDtypeStruct((rows, width), jnp.bfloat16)] * chunks
+    square = jax.ShapeDtypeStruct((modes, modes), jnp.float32)
+    work = 2 * rows * size * modes
+    square_work = 2 * rows * modes * modes
+    traffic = hessian.size * 2 + 3 * rows * modes * 4
+
+    def other_core(parts):
+        return [partner_value(part, *cores) for part in parts]
+
+    def passed_on(value):
+        pairs = [(at, (at + (-2 if at % 2 else 2)) % regions) for at in range(regions)]
+        return lax.ppermute(value, "region", pairs)
+
+    def wrapped(parts):
+        return [part[None] for part in parts]
+
+    if relayed:
+        near_places = [core * row_blocks, (1 - core) * row_blocks]
+        partner_first = region_blocks + halo_blocks * (1 - odd)
+        places = jnp.stack(near_places + [partner_first, region_blocks + halo_blocks * odd]).astype(jnp.int32)
+        side_places = [places, places]
+    else:
+        side_places = [jnp.array([0, 0, 0, region_blocks + side * halo_blocks], jnp.int32) for side in range(2)]
+        places = side_places[0]
+
+    def exchange(parts):
+        if relayed:
+            partner = [partner_value(part, *near) for part in parts]
+            distant = [passed_on(part) for part in partner]
+            return [parts, other_core(parts), partner, other_core(partner)], [distant]
+        (operand,) = parts
+        region = lax.all_gather(operand, "split", axis=0)
+        share = modes // splits
+        blocks = region.reshape(region_blocks, size, modes)
+        sent = lambda listed: lax.dynamic_slice_in_dim(blocks[listed], core * share, share, 2).reshape(-1, share)
+        lower = shifted(sent(halo_lists[0, 1]), "region", 1)
+        upper = shifted(sent(halo_lists[0, 0]), "region", -1)
+        return [[region]], [[lower], [upper]]
+
+    def step(body, outs, exchanged, lists, extra, extra_specs, beside=()):
+        nearby, sides = exchanged
+        nearby = [group if group[0].ndim == 3 else wrapped(group) for group in nearby]
+        operands = [part for group in nearby for part in group]
+        columns = region_blocks + (halo_blocks if relayed else 0) + 1
         call = kernel_call(
-            functools.partial(near_body, region_blocks),
-            wide,
-            [SMEM] * 3 + [VMEM] * (1 + len(own)),
-            work * region_blocks,
+            functools.partial(near_body, region_blocks, halo_blocks, chunks),
+            [wide],
+            [SMEM] * 4 + [VMEM] * (1 + len(operands)),
+            work * columns,
             traffic,
-            (row_blocks, region_blocks + 1),
+            (row_blocks, columns),
         )
-        total = call(block_cols, live_blocks, bases, hessian, *own)
-        lower, upper, total, beside = lax.optimization_barrier((lower, upper, total, beside))
-        pairs = list(zip(gathered(lower), gathered(upper)))
-        for which, pair in enumerate(pairs):
-            last = which == len(pairs) - 1
-            given = (block_cols, live_blocks, lists, bases, hessian, *pair, total) + ((*scalars, *extra) if last else ())
-            specs = [SMEM] * 4 + [VMEM] * 4 + ([SMEM] * len(scalars) + [VMEM] * len(extra) if last else [])
-            body_of = functools.partial(body if last else middle_body, region_blocks, which)
-            cost = 2 * work * halo_blocks // len(pairs)
-            total = kernel_call(body_of, outs if last else wide, specs, cost, traffic, halo_slots)(*given)
-        return (total, beside) if beside else total
-
-    one, one_cast = step(first_body, (wide, narrow), first_near, first_lower, first_upper, (bounds,), (vectors,))
-    two, two_cast = step(second_body, (wide, narrow), *exchange(one_cast), (bounds,), (one, vectors))
-
+        (total,) = call(block_cols, live_blocks, lists[0], places, hessian, *operands)
+        sides, total, beside = lax.optimization_barrier((sides, total, beside))
+        pieces = []
+        for side, parts in enumerate(sides):
+            if relayed:
+                pieces += [(side, 0, wrapped(parts)), (side, 1, wrapped(other_core(parts)))]
+            else:
+                pieces.append((side, 0, [lax.all_gather(parts[0], "split", axis=1, tiled=True)[None]]))
+        for at, (side, which, parts) in enumerate(pieces):
+            last = at == len(pieces) - 1
+            given = (block_cols, live_blocks, lists[-1 if relayed else side], side_places[side], hessian, *parts, total)
+            specs = [SMEM] * 4 + [VMEM] * (2 + len(parts))
+            body_of = functools.partial(body if last else middle_body, halo_blocks, chunks, which)
+            cost, table = work * halo_blocks // len(pieces), (row_blocks, halo_blocks + 1)
+            if last:
+                result = kernel_call(body_of, outs, specs + extra_specs, cost, traffic, table)(*given, *extra)
+            else:
+                (total,) = kernel_call(body_of, [wide], specs, cost, traffic, table)(*given)
+        return (result, beside) if beside else result
+
+    first = vectors.astype(jnp.bfloat16)
+    parts = [first[:, at * width : (at + 1) * width] for at in range(chunks)]
+    if relayed:
+        listed = jnp.pad(halo_lists[0], ((0, LIST_ROWS - 2), (0, width - halo_blocks)))
+        parts[0] = jnp.concatenate([parts[0], listed.astype(jnp.bfloat16)], 0)
+    exchanged = exchange(parts)
+    if relayed:
+        partner, ((distant, *_),) = exchanged[0][2][0], exchanged[1]
+        numbers = lambda part: part[rows : rows + 2, :halo_blocks].astype(jnp.int32)
+        chosen = lambda pair, side: jnp.where(side == 0, pair[0], pair[1])
+        lists = [chosen(numbers(partner), odd), chosen(numbers(distant), 1 - odd)]
+    else:
+        lists = [jnp.arange(halo_blocks, dtype=jnp.int32)] * 2
+
+    filtering = [SMEM, VMEM, VMEM]
+    one, *parts = step(first_body, [wide] + casts, exchanged, lists, (bounds, vectors), filtering[:2])
+    two, *parts = step(second_body, [wide] + casts, exchange(parts), lists, (bounds, one, vectors), filtering)
+
+    tile_rows = len(lower_tiles(modes // TILE)) * TILE
     packed = jax.ShapeDtypeStruct((tile_rows, TILE), jnp.float32)
-    third = exchange(two_cast)
-    gram = kernel_call(gram_body, packed, [SMEM, VMEM], square_work, traffic)(gram_number, two)
-    for step_of in [halving(*cores), halving(*across)] + [doubling(*bit) for bit in between]:
+    third = exchange(parts)
+    (gram,) = kernel_call(gram_body, [packed], [SMEM, VMEM], square_work, traffic)(gram_number, two)
+    for step_of in [halving(*cores), halving(*across), doubling(*near)]:
         gram = step_of(gram)()
-    cross, (gram,) = step(third_body, square, *third, (cross_number,), (two,), (gram,))
-    cross = halving(*cores)(cross)()
+    (cross,), (gram,) = step(third_body, [square], third, lists, (cross_number, two), [SMEM, VMEM], (gram,))
+    cross = halving(*near)(halving(*cores)(cross)())()
 
     fold = modes // TILE
     cut = gram.shape[0] // fold
     folded = jnp.concatenate([gram[at * cut : (at + 1) * cut] for at in range(fold)], 1)
     flat = lambda value: [value[:, at * TILE : (at + 1) * TILE] for at in range(fold)]
-    half = cross.shape[0] // 2
-    got = partner_value(jnp.concatenate([folded, cross[half:]], 0), *near)
-    both = jnp.concatenate([folded, cross[:half]], 0) + got
+    both = jnp.concatenate([folded, cross], 0)
+    for bit in between:
+        both = doubling(*bit)(both)()
     got = partner_value(both, *across)
     gram = joining(*cores)(jnp.concatenate(flat(both[:cut]) + flat(got[:cut]), 0))()
     cross = both[cut:] + got[cut:]
-    stages = factor_stages(float(total_rows), modes // TILE, gram_number, two)
-    steps = [doubling(*bit) for bit in between] + [joining(*near), joining(*cores)]
+    stages = factor_stages(total_rows, modes // TILE, gram_number, two)
+    steps = [joining(*near), joining(*cores)]
     cross, (basis, inverse) = run_beside(cross, steps, gram, stages)
-    body_of = functools.partial(projected_body, float(total_rows))
-    call = kernel_call(body_of, square, [SMEM] + [VMEM] * 2, 2 * square_work, traffic)
-    return basis, call(cross_number, cross, inverse)
+    body_of = functools.partial(projected_body, total_rows)
+    call = kernel_call(body_of, [(None, square)], [SMEM] + [VMEM] * 2, 2 * square_work, traffic)
+    return basis, call(cross_number, cross, inverse)[0]
 
 
 def solution(mesh):

time: 116 us -> 131 us (1.13)
  waiting for transfers between devices: 38.2 us -> 45.4 us
  local copies, waits for them, and re-layouts: 9.61 us -> 15.8 us
  other arithmetic: 2.67 us -> 3.99 us
    ppermute x12 -> x35, starting transfers between devices: 10.9 us -> 27.8 us  [partner_value(): lax.ppermute(value, axis, [(at, at ^ bit) for at in range(lax.axis_size(a...]
    ppermute x15 -> x6, starting transfers between devices: 22.4 us -> 5.63 us  [passed_on(): return lax.ppermute(value, 'region', pairs)]
    ppermute x12 -> x35, waiting for transfers between devices: 22.9 us -> 32.2 us  [partner_value(): lax.ppermute(value, axis, [(at, at ^ bit) for at in range(lax.axis_size(a...]
    unnamed x40 -> x56, local copies, waits for them, and re-layouts: 9.54 us -> 15.1 us
    ppermute x15 -> x6, waiting for transfers between devices: 15.3 us -> 13.2 us  [passed_on(): return lax.ppermute(value, 'region', pairs)]
  transfers between devices with their start and end apart: 27 -> 41, of which waited for: 14 -> 18; matrix products, arithmetic and copies ran while one was open for 1% -> 1% of each run, Pallas kernels for 18% -> 17%
where the time goes in v8:
time: 131 us; the launch traced here: 130 us
  waiting for transfers between devices  45.4 us (35%)
  starting transfers between devices  33.5 us (26%)
  Pallas kernels  30.5 us (23%)
  local copies, waits for them, and re-layouts  15.8 us (12%)
  other arithmetic  3.99 us (3%)
    ppermute x35, waiting for transfers between devices, partner_value(): lax.ppermute(value, axis, [(at, at ^ bit) for at in range(lax.axis_size(a...  32.2 us
    pallas_call x20, Pallas kernels, run(): return call(*placed)  30.5 us
    ppermute x35, starting transfers between devices, partner_value(): lax.ppermute(value, axis, [(at, at ^ bit) for at in range(lax.axis_size(a...  27.8 us
    unnamed x56, local copies, waits for them, and re-layouts  15.1 us
    ppermute x6, waiting for transfers between devices, passed_on(): return lax.ppermute(value, 'region', pairs)  13.2 us
    ppermute x6, starting transfers between devices, passed_on(): return lax.ppermute(value, 'region', pairs)  5.63 us
  transfers between devices with their start and end apart: 41, of which 18 were waited for; matrix products, arithmetic and copies ran while one was open for 1% of the time, Pallas kernels for 17%

profile of v8, /device:TPU:1, one launch (start us, length us, event | category | flops | bytes accessed | tf_op | source)
XLA Modules:
  0.0 130.3 jit_solution(9320745768987432258)
XLA Ops:
  3.8 2.0 %collective-permute-start = (bf16[592,128]{1,0:T(8,128)(2,1)S(1)}, bf16[592,128]{1,0:T(8,128)(2,1)}, u32[]{:S(2)}, u32[]{:S(2)}) collective-permute-start(bf16[592,128]{1,0:T(8,128)(2,1)S(1)} %get-tuple-element.72), channel_id=1, source_target_pairs={{0,2},{2,0},{4,6},{6,4},{8,10},{10,8},{12,14},{14,12},{16,18},{18,... | collective-permute-start | bytes 454664 | tf_op jit(solution)/shard_map/ppermute | solution.py:326
  6.9 5.9 %collective-permute-done.2 = bf16[576,128]{1,0:T(8,128)(2,1)} collective-permute-done((bf16[576,128]{1,0:T(8,128)(2,1)S(1)}, bf16[576,128]{1,0:T(8,128)(2,1)}, u32[]{:S(2)}, u32[]{:S(2)}) %collective-permute-start.2) | collective-permute-done | bytes 147488 | tf_op jit(solution)/shard_map/ppermute | solution.py:326
  14.0 1.5 %collective-permute-start.3 = (bf16[576,128]{1,0:T(8,128)(2,1)}, bf16[576,128]{1,0:T(8,128)(2,1)S(1)}, u32[]{:S(2)}, u32[]{:S(2)}) collective-permute-start(bf16[576,128]{1,0:T(8,128)(2,1)} %collective-permute-done.2), channel_id=1, source_target_pairs={{0,4},{2,30},{4,8},{6,2},{8,12},{10,6},{12,16},{14,10},{16,20},{18... | collective-permute-start | bytes 442376 | tf_op jit(solution)/shard_map/ppermute | solution.py:409
  19.1 2.0 %copy-done = bf16[3,12,192,192]{3,2,1,0:T(8,128)(2,1)S(1)} copy-done((bf16[3,12,192,192]{3,2,1,0:T(8,128)(2,1)S(1)}, bf16[3,12,192,192]{3,2,1,0:T(8,128)(2,1)}, u32[]{:S(2)}) %copy-start) | copy-done | bytes 2654232
  26.0 2.5 %shard_map.77.refs_7_ = f32[576,256]{1,0:T(8,128)S(1)} custom-call(s32[3,12]{1,0:T(4,128)S(1)} %copy-done.14, s32[3]{0:T(128)S(1)} %copy-done.20, s32[6]{0:T(128)S(1)} %fusion.3.refs_2_, s32[4]{0:T(128)S(1)} %pad_add_fusion.refs_3_, bf16[3,12,192,192]{3,2,1,0:T(8,128)(2,1)S(1)} %copy-done, bf16[1,592,128]{2,1,0:T(8,128)(2,1)S(1)} %copy-done.10, ...), custom_call_target="tpu_custom_call" | custom-call | flops 46006272 | bytes 276480 | tf_op jit(solution)/shard_map/pallas_call | solution.py:51
  32.6 3.2 %collective-permute-start.10 = (bf16[576,128]{1,0:T(8,128)(2,1)S(1)}, bf16[576,128]{1,0:T(8,128)(2,1)S(1)}, u32[]{:S(2)}, u32[]{:S(2)}) collective-permute-start(bf16[576,128]{1,0:T(8,128)(2,1)S(1)} %get-tuple-element.38), channel_id=1, source_target_pairs={{0,2},{2,0},{4,6},{6,4},{8,10},{10,8},{12,14},{14,12},{16,18},{18,... | collective-permute-start | bytes 442376 | tf_op jit(solution)/shard_map/ppermute | solution.py:326
  36.6 3.2 %collective-permute-done.10 = bf16[576,128]{1,0:T(8,128)(2,1)S(1)} collective-permute-done((bf16[576,128]{1,0:T(8,128)(2,1)S(1)}, bf16[576,128]{1,0:T(8,128)(2,1)S(1)}, u32[]{:S(2)}, u32[]{:S(2)}) %collective-permute-start.10) | collective-permute-done | bytes 147488 | tf_op jit(solution)/shard_map/ppermute | solution.py:326
  41.2 1.8 %collective-permute-done.12 = bf16[576,128]{1,0:T(8,128)(2,1)S(1)} collective-permute-done((bf16[576,128]{1,0:T(8,128)(2,1)S(1)}, bf16[576,128]{1,0:T(8,128)(2,1)S(1)}, u32[]{:S(2)}, u32[]{:S(2)}) %collective-permute-start.12) | collective-permute-done | bytes 147488 | tf_op jit(solution)/shard_map/ppermute | solution.py:326
  45.1 2.0 %shard_map.80.refs_7_ = f32[576,256]{1,0:T(8,128)S(1)} custom-call(s32[3,12]{1,0:T(4,128)S(1)} %copy-done.14, s32[3]{0:T(128)S(1)} %copy-done.20, s32[6]{0:T(128)S(1)} %fusion.3.refs_2_, s32[4]{0:T(128)S(1)} %pad_add_fusion.refs_3_, bf16[3,12,192,192]{3,2,1,0:T(8,128)(2,1)S(1)} %copy-done.1, bf16[1,576,128]{2,1,0:T(8,128)(2,1)S(1)} %bitcast.61, ...), custom_call_target="tpu_custom_call" | custom-call | flops 46006272 | bytes 276480 | tf_op jit(solution)/shard_map/pallas_call | solution.py:51
  48.4 3.7 %collective-permute-done.11 = bf16[576,128]{1,0:T(8,128)(2,1)} collective-permute-done((bf16[576,128]{1,0:T(8,128)(2,1)S(1)}, bf16[576,128]{1,0:T(8,128)(2,1)}, u32[]{:S(2)}, u32[]{:S(2)}) %collective-permute-start.11) | collective-permute-done | bytes 147488 | tf_op jit(solution)/shard_map/ppermute | solution.py:409
  52.1 3.2 %collective-permute-done.13 = bf16[576,128]{1,0:T(8,128)(2,1)} collective-permute-done((bf16[576,128]{1,0:T(8,128)(2,1)S(1)}, bf16[576,128]{1,0:T(8,128)(2,1)}, u32[]{:S(2)}, u32[]{:S(2)}) %collective-permute-start.13) | collective-permute-done | bytes 147488 | tf_op jit(solution)/shard_map/ppermute | solution.py:409
  57.2 1.6 %shard_map.81.refs_7_ = f32[576,256]{1,0:T(8,128)S(1)} custom-call(s32[3,12]{1,0:T(4,128)S(1)} %copy-done.15, s32[3]{0:T(128)S(1)} %copy-done.21, s32[6]{0:T(128)S(1)} %fusion.2.refs_2_, s32[4]{0:T(128)S(1)} %pad_add_fusion.refs_3_, bf16[3,12,192,192]{3,2,1,0:T(8,128)(2,1)S(1)} %copy-done.1, bf16[1,576,128]{2,1,0:T(8,128)(2,1)} %bitcast.29.refs_5_, ...), custom_call_target="tpu_custom_call" | custom-call | flops 10616832 | bytes 276480 | tf_op jit(solution)/shard_map/pallas_call | solution.py:51
  59.5 1.6 %shard_map.82 = (f32[576,256]{1,0:T(8,128)S(1)}, bf16[576,128]{1,0:T(8,128)(2,1)S(1)}, bf16[576,128]{1,0:T(8,128)(2,1)S(1)}) custom-call(s32[3,12]{1,0:T(4,128)S(1)} %copy-done.15, s32[3]{0:T(128)S(1)} %copy-done.21, s32[6]{0:T(128)S(1)} %fusion.2.refs_2_, s32[4]{0:T(128)S(1)} %pad_add_fusion.refs_3_, bf16[3,12,192,192]{3,2,1,0:T(8,128)(2,1)S(1)} %copy-done.1, ...), custom_call_target="tpu_custom_call" | custom-call | flops 10616832 | bytes 276480 | tf_op jit(solution)/shard_map/pallas_call | solution.py:51
  69.8 2.0 %collective-permute-start.26 = (bf16[576,128]{1,0:T(8,128)(2,1)S(1)}, bf16[576,128]{1,0:T(8,128)(2,1)S(1)}, u32[]{:S(2)}, u32[]{:S(2)}) collective-permute-start(bf16[576,128]{1,0:T(8,128)(2,1)S(1)} %collective-permute-done.20), channel_id=1, source_target_pairs={{0,1},{1,0},{2,3},{3,2},{4,5},{5,4},{6,7},{7,6},{8,9},{9,8},{10,11... | collective-permute-start | bytes 442376 | tf_op jit(solution)/shard_map/ppermute | solution.py:326
  73.0 1.7 %collective-permute-start.27 = (bf16[576,128]{1,0:T(8,128)(2,1)S(1)}, bf16[576,128]{1,0:T(8,128)(2,1)S(1)}, u32[]{:S(2)}, u32[]{:S(2)}) collective-permute-start(bf16[576,128]{1,0:T(8,128)(2,1)S(1)} %collective-permute-done.22), channel_id=1, source_target_pairs={{0,1},{1,0},{2,3},{3,2},{4,5},{5,4},{6,7},{7,6},{8,9},{9,8},{10,11... | collective-permute-start | bytes 442376 | tf_op jit(solution)/shard_map/ppermute | solution.py:326
  74.7 1.4 %collective-permute-start.21 = (bf16[576,128]{1,0:T(8,128)(2,1)S(1)}, bf16[576,128]{1,0:T(8,128)(2,1)}, u32[]{:S(2)}, u32[]{:S(2)}) collective-permute-start(bf16[576,128]{1,0:T(8,128)(2,1)S(1)} %collective-permute-done.20), channel_id=1, source_target_pairs={{0,4},{2,30},{4,8},{6,2},{8,12},{10,6},{12,16},{14,10},{16,20},{18... | collective-permute-start | bytes 442376 | tf_op jit(solution)/shard_map/ppermute | solution.py:409
  77.0 2.0 %shard_map.83.refs_7_ = f32[576,256]{1,0:T(8,128)S(1)} custom-call(s32[3,12]{1,0:T(4,128)S(1)} %copy-done.15, s32[3]{0:T(128)S(1)} %copy-done.21, s32[6]{0:T(128)S(1)} %copy-done.23, s32[4]{0:T(128)S(1)} %pad_add_fusion.refs_3_, bf16[3,12,192,192]{3,2,1,0:T(8,128)(2,1)S(1)} %copy-done.1, bf16[1,576,128]{2,1,0:T(8,128)(2,1)S(1)} %bitcast.55, ...), custom_call_target="tpu_custom_call" | custom-call | flops 46006272 | bytes 276480 | tf_op jit(solution)/shard_map/pallas_call | solution.py:51
  79.8 3.2 %collective-permute-done.21 = bf16[576,128]{1,0:T(8,128)(2,1)} collective-permute-done((bf16[576,128]{1,0:T(8,128)(2,1)S(1)}, bf16[576,128]{1,0:T(8,128)(2,1)}, u32[]{:S(2)}, u32[]{:S(2)}) %collective-permute-start.21) | collective-permute-done | bytes 147488 | tf_op jit(solution)/shard_map/ppermute | solution.py:409
  83.0 3.2 %collective-permute-done.23 = bf16[576,128]{1,0:T(8,128)(2,1)} collective-permute-done((bf16[576,128]{1,0:T(8,128)(2,1)S(1)}, bf16[576,128]{1,0:T(8,128)(2,1)}, u32[]{:S(2)}, u32[]{:S(2)}) %collective-permute-start.23) | collective-permute-done | bytes 147488 | tf_op jit(solution)/shard_map/ppermute | solution.py:409
  88.0 1.6 %shard_map.85.refs_7_ = f32[576,256]{1,0:T(8,128)S(1)} custom-call(s32[3,12]{1,0:T(4,128)S(1)} %copy-done.15, s32[3]{0:T(128)S(1)} %copy-done.21, s32[6]{0:T(128)S(1)} %fusion.2.refs_2_, s32[4]{0:T(128)S(1)} %pad_add_fusion.refs_3_, bf16[3,12,192,192]{3,2,1,0:T(8,128)(2,1)S(1)} %copy-done.1, bf16[1,576,128]{2,1,0:T(8,128)(2,1)} %bitcast.42.refs_5_, ...), custom_call_target="tpu_custom_call" | custom-call | flops 10616832 | bytes 276480 | tf_op jit(solution)/shard_map/pallas_call | solution.py:51
  89.7 2.7 %shard_map.86 = f32[256,256]{1,0:T(8,128)S(1)} custom-call(s32[3,12]{1,0:T(4,128)S(1)} %copy-done.15, s32[3]{0:T(128)S(1)} %copy-done.21, s32[6]{0:T(128)S(1)} %fusion.2.refs_2_, s32[4]{0:T(128)S(1)} %pad_add_fusion.refs_3_, bf16[3,12,192,192]{3,2,1,0:T(8,128)(2,1)S(1)} %copy-done.1, bf16[1,576,128]{2,1,0:T(8,128)(2,1)} %bitcast.40.refs_5_, ...), custom_call_target="tpu_custom_call" | custom-call | flops 10616832 | bytes 276480 | tf_op jit(solution)/shard_map/pallas_call | solution.py:51
  94.1 3.1 %collective-permute-done.34 = f32[64,256]{1,0:T(8,128)S(1)} collective-permute-done((f32[64,256]{1,0:T(8,128)S(1)}, f32[64,256]{1,0:T(8,128)S(1)}, u32[]{:S(2)}, u32[]{:S(2)}) %collective-permute-start.34) | collective-permute-done | bytes 65568 | tf_op jit(solution)/shard_map/ppermute | solution.py:326
  97.3 3.6 %collective-permute-done.35 = f32[112,256]{1,0:T(8,128)S(1)} collective-permute-done((f32[112,256]{1,0:T(8,128)S(1)}, f32[112,256]{1,0:T(8,128)S(1)}, u32[]{:S(2)}, u32[]{:S(2)}) %collective-permute-start.35) | collective-permute-done | bytes 114720 | tf_op jit(solution)/shard_map/ppermute | solution.py:326
  101.0 5.5 %collective-permute-done.36 = f32[112,256]{1,0:T(8,128)S(1)} collective-permute-done((f32[112,256]{1,0:T(8,128)S(1)}, f32[112,256]{1,0:T(8,128)S(1)}, u32[]{:S(2)}, u32[]{:S(2)}) %collective-permute-start.36) | collective-permute-done | bytes 114720 | tf_op jit(solution)/shard_map/ppermute | solution.py:326
  106.6 3.6 %collective-permute-done.37 = f32[112,256]{1,0:T(8,128)S(1)} collective-permute-done((f32[112,256]{1,0:T(8,128)S(1)}, f32[112,256]{1,0:T(8,128)S(1)}, u32[]{:S(2)}, u32[]{:S(2)}) %collective-permute-start.37) | collective-permute-done | bytes 114720 | tf_op jit(solution)/shard_map/ppermute | solution.py:326
  110.3 4.7 %collective-permute-start.38 = (f32[192,128]{1,0:T(8,128)S(1)}, f32[192,128]{1,0:T(8,128)S(1)}, u32[]{:S(2)}, u32[]{:S(2)}) collective-permute-start(f32[192,128]{1,0:T(8,128)S(1)} %pad_maximum_fusion.3), channel_id=1, source_target_pairs={{0,1},{1,0},{2,3},{3,2},{4,5},{5,4},{6,7},{7,6},{8,9},{9,8},{10,11... | collective-permute-start | bytes 294920 | tf_op jit(solution)/shard_map/ppermute | solution.py:326
  116.5 1.5 %shard_map.88.tile_ref = f32[128,128]{1,0:T(8,128)S(1)} custom-call(f32[128,128]{1,0:T(8,128)S(1)} %get-tuple-element.53.tile_ref), custom_call_target="tpu_custom_call" | custom-call | flops 125000000 | bytes 1024 | tf_op jit(solution)/shard_map/pallas_call | solution.py:51
  119.2 1.7 %shard_map.90.refs_0_ = f32[128,128]{1,0:T(8,128)S(1)} custom-call(f32[128,128]{1,0:T(8,128)S(1)} %shard_map.89.tile_ref), custom_call_target="tpu_custom_call" | custom-call | flops 125000000 | bytes 1024 | tf_op jit(solution)/shard_map/pallas_call | solution.py:51
  122.3 1.5 %shard_map.92.tile_ref = f32[128,128]{1,0:T(8,128)S(1)} custom-call(f32[128,128]{1,0:T(8,128)S(1)} %get-tuple-element.62.tile_ref), custom_call_target="tpu_custom_call" | custom-call | flops 125000000 | bytes 1024 | tf_op jit(solution)/shard_map/pallas_call | solution.py:51
  125.0 1.7 %shard_map.94.refs_2_ = f32[128,128]{1,0:T(8,128)S(1)} custom-call(f32[128,128]{1,0:T(8,128)S(1)} %shard_map.93.tile_ref), custom_call_target="tpu_custom_call" | custom-call | flops 125000000 | bytes 1024 | tf_op jit(solution)/shard_map/pallas_call | solution.py:51
  126.7 1.9 %shard_map.95 = (f32[576,256]{1,0:T(8,128)}, f32[256,256]{1,0:T(8,128)S(1)}) custom-call(f32[128,128]{1,0:T(8,128)S(1)} %get-tuple-element.60.refs_0_, f32[128,128]{1,0:T(8,128)S(1)} %get-tuple-element.61.refs_1_, f32[128,128]{1,0:T(8,128)S(1)} %shard_map.94.refs_2_, f32[576,256]{1,0:T(8,128)S(1)} %copy-done.5), custom_call_target="tpu_custom_call" | custom-call | flops 125000000 | bytes 9216 | tf_op jit(solution)/shard_map/pallas_call | solution.py:51
  128.6 1.7 %shard_map.96 = f32[256,256]{1,0:T(8,128)} custom-call(s32[1]{0:T(128)} %bitcast.44.refs_8_.number_ref, f32[256,256]{1,0:T(8,128)S(1)} %pad_maximum_fusion.cross_ref, f32[256,256]{1,0:T(8,128)S(1)} %get-tuple-element.67.inverse_ref), custom_call_target="tpu_custom_call" | custom-call | flops 9437184 | bytes 276480 | tf_op jit(solution)/shard_map/pallas_call | solution.py:51
  (155 shorter events, 46.8 us)
Async XLA Ops:
  3.8 11.7 %collective-permute-start = (bf16[592,128]{1,0:T(8,128)(2,1)S(1)}, bf16[592,128]{1,0:T(8,128)(2,1)}, u32[]{:S(2)}, u32[]{:S(2)}) collective-permute-start(bf16[592,128]{1,0:T(8,128)(2,1)S(1)} %get-tuple-element.72), channel_id=1, source_target_pairs={{0,2},{2,0},{4,6},{6,4},{8,10},{10,8},{12,14},{14,12},{16,18},{18,... | collective-permute-start | bytes 454664 | tf_op jit(solution)/shard_map/ppermute | solution.py:326
  5.9 6.9 %collective-permute-start.2 = (bf16[576,128]{1,0:T(8,128)(2,1)S(1)}, bf16[576,128]{1,0:T(8,128)(2,1)}, u32[]{:S(2)}, u32[]{:S(2)}) collective-permute-start(bf16[576,128]{1,0:T(8,128)(2,1)S(1)} %get-tuple-element.69), channel_id=1, source_target_pairs={{0,2},{2,0},{4,6},{6,4},{8,10},{10,8},{12,14},{14,12},{16,18},{18,... | collective-permute-start | bytes 442376 | tf_op jit(solution)/shard_map/ppermute | solution.py:326
  5.9 12.5 %collective-permute-start.4 = (bf16[592,128]{1,0:T(8,128)(2,1)S(1)}, bf16[592,128]{1,0:T(8,128)(2,1)S(1)}, u32[]{:S(2)}, u32[]{:S(2)}) collective-permute-start(bf16[592,128]{1,0:T(8,128)(2,1)S(1)} %get-tuple-element.72), channel_id=1, source_target_pairs={{0,1},{1,0},{2,3},{3,2},{4,5},{5,4},{6,7},{7,6},{8,9},{9,8},{10,11... | collective-permute-start | bytes 454664 | tf_op jit(solution)/shard_map/ppermute | solution.py:326
  6.9 9.6 %collective-permute-start.5 = (bf16[576,128]{1,0:T(8,128)(2,1)S(1)}, bf16[576,128]{1,0:T(8,128)(2,1)S(1)}, u32[]{:S(2)}, u32[]{:S(2)}) collective-permute-start(bf16[576,128]{1,0:T(8,128)(2,1)S(1)} %get-tuple-element.69), channel_id=1, source_target_pairs={{0,1},{1,0},{2,3},{3,2},{4,5},{5,4},{6,7},{7,6},{8,9},{9,8},{10,11... | collective-permute-start | bytes 442376 | tf_op jit(solution)/shard_map/ppermute | solution.py:326
  12.8 6.3 %collective-permute-start.7 = (bf16[576,128]{1,0:T(8,128)(2,1)}, bf16[576,128]{1,0:T(8,128)(2,1)S(1)}, u32[]{:S(2)}, u32[]{:S(2)}) collective-permute-start(bf16[576,128]{1,0:T(8,128)(2,1)} %collective-permute-done.2), channel_id=1, source_target_pairs={{0,1},{1,0},{2,3},{3,2},{4,5},{5,4},{6,7},{7,6},{8,9},{9,8},{10,11... | collective-permute-start | bytes 442376 | tf_op jit(solution)/shard_map/ppermute | solution.py:326
  14.0 14.6 %collective-permute-start.3 = (bf16[576,128]{1,0:T(8,128)(2,1)}, bf16[576,128]{1,0:T(8,128)(2,1)S(1)}, u32[]{:S(2)}, u32[]{:S(2)}) collective-permute-start(bf16[576,128]{1,0:T(8,128)(2,1)} %collective-permute-done.2), channel_id=1, source_target_pairs={{0,4},{2,30},{4,8},{6,2},{8,12},{10,6},{12,16},{14,10},{16,20},{18... | collective-permute-start | bytes 442376 | tf_op jit(solution)/shard_map/ppermute | solution.py:409
  15.5 3.5 %collective-permute-start.6 = (bf16[592,128]{1,0:T(8,128)(2,1)}, bf16[592,128]{1,0:T(8,128)(2,1)S(1)}, u32[]{:S(2)}, u32[]{:S(2)}) collective-permute-start(bf16[592,128]{1,0:T(8,128)(2,1)} %collective-permute-done), channel_id=1, source_target_pairs={{0,1},{1,0},{2,3},{3,2},{4,5},{5,4},{6,7},{7,6},{8,9},{9,8},{10,11... | collective-permute-start | bytes 454664 | tf_op jit(solution)/shard_map/ppermute | solution.py:326
  17.1 11.5 %collective-permute-start.1 = (bf16[592,128]{1,0:T(8,128)(2,1)}, bf16[592,128]{1,0:T(8,128)(2,1)S(1)}, u32[]{:S(2)}, u32[]{:S(2)}) collective-permute-start(bf16[592,128]{1,0:T(8,128)(2,1)} %collective-permute-done), channel_id=1, source_target_pairs={{0,4},{2,30},{4,8},{6,2},{8,12},{10,6},{12,16},{14,10},{16,20},{18... | collective-permute-start | bytes 454664 | tf_op jit(solution)/shard_map/ppermute | solution.py:409
  32.6 7.2 %collective-permute-start.10 = (bf16[576,128]{1,0:T(8,128)(2,1)S(1)}, bf16[576,128]{1,0:T(8,128)(2,1)S(1)}, u32[]{:S(2)}, u32[]{:S(2)}) collective-permute-start(bf16[576,128]{1,0:T(8,128)(2,1)S(1)} %get-tuple-element.38), channel_id=1, source_target_pairs={{0,2},{2,0},{4,6},{6,4},{8,10},{10,8},{12,14},{14,12},{16,18},{18,... | collective-permute-start | bytes 442376 | tf_op jit(solution)/shard_map/ppermute | solution.py:326
  35.9 7.1 %collective-permute-start.12 = (bf16[576,128]{1,0:T(8,128)(2,1)S(1)}, bf16[576,128]{1,0:T(8,128)(2,1)S(1)}, u32[]{:S(2)}, u32[]{:S(2)}) collective-permute-start(bf16[576,128]{1,0:T(8,128)(2,1)S(1)} %get-tuple-element.39), channel_id=1, source_target_pairs={{0,2},{2,0},{4,6},{6,4},{8,10},{10,8},{12,14},{14,12},{16,18},{18,... | collective-permute-start | bytes 442376 | tf_op jit(solution)/shard_map/ppermute | solution.py:326
  35.9 9.2 %collective-permute-start.14 = (bf16[576,128]{1,0:T(8,128)(2,1)S(1)}, bf16[576,128]{1,0:T(8,128)(2,1)S(1)}, u32[]{:S(2)}, u32[]{:S(2)}) collective-permute-start(bf16[576,128]{1,0:T(8,128)(2,1)S(1)} %get-tuple-element.38), channel_id=1, source_target_pairs={{0,1},{1,0},{2,3},{3,2},{4,5},{5,4},{6,7},{7,6},{8,9},{9,8},{10,11... | collective-permute-start | bytes 442376 | tf_op jit(solution)/shard_map/ppermute | solution.py:326
  36.6 8.6 %collective-permute-start.15 = (bf16[576,128]{1,0:T(8,128)(2,1)S(1)}, bf16[576,128]{1,0:T(8,128)(2,1)S(1)}, u32[]{:S(2)}, u32[]{:S(2)}) collective-permute-start(bf16[576,128]{1,0:T(8,128)(2,1)S(1)} %get-tuple-element.39), channel_id=1, source_target_pairs={{0,1},{1,0},{2,3},{3,2},{4,5},{5,4},{6,7},{7,6},{8,9},{9,8},{10,11... | collective-permute-start | bytes 442376 | tf_op jit(solution)/shard_map/ppermute | solution.py:326
  39.8 5.3 %collective-permute-start.16 = (bf16[576,128]{1,0:T(8,128)(2,1)S(1)}, bf16[576,128]{1,0:T(8,128)(2,1)S(1)}, u32[]{:S(2)}, u32[]{:S(2)}) collective-permute-start(bf16[576,128]{1,0:T(8,128)(2,1)S(1)} %collective-permute-done.10), channel_id=1, source_target_pairs={{0,1},{1,0},{2,3},{3,2},{4,5},{5,4},{6,7},{7,6},{8,9},{9,8},{10,11... | collective-permute-start | bytes 442376 | tf_op jit(solution)/shard_map/ppermute | solution.py:326
  43.8 8.3 %collective-permute-start.11 = (bf16[576,128]{1,0:T(8,128)(2,1)S(1)}, bf16[576,128]{1,0:T(8,128)(2,1)}, u32[]{:S(2)}, u32[]{:S(2)}) collective-permute-start(bf16[576,128]{1,0:T(8,128)(2,1)S(1)} %collective-permute-done.10), channel_id=1, source_target_pairs={{0,4},{2,30},{4,8},{6,2},{8,12},{10,6},{12,16},{14,10},{16,20},{18... | collective-permute-start | bytes 442376 | tf_op jit(solution)/shard_map/ppermute | solution.py:409
  45.1 10.2 %collective-permute-start.13 = (bf16[576,128]{1,0:T(8,128)(2,1)S(1)}, bf16[576,128]{1,0:T(8,128)(2,1)}, u32[]{:S(2)}, u32[]{:S(2)}) collective-permute-start(bf16[576,128]{1,0:T(8,128)(2,1)S(1)} %collective-permute-done.12), channel_id=1, source_target_pairs={{0,4},{2,30},{4,8},{6,2},{8,12},{10,6},{12,16},{14,10},{16,20},{18... | collective-permute-start | bytes 442376 | tf_op jit(solution)/shard_map/ppermute | solution.py:409
  55.3 3.6 %collective-permute-start.18 = (bf16[576,128]{1,0:T(8,128)(2,1)}, bf16[576,128]{1,0:T(8,128)(2,1)}, u32[]{:S(2)}, u32[]{:S(2)}) collective-permute-start(bf16[576,128]{1,0:T(8,128)(2,1)} %collective-permute-done.11), channel_id=1, source_target_pairs={{0,1},{1,0},{2,3},{3,2},{4,5},{5,4},{6,7},{7,6},{8,9},{9,8},{10,11... | collective-permute-start | bytes 442376 | tf_op jit(solution)/shard_map/ppermute | solution.py:326
  64.7 5.1 %collective-permute-start.20 = (bf16[576,128]{1,0:T(8,128)(2,1)S(1)}, bf16[576,128]{1,0:T(8,128)(2,1)S(1)}, u32[]{:S(2)}, u32[]{:S(2)}) collective-permute-start(bf16[576,128]{1,0:T(8,128)(2,1)S(1)} %get-tuple-element.44), channel_id=1, source_target_pairs={{0,2},{2,0},{4,6},{6,4},{8,10},{10,8},{12,14},{14,12},{16,18},{18,... | collective-permute-start | bytes 442376 | tf_op jit(solution)/shard_map/ppermute | solution.py:326
  65.6 9.1 %collective-permute-start.24 = (bf16[576,128]{1,0:T(8,128)(2,1)S(1)}, bf16[576,128]{1,0:T(8,128)(2,1)S(1)}, u32[]{:S(2)}, u32[]{:S(2)}) collective-permute-start(bf16[576,128]{1,0:T(8,128)(2,1)S(1)} %get-tuple-element.44), channel_id=1, source_target_pairs={{0,1},{1,0},{2,3},{3,2},{4,5},{5,4},{6,7},{7,6},{8,9},{9,8},{10,11... | collective-permute-start | bytes 442376 | tf_op jit(solution)/shard_map/ppermute | solution.py:326
  66.5 6.5 %collective-permute-start.22 = (bf16[576,128]{1,0:T(8,128)(2,1)S(1)}, bf16[576,128]{1,0:T(8,128)(2,1)S(1)}, u32[]{:S(2)}, u32[]{:S(2)}) collective-permute-start(bf16[576,128]{1,0:T(8,128)(2,1)S(1)} %get-tuple-element.45), channel_id=1, source_target_pairs={{0,2},{2,0},{4,6},{6,4},{8,10},{10,8},{12,14},{14,12},{16,18},{18,... | collective-permute-start | bytes 442376 | tf_op jit(solution)/shard_map/ppermute | solution.py:326
  67.6 8.5 %collective-permute-start.30 = (f32[96,128]{1,0:T(8,128)S(1)}, f32[96,128]{1,0:T(8,128)S(1)}, u32[]{:S(2)}, u32[]{:S(2)}) collective-permute-start(f32[96,128]{1,0:T(8,128)S(1)} %slice_add_fusion.4), channel_id=1, source_target_pairs={{0,2},{2,0},{4,6},{6,4},{8,10},{10,8},{12,14},{14,12},{16,18},{18,... | collective-permute-start | bytes 147464 | tf_op jit(solution)/shard_map/ppermute | solution.py:326
  68.0 8.9 %collective-permute-start.25 = (bf16[576,128]{1,0:T(8,128)(2,1)S(1)}, bf16[576,128]{1,0:T(8,128)(2,1)S(1)}, u32[]{:S(2)}, u32[]{:S(2)}) collective-permute-start(bf16[576,128]{1,0:T(8,128)(2,1)S(1)} %get-tuple-element.45), channel_id=1, source_target_pairs={{0,1},{1,0},{2,3},{3,2},{4,5},{5,4},{6,7},{7,6},{8,9},{9,8},{10,11... | collective-permute-start | bytes 442376 | tf_op jit(solution)/shard_map/ppermute | solution.py:326
  69.8 7.1 %collective-permute-start.26 = (bf16[576,128]{1,0:T(8,128)(2,1)S(1)}, bf16[576,128]{1,0:T(8,128)(2,1)S(1)}, u32[]{:S(2)}, u32[]{:S(2)}) collective-permute-start(bf16[576,128]{1,0:T(8,128)(2,1)S(1)} %collective-permute-done.20), channel_id=1, source_target_pairs={{0,1},{1,0},{2,3},{3,2},{4,5},{5,4},{6,7},{7,6},{8,9},{9,8},{10,11... | collective-permute-start | bytes 442376 | tf_op jit(solution)/shard_map/ppermute | solution.py:326
  73.0 4.0 %collective-permute-start.27 = (bf16[576,128]{1,0:T(8,128)(2,1)S(1)}, bf16[576,128]{1,0:T(8,128)(2,1)S(1)}, u32[]{:S(2)}, u32[]{:S(2)}) collective-permute-start(bf16[576,128]{1,0:T(8,128)(2,1)S(1)} %collective-permute-done.22), channel_id=1, source_target_pairs={{0,1},{1,0},{2,3},{3,2},{4,5},{5,4},{6,7},{7,6},{8,9},{9,8},{10,11... | collective-permute-start | bytes 442376 | tf_op jit(solution)/shard_map/ppermute | solution.py:326
  74.7 8.3 %collective-permute-start.21 = (bf16[576,128]{1,0:T(8,128)(2,1)S(1)}, bf16[576,128]{1,0:T(8,128)(2,1)}, u32[]{:S(2)}, u32[]{:S(2)}) collective-permute-start(bf16[576,128]{1,0:T(8,128)(2,1)S(1)} %collective-permute-done.20), channel_id=1, source_target_pairs={{0,4},{2,30},{4,8},{6,2},{8,12},{10,6},{12,16},{14,10},{16,20},{18... | collective-permute-start | bytes 442376 | tf_op jit(solution)/shard_map/ppermute | solution.py:409
  76.1 10.1 %collective-permute-start.23 = (bf16[576,128]{1,0:T(8,128)(2,1)S(1)}, bf16[576,128]{1,0:T(8,128)(2,1)}, u32[]{:S(2)}, u32[]{:S(2)}) collective-permute-start(bf16[576,128]{1,0:T(8,128)(2,1)S(1)} %collective-permute-done.22), channel_id=1, source_target_pairs={{0,4},{2,30},{4,8},{6,2},{8,12},{10,6},{12,16},{14,10},{16,20},{18... | collective-permute-start | bytes 442376 | tf_op jit(solution)/shard_map/ppermute | solution.py:409
  86.1 3.5 %collective-permute-start.31 = (bf16[576,128]{1,0:T(8,128)(2,1)}, bf16[576,128]{1,0:T(8,128)(2,1)}, u32[]{:S(2)}, u32[]{:S(2)}) collective-permute-start(bf16[576,128]{1,0:T(8,128)(2,1)} %collective-permute-done.21), channel_id=1, source_target_pairs={{0,1},{1,0},{2,3},{3,2},{4,5},{5,4},{6,7},{7,6},{8,9},{9,8},{10,11... | collective-permute-start | bytes 442376 | tf_op jit(solution)/shard_map/ppermute | solution.py:326
  97.2 3.7 %collective-permute-start.35 = (f32[112,256]{1,0:T(8,128)S(1)}, f32[112,256]{1,0:T(8,128)S(1)}, u32[]{:S(2)}, u32[]{:S(2)}) collective-permute-start(f32[112,256]{1,0:T(8,128)S(1)} %pad_maximum_fusion.2), channel_id=1, source_target_pairs={{0,8},{2,10},{4,12},{6,14},{8,0},{10,2},{12,4},{14,6},{16,24},{18,... | collective-permute-start | bytes 344072 | tf_op jit(solution)/shard_map/ppermute | solution.py:326
  100.9 5.6 %collective-permute-start.36 = (f32[112,256]{1,0:T(8,128)S(1)}, f32[112,256]{1,0:T(8,128)S(1)}, u32[]{:S(2)}, u32[]{:S(2)}) collective-permute-start(f32[112,256]{1,0:T(8,128)S(1)} %fusion.4), channel_id=1, source_target_pairs={{0,16},{2,18},{4,20},{6,22},{8,24},{10,26},{12,28},{14,30},{16,0},... | collective-permute-start | bytes 344072 | tf_op jit(solution)/shard_map/ppermute | solution.py:326
  106.5 3.7 %collective-permute-start.37 = (f32[112,256]{1,0:T(8,128)S(1)}, f32[112,256]{1,0:T(8,128)S(1)}, u32[]{:S(2)}, u32[]{:S(2)}) collective-permute-start(f32[112,256]{1,0:T(8,128)S(1)} %add.66), channel_id=1, source_target_pairs={{0,4},{2,6},{4,0},{6,2},{8,12},{10,14},{12,8},{14,10},{16,20},{18,... | collective-permute-start | bytes 344072 | tf_op jit(solution)/shard_map/ppermute | solution.py:326
  110.3 5.7 %collective-permute-start.38 = (f32[192,128]{1,0:T(8,128)S(1)}, f32[192,128]{1,0:T(8,128)S(1)}, u32[]{:S(2)}, u32[]{:S(2)}) collective-permute-start(f32[192,128]{1,0:T(8,128)S(1)} %pad_maximum_fusion.3), channel_id=1, source_target_pairs={{0,1},{1,0},{2,3},{3,2},{4,5},{5,4},{6,7},{7,6},{8,9},{9,8},{10,11... | collective-permute-start | bytes 294920 | tf_op jit(solution)/shard_map/ppermute | solution.py:326
  116.0 5.6 %collective-permute-start.39 = (f32[64,256]{1,0:T(8,128)S(1)}, f32[64,256]{1,0:T(8,128)S(1)}, u32[]{:S(2)}, u32[]{:S(2)}) collective-permute-start(f32[64,256]{1,0:T(8,128)S(1)} %slice_add_fusion.2), channel_id=1, source_target_pairs={{0,2},{2,0},{4,6},{6,4},{8,10},{10,8},{12,14},{14,12},{16,18},{18,... | collective-permute-start | bytes 196616 | tf_op jit(solution)/shard_map/ppermute | solution.py:326
  121.6 7.0 %collective-permute-start.40 = (f32[128,256]{1,0:T(8,128)S(1)}, f32[128,256]{1,0:T(8,128)S(1)}, u32[]{:S(2)}, u32[]{:S(2)}) collective-permute-start(f32[128,256]{1,0:T(8,128)S(1)} %pad_maximum_fusion.1), channel_id=1, source_target_pairs={{0,1},{1,0},{2,3},{3,2},{4,5},{5,4},{6,7},{7,6},{8,9},{9,8},{10,11... | collective-permute-start | bytes 393224 | tf_op jit(solution)/shard_map/ppermute | solution.py:326
  (36 other events, 118.5 us)

commit v9 on v7

--- a/solution.py
+++ b/solution.py
@@ -38,7 +38,7 @@
         out_specs=jax.tree.map(lambda _: VMEM, out_shape),
         scratch_shapes=[] if slots is None else [pltpu.SMEM(slots, jnp.int32)],
         compiler_params=pltpu.CompilerParams(vmem_limit_bytes=VMEM_LIMIT),
-        cost_estimate=pl.CostEstimate(flops=flops // 16, bytes_accessed=bytes_accessed // 16, transcendentals=0),
+        cost_estimate=pl.CostEstimate(flops=flops, bytes_accessed=bytes_accessed // 16, transcendentals=0),
     )
 
 
@@ -74,12 +74,13 @@
 
 def near_body(count, *refs):
     cols_ref, live_ref, bases_ref, hessian_ref = refs[:4]
-    operands, (out_ref, slots_ref) = refs[4:-2], refs[-2:]
+    operands, (out_ref, token_ref, slots_ref) = refs[4:-3], refs[-3:]
     fill_slots(slots_ref, cols_ref, live_ref, 0, lambda name: name)
     total = None
     for at, operand_ref in enumerate(operands):
         total = accumulate(slots_ref, hessian_ref, operand_ref, bases_ref[at], total)
     out_ref[...] = total
+    token_ref[...] = total[:GROUP, :TILE]
 
 
 def halo_total(first, which, cols_ref, live_ref, lists_ref, bases_ref, hessian_ref, lower_ref, upper_ref, total_ref, slots_ref):
@@ -96,8 +97,10 @@
 
 
 def middle_body(first, which, *refs):
-    out_ref, slots_ref = refs[-2:]
-    out_ref[...] = halo_total(first, which, *refs[:-2], slots_ref)
+    out_ref, token_ref, slots_ref = refs[-3:]
+    total = halo_total(first, which, *refs[:-3], slots_ref)
+    out_ref[...] = total
+    token_ref[...] = total[:GROUP, :TILE]
 
 
 def interval(bounds_ref):
@@ -141,7 +144,7 @@
     return [(row, col) for row in range(count) for col in range(row + 1)]
 
 
-def gram_body(number_ref, two_ref, out_ref):
+def gram_body(number_ref, two_ref, _, out_ref):
     two = two_ref[...]
     cols = [two[:, at * TILE : (at + 1) * TILE] for at in range(two.shape[1] // TILE)]
     tiles = [exact_dot(cols[row], cols[col], TN) for row, col in lower_tiles(len(cols))]
@@ -149,7 +152,7 @@
 
 
 def third_body(first, which, *refs):
-    *operands, number_ref, two_ref, out_ref, slots_ref = refs
+    *operands, number_ref, two_ref, _, out_ref, slots_ref = refs
     image = halo_total(first, which, *operands, slots_ref)
     scatter_pieces(number_ref, out_ref, exact_dot(two_ref[...], image, TN))
 
@@ -257,7 +260,7 @@
     rows, modes = two.shape
     tile = jax.ShapeDtypeStruct((TILE, TILE), jnp.float32)
     names = lower_tiles(count)
-    work = 4 * 10 ** 9
+    work = 10 ** 8
 
     def unpack(gram):
         body = functools.partial(unpack_body, total_rows)
@@ -420,48 +423,62 @@
     gram_number, cross_number = device_number([cores, across]), device_number([cores, near])
     halo_slots = (row_blocks, 2 * halo_blocks + 1)
 
-    def step(body, outs, own, lower, upper, scalars, extra, beside=()):
+    covering, free = 3 * 10 ** 10, 10 ** 7
+    token = jax.ShapeDtypeStruct((GROUP, TILE), jnp.float32)
+
+    def near_total(own):
         call = kernel_call(
             functools.partial(near_body, region_blocks),
-            wide,
+            (wide, token),
             [SMEM] * 3 + [VMEM] * (1 + len(own)),
-            work * region_blocks,
+            free,
             traffic,
             (row_blocks, region_blocks + 1),
         )
-        total = call(block_cols, live_blocks, bases, hessian, *own)
-        lower, upper, total, beside = lax.optimization_barrier((lower, upper, total, beside))
-        pairs = list(zip(gathered(lower), gathered(upper)))
+        return call(block_cols, live_blocks, bases, hessian, *own)
+
+    def halo_part(body, outs, which, pair, total, scalars=(), extra=()):
+        specs = [SMEM] * 4 + [VMEM] * 4 + [SMEM] * len(scalars) + [VMEM] * len(extra)
+        body_of = functools.partial(body, region_blocks, which)
+        call = kernel_call(body_of, outs, specs, covering, traffic, halo_slots)
+        return call(block_cols, live_blocks, lists, bases, hessian, *pair, total, *scalars, *extra)
+
+    def step(body, outs, exchanged, scalars, extra):
+        own, lower, upper = exchanged
+        total, _ = near_total(own)
+        *pairs, last = zip(gathered(lower), gathered(upper))
         for which, pair in enumerate(pairs):
-            last = which == len(pairs) - 1
-            given = (block_cols, live_blocks, lists, bases, hessian, *pair, total) + ((*scalars, *extra) if last else ())
-            specs = [SMEM] * 4 + [VMEM] * 4 + ([SMEM] * len(scalars) + [VMEM] * len(extra) if last else [])
-            body_of = functools.partial(body if last else middle_body, region_blocks, which)
-            cost = 2 * work * halo_blocks // len(pairs)
-            total = kernel_call(body_of, outs if last else wide, specs, cost, traffic, halo_slots)(*given)
-        return (total, beside) if beside else total
-
-    one, one_cast = step(first_body, (wide, narrow), first_near, first_lower, first_upper, (bounds,), (vectors,))
-    two, two_cast = step(second_body, (wide, narrow), *exchange(one_cast), (bounds,), (one, vectors))
-
+            total, _ = halo_part(middle_body, (wide, token), which, pair, total)
+        return halo_part(body, outs, len(pairs), last, total, scalars, extra)
+
+    one, one_cast = step(first_body, (wide, narrow), (first_near, first_lower, first_upper), (bounds,), (vectors,))
+    two, two_cast = step(second_body, (wide, narrow), exchange(one_cast), (bounds,), (one, vectors))
+
+    own, lower, upper = exchange(two_cast)
+    total, after = near_total(own)
     packed = jax.ShapeDtypeStruct((tile_rows, TILE), jnp.float32)
-    third = exchange(two_cast)
-    gram = kernel_call(gram_body, packed, [SMEM, VMEM], square_work, traffic)(gram_number, two)
-    for step_of in [halving(*cores), halving(*across)] + [doubling(*bit) for bit in between]:
+    gram = kernel_call(gram_body, packed, [SMEM, VMEM, VMEM], free, traffic)(gram_number, two, after)
+    for step_of in [halving(*cores), halving(*across)]:
         gram = step_of(gram)()
-    cross, (gram,) = step(third_body, square, *third, (cross_number,), (two,), (gram,))
-    cross = halving(*cores)(cross)()
+    *pairs, last = zip(gathered(lower), gathered(upper))
+    for which, pair in enumerate(pairs):
+        total, after = halo_part(middle_body, (wide, token), which, pair, total)
+    gram, after = tied(gram, after)
+    cross = halo_part(third_body, square, len(pairs), last, total, (cross_number,), (two, after))
+    gram = doubling(*near)(gram)()
+    for bit in between[:-1]:
+        end = doubling(*bit)(gram)
+        cross, gram = tied(halving(*cores)(cross)() if bit is between[0] else cross, end())
+    ends = [doubling(*between[-1])(gram), halving(*near)(cross)]
+    gram, cross = [end() for end in ends]
 
     fold = modes // TILE
     cut = gram.shape[0] // fold
     folded = jnp.concatenate([gram[at * cut : (at + 1) * cut] for at in range(fold)], 1)
     flat = lambda value: [value[:, at * TILE : (at + 1) * TILE] for at in range(fold)]
-    half = cross.shape[0] // 2
-    got = partner_value(jnp.concatenate([folded, cross[half:]], 0), *near)
-    both = jnp.concatenate([folded, cross[:half]], 0) + got
-    got = partner_value(both, *across)
-    gram = joining(*cores)(jnp.concatenate(flat(both[:cut]) + flat(got[:cut]), 0))()
-    cross = both[cut:] + got[cut:]
+    got = partner_value(jnp.concatenate([folded, cross], 0), *across)
+    gram = joining(*cores)(jnp.concatenate(flat(folded) + flat(got[:cut]), 0))()
+    cross = cross + got[cut:]
     stages = factor_stages(float(total_rows), modes // TILE, gram_number, two)
     steps = [doubling(*bit) for bit in between] + [joining(*near), joining(*cores)]
     cross, (basis, inverse) = run_beside(cross, steps, gram, stages)

time: 116 us -> 119 us (1.026)
  starting transfers between devices: 33.4 us -> 41.5 us
  waiting for transfers between devices: 38.2 us -> 33.6 us
  local copies, waits for them, and re-layouts: 9.61 us -> 7.42 us
  Pallas kernels: 30.9 us -> 32.5 us
    ppermute x12 -> x13, waiting for transfers between devices: 22.9 us -> 13.4 us  [partner_value(): lax.ppermute(value, axis, [(at, at ^ bit) for at in range(lax.axis_size(a...]
    ppermute x12 -> x13, starting transfers between devices: 10.9 us -> 19 us  [partner_value(): lax.ppermute(value, axis, [(at, at ^ bit) for at in range(lax.axis_size(a...]
    ppermute x6, waiting for transfers between devices: 15.1 us -> 20.2 us  [shifted(): return lax.ppermute(value, axis, pairs)]
    unnamed x40 -> x28, local copies, waits for them, and re-layouts: 9.54 us -> 6.74 us
    ppermute x9, starting transfers between devices: 5.66 us -> 8.03 us  [local(): swapped = lambda value: lax.ppermute(value, 'split', [(0, 1), (1, 0)])]
    ppermute x6, starting transfers between devices: 16.8 us -> 14.4 us  [shifted(): return lax.ppermute(value, axis, pairs)]
    pallas_call x10, Pallas kernels: 17.8 us -> 19.4 us  [the longest x6 12.9 us: halo_part(): call(block_cols, live_blocks, lists, bases, hessian, *pair, total, *scala...]
  transfers between devices with their start and end apart: 27 -> 28, of which waited for: 14 -> 14; matrix products, arithmetic and copies ran while one was open for 1% -> 1% of each run, Pallas kernels for 18% -> 19%
where the time goes in v9:
time: 119 us
  starting transfers between devices  41.5 us (35%)
  waiting for transfers between devices  33.6 us (28%)
  Pallas kernels  32.5 us (27%)
  local copies, waits for them, and re-layouts  7.42 us (6%)
  other arithmetic  3.02 us (3%)
    ppermute x6, waiting for transfers between devices, shifted(): return lax.ppermute(value, axis, pairs)  20.2 us
    ppermute x13, starting transfers between devices, partner_value(): lax.ppermute(value, axis, [(at, at ^ bit) for at in range(lax.axis_size(a...  19 us
    ppermute x6, starting transfers between devices, shifted(): return lax.ppermute(value, axis, pairs)  14.4 us
    ppermute x13, waiting for transfers between devices, partner_value(): lax.ppermute(value, axis, [(at, at ^ bit) for at in range(lax.axis_size(a...  13.4 us
    pallas_call x6, Pallas kernels, halo_part(): call(block_cols, live_blocks, lists, bases, hessian, *pair, total, *scala...  12.9 us
    pallas_call x6, Pallas kernels, stage(): return tiles[:place] + (call(tiles[place]),) + tiles[place + 1:]  8.78 us
    ppermute x9, starting transfers between devices, local(): swapped = lambda value: lax.ppermute(value, 'split', [(0, 1), (1, 0)])  8.03 us
    unnamed x28, local copies, waits for them, and re-layouts  6.74 us
  transfers between devices with their start and end apart: 28, of which 14 were waited for; matrix products, arithmetic and copies ran while one was open for 1% of the time, Pallas kernels for 19%

profile of v9, /device:TPU:1, one launch (start us, length us, event | category | flops | bytes accessed | tf_op | source)
XLA Modules:
  0.0 119.0 jit_solution(17401268894469609806)
XLA Ops:
  2.5 2.1 %collective-permute-start = (bf16[592,256]{1,0:T(8,128)(2,1)S(1)}, bf16[592,256]{1,0:T(8,128)(2,1)S(1)}, u32[]{:S(2)}, u32[]{:S(2)}) collective-permute-start(bf16[592,256]{1,0:T(8,128)(2,1)S(1)} %get-tuple-element.85), channel_id=1, source_target_pairs={{0,2},{2,4},{4,6},{6,8},{8,10},{10,12},{12,14},{14,16},{16,18},{18... | collective-permute-start | bytes 909320 | tf_op jit(solution)/shard_map/ppermute | solution.py:26
  4.6 4.1 %collective-permute-start.1 = (bf16[592,256]{1,0:T(8,128)(2,1)S(1)}, bf16[592,256]{1,0:T(8,128)(2,1)S(1)}, u32[]{:S(2)}, u32[]{:S(2)}) collective-permute-start(bf16[592,256]{1,0:T(8,128)(2,1)S(1)} %get-tuple-element.85), channel_id=1, source_target_pairs={{0,30},{2,0},{4,2},{6,4},{8,6},{10,8},{12,10},{14,12},{16,14},{18,... | collective-permute-start | bytes 909320 | tf_op jit(solution)/shard_map/ppermute | solution.py:26
  9.7 7.3 %collective-permute-done = bf16[592,256]{1,0:T(8,128)(2,1)S(1)} collective-permute-done((bf16[592,256]{1,0:T(8,128)(2,1)S(1)}, bf16[592,256]{1,0:T(8,128)(2,1)S(1)}, u32[]{:S(2)}, u32[]{:S(2)}) %collective-permute-start) | collective-permute-done | bytes 303136 | tf_op jit(solution)/shard_map/ppermute | solution.py:26
  16.9 1.9 %collective-permute-done.1 = bf16[592,256]{1,0:T(8,128)(2,1)S(1)} collective-permute-done((bf16[592,256]{1,0:T(8,128)(2,1)S(1)}, bf16[592,256]{1,0:T(8,128)(2,1)S(1)}, u32[]{:S(2)}, u32[]{:S(2)}) %collective-permute-start.1) | collective-permute-done | bytes 303136 | tf_op jit(solution)/shard_map/ppermute | solution.py:26
  18.9 2.0 %copy-done = bf16[3,12,192,192]{3,2,1,0:T(8,128)(2,1)S(1)} copy-done((bf16[3,12,192,192]{3,2,1,0:T(8,128)(2,1)S(1)}, bf16[3,12,192,192]{3,2,1,0:T(8,128)(2,1)}, u32[]{:S(2)}) %copy-start) | copy-done | bytes 2654232
  22.2 1.8 %shard_map.77 = (f32[576,256]{1,0:T(8,128)S(1)}, f32[8,128]{1,0:T(8,128)}) custom-call(s32[3,12]{1,0:T(4,128)S(1)} %copy-done.7, s32[3]{0:T(128)S(1)} %copy-done.9, s32[2]{0:T(128)S(1)} %pad_add_fusion.refs_2_.refs_3_, bf16[3,12,192,192]{3,2,1,0:T(8,128)(2,1)S(1)} %copy-done, bf16[1,592,256]{2,1,0:T(8,128)(2,1)S(1)} %get-tuple-element.84.refs_4_, ...), custom_call_target="tpu_custom_call" | custom-call | flops 10000000 | bytes 276480 | tf_op jit(solution)/shard_map/pallas_call | solution.py:438
  24.0 1.5 %collective-permute-start.2 = (bf16[592,256]{1,0:T(8,128)(2,1)S(1)}, bf16[592,256]{1,0:T(8,128)(2,1)S(1)}, u32[]{:S(2)}, u32[]{:S(2)}) collective-permute-start(bf16[592,256]{1,0:T(8,128)(2,1)S(1)} %collective-permute-done), channel_id=1, source_target_pairs={{0,1},{1,0},{2,3},{3,2},{4,5},{5,4},{6,7},{7,6},{8,9},{9,8},{10,11... | collective-permute-start | bytes 909320 | tf_op jit(solution)/shard_map/ppermute | solution.py:371
  25.6 2.0 %shard_map.78 = (f32[576,256]{1,0:T(8,128)S(1)}, f32[8,128]{1,0:T(8,128)}) custom-call(s32[3,12]{1,0:T(4,128)S(1)} %copy-done.8, s32[3]{0:T(128)S(1)} %copy-done.10, s32[2,6]{1,0:T(2,128)S(1)} %maximum_convert_fusion.refs_2_, s32[2]{0:T(128)S(1)} %pad_add_fusion.refs_2_.refs_3_, bf16[3,12,192,192]{3,2,1,0:T(8,128)(2,1)S(1)} %copy-done, ...), custom_call_target="tpu_custom_call" | custom-call | flops 30000001024 | bytes 276480 | tf_op jit(solution)/shard_map/pallas_call | solution.py:444
  29.2 3.2 %collective-permute-start.7 = (bf16[576,256]{1,0:T(8,128)(2,1)S(1)}, bf16[576,256]{1,0:T(8,128)(2,1)S(1)}, u32[]{:S(2)}, u32[]{:S(2)}) collective-permute-start(bf16[576,256]{1,0:T(8,128)(2,1)S(1)} %get-tuple-element.45), channel_id=1, source_target_pairs={{0,30},{2,0},{4,2},{6,4},{8,6},{10,8},{12,10},{14,12},{16,14},{18,... | collective-permute-start | bytes 884744 | tf_op jit(solution)/shard_map/ppermute | solution.py:26
  33.1 5.1 %collective-permute-done.7 = bf16[576,256]{1,0:T(8,128)(2,1)S(1)} collective-permute-done((bf16[576,256]{1,0:T(8,128)(2,1)S(1)}, bf16[576,256]{1,0:T(8,128)(2,1)S(1)}, u32[]{:S(2)}, u32[]{:S(2)}) %collective-permute-start.7) | collective-permute-done | bytes 294944 | tf_op jit(solution)/shard_map/ppermute | solution.py:26
  39.6 1.8 %shard_map.80 = (f32[576,256]{1,0:T(8,128)S(1)}, f32[8,128]{1,0:T(8,128)}) custom-call(s32[3,12]{1,0:T(4,128)S(1)} %copy-done.8, s32[3]{0:T(128)S(1)} %copy-done.10, s32[2]{0:T(128)S(1)} %pad_add_fusion.refs_2_.refs_3_, bf16[3,12,192,192]{3,2,1,0:T(8,128)(2,1)S(1)} %copy-done, bf16[1,576,256]{2,1,0:T(8,128)(2,1)S(1)} %bitcast.26, ...), custom_call_target="tpu_custom_call" | custom-call | flops 10000000 | bytes 276480 | tf_op jit(solution)/shard_map/pallas_call | solution.py:438
  41.4 4.0 %collective-permute-done.5 = bf16[576,256]{1,0:T(8,128)(2,1)S(1)} collective-permute-done((bf16[576,256]{1,0:T(8,128)(2,1)S(1)}, bf16[576,256]{1,0:T(8,128)(2,1)S(1)}, u32[]{:S(2)}, u32[]{:S(2)}) %collective-permute-start.5) | collective-permute-done | bytes 294944 | tf_op jit(solution)/shard_map/ppermute | solution.py:26
  46.2 2.0 %shard_map.81 = (f32[576,256]{1,0:T(8,128)S(1)}, f32[8,128]{1,0:T(8,128)}) custom-call(s32[3,12]{1,0:T(4,128)S(1)} %copy-done.8, s32[3]{0:T(128)S(1)} %copy-done.10, s32[2,6]{1,0:T(2,128)S(1)} %maximum_convert_fusion.refs_2_, s32[2]{0:T(128)S(1)} %pad_add_fusion.refs_2_.refs_3_, bf16[3,12,192,192]{3,2,1,0:T(8,128)(2,1)S(1)} %copy-done, ...), custom_call_target="tpu_custom_call" | custom-call | flops 30000001024 | bytes 276480 | tf_op jit(solution)/shard_map/pallas_call | solution.py:444
  48.1 2.3 %shard_map.82 = (f32[576,256]{1,0:T(8,128)S(1)}, bf16[576,256]{1,0:T(8,128)(2,1)}) custom-call(s32[3,12]{1,0:T(4,128)S(1)} %copy-done.8, s32[3]{0:T(128)S(1)} %copy-done.10, s32[2,6]{1,0:T(2,128)S(1)} %maximum_convert_fusion.refs_2_, s32[2]{0:T(128)S(1)} %pad_add_fusion.refs_2_.refs_3_, bf16[3,12,192,192]{3,2,1,0:T(8,128)(2,1)S(1)} %copy-done, ...), custom_call_target="tpu_custom_call" | custom-call | flops 30000001024 | bytes 276480 | tf_op jit(solution)/shard_map/pallas_call | solution.py:444
  51.5 4.8 %collective-permute-start.12 = (bf16[576,256]{1,0:T(8,128)(2,1)}, bf16[576,256]{1,0:T(8,128)(2,1)}, u32[]{:S(2)}, u32[]{:S(2)}) collective-permute-start(bf16[576,256]{1,0:T(8,128)(2,1)} %get-tuple-element.49), channel_id=1, source_target_pairs={{0,30},{2,0},{4,2},{6,4},{8,6},{10,8},{12,10},{14,12},{16,14},{18,... | collective-permute-start | bytes 884744 | tf_op jit(solution)/shard_map/ppermute | solution.py:26
  56.3 1.9 %shard_map.83 = (f32[576,256]{1,0:T(8,128)S(1)}, f32[8,128]{1,0:T(8,128)S(1)}) custom-call(s32[3,12]{1,0:T(4,128)S(1)} %copy-done.8, s32[3]{0:T(128)S(1)} %copy-done.10, s32[2]{0:T(128)S(1)} %pad_add_fusion.refs_2_.refs_3_, bf16[3,12,192,192]{3,2,1,0:T(8,128)(2,1)S(1)} %copy-done.1, bf16[1,576,256]{2,1,0:T(8,128)(2,1)} %bitcast.19.refs_4_, ...), custom_call_target="tpu_custom_call" | custom-call | flops 10000000 | bytes 276480 | tf_op jit(solution)/shard_map/pallas_call | solution.py:438
  62.4 1.7 %collective-permute-done.10 = bf16[576,256]{1,0:T(8,128)(2,1)} collective-permute-done((bf16[576,256]{1,0:T(8,128)(2,1)}, bf16[576,256]{1,0:T(8,128)(2,1)}, u32[]{:S(2)}, u32[]{:S(2)}) %collective-permute-start.10) | collective-permute-done | bytes 294944 | tf_op jit(solution)/shard_map/ppermute | solution.py:26
  68.0 1.6 %collective-permute-start.16 = (f32[96,128]{1,0:T(8,128)S(1)}, f32[96,128]{1,0:T(8,128)S(1)}, u32[]{:S(2)}, u32[]{:S(2)}) collective-permute-start(f32[96,128]{1,0:T(8,128)S(1)} %slice.70), channel_id=1, source_target_pairs={{0,4},{2,6},{4,0},{6,2},{8,12},{10,14},{12,8},{14,10},{16,20},{18,... | collective-permute-start | bytes 147464 | tf_op jit(solution)/shard_map/ppermute | solution.py:307
  70.6 2.0 %shard_map.84 = (f32[576,256]{1,0:T(8,128)S(1)}, f32[8,128]{1,0:T(8,128)S(1)}) custom-call(s32[3,12]{1,0:T(4,128)S(1)} %copy-done.8, s32[3]{0:T(128)S(1)} %copy-done.10, s32[2,6]{1,0:T(2,128)S(1)} %maximum_convert_fusion.refs_2_, s32[2]{0:T(128)S(1)} %pad_add_fusion.refs_2_.refs_3_, bf16[3,12,192,192]{3,2,1,0:T(8,128)(2,1)S(1)} %copy-done.1, ...), custom_call_target="tpu_custom_call" | custom-call | flops 30000001024 | bytes 276480 | tf_op jit(solution)/shard_map/pallas_call | solution.py:444
  72.7 3.1 %shard_map.86 = f32[256,256]{1,0:T(8,128)S(1)} custom-call(s32[3,12]{1,0:T(4,128)S(1)} %copy-done.8, s32[3]{0:T(128)S(1)} %copy-done.10, s32[2,6]{1,0:T(2,128)S(1)} %maximum_convert_fusion.refs_2_, s32[2]{0:T(128)S(1)} %pad_add_fusion.refs_2_.refs_3_, bf16[3,12,192,192]{3,2,1,0:T(8,128)(2,1)S(1)} %copy-done.1, bf16[1,576,256]{2,1,0:T(8,128)(2,1)S(1)} %bitcast.32, ...), custom_call_target="tpu_custom_call" | custom-call | flops 30000001024 | bytes 276480 | tf_op jit(solution)/shard_map/pallas_call | solution.py:444
  76.6 2.5 %collective-permute-done.18 = f32[96,128]{1,0:T(8,128)S(1)} collective-permute-done((f32[96,128]{1,0:T(8,128)S(1)}, f32[96,128]{1,0:T(8,128)S(1)}, u32[]{:S(2)}, u32[]{:S(2)}) %collective-permute-start.18) | collective-permute-done | bytes 49184 | tf_op jit(solution)/shard_map/ppermute | solution.py:307
  79.1 2.9 %collective-permute-start.19 = (f32[96,128]{1,0:T(8,128)S(1)}, f32[96,128]{1,0:T(8,128)S(1)}, u32[]{:S(2)}, u32[]{:S(2)}) collective-permute-start(f32[96,128]{1,0:T(8,128)S(1)} %add.60), channel_id=1, source_target_pairs={{0,8},{2,10},{4,12},{6,14},{8,0},{10,2},{12,4},{14,6},{16,24},{18,... | collective-permute-start | bytes 147464 | tf_op jit(solution)/shard_map/ppermute | solution.py:307
  83.5 2.5 %collective-permute-start.21 = (f32[96,128]{1,0:T(8,128)S(1)}, f32[96,128]{1,0:T(8,128)S(1)}, u32[]{:S(2)}, u32[]{:S(2)}) collective-permute-start(f32[96,128]{1,0:T(8,128)S(1)} %add.61), channel_id=1, source_target_pairs={{0,16},{2,18},{4,20},{6,22},{8,24},{10,26},{12,28},{14,30},{16,0},... | collective-permute-start | bytes 147464 | tf_op jit(solution)/shard_map/ppermute | solution.py:307
  87.6 1.6 %collective-permute-done.20 = f32[64,256]{1,0:T(8,128)S(1)} collective-permute-done((f32[64,256]{1,0:T(8,128)S(1)}, f32[64,256]{1,0:T(8,128)S(1)}, u32[]{:S(2)}, u32[]{:S(2)}) %collective-permute-start.20) | collective-permute-done | bytes 65568 | tf_op jit(solution)/shard_map/ppermute | solution.py:307
  90.0 2.9 %collective-permute-done.22 = f32[112,256]{1,0:T(8,128)S(1)} collective-permute-done((f32[112,256]{1,0:T(8,128)S(1)}, f32[112,256]{1,0:T(8,128)S(1)}, u32[]{:S(2)}, u32[]{:S(2)}) %collective-permute-start.22) | collective-permute-done | bytes 114720 | tf_op jit(solution)/shard_map/ppermute | solution.py:307
  92.9 5.0 %collective-permute-start.23 = (f32[192,128]{1,0:T(8,128)S(1)}, f32[192,128]{1,0:T(8,128)S(1)}, u32[]{:S(2)}, u32[]{:S(2)}) collective-permute-start(f32[192,128]{1,0:T(8,128)S(1)} %pad_maximum_fusion.4), channel_id=1, source_target_pairs={{0,1},{1,0},{2,3},{3,2},{4,5},{5,4},{6,7},{7,6},{8,9},{9,8},{10,11... | collective-permute-start | bytes 294920 | tf_op jit(solution)/shard_map/ppermute | solution.py:307
  104.0 1.7 %shard_map.90.refs_0_ = f32[128,128]{1,0:T(8,128)S(1)} custom-call(f32[128,128]{1,0:T(8,128)S(1)} %shard_map.89.tile_ref), custom_call_target="tpu_custom_call" | custom-call | flops 50000000 | bytes 1024 | tf_op jit(solution)/shard_map/pallas_call | solution.py:273
  106.3 2.1 %collective-permute-done.25 = f32[64,256]{1,0:T(8,128)S(1)} collective-permute-done((f32[64,256]{1,0:T(8,128)S(1)}, f32[64,256]{1,0:T(8,128)S(1)}, u32[]{:S(2)}, u32[]{:S(2)}) %collective-permute-start.25) | collective-permute-done | bytes 65568 | tf_op jit(solution)/shard_map/ppermute | solution.py:307
  111.6 2.0 %collective-permute-start.27 = (f32[128,256]{1,0:T(8,128)S(1)}, f32[128,256]{1,0:T(8,128)S(1)}, u32[]{:S(2)}, u32[]{:S(2)}) collective-permute-start(f32[128,256]{1,0:T(8,128)S(1)} %pad_maximum_fusion.2), channel_id=1, source_target_pairs={{0,1},{1,0},{2,3},{3,2},{4,5},{5,4},{6,7},{7,6},{8,9},{9,8},{10,11... | collective-permute-start | bytes 393224 | tf_op jit(solution)/shard_map/ppermute | solution.py:307
  113.6 1.7 %shard_map.94.refs_2_ = f32[128,128]{1,0:T(8,128)S(1)} custom-call(f32[128,128]{1,0:T(8,128)S(1)} %shard_map.93.tile_ref), custom_call_target="tpu_custom_call" | custom-call | flops 50000000 | bytes 1024 | tf_op jit(solution)/shard_map/pallas_call | solution.py:273
  115.3 1.9 %shard_map.95 = (f32[576,256]{1,0:T(8,128)}, f32[256,256]{1,0:T(8,128)S(1)}) custom-call(f32[128,128]{1,0:T(8,128)S(1)} %get-tuple-element.76.refs_0_, f32[128,128]{1,0:T(8,128)S(1)} %get-tuple-element.77.refs_1_, f32[128,128]{1,0:T(8,128)S(1)} %shard_map.94.refs_2_, f32[576,256]{1,0:T(8,128)S(1)} %copy-done.4), custom_call_target="tpu_custom_call" | custom-call | flops 50000000 | bytes 9216 | tf_op jit(solution)/shard_map/pallas_call | solution.py:290
  117.3 1.7 %shard_map.96 = f32[256,256]{1,0:T(8,128)} custom-call(s32[1]{0:T(128)} %bitcast.21.refs_8_.number_ref, f32[256,256]{1,0:T(8,128)S(1)} %pad_maximum_fusion.cross_ref, f32[256,256]{1,0:T(8,128)S(1)} %get-tuple-element.83.inverse_ref), custom_call_target="tpu_custom_call" | custom-call | flops 150994944 | bytes 276480 | tf_op jit(solution)/shard_map/pallas_call | solution.py:487
  (100 shorter events, 33.4 us)
Async XLA Ops:
  0.6 25.0 %copy-start.8 = (s32[3,12]{1,0:T(4,128)S(1)}, s32[3,12]{1,0:T(4,128)}, u32[]{:S(2)}) copy-start(s32[3,12]{1,0:T(4,128)} %refs_0_.17) | copy-start | bytes 436
  0.6 25.0 %copy-start.10 = (s32[3]{0:T(128)S(1)}, s32[3]{0:T(128)}, u32[]{:S(2)}) copy-start(s32[3]{0:T(128)} %refs_1_.17) | copy-start | bytes 40
  2.5 14.4 %collective-permute-start = (bf16[592,256]{1,0:T(8,128)(2,1)S(1)}, bf16[592,256]{1,0:T(8,128)(2,1)S(1)}, u32[]{:S(2)}, u32[]{:S(2)}) collective-permute-start(bf16[592,256]{1,0:T(8,128)(2,1)S(1)} %get-tuple-element.85), channel_id=1, source_target_pairs={{0,2},{2,4},{4,6},{6,8},{8,10},{10,12},{12,14},{14,16},{16,18},{18... | collective-permute-start | bytes 909320 | tf_op jit(solution)/shard_map/ppermute | solution.py:26
  4.6 14.3 %collective-permute-start.1 = (bf16[592,256]{1,0:T(8,128)(2,1)S(1)}, bf16[592,256]{1,0:T(8,128)(2,1)S(1)}, u32[]{:S(2)}, u32[]{:S(2)}) collective-permute-start(bf16[592,256]{1,0:T(8,128)(2,1)S(1)} %get-tuple-element.85), channel_id=1, source_target_pairs={{0,30},{2,0},{4,2},{6,4},{8,6},{10,8},{12,10},{14,12},{16,14},{18,... | collective-permute-start | bytes 909320 | tf_op jit(solution)/shard_map/ppermute | solution.py:26
  8.6 10.3 %collective-permute-start.4 = (bf16[592,256]{1,0:T(8,128)(2,1)S(1)}, bf16[592,256]{1,0:T(8,128)(2,1)S(1)}, u32[]{:S(2)}, u32[]{:S(2)}) collective-permute-start(bf16[592,256]{1,0:T(8,128)(2,1)S(1)} %get-tuple-element.85), channel_id=1, source_target_pairs={{0,1},{1,0},{2,3},{3,2},{4,5},{5,4},{6,7},{7,6},{8,9},{9,8},{10,11... | collective-permute-start | bytes 909320 | tf_op jit(solution)/shard_map/ppermute | solution.py:371
  24.0 3.6 %collective-permute-start.2 = (bf16[592,256]{1,0:T(8,128)(2,1)S(1)}, bf16[592,256]{1,0:T(8,128)(2,1)S(1)}, u32[]{:S(2)}, u32[]{:S(2)}) collective-permute-start(bf16[592,256]{1,0:T(8,128)(2,1)S(1)} %collective-permute-done), channel_id=1, source_target_pairs={{0,1},{1,0},{2,3},{3,2},{4,5},{5,4},{6,7},{7,6},{8,9},{9,8},{10,11... | collective-permute-start | bytes 909320 | tf_op jit(solution)/shard_map/ppermute | solution.py:371
  25.6 2.0 %collective-permute-start.3 = (bf16[592,256]{1,0:T(8,128)(2,1)S(1)}, bf16[592,256]{1,0:T(8,128)(2,1)S(1)}, u32[]{:S(2)}, u32[]{:S(2)}) collective-permute-start(bf16[592,256]{1,0:T(8,128)(2,1)S(1)} %collective-permute-done.1), channel_id=1, source_target_pairs={{0,1},{1,0},{2,3},{3,2},{4,5},{5,4},{6,7},{7,6},{8,9},{9,8},{10,11... | collective-permute-start | bytes 909320 | tf_op jit(solution)/shard_map/ppermute | solution.py:371
  29.2 9.1 %collective-permute-start.7 = (bf16[576,256]{1,0:T(8,128)(2,1)S(1)}, bf16[576,256]{1,0:T(8,128)(2,1)S(1)}, u32[]{:S(2)}, u32[]{:S(2)}) collective-permute-start(bf16[576,256]{1,0:T(8,128)(2,1)S(1)} %get-tuple-element.45), channel_id=1, source_target_pairs={{0,30},{2,0},{4,2},{6,4},{8,6},{10,8},{12,10},{14,12},{16,14},{18,... | collective-permute-start | bytes 884744 | tf_op jit(solution)/shard_map/ppermute | solution.py:26
  32.4 7.2 %collective-permute-start.9 = (bf16[576,256]{1,0:T(8,128)(2,1)S(1)}, bf16[576,256]{1,0:T(8,128)(2,1)S(1)}, u32[]{:S(2)}, u32[]{:S(2)}) collective-permute-start(bf16[576,256]{1,0:T(8,128)(2,1)S(1)} %get-tuple-element.45), channel_id=1, source_target_pairs={{0,1},{1,0},{2,3},{3,2},{4,5},{5,4},{6,7},{7,6},{8,9},{9,8},{10,11... | collective-permute-start | bytes 884744 | tf_op jit(solution)/shard_map/ppermute | solution.py:371
  33.1 12.2 %collective-permute-start.5 = (bf16[576,256]{1,0:T(8,128)(2,1)S(1)}, bf16[576,256]{1,0:T(8,128)(2,1)S(1)}, u32[]{:S(2)}, u32[]{:S(2)}) collective-permute-start(bf16[576,256]{1,0:T(8,128)(2,1)S(1)} %get-tuple-element.45), channel_id=1, source_target_pairs={{0,2},{2,4},{4,6},{6,8},{8,10},{10,12},{12,14},{14,16},{16,18},{18... | collective-permute-start | bytes 884744 | tf_op jit(solution)/shard_map/ppermute | solution.py:26
  38.2 9.9 %collective-permute-start.8 = (bf16[576,256]{1,0:T(8,128)(2,1)S(1)}, bf16[576,256]{1,0:T(8,128)(2,1)S(1)}, u32[]{:S(2)}, u32[]{:S(2)}) collective-permute-start(bf16[576,256]{1,0:T(8,128)(2,1)S(1)} %collective-permute-done.7), channel_id=1, source_target_pairs={{0,1},{1,0},{2,3},{3,2},{4,5},{5,4},{6,7},{7,6},{8,9},{9,8},{10,11... | collective-permute-start | bytes 884744 | tf_op jit(solution)/shard_map/ppermute | solution.py:371
  45.4 2.8 %collective-permute-start.6 = (bf16[576,256]{1,0:T(8,128)(2,1)S(1)}, bf16[576,256]{1,0:T(8,128)(2,1)S(1)}, u32[]{:S(2)}, u32[]{:S(2)}) collective-permute-start(bf16[576,256]{1,0:T(8,128)(2,1)S(1)} %collective-permute-done.5), channel_id=1, source_target_pairs={{0,1},{1,0},{2,3},{3,2},{4,5},{5,4},{6,7},{7,6},{8,9},{9,8},{10,11... | collective-permute-start | bytes 884744 | tf_op jit(solution)/shard_map/ppermute | solution.py:371
  48.1 8.2 %copy-start.1 = (bf16[3,12,192,192]{3,2,1,0:T(8,128)(2,1)S(1)}, bf16[3,12,192,192]{3,2,1,0:T(8,128)(2,1)}, u32[]{:S(2)}) copy-start(bf16[3,12,192,192]{3,2,1,0:T(8,128)(2,1)} %refs_4_.11) | copy-start | bytes 7962628
  51.2 5.1 %collective-permute-start.14 = (bf16[576,256]{1,0:T(8,128)(2,1)}, bf16[576,256]{1,0:T(8,128)(2,1)}, u32[]{:S(2)}, u32[]{:S(2)}) collective-permute-start(bf16[576,256]{1,0:T(8,128)(2,1)} %get-tuple-element.49), channel_id=1, source_target_pairs={{0,1},{1,0},{2,3},{3,2},{4,5},{5,4},{6,7},{7,6},{8,9},{9,8},{10,11... | collective-permute-start | bytes 884744 | tf_op jit(solution)/shard_map/ppermute | solution.py:371
  51.3 12.9 %collective-permute-start.10 = (bf16[576,256]{1,0:T(8,128)(2,1)}, bf16[576,256]{1,0:T(8,128)(2,1)}, u32[]{:S(2)}, u32[]{:S(2)}) collective-permute-start(bf16[576,256]{1,0:T(8,128)(2,1)} %get-tuple-element.49), channel_id=1, source_target_pairs={{0,2},{2,4},{4,6},{6,8},{8,10},{10,12},{12,14},{14,16},{16,18},{18... | collective-permute-start | bytes 884744 | tf_op jit(solution)/shard_map/ppermute | solution.py:26
  51.5 14.1 %collective-permute-start.12 = (bf16[576,256]{1,0:T(8,128)(2,1)}, bf16[576,256]{1,0:T(8,128)(2,1)}, u32[]{:S(2)}, u32[]{:S(2)}) collective-permute-start(bf16[576,256]{1,0:T(8,128)(2,1)} %get-tuple-element.49), channel_id=1, source_target_pairs={{0,30},{2,0},{4,2},{6,4},{8,6},{10,8},{12,10},{14,12},{16,14},{18,... | collective-permute-start | bytes 884744 | tf_op jit(solution)/shard_map/ppermute | solution.py:26
  56.3 2.7 %copy-start.3 = (f32[576,256]{1,0:T(8,128)S(1)}, f32[576,256]{1,0:T(8,128)}, u32[]{:S(2)}) copy-start(f32[576,256]{1,0:T(8,128)} %copy-done.2) | copy-start | bytes 1769476
  61.4 5.6 %collective-permute-start.15 = (f32[192,128]{1,0:T(8,128)}, f32[192,128]{1,0:T(8,128)}, u32[]{:S(2)}, u32[]{:S(2)}) collective-permute-start(f32[192,128]{1,0:T(8,128)} %slice.68), channel_id=1, source_target_pairs={{0,1},{1,0},{2,3},{3,2},{4,5},{5,4},{6,7},{7,6},{8,9},{9,8},{10,11... | collective-permute-start | bytes 294920 | tf_op jit(solution)/shard_map/ppermute | solution.py:307
  64.1 8.6 %collective-permute-start.11 = (bf16[576,256]{1,0:T(8,128)(2,1)}, bf16[576,256]{1,0:T(8,128)(2,1)S(1)}, u32[]{:S(2)}, u32[]{:S(2)}) collective-permute-start(bf16[576,256]{1,0:T(8,128)(2,1)} %collective-permute-done.10), channel_id=1, source_target_pairs={{0,1},{1,0},{2,3},{3,2},{4,5},{5,4},{6,7},{7,6},{8,9},{9,8},{10,11... | collective-permute-start | bytes 884744 | tf_op jit(solution)/shard_map/ppermute | solution.py:371
  65.6 7.1 %collective-permute-start.13 = (bf16[576,256]{1,0:T(8,128)(2,1)}, bf16[576,256]{1,0:T(8,128)(2,1)S(1)}, u32[]{:S(2)}, u32[]{:S(2)}) collective-permute-start(bf16[576,256]{1,0:T(8,128)(2,1)} %collective-permute-done.12), channel_id=1, source_target_pairs={{0,1},{1,0},{2,3},{3,2},{4,5},{5,4},{6,7},{7,6},{8,9},{9,8},{10,11... | collective-permute-start | bytes 884744 | tf_op jit(solution)/shard_map/ppermute | solution.py:371
  68.0 4.7 %collective-permute-start.16 = (f32[96,128]{1,0:T(8,128)S(1)}, f32[96,128]{1,0:T(8,128)S(1)}, u32[]{:S(2)}, u32[]{:S(2)}) collective-permute-start(f32[96,128]{1,0:T(8,128)S(1)} %slice.70), channel_id=1, source_target_pairs={{0,4},{2,6},{4,0},{6,2},{8,12},{10,14},{12,8},{14,10},{16,20},{18,... | collective-permute-start | bytes 147464 | tf_op jit(solution)/shard_map/ppermute | solution.py:307
  75.8 7.7 %collective-permute-start.17 = (f32[128,256]{1,0:T(8,128)S(1)}, f32[128,256]{1,0:T(8,128)S(1)}, u32[]{:S(2)}, u32[]{:S(2)}) collective-permute-start(f32[128,256]{1,0:T(8,128)S(1)} %slice.72), channel_id=1, source_target_pairs={{0,1},{1,0},{2,3},{3,2},{4,5},{5,4},{6,7},{7,6},{8,9},{9,8},{10,11... | collective-permute-start | bytes 393224 | tf_op jit(solution)/shard_map/ppermute | solution.py:307
  76.2 2.9 %collective-permute-start.18 = (f32[96,128]{1,0:T(8,128)S(1)}, f32[96,128]{1,0:T(8,128)S(1)}, u32[]{:S(2)}, u32[]{:S(2)}) collective-permute-start(f32[96,128]{1,0:T(8,128)S(1)} %slice_add_fusion.4), channel_id=1, source_target_pairs={{0,2},{2,0},{4,6},{6,4},{8,10},{10,8},{12,14},{14,12},{16,18},{18,... | collective-permute-start | bytes 147464 | tf_op jit(solution)/shard_map/ppermute | solution.py:307
  79.1 4.3 %collective-permute-start.19 = (f32[96,128]{1,0:T(8,128)S(1)}, f32[96,128]{1,0:T(8,128)S(1)}, u32[]{:S(2)}, u32[]{:S(2)}) collective-permute-start(f32[96,128]{1,0:T(8,128)S(1)} %add.60), channel_id=1, source_target_pairs={{0,8},{2,10},{4,12},{6,14},{8,0},{10,2},{12,4},{14,6},{16,24},{18,... | collective-permute-start | bytes 147464 | tf_op jit(solution)/shard_map/ppermute | solution.py:307
  83.5 4.0 %collective-permute-start.21 = (f32[96,128]{1,0:T(8,128)S(1)}, f32[96,128]{1,0:T(8,128)S(1)}, u32[]{:S(2)}, u32[]{:S(2)}) collective-permute-start(f32[96,128]{1,0:T(8,128)S(1)} %add.61), channel_id=1, source_target_pairs={{0,16},{2,18},{4,20},{6,22},{8,24},{10,26},{12,28},{14,30},{16,0},... | collective-permute-start | bytes 147464 | tf_op jit(solution)/shard_map/ppermute | solution.py:307
  86.1 3.1 %collective-permute-start.20 = (f32[64,256]{1,0:T(8,128)S(1)}, f32[64,256]{1,0:T(8,128)S(1)}, u32[]{:S(2)}, u32[]{:S(2)}) collective-permute-start(f32[64,256]{1,0:T(8,128)S(1)} %slice.59), channel_id=1, source_target_pairs={{0,2},{2,0},{4,6},{6,4},{8,10},{10,8},{12,14},{14,12},{16,18},{18,... | collective-permute-start | bytes 196616 | tf_op jit(solution)/shard_map/ppermute | solution.py:307
  89.2 3.7 %collective-permute-start.22 = (f32[112,256]{1,0:T(8,128)S(1)}, f32[112,256]{1,0:T(8,128)S(1)}, u32[]{:S(2)}, u32[]{:S(2)}) collective-permute-start(f32[112,256]{1,0:T(8,128)S(1)} %pad_maximum_fusion.3), channel_id=1, source_target_pairs={{0,4},{2,6},{4,0},{6,2},{8,12},{10,14},{12,8},{14,10},{16,20},{18,... | collective-permute-start | bytes 344072 | tf_op jit(solution)/shard_map/ppermute | solution.py:307
  92.9 6.0 %collective-permute-start.23 = (f32[192,128]{1,0:T(8,128)S(1)}, f32[192,128]{1,0:T(8,128)S(1)}, u32[]{:S(2)}, u32[]{:S(2)}) collective-permute-start(f32[192,128]{1,0:T(8,128)S(1)} %pad_maximum_fusion.4), channel_id=1, source_target_pairs={{0,1},{1,0},{2,3},{3,2},{4,5},{5,4},{6,7},{7,6},{8,9},{9,8},{10,11... | collective-permute-start | bytes 294920 | tf_op jit(solution)/shard_map/ppermute | solution.py:307
  98.9 4.1 %collective-permute-start.24 = (f32[64,256]{1,0:T(8,128)S(1)}, f32[64,256]{1,0:T(8,128)S(1)}, u32[]{:S(2)}, u32[]{:S(2)}) collective-permute-start(f32[64,256]{1,0:T(8,128)S(1)} %slice_add_fusion.2), channel_id=1, source_target_pairs={{0,8},{2,10},{4,12},{6,14},{8,0},{10,2},{12,4},{14,6},{16,24},{18,... | collective-permute-start | bytes 196616 | tf_op jit(solution)/shard_map/ppermute | solution.py:307
  103.0 5.4 %collective-permute-start.25 = (f32[64,256]{1,0:T(8,128)S(1)}, f32[64,256]{1,0:T(8,128)S(1)}, u32[]{:S(2)}, u32[]{:S(2)}) collective-permute-start(f32[64,256]{1,0:T(8,128)S(1)} %add.65), channel_id=1, source_target_pairs={{0,16},{2,18},{4,20},{6,22},{8,24},{10,26},{12,28},{14,30},{16,0},... | collective-permute-start | bytes 196616 | tf_op jit(solution)/shard_map/ppermute | solution.py:307
  108.4 3.2 %collective-permute-start.26 = (f32[64,256]{1,0:T(8,128)S(1)}, f32[64,256]{1,0:T(8,128)S(1)}, u32[]{:S(2)}, u32[]{:S(2)}) collective-permute-start(f32[64,256]{1,0:T(8,128)S(1)} %add.66), channel_id=1, source_target_pairs={{0,2},{2,0},{4,6},{6,4},{8,10},{10,8},{12,14},{14,12},{16,18},{18,... | collective-permute-start | bytes 196616 | tf_op jit(solution)/shard_map/ppermute | solution.py:307
  111.6 5.6 %collective-permute-start.27 = (f32[128,256]{1,0:T(8,128)S(1)}, f32[128,256]{1,0:T(8,128)S(1)}, u32[]{:S(2)}, u32[]{:S(2)}) collective-permute-start(f32[128,256]{1,0:T(8,128)S(1)} %pad_maximum_fusion.2), channel_id=1, source_target_pairs={{0,1},{1,0},{2,3},{3,2},{4,5},{5,4},{6,7},{7,6},{8,9},{9,8},{10,11... | collective-permute-start | bytes 393224 | tf_op jit(solution)/shard_map/ppermute | solution.py:307
  (10 other events, 12.8 us)

commit v10 on v9

--- a/solution.py
+++ b/solution.py
@@ -72,6 +72,10 @@
     return total
 
 
+def hold_body(blocks_ref, out_ref):
+    pltpu.sync_copy(blocks_ref, out_ref)
+
+
 def near_body(count, *refs):
     cols_ref, live_ref, bases_ref, hessian_ref = refs[:4]
     operands, (out_ref, token_ref, slots_ref) = refs[4:-3], refs[-3:]
@@ -165,12 +169,12 @@
     return jnp.broadcast_to(value[row : row + 1, :], value.shape)
 
 
-def eliminate(tile, first, last):
+def eliminate(tile):
     count = tile.shape[0] // GROUP
     rows = [tile[index * GROUP : (index + 1) * GROUP, :] for index in range(count)]
     sub = lax.broadcasted_iota(jnp.int32, rows[0].shape, 0)
     lane = lax.broadcasted_iota(jnp.int32, rows[0].shape, 1)
-    for step in range(first, last):
+    for step in range(count):
         start = step * GROUP
         pivot_cols = [over_lanes(rows[step], start + col) for col in range(GROUP)]
         factors = {
@@ -180,19 +184,33 @@
         inside = (lane >= start) & (lane < start + GROUP)
         forward = jnp.where(inside, jnp.where(lane - start == sub, 1.0, 0.0), rows[step])
         solved = forward
-        for pivot in range(GROUP):
-            here = sub == pivot
-            value = over_rows(pivot_cols[pivot], pivot)
-            inverse = 1.0 / value
-            ratio = pivot_cols[pivot] * inverse
-            row = over_rows(forward, pivot)
-            forward = jnp.where(
-                here, row * lax.rsqrt(value), jnp.where(sub > pivot, forward - ratio * row, forward)
-            )
-            solved = jnp.where(here, row * inverse, solved - ratio * row)
-            for col in range(pivot + 1, GROUP):
-                top = over_rows(pivot_cols[col], pivot)
-                pivot_cols[col] = jnp.where(here, top * inverse, pivot_cols[col] - ratio * top)
+        for one in range(0, GROUP, 2):
+            two = one + 1
+            left, right = pivot_cols[one], pivot_cols[two]
+            top, cross, low = over_rows(left, one), over_rows(left, two), over_rows(right, two)
+            inverse = 1.0 / (top * low - cross * cross)
+            top_inverse, cross_inverse, low_inverse = low * inverse, -(cross * inverse), top * inverse
+
+            def solve(value):
+                upper, lower = over_rows(value, one), over_rows(value, two)
+                return top_inverse * upper + cross_inverse * lower, cross_inverse * upper + low_inverse * lower
+
+            def without(value, upper, lower):
+                return value - (left * upper + right * lower)
+
+            def reduced(value):
+                upper, lower = solve(value)
+                return jnp.where(sub == one, upper, jnp.where(sub == two, lower, without(value, upper, lower)))
+
+            for col in range(two + 1, GROUP):
+                pivot_cols[col] = reduced(pivot_cols[col])
+            upper, lower = solve(forward)
+            over_top = 1.0 / top
+            first, second = over_rows(forward, one), over_rows(forward, two)
+            below_first = (second - cross * over_top * first) * lax.rsqrt(low - cross * cross * over_top)
+            below = jnp.where(sub > two, without(forward, upper, lower), forward)
+            solved = reduced(solved)
+            forward = jnp.where(sub == one, first * lax.rsqrt(top), jnp.where(sub == two, below_first, below))
         rows[step] = jnp.where(lane < start + GROUP, forward, 0.0)
         solved_rows = [over_rows(solved, pivot) for pivot in range(GROUP)]
         for below in range(step + 1, count):
@@ -203,33 +221,45 @@
     return jnp.concatenate(rows, 0)
 
 
-def unpack_body(total_rows, number_ref, gram_ref, *tile_refs):
-    tiles = ordered_pieces(number_ref, gram_ref) / total_rows
-    for at, tile_ref in enumerate(tile_refs):
-        tile_ref[...] = tiles[at * TILE : (at + 1) * TILE, :]
-
-
-def eliminate_body(first, last, tile_ref, out_ref):
-    out_ref[...] = eliminate(tile_ref[...], first, last)
-
-
-def update_body(at, count, *refs):
-    inputs = refs[: len(refs) // 2]
-    outputs = refs[len(refs) // 2 :]
-    names = [name for name in lower_tiles(count) if name[1] >= at]
-    tiles = {name: ref[...] for name, ref in zip(names, inputs)}
-    column = {row: exact_dot(tiles[row, at], tiles[at, at], NT) for row in range(at + 1, count)}
-    for (row, col), out_ref in zip(names, outputs):
-        if row == at:
-            out_ref[...] = tiles[row, col]
-        elif col == at:
-            out_ref[...] = column[row]
-        else:
-            out_ref[...] = tiles[row, col] - exact_dot(column[row], column[col], NT)
+def scaled_tiles(tiles, count):
+    names = lower_tiles(count)
+    index = lambda dim: lax.broadcasted_iota(jnp.int32, (TILE, TILE), dim)
+    diagonal = {row: jnp.where(index(0) == index(1), tiles[names.index((row, row))], 0.0) for row in range(count)}
+    down = {row: lax.rsqrt(jnp.sum(diagonal[row], 1, keepdims=True)) for row in range(count)}
+    along = {row: lax.rsqrt(jnp.sum(diagonal[row], 0, keepdims=True)) for row in range(count)}
+    return [tile * down[row] * along[col] for (row, col), tile in zip(names, tiles)], along
+
+
+def first_tile_body(count, total_rows, number_ref, gram_ref, *refs):
+    *tile_refs, scale_ref = refs
+    packed = ordered_pieces(number_ref, gram_ref) / total_rows
+    tiles = [packed[at * TILE : (at + 1) * TILE, :] for at in range(len(tile_refs))]
+    tiles, along = scaled_tiles(tiles, count)
+    for row in range(count):
+        scale_ref[row * GROUP : (row + 1) * GROUP, :] = jnp.broadcast_to(along[row], (GROUP, TILE))
+    finish_tile(0, count, dict(zip(lower_tiles(count), tiles)), tile_refs)
+
+
+def next_tile_body(at, count, *refs):
+    names = lower_tiles(count)
+    tiles = {name: ref[...] for name, ref in zip(names, refs)}
+    finish_tile(at, count, tiles, refs[len(names) :])
+
+
+def finish_tile(at, count, tiles, out_refs):
+    tiles = dict(tiles)
+    tiles[at, at] = eliminate(tiles[at, at])
+    for row in range(at + 1, count):
+        tiles[row, at] = exact_dot(tiles[row, at], tiles[at, at], NT)
+    for row in range(at + 1, count):
+        for col in range(at + 1, row + 1):
+            tiles[row, col] = tiles[row, col] - exact_dot(tiles[row, at], tiles[col, at], NT)
+    for name, out_ref in zip(lower_tiles(count), out_refs):
+        out_ref[...] = tiles[name]
 
 
 def basis_body(count, *refs):
-    *tile_refs, two_ref, basis_ref, inverse_ref = refs
+    *tile_refs, scale_ref, two_ref, basis_ref, inverse_ref = refs
     tiles = {name: ref[...] for name, ref in zip(lower_tiles(count), tile_refs)}
     inverse = {}
     for row in range(count):
@@ -242,7 +272,9 @@
     zero = jnp.zeros((TILE, TILE), jnp.float32)
     whole = jnp.concatenate(
         [
-            jnp.concatenate([inverse[row, col] if col <= row else zero for col in range(count)], 1)
+            jnp.concatenate(
+                [inverse[row, col] * scale_ref[col * GROUP, :][None] if col <= row else zero for col in range(count)], 1
+            )
             for row in range(count)
         ],
         0,
@@ -259,44 +291,28 @@
 def factor_stages(total_rows, count, number, two):
     rows, modes = two.shape
     tile = jax.ShapeDtypeStruct((TILE, TILE), jnp.float32)
+    scale = jax.ShapeDtypeStruct((count * GROUP, TILE), jnp.float32)
     names = lower_tiles(count)
-    work = 10 ** 8
-
-    def unpack(gram):
-        body = functools.partial(unpack_body, total_rows)
-        return kernel_call(body, (tile,) * len(names), [SMEM, VMEM], work // 8, gram.size)(number, gram)
-
-    def elimination(at, first, last):
-        def stage(tiles):
-            place = names.index((at, at))
-            call = kernel_call(functools.partial(eliminate_body, first, last), tile, [VMEM], work // 2, TILE * TILE)
-            return tiles[:place] + (call(tiles[place]),) + tiles[place + 1 :]
+    work = 10**8
+
+    def first(gram):
+        body = functools.partial(first_tile_body, count, total_rows)
+        return tuple(kernel_call(body, (tile,) * len(names) + (scale,), [SMEM, VMEM], work, gram.size)(number, gram))
+
+    def following(at):
+        def stage(state):
+            body = functools.partial(next_tile_body, at, count)
+            call = kernel_call(body, (tile,) * len(names), [VMEM] * len(names), work, TILE * TILE)
+            return tuple(call(*state[:-1])) + state[-1:]
 
         return stage
 
-    def update(at):
-        def stage(tiles):
-            picked = [index for index, name in enumerate(names) if name[1] >= at]
-            body = functools.partial(update_body, at, count)
-            call = kernel_call(body, (tile,) * len(picked), [VMEM] * len(picked), work // 4, TILE * TILE)
-            new = call(*[tiles[index] for index in picked])
-            return tuple(new[picked.index(index)] if index in picked else old for index, old in enumerate(tiles))
-
-        return stage
-
-    def finish(tiles):
+    def finish(state):
         outs = (jax.ShapeDtypeStruct((rows, modes), jnp.float32), jax.ShapeDtypeStruct((modes, modes), jnp.float32))
         body = functools.partial(basis_body, count)
-        return kernel_call(body, outs, [VMEM] * (len(names) + 1), work // 2, rows * modes)(*tiles, two)
-
-    groups = TILE // GROUP
-    cuts = [0, groups // 4, groups // 2 + 1, groups]
-    stages = [unpack]
-    for at in range(count):
-        stages += [elimination(at, first, last) for first, last in zip(cuts, cuts[1:])]
-        if at + 1 < count:
-            stages.append(update(at))
-    return stages + [finish]
+        return tuple(kernel_call(body, outs, [VMEM] * (len(names) + 2), work, rows * modes)(*state, two))
+
+    return [first] + [following(at) for at in range(1, count)] + [finish]
 
 
 def tied(left, right):
@@ -426,6 +442,14 @@
     covering, free = 3 * 10 ** 10, 10 ** 7
     token = jax.ShapeDtypeStruct((GROUP, TILE), jnp.float32)
 
+    held = pl.pallas_call(
+        hold_body,
+        out_shape=pltpu.VMEM(hessian.shape, hessian.dtype),
+        in_specs=[pl.BlockSpec(memory_space=pl.ANY)],
+        out_specs=VMEM,
+        compiler_params=pltpu.CompilerParams(vmem_limit_bytes=VMEM_LIMIT),
+    )(hessian)
+
     def near_total(own):
         call = kernel_call(
             functools.partial(near_body, region_blocks),
@@ -435,13 +459,13 @@
             traffic,
             (row_blocks, region_blocks + 1),
         )
-        return call(block_cols, live_blocks, bases, hessian, *own)
+        return call(block_cols, live_blocks, bases, held, *own)
 
     def halo_part(body, outs, which, pair, total, scalars=(), extra=()):
         specs = [SMEM] * 4 + [VMEM] * 4 + [SMEM] * len(scalars) + [VMEM] * len(extra)
         body_of = functools.partial(body, region_blocks, which)
         call = kernel_call(body_of, outs, specs, covering, traffic, halo_slots)
-        return call(block_cols, live_blocks, lists, bases, hessian, *pair, total, *scalars, *extra)
+        return call(block_cols, live_blocks, lists, bases, held, *pair, total, *scalars, *extra)
 
     def step(body, outs, exchanged, scalars, extra):
         own, lower, upper = exchanged
@@ -465,22 +489,22 @@
         total, after = halo_part(middle_body, (wide, token), which, pair, total)
     gram, after = tied(gram, after)
     cross = halo_part(third_body, square, len(pairs), last, total, (cross_number,), (two, after))
-    gram = doubling(*near)(gram)()
-    for bit in between[:-1]:
-        end = doubling(*bit)(gram)
-        cross, gram = tied(halving(*cores)(cross)() if bit is between[0] else cross, end())
-    ends = [doubling(*between[-1])(gram), halving(*near)(cross)]
-    gram, cross = [end() for end in ends]
+    cross = halving(*cores)(cross)()
 
     fold = modes // TILE
     cut = gram.shape[0] // fold
     folded = jnp.concatenate([gram[at * cut : (at + 1) * cut] for at in range(fold)], 1)
     flat = lambda value: [value[:, at * TILE : (at + 1) * TILE] for at in range(fold)]
-    got = partner_value(jnp.concatenate([folded, cross], 0), *across)
-    gram = joining(*cores)(jnp.concatenate(flat(folded) + flat(got[:cut]), 0))()
-    cross = cross + got[cut:]
+    half = cross.shape[0] // 2
+    got = partner_value(jnp.concatenate([folded, cross[half:]], 0), *near)
+    both = jnp.concatenate([folded, cross[:half]], 0) + got
+    for bit in between:
+        both = doubling(*bit)(both)()
+    got = partner_value(both, *across)
+    gram = joining(*cores)(jnp.concatenate(flat(both[:cut]) + flat(got[:cut]), 0))()
+    cross = both[cut:] + got[cut:]
     stages = factor_stages(float(total_rows), modes // TILE, gram_number, two)
-    steps = [doubling(*bit) for bit in between] + [joining(*near), joining(*cores)]
+    steps = [joining(*near), joining(*cores)]
     cross, (basis, inverse) = run_beside(cross, steps, gram, stages)
     body_of = functools.partial(projected_body, float(total_rows))
     call = kernel_call(body_of, square, [SMEM] + [VMEM] * 2, 2 * square_work, traffic)

time: 119 us -> 117 us (0.983)
  starting transfers between devices: 41.5 us -> 37.2 us
  Pallas kernels: 32.5 us -> 34.6 us
    ppermute x13 -> x10, starting transfers between devices: 19 us -> 13.7 us  [partner_value(): lax.ppermute(value, axis, [(at, at ^ bit) for at in range(lax.axis_size(a...]
    pallas_call x18 -> x13, Pallas kernels: 29.7 us -> 31.9 us  [the longest x6 13.4 us: halo_part(): call(block_cols, live_blocks, lists, bases, held, *pair, total, *scalars,...]
    ppermute x6, waiting for transfers between devices: 20.2 us -> 18.2 us  [shifted(): return lax.ppermute(value, axis, pairs)]
    ppermute x6, starting transfers between devices: 14.4 us -> 16.2 us  [shifted(): return lax.ppermute(value, axis, pairs)]
    ppermute x13 -> x10, waiting for transfers between devices: 13.4 us -> 14.7 us  [partner_value(): lax.ppermute(value, axis, [(at, at ^ bit) for at in range(lax.axis_size(a...]
    unnamed x28 -> x26, local copies, waits for them, and re-layouts: 6.74 us -> 5.4 us
  transfers between devices with their start and end apart: 28 -> 25, of which waited for: 14 -> 10; matrix products, arithmetic and copies ran while one was open for 1% -> 3% of each run, Pallas kernels for 19% -> 20%
where the time goes in v10:
time: 117 us
  starting transfers between devices  37.2 us (32%)
  Pallas kernels  34.6 us (30%)
  waiting for transfers between devices  33 us (28%)
  local copies, waits for them, and re-layouts  7.43 us (6%)
  other arithmetic  3.81 us (3%)
    ppermute x6, waiting for transfers between devices, shifted(): return lax.ppermute(value, axis, pairs)  18.2 us
    ppermute x6, starting transfers between devices, shifted(): return lax.ppermute(value, axis, pairs)  16.2 us
    ppermute x10, waiting for transfers between devices, partner_value(): lax.ppermute(value, axis, [(at, at ^ bit) for at in range(lax.axis_size(a...  14.7 us
    ppermute x10, starting transfers between devices, partner_value(): lax.ppermute(value, axis, [(at, at ^ bit) for at in range(lax.axis_size(a...  13.7 us
    pallas_call x6, Pallas kernels, halo_part(): call(block_cols, live_blocks, lists, bases, held, *pair, total, *scalars,...  13.4 us
    ppermute x9, starting transfers between devices, local(): swapped = lambda value: lax.ppermute(value, 'split', [(0, 1), (1, 0)])  7.3 us
    pallas_call x3, Pallas kernels, near_total(): return call(block_cols, live_blocks, bases, held, *own)  5.91 us
    pallas_call x1, Pallas kernels, first(): kernel_call(body, (tile,) * len(names) + (scale,), [SMEM, VMEM], work, gr...  5.88 us
  transfers between devices with their start and end apart: 25, of which 10 were waited for; matrix products, arithmetic and copies ran while one was open for 3% of the time, Pallas kernels for 20%

profile of v10, /device:TPU:1, one launch (start us, length us, event | category | flops | bytes accessed | tf_op | source)
XLA Modules:
  0.0 117.0 jit_solution(7118022643669723125)
XLA Ops:
  3.3 2.0 %collective-permute-start = (bf16[592,256]{1,0:T(8,128)(2,1)}, bf16[592,256]{1,0:T(8,128)(2,1)}, u32[]{:S(2)}, u32[]{:S(2)}) collective-permute-start(bf16[592,256]{1,0:T(8,128)(2,1)} %get-tuple-element.69), channel_id=1, source_target_pairs={{0,2},{2,4},{4,6},{6,8},{8,10},{10,12},{12,14},{14,16},{16,18},{18... | collective-permute-start | bytes 909320 | tf_op jit(solution)/shard_map/ppermute | solution.py:26
  5.3 4.0 %collective-permute-start.1 = (bf16[592,256]{1,0:T(8,128)(2,1)}, bf16[592,256]{1,0:T(8,128)(2,1)}, u32[]{:S(2)}, u32[]{:S(2)}) collective-permute-start(bf16[592,256]{1,0:T(8,128)(2,1)} %get-tuple-element.69), channel_id=1, source_target_pairs={{0,30},{2,0},{4,2},{6,4},{8,6},{10,8},{12,10},{14,12},{16,14},{18,... | collective-permute-start | bytes 909320 | tf_op jit(solution)/shard_map/ppermute | solution.py:26
  10.3 2.0 %copy-done = bf16[3,12,192,192]{3,2,1,0:T(8,128)(2,1)S(1)} copy-done((bf16[3,12,192,192]{3,2,1,0:T(8,128)(2,1)S(1)}, bf16[3,12,192,192]{3,2,1,0:T(8,128)(2,1)}, u32[]{:S(2)}) %copy-start) | copy-done | bytes 2654232
  12.8 5.2 %collective-permute-done = bf16[592,256]{1,0:T(8,128)(2,1)} collective-permute-done((bf16[592,256]{1,0:T(8,128)(2,1)}, bf16[592,256]{1,0:T(8,128)(2,1)}, u32[]{:S(2)}, u32[]{:S(2)}) %collective-permute-start) | collective-permute-done | bytes 303136 | tf_op jit(solution)/shard_map/ppermute | solution.py:26
  18.7 1.3 %collective-permute-done.1 = bf16[592,256]{1,0:T(8,128)(2,1)} collective-permute-done((bf16[592,256]{1,0:T(8,128)(2,1)}, bf16[592,256]{1,0:T(8,128)(2,1)}, u32[]{:S(2)}, u32[]{:S(2)}) %collective-permute-start.1) | collective-permute-done | bytes 303136 | tf_op jit(solution)/shard_map/ppermute | solution.py:26
  20.6 2.2 %shard_map.78 = (f32[576,256]{1,0:T(8,128)S(1)}, f32[8,128]{1,0:T(8,128)}) custom-call(s32[3,12]{1,0:T(4,128)S(1)} %copy-done.7, s32[3]{0:T(128)S(1)} %copy-done.8, s32[2]{0:T(128)S(1)} %pad_add_fusion.refs_2_.refs_3_, bf16[3,12,192,192]{3,2,1,0:T(8,128)(2,1)S(1)} %shard_map.77.refs_3_.refs_4_, bf16[1,592,256]{2,1,0:T(8,128)(2,1)S(1)} %copy-done.4, ...), custom_call_target="tpu_custom_call" | custom-call | flops 10000000 | bytes 276480 | tf_op jit(solution)/shard_map/pallas_call | solution.py:462
  22.8 1.5 %collective-permute-start.2 = (bf16[592,256]{1,0:T(8,128)(2,1)}, bf16[592,256]{1,0:T(8,128)(2,1)S(1)}, u32[]{:S(2)}, u32[]{:S(2)}) collective-permute-start(bf16[592,256]{1,0:T(8,128)(2,1)} %collective-permute-done), channel_id=1, source_target_pairs={{0,1},{1,0},{2,3},{3,2},{4,5},{5,4},{6,7},{7,6},{8,9},{9,8},{10,11... | collective-permute-start | bytes 909320 | tf_op jit(solution)/shard_map/ppermute | solution.py:387
  24.4 2.5 %shard_map.79 = (f32[576,256]{1,0:T(8,128)S(1)}, f32[8,128]{1,0:T(8,128)}) custom-call(s32[3,12]{1,0:T(4,128)S(1)} %copy-done.7, s32[3]{0:T(128)S(1)} %copy-done.8, s32[2,6]{1,0:T(2,128)S(1)} %maximum_convert_fusion.refs_2_, s32[2]{0:T(128)S(1)} %pad_add_fusion.refs_2_.refs_3_, bf16[3,12,192,192]{3,2,1,0:T(8,128)(2,1)S(1)} %shard_map.77.refs_3_.refs_4_, ...), custom_call_target="tpu_custom_call" | custom-call | flops 30000001024 | bytes 276480 | tf_op jit(solution)/shard_map/pallas_call | solution.py:468
  26.9 1.5 %shard_map.80 = (f32[576,256]{1,0:T(8,128)S(1)}, bf16[576,256]{1,0:T(8,128)(2,1)S(1)}) custom-call(s32[3,12]{1,0:T(4,128)S(1)} %copy-done.7, s32[3]{0:T(128)S(1)} %copy-done.8, s32[2,6]{1,0:T(2,128)S(1)} %maximum_convert_fusion.refs_2_, s32[2]{0:T(128)S(1)} %pad_add_fusion.refs_2_.refs_3_, bf16[3,12,192,192]{3,2,1,0:T(8,128)(2,1)S(1)} %shard_map.77.refs_3_.refs_4_, ...), custom_call_target="tpu_custom_call" | custom-call | flops 30000001024 | bytes 276480 | tf_op jit(solution)/shard_map/pallas_call | solution.py:468
  30.5 3.8 %collective-permute-start.7 = (bf16[576,256]{1,0:T(8,128)(2,1)S(1)}, bf16[576,256]{1,0:T(8,128)(2,1)S(1)}, u32[]{:S(2)}, u32[]{:S(2)}) collective-permute-start(bf16[576,256]{1,0:T(8,128)(2,1)S(1)} %get-tuple-element.37), channel_id=1, source_target_pairs={{0,30},{2,0},{4,2},{6,4},{8,6},{10,8},{12,10},{14,12},{16,14},{18,... | collective-permute-start | bytes 884744 | tf_op jit(solution)/shard_map/ppermute | solution.py:26
  34.4 7.5 %collective-permute-done.5 = bf16[576,256]{1,0:T(8,128)(2,1)S(1)} collective-permute-done((bf16[576,256]{1,0:T(8,128)(2,1)S(1)}, bf16[576,256]{1,0:T(8,128)(2,1)S(1)}, u32[]{:S(2)}, u32[]{:S(2)}) %collective-permute-start.5) | collective-permute-done | bytes 294944 | tf_op jit(solution)/shard_map/ppermute | solution.py:26
  41.9 1.4 %collective-permute-start.6 = (bf16[576,256]{1,0:T(8,128)(2,1)S(1)}, bf16[576,256]{1,0:T(8,128)(2,1)S(1)}, u32[]{:S(2)}, u32[]{:S(2)}) collective-permute-start(bf16[576,256]{1,0:T(8,128)(2,1)S(1)} %collective-permute-done.5), channel_id=1, source_target_pairs={{0,1},{1,0},{2,3},{3,2},{4,5},{5,4},{6,7},{7,6},{8,9},{9,8},{10,11... | collective-permute-start | bytes 884744 | tf_op jit(solution)/shard_map/ppermute | solution.py:387
  43.3 1.8 %shard_map.81 = (f32[576,256]{1,0:T(8,128)S(1)}, f32[8,128]{1,0:T(8,128)}) custom-call(s32[3,12]{1,0:T(4,128)S(1)} %copy-done.7, s32[3]{0:T(128)S(1)} %copy-done.8, s32[2]{0:T(128)S(1)} %pad_add_fusion.refs_2_.refs_3_, bf16[3,12,192,192]{3,2,1,0:T(8,128)(2,1)S(1)} %shard_map.77.refs_3_.refs_4_, bf16[1,576,256]{2,1,0:T(8,128)(2,1)S(1)} %bitcast.25, ...), custom_call_target="tpu_custom_call" | custom-call | flops 10000000 | bytes 276480 | tf_op jit(solution)/shard_map/pallas_call | solution.py:462
  45.5 2.0 %shard_map.82 = (f32[576,256]{1,0:T(8,128)S(1)}, f32[8,128]{1,0:T(8,128)}) custom-call(s32[3,12]{1,0:T(4,128)S(1)} %copy-done.7, s32[3]{0:T(128)S(1)} %copy-done.8, s32[2,6]{1,0:T(2,128)S(1)} %maximum_convert_fusion.refs_2_, s32[2]{0:T(128)S(1)} %pad_add_fusion.refs_2_.refs_3_, bf16[3,12,192,192]{3,2,1,0:T(8,128)(2,1)S(1)} %shard_map.77.refs_3_.refs_4_, ...), custom_call_target="tpu_custom_call" | custom-call | flops 30000001024 | bytes 276480 | tf_op jit(solution)/shard_map/pallas_call | solution.py:468
  47.4 2.3 %shard_map.83 = (f32[576,256]{1,0:T(8,128)S(1)}, bf16[576,256]{1,0:T(8,128)(2,1)}) custom-call(s32[3,12]{1,0:T(4,128)S(1)} %copy-done.7, s32[3]{0:T(128)S(1)} %copy-done.8, s32[2,6]{1,0:T(2,128)S(1)} %maximum_convert_fusion.refs_2_, s32[2]{0:T(128)S(1)} %pad_add_fusion.refs_2_.refs_3_, bf16[3,12,192,192]{3,2,1,0:T(8,128)(2,1)S(1)} %shard_map.77.refs_3_.refs_4_, ...), custom_call_target="tpu_custom_call" | custom-call | flops 30000001024 | bytes 276480 | tf_op jit(solution)/shard_map/pallas_call | solution.py:468
  50.7 2.2 %collective-permute-start.13 = (bf16[576,256]{1,0:T(8,128)(2,1)}, bf16[576,256]{1,0:T(8,128)(2,1)}, u32[]{:S(2)}, u32[]{:S(2)}) collective-permute-start(bf16[576,256]{1,0:T(8,128)(2,1)} %get-tuple-element.42), channel_id=1, source_target_pairs={{0,2},{2,4},{4,6},{6,8},{8,10},{10,12},{12,14},{14,16},{16,18},{18... | collective-permute-start | bytes 884744 | tf_op jit(solution)/shard_map/ppermute | solution.py:26
  52.9 2.9 %collective-permute-start.14 = (bf16[576,256]{1,0:T(8,128)(2,1)}, bf16[576,256]{1,0:T(8,128)(2,1)}, u32[]{:S(2)}, u32[]{:S(2)}) collective-permute-start(bf16[576,256]{1,0:T(8,128)(2,1)} %get-tuple-element.42), channel_id=1, source_target_pairs={{0,30},{2,0},{4,2},{6,4},{8,6},{10,8},{12,10},{14,12},{16,14},{18,... | collective-permute-start | bytes 884744 | tf_op jit(solution)/shard_map/ppermute | solution.py:26
  55.8 1.9 %shard_map.84 = (f32[576,256]{1,0:T(8,128)S(1)}, f32[8,128]{1,0:T(8,128)S(1)}) custom-call(s32[3,12]{1,0:T(4,128)S(1)} %copy-done.7, s32[3]{0:T(128)S(1)} %copy-done.8, s32[2]{0:T(128)S(1)} %pad_add_fusion.refs_2_.refs_3_, bf16[3,12,192,192]{3,2,1,0:T(8,128)(2,1)S(1)} %shard_map.77.refs_3_.refs_4_, bf16[1,576,256]{2,1,0:T(8,128)(2,1)} %bitcast.16.refs_4_, ...), custom_call_target="tpu_custom_call" | custom-call | flops 10000000 | bytes 276480 | tf_op jit(solution)/shard_map/pallas_call | solution.py:462
  61.8 4.2 %collective-permute-done.13 = bf16[576,256]{1,0:T(8,128)(2,1)} collective-permute-done((bf16[576,256]{1,0:T(8,128)(2,1)}, bf16[576,256]{1,0:T(8,128)(2,1)}, u32[]{:S(2)}, u32[]{:S(2)}) %collective-permute-start.13) | collective-permute-done | bytes 294944 | tf_op jit(solution)/shard_map/ppermute | solution.py:26
  66.8 1.4 %collective-permute-start.16 = (bf16[576,256]{1,0:T(8,128)(2,1)}, bf16[576,256]{1,0:T(8,128)(2,1)S(1)}, u32[]{:S(2)}, u32[]{:S(2)}) collective-permute-start(bf16[576,256]{1,0:T(8,128)(2,1)} %collective-permute-done.14), channel_id=1, source_target_pairs={{0,1},{1,0},{2,3},{3,2},{4,5},{5,4},{6,7},{7,6},{8,9},{9,8},{10,11... | collective-permute-start | bytes 884744 | tf_op jit(solution)/shard_map/ppermute | solution.py:387
  71.1 2.0 %shard_map.86 = (f32[576,256]{1,0:T(8,128)S(1)}, f32[8,128]{1,0:T(8,128)S(1)}) custom-call(s32[3,12]{1,0:T(4,128)S(1)} %copy-done.7, s32[3]{0:T(128)S(1)} %copy-done.8, s32[2,6]{1,0:T(2,128)S(1)} %maximum_convert_fusion.refs_2_, s32[2]{0:T(128)S(1)} %pad_add_fusion.refs_2_.refs_3_, bf16[3,12,192,192]{3,2,1,0:T(8,128)(2,1)S(1)} %shard_map.77.refs_3_.refs_4_, ...), custom_call_target="tpu_custom_call" | custom-call | flops 30000001024 | bytes 276480 | tf_op jit(solution)/shard_map/pallas_call | solution.py:468
  73.2 3.1 %shard_map.87 = f32[256,256]{1,0:T(8,128)S(1)} custom-call(s32[3,12]{1,0:T(4,128)S(1)} %copy-done.7, s32[3]{0:T(128)S(1)} %copy-done.8, s32[2,6]{1,0:T(2,128)S(1)} %maximum_convert_fusion.refs_2_, s32[2]{0:T(128)S(1)} %pad_add_fusion.refs_2_.refs_3_, bf16[3,12,192,192]{3,2,1,0:T(8,128)(2,1)S(1)} %shard_map.77.refs_3_.refs_4_, ...), custom_call_target="tpu_custom_call" | custom-call | flops 30000001024 | bytes 276480 | tf_op jit(solution)/shard_map/pallas_call | solution.py:468
  78.9 3.4 %collective-permute-done.18 = f32[112,256]{1,0:T(8,128)S(1)} collective-permute-done((f32[112,256]{1,0:T(8,128)S(1)}, f32[112,256]{1,0:T(8,128)S(1)}, u32[]{:S(2)}, u32[]{:S(2)}) %collective-permute-start.18) | collective-permute-done | bytes 114720 | tf_op jit(solution)/shard_map/ppermute | solution.py:323
  83.5 2.6 %collective-permute-done.19 = f32[112,256]{1,0:T(8,128)S(1)} collective-permute-done((f32[112,256]{1,0:T(8,128)S(1)}, f32[112,256]{1,0:T(8,128)S(1)}, u32[]{:S(2)}, u32[]{:S(2)}) %collective-permute-start.19) | collective-permute-done | bytes 114720 | tf_op jit(solution)/shard_map/ppermute | solution.py:323
  86.0 2.2 %collective-permute-start.20 = (f32[112,256]{1,0:T(8,128)S(1)}, f32[112,256]{1,0:T(8,128)S(1)}, u32[]{:S(2)}, u32[]{:S(2)}) collective-permute-start(f32[112,256]{1,0:T(8,128)S(1)} %add.52), channel_id=1, source_target_pairs={{0,16},{2,18},{4,20},{6,22},{8,24},{10,26},{12,28},{14,30},{16,0},... | collective-permute-start | bytes 344072 | tf_op jit(solution)/shard_map/ppermute | solution.py:323
  88.2 3.7 %collective-permute-done.20 = f32[112,256]{1,0:T(8,128)S(1)} collective-permute-done((f32[112,256]{1,0:T(8,128)S(1)}, f32[112,256]{1,0:T(8,128)S(1)}, u32[]{:S(2)}, u32[]{:S(2)}) %collective-permute-start.20) | collective-permute-done | bytes 114720 | tf_op jit(solution)/shard_map/ppermute | solution.py:323
  92.5 3.1 %collective-permute-done.21 = f32[112,256]{1,0:T(8,128)S(1)} collective-permute-done((f32[112,256]{1,0:T(8,128)S(1)}, f32[112,256]{1,0:T(8,128)S(1)}, u32[]{:S(2)}, u32[]{:S(2)}) %collective-permute-start.21) | collective-permute-done | bytes 114720 | tf_op jit(solution)/shard_map/ppermute | solution.py:323
  95.6 4.6 %collective-permute-start.22 = (f32[192,128]{1,0:T(8,128)S(1)}, f32[192,128]{1,0:T(8,128)S(1)}, u32[]{:S(2)}, u32[]{:S(2)}) collective-permute-start(f32[192,128]{1,0:T(8,128)S(1)} %pad_maximum_fusion.3), channel_id=1, source_target_pairs={{0,1},{1,0},{2,3},{3,2},{4,5},{5,4},{6,7},{7,6},{8,9},{9,8},{10,11... | collective-permute-start | bytes 294920 | tf_op jit(solution)/shard_map/ppermute | solution.py:323
  102.3 5.9 %shard_map.88 = (f32[128,128]{1,0:T(8,128)S(1)}, f32[128,128]{1,0:T(8,128)S(1)}, f32[128,128]{1,0:T(8,128)S(1)}, f32[16,128]{1,0:T(8,128)S(1)}) custom-call(s32[1]{0:T(128)} %bitcast.number_ref, f32[384,128]{1,0:T(8,128)S(1)} %constant_dynamic-update-slice_fusion.gram_ref), custom_call_target="tpu_custom_call" | custom-call | flops 100000000 | bytes 3072 | tf_op jit(solution)/shard_map/pallas_call | solution.py:300
  108.2 4.4 %shard_map.89 = (f32[128,128]{1,0:T(8,128)S(1)}, f32[128,128]{1,0:T(8,128)S(1)}, f32[128,128]{1,0:T(8,128)S(1)}) custom-call(f32[128,128]{1,0:T(8,128)S(1)} %get-tuple-element.51.refs_0_, f32[128,128]{1,0:T(8,128)S(1)} %get-tuple-element.52.refs_1_, f32[128,128]{1,0:T(8,128)S(1)} %get-tuple-element.53.refs_2_), custom_call_target="tpu_custom_call" | custom-call | flops 100000000 | bytes 1024 | tf_op jit(solution)/shard_map/pallas_call | solution.py:306
  113.4 1.9 %shard_map.90 = (f32[576,256]{1,0:T(8,128)}, f32[256,256]{1,0:T(8,128)S(1)}) custom-call(f32[128,128]{1,0:T(8,128)S(1)} %get-tuple-element.59.refs_0_, f32[128,128]{1,0:T(8,128)S(1)} %get-tuple-element.60.refs_1_, f32[128,128]{1,0:T(8,128)S(1)} %get-tuple-element.61.refs_2_, f32[16,128]{1,0:T(8,128)S(1)} %get-tuple-element.62.refs_3_, f32[576,256]{1,0:T(8,128)S(1)} %copy-done.3), custom_call_target="tpu_custom_call" | custom-call | flops 100000000 | bytes 9216 | tf_op jit(solution)/shard_map/pallas_call | solution.py:313
  115.3 1.7 %shard_map.91 = f32[256,256]{1,0:T(8,128)} custom-call(s32[1]{0:T(128)} %bitcast.22.refs_8_.number_ref, f32[256,256]{1,0:T(8,128)S(1)} %pad_maximum_fusion.cross_ref, f32[256,256]{1,0:T(8,128)S(1)} %get-tuple-element.67.inverse_ref), custom_call_target="tpu_custom_call" | custom-call | flops 150994944 | bytes 276480 | tf_op jit(solution)/shard_map/pallas_call | solution.py:511
  (85 shorter events, 23.9 us)
Async XLA Ops:
  3.3 14.7 %collective-permute-start = (bf16[592,256]{1,0:T(8,128)(2,1)}, bf16[592,256]{1,0:T(8,128)(2,1)}, u32[]{:S(2)}, u32[]{:S(2)}) collective-permute-start(bf16[592,256]{1,0:T(8,128)(2,1)} %get-tuple-element.69), channel_id=1, source_target_pairs={{0,2},{2,4},{4,6},{6,8},{8,10},{10,12},{12,14},{14,16},{16,18},{18... | collective-permute-start | bytes 909320 | tf_op jit(solution)/shard_map/ppermute | solution.py:26
  5.3 14.6 %collective-permute-start.1 = (bf16[592,256]{1,0:T(8,128)(2,1)}, bf16[592,256]{1,0:T(8,128)(2,1)}, u32[]{:S(2)}, u32[]{:S(2)}) collective-permute-start(bf16[592,256]{1,0:T(8,128)(2,1)} %get-tuple-element.69), channel_id=1, source_target_pairs={{0,30},{2,0},{4,2},{6,4},{8,6},{10,8},{12,10},{14,12},{16,14},{18,... | collective-permute-start | bytes 909320 | tf_op jit(solution)/shard_map/ppermute | solution.py:26
  9.3 11.3 %collective-permute-start.4 = (bf16[592,256]{1,0:T(8,128)(2,1)}, bf16[592,256]{1,0:T(8,128)(2,1)}, u32[]{:S(2)}, u32[]{:S(2)}) collective-permute-start(bf16[592,256]{1,0:T(8,128)(2,1)} %get-tuple-element.69), channel_id=1, source_target_pairs={{0,1},{1,0},{2,3},{3,2},{4,5},{5,4},{6,7},{7,6},{8,9},{9,8},{10,11... | collective-permute-start | bytes 909320 | tf_op jit(solution)/shard_map/ppermute | solution.py:387
  12.3 8.3 %copy-start.4 = (bf16[1,592,256]{2,1,0:T(8,128)(2,1)S(1)}, bf16[1,592,256]{2,1,0:T(8,128)(2,1)}, u32[]{:S(2)}) copy-start(bf16[1,592,256]{2,1,0:T(8,128)(2,1)} %get-tuple-element.68.refs_4_) | copy-start | bytes 909316
  12.3 8.4 %copy-start.7 = (s32[3,12]{1,0:T(4,128)S(1)}, s32[3,12]{1,0:T(4,128)}, u32[]{:S(2)}) copy-start(s32[3,12]{1,0:T(4,128)} %refs_0_.17) | copy-start | bytes 436
  12.3 8.4 %copy-start.8 = (s32[3]{0:T(128)S(1)}, s32[3]{0:T(128)}, u32[]{:S(2)}) copy-start(s32[3]{0:T(128)} %refs_1_.17) | copy-start | bytes 40
  22.8 4.1 %collective-permute-start.2 = (bf16[592,256]{1,0:T(8,128)(2,1)}, bf16[592,256]{1,0:T(8,128)(2,1)S(1)}, u32[]{:S(2)}, u32[]{:S(2)}) collective-permute-start(bf16[592,256]{1,0:T(8,128)(2,1)} %collective-permute-done), channel_id=1, source_target_pairs={{0,1},{1,0},{2,3},{3,2},{4,5},{5,4},{6,7},{7,6},{8,9},{9,8},{10,11... | collective-permute-start | bytes 909320 | tf_op jit(solution)/shard_map/ppermute | solution.py:387
  24.4 2.5 %collective-permute-start.3 = (bf16[592,256]{1,0:T(8,128)(2,1)}, bf16[592,256]{1,0:T(8,128)(2,1)S(1)}, u32[]{:S(2)}, u32[]{:S(2)}) collective-permute-start(bf16[592,256]{1,0:T(8,128)(2,1)} %collective-permute-done.1), channel_id=1, source_target_pairs={{0,1},{1,0},{2,3},{3,2},{4,5},{5,4},{6,7},{7,6},{8,9},{9,8},{10,11... | collective-permute-start | bytes 909320 | tf_op jit(solution)/shard_map/ppermute | solution.py:387
  24.4 2.5 %copy-start.6 = (f32[576,256]{1,0:T(8,128)S(1)}, f32[576,256]{1,0:T(8,128)}, u32[]{:S(2)}) copy-start(f32[576,256]{1,0:T(8,128)} %refs_10_.1) | copy-start | bytes 1769476
  24.4 2.5 %copy-start.11 = (f32[2]{0:T(128)S(1)}, f32[2]{0:T(128)}, u32[]{:S(2)}) copy-start(f32[2]{0:T(128)} %refs_8_.3) | copy-start | bytes 28
  28.5 13.4 %collective-permute-start.5 = (bf16[576,256]{1,0:T(8,128)(2,1)S(1)}, bf16[576,256]{1,0:T(8,128)(2,1)S(1)}, u32[]{:S(2)}, u32[]{:S(2)}) collective-permute-start(bf16[576,256]{1,0:T(8,128)(2,1)S(1)} %get-tuple-element.37), channel_id=1, source_target_pairs={{0,2},{2,4},{4,6},{6,8},{8,10},{10,12},{12,14},{14,16},{16,18},{18... | collective-permute-start | bytes 884744 | tf_op jit(solution)/shard_map/ppermute | solution.py:26
  29.7 13.5 %collective-permute-start.9 = (bf16[576,256]{1,0:T(8,128)(2,1)S(1)}, bf16[576,256]{1,0:T(8,128)(2,1)S(1)}, u32[]{:S(2)}, u32[]{:S(2)}) collective-permute-start(bf16[576,256]{1,0:T(8,128)(2,1)S(1)} %get-tuple-element.37), channel_id=1, source_target_pairs={{0,1},{1,0},{2,3},{3,2},{4,5},{5,4},{6,7},{7,6},{8,9},{9,8},{10,11... | collective-permute-start | bytes 884744 | tf_op jit(solution)/shard_map/ppermute | solution.py:387
  30.5 14.6 %collective-permute-start.7 = (bf16[576,256]{1,0:T(8,128)(2,1)S(1)}, bf16[576,256]{1,0:T(8,128)(2,1)S(1)}, u32[]{:S(2)}, u32[]{:S(2)}) collective-permute-start(bf16[576,256]{1,0:T(8,128)(2,1)S(1)} %get-tuple-element.37), channel_id=1, source_target_pairs={{0,30},{2,0},{4,2},{6,4},{8,6},{10,8},{12,10},{14,12},{16,14},{18,... | collective-permute-start | bytes 884744 | tf_op jit(solution)/shard_map/ppermute | solution.py:26
  41.9 5.5 %collective-permute-start.6 = (bf16[576,256]{1,0:T(8,128)(2,1)S(1)}, bf16[576,256]{1,0:T(8,128)(2,1)S(1)}, u32[]{:S(2)}, u32[]{:S(2)}) collective-permute-start(bf16[576,256]{1,0:T(8,128)(2,1)S(1)} %collective-permute-done.5), channel_id=1, source_target_pairs={{0,1},{1,0},{2,3},{3,2},{4,5},{5,4},{6,7},{7,6},{8,9},{9,8},{10,11... | collective-permute-start | bytes 884744 | tf_op jit(solution)/shard_map/ppermute | solution.py:387
  45.1 2.4 %collective-permute-start.8 = (bf16[576,256]{1,0:T(8,128)(2,1)S(1)}, bf16[576,256]{1,0:T(8,128)(2,1)S(1)}, u32[]{:S(2)}, u32[]{:S(2)}) collective-permute-start(bf16[576,256]{1,0:T(8,128)(2,1)S(1)} %collective-permute-done.7), channel_id=1, source_target_pairs={{0,1},{1,0},{2,3},{3,2},{4,5},{5,4},{6,7},{7,6},{8,9},{9,8},{10,11... | collective-permute-start | bytes 884744 | tf_op jit(solution)/shard_map/ppermute | solution.py:387
  50.6 5.2 %collective-permute-start.10 = (bf16[576,256]{1,0:T(8,128)(2,1)}, bf16[576,256]{1,0:T(8,128)(2,1)}, u32[]{:S(2)}, u32[]{:S(2)}) collective-permute-start(bf16[576,256]{1,0:T(8,128)(2,1)} %get-tuple-element.42), channel_id=1, source_target_pairs={{0,1},{1,0},{2,3},{3,2},{4,5},{5,4},{6,7},{7,6},{8,9},{9,8},{10,11... | collective-permute-start | bytes 884744 | tf_op jit(solution)/shard_map/ppermute | solution.py:387
  50.7 15.3 %collective-permute-start.13 = (bf16[576,256]{1,0:T(8,128)(2,1)}, bf16[576,256]{1,0:T(8,128)(2,1)}, u32[]{:S(2)}, u32[]{:S(2)}) collective-permute-start(bf16[576,256]{1,0:T(8,128)(2,1)} %get-tuple-element.42), channel_id=1, source_target_pairs={{0,2},{2,4},{4,6},{6,8},{8,10},{10,12},{12,14},{14,16},{16,18},{18... | collective-permute-start | bytes 884744 | tf_op jit(solution)/shard_map/ppermute | solution.py:26
  52.9 13.9 %collective-permute-start.14 = (bf16[576,256]{1,0:T(8,128)(2,1)}, bf16[576,256]{1,0:T(8,128)(2,1)}, u32[]{:S(2)}, u32[]{:S(2)}) collective-permute-start(bf16[576,256]{1,0:T(8,128)(2,1)} %get-tuple-element.42), channel_id=1, source_target_pairs={{0,30},{2,0},{4,2},{6,4},{8,6},{10,8},{12,10},{14,12},{16,14},{18,... | collective-permute-start | bytes 884744 | tf_op jit(solution)/shard_map/ppermute | solution.py:26
  55.7 2.7 %copy-start.2 = (f32[576,256]{1,0:T(8,128)S(1)}, f32[576,256]{1,0:T(8,128)}, u32[]{:S(2)}) copy-start(f32[576,256]{1,0:T(8,128)} %copy-done.1) | copy-start | bytes 1769476
  60.8 7.3 %collective-permute-start.11 = (f32[192,128]{1,0:T(8,128)}, f32[192,128]{1,0:T(8,128)}, u32[]{:S(2)}, u32[]{:S(2)}) collective-permute-start(f32[192,128]{1,0:T(8,128)} %slice.81), channel_id=1, source_target_pairs={{0,1},{1,0},{2,3},{3,2},{4,5},{5,4},{6,7},{7,6},{8,9},{9,8},{10,11... | collective-permute-start | bytes 294920 | tf_op jit(solution)/shard_map/ppermute | solution.py:323
  66.0 7.2 %collective-permute-start.15 = (bf16[576,256]{1,0:T(8,128)(2,1)}, bf16[576,256]{1,0:T(8,128)(2,1)S(1)}, u32[]{:S(2)}, u32[]{:S(2)}) collective-permute-start(bf16[576,256]{1,0:T(8,128)(2,1)} %collective-permute-done.13), channel_id=1, source_target_pairs={{0,1},{1,0},{2,3},{3,2},{4,5},{5,4},{6,7},{7,6},{8,9},{9,8},{10,11... | collective-permute-start | bytes 884744 | tf_op jit(solution)/shard_map/ppermute | solution.py:387
  66.8 6.4 %collective-permute-start.16 = (bf16[576,256]{1,0:T(8,128)(2,1)}, bf16[576,256]{1,0:T(8,128)(2,1)S(1)}, u32[]{:S(2)}, u32[]{:S(2)}) collective-permute-start(bf16[576,256]{1,0:T(8,128)(2,1)} %collective-permute-done.14), channel_id=1, source_target_pairs={{0,1},{1,0},{2,3},{3,2},{4,5},{5,4},{6,7},{7,6},{8,9},{9,8},{10,11... | collective-permute-start | bytes 884744 | tf_op jit(solution)/shard_map/ppermute | solution.py:387
  69.1 4.0 %collective-permute-start.12 = (f32[96,128]{1,0:T(8,128)S(1)}, f32[96,128]{1,0:T(8,128)S(1)}, u32[]{:S(2)}, u32[]{:S(2)}) collective-permute-start(f32[96,128]{1,0:T(8,128)S(1)} %slice.83), channel_id=1, source_target_pairs={{0,4},{2,6},{4,0},{6,2},{8,12},{10,14},{12,8},{14,10},{16,20},{18,... | collective-permute-start | bytes 147464 | tf_op jit(solution)/shard_map/ppermute | solution.py:323
  71.1 2.1 %copy-start.3 = (f32[576,256]{1,0:T(8,128)S(1)}, f32[576,256]{1,0:T(8,128)}, u32[]{:S(2)}) copy-start(f32[576,256]{1,0:T(8,128)} %copy-done.1) | copy-start | bytes 1769476
  76.3 1.4 %collective-permute-start.17 = (f32[128,256]{1,0:T(8,128)S(1)}, f32[128,256]{1,0:T(8,128)S(1)}, u32[]{:S(2)}, u32[]{:S(2)}) collective-permute-start(f32[128,256]{1,0:T(8,128)S(1)} %slice.85), channel_id=1, source_target_pairs={{0,1},{1,0},{2,3},{3,2},{4,5},{5,4},{6,7},{7,6},{8,9},{9,8},{10,11... | collective-permute-start | bytes 393224 | tf_op jit(solution)/shard_map/ppermute | solution.py:323
  77.8 4.5 %collective-permute-start.18 = (f32[112,256]{1,0:T(8,128)S(1)}, f32[112,256]{1,0:T(8,128)S(1)}, u32[]{:S(2)}, u32[]{:S(2)}) collective-permute-start(f32[112,256]{1,0:T(8,128)S(1)} %fusion.2), channel_id=1, source_target_pairs={{0,2},{2,0},{4,6},{6,4},{8,10},{10,8},{12,14},{14,12},{16,18},{18,... | collective-permute-start | bytes 344072 | tf_op jit(solution)/shard_map/ppermute | solution.py:323
  82.3 3.7 %collective-permute-start.19 = (f32[112,256]{1,0:T(8,128)S(1)}, f32[112,256]{1,0:T(8,128)S(1)}, u32[]{:S(2)}, u32[]{:S(2)}) collective-permute-start(f32[112,256]{1,0:T(8,128)S(1)} %maximum_add_fusion), channel_id=1, source_target_pairs={{0,8},{2,10},{4,12},{6,14},{8,0},{10,2},{12,4},{14,6},{16,24},{18,... | collective-permute-start | bytes 344072 | tf_op jit(solution)/shard_map/ppermute | solution.py:323
  86.0 5.8 %collective-permute-start.20 = (f32[112,256]{1,0:T(8,128)S(1)}, f32[112,256]{1,0:T(8,128)S(1)}, u32[]{:S(2)}, u32[]{:S(2)}) collective-permute-start(f32[112,256]{1,0:T(8,128)S(1)} %add.52), channel_id=1, source_target_pairs={{0,16},{2,18},{4,20},{6,22},{8,24},{10,26},{12,28},{14,30},{16,0},... | collective-permute-start | bytes 344072 | tf_op jit(solution)/shard_map/ppermute | solution.py:323
  91.9 3.7 %collective-permute-start.21 = (f32[112,256]{1,0:T(8,128)S(1)}, f32[112,256]{1,0:T(8,128)S(1)}, u32[]{:S(2)}, u32[]{:S(2)}) collective-permute-start(f32[112,256]{1,0:T(8,128)S(1)} %add.53), channel_id=1, source_target_pairs={{0,4},{2,6},{4,0},{6,2},{8,12},{10,14},{12,8},{14,10},{16,20},{18,... | collective-permute-start | bytes 344072 | tf_op jit(solution)/shard_map/ppermute | solution.py:323
  95.6 5.6 %collective-permute-start.22 = (f32[192,128]{1,0:T(8,128)S(1)}, f32[192,128]{1,0:T(8,128)S(1)}, u32[]{:S(2)}, u32[]{:S(2)}) collective-permute-start(f32[192,128]{1,0:T(8,128)S(1)} %pad_maximum_fusion.3), channel_id=1, source_target_pairs={{0,1},{1,0},{2,3},{3,2},{4,5},{5,4},{6,7},{7,6},{8,9},{9,8},{10,11... | collective-permute-start | bytes 294920 | tf_op jit(solution)/shard_map/ppermute | solution.py:323
  101.2 11.5 %collective-permute-start.23 = (f32[64,256]{1,0:T(8,128)S(1)}, f32[64,256]{1,0:T(8,128)S(1)}, u32[]{:S(2)}, u32[]{:S(2)}) collective-permute-start(f32[64,256]{1,0:T(8,128)S(1)} %slice_add_fusion.2), channel_id=1, source_target_pairs={{0,2},{2,0},{4,6},{6,4},{8,10},{10,8},{12,14},{14,12},{16,18},{18,... | collective-permute-start | bytes 196616 | tf_op jit(solution)/shard_map/ppermute | solution.py:323
  112.7 2.6 %collective-permute-start.24 = (f32[128,256]{1,0:T(8,128)S(1)}, f32[128,256]{1,0:T(8,128)S(1)}, u32[]{:S(2)}, u32[]{:S(2)}) collective-permute-start(f32[128,256]{1,0:T(8,128)S(1)} %pad_maximum_fusion.1), channel_id=1, source_target_pairs={{0,1},{1,0},{2,3},{3,2},{4,5},{5,4},{6,7},{7,6},{8,9},{9,8},{10,11... | collective-permute-start | bytes 393224 | tf_op jit(solution)/shard_map/ppermute | solution.py:323
  (5 other events, 5.4 us)

commit v11 on v10

--- a/solution.py
+++ b/solution.py
@@ -30,13 +30,13 @@
     return lax.dot_general(left, right, dims, precision=EXACT, preferred_element_type=jnp.float32)
 
 
-def kernel_call(body, out_shape, in_specs, flops, bytes_accessed, slots=None):
+def kernel_call(body, out_shape, in_specs, flops, bytes_accessed, slots=None, scratch=()):
     return pl.pallas_call(
         body,
         out_shape=out_shape,
         in_specs=in_specs,
         out_specs=jax.tree.map(lambda _: VMEM, out_shape),
-        scratch_shapes=[] if slots is None else [pltpu.SMEM(slots, jnp.int32)],
+        scratch_shapes=([] if slots is None else [pltpu.SMEM(slots, jnp.int32)]) + list(scratch),
         compiler_params=pltpu.CompilerParams(vmem_limit_bytes=VMEM_LIMIT),
         cost_estimate=pl.CostEstimate(flops=flops, bytes_accessed=bytes_accessed // 16, transcendentals=0),
     )
@@ -45,31 +45,37 @@
 def fill_slots(slots_ref, cols_ref, live_ref, first, place_of):
     rows, stored = cols_ref.shape
     count = slots_ref.shape[1] - 1
-    for row in range(rows):
-        for index in range(count):
+
+    @pl.loop(0, count)
+    def _(index):
+        for row in range(rows):
             slots_ref[row, index] = -1
-        for at in range(stored):
+
+    @pl.loop(0, stored)
+    def _(at):
+        for row in range(rows):
             name = cols_ref[row, at] - first
             inside = (name >= 0) & (name < count) & (at < live_ref[row])
             slots_ref[row, jnp.where(inside, place_of(jnp.clip(name, 0, count - 1)), count)] = at
 
 
-def accumulate(slots_ref, hessian_ref, operand_ref, base, total):
+def accumulate(slots_ref, hessian_ref, operand_ref, base, total_ref):
     rows, _, size, _ = hessian_ref.shape
     shards, shard_rows, _ = operand_ref.shape
     each = shard_rows // size
-    for index in range(shards * each):
-        start = index % each * size
-        block = operand_ref[index // each, start : start + size, :]
-        parts = []
-        for row in range(rows):
-            slot = slots_ref[row, base + index]
-            live = jnp.where(slot >= 0, 1.0, 0.0).astype(jnp.float32)
-            stored = hessian_ref[row, jnp.maximum(slot, 0)]
-            parts.append(stored * jnp.broadcast_to(live, (size, size)).astype(jnp.bfloat16))
-        term = jnp.dot(jnp.concatenate(parts, 0), block, preferred_element_type=jnp.float32)
-        total = term if total is None else total + term
-    return total
+    for shard in range(shards):
+
+        @pl.loop(0, each)
+        def _(at):
+            block = operand_ref[shard, pl.ds(pl.multiple_of(at * size, size), size), :]
+            for row in range(rows):
+                slot = slots_ref[row, base + shard * each + at]
+                live = jnp.where(slot >= 0, 1.0, 0.0).astype(jnp.float32)
+                stored = hessian_ref[row, jnp.maximum(slot, 0)]
+                masked = stored * jnp.broadcast_to(live, (size, size)).astype(jnp.bfloat16)
+                term = jnp.dot(masked, block, preferred_element_type=jnp.float32)
+                place = slice(row * size, (row + 1) * size)
+                total_ref[place, :] += term
 
 
 def hold_body(blocks_ref, out_ref):
@@ -80,18 +86,18 @@
     cols_ref, live_ref, bases_ref, hessian_ref = refs[:4]
     operands, (out_ref, token_ref, slots_ref) = refs[4:-3], refs[-3:]
     fill_slots(slots_ref, cols_ref, live_ref, 0, lambda name: name)
-    total = None
+    out_ref[...] = jnp.zeros_like(out_ref)
     for at, operand_ref in enumerate(operands):
-        total = accumulate(slots_ref, hessian_ref, operand_ref, bases_ref[at], total)
-    out_ref[...] = total
-    token_ref[...] = total[:GROUP, :TILE]
-
-
-def halo_total(first, which, cols_ref, live_ref, lists_ref, bases_ref, hessian_ref, lower_ref, upper_ref, total_ref, slots_ref):
+        accumulate(slots_ref, hessian_ref, operand_ref, bases_ref[at], out_ref)
+    token_ref[...] = out_ref[:GROUP, :TILE]
+
+
+def halo_total(first, which, out_ref, cols_ref, live_ref, lists_ref, bases_ref, hessian_ref, lower_ref, upper_ref, total_ref, slots_ref):
+    out_ref[...] = total_ref[...]
     halo = lists_ref.shape[1]
     fill_slots(slots_ref, cols_ref, live_ref, first, lambda name: list_place(lists_ref, name))
-    total = accumulate(slots_ref, hessian_ref, lower_ref, bases_ref[which], total_ref[...])
-    return accumulate(slots_ref, hessian_ref, upper_ref, halo + bases_ref[which], total)
+    accumulate(slots_ref, hessian_ref, lower_ref, bases_ref[which], out_ref)
+    accumulate(slots_ref, hessian_ref, upper_ref, halo + bases_ref[which], out_ref)
 
 
 def list_place(lists_ref, name):
@@ -102,9 +108,8 @@
 
 def middle_body(first, which, *refs):
     out_ref, token_ref, slots_ref = refs[-3:]
-    total = halo_total(first, which, *refs[:-3], slots_ref)
-    out_ref[...] = total
-    token_ref[...] = total[:GROUP, :TILE]
+    halo_total(first, which, out_ref, *refs[:-3], slots_ref)
+    token_ref[...] = out_ref[:GROUP, :TILE]
 
 
 def interval(bounds_ref):
@@ -114,8 +119,8 @@
 def first_body(first, which, *refs):
     *operands, bounds_ref, vectors_ref, one_ref, cast_ref, slots_ref = refs
     centre, half = interval(bounds_ref)
-    total = halo_total(first, which, *operands, slots_ref)
-    one = (total - centre * vectors_ref[...]) / half
+    halo_total(first, which, one_ref, *operands, slots_ref)
+    one = (one_ref[...] - centre * vectors_ref[...]) / half
     one_ref[...] = one
     cast_ref[...] = one.astype(jnp.bfloat16)
 
@@ -123,8 +128,8 @@
 def second_body(first, which, *refs):
     *operands, bounds_ref, one_ref, vectors_ref, two_ref, cast_ref, slots_ref = refs
     centre, half = interval(bounds_ref)
-    total = halo_total(first, which, *operands, slots_ref)
-    two = 2.0 * (total - centre * one_ref[...]) / half - vectors_ref[...]
+    halo_total(first, which, two_ref, *operands, slots_ref)
+    two = 2.0 * (two_ref[...] - centre * one_ref[...]) / half - vectors_ref[...]
     two_ref[...] = two
     cast_ref[...] = two.astype(jnp.bfloat16)
 
@@ -156,69 +161,76 @@
 
 
 def third_body(first, which, *refs):
-    *operands, number_ref, two_ref, _, out_ref, slots_ref = refs
-    image = halo_total(first, which, *operands, slots_ref)
-    scatter_pieces(number_ref, out_ref, exact_dot(two_ref[...], image, TN))
+    *operands, number_ref, two_ref, _, out_ref, slots_ref, image_ref = refs
+    halo_total(first, which, image_ref, *operands, slots_ref)
+    scatter_pieces(number_ref, out_ref, exact_dot(two_ref[...], image_ref[...], TN))
 
 
 def over_lanes(value, lane):
-    return jnp.broadcast_to(value[:, lane : lane + 1], value.shape)
+    return jnp.take_along_axis(value, jnp.full(value.shape, lane, jnp.int32), axis=1)
 
 
 def over_rows(value, row):
     return jnp.broadcast_to(value[row : row + 1, :], value.shape)
 
 
-def eliminate(tile):
-    count = tile.shape[0] // GROUP
-    rows = [tile[index * GROUP : (index + 1) * GROUP, :] for index in range(count)]
-    sub = lax.broadcasted_iota(jnp.int32, rows[0].shape, 0)
-    lane = lax.broadcasted_iota(jnp.int32, rows[0].shape, 1)
-    for step in range(count):
-        start = step * GROUP
-        pivot_cols = [over_lanes(rows[step], start + col) for col in range(GROUP)]
-        factors = {
-            below: [over_lanes(rows[below], start + col) for col in range(GROUP)]
-            for below in range(step + 1, count)
-        }
-        inside = (lane >= start) & (lane < start + GROUP)
-        forward = jnp.where(inside, jnp.where(lane - start == sub, 1.0, 0.0), rows[step])
-        solved = forward
-        for one in range(0, GROUP, 2):
-            two = one + 1
-            left, right = pivot_cols[one], pivot_cols[two]
-            top, cross, low = over_rows(left, one), over_rows(left, two), over_rows(right, two)
-            inverse = 1.0 / (top * low - cross * cross)
-            top_inverse, cross_inverse, low_inverse = low * inverse, -(cross * inverse), top * inverse
-
-            def solve(value):
-                upper, lower = over_rows(value, one), over_rows(value, two)
-                return top_inverse * upper + cross_inverse * lower, cross_inverse * upper + low_inverse * lower
-
-            def without(value, upper, lower):
-                return value - (left * upper + right * lower)
-
-            def reduced(value):
-                upper, lower = solve(value)
-                return jnp.where(sub == one, upper, jnp.where(sub == two, lower, without(value, upper, lower)))
-
-            for col in range(two + 1, GROUP):
-                pivot_cols[col] = reduced(pivot_cols[col])
-            upper, lower = solve(forward)
-            over_top = 1.0 / top
-            first, second = over_rows(forward, one), over_rows(forward, two)
-            below_first = (second - cross * over_top * first) * lax.rsqrt(low - cross * cross * over_top)
-            below = jnp.where(sub > two, without(forward, upper, lower), forward)
-            solved = reduced(solved)
-            forward = jnp.where(sub == one, first * lax.rsqrt(top), jnp.where(sub == two, below_first, below))
-        rows[step] = jnp.where(lane < start + GROUP, forward, 0.0)
-        solved_rows = [over_rows(solved, pivot) for pivot in range(GROUP)]
-        for below in range(step + 1, count):
-            terms = [factors[below][col] * solved_rows[col] for col in range(GROUP)]
-            while len(terms) > 1:
-                terms = [terms[at] + terms[at + 1] for at in range(0, len(terms), 2)]
-            rows[below] = jnp.where(inside, 0.0, rows[below]) - terms[0]
-    return jnp.concatenate(rows, 0)
+def pivot_rows(block, start):
+    sub = lax.broadcasted_iota(jnp.int32, block.shape, 0)
+    lane = lax.broadcasted_iota(jnp.int32, block.shape, 1)
+    pivot_cols = [over_lanes(block, start + col) for col in range(GROUP)]
+    inside = (lane >= start) & (lane < start + GROUP)
+    forward = jnp.where(inside, jnp.where(lane - start == sub, 1.0, 0.0), block)
+    solved = forward
+    for one in range(0, GROUP, 2):
+        two = one + 1
+        left, right = pivot_cols[one], pivot_cols[two]
+        top, cross, low = over_rows(left, one), over_rows(left, two), over_rows(right, two)
+        inverse = 1.0 / (top * low - cross * cross)
+        top_inverse, cross_inverse, low_inverse = low * inverse, -(cross * inverse), top * inverse
+
+        def solve(value):
+            upper, lower = over_rows(value, one), over_rows(value, two)
+            return top_inverse * upper + cross_inverse * lower, cross_inverse * upper + low_inverse * lower
+
+        def without(value, upper, lower):
+            return value - (left * upper + right * lower)
+
+        def reduced(value):
+            upper, lower = solve(value)
+            return jnp.where(sub == one, upper, jnp.where(sub == two, lower, without(value, upper, lower)))
+
+        for col in range(two + 1, GROUP):
+            pivot_cols[col] = reduced(pivot_cols[col])
+        upper, lower = solve(forward)
+        over_top = 1.0 / top
+        first, second = over_rows(forward, one), over_rows(forward, two)
+        below_first = (second - cross * over_top * first) * lax.rsqrt(low - cross * cross * over_top)
+        below = jnp.where(sub > two, without(forward, upper, lower), forward)
+        solved = reduced(solved)
+        forward = jnp.where(sub == one, first * lax.rsqrt(top), jnp.where(sub == two, below_first, below))
+    return jnp.where(lane < start + GROUP, forward, 0.0), solved
+
+
+def eliminate(tile_ref):
+    count = tile_ref.shape[0] // GROUP
+    cuts = [0, count // 2, count]
+    for begin, end in zip(cuts, cuts[1:]):
+
+        @pl.loop(begin, end)
+        def _(step):
+            start = pl.multiple_of(step * GROUP, GROUP)
+            lane = lax.broadcasted_iota(jnp.int32, (GROUP, tile_ref.shape[1]), 1)
+            inside = (lane >= start) & (lane < start + GROUP)
+            forward, solved = pivot_rows(tile_ref[pl.ds(start, GROUP), :], start)
+            solved_rows = [over_rows(solved, pivot) for pivot in range(GROUP)]
+            for below in range(begin, count):
+                place = slice(below * GROUP, (below + 1) * GROUP)
+                block = tile_ref[place, :]
+                terms = [over_lanes(block, start + col) * solved_rows[col] for col in range(GROUP)]
+                while len(terms) > 1:
+                    terms = [terms[at] + terms[at + 1] for at in range(0, len(terms), 2)]
+                kept = jnp.where(inside, 0.0, block) - terms[0]
+                tile_ref[place, :] = jnp.where(below > step, kept, jnp.where(below == step, forward, block))
 
 
 def scaled_tiles(tiles, count):
@@ -248,7 +260,10 @@
 
 def finish_tile(at, count, tiles, out_refs):
     tiles = dict(tiles)
-    tiles[at, at] = eliminate(tiles[at, at])
+    pivot_ref = out_refs[lower_tiles(count).index((at, at))]
+    pivot_ref[...] = tiles[at, at]
+    eliminate(pivot_ref)
+    tiles[at, at] = pivot_ref[...]
     for row in range(at + 1, count):
         tiles[row, at] = exact_dot(tiles[row, at], tiles[at, at], NT)
     for row in range(at + 1, count):
@@ -461,10 +476,10 @@
         )
         return call(block_cols, live_blocks, bases, held, *own)
 
-    def halo_part(body, outs, which, pair, total, scalars=(), extra=()):
+    def halo_part(body, outs, which, pair, total, scalars=(), extra=(), scratch=()):
         specs = [SMEM] * 4 + [VMEM] * 4 + [SMEM] * len(scalars) + [VMEM] * len(extra)
         body_of = functools.partial(body, region_blocks, which)
-        call = kernel_call(body_of, outs, specs, covering, traffic, halo_slots)
+        call = kernel_call(body_of, outs, specs, covering, traffic, halo_slots, scratch)
         return call(block_cols, live_blocks, lists, bases, held, *pair, total, *scalars, *extra)
 
     def step(body, outs, exchanged, scalars, extra):
@@ -488,7 +503,8 @@
     for which, pair in enumerate(pairs):
         total, after = halo_part(middle_body, (wide, token), which, pair, total)
     gram, after = tied(gram, after)
-    cross = halo_part(third_body, square, len(pairs), last, total, (cross_number,), (two, after))
+    image = pltpu.VMEM((rows, modes), jnp.float32)
+    cross = halo_part(third_body, square, len(pairs), last, total, (cross_number,), (two, after), (image,))
     cross = halving(*cores)(cross)()
 
     fold = modes // TILE

time: 117 us -> 127 us (1.085)
  Pallas kernels: 34.6 us -> 46 us
  starting transfers between devices: 37.2 us -> 35 us
    pallas_call x6, Pallas kernels: 13.4 us -> 19.4 us  [halo_part(): call(block_cols, live_blocks, lists, bases, held, *pair, total, *scalars,...]
    pallas_call x3, Pallas kernels: 5.91 us -> 9.11 us  [near_total(): return call(block_cols, live_blocks, bases, held, *own)]
    ppermute x10, starting transfers between devices: 13.7 us -> 12.1 us  [partner_value(): lax.ppermute(value, axis, [(at, at ^ bit) for at in range(lax.axis_size(a...]
    pallas_call x1, Pallas kernels: 4.43 us -> 5.85 us  [stage(): return tuple(call(*state[:-1])) + state[-1:]]
  transfers between devices with their start and end apart: 25 -> 25, of which waited for: 10 -> 10; matrix products, arithmetic and copies ran while one was open for 3% -> 2% of each run, Pallas kernels for 20% -> 25%
where the time goes in v11:
time: 127 us; the launch traced here: 126 us
  Pallas kernels  46 us (36%)
  starting transfers between devices  35 us (28%)
  waiting for transfers between devices  33.3 us (26%)
  local copies, waits for them, and re-layouts  7.43 us (6%)
  other arithmetic  3.81 us (3%)
    pallas_call x6, Pallas kernels, halo_part(): call(block_cols, live_blocks, lists, bases, held, *pair, total, *scalars,...  19.4 us
    ppermute x6, waiting for transfers between devices, shifted(): return lax.ppermute(value, axis, pairs)  17.7 us
    ppermute x6, starting transfers between devices, shifted(): return lax.ppermute(value, axis, pairs)  16.2 us
    ppermute x10, waiting for transfers between devices, partner_value(): lax.ppermute(value, axis, [(at, at ^ bit) for at in range(lax.axis_size(a...  15.6 us
    ppermute x10, starting transfers between devices, partner_value(): lax.ppermute(value, axis, [(at, at ^ bit) for at in range(lax.axis_size(a...  12.1 us
    pallas_call x3, Pallas kernels, near_total(): return call(block_cols, live_blocks, bases, held, *own)  9.11 us
    ppermute x9, starting transfers between devices, local(): swapped = lambda value: lax.ppermute(value, 'split', [(0, 1), (1, 0)])  6.65 us
    pallas_call x1, Pallas kernels, first(): kernel_call(body, (tile,) * len(names) + (scale,), [SMEM, VMEM], work, gr...  6.62 us
  transfers between devices with their start and end apart: 25, of which 10 were waited for; matrix products, arithmetic and copies ran while one was open for 2% of the time, Pallas kernels for 25%

profile of v11, /device:TPU:1, one launch (start us, length us, event | category | flops | bytes accessed | tf_op | source)
XLA Modules:
  0.0 126.5 jit_solution(6582019218655907054)
XLA Ops:
  3.3 2.0 %collective-permute-start = (bf16[592,256]{1,0:T(8,128)(2,1)}, bf16[592,256]{1,0:T(8,128)(2,1)}, u32[]{:S(2)}, u32[]{:S(2)}) collective-permute-start(bf16[592,256]{1,0:T(8,128)(2,1)} %get-tuple-element.69), channel_id=1, source_target_pairs={{0,2},{2,4},{4,6},{6,8},{8,10},{10,12},{12,14},{14,16},{16,18},{18... | collective-permute-start | bytes 909320 | tf_op jit(solution)/shard_map/ppermute | solution.py:26
  5.3 4.0 %collective-permute-start.1 = (bf16[592,256]{1,0:T(8,128)(2,1)}, bf16[592,256]{1,0:T(8,128)(2,1)}, u32[]{:S(2)}, u32[]{:S(2)}) collective-permute-start(bf16[592,256]{1,0:T(8,128)(2,1)} %get-tuple-element.69), channel_id=1, source_target_pairs={{0,30},{2,0},{4,2},{6,4},{8,6},{10,8},{12,10},{14,12},{16,14},{18,... | collective-permute-start | bytes 909320 | tf_op jit(solution)/shard_map/ppermute | solution.py:26
  10.3 2.0 %copy-done = bf16[3,12,192,192]{3,2,1,0:T(8,128)(2,1)S(1)} copy-done((bf16[3,12,192,192]{3,2,1,0:T(8,128)(2,1)S(1)}, bf16[3,12,192,192]{3,2,1,0:T(8,128)(2,1)}, u32[]{:S(2)}) %copy-start) | copy-done | bytes 2654232
  12.8 5.2 %collective-permute-done = bf16[592,256]{1,0:T(8,128)(2,1)} collective-permute-done((bf16[592,256]{1,0:T(8,128)(2,1)}, bf16[592,256]{1,0:T(8,128)(2,1)}, u32[]{:S(2)}, u32[]{:S(2)}) %collective-permute-start) | collective-permute-done | bytes 303136 | tf_op jit(solution)/shard_map/ppermute | solution.py:26
  20.6 3.3 %shard_map.78 = (f32[576,256]{1,0:T(8,128)S(1)}, f32[8,128]{1,0:T(8,128)}) custom-call(s32[3,12]{1,0:T(4,128)S(1)} %copy-done.7, s32[3]{0:T(128)S(1)} %copy-done.8, s32[2]{0:T(128)S(1)} %pad_add_fusion.refs_2_.refs_3_, bf16[3,12,192,192]{3,2,1,0:T(8,128)(2,1)S(1)} %shard_map.77.refs_3_.refs_4_, bf16[1,592,256]{2,1,0:T(8,128)(2,1)S(1)} %copy-done.4, ...), custom_call_target="tpu_custom_call" | custom-call | flops 10000000 | bytes 276480 | tf_op jit(solution)/shard_map/pallas_call | solution.py:477
  24.0 1.5 %collective-permute-start.2 = (bf16[592,256]{1,0:T(8,128)(2,1)}, bf16[592,256]{1,0:T(8,128)(2,1)S(1)}, u32[]{:S(2)}, u32[]{:S(2)}) collective-permute-start(bf16[592,256]{1,0:T(8,128)(2,1)} %collective-permute-done), channel_id=1, source_target_pairs={{0,1},{1,0},{2,3},{3,2},{4,5},{5,4},{6,7},{7,6},{8,9},{9,8},{10,11... | collective-permute-start | bytes 909320 | tf_op jit(solution)/shard_map/ppermute | solution.py:402
  25.5 3.7 %shard_map.79 = (f32[576,256]{1,0:T(8,128)S(1)}, f32[8,128]{1,0:T(8,128)}) custom-call(s32[3,12]{1,0:T(4,128)S(1)} %copy-done.7, s32[3]{0:T(128)S(1)} %copy-done.8, s32[2,6]{1,0:T(2,128)S(1)} %maximum_convert_fusion.refs_2_, s32[2]{0:T(128)S(1)} %pad_add_fusion.refs_2_.refs_3_, bf16[3,12,192,192]{3,2,1,0:T(8,128)(2,1)S(1)} %shard_map.77.refs_3_.refs_4_, ...), custom_call_target="tpu_custom_call" | custom-call | flops 30000001024 | bytes 276480 | tf_op jit(solution)/shard_map/pallas_call | solution.py:483
  29.2 2.7 %shard_map.80 = (f32[576,256]{1,0:T(8,128)S(1)}, bf16[576,256]{1,0:T(8,128)(2,1)S(1)}) custom-call(s32[3,12]{1,0:T(4,128)S(1)} %copy-done.7, s32[3]{0:T(128)S(1)} %copy-done.8, s32[2,6]{1,0:T(2,128)S(1)} %maximum_convert_fusion.refs_2_, s32[2]{0:T(128)S(1)} %pad_add_fusion.refs_2_.refs_3_, bf16[3,12,192,192]{3,2,1,0:T(8,128)(2,1)S(1)} %shard_map.77.refs_3_.refs_4_, ...), custom_call_target="tpu_custom_call" | custom-call | flops 30000001024 | bytes 276480 | tf_op jit(solution)/shard_map/pallas_call | solution.py:483
  31.9 1.3 %collective-permute-start.5 = (bf16[576,256]{1,0:T(8,128)(2,1)S(1)}, bf16[576,256]{1,0:T(8,128)(2,1)S(1)}, u32[]{:S(2)}, u32[]{:S(2)}) collective-permute-start(bf16[576,256]{1,0:T(8,128)(2,1)S(1)} %get-tuple-element.37), channel_id=1, source_target_pairs={{0,2},{2,4},{4,6},{6,8},{8,10},{10,12},{12,14},{14,16},{16,18},{18... | collective-permute-start | bytes 884744 | tf_op jit(solution)/shard_map/ppermute | solution.py:26
  34.0 3.8 %collective-permute-start.7 = (bf16[576,256]{1,0:T(8,128)(2,1)S(1)}, bf16[576,256]{1,0:T(8,128)(2,1)S(1)}, u32[]{:S(2)}, u32[]{:S(2)}) collective-permute-start(bf16[576,256]{1,0:T(8,128)(2,1)S(1)} %get-tuple-element.37), channel_id=1, source_target_pairs={{0,30},{2,0},{4,2},{6,4},{8,6},{10,8},{12,10},{14,12},{16,14},{18,... | collective-permute-start | bytes 884744 | tf_op jit(solution)/shard_map/ppermute | solution.py:26
  37.8 7.6 %collective-permute-done.5 = bf16[576,256]{1,0:T(8,128)(2,1)S(1)} collective-permute-done((bf16[576,256]{1,0:T(8,128)(2,1)S(1)}, bf16[576,256]{1,0:T(8,128)(2,1)S(1)}, u32[]{:S(2)}, u32[]{:S(2)}) %collective-permute-start.5) | collective-permute-done | bytes 294944 | tf_op jit(solution)/shard_map/ppermute | solution.py:26
  45.4 1.4 %collective-permute-start.6 = (bf16[576,256]{1,0:T(8,128)(2,1)S(1)}, bf16[576,256]{1,0:T(8,128)(2,1)S(1)}, u32[]{:S(2)}, u32[]{:S(2)}) collective-permute-start(bf16[576,256]{1,0:T(8,128)(2,1)S(1)} %collective-permute-done.5), channel_id=1, source_target_pairs={{0,1},{1,0},{2,3},{3,2},{4,5},{5,4},{6,7},{7,6},{8,9},{9,8},{10,11... | collective-permute-start | bytes 884744 | tf_op jit(solution)/shard_map/ppermute | solution.py:402
  46.7 2.9 %shard_map.81 = (f32[576,256]{1,0:T(8,128)S(1)}, f32[8,128]{1,0:T(8,128)}) custom-call(s32[3,12]{1,0:T(4,128)S(1)} %copy-done.7, s32[3]{0:T(128)S(1)} %copy-done.8, s32[2]{0:T(128)S(1)} %pad_add_fusion.refs_2_.refs_3_, bf16[3,12,192,192]{3,2,1,0:T(8,128)(2,1)S(1)} %shard_map.77.refs_3_.refs_4_, bf16[1,576,256]{2,1,0:T(8,128)(2,1)S(1)} %bitcast.25, ...), custom_call_target="tpu_custom_call" | custom-call | flops 10000000 | bytes 276480 | tf_op jit(solution)/shard_map/pallas_call | solution.py:477
  49.6 3.1 %shard_map.82 = (f32[576,256]{1,0:T(8,128)S(1)}, f32[8,128]{1,0:T(8,128)}) custom-call(s32[3,12]{1,0:T(4,128)S(1)} %copy-done.7, s32[3]{0:T(128)S(1)} %copy-done.8, s32[2,6]{1,0:T(2,128)S(1)} %maximum_convert_fusion.refs_2_, s32[2]{0:T(128)S(1)} %pad_add_fusion.refs_2_.refs_3_, bf16[3,12,192,192]{3,2,1,0:T(8,128)(2,1)S(1)} %shard_map.77.refs_3_.refs_4_, ...), custom_call_target="tpu_custom_call" | custom-call | flops 30000001024 | bytes 276480 | tf_op jit(solution)/shard_map/pallas_call | solution.py:483
  52.8 3.4 %shard_map.83 = (f32[576,256]{1,0:T(8,128)S(1)}, bf16[576,256]{1,0:T(8,128)(2,1)}) custom-call(s32[3,12]{1,0:T(4,128)S(1)} %copy-done.7, s32[3]{0:T(128)S(1)} %copy-done.8, s32[2,6]{1,0:T(2,128)S(1)} %maximum_convert_fusion.refs_2_, s32[2]{0:T(128)S(1)} %pad_add_fusion.refs_2_.refs_3_, bf16[3,12,192,192]{3,2,1,0:T(8,128)(2,1)S(1)} %shard_map.77.refs_3_.refs_4_, ...), custom_call_target="tpu_custom_call" | custom-call | flops 30000001024 | bytes 276480 | tf_op jit(solution)/shard_map/pallas_call | solution.py:483
  57.5 2.2 %collective-permute-start.13 = (bf16[576,256]{1,0:T(8,128)(2,1)}, bf16[576,256]{1,0:T(8,128)(2,1)}, u32[]{:S(2)}, u32[]{:S(2)}) collective-permute-start(bf16[576,256]{1,0:T(8,128)(2,1)} %get-tuple-element.42), channel_id=1, source_target_pairs={{0,2},{2,4},{4,6},{6,8},{8,10},{10,12},{12,14},{14,16},{16,18},{18... | collective-permute-start | bytes 884744 | tf_op jit(solution)/shard_map/ppermute | solution.py:26
  59.7 2.9 %collective-permute-start.14 = (bf16[576,256]{1,0:T(8,128)(2,1)}, bf16[576,256]{1,0:T(8,128)(2,1)}, u32[]{:S(2)}, u32[]{:S(2)}) collective-permute-start(bf16[576,256]{1,0:T(8,128)(2,1)} %get-tuple-element.42), channel_id=1, source_target_pairs={{0,30},{2,0},{4,2},{6,4},{8,6},{10,8},{12,10},{14,12},{16,14},{18,... | collective-permute-start | bytes 884744 | tf_op jit(solution)/shard_map/ppermute | solution.py:26
  62.6 2.9 %shard_map.84 = (f32[576,256]{1,0:T(8,128)S(1)}, f32[8,128]{1,0:T(8,128)S(1)}) custom-call(s32[3,12]{1,0:T(4,128)S(1)} %copy-done.7, s32[3]{0:T(128)S(1)} %copy-done.8, s32[2]{0:T(128)S(1)} %pad_add_fusion.refs_2_.refs_3_, bf16[3,12,192,192]{3,2,1,0:T(8,128)(2,1)S(1)} %shard_map.77.refs_3_.refs_4_, bf16[1,576,256]{2,1,0:T(8,128)(2,1)} %bitcast.16.refs_4_, ...), custom_call_target="tpu_custom_call" | custom-call | flops 10000000 | bytes 276480 | tf_op jit(solution)/shard_map/pallas_call | solution.py:477
  69.2 3.6 %collective-permute-done.13 = bf16[576,256]{1,0:T(8,128)(2,1)} collective-permute-done((bf16[576,256]{1,0:T(8,128)(2,1)}, bf16[576,256]{1,0:T(8,128)(2,1)}, u32[]{:S(2)}, u32[]{:S(2)}) %collective-permute-start.13) | collective-permute-done | bytes 294944 | tf_op jit(solution)/shard_map/ppermute | solution.py:26
  75.3 1.6 %collective-permute-start.12 = (f32[96,128]{1,0:T(8,128)S(1)}, f32[96,128]{1,0:T(8,128)S(1)}, u32[]{:S(2)}, u32[]{:S(2)}) collective-permute-start(f32[96,128]{1,0:T(8,128)S(1)} %slice.83), channel_id=1, source_target_pairs={{0,4},{2,6},{4,0},{6,2},{8,12},{10,14},{12,8},{14,10},{16,20},{18,... | collective-permute-start | bytes 147464 | tf_op jit(solution)/shard_map/ppermute | solution.py:338
  77.9 3.1 %shard_map.86 = (f32[576,256]{1,0:T(8,128)S(1)}, f32[8,128]{1,0:T(8,128)S(1)}) custom-call(s32[3,12]{1,0:T(4,128)S(1)} %copy-done.7, s32[3]{0:T(128)S(1)} %copy-done.8, s32[2,6]{1,0:T(2,128)S(1)} %maximum_convert_fusion.refs_2_, s32[2]{0:T(128)S(1)} %pad_add_fusion.refs_2_.refs_3_, bf16[3,12,192,192]{3,2,1,0:T(8,128)(2,1)S(1)} %shard_map.77.refs_3_.refs_4_, ...), custom_call_target="tpu_custom_call" | custom-call | flops 30000001024 | bytes 276480 | tf_op jit(solution)/shard_map/pallas_call | solution.py:483
  81.1 3.4 %shard_map.87 = f32[256,256]{1,0:T(8,128)S(1)} custom-call(s32[3,12]{1,0:T(4,128)S(1)} %copy-done.7, s32[3]{0:T(128)S(1)} %copy-done.8, s32[2,6]{1,0:T(2,128)S(1)} %maximum_convert_fusion.refs_2_, s32[2]{0:T(128)S(1)} %pad_add_fusion.refs_2_.refs_3_, bf16[3,12,192,192]{3,2,1,0:T(8,128)(2,1)S(1)} %shard_map.77.refs_3_.refs_4_, ...), custom_call_target="tpu_custom_call" | custom-call | flops 30000001024 | bytes 276480 | tf_op jit(solution)/shard_map/pallas_call | solution.py:483
  86.2 4.3 %collective-permute-done.18 = f32[112,256]{1,0:T(8,128)S(1)} collective-permute-done((f32[112,256]{1,0:T(8,128)S(1)}, f32[112,256]{1,0:T(8,128)S(1)}, u32[]{:S(2)}, u32[]{:S(2)}) %collective-permute-start.18) | collective-permute-done | bytes 114720 | tf_op jit(solution)/shard_map/ppermute | solution.py:338
  91.6 2.6 %collective-permute-done.19 = f32[112,256]{1,0:T(8,128)S(1)} collective-permute-done((f32[112,256]{1,0:T(8,128)S(1)}, f32[112,256]{1,0:T(8,128)S(1)}, u32[]{:S(2)}, u32[]{:S(2)}) %collective-permute-start.19) | collective-permute-done | bytes 114720 | tf_op jit(solution)/shard_map/ppermute | solution.py:338
  94.3 2.1 %collective-permute-start.20 = (f32[112,256]{1,0:T(8,128)S(1)}, f32[112,256]{1,0:T(8,128)S(1)}, u32[]{:S(2)}, u32[]{:S(2)}) collective-permute-start(f32[112,256]{1,0:T(8,128)S(1)} %add.52), channel_id=1, source_target_pairs={{0,16},{2,18},{4,20},{6,22},{8,24},{10,26},{12,28},{14,30},{16,0},... | collective-permute-start | bytes 344072 | tf_op jit(solution)/shard_map/ppermute | solution.py:338
  96.4 3.7 %collective-permute-done.20 = f32[112,256]{1,0:T(8,128)S(1)} collective-permute-done((f32[112,256]{1,0:T(8,128)S(1)}, f32[112,256]{1,0:T(8,128)S(1)}, u32[]{:S(2)}, u32[]{:S(2)}) %collective-permute-start.20) | collective-permute-done | bytes 114720 | tf_op jit(solution)/shard_map/ppermute | solution.py:338
  100.8 3.0 %collective-permute-done.21 = f32[112,256]{1,0:T(8,128)S(1)} collective-permute-done((f32[112,256]{1,0:T(8,128)S(1)}, f32[112,256]{1,0:T(8,128)S(1)}, u32[]{:S(2)}, u32[]{:S(2)}) %collective-permute-start.21) | collective-permute-done | bytes 114720 | tf_op jit(solution)/shard_map/ppermute | solution.py:338
  103.9 4.6 %collective-permute-start.22 = (f32[192,128]{1,0:T(8,128)S(1)}, f32[192,128]{1,0:T(8,128)S(1)}, u32[]{:S(2)}, u32[]{:S(2)}) collective-permute-start(f32[192,128]{1,0:T(8,128)S(1)} %pad_maximum_fusion.3), channel_id=1, source_target_pairs={{0,1},{1,0},{2,3},{3,2},{4,5},{5,4},{6,7},{7,6},{8,9},{9,8},{10,11... | collective-permute-start | bytes 294920 | tf_op jit(solution)/shard_map/ppermute | solution.py:338
  109.6 6.6 %shard_map.88 = (f32[128,128]{1,0:T(8,128)S(1)}, f32[128,128]{1,0:T(8,128)S(1)}, f32[128,128]{1,0:T(8,128)S(1)}, f32[16,128]{1,0:T(8,128)S(1)}) custom-call(s32[1]{0:T(128)} %bitcast.number_ref, f32[384,128]{1,0:T(8,128)S(1)} %constant_dynamic-update-slice_fusion.gram_ref), custom_call_target="tpu_custom_call" | custom-call | flops 100000000 | bytes 3072 | tf_op jit(solution)/shard_map/pallas_call | solution.py:315
  116.2 5.8 %shard_map.89 = (f32[128,128]{1,0:T(8,128)S(1)}, f32[128,128]{1,0:T(8,128)S(1)}, f32[128,128]{1,0:T(8,128)S(1)}) custom-call(f32[128,128]{1,0:T(8,128)S(1)} %get-tuple-element.51.refs_0_, f32[128,128]{1,0:T(8,128)S(1)} %get-tuple-element.52.refs_1_, f32[128,128]{1,0:T(8,128)S(1)} %get-tuple-element.53.refs_2_), custom_call_target="tpu_custom_call" | custom-call | flops 100000000 | bytes 1024 | tf_op jit(solution)/shard_map/pallas_call | solution.py:321
  122.8 1.9 %shard_map.90 = (f32[576,256]{1,0:T(8,128)}, f32[256,256]{1,0:T(8,128)S(1)}) custom-call(f32[128,128]{1,0:T(8,128)S(1)} %get-tuple-element.59.refs_0_, f32[128,128]{1,0:T(8,128)S(1)} %get-tuple-element.60.refs_1_, f32[128,128]{1,0:T(8,128)S(1)} %get-tuple-element.61.refs_2_, f32[16,128]{1,0:T(8,128)S(1)} %get-tuple-element.62.refs_3_, f32[576,256]{1,0:T(8,128)S(1)} %copy-done.3), custom_call_target="tpu_custom_call" | custom-call | flops 100000000 | bytes 9216 | tf_op jit(solution)/shard_map/pallas_call | solution.py:328
  124.7 1.7 %shard_map.91 = f32[256,256]{1,0:T(8,128)} custom-call(s32[1]{0:T(128)} %bitcast.22.refs_8_.number_ref, f32[256,256]{1,0:T(8,128)S(1)} %pad_maximum_fusion.cross_ref, f32[256,256]{1,0:T(8,128)S(1)} %get-tuple-element.67.inverse_ref), custom_call_target="tpu_custom_call" | custom-call | flops 150994944 | bytes 276480 | tf_op jit(solution)/shard_map/pallas_call | solution.py:527
  (85 shorter events, 21.5 us)
Async XLA Ops:
  3.3 14.7 %collective-permute-start = (bf16[592,256]{1,0:T(8,128)(2,1)}, bf16[592,256]{1,0:T(8,128)(2,1)}, u32[]{:S(2)}, u32[]{:S(2)}) collective-permute-start(bf16[592,256]{1,0:T(8,128)(2,1)} %get-tuple-element.69), channel_id=1, source_target_pairs={{0,2},{2,4},{4,6},{6,8},{8,10},{10,12},{12,14},{14,16},{16,18},{18... | collective-permute-start | bytes 909320 | tf_op jit(solution)/shard_map/ppermute | solution.py:26
  5.3 14.6 %collective-permute-start.1 = (bf16[592,256]{1,0:T(8,128)(2,1)}, bf16[592,256]{1,0:T(8,128)(2,1)}, u32[]{:S(2)}, u32[]{:S(2)}) collective-permute-start(bf16[592,256]{1,0:T(8,128)(2,1)} %get-tuple-element.69), channel_id=1, source_target_pairs={{0,30},{2,0},{4,2},{6,4},{8,6},{10,8},{12,10},{14,12},{16,14},{18,... | collective-permute-start | bytes 909320 | tf_op jit(solution)/shard_map/ppermute | solution.py:26
  9.3 11.3 %collective-permute-start.4 = (bf16[592,256]{1,0:T(8,128)(2,1)}, bf16[592,256]{1,0:T(8,128)(2,1)}, u32[]{:S(2)}, u32[]{:S(2)}) collective-permute-start(bf16[592,256]{1,0:T(8,128)(2,1)} %get-tuple-element.69), channel_id=1, source_target_pairs={{0,1},{1,0},{2,3},{3,2},{4,5},{5,4},{6,7},{7,6},{8,9},{9,8},{10,11... | collective-permute-start | bytes 909320 | tf_op jit(solution)/shard_map/ppermute | solution.py:402
  12.3 8.3 %copy-start.4 = (bf16[1,592,256]{2,1,0:T(8,128)(2,1)S(1)}, bf16[1,592,256]{2,1,0:T(8,128)(2,1)}, u32[]{:S(2)}) copy-start(bf16[1,592,256]{2,1,0:T(8,128)(2,1)} %get-tuple-element.68.refs_4_) | copy-start | bytes 909316
  12.3 8.4 %copy-start.7 = (s32[3,12]{1,0:T(4,128)S(1)}, s32[3,12]{1,0:T(4,128)}, u32[]{:S(2)}) copy-start(s32[3,12]{1,0:T(4,128)} %refs_0_.17) | copy-start | bytes 436
  12.3 8.4 %copy-start.8 = (s32[3]{0:T(128)S(1)}, s32[3]{0:T(128)}, u32[]{:S(2)}) copy-start(s32[3]{0:T(128)} %refs_1_.17) | copy-start | bytes 40
  24.0 5.2 %collective-permute-start.2 = (bf16[592,256]{1,0:T(8,128)(2,1)}, bf16[592,256]{1,0:T(8,128)(2,1)S(1)}, u32[]{:S(2)}, u32[]{:S(2)}) collective-permute-start(bf16[592,256]{1,0:T(8,128)(2,1)} %collective-permute-done), channel_id=1, source_target_pairs={{0,1},{1,0},{2,3},{3,2},{4,5},{5,4},{6,7},{7,6},{8,9},{9,8},{10,11... | collective-permute-start | bytes 909320 | tf_op jit(solution)/shard_map/ppermute | solution.py:402
  25.5 3.7 %collective-permute-start.3 = (bf16[592,256]{1,0:T(8,128)(2,1)}, bf16[592,256]{1,0:T(8,128)(2,1)S(1)}, u32[]{:S(2)}, u32[]{:S(2)}) collective-permute-start(bf16[592,256]{1,0:T(8,128)(2,1)} %collective-permute-done.1), channel_id=1, source_target_pairs={{0,1},{1,0},{2,3},{3,2},{4,5},{5,4},{6,7},{7,6},{8,9},{9,8},{10,11... | collective-permute-start | bytes 909320 | tf_op jit(solution)/shard_map/ppermute | solution.py:402
  25.5 3.7 %copy-start.6 = (f32[576,256]{1,0:T(8,128)S(1)}, f32[576,256]{1,0:T(8,128)}, u32[]{:S(2)}) copy-start(f32[576,256]{1,0:T(8,128)} %refs_10_.1) | copy-start | bytes 1769476
  25.5 3.7 %copy-start.11 = (f32[2]{0:T(128)S(1)}, f32[2]{0:T(128)}, u32[]{:S(2)}) copy-start(f32[2]{0:T(128)} %refs_8_.3) | copy-start | bytes 28
  31.9 13.5 %collective-permute-start.5 = (bf16[576,256]{1,0:T(8,128)(2,1)S(1)}, bf16[576,256]{1,0:T(8,128)(2,1)S(1)}, u32[]{:S(2)}, u32[]{:S(2)}) collective-permute-start(bf16[576,256]{1,0:T(8,128)(2,1)S(1)} %get-tuple-element.37), channel_id=1, source_target_pairs={{0,2},{2,4},{4,6},{6,8},{8,10},{10,12},{12,14},{14,16},{16,18},{18... | collective-permute-start | bytes 884744 | tf_op jit(solution)/shard_map/ppermute | solution.py:26
  33.2 13.5 %collective-permute-start.9 = (bf16[576,256]{1,0:T(8,128)(2,1)S(1)}, bf16[576,256]{1,0:T(8,128)(2,1)S(1)}, u32[]{:S(2)}, u32[]{:S(2)}) collective-permute-start(bf16[576,256]{1,0:T(8,128)(2,1)S(1)} %get-tuple-element.37), channel_id=1, source_target_pairs={{0,1},{1,0},{2,3},{3,2},{4,5},{5,4},{6,7},{7,6},{8,9},{9,8},{10,11... | collective-permute-start | bytes 884744 | tf_op jit(solution)/shard_map/ppermute | solution.py:402
  34.0 15.7 %collective-permute-start.7 = (bf16[576,256]{1,0:T(8,128)(2,1)S(1)}, bf16[576,256]{1,0:T(8,128)(2,1)S(1)}, u32[]{:S(2)}, u32[]{:S(2)}) collective-permute-start(bf16[576,256]{1,0:T(8,128)(2,1)S(1)} %get-tuple-element.37), channel_id=1, source_target_pairs={{0,30},{2,0},{4,2},{6,4},{8,6},{10,8},{12,10},{14,12},{16,14},{18,... | collective-permute-start | bytes 884744 | tf_op jit(solution)/shard_map/ppermute | solution.py:26
  45.4 7.4 %collective-permute-start.6 = (bf16[576,256]{1,0:T(8,128)(2,1)S(1)}, bf16[576,256]{1,0:T(8,128)(2,1)S(1)}, u32[]{:S(2)}, u32[]{:S(2)}) collective-permute-start(bf16[576,256]{1,0:T(8,128)(2,1)S(1)} %collective-permute-done.5), channel_id=1, source_target_pairs={{0,1},{1,0},{2,3},{3,2},{4,5},{5,4},{6,7},{7,6},{8,9},{9,8},{10,11... | collective-permute-start | bytes 884744 | tf_op jit(solution)/shard_map/ppermute | solution.py:402
  49.6 3.1 %collective-permute-start.8 = (bf16[576,256]{1,0:T(8,128)(2,1)S(1)}, bf16[576,256]{1,0:T(8,128)(2,1)S(1)}, u32[]{:S(2)}, u32[]{:S(2)}) collective-permute-start(bf16[576,256]{1,0:T(8,128)(2,1)S(1)} %collective-permute-done.7), channel_id=1, source_target_pairs={{0,1},{1,0},{2,3},{3,2},{4,5},{5,4},{6,7},{7,6},{8,9},{9,8},{10,11... | collective-permute-start | bytes 884744 | tf_op jit(solution)/shard_map/ppermute | solution.py:402
  57.0 5.6 %collective-permute-start.10 = (bf16[576,256]{1,0:T(8,128)(2,1)}, bf16[576,256]{1,0:T(8,128)(2,1)}, u32[]{:S(2)}, u32[]{:S(2)}) collective-permute-start(bf16[576,256]{1,0:T(8,128)(2,1)} %get-tuple-element.42), channel_id=1, source_target_pairs={{0,1},{1,0},{2,3},{3,2},{4,5},{5,4},{6,7},{7,6},{8,9},{9,8},{10,11... | collective-permute-start | bytes 884744 | tf_op jit(solution)/shard_map/ppermute | solution.py:402
  57.5 15.3 %collective-permute-start.13 = (bf16[576,256]{1,0:T(8,128)(2,1)}, bf16[576,256]{1,0:T(8,128)(2,1)}, u32[]{:S(2)}, u32[]{:S(2)}) collective-permute-start(bf16[576,256]{1,0:T(8,128)(2,1)} %get-tuple-element.42), channel_id=1, source_target_pairs={{0,2},{2,4},{4,6},{6,8},{8,10},{10,12},{12,14},{14,16},{16,18},{18... | collective-permute-start | bytes 884744 | tf_op jit(solution)/shard_map/ppermute | solution.py:26
  59.7 13.9 %collective-permute-start.14 = (bf16[576,256]{1,0:T(8,128)(2,1)}, bf16[576,256]{1,0:T(8,128)(2,1)}, u32[]{:S(2)}, u32[]{:S(2)}) collective-permute-start(bf16[576,256]{1,0:T(8,128)(2,1)} %get-tuple-element.42), channel_id=1, source_target_pairs={{0,30},{2,0},{4,2},{6,4},{8,6},{10,8},{12,10},{14,12},{16,14},{18,... | collective-permute-start | bytes 884744 | tf_op jit(solution)/shard_map/ppermute | solution.py:26
  62.6 3.7 %copy-start.2 = (f32[576,256]{1,0:T(8,128)S(1)}, f32[576,256]{1,0:T(8,128)}, u32[]{:S(2)}) copy-start(f32[576,256]{1,0:T(8,128)} %copy-done.1) | copy-start | bytes 1769476
  68.6 5.7 %collective-permute-start.11 = (f32[192,128]{1,0:T(8,128)}, f32[192,128]{1,0:T(8,128)}, u32[]{:S(2)}, u32[]{:S(2)}) collective-permute-start(f32[192,128]{1,0:T(8,128)} %slice.81), channel_id=1, source_target_pairs={{0,1},{1,0},{2,3},{3,2},{4,5},{5,4},{6,7},{7,6},{8,9},{9,8},{10,11... | collective-permute-start | bytes 294920 | tf_op jit(solution)/shard_map/ppermute | solution.py:338
  72.8 8.2 %collective-permute-start.15 = (bf16[576,256]{1,0:T(8,128)(2,1)}, bf16[576,256]{1,0:T(8,128)(2,1)S(1)}, u32[]{:S(2)}, u32[]{:S(2)}) collective-permute-start(bf16[576,256]{1,0:T(8,128)(2,1)} %collective-permute-done.13), channel_id=1, source_target_pairs={{0,1},{1,0},{2,3},{3,2},{4,5},{5,4},{6,7},{7,6},{8,9},{9,8},{10,11... | collective-permute-start | bytes 884744 | tf_op jit(solution)/shard_map/ppermute | solution.py:402
  73.6 7.5 %collective-permute-start.16 = (bf16[576,256]{1,0:T(8,128)(2,1)}, bf16[576,256]{1,0:T(8,128)(2,1)S(1)}, u32[]{:S(2)}, u32[]{:S(2)}) collective-permute-start(bf16[576,256]{1,0:T(8,128)(2,1)} %collective-permute-done.14), channel_id=1, source_target_pairs={{0,1},{1,0},{2,3},{3,2},{4,5},{5,4},{6,7},{7,6},{8,9},{9,8},{10,11... | collective-permute-start | bytes 884744 | tf_op jit(solution)/shard_map/ppermute | solution.py:402
  75.3 5.7 %collective-permute-start.12 = (f32[96,128]{1,0:T(8,128)S(1)}, f32[96,128]{1,0:T(8,128)S(1)}, u32[]{:S(2)}, u32[]{:S(2)}) collective-permute-start(f32[96,128]{1,0:T(8,128)S(1)} %slice.83), channel_id=1, source_target_pairs={{0,4},{2,6},{4,0},{6,2},{8,12},{10,14},{12,8},{14,10},{16,20},{18,... | collective-permute-start | bytes 147464 | tf_op jit(solution)/shard_map/ppermute | solution.py:338
  77.9 3.1 %copy-start.3 = (f32[576,256]{1,0:T(8,128)S(1)}, f32[576,256]{1,0:T(8,128)}, u32[]{:S(2)}) copy-start(f32[576,256]{1,0:T(8,128)} %copy-done.1) | copy-start | bytes 1769476
  84.5 1.4 %collective-permute-start.17 = (f32[128,256]{1,0:T(8,128)S(1)}, f32[128,256]{1,0:T(8,128)S(1)}, u32[]{:S(2)}, u32[]{:S(2)}) collective-permute-start(f32[128,256]{1,0:T(8,128)S(1)} %slice.85), channel_id=1, source_target_pairs={{0,1},{1,0},{2,3},{3,2},{4,5},{5,4},{6,7},{7,6},{8,9},{9,8},{10,11... | collective-permute-start | bytes 393224 | tf_op jit(solution)/shard_map/ppermute | solution.py:338
  86.0 4.5 %collective-permute-start.18 = (f32[112,256]{1,0:T(8,128)S(1)}, f32[112,256]{1,0:T(8,128)S(1)}, u32[]{:S(2)}, u32[]{:S(2)}) collective-permute-start(f32[112,256]{1,0:T(8,128)S(1)} %fusion.2), channel_id=1, source_target_pairs={{0,2},{2,0},{4,6},{6,4},{8,10},{10,8},{12,14},{14,12},{16,18},{18,... | collective-permute-start | bytes 344072 | tf_op jit(solution)/shard_map/ppermute | solution.py:338
  90.5 3.7 %collective-permute-start.19 = (f32[112,256]{1,0:T(8,128)S(1)}, f32[112,256]{1,0:T(8,128)S(1)}, u32[]{:S(2)}, u32[]{:S(2)}) collective-permute-start(f32[112,256]{1,0:T(8,128)S(1)} %maximum_add_fusion), channel_id=1, source_target_pairs={{0,8},{2,10},{4,12},{6,14},{8,0},{10,2},{12,4},{14,6},{16,24},{18,... | collective-permute-start | bytes 344072 | tf_op jit(solution)/shard_map/ppermute | solution.py:338
  94.3 5.8 %collective-permute-start.20 = (f32[112,256]{1,0:T(8,128)S(1)}, f32[112,256]{1,0:T(8,128)S(1)}, u32[]{:S(2)}, u32[]{:S(2)}) collective-permute-start(f32[112,256]{1,0:T(8,128)S(1)} %add.52), channel_id=1, source_target_pairs={{0,16},{2,18},{4,20},{6,22},{8,24},{10,26},{12,28},{14,30},{16,0},... | collective-permute-start | bytes 344072 | tf_op jit(solution)/shard_map/ppermute | solution.py:338
  100.1 3.7 %collective-permute-start.21 = (f32[112,256]{1,0:T(8,128)S(1)}, f32[112,256]{1,0:T(8,128)S(1)}, u32[]{:S(2)}, u32[]{:S(2)}) collective-permute-start(f32[112,256]{1,0:T(8,128)S(1)} %add.53), channel_id=1, source_target_pairs={{0,4},{2,6},{4,0},{6,2},{8,12},{10,14},{12,8},{14,10},{16,20},{18,... | collective-permute-start | bytes 344072 | tf_op jit(solution)/shard_map/ppermute | solution.py:338
  103.9 5.6 %collective-permute-start.22 = (f32[192,128]{1,0:T(8,128)S(1)}, f32[192,128]{1,0:T(8,128)S(1)}, u32[]{:S(2)}, u32[]{:S(2)}) collective-permute-start(f32[192,128]{1,0:T(8,128)S(1)} %pad_maximum_fusion.3), channel_id=1, source_target_pairs={{0,1},{1,0},{2,3},{3,2},{4,5},{5,4},{6,7},{7,6},{8,9},{9,8},{10,11... | collective-permute-start | bytes 294920 | tf_op jit(solution)/shard_map/ppermute | solution.py:338
  109.4 12.7 %collective-permute-start.23 = (f32[64,256]{1,0:T(8,128)S(1)}, f32[64,256]{1,0:T(8,128)S(1)}, u32[]{:S(2)}, u32[]{:S(2)}) collective-permute-start(f32[64,256]{1,0:T(8,128)S(1)} %slice_add_fusion.2), channel_id=1, source_target_pairs={{0,2},{2,0},{4,6},{6,4},{8,10},{10,8},{12,14},{14,12},{16,18},{18,... | collective-permute-start | bytes 196616 | tf_op jit(solution)/shard_map/ppermute | solution.py:338
  122.1 2.6 %collective-permute-start.24 = (f32[128,256]{1,0:T(8,128)S(1)}, f32[128,256]{1,0:T(8,128)S(1)}, u32[]{:S(2)}, u32[]{:S(2)}) collective-permute-start(f32[128,256]{1,0:T(8,128)S(1)} %pad_maximum_fusion.1), channel_id=1, source_target_pairs={{0,1},{1,0},{2,3},{3,2},{4,5},{5,4},{6,7},{7,6},{8,9},{9,8},{10,11... | collective-permute-start | bytes 393224 | tf_op jit(solution)/shard_map/ppermute | solution.py:338
  (5 other events, 5.4 us)

commit v12 on v10

--- a/solution.py
+++ b/solution.py
@@ -14,6 +14,7 @@
 NT = (((1,), (1,)), ((), ()))
 TN = (((0,), (0,)), ((), ()))
 GROUP = 8
+PIVOTS = 16
 TILE = 128
 VMEM_LIMIT = 12 * 1024 * 1024
 LIST_ROWS = 16
@@ -35,7 +36,7 @@
         body,
         out_shape=out_shape,
         in_specs=in_specs,
-        out_specs=jax.tree.map(lambda _: VMEM, out_shape),
+        out_specs=jax.tree.map(lambda out: SMEM if out.dtype == jnp.int32 else VMEM, out_shape),
         scratch_shapes=[] if slots is None else [pltpu.SMEM(slots, jnp.int32)],
         compiler_params=pltpu.CompilerParams(vmem_limit_bytes=VMEM_LIMIT),
         cost_estimate=pl.CostEstimate(flops=flops, bytes_accessed=bytes_accessed // 16, transcendentals=0),
@@ -76,22 +77,13 @@
     pltpu.sync_copy(blocks_ref, out_ref)
 
 
-def near_body(count, *refs):
-    cols_ref, live_ref, bases_ref, hessian_ref = refs[:4]
-    operands, (out_ref, token_ref, slots_ref) = refs[4:-3], refs[-3:]
+def near_body(count, tokens, *refs):
+    cols_ref, live_ref, bases_ref, hessian_ref, region_ref, out_ref, *token_refs, slots_ref = refs
     fill_slots(slots_ref, cols_ref, live_ref, 0, lambda name: name)
-    total = None
-    for at, operand_ref in enumerate(operands):
-        total = accumulate(slots_ref, hessian_ref, operand_ref, bases_ref[at], total)
+    total = accumulate(slots_ref, hessian_ref, region_ref, 0, None)
     out_ref[...] = total
-    token_ref[...] = total[:GROUP, :TILE]
-
-
-def halo_total(first, which, cols_ref, live_ref, lists_ref, bases_ref, hessian_ref, lower_ref, upper_ref, total_ref, slots_ref):
-    halo = lists_ref.shape[1]
-    fill_slots(slots_ref, cols_ref, live_ref, first, lambda name: list_place(lists_ref, name))
-    total = accumulate(slots_ref, hessian_ref, lower_ref, bases_ref[which], total_ref[...])
-    return accumulate(slots_ref, hessian_ref, upper_ref, halo + bases_ref[which], total)
+    for token_ref in token_refs:
+        token_ref[...] = total[:GROUP, :TILE]
 
 
 def list_place(lists_ref, name):
@@ -100,30 +92,43 @@
     return side * halo + lists_ref[side, name - side * halo]
 
 
-def middle_body(first, which, *refs):
-    out_ref, token_ref, slots_ref = refs[-3:]
-    total = halo_total(first, which, *refs[:-3], slots_ref)
+def halo_total(which, slots_ref, bases_ref, hessian_ref, lower_ref, upper_ref, total_ref):
+    halo = (slots_ref.shape[1] - 1) // 2
+    total = accumulate(slots_ref, hessian_ref, lower_ref, bases_ref[which], total_ref[...])
+    return accumulate(slots_ref, hessian_ref, upper_ref, halo + bases_ref[which], total)
+
+
+def table_body(first, which, cols_ref, live_ref, lists_ref, *refs):
+    *operands, out_ref, slots_ref = refs
+    fill_slots(slots_ref, cols_ref, live_ref, first, lambda name: list_place(lists_ref, name))
+    out_ref[...] = halo_total(which, slots_ref, *operands)
+
+
+def middle_body(which, *refs):
+    operands, (out_ref, *token_refs) = refs[:6], refs[6:]
+    total = halo_total(which, *operands)
     out_ref[...] = total
-    token_ref[...] = total[:GROUP, :TILE]
+    for token_ref in token_refs:
+        token_ref[...] = total[:GROUP, :TILE]
 
 
 def interval(bounds_ref):
     return 0.5 * (bounds_ref[0] + bounds_ref[1]), 0.5 * (bounds_ref[1] - bounds_ref[0])
 
 
-def first_body(first, which, *refs):
-    *operands, bounds_ref, vectors_ref, one_ref, cast_ref, slots_ref = refs
+def first_body(which, *refs):
+    *operands, bounds_ref, vectors_ref, one_ref, cast_ref = refs
     centre, half = interval(bounds_ref)
-    total = halo_total(first, which, *operands, slots_ref)
+    total = halo_total(which, *operands)
     one = (total - centre * vectors_ref[...]) / half
     one_ref[...] = one
     cast_ref[...] = one.astype(jnp.bfloat16)
 
 
-def second_body(first, which, *refs):
-    *operands, bounds_ref, one_ref, vectors_ref, two_ref, cast_ref, slots_ref = refs
+def second_body(which, *refs):
+    *operands, bounds_ref, one_ref, vectors_ref, two_ref, cast_ref = refs
     centre, half = interval(bounds_ref)
-    total = halo_total(first, which, *operands, slots_ref)
+    total = halo_total(which, *operands)
     two = 2.0 * (total - centre * one_ref[...]) / half - vectors_ref[...]
     two_ref[...] = two
     cast_ref[...] = two.astype(jnp.bfloat16)
@@ -155,9 +160,9 @@
     scatter_pieces(number_ref, out_ref, jnp.concatenate(tiles, 0))
 
 
-def third_body(first, which, *refs):
-    *operands, number_ref, two_ref, _, out_ref, slots_ref = refs
-    image = halo_total(first, which, *operands, slots_ref)
+def third_body(which, *refs):
+    *operands, number_ref, two_ref, _, out_ref = refs
+    image = halo_total(which, *operands)
     scatter_pieces(number_ref, out_ref, exact_dot(two_ref[...], image, TN))
 
 
@@ -170,21 +175,21 @@
 
 
 def eliminate(tile):
-    count = tile.shape[0] // GROUP
-    rows = [tile[index * GROUP : (index + 1) * GROUP, :] for index in range(count)]
+    count = tile.shape[0] // PIVOTS
+    rows = [tile[index * PIVOTS : (index + 1) * PIVOTS, :] for index in range(count)]
     sub = lax.broadcasted_iota(jnp.int32, rows[0].shape, 0)
     lane = lax.broadcasted_iota(jnp.int32, rows[0].shape, 1)
     for step in range(count):
-        start = step * GROUP
-        pivot_cols = [over_lanes(rows[step], start + col) for col in range(GROUP)]
+        start = step * PIVOTS
+        pivot_cols = [over_lanes(rows[step], start + col) for col in range(PIVOTS)]
         factors = {
-            below: [over_lanes(rows[below], start + col) for col in range(GROUP)]
+            below: [over_lanes(rows[below], start + col) for col in range(PIVOTS)]
             for below in range(step + 1, count)
         }
-        inside = (lane >= start) & (lane < start + GROUP)
+        inside = (lane >= start) & (lane < start + PIVOTS)
         forward = jnp.where(inside, jnp.where(lane - start == sub, 1.0, 0.0), rows[step])
         solved = forward
-        for one in range(0, GROUP, 2):
+        for one in range(0, PIVOTS, 2):
             two = one + 1
             left, right = pivot_cols[one], pivot_cols[two]
             top, cross, low = over_rows(left, one), over_rows(left, two), over_rows(right, two)
@@ -202,7 +207,7 @@
                 upper, lower = solve(value)
                 return jnp.where(sub == one, upper, jnp.where(sub == two, lower, without(value, upper, lower)))
 
-            for col in range(two + 1, GROUP):
+            for col in range(two + 1, PIVOTS):
                 pivot_cols[col] = reduced(pivot_cols[col])
             upper, lower = solve(forward)
             over_top = 1.0 / top
@@ -211,10 +216,10 @@
             below = jnp.where(sub > two, without(forward, upper, lower), forward)
             solved = reduced(solved)
             forward = jnp.where(sub == one, first * lax.rsqrt(top), jnp.where(sub == two, below_first, below))
-        rows[step] = jnp.where(lane < start + GROUP, forward, 0.0)
-        solved_rows = [over_rows(solved, pivot) for pivot in range(GROUP)]
+        rows[step] = jnp.where(lane < start + PIVOTS, forward, 0.0)
+        solved_rows = [over_rows(solved, pivot) for pivot in range(PIVOTS)]
         for below in range(step + 1, count):
-            terms = [factors[below][col] * solved_rows[col] for col in range(GROUP)]
+            terms = [factors[below][col] * solved_rows[col] for col in range(PIVOTS)]
             while len(terms) > 1:
                 terms = [terms[at] + terms[at + 1] for at in range(0, len(terms), 2)]
             rows[below] = jnp.where(inside, 0.0, rows[below]) - terms[0]
@@ -385,8 +390,8 @@
     paired = whole and splits == 2
     core = lax.axis_index("split").astype(jnp.int32)
     swapped = lambda value: lax.ppermute(value, "split", [(0, 1), (1, 0)])
-    near_first = [core * row_blocks, (1 - core) * row_blocks] if paired else [0]
-    bases = jnp.stack(near_first).astype(jnp.int32) if paired else jnp.zeros((1,), jnp.int32)
+    halo_first = [core * row_blocks, (1 - core) * row_blocks] if paired else [0]
+    bases = jnp.stack(halo_first).astype(jnp.int32) if paired else jnp.zeros((1,), jnp.int32)
 
     def sent(operand, region):
         if whole:
@@ -409,17 +414,12 @@
     if whole:
         first = jnp.concatenate([first, listed.astype(jnp.bfloat16)], 0)
 
-    def near_parts(operand):
-        if paired:
-            return [operand[None], swapped(operand)[None]]
-        return [lax.all_gather(operand, "split", axis=0)]
-
     def exchange(operand):
-        near = near_parts(operand)
-        up, down = sent(operand, near[0])
-        return near, shifted(up, "region", 1), shifted(down, "region", -1)
-
-    first_near, first_lower, first_upper = exchange(first)
+        region = lax.all_gather(operand, "split", axis=0)
+        up, down = sent(operand, region)
+        return region, shifted(up, "region", 1), shifted(down, "region", -1)
+
+    first_region, first_lower, first_upper = exchange(first)
     if whole:
         orders = [first_lower[rows + 1, :halo_blocks], first_upper[rows, :halo_blocks]]
         lists = jnp.stack(orders).astype(jnp.int32)
@@ -450,61 +450,75 @@
         compiler_params=pltpu.CompilerParams(vmem_limit_bytes=VMEM_LIMIT),
     )(hessian)
 
-    def near_total(own):
+    def near_total(region, tokens=()):
         call = kernel_call(
-            functools.partial(near_body, region_blocks),
-            (wide, token),
-            [SMEM] * 3 + [VMEM] * (1 + len(own)),
+            functools.partial(near_body, region_blocks, len(tokens)),
+            (wide,) + tokens,
+            [SMEM] * 3 + [VMEM] * 2,
             free,
             traffic,
             (row_blocks, region_blocks + 1),
         )
-        return call(block_cols, live_blocks, bases, held, *own)
-
-    def halo_part(body, outs, which, pair, total, scalars=(), extra=()):
-        specs = [SMEM] * 4 + [VMEM] * 4 + [SMEM] * len(scalars) + [VMEM] * len(extra)
-        body_of = functools.partial(body, region_blocks, which)
-        call = kernel_call(body_of, outs, specs, covering, traffic, halo_slots)
-        return call(block_cols, live_blocks, lists, bases, held, *pair, total, *scalars, *extra)
-
-    def step(body, outs, exchanged, scalars, extra):
-        own, lower, upper = exchanged
-        total, _ = near_total(own)
+        return call(block_cols, live_blocks, bases, held, region)
+
+    def halo_part(body, outs, table, pair, total, scalars=(), extra=()):
+        specs = [SMEM] * 2 + [VMEM] * 4 + [SMEM] * len(scalars) + [VMEM] * len(extra)
+        call = kernel_call(body, outs, specs, covering, traffic)
+        return call(table, bases, held, *pair, total, *scalars, *extra)
+
+    def pairs_of(lower, upper):
         *pairs, last = zip(gathered(lower), gathered(upper))
-        for which, pair in enumerate(pairs):
-            total, _ = halo_part(middle_body, (wide, token), which, pair, total)
-        return halo_part(body, outs, len(pairs), last, total, scalars, extra)
-
-    one, one_cast = step(first_body, (wide, narrow), (first_near, first_lower, first_upper), (bounds,), (vectors,))
-    two, two_cast = step(second_body, (wide, narrow), exchange(one_cast), (bounds,), (one, vectors))
-
-    own, lower, upper = exchange(two_cast)
-    total, after = near_total(own)
+        return pairs, last
+
+    (total,) = near_total(first_region)
+    pairs, last = pairs_of(first_lower, first_upper)
+    pairs.append(last)
+    body_of = functools.partial(table_body, region_blocks, 0)
+    table_shape = jax.ShapeDtypeStruct(halo_slots, jnp.int32)
+    specs = [SMEM] * 4 + [VMEM] * 4
+    call = kernel_call(body_of, (wide, table_shape), specs, covering, traffic)
+    if len(pairs) == 1:
+        pairs.append(tuple(jnp.zeros_like(part) for part in last))
+    total, table = call(block_cols, live_blocks, lists, bases, held, *pairs[0], total)
+    which = len(pairs) - 1 if paired else 0
+    body_of = functools.partial(first_body, which)
+    one, one_cast = halo_part(body_of, (wide, narrow), table, pairs[-1], total, (bounds,), (vectors,))
+
+    region, lower, upper = exchange(one_cast)
+    (total,) = near_total(region)
+    pairs, last = pairs_of(lower, upper)
+    for which, pair in enumerate(pairs):
+        (total,) = halo_part(functools.partial(middle_body, which), (wide,), table, pair, total)
+    body_of = functools.partial(second_body, len(pairs))
+    two, two_cast = halo_part(body_of, (wide, narrow), table, last, total, (bounds,), (one, vectors))
+
+    region, lower, upper = exchange(two_cast)
+    total, after = near_total(region, (token,))
     packed = jax.ShapeDtypeStruct((tile_rows, TILE), jnp.float32)
     gram = kernel_call(gram_body, packed, [SMEM, VMEM, VMEM], free, traffic)(gram_number, two, after)
     for step_of in [halving(*cores), halving(*across)]:
         gram = step_of(gram)()
-    *pairs, last = zip(gathered(lower), gathered(upper))
+    pairs, last = pairs_of(lower, upper)
     for which, pair in enumerate(pairs):
-        total, after = halo_part(middle_body, (wide, token), which, pair, total)
+        total, after = halo_part(functools.partial(middle_body, which), (wide, token), table, pair, total)
     gram, after = tied(gram, after)
-    cross = halo_part(third_body, square, len(pairs), last, total, (cross_number,), (two, after))
+    body_of = functools.partial(third_body, len(pairs))
+    cross = halo_part(body_of, square, table, last, total, (cross_number,), (two, after))
     cross = halving(*cores)(cross)()
 
     fold = modes // TILE
     cut = gram.shape[0] // fold
     folded = jnp.concatenate([gram[at * cut : (at + 1) * cut] for at in range(fold)], 1)
-    flat = lambda value: [value[:, at * TILE : (at + 1) * TILE] for at in range(fold)]
     half = cross.shape[0] // 2
     got = partner_value(jnp.concatenate([folded, cross[half:]], 0), *near)
     both = jnp.concatenate([folded, cross[:half]], 0) + got
-    for bit in between:
-        both = doubling(*bit)(both)()
-    got = partner_value(both, *across)
-    gram = joining(*cores)(jnp.concatenate(flat(both[:cut]) + flat(got[:cut]), 0))()
-    cross = both[cut:] + got[cut:]
+    both = doubling(*between[0])(both)()
+    gram = jnp.concatenate([both[:cut, at * TILE : (at + 1) * TILE] for at in range(fold)], 0)
+    cross = both[cut:]
+    for step_of in [doubling(*bit) for bit in between[1:]] + [joining(*across), joining(*cores)]:
+        gram = step_of(gram)()
     stages = factor_stages(float(total_rows), modes // TILE, gram_number, two)
-    steps = [joining(*near), joining(*cores)]
+    steps = [doubling(*bit) for bit in between[1:]] + [doubling(*across), joining(*near), joining(*cores)]
     cross, (basis, inverse) = run_beside(cross, steps, gram, stages)
     body_of = functools.partial(projected_body, float(total_rows))
     call = kernel_call(body_of, square, [SMEM] + [VMEM] * 2, 2 * square_work, traffic)

time: 117 us -> 119 us (1.017)
  blocking collectives: 0 us -> 8.48 us
  Pallas kernels: 34.6 us -> 31.2 us
  starting transfers between devices: 37.2 us -> 35 us
  waiting for transfers between devices: 33 us -> 31.8 us
    all_gather x0 -> x3, blocking collectives: none -> 8.48 us  [exchange(): region = lax.all_gather(operand, 'split', axis=0)]
    ppermute x6, waiting for transfers between devices: 18.2 us -> 10 us  [shifted(): return lax.ppermute(value, axis, pairs)]
    ppermute x10 -> x12, waiting for transfers between devices: 14.7 us -> 21.7 us  [partner_value(): lax.ppermute(value, axis, [(at, at ^ bit) for at in range(lax.axis_size(a...]
    pallas_call x9, Pallas kernels: 19.3 us -> 16.7 us  [the longest x5 10.1 us: halo_part(): return call(table, bases, held, *pair, total, *scalars, *extra)]
    ppermute x6, starting transfers between devices: 16.2 us -> 14.2 us  [shifted(): return lax.ppermute(value, axis, pairs)]
    ppermute x9 -> x6, starting transfers between devices: 7.3 us -> 6.18 us  [local(): swapped = lambda value: lax.ppermute(value, 'split', [(0, 1), (1, 0)])]
    ppermute x10 -> x12, starting transfers between devices: 13.7 us -> 14.5 us  [partner_value(): lax.ppermute(value, axis, [(at, at ^ bit) for at in range(lax.axis_size(a...]
    unnamed x26 -> x32, local copies, waits for them, and re-layouts: 5.4 us -> 5.36 us
  transfers between devices with their start and end apart: 25 -> 24, of which waited for: 10 -> 14; matrix products, arithmetic and copies ran while one was open for 3% -> 2% of each run, Pallas kernels for 20% -> 17%
where the time goes in v12:
time: 119 us; the launch traced here: 118 us
  starting transfers between devices  35 us (29%)
  waiting for transfers between devices  31.8 us (27%)
  Pallas kernels  31.2 us (26%)
  blocking collectives  8.48 us (7%)
  local copies, waits for them, and re-layouts  7.38 us (6%)
  other arithmetic  3.6 us (3%)
    ppermute x12, waiting for transfers between devices, partner_value(): lax.ppermute(value, axis, [(at, at ^ bit) for at in range(lax.axis_size(a...  21.7 us
    ppermute x12, starting transfers between devices, partner_value(): lax.ppermute(value, axis, [(at, at ^ bit) for at in range(lax.axis_size(a...  14.5 us
    ppermute x6, starting transfers between devices, shifted(): return lax.ppermute(value, axis, pairs)  14.2 us
    pallas_call x5, Pallas kernels, halo_part(): return call(table, bases, held, *pair, total, *scalars, *extra)  10.1 us
    ppermute x6, waiting for transfers between devices, shifted(): return lax.ppermute(value, axis, pairs)  10 us
    all_gather x3, blocking collectives, exchange(): region = lax.all_gather(operand, 'split', axis=0)  8.48 us
    ppermute x6, starting transfers between devices, local(): swapped = lambda value: lax.ppermute(value, 'split', [(0, 1), (1, 0)])  6.18 us
    unnamed x32, local copies, waits for them, and re-layouts  5.36 us
  transfers between devices with their start and end apart: 24, of which 14 were waited for; matrix products, arithmetic and copies ran while one was open for 2% of the time, Pallas kernels for 17%

profile of v12, /device:TPU:1, one launch (start us, length us, event | category | flops | bytes accessed | tf_op | source)
XLA Modules:
  0.0 118.4 jit_solution(9323438262397338113)
XLA Ops:
  3.2 2.0 %collective-permute-start = (bf16[592,256]{1,0:T(8,128)(2,1)}, bf16[592,256]{1,0:T(8,128)(2,1)}, u32[]{:S(2)}, u32[]{:S(2)}) collective-permute-start(bf16[592,256]{1,0:T(8,128)(2,1)} %fusion.1), channel_id=1, source_target_pairs={{0,2},{2,4},{4,6},{6,8},{8,10},{10,12},{12,14},{14,16},{16,18},{18... | collective-permute-start | bytes 909320 | tf_op jit(solution)/shard_map/ppermute | solution.py:27
  5.2 4.0 %collective-permute-start.1 = (bf16[592,256]{1,0:T(8,128)(2,1)}, bf16[592,256]{1,0:T(8,128)(2,1)}, u32[]{:S(2)}, u32[]{:S(2)}) collective-permute-start(bf16[592,256]{1,0:T(8,128)(2,1)} %fusion.1), channel_id=1, source_target_pairs={{0,30},{2,0},{4,2},{6,4},{8,6},{10,8},{12,10},{14,12},{16,14},{18,... | collective-permute-start | bytes 909320 | tf_op jit(solution)/shard_map/ppermute | solution.py:27
  9.2 2.0 %copy-done = bf16[3,12,192,192]{3,2,1,0:T(8,128)(2,1)S(1)} copy-done((bf16[3,12,192,192]{3,2,1,0:T(8,128)(2,1)S(1)}, bf16[3,12,192,192]{3,2,1,0:T(8,128)(2,1)}, u32[]{:S(2)}) %copy-start) | copy-done | bytes 2654232
  11.7 3.0 %all-gather = bf16[1184,256]{1,0:T(8,128)(2,1)S(1)} all-gather(bf16[592,256]{1,0:T(8,128)(2,1)} %fusion.1), channel_id=2, replica_groups=mesh['region'=16,'split'=2] {'split'}, dimensions={0}, use_global_device_ids=true | all-gather | bytes 909312 | tf_op jit(solution)/shard_map/all_gather | solution.py:418
  16.1 1.8 %collective-permute-done = bf16[592,256]{1,0:T(8,128)(2,1)} collective-permute-done((bf16[592,256]{1,0:T(8,128)(2,1)}, bf16[592,256]{1,0:T(8,128)(2,1)}, u32[]{:S(2)}, u32[]{:S(2)}) %collective-permute-start) | collective-permute-done | bytes 303136 | tf_op jit(solution)/shard_map/ppermute | solution.py:27
  20.5 1.6 %collective-permute-start.2 = (bf16[592,256]{1,0:T(8,128)(2,1)}, bf16[592,256]{1,0:T(8,128)(2,1)S(1)}, u32[]{:S(2)}, u32[]{:S(2)}) collective-permute-start(bf16[592,256]{1,0:T(8,128)(2,1)} %collective-permute-done), channel_id=1, source_target_pairs={{0,1},{1,0},{2,3},{3,2},{4,5},{5,4},{6,7},{7,6},{8,9},{9,8},{10,11... | collective-permute-start | bytes 909320 | tf_op jit(solution)/shard_map/ppermute | solution.py:392
  22.2 2.4 %shard_map.79 = (f32[576,256]{1,0:T(8,128)S(1)}, s32[3,13]{1,0:T(4,128)S(1)}) custom-call(s32[3,12]{1,0:T(4,128)S(1)} %copy-done.5, s32[3]{0:T(128)S(1)} %copy-done.6, s32[2,6]{1,0:T(2,128)S(1)} %maximum_convert_fusion.lists_ref, s32[2]{0:T(128)S(1)} %pad_add_fusion.refs_2_.refs_0_.refs_1_, bf16[3,12,192,192]{3,2,1,0:T(8,128)(2,1)S(1)} %shard_map.77.refs_3_.refs_1_.refs_2_, ...), custom_call_target="tpu_custom_call" | custom-call | flops 30000001024 | bytes 276480 | tf_op jit(solution)/shard_map/pallas_call | solution.py:482
  24.7 1.9 %shard_map.80 = (f32[576,256]{1,0:T(8,128)S(1)}, bf16[576,256]{1,0:T(8,128)(2,1)}) custom-call(s32[3,13]{1,0:T(4,128)S(1)} %get-tuple-element.38.refs_0_, s32[2]{0:T(128)S(1)} %pad_add_fusion.refs_2_.refs_0_.refs_1_, bf16[3,12,192,192]{3,2,1,0:T(8,128)(2,1)S(1)} %shard_map.77.refs_3_.refs_1_.refs_2_, bf16[1,592,256]{2,1,0:T(8,128)(2,1)S(1)} %bitcast.24, ...), custom_call_target="tpu_custom_call" | custom-call | flops 30000001024 | bytes 276480 | tf_op jit(solution)/shard_map/pallas_call | solution.py:467
  27.4 3.1 %collective-permute-start.6 = (bf16[576,256]{1,0:T(8,128)(2,1)}, bf16[576,256]{1,0:T(8,128)(2,1)}, u32[]{:S(2)}, u32[]{:S(2)}) collective-permute-start(bf16[576,256]{1,0:T(8,128)(2,1)} %get-tuple-element.40), channel_id=1, source_target_pairs={{0,30},{2,0},{4,2},{6,4},{8,6},{10,8},{12,10},{14,12},{16,14},{18,... | collective-permute-start | bytes 884744 | tf_op jit(solution)/shard_map/ppermute | solution.py:27
  30.6 2.9 %all-gather.1 = bf16[1152,256]{1,0:T(8,128)(2,1)S(1)} all-gather(bf16[576,256]{1,0:T(8,128)(2,1)} %get-tuple-element.40), channel_id=3, replica_groups=mesh['region'=16,'split'=2] {'split'}, dimensions={0}, use_global_device_ids=true | all-gather | bytes 884736 | tf_op jit(solution)/shard_map/all_gather | solution.py:418
  34.8 2.0 %collective-permute-done.6 = bf16[576,256]{1,0:T(8,128)(2,1)} collective-permute-done((bf16[576,256]{1,0:T(8,128)(2,1)}, bf16[576,256]{1,0:T(8,128)(2,1)}, u32[]{:S(2)}, u32[]{:S(2)}) %collective-permute-start.6) | collective-permute-done | bytes 294944 | tf_op jit(solution)/shard_map/ppermute | solution.py:27
  38.1 4.2 %collective-permute-done.4 = bf16[576,256]{1,0:T(8,128)(2,1)} collective-permute-done((bf16[576,256]{1,0:T(8,128)(2,1)}, bf16[576,256]{1,0:T(8,128)(2,1)}, u32[]{:S(2)}, u32[]{:S(2)}) %collective-permute-start.4) | collective-permute-done | bytes 294944 | tf_op jit(solution)/shard_map/ppermute | solution.py:27
  42.3 1.7 %collective-permute-start.5 = (bf16[576,256]{1,0:T(8,128)(2,1)}, bf16[576,256]{1,0:T(8,128)(2,1)S(1)}, u32[]{:S(2)}, u32[]{:S(2)}) collective-permute-start(bf16[576,256]{1,0:T(8,128)(2,1)} %collective-permute-done.4), channel_id=1, source_target_pairs={{0,1},{1,0},{2,3},{3,2},{4,5},{5,4},{6,7},{7,6},{8,9},{9,8},{10,11... | collective-permute-start | bytes 884744 | tf_op jit(solution)/shard_map/ppermute | solution.py:392
  44.0 1.8 %shard_map.82.refs_5_ = f32[576,256]{1,0:T(8,128)S(1)} custom-call(s32[3,13]{1,0:T(4,128)S(1)} %copy-done.13, s32[2]{0:T(128)S(1)} %pad_add_fusion.refs_2_.refs_0_.refs_1_, bf16[3,12,192,192]{3,2,1,0:T(8,128)(2,1)S(1)} %shard_map.77.refs_3_.refs_1_.refs_2_, bf16[1,576,256]{2,1,0:T(8,128)(2,1)} %bitcast.11.refs_3_, bf16[1,576,256]{2,1,0:T(8,128)(2,1)} %bitcast.12.refs_4_, ...), custom_call_target="tpu_custom_call" | custom-call | flops 30000001024 | bytes 276480 | tf_op jit(solution)/shard_map/pallas_call | solution.py:467
  45.8 1.9 %shard_map.83 = (f32[576,256]{1,0:T(8,128)S(1)}, bf16[576,256]{1,0:T(8,128)(2,1)}) custom-call(s32[3,13]{1,0:T(4,128)S(1)} %copy-done.13, s32[2]{0:T(128)S(1)} %pad_add_fusion.refs_2_.refs_0_.refs_1_, bf16[3,12,192,192]{3,2,1,0:T(8,128)(2,1)S(1)} %shard_map.77.refs_3_.refs_1_.refs_2_, bf16[1,576,256]{2,1,0:T(8,128)(2,1)S(1)} %bitcast.29, ...), custom_call_target="tpu_custom_call" | custom-call | flops 30000001024 | bytes 276480 | tf_op jit(solution)/shard_map/pallas_call | solution.py:467
  47.8 2.6 %all-gather.2 = bf16[1152,256]{1,0:T(8,128)(2,1)S(1)} all-gather(bf16[576,256]{1,0:T(8,128)(2,1)} %get-tuple-element.43), channel_id=4, replica_groups=mesh['region'=16,'split'=2] {'split'}, dimensions={0}, use_global_device_ids=true | all-gather | bytes 884736 | tf_op jit(solution)/shard_map/all_gather | solution.py:418
  54.6 4.2 %collective-permute-start.11 = (bf16[576,256]{1,0:T(8,128)(2,1)}, bf16[576,256]{1,0:T(8,128)(2,1)}, u32[]{:S(2)}, u32[]{:S(2)}) collective-permute-start(bf16[576,256]{1,0:T(8,128)(2,1)} %get-tuple-element.43), channel_id=1, source_target_pairs={{0,30},{2,0},{4,2},{6,4},{8,6},{10,8},{12,10},{14,12},{16,14},{18,... | collective-permute-start | bytes 884744 | tf_op jit(solution)/shard_map/ppermute | solution.py:27
  60.1 7.7 %collective-permute-done.9 = f32[96,128]{1,0:T(8,128)} collective-permute-done((f32[96,128]{1,0:T(8,128)}, f32[96,128]{1,0:T(8,128)}, u32[]{:S(2)}, u32[]{:S(2)}) %collective-permute-start.9) | collective-permute-done | bytes 49184 | tf_op jit(solution)/shard_map/ppermute | solution.py:328
  72.0 1.7 %shard_map.86 = (f32[576,256]{1,0:T(8,128)S(1)}, f32[8,128]{1,0:T(8,128)S(1)}) custom-call(s32[3,13]{1,0:T(4,128)S(1)} %copy-done.14, s32[2]{0:T(128)S(1)} %pad_add_fusion.refs_2_.refs_0_.refs_1_, bf16[3,12,192,192]{3,2,1,0:T(8,128)(2,1)S(1)} %shard_map.77.refs_3_.refs_1_.refs_2_, bf16[1,576,256]{2,1,0:T(8,128)(2,1)} %bitcast.15.refs_3_, ...), custom_call_target="tpu_custom_call" | custom-call | flops 30000001024 | bytes 276480 | tf_op jit(solution)/shard_map/pallas_call | solution.py:467
  73.8 2.8 %shard_map.87 = f32[256,256]{1,0:T(8,128)S(1)} custom-call(s32[3,13]{1,0:T(4,128)S(1)} %copy-done.14, s32[2]{0:T(128)S(1)} %pad_add_fusion.refs_2_.refs_0_.refs_1_, bf16[3,12,192,192]{3,2,1,0:T(8,128)(2,1)S(1)} %shard_map.77.refs_3_.refs_1_.refs_2_, bf16[1,576,256]{2,1,0:T(8,128)(2,1)S(1)} %bitcast.26, bf16[1,576,256]{2,1,0:T(8,128)(2,1)S(1)} %bitcast.28, ...), custom_call_target="tpu_custom_call" | custom-call | flops 30000001024 | bytes 276480 | tf_op jit(solution)/shard_map/pallas_call | solution.py:467
  78.6 4.1 %collective-permute-done.15 = f32[112,256]{1,0:T(8,128)S(1)} collective-permute-done((f32[112,256]{1,0:T(8,128)S(1)}, f32[112,256]{1,0:T(8,128)S(1)}, u32[]{:S(2)}, u32[]{:S(2)}) %collective-permute-start.15) | collective-permute-done | bytes 114720 | tf_op jit(solution)/shard_map/ppermute | solution.py:328
  83.7 2.7 %collective-permute-done.16 = f32[112,256]{1,0:T(8,128)S(1)} collective-permute-done((f32[112,256]{1,0:T(8,128)S(1)}, f32[112,256]{1,0:T(8,128)S(1)}, u32[]{:S(2)}, u32[]{:S(2)}) %collective-permute-start.16) | collective-permute-done | bytes 114720 | tf_op jit(solution)/shard_map/ppermute | solution.py:328
  86.5 2.0 %collective-permute-start.17 = (f32[96,128]{1,0:T(8,128)S(1)}, f32[96,128]{1,0:T(8,128)S(1)}, u32[]{:S(2)}, u32[]{:S(2)}) collective-permute-start(f32[96,128]{1,0:T(8,128)S(1)} %pad_maximum_fusion.5), channel_id=1, source_target_pairs={{0,16},{2,18},{4,20},{6,22},{8,24},{10,26},{12,28},{14,30},{16,0},... | collective-permute-start | bytes 147464 | tf_op jit(solution)/shard_map/ppermute | solution.py:328
  88.5 1.9 %collective-permute-done.17 = f32[96,128]{1,0:T(8,128)S(1)} collective-permute-done((f32[96,128]{1,0:T(8,128)S(1)}, f32[96,128]{1,0:T(8,128)S(1)}, u32[]{:S(2)}, u32[]{:S(2)}) %collective-permute-start.17) | collective-permute-done | bytes 49184 | tf_op jit(solution)/shard_map/ppermute | solution.py:328
  91.7 1.7 %collective-permute-done.18 = f32[96,128]{1,0:T(8,128)S(1)} collective-permute-done((f32[96,128]{1,0:T(8,128)S(1)}, f32[96,128]{1,0:T(8,128)S(1)}, u32[]{:S(2)}, u32[]{:S(2)}) %collective-permute-start.18) | collective-permute-done | bytes 49184 | tf_op jit(solution)/shard_map/ppermute | solution.py:328
  93.4 4.5 %collective-permute-start.19 = (f32[192,128]{1,0:T(8,128)S(1)}, f32[192,128]{1,0:T(8,128)S(1)}, u32[]{:S(2)}, u32[]{:S(2)}) collective-permute-start(f32[192,128]{1,0:T(8,128)S(1)} %pad_maximum_fusion.4), channel_id=1, source_target_pairs={{0,1},{1,0},{2,3},{3,2},{4,5},{5,4},{6,7},{7,6},{8,9},{9,8},{10,11... | collective-permute-start | bytes 294920 | tf_op jit(solution)/shard_map/ppermute | solution.py:328
  98.8 2.1 %collective-permute-start.20 = (f32[64,256]{1,0:T(8,128)S(1)}, f32[64,256]{1,0:T(8,128)S(1)}, u32[]{:S(2)}, u32[]{:S(2)}) collective-permute-start(f32[64,256]{1,0:T(8,128)S(1)} %slice.70), channel_id=1, source_target_pairs={{0,16},{2,18},{4,20},{6,22},{8,24},{10,26},{12,28},{14,30},{16,0},... | collective-permute-start | bytes 196616 | tf_op jit(solution)/shard_map/ppermute | solution.py:328
  100.9 5.2 %shard_map.88 = (f32[128,128]{1,0:T(8,128)S(1)}, f32[128,128]{1,0:T(8,128)S(1)}, f32[128,128]{1,0:T(8,128)S(1)}, f32[16,128]{1,0:T(8,128)S(1)}) custom-call(s32[1]{0:T(128)} %bitcast.number_ref, f32[384,128]{1,0:T(8,128)S(1)} %pad_maximum_fusion.1.gram_ref), custom_call_target="tpu_custom_call" | custom-call | flops 100000000 | bytes 3072 | tf_op jit(solution)/shard_map/pallas_call | solution.py:305
  106.2 4.4 %shard_map.89 = (f32[128,128]{1,0:T(8,128)S(1)}, f32[128,128]{1,0:T(8,128)S(1)}, f32[128,128]{1,0:T(8,128)S(1)}) custom-call(f32[128,128]{1,0:T(8,128)S(1)} %get-tuple-element.57.refs_0_, f32[128,128]{1,0:T(8,128)S(1)} %get-tuple-element.58.refs_1_, f32[128,128]{1,0:T(8,128)S(1)} %get-tuple-element.59.refs_2_), custom_call_target="tpu_custom_call" | custom-call | flops 100000000 | bytes 1024 | tf_op jit(solution)/shard_map/pallas_call | solution.py:311
  111.5 1.9 %shard_map.90 = (f32[576,256]{1,0:T(8,128)}, f32[256,256]{1,0:T(8,128)S(1)}) custom-call(f32[128,128]{1,0:T(8,128)S(1)} %get-tuple-element.65.refs_0_, f32[128,128]{1,0:T(8,128)S(1)} %get-tuple-element.66.refs_1_, f32[128,128]{1,0:T(8,128)S(1)} %get-tuple-element.67.refs_2_, f32[16,128]{1,0:T(8,128)S(1)} %get-tuple-element.68.refs_3_, f32[576,256]{1,0:T(8,128)S(1)} %copy-done.2), custom_call_target="tpu_custom_call" | custom-call | flops 100000000 | bytes 9216 | tf_op jit(solution)/shard_map/pallas_call | solution.py:318
  113.8 1.9 %collective-permute-start.23 = (f32[128,256]{1,0:T(8,128)S(1)}, f32[128,256]{1,0:T(8,128)S(1)}, u32[]{:S(2)}, u32[]{:S(2)}) collective-permute-start(f32[128,256]{1,0:T(8,128)S(1)} %pad_maximum_fusion.2), channel_id=1, source_target_pairs={{0,1},{1,0},{2,3},{3,2},{4,5},{5,4},{6,7},{7,6},{8,9},{9,8},{10,11... | collective-permute-start | bytes 393224 | tf_op jit(solution)/shard_map/ppermute | solution.py:328
  116.6 1.7 %shard_map.91 = f32[256,256]{1,0:T(8,128)} custom-call(s32[1]{0:T(128)} %bitcast.19.refs_6_.number_ref, f32[256,256]{1,0:T(8,128)S(1)} %pad_maximum_fusion.cross_ref, f32[256,256]{1,0:T(8,128)S(1)} %get-tuple-element.73.inverse_ref), custom_call_target="tpu_custom_call" | custom-call | flops 150994944 | bytes 276480 | tf_op jit(solution)/shard_map/pallas_call | solution.py:525
  (94 shorter events, 28.0 us)
Async XLA Ops:
  3.2 14.7 %collective-permute-start = (bf16[592,256]{1,0:T(8,128)(2,1)}, bf16[592,256]{1,0:T(8,128)(2,1)}, u32[]{:S(2)}, u32[]{:S(2)}) collective-permute-start(bf16[592,256]{1,0:T(8,128)(2,1)} %fusion.1), channel_id=1, source_target_pairs={{0,2},{2,4},{4,6},{6,8},{8,10},{10,12},{12,14},{14,16},{16,18},{18... | collective-permute-start | bytes 909320 | tf_op jit(solution)/shard_map/ppermute | solution.py:27
  5.2 14.6 %collective-permute-start.1 = (bf16[592,256]{1,0:T(8,128)(2,1)}, bf16[592,256]{1,0:T(8,128)(2,1)}, u32[]{:S(2)}, u32[]{:S(2)}) collective-permute-start(bf16[592,256]{1,0:T(8,128)(2,1)} %fusion.1), channel_id=1, source_target_pairs={{0,30},{2,0},{4,2},{6,4},{8,6},{10,8},{12,10},{14,12},{16,14},{18,... | collective-permute-start | bytes 909320 | tf_op jit(solution)/shard_map/ppermute | solution.py:27
  9.2 2.0 %copy-start = (bf16[3,12,192,192]{3,2,1,0:T(8,128)(2,1)S(1)}, bf16[3,12,192,192]{3,2,1,0:T(8,128)(2,1)}, u32[]{:S(2)}) copy-start(bf16[3,12,192,192]{3,2,1,0:T(8,128)(2,1)} %blocks_ref.1) | copy-start | bytes 7962628
  11.2 3.5 %copy-start.5 = (s32[3,12]{1,0:T(4,128)S(1)}, s32[3,12]{1,0:T(4,128)}, u32[]{:S(2)}) copy-start(s32[3,12]{1,0:T(4,128)} %refs_0_.5) | copy-start | bytes 436
  11.2 3.5 %copy-start.6 = (s32[3]{0:T(128)S(1)}, s32[3]{0:T(128)}, u32[]{:S(2)}) copy-start(s32[3]{0:T(128)} %refs_1_.5) | copy-start | bytes 40
  20.5 4.2 %collective-permute-start.2 = (bf16[592,256]{1,0:T(8,128)(2,1)}, bf16[592,256]{1,0:T(8,128)(2,1)S(1)}, u32[]{:S(2)}, u32[]{:S(2)}) collective-permute-start(bf16[592,256]{1,0:T(8,128)(2,1)} %collective-permute-done), channel_id=1, source_target_pairs={{0,1},{1,0},{2,3},{3,2},{4,5},{5,4},{6,7},{7,6},{8,9},{9,8},{10,11... | collective-permute-start | bytes 909320 | tf_op jit(solution)/shard_map/ppermute | solution.py:392
  22.1 2.6 %collective-permute-start.3 = (bf16[592,256]{1,0:T(8,128)(2,1)}, bf16[592,256]{1,0:T(8,128)(2,1)S(1)}, u32[]{:S(2)}, u32[]{:S(2)}) collective-permute-start(bf16[592,256]{1,0:T(8,128)(2,1)} %collective-permute-done.1), channel_id=1, source_target_pairs={{0,1},{1,0},{2,3},{3,2},{4,5},{5,4},{6,7},{7,6},{8,9},{9,8},{10,11... | collective-permute-start | bytes 909320 | tf_op jit(solution)/shard_map/ppermute | solution.py:392
  22.2 2.5 %copy-start.3 = (f32[576,256]{1,0:T(8,128)S(1)}, f32[576,256]{1,0:T(8,128)}, u32[]{:S(2)}) copy-start(f32[576,256]{1,0:T(8,128)} %refs_8_.1) | copy-start | bytes 1769476
  22.2 2.5 %copy-start.9 = (f32[2]{0:T(128)S(1)}, f32[2]{0:T(128)}, u32[]{:S(2)}) copy-start(f32[2]{0:T(128)} %refs_6_.3) | copy-start | bytes 28
  27.4 9.4 %collective-permute-start.6 = (bf16[576,256]{1,0:T(8,128)(2,1)}, bf16[576,256]{1,0:T(8,128)(2,1)}, u32[]{:S(2)}, u32[]{:S(2)}) collective-permute-start(bf16[576,256]{1,0:T(8,128)(2,1)} %get-tuple-element.40), channel_id=1, source_target_pairs={{0,30},{2,0},{4,2},{6,4},{8,6},{10,8},{12,10},{14,12},{16,14},{18,... | collective-permute-start | bytes 884744 | tf_op jit(solution)/shard_map/ppermute | solution.py:27
  30.6 11.7 %collective-permute-start.4 = (bf16[576,256]{1,0:T(8,128)(2,1)}, bf16[576,256]{1,0:T(8,128)(2,1)}, u32[]{:S(2)}, u32[]{:S(2)}) collective-permute-start(bf16[576,256]{1,0:T(8,128)(2,1)} %get-tuple-element.40), channel_id=1, source_target_pairs={{0,2},{2,4},{4,6},{6,8},{8,10},{10,12},{12,14},{14,16},{16,18},{18... | collective-permute-start | bytes 884744 | tf_op jit(solution)/shard_map/ppermute | solution.py:27
  30.6 13.4 %copy-start.13 = (s32[3,13]{1,0:T(4,128)S(1)}, s32[3,13]{1,0:T(4,128)}, u32[]{:S(2)}) copy-start(s32[3,13]{1,0:T(4,128)} %copy-done.12) | copy-start | bytes 472
  36.8 9.0 %collective-permute-start.7 = (bf16[576,256]{1,0:T(8,128)(2,1)}, bf16[576,256]{1,0:T(8,128)(2,1)S(1)}, u32[]{:S(2)}, u32[]{:S(2)}) collective-permute-start(bf16[576,256]{1,0:T(8,128)(2,1)} %collective-permute-done.6), channel_id=1, source_target_pairs={{0,1},{1,0},{2,3},{3,2},{4,5},{5,4},{6,7},{7,6},{8,9},{9,8},{10,11... | collective-permute-start | bytes 884744 | tf_op jit(solution)/shard_map/ppermute | solution.py:392
  42.3 3.5 %collective-permute-start.5 = (bf16[576,256]{1,0:T(8,128)(2,1)}, bf16[576,256]{1,0:T(8,128)(2,1)S(1)}, u32[]{:S(2)}, u32[]{:S(2)}) collective-permute-start(bf16[576,256]{1,0:T(8,128)(2,1)} %collective-permute-done.4), channel_id=1, source_target_pairs={{0,1},{1,0},{2,3},{3,2},{4,5},{5,4},{6,7},{7,6},{8,9},{9,8},{10,11... | collective-permute-start | bytes 884744 | tf_op jit(solution)/shard_map/ppermute | solution.py:392
  47.8 4.8 %copy-start.1 = (f32[576,256]{1,0:T(8,128)}, f32[576,256]{1,0:T(8,128)S(1)}, u32[]{:S(2)}) copy-start(f32[576,256]{1,0:T(8,128)S(1)} %get-tuple-element.42.two_ref.refs_7_.refs_4_) | copy-start | bytes 1769476
  47.8 23.1 %copy-start.14 = (s32[3,13]{1,0:T(4,128)S(1)}, s32[3,13]{1,0:T(4,128)}, u32[]{:S(2)}) copy-start(s32[3,13]{1,0:T(4,128)} %copy-done.12) | copy-start | bytes 472
  53.6 5.3 %collective-permute-start.8 = (f32[192,128]{1,0:T(8,128)S(1)}, f32[192,128]{1,0:T(8,128)S(1)}, u32[]{:S(2)}, u32[]{:S(2)}) collective-permute-start(f32[192,128]{1,0:T(8,128)S(1)} %slice.63), channel_id=1, source_target_pairs={{0,1},{1,0},{2,3},{3,2},{4,5},{5,4},{6,7},{7,6},{8,9},{9,8},{10,11... | collective-permute-start | bytes 294920 | tf_op jit(solution)/shard_map/ppermute | solution.py:328
  53.8 14.8 %collective-permute-start.10 = (bf16[576,256]{1,0:T(8,128)(2,1)}, bf16[576,256]{1,0:T(8,128)(2,1)}, u32[]{:S(2)}, u32[]{:S(2)}) collective-permute-start(bf16[576,256]{1,0:T(8,128)(2,1)} %get-tuple-element.43), channel_id=1, source_target_pairs={{0,2},{2,4},{4,6},{6,8},{8,10},{10,12},{12,14},{14,16},{16,18},{18... | collective-permute-start | bytes 884744 | tf_op jit(solution)/shard_map/ppermute | solution.py:27
  54.6 15.3 %collective-permute-start.11 = (bf16[576,256]{1,0:T(8,128)(2,1)}, bf16[576,256]{1,0:T(8,128)(2,1)}, u32[]{:S(2)}, u32[]{:S(2)}) collective-permute-start(bf16[576,256]{1,0:T(8,128)(2,1)} %get-tuple-element.43), channel_id=1, source_target_pairs={{0,30},{2,0},{4,2},{6,4},{8,6},{10,8},{12,10},{14,12},{16,14},{18,... | collective-permute-start | bytes 884744 | tf_op jit(solution)/shard_map/ppermute | solution.py:27
  60.1 7.7 %collective-permute-start.9 = (f32[96,128]{1,0:T(8,128)}, f32[96,128]{1,0:T(8,128)}, u32[]{:S(2)}, u32[]{:S(2)}) collective-permute-start(f32[96,128]{1,0:T(8,128)} %slice.65), channel_id=1, source_target_pairs={{0,4},{2,6},{4,0},{6,2},{8,12},{10,14},{12,8},{14,10},{16,20},{18,... | collective-permute-start | bytes 147464 | tf_op jit(solution)/shard_map/ppermute | solution.py:328
  68.6 5.1 %collective-permute-start.12 = (bf16[576,256]{1,0:T(8,128)(2,1)}, bf16[576,256]{1,0:T(8,128)(2,1)S(1)}, u32[]{:S(2)}, u32[]{:S(2)}) collective-permute-start(bf16[576,256]{1,0:T(8,128)(2,1)} %collective-permute-done.10), channel_id=1, source_target_pairs={{0,1},{1,0},{2,3},{3,2},{4,5},{5,4},{6,7},{7,6},{8,9},{9,8},{10,11... | collective-permute-start | bytes 884744 | tf_op jit(solution)/shard_map/ppermute | solution.py:392
  70.0 3.8 %collective-permute-start.13 = (bf16[576,256]{1,0:T(8,128)(2,1)}, bf16[576,256]{1,0:T(8,128)(2,1)S(1)}, u32[]{:S(2)}, u32[]{:S(2)}) collective-permute-start(bf16[576,256]{1,0:T(8,128)(2,1)} %collective-permute-done.11), channel_id=1, source_target_pairs={{0,1},{1,0},{2,3},{3,2},{4,5},{5,4},{6,7},{7,6},{8,9},{9,8},{10,11... | collective-permute-start | bytes 884744 | tf_op jit(solution)/shard_map/ppermute | solution.py:392
  76.6 1.4 %collective-permute-start.14 = (f32[128,256]{1,0:T(8,128)S(1)}, f32[128,256]{1,0:T(8,128)S(1)}, u32[]{:S(2)}, u32[]{:S(2)}) collective-permute-start(f32[128,256]{1,0:T(8,128)S(1)} %slice.67), channel_id=1, source_target_pairs={{0,1},{1,0},{2,3},{3,2},{4,5},{5,4},{6,7},{7,6},{8,9},{9,8},{10,11... | collective-permute-start | bytes 393224 | tf_op jit(solution)/shard_map/ppermute | solution.py:328
  78.0 4.7 %collective-permute-start.15 = (f32[112,256]{1,0:T(8,128)S(1)}, f32[112,256]{1,0:T(8,128)S(1)}, u32[]{:S(2)}, u32[]{:S(2)}) collective-permute-start(f32[112,256]{1,0:T(8,128)S(1)} %fusion.2), channel_id=1, source_target_pairs={{0,2},{2,0},{4,6},{6,4},{8,10},{10,8},{12,14},{14,12},{16,18},{18,... | collective-permute-start | bytes 344072 | tf_op jit(solution)/shard_map/ppermute | solution.py:328
  82.7 3.7 %collective-permute-start.16 = (f32[112,256]{1,0:T(8,128)S(1)}, f32[112,256]{1,0:T(8,128)S(1)}, u32[]{:S(2)}, u32[]{:S(2)}) collective-permute-start(f32[112,256]{1,0:T(8,128)S(1)} %maximum_add_fusion), channel_id=1, source_target_pairs={{0,8},{2,10},{4,12},{6,14},{8,0},{10,2},{12,4},{14,6},{16,24},{18,... | collective-permute-start | bytes 344072 | tf_op jit(solution)/shard_map/ppermute | solution.py:328
  86.5 3.9 %collective-permute-start.17 = (f32[96,128]{1,0:T(8,128)S(1)}, f32[96,128]{1,0:T(8,128)S(1)}, u32[]{:S(2)}, u32[]{:S(2)}) collective-permute-start(f32[96,128]{1,0:T(8,128)S(1)} %pad_maximum_fusion.5), channel_id=1, source_target_pairs={{0,16},{2,18},{4,20},{6,22},{8,24},{10,26},{12,28},{14,30},{16,0},... | collective-permute-start | bytes 147464 | tf_op jit(solution)/shard_map/ppermute | solution.py:328
  90.4 3.0 %collective-permute-start.18 = (f32[96,128]{1,0:T(8,128)S(1)}, f32[96,128]{1,0:T(8,128)S(1)}, u32[]{:S(2)}, u32[]{:S(2)}) collective-permute-start(f32[96,128]{1,0:T(8,128)S(1)} %fusion.3), channel_id=1, source_target_pairs={{0,4},{2,6},{4,0},{6,2},{8,12},{10,14},{12,8},{14,10},{16,20},{18,... | collective-permute-start | bytes 147464 | tf_op jit(solution)/shard_map/ppermute | solution.py:328
  93.4 5.4 %collective-permute-start.19 = (f32[192,128]{1,0:T(8,128)S(1)}, f32[192,128]{1,0:T(8,128)S(1)}, u32[]{:S(2)}, u32[]{:S(2)}) collective-permute-start(f32[192,128]{1,0:T(8,128)S(1)} %pad_maximum_fusion.4), channel_id=1, source_target_pairs={{0,1},{1,0},{2,3},{3,2},{4,5},{5,4},{6,7},{7,6},{8,9},{9,8},{10,11... | collective-permute-start | bytes 294920 | tf_op jit(solution)/shard_map/ppermute | solution.py:328
  98.8 7.2 %collective-permute-start.20 = (f32[64,256]{1,0:T(8,128)S(1)}, f32[64,256]{1,0:T(8,128)S(1)}, u32[]{:S(2)}, u32[]{:S(2)}) collective-permute-start(f32[64,256]{1,0:T(8,128)S(1)} %slice.70), channel_id=1, source_target_pairs={{0,16},{2,18},{4,20},{6,22},{8,24},{10,26},{12,28},{14,30},{16,0},... | collective-permute-start | bytes 196616 | tf_op jit(solution)/shard_map/ppermute | solution.py:328
  106.1 4.4 %collective-permute-start.21 = (f32[64,256]{1,0:T(8,128)S(1)}, f32[64,256]{1,0:T(8,128)S(1)}, u32[]{:S(2)}, u32[]{:S(2)}) collective-permute-start(f32[64,256]{1,0:T(8,128)S(1)} %add.57), channel_id=1, source_target_pairs={{0,4},{2,6},{4,0},{6,2},{8,12},{10,14},{12,8},{14,10},{16,20},{18,... | collective-permute-start | bytes 196616 | tf_op jit(solution)/shard_map/ppermute | solution.py:328
  110.6 3.2 %collective-permute-start.22 = (f32[64,256]{1,0:T(8,128)S(1)}, f32[64,256]{1,0:T(8,128)S(1)}, u32[]{:S(2)}, u32[]{:S(2)}) collective-permute-start(f32[64,256]{1,0:T(8,128)S(1)} %add.58), channel_id=1, source_target_pairs={{0,2},{2,0},{4,6},{6,4},{8,10},{10,8},{12,14},{14,12},{16,18},{18,... | collective-permute-start | bytes 196616 | tf_op jit(solution)/shard_map/ppermute | solution.py:328
  113.8 2.8 %collective-permute-start.23 = (f32[128,256]{1,0:T(8,128)S(1)}, f32[128,256]{1,0:T(8,128)S(1)}, u32[]{:S(2)}, u32[]{:S(2)}) collective-permute-start(f32[128,256]{1,0:T(8,128)S(1)} %pad_maximum_fusion.2), channel_id=1, source_target_pairs={{0,1},{1,0},{2,3},{3,2},{4,5},{5,4},{6,7},{7,6},{8,9},{9,8},{10,11... | collective-permute-start | bytes 393224 | tf_op jit(solution)/shard_map/ppermute | solution.py:328
  (8 other events, 10.7 us)

commit v13 on v12

--- a/solution.py
+++ b/solution.py
@@ -77,13 +77,32 @@
     pltpu.sync_copy(blocks_ref, out_ref)
 
 
-def near_body(count, tokens, *refs):
-    cols_ref, live_ref, bases_ref, hessian_ref, region_ref, out_ref, *token_refs, slots_ref = refs
+def near_body(groups, tokens, linear, *refs):
+    cols_ref, live_ref, bases_ref, hessian_ref = refs[:4]
+    operands, refs = refs[4 : 4 + groups], refs[4 + groups :]
+    *terms, out_ref = refs[: len(refs) - 1 - tokens]
+    *token_refs, slots_ref = refs[len(refs) - 1 - tokens :]
     fill_slots(slots_ref, cols_ref, live_ref, 0, lambda name: name)
-    total = accumulate(slots_ref, hessian_ref, region_ref, 0, None)
-    out_ref[...] = total
+    total = None
+    for at, operand_ref in enumerate(operands):
+        total = accumulate(slots_ref, hessian_ref, operand_ref, bases_ref[at], total)
+    out_ref[...] = linear(total, *terms)
     for token_ref in token_refs:
         token_ref[...] = total[:GROUP, :TILE]
+
+
+def no_terms(total):
+    return total
+
+
+def first_terms(total, bounds_ref, vectors_ref):
+    centre, _ = interval(bounds_ref)
+    return total - centre * vectors_ref[...]
+
+
+def second_terms(total, bounds_ref, one_ref, vectors_ref):
+    centre, half = interval(bounds_ref)
+    return total - centre * one_ref[...] - (0.5 * half) * vectors_ref[...]
 
 
 def list_place(lists_ref, name):
@@ -116,22 +135,12 @@
     return 0.5 * (bounds_ref[0] + bounds_ref[1]), 0.5 * (bounds_ref[1] - bounds_ref[0])
 
 
-def first_body(which, *refs):
-    *operands, bounds_ref, vectors_ref, one_ref, cast_ref = refs
-    centre, half = interval(bounds_ref)
-    total = halo_total(which, *operands)
-    one = (total - centre * vectors_ref[...]) / half
-    one_ref[...] = one
-    cast_ref[...] = one.astype(jnp.bfloat16)
-
-
-def second_body(which, *refs):
-    *operands, bounds_ref, one_ref, vectors_ref, two_ref, cast_ref = refs
-    centre, half = interval(bounds_ref)
-    total = halo_total(which, *operands)
-    two = 2.0 * (total - centre * one_ref[...]) / half - vectors_ref[...]
-    two_ref[...] = two
-    cast_ref[...] = two.astype(jnp.bfloat16)
+def scaled_body(which, factor, *refs):
+    *operands, bounds_ref, out_ref, cast_ref = refs
+    _, half = interval(bounds_ref)
+    value = factor * halo_total(which, *operands) / half
+    out_ref[...] = value
+    cast_ref[...] = value.astype(jnp.bfloat16)
 
 
 def place_rows(number_ref, piece, rows):
@@ -414,12 +423,15 @@
     if whole:
         first = jnp.concatenate([first, listed.astype(jnp.bfloat16)], 0)
 
-    def exchange(operand):
-        region = lax.all_gather(operand, "split", axis=0)
-        up, down = sent(operand, region)
-        return region, shifted(up, "region", 1), shifted(down, "region", -1)
-
-    first_region, first_lower, first_upper = exchange(first)
+    def exchange(operand, gather=True):
+        if gather or not paired:
+            groups = [lax.all_gather(operand, "split", axis=0)]
+        else:
+            groups = [operand[None], swapped(operand)[None]]
+        up, down = sent(operand, groups[0])
+        return groups, shifted(up, "region", 1), shifted(down, "region", -1)
+
+    first_near, first_lower, first_upper = exchange(first)
     if whole:
         orders = [first_lower[rows + 1, :halo_blocks], first_upper[rows, :halo_blocks]]
         lists = jnp.stack(orders).astype(jnp.int32)
@@ -450,16 +462,17 @@
         compiler_params=pltpu.CompilerParams(vmem_limit_bytes=VMEM_LIMIT),
     )(hessian)
 
-    def near_total(region, tokens=()):
+    def near_total(groups, linear, scalars=(), terms=(), tokens=()):
         call = kernel_call(
-            functools.partial(near_body, region_blocks, len(tokens)),
+            functools.partial(near_body, len(groups), len(tokens), linear),
             (wide,) + tokens,
-            [SMEM] * 3 + [VMEM] * 2,
+            [SMEM] * 3 + [VMEM] * (1 + len(groups)) + [SMEM] * len(scalars) + [VMEM] * len(terms),
             free,
             traffic,
             (row_blocks, region_blocks + 1),
         )
-        return call(block_cols, live_blocks, bases, held, region)
+        near_bases = bases if len(groups) > 1 else jnp.zeros_like(bases)
+        return call(block_cols, live_blocks, near_bases, held, *groups, *scalars, *terms)
 
     def halo_part(body, outs, table, pair, total, scalars=(), extra=()):
         specs = [SMEM] * 2 + [VMEM] * 4 + [SMEM] * len(scalars) + [VMEM] * len(extra)
@@ -470,7 +483,7 @@
         *pairs, last = zip(gathered(lower), gathered(upper))
         return pairs, last
 
-    (total,) = near_total(first_region)
+    (total,) = near_total(first_near, first_terms, (bounds,), (vectors,))
     pairs, last = pairs_of(first_lower, first_upper)
     pairs.append(last)
     body_of = functools.partial(table_body, region_blocks, 0)
@@ -481,19 +494,19 @@
         pairs.append(tuple(jnp.zeros_like(part) for part in last))
     total, table = call(block_cols, live_blocks, lists, bases, held, *pairs[0], total)
     which = len(pairs) - 1 if paired else 0
-    body_of = functools.partial(first_body, which)
-    one, one_cast = halo_part(body_of, (wide, narrow), table, pairs[-1], total, (bounds,), (vectors,))
-
-    region, lower, upper = exchange(one_cast)
-    (total,) = near_total(region)
+    body_of = functools.partial(scaled_body, which, 1.0)
+    one, one_cast = halo_part(body_of, (wide, narrow), table, pairs[-1], total, (bounds,))
+
+    own, lower, upper = exchange(one_cast)
+    (total,) = near_total(own, second_terms, (bounds,), (one, vectors))
     pairs, last = pairs_of(lower, upper)
     for which, pair in enumerate(pairs):
         (total,) = halo_part(functools.partial(middle_body, which), (wide,), table, pair, total)
-    body_of = functools.partial(second_body, len(pairs))
-    two, two_cast = halo_part(body_of, (wide, narrow), table, last, total, (bounds,), (one, vectors))
-
-    region, lower, upper = exchange(two_cast)
-    total, after = near_total(region, (token,))
+    body_of = functools.partial(scaled_body, len(pairs), 2.0)
+    two, two_cast = halo_part(body_of, (wide, narrow), table, last, total, (bounds,))
+
+    own, lower, upper = exchange(two_cast, gather=False)
+    total, after = near_total(own, no_terms, tokens=(token,))
     packed = jax.ShapeDtypeStruct((tile_rows, TILE), jnp.float32)
     gram = kernel_call(gram_body, packed, [SMEM, VMEM, VMEM], free, traffic)(gram_number, two, after)
     for step_of in [halving(*cores), halving(*across)]:
@@ -509,16 +522,17 @@
     fold = modes // TILE
     cut = gram.shape[0] // fold
     folded = jnp.concatenate([gram[at * cut : (at + 1) * cut] for at in range(fold)], 1)
+    flat = lambda value: [value[:, at * TILE : (at + 1) * TILE] for at in range(fold)]
     half = cross.shape[0] // 2
     got = partner_value(jnp.concatenate([folded, cross[half:]], 0), *near)
     both = jnp.concatenate([folded, cross[:half]], 0) + got
-    both = doubling(*between[0])(both)()
-    gram = jnp.concatenate([both[:cut, at * TILE : (at + 1) * TILE] for at in range(fold)], 0)
-    cross = both[cut:]
-    for step_of in [doubling(*bit) for bit in between[1:]] + [joining(*across), joining(*cores)]:
-        gram = step_of(gram)()
+    for bit in between:
+        both = doubling(*bit)(both)()
+    got = partner_value(both, *across)
+    gram = joining(*cores)(jnp.concatenate(flat(both[:cut]) + flat(got[:cut]), 0))()
+    cross = both[cut:] + got[cut:]
     stages = factor_stages(float(total_rows), modes // TILE, gram_number, two)
-    steps = [doubling(*bit) for bit in between[1:]] + [doubling(*across), joining(*near), joining(*cores)]
+    steps = [joining(*near), joining(*cores)]
     cross, (basis, inverse) = run_beside(cross, steps, gram, stages)
     body_of = functools.partial(projected_body, float(total_rows))
     call = kernel_call(body_of, square, [SMEM] + [VMEM] * 2, 2 * square_work, traffic)

time: 119 us -> 111 us (0.933)
  waiting for transfers between devices: 31.8 us -> 28.9 us
  blocking collectives: 8.48 us -> 5.59 us
  starting transfers between devices: 35 us -> 33.7 us
    ppermute x12 -> x10, waiting for transfers between devices: 21.7 us -> 15.2 us  [partner_value(): lax.ppermute(value, axis, [(at, at ^ bit) for at in range(lax.axis_size(a...]
    ppermute x6, waiting for transfers between devices: 10 us -> 13.6 us  [shifted(): return lax.ppermute(value, axis, pairs)]
    all_gather x3 -> x2, blocking collectives: 8.48 us -> 5.59 us  [exchange(): groups = [lax.all_gather(operand, 'split', axis=0)]]
    ppermute x12 -> x10, starting transfers between devices: 14.5 us -> 12.5 us  [partner_value(): lax.ppermute(value, axis, [(at, at ^ bit) for at in range(lax.axis_size(a...]
    pallas_call x5, Pallas kernels: 10.1 us -> 8.79 us  [halo_part(): return call(table, bases, held, *pair, total, *scalars, *extra)]
    ppermute x6 -> x7, starting transfers between devices: 6.18 us -> 6.95 us  [local(): swapped = lambda value: lax.ppermute(value, 'split', [(0, 1), (1, 0)])]
    unnamed x32 -> x24, local copies, waits for them, and re-layouts: 5.36 us -> 5.4 us
  transfers between devices with their start and end apart: 24 -> 23, of which waited for: 14 -> 12; matrix products, arithmetic and copies ran while one was open for 2% -> 2% of each run, Pallas kernels for 17% -> 21%
where the time goes in v13:
time: 111 us
  starting transfers between devices  33.7 us (30%)
  Pallas kernels  30.3 us (27%)
  waiting for transfers between devices  28.9 us (26%)
  local copies, waits for them, and re-layouts  7.45 us (7%)
  blocking collectives  5.59 us (5%)
  other arithmetic  3.69 us (3%)
    ppermute x10, waiting for transfers between devices, partner_value(): lax.ppermute(value, axis, [(at, at ^ bit) for at in range(lax.axis_size(a...  15.2 us
    ppermute x6, starting transfers between devices, shifted(): return lax.ppermute(value, axis, pairs)  14.3 us
    ppermute x6, waiting for transfers between devices, shifted(): return lax.ppermute(value, axis, pairs)  13.6 us
    ppermute x10, starting transfers between devices, partner_value(): lax.ppermute(value, axis, [(at, at ^ bit) for at in range(lax.axis_size(a...  12.5 us
    pallas_call x5, Pallas kernels, halo_part(): return call(table, bases, held, *pair, total, *scalars, *extra)  8.79 us
    ppermute x7, starting transfers between devices, local(): swapped = lambda value: lax.ppermute(value, 'split', [(0, 1), (1, 0)])  6.95 us
    all_gather x2, blocking collectives, exchange(): groups = [lax.all_gather(operand, 'split', axis=0)]  5.59 us
    unnamed x24, local copies, waits for them, and re-layouts  5.4 us
  transfers between devices with their start and end apart: 23, of which 12 were waited for; matrix products, arithmetic and copies ran while one was open for 2% of the time, Pallas kernels for 21%

profile of v13, /device:TPU:1, one launch (start us, length us, event | category | flops | bytes accessed | tf_op | source)
XLA Modules:
  0.0 110.6 jit_solution(10636305299655415285)
XLA Ops:
  3.2 2.0 %collective-permute-start = (bf16[592,256]{1,0:T(8,128)(2,1)}, bf16[592,256]{1,0:T(8,128)(2,1)}, u32[]{:S(2)}, u32[]{:S(2)}) collective-permute-start(bf16[592,256]{1,0:T(8,128)(2,1)} %fusion.1), channel_id=1, source_target_pairs={{0,2},{2,4},{4,6},{6,8},{8,10},{10,12},{12,14},{14,16},{16,18},{18... | collective-permute-start | bytes 909320 | tf_op jit(solution)/shard_map/ppermute | solution.py:27
  5.2 4.0 %collective-permute-start.1 = (bf16[592,256]{1,0:T(8,128)(2,1)}, bf16[592,256]{1,0:T(8,128)(2,1)}, u32[]{:S(2)}, u32[]{:S(2)}) collective-permute-start(bf16[592,256]{1,0:T(8,128)(2,1)} %fusion.1), channel_id=1, source_target_pairs={{0,30},{2,0},{4,2},{6,4},{8,6},{10,8},{12,10},{14,12},{16,14},{18,... | collective-permute-start | bytes 909320 | tf_op jit(solution)/shard_map/ppermute | solution.py:27
  9.2 2.0 %copy-done.1 = bf16[3,12,192,192]{3,2,1,0:T(8,128)(2,1)S(1)} copy-done((bf16[3,12,192,192]{3,2,1,0:T(8,128)(2,1)S(1)}, bf16[3,12,192,192]{3,2,1,0:T(8,128)(2,1)}, u32[]{:S(2)}) %copy-start.1) | copy-done | bytes 2654232
  11.6 3.0 %all-gather = bf16[1184,256]{1,0:T(8,128)(2,1)S(1)} all-gather(bf16[592,256]{1,0:T(8,128)(2,1)} %fusion.1), channel_id=2, replica_groups=mesh['region'=16,'split'=2] {'split'}, dimensions={0}, use_global_device_ids=true | all-gather | bytes 909312 | tf_op jit(solution)/shard_map/all_gather | solution.py:428
  14.7 1.4 %shard_map.78.refs_4_ = f32[576,256]{1,0:T(8,128)S(1)} custom-call(s32[3,12]{1,0:T(4,128)S(1)} %copy-done.6, s32[3]{0:T(128)S(1)} %copy-done.7, s32[2]{0:T(128)S(1)} %broadcast_1_refs_2_.2.refs_2_, bf16[3,12,192,192]{3,2,1,0:T(8,128)(2,1)S(1)} %shard_map.77.refs_3_.refs_1_.refs_2_, bf16[2,592,256]{2,1,0:T(8,128)(2,1)S(1)} %bitcast.22, f32[2]{0:T(128)S(1)} %copy-done.8, ...), custom_call_target="tpu_custom_call" | custom-call | flops 10000000 | bytes 276480 | tf_op jit(solution)/shard_map/pallas_call | solution.py:475
  16.1 1.7 %collective-permute-done = bf16[592,256]{1,0:T(8,128)(2,1)} collective-permute-done((bf16[592,256]{1,0:T(8,128)(2,1)}, bf16[592,256]{1,0:T(8,128)(2,1)}, u32[]{:S(2)}, u32[]{:S(2)}) %collective-permute-start) | collective-permute-done | bytes 303136 | tf_op jit(solution)/shard_map/ppermute | solution.py:27
  20.5 1.6 %collective-permute-start.2 = (bf16[592,256]{1,0:T(8,128)(2,1)}, bf16[592,256]{1,0:T(8,128)(2,1)S(1)}, u32[]{:S(2)}, u32[]{:S(2)}) collective-permute-start(bf16[592,256]{1,0:T(8,128)(2,1)} %collective-permute-done), channel_id=1, source_target_pairs={{0,1},{1,0},{2,3},{3,2},{4,5},{5,4},{6,7},{7,6},{8,9},{9,8},{10,11... | collective-permute-start | bytes 909320 | tf_op jit(solution)/shard_map/ppermute | solution.py:401
  22.2 2.4 %shard_map.79 = (f32[576,256]{1,0:T(8,128)S(1)}, s32[3,13]{1,0:T(4,128)S(1)}) custom-call(s32[3,12]{1,0:T(4,128)S(1)} %copy-done.6, s32[3]{0:T(128)S(1)} %copy-done.7, s32[2,6]{1,0:T(2,128)S(1)} %maximum_convert_fusion.lists_ref, s32[2]{0:T(128)S(1)} %pad_add_fusion.refs_0_.refs_1_.refs_2_, bf16[3,12,192,192]{3,2,1,0:T(8,128)(2,1)S(1)} %shard_map.77.refs_3_.refs_1_.refs_2_, ...), custom_call_target="tpu_custom_call" | custom-call | flops 30000001024 | bytes 276480 | tf_op jit(solution)/shard_map/pallas_call | solution.py:495
  25.8 3.2 %collective-permute-start.6 = (bf16[576,256]{1,0:T(8,128)(2,1)S(1)}, bf16[576,256]{1,0:T(8,128)(2,1)S(1)}, u32[]{:S(2)}, u32[]{:S(2)}) collective-permute-start(bf16[576,256]{1,0:T(8,128)(2,1)S(1)} %get-tuple-element.35), channel_id=1, source_target_pairs={{0,30},{2,0},{4,2},{6,4},{8,6},{10,8},{12,10},{14,12},{16,14},{18,... | collective-permute-start | bytes 884744 | tf_op jit(solution)/shard_map/ppermute | solution.py:27
  29.0 2.6 %all-gather.1 = bf16[1152,256]{1,0:T(8,128)(2,1)S(1)} all-gather(bf16[576,256]{1,0:T(8,128)(2,1)S(1)} %get-tuple-element.35), channel_id=3, replica_groups=mesh['region'=16,'split'=2] {'split'}, dimensions={0}, use_global_device_ids=true | all-gather | bytes 884736 | tf_op jit(solution)/shard_map/all_gather | solution.py:428
  31.6 1.4 %shard_map.81.refs_5_ = f32[576,256]{1,0:T(8,128)S(1)} custom-call(s32[3,12]{1,0:T(4,128)S(1)} %copy-done.6, s32[3]{0:T(128)S(1)} %copy-done.7, s32[2]{0:T(128)S(1)} %broadcast_1_refs_2_.2.refs_2_, bf16[3,12,192,192]{3,2,1,0:T(8,128)(2,1)S(1)} %shard_map.77.refs_3_.refs_1_.refs_2_, bf16[2,576,256]{2,1,0:T(8,128)(2,1)S(1)} %bitcast.23, f32[2]{0:T(128)S(1)} %copy-done.8, ...), custom_call_target="tpu_custom_call" | custom-call | flops 10000000 | bytes 276480 | tf_op jit(solution)/shard_map/pallas_call | solution.py:475
  32.9 2.0 %collective-permute-done.6 = bf16[576,256]{1,0:T(8,128)(2,1)S(1)} collective-permute-done((bf16[576,256]{1,0:T(8,128)(2,1)S(1)}, bf16[576,256]{1,0:T(8,128)(2,1)S(1)}, u32[]{:S(2)}, u32[]{:S(2)}) %collective-permute-start.6) | collective-permute-done | bytes 294944 | tf_op jit(solution)/shard_map/ppermute | solution.py:27
  34.9 1.3 %collective-permute-start.7 = (bf16[576,256]{1,0:T(8,128)(2,1)S(1)}, bf16[576,256]{1,0:T(8,128)(2,1)S(1)}, u32[]{:S(2)}, u32[]{:S(2)}) collective-permute-start(bf16[576,256]{1,0:T(8,128)(2,1)S(1)} %collective-permute-done.6), channel_id=1, source_target_pairs={{0,1},{1,0},{2,3},{3,2},{4,5},{5,4},{6,7},{7,6},{8,9},{9,8},{10,11... | collective-permute-start | bytes 884744 | tf_op jit(solution)/shard_map/ppermute | solution.py:401
  36.2 4.2 %collective-permute-done.4 = bf16[576,256]{1,0:T(8,128)(2,1)S(1)} collective-permute-done((bf16[576,256]{1,0:T(8,128)(2,1)S(1)}, bf16[576,256]{1,0:T(8,128)(2,1)S(1)}, u32[]{:S(2)}, u32[]{:S(2)}) %collective-permute-start.4) | collective-permute-done | bytes 294944 | tf_op jit(solution)/shard_map/ppermute | solution.py:27
  40.4 1.7 %collective-permute-start.5 = (bf16[576,256]{1,0:T(8,128)(2,1)S(1)}, bf16[576,256]{1,0:T(8,128)(2,1)S(1)}, u32[]{:S(2)}, u32[]{:S(2)}) collective-permute-start(bf16[576,256]{1,0:T(8,128)(2,1)S(1)} %collective-permute-done.4), channel_id=1, source_target_pairs={{0,1},{1,0},{2,3},{3,2},{4,5},{5,4},{6,7},{7,6},{8,9},{9,8},{10,11... | collective-permute-start | bytes 884744 | tf_op jit(solution)/shard_map/ppermute | solution.py:401
  43.3 1.9 %shard_map.83 = (f32[576,256]{1,0:T(8,128)S(1)}, bf16[576,256]{1,0:T(8,128)(2,1)}) custom-call(s32[3,13]{1,0:T(4,128)S(1)} %get-tuple-element.33.refs_0_, s32[2]{0:T(128)S(1)} %pad_add_fusion.refs_0_.refs_1_.refs_2_, bf16[3,12,192,192]{3,2,1,0:T(8,128)(2,1)S(1)} %shard_map.77.refs_3_.refs_1_.refs_2_, bf16[1,576,256]{2,1,0:T(8,128)(2,1)S(1)} %bitcast.31, ...), custom_call_target="tpu_custom_call" | custom-call | flops 30000001024 | bytes 276480 | tf_op jit(solution)/shard_map/pallas_call | solution.py:480
  47.3 4.2 %collective-permute-start.12 = (bf16[576,256]{1,0:T(8,128)(2,1)}, bf16[576,256]{1,0:T(8,128)(2,1)}, u32[]{:S(2)}, u32[]{:S(2)}) collective-permute-start(bf16[576,256]{1,0:T(8,128)(2,1)} %get-tuple-element.38), channel_id=1, source_target_pairs={{0,30},{2,0},{4,2},{6,4},{8,6},{10,8},{12,10},{14,12},{16,14},{18,... | collective-permute-start | bytes 884744 | tf_op jit(solution)/shard_map/ppermute | solution.py:27
  51.5 1.9 %shard_map.84 = (f32[576,256]{1,0:T(8,128)S(1)}, f32[8,128]{1,0:T(8,128)S(1)}) custom-call(s32[3,12]{1,0:T(4,128)S(1)} %copy-done.6, s32[3]{0:T(128)S(1)} %copy-done.7, s32[2]{0:T(128)S(1)} %pad_add_fusion.refs_0_.refs_1_.refs_2_, bf16[3,12,192,192]{3,2,1,0:T(8,128)(2,1)S(1)} %shard_map.77.refs_3_.refs_1_.refs_2_, bf16[1,576,256]{2,1,0:T(8,128)(2,1)} %bitcast.14.refs_4_, ...), custom_call_target="tpu_custom_call" | custom-call | flops 10000000 | bytes 276480 | tf_op jit(solution)/shard_map/pallas_call | solution.py:475
  57.3 2.9 %collective-permute-done.11 = bf16[576,256]{1,0:T(8,128)(2,1)} collective-permute-done((bf16[576,256]{1,0:T(8,128)(2,1)}, bf16[576,256]{1,0:T(8,128)(2,1)}, u32[]{:S(2)}, u32[]{:S(2)}) %collective-permute-start.11) | collective-permute-done | bytes 294944 | tf_op jit(solution)/shard_map/ppermute | solution.py:27
  61.1 1.5 %collective-permute-done.12 = bf16[576,256]{1,0:T(8,128)(2,1)} collective-permute-done((bf16[576,256]{1,0:T(8,128)(2,1)}, bf16[576,256]{1,0:T(8,128)(2,1)}, u32[]{:S(2)}, u32[]{:S(2)}) %collective-permute-start.12) | collective-permute-done | bytes 294944 | tf_op jit(solution)/shard_map/ppermute | solution.py:27
  66.5 1.7 %shard_map.86 = (f32[576,256]{1,0:T(8,128)S(1)}, f32[8,128]{1,0:T(8,128)S(1)}) custom-call(s32[3,13]{1,0:T(4,128)S(1)} %get-tuple-element.33.refs_0_, s32[2]{0:T(128)S(1)} %pad_add_fusion.refs_0_.refs_1_.refs_2_, bf16[3,12,192,192]{3,2,1,0:T(8,128)(2,1)S(1)} %shard_map.77.refs_3_.refs_1_.refs_2_, bf16[1,576,256]{2,1,0:T(8,128)(2,1)} %bitcast.16.refs_3_, ...), custom_call_target="tpu_custom_call" | custom-call | flops 30000001024 | bytes 276480 | tf_op jit(solution)/shard_map/pallas_call | solution.py:480
  68.3 2.8 %shard_map.87 = f32[256,256]{1,0:T(8,128)S(1)} custom-call(s32[3,13]{1,0:T(4,128)S(1)} %get-tuple-element.33.refs_0_, s32[2]{0:T(128)S(1)} %pad_add_fusion.refs_0_.refs_1_.refs_2_, bf16[3,12,192,192]{3,2,1,0:T(8,128)(2,1)S(1)} %shard_map.77.refs_3_.refs_1_.refs_2_, bf16[1,576,256]{2,1,0:T(8,128)(2,1)S(1)} %bitcast.26, bf16[1,576,256]{2,1,0:T(8,128)(2,1)S(1)} %bitcast.27, ...), custom_call_target="tpu_custom_call" | custom-call | flops 30000001024 | bytes 276480 | tf_op jit(solution)/shard_map/pallas_call | solution.py:480
  73.3 3.9 %collective-permute-done.16 = f32[112,256]{1,0:T(8,128)S(1)} collective-permute-done((f32[112,256]{1,0:T(8,128)S(1)}, f32[112,256]{1,0:T(8,128)S(1)}, u32[]{:S(2)}, u32[]{:S(2)}) %collective-permute-start.16) | collective-permute-done | bytes 114720 | tf_op jit(solution)/shard_map/ppermute | solution.py:337
  78.2 2.7 %collective-permute-done.17 = f32[112,256]{1,0:T(8,128)S(1)} collective-permute-done((f32[112,256]{1,0:T(8,128)S(1)}, f32[112,256]{1,0:T(8,128)S(1)}, u32[]{:S(2)}, u32[]{:S(2)}) %collective-permute-start.17) | collective-permute-done | bytes 114720 | tf_op jit(solution)/shard_map/ppermute | solution.py:337
  80.9 2.0 %collective-permute-start.18 = (f32[112,256]{1,0:T(8,128)S(1)}, f32[112,256]{1,0:T(8,128)S(1)}, u32[]{:S(2)}, u32[]{:S(2)}) collective-permute-start(f32[112,256]{1,0:T(8,128)S(1)} %add.52), channel_id=1, source_target_pairs={{0,16},{2,18},{4,20},{6,22},{8,24},{10,26},{12,28},{14,30},{16,0},... | collective-permute-start | bytes 344072 | tf_op jit(solution)/shard_map/ppermute | solution.py:337
  82.9 3.8 %collective-permute-done.18 = f32[112,256]{1,0:T(8,128)S(1)} collective-permute-done((f32[112,256]{1,0:T(8,128)S(1)}, f32[112,256]{1,0:T(8,128)S(1)}, u32[]{:S(2)}, u32[]{:S(2)}) %collective-permute-start.18) | collective-permute-done | bytes 114720 | tf_op jit(solution)/shard_map/ppermute | solution.py:337
  87.6 2.9 %collective-permute-done.19 = f32[112,256]{1,0:T(8,128)S(1)} collective-permute-done((f32[112,256]{1,0:T(8,128)S(1)}, f32[112,256]{1,0:T(8,128)S(1)}, u32[]{:S(2)}, u32[]{:S(2)}) %collective-permute-start.19) | collective-permute-done | bytes 114720 | tf_op jit(solution)/shard_map/ppermute | solution.py:337
  90.5 4.7 %collective-permute-start.20 = (f32[192,128]{1,0:T(8,128)S(1)}, f32[192,128]{1,0:T(8,128)S(1)}, u32[]{:S(2)}, u32[]{:S(2)}) collective-permute-start(f32[192,128]{1,0:T(8,128)S(1)} %pad_maximum_fusion.3), channel_id=1, source_target_pairs={{0,1},{1,0},{2,3},{3,2},{4,5},{5,4},{6,7},{7,6},{8,9},{9,8},{10,11... | collective-permute-start | bytes 294920 | tf_op jit(solution)/shard_map/ppermute | solution.py:337
  96.7 5.2 %shard_map.88 = (f32[128,128]{1,0:T(8,128)S(1)}, f32[128,128]{1,0:T(8,128)S(1)}, f32[128,128]{1,0:T(8,128)S(1)}, f32[16,128]{1,0:T(8,128)S(1)}) custom-call(s32[1]{0:T(128)} %bitcast.number_ref, f32[384,128]{1,0:T(8,128)S(1)} %constant_dynamic-update-slice_fusion.gram_ref), custom_call_target="tpu_custom_call" | custom-call | flops 100000000 | bytes 3072 | tf_op jit(solution)/shard_map/pallas_call | solution.py:314
  101.9 4.4 %shard_map.89 = (f32[128,128]{1,0:T(8,128)S(1)}, f32[128,128]{1,0:T(8,128)S(1)}, f32[128,128]{1,0:T(8,128)S(1)}) custom-call(f32[128,128]{1,0:T(8,128)S(1)} %get-tuple-element.47.refs_0_, f32[128,128]{1,0:T(8,128)S(1)} %get-tuple-element.48.refs_1_, f32[128,128]{1,0:T(8,128)S(1)} %get-tuple-element.49.refs_2_), custom_call_target="tpu_custom_call" | custom-call | flops 100000000 | bytes 1024 | tf_op jit(solution)/shard_map/pallas_call | solution.py:320
  107.0 1.9 %shard_map.90 = (f32[576,256]{1,0:T(8,128)}, f32[256,256]{1,0:T(8,128)S(1)}) custom-call(f32[128,128]{1,0:T(8,128)S(1)} %get-tuple-element.55.refs_0_, f32[128,128]{1,0:T(8,128)S(1)} %get-tuple-element.56.refs_1_, f32[128,128]{1,0:T(8,128)S(1)} %get-tuple-element.57.refs_2_, f32[16,128]{1,0:T(8,128)S(1)} %get-tuple-element.58.refs_3_, f32[576,256]{1,0:T(8,128)S(1)} %copy-done.4), custom_call_target="tpu_custom_call" | custom-call | flops 100000000 | bytes 9216 | tf_op jit(solution)/shard_map/pallas_call | solution.py:327
  108.9 1.7 %shard_map.91 = f32[256,256]{1,0:T(8,128)} custom-call(s32[1]{0:T(128)} %bitcast.20.refs_6_.number_ref, f32[256,256]{1,0:T(8,128)S(1)} %pad_maximum_fusion.cross_ref, f32[256,256]{1,0:T(8,128)S(1)} %get-tuple-element.63.inverse_ref), custom_call_target="tpu_custom_call" | custom-call | flops 150994944 | bytes 276480 | tf_op jit(solution)/shard_map/pallas_call | solution.py:539
  (82 shorter events, 25.1 us)
Async XLA Ops:
  3.2 14.7 %collective-permute-start = (bf16[592,256]{1,0:T(8,128)(2,1)}, bf16[592,256]{1,0:T(8,128)(2,1)}, u32[]{:S(2)}, u32[]{:S(2)}) collective-permute-start(bf16[592,256]{1,0:T(8,128)(2,1)} %fusion.1), channel_id=1, source_target_pairs={{0,2},{2,4},{4,6},{6,8},{8,10},{10,12},{12,14},{14,16},{16,18},{18... | collective-permute-start | bytes 909320 | tf_op jit(solution)/shard_map/ppermute | solution.py:27
  5.2 14.6 %collective-permute-start.1 = (bf16[592,256]{1,0:T(8,128)(2,1)}, bf16[592,256]{1,0:T(8,128)(2,1)}, u32[]{:S(2)}, u32[]{:S(2)}) collective-permute-start(bf16[592,256]{1,0:T(8,128)(2,1)} %fusion.1), channel_id=1, source_target_pairs={{0,30},{2,0},{4,2},{6,4},{8,6},{10,8},{12,10},{14,12},{16,14},{18,... | collective-permute-start | bytes 909320 | tf_op jit(solution)/shard_map/ppermute | solution.py:27
  9.2 2.0 %copy-start.1 = (bf16[3,12,192,192]{3,2,1,0:T(8,128)(2,1)S(1)}, bf16[3,12,192,192]{3,2,1,0:T(8,128)(2,1)}, u32[]{:S(2)}) copy-start(bf16[3,12,192,192]{3,2,1,0:T(8,128)(2,1)} %blocks_ref.1) | copy-start | bytes 7962628
  11.2 3.5 %copy-start = (f32[576,256]{1,0:T(8,128)S(1)}, f32[576,256]{1,0:T(8,128)}, u32[]{:S(2)}) copy-start(f32[576,256]{1,0:T(8,128)} %refs_7_.1) | copy-start | bytes 1769476
  11.2 3.5 %copy-start.6 = (s32[3,12]{1,0:T(4,128)S(1)}, s32[3,12]{1,0:T(4,128)}, u32[]{:S(2)}) copy-start(s32[3,12]{1,0:T(4,128)} %refs_0_.5) | copy-start | bytes 436
  11.2 3.5 %copy-start.7 = (s32[3]{0:T(128)S(1)}, s32[3]{0:T(128)}, u32[]{:S(2)}) copy-start(s32[3]{0:T(128)} %refs_1_.5) | copy-start | bytes 40
  11.2 3.5 %copy-start.8 = (f32[2]{0:T(128)S(1)}, f32[2]{0:T(128)}, u32[]{:S(2)}) copy-start(f32[2]{0:T(128)} %refs_6_.5) | copy-start | bytes 28
  20.5 4.1 %collective-permute-start.2 = (bf16[592,256]{1,0:T(8,128)(2,1)}, bf16[592,256]{1,0:T(8,128)(2,1)S(1)}, u32[]{:S(2)}, u32[]{:S(2)}) collective-permute-start(bf16[592,256]{1,0:T(8,128)(2,1)} %collective-permute-done), channel_id=1, source_target_pairs={{0,1},{1,0},{2,3},{3,2},{4,5},{5,4},{6,7},{7,6},{8,9},{9,8},{10,11... | collective-permute-start | bytes 909320 | tf_op jit(solution)/shard_map/ppermute | solution.py:401
  22.1 2.5 %collective-permute-start.3 = (bf16[592,256]{1,0:T(8,128)(2,1)}, bf16[592,256]{1,0:T(8,128)(2,1)S(1)}, u32[]{:S(2)}, u32[]{:S(2)}) collective-permute-start(bf16[592,256]{1,0:T(8,128)(2,1)} %collective-permute-done.1), channel_id=1, source_target_pairs={{0,1},{1,0},{2,3},{3,2},{4,5},{5,4},{6,7},{7,6},{8,9},{9,8},{10,11... | collective-permute-start | bytes 909320 | tf_op jit(solution)/shard_map/ppermute | solution.py:401
  25.8 9.1 %collective-permute-start.6 = (bf16[576,256]{1,0:T(8,128)(2,1)S(1)}, bf16[576,256]{1,0:T(8,128)(2,1)S(1)}, u32[]{:S(2)}, u32[]{:S(2)}) collective-permute-start(bf16[576,256]{1,0:T(8,128)(2,1)S(1)} %get-tuple-element.35), channel_id=1, source_target_pairs={{0,30},{2,0},{4,2},{6,4},{8,6},{10,8},{12,10},{14,12},{16,14},{18,... | collective-permute-start | bytes 884744 | tf_op jit(solution)/shard_map/ppermute | solution.py:27
  29.0 11.4 %collective-permute-start.4 = (bf16[576,256]{1,0:T(8,128)(2,1)S(1)}, bf16[576,256]{1,0:T(8,128)(2,1)S(1)}, u32[]{:S(2)}, u32[]{:S(2)}) collective-permute-start(bf16[576,256]{1,0:T(8,128)(2,1)S(1)} %get-tuple-element.35), channel_id=1, source_target_pairs={{0,2},{2,4},{4,6},{6,8},{8,10},{10,12},{12,14},{14,16},{16,18},{18... | collective-permute-start | bytes 884744 | tf_op jit(solution)/shard_map/ppermute | solution.py:27
  34.9 8.4 %collective-permute-start.7 = (bf16[576,256]{1,0:T(8,128)(2,1)S(1)}, bf16[576,256]{1,0:T(8,128)(2,1)S(1)}, u32[]{:S(2)}, u32[]{:S(2)}) collective-permute-start(bf16[576,256]{1,0:T(8,128)(2,1)S(1)} %collective-permute-done.6), channel_id=1, source_target_pairs={{0,1},{1,0},{2,3},{3,2},{4,5},{5,4},{6,7},{7,6},{8,9},{9,8},{10,11... | collective-permute-start | bytes 884744 | tf_op jit(solution)/shard_map/ppermute | solution.py:401
  40.4 2.9 %collective-permute-start.5 = (bf16[576,256]{1,0:T(8,128)(2,1)S(1)}, bf16[576,256]{1,0:T(8,128)(2,1)S(1)}, u32[]{:S(2)}, u32[]{:S(2)}) collective-permute-start(bf16[576,256]{1,0:T(8,128)(2,1)S(1)} %collective-permute-done.4), channel_id=1, source_target_pairs={{0,1},{1,0},{2,3},{3,2},{4,5},{5,4},{6,7},{7,6},{8,9},{9,8},{10,11... | collective-permute-start | bytes 884744 | tf_op jit(solution)/shard_map/ppermute | solution.py:401
  46.1 5.4 %collective-permute-start.8 = (bf16[576,256]{1,0:T(8,128)(2,1)}, bf16[576,256]{1,0:T(8,128)(2,1)}, u32[]{:S(2)}, u32[]{:S(2)}) collective-permute-start(bf16[576,256]{1,0:T(8,128)(2,1)} %get-tuple-element.38), channel_id=1, source_target_pairs={{0,1},{1,0},{2,3},{3,2},{4,5},{5,4},{6,7},{7,6},{8,9},{9,8},{10,11... | collective-permute-start | bytes 884744 | tf_op jit(solution)/shard_map/ppermute | solution.py:401
  46.4 13.7 %collective-permute-start.11 = (bf16[576,256]{1,0:T(8,128)(2,1)}, bf16[576,256]{1,0:T(8,128)(2,1)}, u32[]{:S(2)}, u32[]{:S(2)}) collective-permute-start(bf16[576,256]{1,0:T(8,128)(2,1)} %get-tuple-element.38), channel_id=1, source_target_pairs={{0,2},{2,4},{4,6},{6,8},{8,10},{10,12},{12,14},{14,16},{16,18},{18... | collective-permute-start | bytes 884744 | tf_op jit(solution)/shard_map/ppermute | solution.py:27
  47.3 15.4 %collective-permute-start.12 = (bf16[576,256]{1,0:T(8,128)(2,1)}, bf16[576,256]{1,0:T(8,128)(2,1)}, u32[]{:S(2)}, u32[]{:S(2)}) collective-permute-start(bf16[576,256]{1,0:T(8,128)(2,1)} %get-tuple-element.38), channel_id=1, source_target_pairs={{0,30},{2,0},{4,2},{6,4},{8,6},{10,8},{12,10},{14,12},{16,14},{18,... | collective-permute-start | bytes 884744 | tf_op jit(solution)/shard_map/ppermute | solution.py:27
  51.5 2.7 %copy-start.3 = (f32[576,256]{1,0:T(8,128)S(1)}, f32[576,256]{1,0:T(8,128)}, u32[]{:S(2)}) copy-start(f32[576,256]{1,0:T(8,128)} %copy-done.2) | copy-start | bytes 1769476
  53.4 0.8 copy-start.9
  56.6 7.0 %collective-permute-start.9 = (f32[192,128]{1,0:T(8,128)}, f32[192,128]{1,0:T(8,128)}, u32[]{:S(2)}, u32[]{:S(2)}) collective-permute-start(f32[192,128]{1,0:T(8,128)} %slice.81), channel_id=1, source_target_pairs={{0,1},{1,0},{2,3},{3,2},{4,5},{5,4},{6,7},{7,6},{8,9},{9,8},{10,11... | collective-permute-start | bytes 294920 | tf_op jit(solution)/shard_map/ppermute | solution.py:337
  60.2 8.1 %collective-permute-start.13 = (bf16[576,256]{1,0:T(8,128)(2,1)}, bf16[576,256]{1,0:T(8,128)(2,1)S(1)}, u32[]{:S(2)}, u32[]{:S(2)}) collective-permute-start(bf16[576,256]{1,0:T(8,128)(2,1)} %collective-permute-done.11), channel_id=1, source_target_pairs={{0,1},{1,0},{2,3},{3,2},{4,5},{5,4},{6,7},{7,6},{8,9},{9,8},{10,11... | collective-permute-start | bytes 884744 | tf_op jit(solution)/shard_map/ppermute | solution.py:401
  62.6 5.6 %collective-permute-start.14 = (bf16[576,256]{1,0:T(8,128)(2,1)}, bf16[576,256]{1,0:T(8,128)(2,1)S(1)}, u32[]{:S(2)}, u32[]{:S(2)}) collective-permute-start(bf16[576,256]{1,0:T(8,128)(2,1)} %collective-permute-done.12), channel_id=1, source_target_pairs={{0,1},{1,0},{2,3},{3,2},{4,5},{5,4},{6,7},{7,6},{8,9},{9,8},{10,11... | collective-permute-start | bytes 884744 | tf_op jit(solution)/shard_map/ppermute | solution.py:401
  64.6 3.6 %collective-permute-start.10 = (f32[96,128]{1,0:T(8,128)S(1)}, f32[96,128]{1,0:T(8,128)S(1)}, u32[]{:S(2)}, u32[]{:S(2)}) collective-permute-start(f32[96,128]{1,0:T(8,128)S(1)} %slice.83), channel_id=1, source_target_pairs={{0,4},{2,6},{4,0},{6,2},{8,12},{10,14},{12,8},{14,10},{16,20},{18,... | collective-permute-start | bytes 147464 | tf_op jit(solution)/shard_map/ppermute | solution.py:337
  65.4 1.1 copy-start.10
  66.5 1.8 %copy-start.4 = (f32[576,256]{1,0:T(8,128)S(1)}, f32[576,256]{1,0:T(8,128)}, u32[]{:S(2)}) copy-start(f32[576,256]{1,0:T(8,128)} %copy-done.2) | copy-start | bytes 1769476
  71.0 1.6 %collective-permute-start.15 = (f32[128,256]{1,0:T(8,128)S(1)}, f32[128,256]{1,0:T(8,128)S(1)}, u32[]{:S(2)}, u32[]{:S(2)}) collective-permute-start(f32[128,256]{1,0:T(8,128)S(1)} %slice.85), channel_id=1, source_target_pairs={{0,1},{1,0},{2,3},{3,2},{4,5},{5,4},{6,7},{7,6},{8,9},{9,8},{10,11... | collective-permute-start | bytes 393224 | tf_op jit(solution)/shard_map/ppermute | solution.py:337
  72.7 4.4 %collective-permute-start.16 = (f32[112,256]{1,0:T(8,128)S(1)}, f32[112,256]{1,0:T(8,128)S(1)}, u32[]{:S(2)}, u32[]{:S(2)}) collective-permute-start(f32[112,256]{1,0:T(8,128)S(1)} %fusion.2), channel_id=1, source_target_pairs={{0,2},{2,0},{4,6},{6,4},{8,10},{10,8},{12,14},{14,12},{16,18},{18,... | collective-permute-start | bytes 344072 | tf_op jit(solution)/shard_map/ppermute | solution.py:337
  77.2 3.7 %collective-permute-start.17 = (f32[112,256]{1,0:T(8,128)S(1)}, f32[112,256]{1,0:T(8,128)S(1)}, u32[]{:S(2)}, u32[]{:S(2)}) collective-permute-start(f32[112,256]{1,0:T(8,128)S(1)} %maximum_add_fusion), channel_id=1, source_target_pairs={{0,8},{2,10},{4,12},{6,14},{8,0},{10,2},{12,4},{14,6},{16,24},{18,... | collective-permute-start | bytes 344072 | tf_op jit(solution)/shard_map/ppermute | solution.py:337
  80.9 5.8 %collective-permute-start.18 = (f32[112,256]{1,0:T(8,128)S(1)}, f32[112,256]{1,0:T(8,128)S(1)}, u32[]{:S(2)}, u32[]{:S(2)}) collective-permute-start(f32[112,256]{1,0:T(8,128)S(1)} %add.52), channel_id=1, source_target_pairs={{0,16},{2,18},{4,20},{6,22},{8,24},{10,26},{12,28},{14,30},{16,0},... | collective-permute-start | bytes 344072 | tf_op jit(solution)/shard_map/ppermute | solution.py:337
  86.8 3.7 %collective-permute-start.19 = (f32[112,256]{1,0:T(8,128)S(1)}, f32[112,256]{1,0:T(8,128)S(1)}, u32[]{:S(2)}, u32[]{:S(2)}) collective-permute-start(f32[112,256]{1,0:T(8,128)S(1)} %add.53), channel_id=1, source_target_pairs={{0,4},{2,6},{4,0},{6,2},{8,12},{10,14},{12,8},{14,10},{16,20},{18,... | collective-permute-start | bytes 344072 | tf_op jit(solution)/shard_map/ppermute | solution.py:337
  90.5 5.6 %collective-permute-start.20 = (f32[192,128]{1,0:T(8,128)S(1)}, f32[192,128]{1,0:T(8,128)S(1)}, u32[]{:S(2)}, u32[]{:S(2)}) collective-permute-start(f32[192,128]{1,0:T(8,128)S(1)} %pad_maximum_fusion.3), channel_id=1, source_target_pairs={{0,1},{1,0},{2,3},{3,2},{4,5},{5,4},{6,7},{7,6},{8,9},{9,8},{10,11... | collective-permute-start | bytes 294920 | tf_op jit(solution)/shard_map/ppermute | solution.py:337
  96.1 10.1 %collective-permute-start.21 = (f32[64,256]{1,0:T(8,128)S(1)}, f32[64,256]{1,0:T(8,128)S(1)}, u32[]{:S(2)}, u32[]{:S(2)}) collective-permute-start(f32[64,256]{1,0:T(8,128)S(1)} %slice_add_fusion.2), channel_id=1, source_target_pairs={{0,2},{2,0},{4,6},{6,4},{8,10},{10,8},{12,14},{14,12},{16,18},{18,... | collective-permute-start | bytes 196616 | tf_op jit(solution)/shard_map/ppermute | solution.py:337
  106.3 2.6 %collective-permute-start.22 = (f32[128,256]{1,0:T(8,128)S(1)}, f32[128,256]{1,0:T(8,128)S(1)}, u32[]{:S(2)}, u32[]{:S(2)}) collective-permute-start(f32[128,256]{1,0:T(8,128)S(1)} %pad_maximum_fusion.1), channel_id=1, source_target_pairs={{0,1},{1,0},{2,3},{3,2},{4,5},{5,4},{6,7},{7,6},{8,9},{9,8},{10,11... | collective-permute-start | bytes 393224 | tf_op jit(solution)/shard_map/ppermute | solution.py:337
  (2 other events, 1.5 us)

commit v14 on v13

--- a/solution.py
+++ b/solution.py
@@ -16,7 +16,7 @@
 GROUP = 8
 PIVOTS = 16
 TILE = 128
-VMEM_LIMIT = 12 * 1024 * 1024
+VMEM_LIMIT = 6 * 1024 * 1024
 LIST_ROWS = 16
 PIECES = 4
 

time: 111 us -> 111 us (level)
  no operation moved by 1% of the time
where the time goes in v14:
time: 111 us
  starting transfers between devices  33.8 us (30%)
  Pallas kernels  30.4 us (27%)
  waiting for transfers between devices  28.8 us (26%)
  local copies, waits for them, and re-layouts  7.45 us (7%)
  blocking collectives  5.59 us (5%)
  other arithmetic  3.69 us (3%)
    ppermute x10, waiting for transfers between devices, partner_value(): lax.ppermute(value, axis, [(at, at ^ bit) for at in range(lax.axis_size(a...  15.2 us
    ppermute x6, starting transfers between devices, shifted(): return lax.ppermute(value, axis, pairs)  14.3 us
    ppermute x6, waiting for transfers between devices, shifted(): return lax.ppermute(value, axis, pairs)  13.6 us
    ppermute x10, starting transfers between devices, partner_value(): lax.ppermute(value, axis, [(at, at ^ bit) for at in range(lax.axis_size(a...  12.5 us
    pallas_call x5, Pallas kernels, halo_part(): return call(table, bases, held, *pair, total, *scalars, *extra)  8.81 us
    ppermute x7, starting transfers between devices, local(): swapped = lambda value: lax.ppermute(value, 'split', [(0, 1), (1, 0)])  6.95 us
    all_gather x2, blocking collectives, exchange(): groups = [lax.all_gather(operand, 'split', axis=0)]  5.59 us
    unnamed x24, local copies, waits for them, and re-layouts  5.4 us
  transfers between devices with their start and end apart: 23, of which 12 were waited for; matrix products, arithmetic and copies ran while one was open for 2% of the time, Pallas kernels for 21%

profile of v14, /device:TPU:1, one launch (start us, length us, event | category | flops | bytes accessed | tf_op | source)
XLA Modules:
  0.0 110.6 jit_solution(6484153501670128877)
XLA Ops:
  3.2 2.0 %collective-permute-start = (bf16[592,256]{1,0:T(8,128)(2,1)}, bf16[592,256]{1,0:T(8,128)(2,1)}, u32[]{:S(2)}, u32[]{:S(2)}) collective-permute-start(bf16[592,256]{1,0:T(8,128)(2,1)} %fusion.1), channel_id=1, source_target_pairs={{0,2},{2,4},{4,6},{6,8},{8,10},{10,12},{12,14},{14,16},{16,18},{18... | collective-permute-start | bytes 909320 | tf_op jit(solution)/shard_map/ppermute | solution.py:27
  5.2 4.0 %collective-permute-start.1 = (bf16[592,256]{1,0:T(8,128)(2,1)}, bf16[592,256]{1,0:T(8,128)(2,1)}, u32[]{:S(2)}, u32[]{:S(2)}) collective-permute-start(bf16[592,256]{1,0:T(8,128)(2,1)} %fusion.1), channel_id=1, source_target_pairs={{0,30},{2,0},{4,2},{6,4},{8,6},{10,8},{12,10},{14,12},{16,14},{18,... | collective-permute-start | bytes 909320 | tf_op jit(solution)/shard_map/ppermute | solution.py:27
  9.2 2.0 %copy-done.1 = bf16[3,12,192,192]{3,2,1,0:T(8,128)(2,1)S(1)} copy-done((bf16[3,12,192,192]{3,2,1,0:T(8,128)(2,1)S(1)}, bf16[3,12,192,192]{3,2,1,0:T(8,128)(2,1)}, u32[]{:S(2)}) %copy-start.1) | copy-done | bytes 2654232
  11.6 3.0 %all-gather = bf16[1184,256]{1,0:T(8,128)(2,1)S(1)} all-gather(bf16[592,256]{1,0:T(8,128)(2,1)} %fusion.1), channel_id=2, replica_groups=mesh['region'=16,'split'=2] {'split'}, dimensions={0}, use_global_device_ids=true | all-gather | bytes 909312 | tf_op jit(solution)/shard_map/all_gather | solution.py:428
  14.7 1.4 %shard_map.78.refs_4_ = f32[576,256]{1,0:T(8,128)S(1)} custom-call(s32[3,12]{1,0:T(4,128)S(1)} %copy-done.6, s32[3]{0:T(128)S(1)} %copy-done.7, s32[2]{0:T(128)S(1)} %broadcast_1_refs_2_.2.refs_2_, bf16[3,12,192,192]{3,2,1,0:T(8,128)(2,1)S(1)} %shard_map.77.refs_3_.refs_1_.refs_2_, bf16[2,592,256]{2,1,0:T(8,128)(2,1)S(1)} %bitcast.22, f32[2]{0:T(128)S(1)} %copy-done.8, ...), custom_call_target="tpu_custom_call" | custom-call | flops 10000000 | bytes 276480 | tf_op jit(solution)/shard_map/pallas_call | solution.py:475
  16.1 1.7 %collective-permute-done = bf16[592,256]{1,0:T(8,128)(2,1)} collective-permute-done((bf16[592,256]{1,0:T(8,128)(2,1)}, bf16[592,256]{1,0:T(8,128)(2,1)}, u32[]{:S(2)}, u32[]{:S(2)}) %collective-permute-start) | collective-permute-done | bytes 303136 | tf_op jit(solution)/shard_map/ppermute | solution.py:27
  20.5 1.6 %collective-permute-start.2 = (bf16[592,256]{1,0:T(8,128)(2,1)}, bf16[592,256]{1,0:T(8,128)(2,1)S(1)}, u32[]{:S(2)}, u32[]{:S(2)}) collective-permute-start(bf16[592,256]{1,0:T(8,128)(2,1)} %collective-permute-done), channel_id=1, source_target_pairs={{0,1},{1,0},{2,3},{3,2},{4,5},{5,4},{6,7},{7,6},{8,9},{9,8},{10,11... | collective-permute-start | bytes 909320 | tf_op jit(solution)/shard_map/ppermute | solution.py:401
  22.2 2.4 %shard_map.79 = (f32[576,256]{1,0:T(8,128)S(1)}, s32[3,13]{1,0:T(4,128)S(1)}) custom-call(s32[3,12]{1,0:T(4,128)S(1)} %copy-done.6, s32[3]{0:T(128)S(1)} %copy-done.7, s32[2,6]{1,0:T(2,128)S(1)} %maximum_convert_fusion.lists_ref, s32[2]{0:T(128)S(1)} %pad_add_fusion.refs_0_.refs_1_.refs_2_, bf16[3,12,192,192]{3,2,1,0:T(8,128)(2,1)S(1)} %shard_map.77.refs_3_.refs_1_.refs_2_, ...), custom_call_target="tpu_custom_call" | custom-call | flops 30000001024 | bytes 276480 | tf_op jit(solution)/shard_map/pallas_call | solution.py:495
  25.8 3.2 %collective-permute-start.6 = (bf16[576,256]{1,0:T(8,128)(2,1)S(1)}, bf16[576,256]{1,0:T(8,128)(2,1)S(1)}, u32[]{:S(2)}, u32[]{:S(2)}) collective-permute-start(bf16[576,256]{1,0:T(8,128)(2,1)S(1)} %get-tuple-element.35), channel_id=1, source_target_pairs={{0,30},{2,0},{4,2},{6,4},{8,6},{10,8},{12,10},{14,12},{16,14},{18,... | collective-permute-start | bytes 884744 | tf_op jit(solution)/shard_map/ppermute | solution.py:27
  29.0 2.6 %all-gather.1 = bf16[1152,256]{1,0:T(8,128)(2,1)S(1)} all-gather(bf16[576,256]{1,0:T(8,128)(2,1)S(1)} %get-tuple-element.35), channel_id=3, replica_groups=mesh['region'=16,'split'=2] {'split'}, dimensions={0}, use_global_device_ids=true | all-gather | bytes 884736 | tf_op jit(solution)/shard_map/all_gather | solution.py:428
  31.6 1.4 %shard_map.81.refs_5_ = f32[576,256]{1,0:T(8,128)S(1)} custom-call(s32[3,12]{1,0:T(4,128)S(1)} %copy-done.6, s32[3]{0:T(128)S(1)} %copy-done.7, s32[2]{0:T(128)S(1)} %broadcast_1_refs_2_.2.refs_2_, bf16[3,12,192,192]{3,2,1,0:T(8,128)(2,1)S(1)} %shard_map.77.refs_3_.refs_1_.refs_2_, bf16[2,576,256]{2,1,0:T(8,128)(2,1)S(1)} %bitcast.23, f32[2]{0:T(128)S(1)} %copy-done.8, ...), custom_call_target="tpu_custom_call" | custom-call | flops 10000000 | bytes 276480 | tf_op jit(solution)/shard_map/pallas_call | solution.py:475
  32.9 2.0 %collective-permute-done.6 = bf16[576,256]{1,0:T(8,128)(2,1)S(1)} collective-permute-done((bf16[576,256]{1,0:T(8,128)(2,1)S(1)}, bf16[576,256]{1,0:T(8,128)(2,1)S(1)}, u32[]{:S(2)}, u32[]{:S(2)}) %collective-permute-start.6) | collective-permute-done | bytes 294944 | tf_op jit(solution)/shard_map/ppermute | solution.py:27
  34.9 1.3 %collective-permute-start.7 = (bf16[576,256]{1,0:T(8,128)(2,1)S(1)}, bf16[576,256]{1,0:T(8,128)(2,1)S(1)}, u32[]{:S(2)}, u32[]{:S(2)}) collective-permute-start(bf16[576,256]{1,0:T(8,128)(2,1)S(1)} %collective-permute-done.6), channel_id=1, source_target_pairs={{0,1},{1,0},{2,3},{3,2},{4,5},{5,4},{6,7},{7,6},{8,9},{9,8},{10,11... | collective-permute-start | bytes 884744 | tf_op jit(solution)/shard_map/ppermute | solution.py:401
  36.2 4.2 %collective-permute-done.4 = bf16[576,256]{1,0:T(8,128)(2,1)S(1)} collective-permute-done((bf16[576,256]{1,0:T(8,128)(2,1)S(1)}, bf16[576,256]{1,0:T(8,128)(2,1)S(1)}, u32[]{:S(2)}, u32[]{:S(2)}) %collective-permute-start.4) | collective-permute-done | bytes 294944 | tf_op jit(solution)/shard_map/ppermute | solution.py:27
  40.4 1.7 %collective-permute-start.5 = (bf16[576,256]{1,0:T(8,128)(2,1)S(1)}, bf16[576,256]{1,0:T(8,128)(2,1)S(1)}, u32[]{:S(2)}, u32[]{:S(2)}) collective-permute-start(bf16[576,256]{1,0:T(8,128)(2,1)S(1)} %collective-permute-done.4), channel_id=1, source_target_pairs={{0,1},{1,0},{2,3},{3,2},{4,5},{5,4},{6,7},{7,6},{8,9},{9,8},{10,11... | collective-permute-start | bytes 884744 | tf_op jit(solution)/shard_map/ppermute | solution.py:401
  43.3 1.9 %shard_map.83 = (f32[576,256]{1,0:T(8,128)S(1)}, bf16[576,256]{1,0:T(8,128)(2,1)}) custom-call(s32[3,13]{1,0:T(4,128)S(1)} %get-tuple-element.33.refs_0_, s32[2]{0:T(128)S(1)} %pad_add_fusion.refs_0_.refs_1_.refs_2_, bf16[3,12,192,192]{3,2,1,0:T(8,128)(2,1)S(1)} %shard_map.77.refs_3_.refs_1_.refs_2_, bf16[1,576,256]{2,1,0:T(8,128)(2,1)S(1)} %bitcast.31, ...), custom_call_target="tpu_custom_call" | custom-call | flops 30000001024 | bytes 276480 | tf_op jit(solution)/shard_map/pallas_call | solution.py:480
  47.3 4.2 %collective-permute-start.12 = (bf16[576,256]{1,0:T(8,128)(2,1)}, bf16[576,256]{1,0:T(8,128)(2,1)}, u32[]{:S(2)}, u32[]{:S(2)}) collective-permute-start(bf16[576,256]{1,0:T(8,128)(2,1)} %get-tuple-element.38), channel_id=1, source_target_pairs={{0,30},{2,0},{4,2},{6,4},{8,6},{10,8},{12,10},{14,12},{16,14},{18,... | collective-permute-start | bytes 884744 | tf_op jit(solution)/shard_map/ppermute | solution.py:27
  51.5 1.9 %shard_map.84 = (f32[576,256]{1,0:T(8,128)S(1)}, f32[8,128]{1,0:T(8,128)S(1)}) custom-call(s32[3,12]{1,0:T(4,128)S(1)} %copy-done.6, s32[3]{0:T(128)S(1)} %copy-done.7, s32[2]{0:T(128)S(1)} %pad_add_fusion.refs_0_.refs_1_.refs_2_, bf16[3,12,192,192]{3,2,1,0:T(8,128)(2,1)S(1)} %shard_map.77.refs_3_.refs_1_.refs_2_, bf16[1,576,256]{2,1,0:T(8,128)(2,1)} %bitcast.14.refs_4_, ...), custom_call_target="tpu_custom_call" | custom-call | flops 10000000 | bytes 276480 | tf_op jit(solution)/shard_map/pallas_call | solution.py:475
  57.3 2.9 %collective-permute-done.11 = bf16[576,256]{1,0:T(8,128)(2,1)} collective-permute-done((bf16[576,256]{1,0:T(8,128)(2,1)}, bf16[576,256]{1,0:T(8,128)(2,1)}, u32[]{:S(2)}, u32[]{:S(2)}) %collective-permute-start.11) | collective-permute-done | bytes 294944 | tf_op jit(solution)/shard_map/ppermute | solution.py:27
  61.1 1.5 %collective-permute-done.12 = bf16[576,256]{1,0:T(8,128)(2,1)} collective-permute-done((bf16[576,256]{1,0:T(8,128)(2,1)}, bf16[576,256]{1,0:T(8,128)(2,1)}, u32[]{:S(2)}, u32[]{:S(2)}) %collective-permute-start.12) | collective-permute-done | bytes 294944 | tf_op jit(solution)/shard_map/ppermute | solution.py:27
  66.5 1.7 %shard_map.86 = (f32[576,256]{1,0:T(8,128)S(1)}, f32[8,128]{1,0:T(8,128)S(1)}) custom-call(s32[3,13]{1,0:T(4,128)S(1)} %get-tuple-element.33.refs_0_, s32[2]{0:T(128)S(1)} %pad_add_fusion.refs_0_.refs_1_.refs_2_, bf16[3,12,192,192]{3,2,1,0:T(8,128)(2,1)S(1)} %shard_map.77.refs_3_.refs_1_.refs_2_, bf16[1,576,256]{2,1,0:T(8,128)(2,1)} %bitcast.16.refs_3_, ...), custom_call_target="tpu_custom_call" | custom-call | flops 30000001024 | bytes 276480 | tf_op jit(solution)/shard_map/pallas_call | solution.py:480
  68.3 2.8 %shard_map.87 = f32[256,256]{1,0:T(8,128)S(1)} custom-call(s32[3,13]{1,0:T(4,128)S(1)} %get-tuple-element.33.refs_0_, s32[2]{0:T(128)S(1)} %pad_add_fusion.refs_0_.refs_1_.refs_2_, bf16[3,12,192,192]{3,2,1,0:T(8,128)(2,1)S(1)} %shard_map.77.refs_3_.refs_1_.refs_2_, bf16[1,576,256]{2,1,0:T(8,128)(2,1)S(1)} %bitcast.26, bf16[1,576,256]{2,1,0:T(8,128)(2,1)S(1)} %bitcast.27, ...), custom_call_target="tpu_custom_call" | custom-call | flops 30000001024 | bytes 276480 | tf_op jit(solution)/shard_map/pallas_call | solution.py:480
  73.3 3.9 %collective-permute-done.16 = f32[112,256]{1,0:T(8,128)S(1)} collective-permute-done((f32[112,256]{1,0:T(8,128)S(1)}, f32[112,256]{1,0:T(8,128)S(1)}, u32[]{:S(2)}, u32[]{:S(2)}) %collective-permute-start.16) | collective-permute-done | bytes 114720 | tf_op jit(solution)/shard_map/ppermute | solution.py:337
  78.2 2.7 %collective-permute-done.17 = f32[112,256]{1,0:T(8,128)S(1)} collective-permute-done((f32[112,256]{1,0:T(8,128)S(1)}, f32[112,256]{1,0:T(8,128)S(1)}, u32[]{:S(2)}, u32[]{:S(2)}) %collective-permute-start.17) | collective-permute-done | bytes 114720 | tf_op jit(solution)/shard_map/ppermute | solution.py:337
  80.9 2.0 %collective-permute-start.18 = (f32[112,256]{1,0:T(8,128)S(1)}, f32[112,256]{1,0:T(8,128)S(1)}, u32[]{:S(2)}, u32[]{:S(2)}) collective-permute-start(f32[112,256]{1,0:T(8,128)S(1)} %add.52), channel_id=1, source_target_pairs={{0,16},{2,18},{4,20},{6,22},{8,24},{10,26},{12,28},{14,30},{16,0},... | collective-permute-start | bytes 344072 | tf_op jit(solution)/shard_map/ppermute | solution.py:337
  82.9 3.8 %collective-permute-done.18 = f32[112,256]{1,0:T(8,128)S(1)} collective-permute-done((f32[112,256]{1,0:T(8,128)S(1)}, f32[112,256]{1,0:T(8,128)S(1)}, u32[]{:S(2)}, u32[]{:S(2)}) %collective-permute-start.18) | collective-permute-done | bytes 114720 | tf_op jit(solution)/shard_map/ppermute | solution.py:337
  87.6 2.9 %collective-permute-done.19 = f32[112,256]{1,0:T(8,128)S(1)} collective-permute-done((f32[112,256]{1,0:T(8,128)S(1)}, f32[112,256]{1,0:T(8,128)S(1)}, u32[]{:S(2)}, u32[]{:S(2)}) %collective-permute-start.19) | collective-permute-done | bytes 114720 | tf_op jit(solution)/shard_map/ppermute | solution.py:337
  90.5 4.7 %collective-permute-start.20 = (f32[192,128]{1,0:T(8,128)S(1)}, f32[192,128]{1,0:T(8,128)S(1)}, u32[]{:S(2)}, u32[]{:S(2)}) collective-permute-start(f32[192,128]{1,0:T(8,128)S(1)} %pad_maximum_fusion.3), channel_id=1, source_target_pairs={{0,1},{1,0},{2,3},{3,2},{4,5},{5,4},{6,7},{7,6},{8,9},{9,8},{10,11... | collective-permute-start | bytes 294920 | tf_op jit(solution)/shard_map/ppermute | solution.py:337
  96.7 5.2 %shard_map.88 = (f32[128,128]{1,0:T(8,128)S(1)}, f32[128,128]{1,0:T(8,128)S(1)}, f32[128,128]{1,0:T(8,128)S(1)}, f32[16,128]{1,0:T(8,128)S(1)}) custom-call(s32[1]{0:T(128)} %bitcast.number_ref, f32[384,128]{1,0:T(8,128)S(1)} %constant_dynamic-update-slice_fusion.gram_ref), custom_call_target="tpu_custom_call" | custom-call | flops 100000000 | bytes 3072 | tf_op jit(solution)/shard_map/pallas_call | solution.py:314
  101.9 4.4 %shard_map.89 = (f32[128,128]{1,0:T(8,128)S(1)}, f32[128,128]{1,0:T(8,128)S(1)}, f32[128,128]{1,0:T(8,128)S(1)}) custom-call(f32[128,128]{1,0:T(8,128)S(1)} %get-tuple-element.47.refs_0_, f32[128,128]{1,0:T(8,128)S(1)} %get-tuple-element.48.refs_1_, f32[128,128]{1,0:T(8,128)S(1)} %get-tuple-element.49.refs_2_), custom_call_target="tpu_custom_call" | custom-call | flops 100000000 | bytes 1024 | tf_op jit(solution)/shard_map/pallas_call | solution.py:320
  107.0 1.9 %shard_map.90 = (f32[576,256]{1,0:T(8,128)}, f32[256,256]{1,0:T(8,128)S(1)}) custom-call(f32[128,128]{1,0:T(8,128)S(1)} %get-tuple-element.55.refs_0_, f32[128,128]{1,0:T(8,128)S(1)} %get-tuple-element.56.refs_1_, f32[128,128]{1,0:T(8,128)S(1)} %get-tuple-element.57.refs_2_, f32[16,128]{1,0:T(8,128)S(1)} %get-tuple-element.58.refs_3_, f32[576,256]{1,0:T(8,128)S(1)} %copy-done.4), custom_call_target="tpu_custom_call" | custom-call | flops 100000000 | bytes 9216 | tf_op jit(solution)/shard_map/pallas_call | solution.py:327
  108.9 1.7 %shard_map.91 = f32[256,256]{1,0:T(8,128)} custom-call(s32[1]{0:T(128)} %bitcast.20.refs_6_.number_ref, f32[256,256]{1,0:T(8,128)S(1)} %pad_maximum_fusion.cross_ref, f32[256,256]{1,0:T(8,128)S(1)} %get-tuple-element.63.inverse_ref), custom_call_target="tpu_custom_call" | custom-call | flops 150994944 | bytes 276480 | tf_op jit(solution)/shard_map/pallas_call | solution.py:539
  (82 shorter events, 25.1 us)
Async XLA Ops:
  3.2 14.7 %collective-permute-start = (bf16[592,256]{1,0:T(8,128)(2,1)}, bf16[592,256]{1,0:T(8,128)(2,1)}, u32[]{:S(2)}, u32[]{:S(2)}) collective-permute-start(bf16[592,256]{1,0:T(8,128)(2,1)} %fusion.1), channel_id=1, source_target_pairs={{0,2},{2,4},{4,6},{6,8},{8,10},{10,12},{12,14},{14,16},{16,18},{18... | collective-permute-start | bytes 909320 | tf_op jit(solution)/shard_map/ppermute | solution.py:27
  5.2 14.6 %collective-permute-start.1 = (bf16[592,256]{1,0:T(8,128)(2,1)}, bf16[592,256]{1,0:T(8,128)(2,1)}, u32[]{:S(2)}, u32[]{:S(2)}) collective-permute-start(bf16[592,256]{1,0:T(8,128)(2,1)} %fusion.1), channel_id=1, source_target_pairs={{0,30},{2,0},{4,2},{6,4},{8,6},{10,8},{12,10},{14,12},{16,14},{18,... | collective-permute-start | bytes 909320 | tf_op jit(solution)/shard_map/ppermute | solution.py:27
  9.2 2.0 %copy-start.1 = (bf16[3,12,192,192]{3,2,1,0:T(8,128)(2,1)S(1)}, bf16[3,12,192,192]{3,2,1,0:T(8,128)(2,1)}, u32[]{:S(2)}) copy-start(bf16[3,12,192,192]{3,2,1,0:T(8,128)(2,1)} %blocks_ref.1) | copy-start | bytes 7962628
  11.2 3.5 %copy-start = (f32[576,256]{1,0:T(8,128)S(1)}, f32[576,256]{1,0:T(8,128)}, u32[]{:S(2)}) copy-start(f32[576,256]{1,0:T(8,128)} %refs_7_.1) | copy-start | bytes 1769476
  11.2 3.5 %copy-start.6 = (s32[3,12]{1,0:T(4,128)S(1)}, s32[3,12]{1,0:T(4,128)}, u32[]{:S(2)}) copy-start(s32[3,12]{1,0:T(4,128)} %refs_0_.5) | copy-start | bytes 436
  11.2 3.5 %copy-start.7 = (s32[3]{0:T(128)S(1)}, s32[3]{0:T(128)}, u32[]{:S(2)}) copy-start(s32[3]{0:T(128)} %refs_1_.5) | copy-start | bytes 40
  11.2 3.5 %copy-start.8 = (f32[2]{0:T(128)S(1)}, f32[2]{0:T(128)}, u32[]{:S(2)}) copy-start(f32[2]{0:T(128)} %refs_6_.5) | copy-start | bytes 28
  20.5 4.1 %collective-permute-start.2 = (bf16[592,256]{1,0:T(8,128)(2,1)}, bf16[592,256]{1,0:T(8,128)(2,1)S(1)}, u32[]{:S(2)}, u32[]{:S(2)}) collective-permute-start(bf16[592,256]{1,0:T(8,128)(2,1)} %collective-permute-done), channel_id=1, source_target_pairs={{0,1},{1,0},{2,3},{3,2},{4,5},{5,4},{6,7},{7,6},{8,9},{9,8},{10,11... | collective-permute-start | bytes 909320 | tf_op jit(solution)/shard_map/ppermute | solution.py:401
  22.1 2.5 %collective-permute-start.3 = (bf16[592,256]{1,0:T(8,128)(2,1)}, bf16[592,256]{1,0:T(8,128)(2,1)S(1)}, u32[]{:S(2)}, u32[]{:S(2)}) collective-permute-start(bf16[592,256]{1,0:T(8,128)(2,1)} %collective-permute-done.1), channel_id=1, source_target_pairs={{0,1},{1,0},{2,3},{3,2},{4,5},{5,4},{6,7},{7,6},{8,9},{9,8},{10,11... | collective-permute-start | bytes 909320 | tf_op jit(solution)/shard_map/ppermute | solution.py:401
  25.8 9.1 %collective-permute-start.6 = (bf16[576,256]{1,0:T(8,128)(2,1)S(1)}, bf16[576,256]{1,0:T(8,128)(2,1)S(1)}, u32[]{:S(2)}, u32[]{:S(2)}) collective-permute-start(bf16[576,256]{1,0:T(8,128)(2,1)S(1)} %get-tuple-element.35), channel_id=1, source_target_pairs={{0,30},{2,0},{4,2},{6,4},{8,6},{10,8},{12,10},{14,12},{16,14},{18,... | collective-permute-start | bytes 884744 | tf_op jit(solution)/shard_map/ppermute | solution.py:27
  29.0 11.4 %collective-permute-start.4 = (bf16[576,256]{1,0:T(8,128)(2,1)S(1)}, bf16[576,256]{1,0:T(8,128)(2,1)S(1)}, u32[]{:S(2)}, u32[]{:S(2)}) collective-permute-start(bf16[576,256]{1,0:T(8,128)(2,1)S(1)} %get-tuple-element.35), channel_id=1, source_target_pairs={{0,2},{2,4},{4,6},{6,8},{8,10},{10,12},{12,14},{14,16},{16,18},{18... | collective-permute-start | bytes 884744 | tf_op jit(solution)/shard_map/ppermute | solution.py:27
  34.9 8.4 %collective-permute-start.7 = (bf16[576,256]{1,0:T(8,128)(2,1)S(1)}, bf16[576,256]{1,0:T(8,128)(2,1)S(1)}, u32[]{:S(2)}, u32[]{:S(2)}) collective-permute-start(bf16[576,256]{1,0:T(8,128)(2,1)S(1)} %collective-permute-done.6), channel_id=1, source_target_pairs={{0,1},{1,0},{2,3},{3,2},{4,5},{5,4},{6,7},{7,6},{8,9},{9,8},{10,11... | collective-permute-start | bytes 884744 | tf_op jit(solution)/shard_map/ppermute | solution.py:401
  40.4 2.9 %collective-permute-start.5 = (bf16[576,256]{1,0:T(8,128)(2,1)S(1)}, bf16[576,256]{1,0:T(8,128)(2,1)S(1)}, u32[]{:S(2)}, u32[]{:S(2)}) collective-permute-start(bf16[576,256]{1,0:T(8,128)(2,1)S(1)} %collective-permute-done.4), channel_id=1, source_target_pairs={{0,1},{1,0},{2,3},{3,2},{4,5},{5,4},{6,7},{7,6},{8,9},{9,8},{10,11... | collective-permute-start | bytes 884744 | tf_op jit(solution)/shard_map/ppermute | solution.py:401
  46.1 5.4 %collective-permute-start.8 = (bf16[576,256]{1,0:T(8,128)(2,1)}, bf16[576,256]{1,0:T(8,128)(2,1)}, u32[]{:S(2)}, u32[]{:S(2)}) collective-permute-start(bf16[576,256]{1,0:T(8,128)(2,1)} %get-tuple-element.38), channel_id=1, source_target_pairs={{0,1},{1,0},{2,3},{3,2},{4,5},{5,4},{6,7},{7,6},{8,9},{9,8},{10,11... | collective-permute-start | bytes 884744 | tf_op jit(solution)/shard_map/ppermute | solution.py:401
  46.4 13.7 %collective-permute-start.11 = (bf16[576,256]{1,0:T(8,128)(2,1)}, bf16[576,256]{1,0:T(8,128)(2,1)}, u32[]{:S(2)}, u32[]{:S(2)}) collective-permute-start(bf16[576,256]{1,0:T(8,128)(2,1)} %get-tuple-element.38), channel_id=1, source_target_pairs={{0,2},{2,4},{4,6},{6,8},{8,10},{10,12},{12,14},{14,16},{16,18},{18... | collective-permute-start | bytes 884744 | tf_op jit(solution)/shard_map/ppermute | solution.py:27
  47.3 15.4 %collective-permute-start.12 = (bf16[576,256]{1,0:T(8,128)(2,1)}, bf16[576,256]{1,0:T(8,128)(2,1)}, u32[]{:S(2)}, u32[]{:S(2)}) collective-permute-start(bf16[576,256]{1,0:T(8,128)(2,1)} %get-tuple-element.38), channel_id=1, source_target_pairs={{0,30},{2,0},{4,2},{6,4},{8,6},{10,8},{12,10},{14,12},{16,14},{18,... | collective-permute-start | bytes 884744 | tf_op jit(solution)/shard_map/ppermute | solution.py:27
  51.5 2.7 %copy-start.3 = (f32[576,256]{1,0:T(8,128)S(1)}, f32[576,256]{1,0:T(8,128)}, u32[]{:S(2)}) copy-start(f32[576,256]{1,0:T(8,128)} %copy-done.2) | copy-start | bytes 1769476
  53.4 0.8 copy-start.9
  56.6 7.0 %collective-permute-start.9 = (f32[192,128]{1,0:T(8,128)}, f32[192,128]{1,0:T(8,128)}, u32[]{:S(2)}, u32[]{:S(2)}) collective-permute-start(f32[192,128]{1,0:T(8,128)} %slice.81), channel_id=1, source_target_pairs={{0,1},{1,0},{2,3},{3,2},{4,5},{5,4},{6,7},{7,6},{8,9},{9,8},{10,11... | collective-permute-start | bytes 294920 | tf_op jit(solution)/shard_map/ppermute | solution.py:337
  60.2 8.1 %collective-permute-start.13 = (bf16[576,256]{1,0:T(8,128)(2,1)}, bf16[576,256]{1,0:T(8,128)(2,1)S(1)}, u32[]{:S(2)}, u32[]{:S(2)}) collective-permute-start(bf16[576,256]{1,0:T(8,128)(2,1)} %collective-permute-done.11), channel_id=1, source_target_pairs={{0,1},{1,0},{2,3},{3,2},{4,5},{5,4},{6,7},{7,6},{8,9},{9,8},{10,11... | collective-permute-start | bytes 884744 | tf_op jit(solution)/shard_map/ppermute | solution.py:401
  62.6 5.6 %collective-permute-start.14 = (bf16[576,256]{1,0:T(8,128)(2,1)}, bf16[576,256]{1,0:T(8,128)(2,1)S(1)}, u32[]{:S(2)}, u32[]{:S(2)}) collective-permute-start(bf16[576,256]{1,0:T(8,128)(2,1)} %collective-permute-done.12), channel_id=1, source_target_pairs={{0,1},{1,0},{2,3},{3,2},{4,5},{5,4},{6,7},{7,6},{8,9},{9,8},{10,11... | collective-permute-start | bytes 884744 | tf_op jit(solution)/shard_map/ppermute | solution.py:401
  64.6 3.6 %collective-permute-start.10 = (f32[96,128]{1,0:T(8,128)S(1)}, f32[96,128]{1,0:T(8,128)S(1)}, u32[]{:S(2)}, u32[]{:S(2)}) collective-permute-start(f32[96,128]{1,0:T(8,128)S(1)} %slice.83), channel_id=1, source_target_pairs={{0,4},{2,6},{4,0},{6,2},{8,12},{10,14},{12,8},{14,10},{16,20},{18,... | collective-permute-start | bytes 147464 | tf_op jit(solution)/shard_map/ppermute | solution.py:337
  65.4 1.1 copy-start.10
  66.5 1.8 %copy-start.4 = (f32[576,256]{1,0:T(8,128)S(1)}, f32[576,256]{1,0:T(8,128)}, u32[]{:S(2)}) copy-start(f32[576,256]{1,0:T(8,128)} %copy-done.2) | copy-start | bytes 1769476
  71.1 1.6 %collective-permute-start.15 = (f32[128,256]{1,0:T(8,128)S(1)}, f32[128,256]{1,0:T(8,128)S(1)}, u32[]{:S(2)}, u32[]{:S(2)}) collective-permute-start(f32[128,256]{1,0:T(8,128)S(1)} %slice.85), channel_id=1, source_target_pairs={{0,1},{1,0},{2,3},{3,2},{4,5},{5,4},{6,7},{7,6},{8,9},{9,8},{10,11... | collective-permute-start | bytes 393224 | tf_op jit(solution)/shard_map/ppermute | solution.py:337
  72.7 4.4 %collective-permute-start.16 = (f32[112,256]{1,0:T(8,128)S(1)}, f32[112,256]{1,0:T(8,128)S(1)}, u32[]{:S(2)}, u32[]{:S(2)}) collective-permute-start(f32[112,256]{1,0:T(8,128)S(1)} %fusion.2), channel_id=1, source_target_pairs={{0,2},{2,0},{4,6},{6,4},{8,10},{10,8},{12,14},{14,12},{16,18},{18,... | collective-permute-start | bytes 344072 | tf_op jit(solution)/shard_map/ppermute | solution.py:337
  77.2 3.7 %collective-permute-start.17 = (f32[112,256]{1,0:T(8,128)S(1)}, f32[112,256]{1,0:T(8,128)S(1)}, u32[]{:S(2)}, u32[]{:S(2)}) collective-permute-start(f32[112,256]{1,0:T(8,128)S(1)} %maximum_add_fusion), channel_id=1, source_target_pairs={{0,8},{2,10},{4,12},{6,14},{8,0},{10,2},{12,4},{14,6},{16,24},{18,... | collective-permute-start | bytes 344072 | tf_op jit(solution)/shard_map/ppermute | solution.py:337
  80.9 5.8 %collective-permute-start.18 = (f32[112,256]{1,0:T(8,128)S(1)}, f32[112,256]{1,0:T(8,128)S(1)}, u32[]{:S(2)}, u32[]{:S(2)}) collective-permute-start(f32[112,256]{1,0:T(8,128)S(1)} %add.52), channel_id=1, source_target_pairs={{0,16},{2,18},{4,20},{6,22},{8,24},{10,26},{12,28},{14,30},{16,0},... | collective-permute-start | bytes 344072 | tf_op jit(solution)/shard_map/ppermute | solution.py:337
  86.8 3.7 %collective-permute-start.19 = (f32[112,256]{1,0:T(8,128)S(1)}, f32[112,256]{1,0:T(8,128)S(1)}, u32[]{:S(2)}, u32[]{:S(2)}) collective-permute-start(f32[112,256]{1,0:T(8,128)S(1)} %add.53), channel_id=1, source_target_pairs={{0,4},{2,6},{4,0},{6,2},{8,12},{10,14},{12,8},{14,10},{16,20},{18,... | collective-permute-start | bytes 344072 | tf_op jit(solution)/shard_map/ppermute | solution.py:337
  90.5 5.6 %collective-permute-start.20 = (f32[192,128]{1,0:T(8,128)S(1)}, f32[192,128]{1,0:T(8,128)S(1)}, u32[]{:S(2)}, u32[]{:S(2)}) collective-permute-start(f32[192,128]{1,0:T(8,128)S(1)} %pad_maximum_fusion.3), channel_id=1, source_target_pairs={{0,1},{1,0},{2,3},{3,2},{4,5},{5,4},{6,7},{7,6},{8,9},{9,8},{10,11... | collective-permute-start | bytes 294920 | tf_op jit(solution)/shard_map/ppermute | solution.py:337
  96.2 10.1 %collective-permute-start.21 = (f32[64,256]{1,0:T(8,128)S(1)}, f32[64,256]{1,0:T(8,128)S(1)}, u32[]{:S(2)}, u32[]{:S(2)}) collective-permute-start(f32[64,256]{1,0:T(8,128)S(1)} %slice_add_fusion.2), channel_id=1, source_target_pairs={{0,2},{2,0},{4,6},{6,4},{8,10},{10,8},{12,14},{14,12},{16,18},{18,... | collective-permute-start | bytes 196616 | tf_op jit(solution)/shard_map/ppermute | solution.py:337
  106.3 2.6 %collective-permute-start.22 = (f32[128,256]{1,0:T(8,128)S(1)}, f32[128,256]{1,0:T(8,128)S(1)}, u32[]{:S(2)}, u32[]{:S(2)}) collective-permute-start(f32[128,256]{1,0:T(8,128)S(1)} %pad_maximum_fusion.1), channel_id=1, source_target_pairs={{0,1},{1,0},{2,3},{3,2},{4,5},{5,4},{6,7},{7,6},{8,9},{9,8},{10,11... | collective-permute-start | bytes 393224 | tf_op jit(solution)/shard_map/ppermute | solution.py:337
  (2 other events, 1.5 us)

commit v15 on v14

--- a/solution.py
+++ b/solution.py
@@ -14,7 +14,7 @@
 NT = (((1,), (1,)), ((), ()))
 TN = (((0,), (0,)), ((), ()))
 GROUP = 8
-PIVOTS = 16
+PANEL = 32
 TILE = 128
 VMEM_LIMIT = 6 * 1024 * 1024
 LIST_ROWS = 16
@@ -77,22 +77,20 @@
     pltpu.sync_copy(blocks_ref, out_ref)
 
 
-def near_body(groups, tokens, linear, *refs):
+def near_body(groups, linear, *refs):
     cols_ref, live_ref, bases_ref, hessian_ref = refs[:4]
-    operands, refs = refs[4 : 4 + groups], refs[4 + groups :]
-    *terms, out_ref = refs[: len(refs) - 1 - tokens]
-    *token_refs, slots_ref = refs[len(refs) - 1 - tokens :]
+    operands, (*terms, out_ref, slots_ref) = refs[4 : 4 + groups], refs[4 + groups :]
     fill_slots(slots_ref, cols_ref, live_ref, 0, lambda name: name)
     total = None
     for at, operand_ref in enumerate(operands):
         total = accumulate(slots_ref, hessian_ref, operand_ref, bases_ref[at], total)
     out_ref[...] = linear(total, *terms)
-    for token_ref in token_refs:
-        token_ref[...] = total[:GROUP, :TILE]
-
-
-def no_terms(total):
-    return total
+
+
+def near_gram_body(groups, *refs):
+    *operands, number_ref, two_ref, out_ref, gram_ref, slots_ref = refs
+    near_body(groups, lambda total: total, *operands, out_ref, slots_ref)
+    gram_part(number_ref, two_ref, gram_ref)
 
 
 def first_terms(total, bounds_ref, vectors_ref):
@@ -162,7 +160,7 @@
     return [(row, col) for row in range(count) for col in range(row + 1)]
 
 
-def gram_body(number_ref, two_ref, _, out_ref):
+def gram_part(number_ref, two_ref, out_ref):
     two = two_ref[...]
     cols = [two[:, at * TILE : (at + 1) * TILE] for at in range(two.shape[1] // TILE)]
     tiles = [exact_dot(cols[row], cols[col], TN) for row, col in lower_tiles(len(cols))]
@@ -184,73 +182,55 @@
 
 
 def eliminate(tile):
-    count = tile.shape[0] // PIVOTS
-    rows = [tile[index * PIVOTS : (index + 1) * PIVOTS, :] for index in range(count)]
+    count, panel = tile.shape[0] // GROUP, PANEL // GROUP
+    rows = [tile[index * GROUP : (index + 1) * GROUP, :] for index in range(count)]
     sub = lax.broadcasted_iota(jnp.int32, rows[0].shape, 0)
     lane = lax.broadcasted_iota(jnp.int32, rows[0].shape, 1)
-    for step in range(count):
-        start = step * PIVOTS
-        pivot_cols = [over_lanes(rows[step], start + col) for col in range(PIVOTS)]
-        factors = {
-            below: [over_lanes(rows[below], start + col) for col in range(PIVOTS)]
-            for below in range(step + 1, count)
-        }
-        inside = (lane >= start) & (lane < start + PIVOTS)
-        forward = jnp.where(inside, jnp.where(lane - start == sub, 1.0, 0.0), rows[step])
-        solved = forward
-        for one in range(0, PIVOTS, 2):
-            two = one + 1
-            left, right = pivot_cols[one], pivot_cols[two]
-            top, cross, low = over_rows(left, one), over_rows(left, two), over_rows(right, two)
-            inverse = 1.0 / (top * low - cross * cross)
-            top_inverse, cross_inverse, low_inverse = low * inverse, -(cross * inverse), top * inverse
-
-            def solve(value):
-                upper, lower = over_rows(value, one), over_rows(value, two)
-                return top_inverse * upper + cross_inverse * lower, cross_inverse * upper + low_inverse * lower
-
-            def without(value, upper, lower):
-                return value - (left * upper + right * lower)
-
-            def reduced(value):
-                upper, lower = solve(value)
-                return jnp.where(sub == one, upper, jnp.where(sub == two, lower, without(value, upper, lower)))
-
-            for col in range(two + 1, PIVOTS):
-                pivot_cols[col] = reduced(pivot_cols[col])
-            upper, lower = solve(forward)
-            over_top = 1.0 / top
-            first, second = over_rows(forward, one), over_rows(forward, two)
-            below_first = (second - cross * over_top * first) * lax.rsqrt(low - cross * cross * over_top)
-            below = jnp.where(sub > two, without(forward, upper, lower), forward)
-            solved = reduced(solved)
-            forward = jnp.where(sub == one, first * lax.rsqrt(top), jnp.where(sub == two, below_first, below))
-        rows[step] = jnp.where(lane < start + PIVOTS, forward, 0.0)
-        solved_rows = [over_rows(solved, pivot) for pivot in range(PIVOTS)]
-        for below in range(step + 1, count):
-            terms = [factors[below][col] * solved_rows[col] for col in range(PIVOTS)]
-            while len(terms) > 1:
-                terms = [terms[at] + terms[at + 1] for at in range(0, len(terms), 2)]
-            rows[below] = jnp.where(inside, 0.0, rows[below]) - terms[0]
+    for begin in range(0, count, panel):
+        end = begin + panel
+        reduced = []
+        for step in range(begin, end):
+            start = step * GROUP
+            pivot_cols = [over_lanes(rows[step], start + col) for col in range(GROUP)]
+            factors = {
+                below: [over_lanes(rows[below], start + col) for col in range(GROUP)] for below in range(step + 1, end)
+            }
+            inside = (lane >= start) & (lane < start + GROUP)
+            forward = jnp.where(inside, jnp.where(lane - start == sub, 1.0, 0.0), rows[step])
+            solved = forward
+            for pivot in range(GROUP):
+                here = sub == pivot
+                value = over_rows(pivot_cols[pivot], pivot)
+                inverse = 1.0 / value
+                ratio = pivot_cols[pivot] * inverse
+                row = over_rows(forward, pivot)
+                below_row = jnp.where(sub > pivot, forward - ratio * row, forward)
+                forward = jnp.where(here, row * lax.rsqrt(value), below_row)
+                solved = jnp.where(here, row * inverse, solved - ratio * row)
+                for col in range(pivot + 1, GROUP):
+                    top = over_rows(pivot_cols[col], pivot)
+                    pivot_cols[col] = jnp.where(here, top * inverse, pivot_cols[col] - ratio * top)
+            own_part = (lane < start + GROUP) | (lane >= end * GROUP)
+            reduced.append((forward, jnp.where(own_part, forward, 0.0)))
+            rows[step] = jnp.where(lane < start + GROUP, forward, 0.0)
+            solved_rows = [over_rows(solved, pivot) for pivot in range(GROUP)]
+            for below in range(step + 1, end):
+                terms = [factors[below][col] * solved_rows[col] for col in range(GROUP)]
+                while len(terms) > 1:
+                    terms = [terms[at] + terms[at + 1] for at in range(0, len(terms), 2)]
+                rows[below] = jnp.where(inside, 0.0, rows[below]) - terms[0]
+        if end < count:
+            factor_rows, solved_rows = [jnp.concatenate(parts, 0) for parts in zip(*reduced)]
+            share = exact_dot(factor_rows, solved_rows, TN)
+            inside = (lane >= begin * GROUP) & (lane < end * GROUP)
+            for below in range(end, count):
+                rows[below] = jnp.where(inside, 0.0, rows[below]) - share[below * GROUP : (below + 1) * GROUP, :]
     return jnp.concatenate(rows, 0)
 
 
-def scaled_tiles(tiles, count):
-    names = lower_tiles(count)
-    index = lambda dim: lax.broadcasted_iota(jnp.int32, (TILE, TILE), dim)
-    diagonal = {row: jnp.where(index(0) == index(1), tiles[names.index((row, row))], 0.0) for row in range(count)}
-    down = {row: lax.rsqrt(jnp.sum(diagonal[row], 1, keepdims=True)) for row in range(count)}
-    along = {row: lax.rsqrt(jnp.sum(diagonal[row], 0, keepdims=True)) for row in range(count)}
-    return [tile * down[row] * along[col] for (row, col), tile in zip(names, tiles)], along
-
-
-def first_tile_body(count, total_rows, number_ref, gram_ref, *refs):
-    *tile_refs, scale_ref = refs
+def first_tile_body(count, total_rows, number_ref, gram_ref, *tile_refs):
     packed = ordered_pieces(number_ref, gram_ref) / total_rows
     tiles = [packed[at * TILE : (at + 1) * TILE, :] for at in range(len(tile_refs))]
-    tiles, along = scaled_tiles(tiles, count)
-    for row in range(count):
-        scale_ref[row * GROUP : (row + 1) * GROUP, :] = jnp.broadcast_to(along[row], (GROUP, TILE))
     finish_tile(0, count, dict(zip(lower_tiles(count), tiles)), tile_refs)
 
 
@@ -273,7 +253,7 @@
 
 
 def basis_body(count, *refs):
-    *tile_refs, scale_ref, two_ref, basis_ref, inverse_ref = refs
+    *tile_refs, two_ref, basis_ref, inverse_ref = refs
     tiles = {name: ref[...] for name, ref in zip(lower_tiles(count), tile_refs)}
     inverse = {}
     for row in range(count):
@@ -286,9 +266,7 @@
     zero = jnp.zeros((TILE, TILE), jnp.float32)
     whole = jnp.concatenate(
         [
-            jnp.concatenate(
-                [inverse[row, col] * scale_ref[col * GROUP, :][None] if col <= row else zero for col in range(count)], 1
-            )
+            jnp.concatenate([inverse[row, col] if col <= row else zero for col in range(count)], 1)
             for row in range(count)
         ],
         0,
@@ -305,26 +283,25 @@
 def factor_stages(total_rows, count, number, two):
     rows, modes = two.shape
     tile = jax.ShapeDtypeStruct((TILE, TILE), jnp.float32)
-    scale = jax.ShapeDtypeStruct((count * GROUP, TILE), jnp.float32)
     names = lower_tiles(count)
     work = 10**8
 
     def first(gram):
         body = functools.partial(first_tile_body, count, total_rows)
-        return tuple(kernel_call(body, (tile,) * len(names) + (scale,), [SMEM, VMEM], work, gram.size)(number, gram))
+        return tuple(kernel_call(body, (tile,) * len(names), [SMEM, VMEM], work, gram.size)(number, gram))
 
     def following(at):
         def stage(state):
             body = functools.partial(next_tile_body, at, count)
             call = kernel_call(body, (tile,) * len(names), [VMEM] * len(names), work, TILE * TILE)
-            return tuple(call(*state[:-1])) + state[-1:]
+            return tuple(call(*state))
 
         return stage
 
     def finish(state):
         outs = (jax.ShapeDtypeStruct((rows, modes), jnp.float32), jax.ShapeDtypeStruct((modes, modes), jnp.float32))
         body = functools.partial(basis_body, count)
-        return tuple(kernel_call(body, outs, [VMEM] * (len(names) + 2), work, rows * modes)(*state, two))
+        return tuple(kernel_call(body, outs, [VMEM] * (len(names) + 1), work, rows * modes)(*state, two))
 
     return [first] + [following(at) for at in range(1, count)] + [finish]
 
@@ -462,15 +439,9 @@
         compiler_params=pltpu.CompilerParams(vmem_limit_bytes=VMEM_LIMIT),
     )(hessian)
 
-    def near_total(groups, linear, scalars=(), terms=(), tokens=()):
-        call = kernel_call(
-            functools.partial(near_body, len(groups), len(tokens), linear),
-            (wide,) + tokens,
-            [SMEM] * 3 + [VMEM] * (1 + len(groups)) + [SMEM] * len(scalars) + [VMEM] * len(terms),
-            free,
-            traffic,
-            (row_blocks, region_blocks + 1),
-        )
+    def near_total(body, outs, groups, scalars, terms):
+        specs = [SMEM] * 3 + [VMEM] * (1 + len(groups)) + [SMEM] * len(scalars) + [VMEM] * len(terms)
+        call = kernel_call(body, outs, specs, free, traffic, (row_blocks, region_blocks + 1))
         near_bases = bases if len(groups) > 1 else jnp.zeros_like(bases)
         return call(block_cols, live_blocks, near_bases, held, *groups, *scalars, *terms)
 
@@ -483,7 +454,8 @@
         *pairs, last = zip(gathered(lower), gathered(upper))
         return pairs, last
 
-    (total,) = near_total(first_near, first_terms, (bounds,), (vectors,))
+    body_of = functools.partial(near_body, len(first_near), first_terms)
+    (total,) = near_total(body_of, (wide,), first_near, (bounds,), (vectors,))
     pairs, last = pairs_of(first_lower, first_upper)
     pairs.append(last)
     body_of = functools.partial(table_body, region_blocks, 0)
@@ -498,7 +470,8 @@
     one, one_cast = halo_part(body_of, (wide, narrow), table, pairs[-1], total, (bounds,))
 
     own, lower, upper = exchange(one_cast)
-    (total,) = near_total(own, second_terms, (bounds,), (one, vectors))
+    body_of = functools.partial(near_body, len(own), second_terms)
+    (total,) = near_total(body_of, (wide,), own, (bounds,), (one, vectors))
     pairs, last = pairs_of(lower, upper)
     for which, pair in enumerate(pairs):
         (total,) = halo_part(functools.partial(middle_body, which), (wide,), table, pair, total)
@@ -506,12 +479,13 @@
     two, two_cast = halo_part(body_of, (wide, narrow), table, last, total, (bounds,))
 
     own, lower, upper = exchange(two_cast, gather=False)
-    total, after = near_total(own, no_terms, tokens=(token,))
     packed = jax.ShapeDtypeStruct((tile_rows, TILE), jnp.float32)
-    gram = kernel_call(gram_body, packed, [SMEM, VMEM, VMEM], free, traffic)(gram_number, two, after)
+    body_of = functools.partial(near_gram_body, len(own))
+    total, gram = near_total(body_of, (wide, packed), own, (gram_number,), (two,))
     for step_of in [halving(*cores), halving(*across)]:
         gram = step_of(gram)()
     pairs, last = pairs_of(lower, upper)
+    after = jnp.zeros(token.shape, token.dtype)
     for which, pair in enumerate(pairs):
         total, after = halo_part(functools.partial(middle_body, which), (wide, token), table, pair, total)
     gram, after = tied(gram, after)

time: 111 us -> 111 us (level)
  waiting for transfers between devices: 28.8 us -> 26.8 us
    ppermute x6, waiting for transfers between devices: 13.6 us -> 11.3 us  [shifted(): return lax.ppermute(value, axis, pairs)]
    ppermute x6, starting transfers between devices: 14.3 us -> 16.2 us  [shifted(): return lax.ppermute(value, axis, pairs)]
    pallas_call x4 -> x3, Pallas kernels: 12.4 us -> 10.9 us  [the longest x1 4.81 us: first(): kernel_call(body, (tile,) * len(names), [SMEM, VMEM], work, gram.size)]
  transfers between devices with their start and end apart: 23 -> 23, of which waited for: 12 -> 12; matrix products, arithmetic and copies ran while one was open for 2% -> 2% of each run, Pallas kernels for 21% -> 20%
where the time goes in v15:
time: 111 us; the launch traced here: 110 us
  starting transfers between devices  34.7 us (31%)
  Pallas kernels  29.5 us (27%)
  waiting for transfers between devices  26.8 us (24%)
  local copies, waits for them, and re-layouts  8.52 us (8%)
  blocking collectives  5.87 us (5%)
  other arithmetic  3.69 us (3%)
    ppermute x6, starting transfers between devices, shifted(): return lax.ppermute(value, axis, pairs)  16.2 us
    ppermute x10, waiting for transfers between devices, partner_value(): lax.ppermute(value, axis, [(at, at ^ bit) for at in range(lax.axis_size(a...  15.4 us
    ppermute x10, starting transfers between devices, partner_value(): lax.ppermute(value, axis, [(at, at ^ bit) for at in range(lax.axis_size(a...  12 us
    ppermute x6, waiting for transfers between devices, shifted(): return lax.ppermute(value, axis, pairs)  11.3 us
    pallas_call x5, Pallas kernels, halo_part(): return call(table, bases, held, *pair, total, *scalars, *extra)  8.8 us
    ppermute x7, starting transfers between devices, local(): swapped = lambda value: lax.ppermute(value, 'split', [(0, 1), (1, 0)])  6.52 us
    unnamed x24, local copies, waits for them, and re-layouts  6.46 us
    all_gather x2, blocking collectives, exchange(): groups = [lax.all_gather(operand, 'split', axis=0)]  5.87 us
  transfers between devices with their start and end apart: 23, of which 12 were waited for; matrix products, arithmetic and copies ran while one was open for 2% of the time, Pallas kernels for 20%

profile of v15, /device:TPU:1, one launch (start us, length us, event | category | flops | bytes accessed | tf_op | source)
XLA Modules:
  0.0 110.1 jit_solution(832541219774554578)
XLA Ops:
  3.2 2.0 %collective-permute-start = (bf16[592,256]{1,0:T(8,128)(2,1)}, bf16[592,256]{1,0:T(8,128)(2,1)}, u32[]{:S(2)}, u32[]{:S(2)}) collective-permute-start(bf16[592,256]{1,0:T(8,128)(2,1)} %fusion.1), channel_id=1, source_target_pairs={{0,2},{2,4},{4,6},{6,8},{8,10},{10,12},{12,14},{14,16},{16,18},{18... | collective-permute-start | bytes 909320 | tf_op jit(solution)/shard_map/ppermute | solution.py:27
  5.2 4.0 %collective-permute-start.1 = (bf16[592,256]{1,0:T(8,128)(2,1)}, bf16[592,256]{1,0:T(8,128)(2,1)}, u32[]{:S(2)}, u32[]{:S(2)}) collective-permute-start(bf16[592,256]{1,0:T(8,128)(2,1)} %fusion.1), channel_id=1, source_target_pairs={{0,30},{2,0},{4,2},{6,4},{8,6},{10,8},{12,10},{14,12},{16,14},{18,... | collective-permute-start | bytes 909320 | tf_op jit(solution)/shard_map/ppermute | solution.py:27
  9.2 2.0 %copy-done.1 = bf16[3,12,192,192]{3,2,1,0:T(8,128)(2,1)S(1)} copy-done((bf16[3,12,192,192]{3,2,1,0:T(8,128)(2,1)S(1)}, bf16[3,12,192,192]{3,2,1,0:T(8,128)(2,1)}, u32[]{:S(2)}) %copy-start.1) | copy-done | bytes 2654232
  11.6 3.0 %all-gather = bf16[1184,256]{1,0:T(8,128)(2,1)S(1)} all-gather(bf16[592,256]{1,0:T(8,128)(2,1)} %fusion.1), channel_id=2, replica_groups=mesh['region'=16,'split'=2] {'split'}, dimensions={0}, use_global_device_ids=true | all-gather | bytes 909312 | tf_op jit(solution)/shard_map/all_gather | solution.py:405
  14.7 1.4 %shard_map.78.refs_4_ = f32[576,256]{1,0:T(8,128)S(1)} custom-call(s32[3,12]{1,0:T(4,128)S(1)} %copy-done.6, s32[3]{0:T(128)S(1)} %copy-done.7, s32[2]{0:T(128)S(1)} %broadcast_1_refs_2_.2.refs_2_, bf16[3,12,192,192]{3,2,1,0:T(8,128)(2,1)S(1)} %shard_map.77.refs_3_.refs_1_.refs_2_, bf16[2,592,256]{2,1,0:T(8,128)(2,1)S(1)} %bitcast.22, f32[2]{0:T(128)S(1)} %copy-done.8, ...), custom_call_target="tpu_custom_call" | custom-call | flops 10000000 | bytes 276480 | tf_op jit(solution)/shard_map/pallas_call | solution.py:446
  16.1 1.7 %collective-permute-done = bf16[592,256]{1,0:T(8,128)(2,1)} collective-permute-done((bf16[592,256]{1,0:T(8,128)(2,1)}, bf16[592,256]{1,0:T(8,128)(2,1)}, u32[]{:S(2)}, u32[]{:S(2)}) %collective-permute-start) | collective-permute-done | bytes 303136 | tf_op jit(solution)/shard_map/ppermute | solution.py:27
  20.5 1.6 %collective-permute-start.2 = (bf16[592,256]{1,0:T(8,128)(2,1)}, bf16[592,256]{1,0:T(8,128)(2,1)S(1)}, u32[]{:S(2)}, u32[]{:S(2)}) collective-permute-start(bf16[592,256]{1,0:T(8,128)(2,1)} %collective-permute-done), channel_id=1, source_target_pairs={{0,1},{1,0},{2,3},{3,2},{4,5},{5,4},{6,7},{7,6},{8,9},{9,8},{10,11... | collective-permute-start | bytes 909320 | tf_op jit(solution)/shard_map/ppermute | solution.py:378
  22.2 2.4 %shard_map.79 = (f32[576,256]{1,0:T(8,128)S(1)}, s32[3,13]{1,0:T(4,128)S(1)}) custom-call(s32[3,12]{1,0:T(4,128)S(1)} %copy-done.6, s32[3]{0:T(128)S(1)} %copy-done.7, s32[2,6]{1,0:T(2,128)S(1)} %maximum_convert_fusion.lists_ref, s32[2]{0:T(128)S(1)} %pad_add_fusion.refs_0_.refs_1_.refs_2_, bf16[3,12,192,192]{3,2,1,0:T(8,128)(2,1)S(1)} %shard_map.77.refs_3_.refs_1_.refs_2_, ...), custom_call_target="tpu_custom_call" | custom-call | flops 30000001024 | bytes 276480 | tf_op jit(solution)/shard_map/pallas_call | solution.py:467
  25.8 1.3 %collective-permute-start.4 = (bf16[576,256]{1,0:T(8,128)(2,1)S(1)}, bf16[576,256]{1,0:T(8,128)(2,1)S(1)}, u32[]{:S(2)}, u32[]{:S(2)}) collective-permute-start(bf16[576,256]{1,0:T(8,128)(2,1)S(1)} %get-tuple-element.33), channel_id=1, source_target_pairs={{0,2},{2,4},{4,6},{6,8},{8,10},{10,12},{12,14},{14,16},{16,18},{18... | collective-permute-start | bytes 884744 | tf_op jit(solution)/shard_map/ppermute | solution.py:27
  27.1 3.8 %collective-permute-start.6 = (bf16[576,256]{1,0:T(8,128)(2,1)S(1)}, bf16[576,256]{1,0:T(8,128)(2,1)S(1)}, u32[]{:S(2)}, u32[]{:S(2)}) collective-permute-start(bf16[576,256]{1,0:T(8,128)(2,1)S(1)} %get-tuple-element.33), channel_id=1, source_target_pairs={{0,30},{2,0},{4,2},{6,4},{8,6},{10,8},{12,10},{14,12},{16,14},{18,... | collective-permute-start | bytes 884744 | tf_op jit(solution)/shard_map/ppermute | solution.py:27
  30.9 2.8 %all-gather.1 = bf16[1152,256]{1,0:T(8,128)(2,1)S(1)} all-gather(bf16[576,256]{1,0:T(8,128)(2,1)S(1)} %get-tuple-element.33), channel_id=3, replica_groups=mesh['region'=16,'split'=2] {'split'}, dimensions={0}, use_global_device_ids=true | all-gather | bytes 884736 | tf_op jit(solution)/shard_map/all_gather | solution.py:405
  33.7 1.4 %shard_map.81.refs_5_ = f32[576,256]{1,0:T(8,128)S(1)} custom-call(s32[3,12]{1,0:T(4,128)S(1)} %copy-done.6, s32[3]{0:T(128)S(1)} %copy-done.7, s32[2]{0:T(128)S(1)} %broadcast_1_refs_2_.2.refs_2_, bf16[3,12,192,192]{3,2,1,0:T(8,128)(2,1)S(1)} %shard_map.77.refs_3_.refs_1_.refs_2_, bf16[2,576,256]{2,1,0:T(8,128)(2,1)S(1)} %bitcast.23, f32[2]{0:T(128)S(1)} %copy-done.8, ...), custom_call_target="tpu_custom_call" | custom-call | flops 10000000 | bytes 276480 | tf_op jit(solution)/shard_map/pallas_call | solution.py:446
  35.1 4.2 %collective-permute-done.4 = bf16[576,256]{1,0:T(8,128)(2,1)S(1)} collective-permute-done((bf16[576,256]{1,0:T(8,128)(2,1)S(1)}, bf16[576,256]{1,0:T(8,128)(2,1)S(1)}, u32[]{:S(2)}, u32[]{:S(2)}) %collective-permute-start.4) | collective-permute-done | bytes 294944 | tf_op jit(solution)/shard_map/ppermute | solution.py:27
  39.3 1.3 %collective-permute-start.5 = (bf16[576,256]{1,0:T(8,128)(2,1)S(1)}, bf16[576,256]{1,0:T(8,128)(2,1)S(1)}, u32[]{:S(2)}, u32[]{:S(2)}) collective-permute-start(bf16[576,256]{1,0:T(8,128)(2,1)S(1)} %collective-permute-done.4), channel_id=1, source_target_pairs={{0,1},{1,0},{2,3},{3,2},{4,5},{5,4},{6,7},{7,6},{8,9},{9,8},{10,11... | collective-permute-start | bytes 884744 | tf_op jit(solution)/shard_map/ppermute | solution.py:378
  41.5 1.3 %collective-permute-start.7 = (bf16[576,256]{1,0:T(8,128)(2,1)S(1)}, bf16[576,256]{1,0:T(8,128)(2,1)S(1)}, u32[]{:S(2)}, u32[]{:S(2)}) collective-permute-start(bf16[576,256]{1,0:T(8,128)(2,1)S(1)} %collective-permute-done.6), channel_id=1, source_target_pairs={{0,1},{1,0},{2,3},{3,2},{4,5},{5,4},{6,7},{7,6},{8,9},{9,8},{10,11... | collective-permute-start | bytes 884744 | tf_op jit(solution)/shard_map/ppermute | solution.py:378
  44.0 1.9 %shard_map.83 = (f32[576,256]{1,0:T(8,128)S(1)}, bf16[576,256]{1,0:T(8,128)(2,1)}) custom-call(s32[3,13]{1,0:T(4,128)S(1)} %get-tuple-element.31.refs_0_, s32[2]{0:T(128)S(1)} %pad_add_fusion.refs_0_.refs_1_.refs_2_, bf16[3,12,192,192]{3,2,1,0:T(8,128)(2,1)S(1)} %shard_map.77.refs_3_.refs_1_.refs_2_, bf16[1,576,256]{2,1,0:T(8,128)(2,1)S(1)} %bitcast.30, ...), custom_call_target="tpu_custom_call" | custom-call | flops 30000001024 | bytes 276480 | tf_op jit(solution)/shard_map/pallas_call | solution.py:451
  47.5 4.6 %collective-permute-start.12 = (bf16[576,256]{1,0:T(8,128)(2,1)}, bf16[576,256]{1,0:T(8,128)(2,1)}, u32[]{:S(2)}, u32[]{:S(2)}) collective-permute-start(bf16[576,256]{1,0:T(8,128)(2,1)} %get-tuple-element.35), channel_id=1, source_target_pairs={{0,30},{2,0},{4,2},{6,4},{8,6},{10,8},{12,10},{14,12},{16,14},{18,... | collective-permute-start | bytes 884744 | tf_op jit(solution)/shard_map/ppermute | solution.py:27
  53.2 2.6 %shard_map.84 = (f32[576,256]{1,0:T(8,128)S(1)}, f32[384,128]{1,0:T(8,128)S(1)}) custom-call(s32[3,12]{1,0:T(4,128)S(1)} %copy-done.6, s32[3]{0:T(128)S(1)} %copy-done.7, s32[2]{0:T(128)S(1)} %pad_add_fusion.refs_0_.refs_1_.refs_2_, bf16[3,12,192,192]{3,2,1,0:T(8,128)(2,1)S(1)} %shard_map.77.refs_3_.refs_1_.refs_2_, bf16[1,576,256]{2,1,0:T(8,128)(2,1)} %bitcast.13.refs_4_, ...), custom_call_target="tpu_custom_call" | custom-call | flops 10000000 | bytes 276480 | tf_op jit(solution)/shard_map/pallas_call | solution.py:446
  58.7 1.7 %collective-permute-done.11 = bf16[576,256]{1,0:T(8,128)(2,1)} collective-permute-done((bf16[576,256]{1,0:T(8,128)(2,1)}, bf16[576,256]{1,0:T(8,128)(2,1)}, u32[]{:S(2)}, u32[]{:S(2)}) %collective-permute-start.11) | collective-permute-done | bytes 294944 | tf_op jit(solution)/shard_map/ppermute | solution.py:27
  61.4 1.5 %collective-permute-done.12 = bf16[576,256]{1,0:T(8,128)(2,1)} collective-permute-done((bf16[576,256]{1,0:T(8,128)(2,1)}, bf16[576,256]{1,0:T(8,128)(2,1)}, u32[]{:S(2)}, u32[]{:S(2)}) %collective-permute-start.12) | collective-permute-done | bytes 294944 | tf_op jit(solution)/shard_map/ppermute | solution.py:27
  67.1 1.7 %shard_map.85 = (f32[576,256]{1,0:T(8,128)S(1)}, f32[8,128]{1,0:T(8,128)S(1)}) custom-call(s32[3,13]{1,0:T(4,128)S(1)} %get-tuple-element.31.refs_0_, s32[2]{0:T(128)S(1)} %pad_add_fusion.refs_0_.refs_1_.refs_2_, bf16[3,12,192,192]{3,2,1,0:T(8,128)(2,1)S(1)} %shard_map.77.refs_3_.refs_1_.refs_2_, bf16[1,576,256]{2,1,0:T(8,128)(2,1)} %bitcast.16.refs_3_, ...), custom_call_target="tpu_custom_call" | custom-call | flops 30000001024 | bytes 276480 | tf_op jit(solution)/shard_map/pallas_call | solution.py:451
  68.9 2.8 %shard_map.86 = f32[256,256]{1,0:T(8,128)S(1)} custom-call(s32[3,13]{1,0:T(4,128)S(1)} %get-tuple-element.31.refs_0_, s32[2]{0:T(128)S(1)} %pad_add_fusion.refs_0_.refs_1_.refs_2_, bf16[3,12,192,192]{3,2,1,0:T(8,128)(2,1)S(1)} %shard_map.77.refs_3_.refs_1_.refs_2_, bf16[1,576,256]{2,1,0:T(8,128)(2,1)S(1)} %bitcast.26, bf16[1,576,256]{2,1,0:T(8,128)(2,1)S(1)} %bitcast.27, ...), custom_call_target="tpu_custom_call" | custom-call | flops 30000001024 | bytes 276480 | tf_op jit(solution)/shard_map/pallas_call | solution.py:451
  73.3 4.4 %collective-permute-done.16 = f32[112,256]{1,0:T(8,128)S(1)} collective-permute-done((f32[112,256]{1,0:T(8,128)S(1)}, f32[112,256]{1,0:T(8,128)S(1)}, u32[]{:S(2)}, u32[]{:S(2)}) %collective-permute-start.16) | collective-permute-done | bytes 114720 | tf_op jit(solution)/shard_map/ppermute | solution.py:314
  78.9 2.6 %collective-permute-done.17 = f32[112,256]{1,0:T(8,128)S(1)} collective-permute-done((f32[112,256]{1,0:T(8,128)S(1)}, f32[112,256]{1,0:T(8,128)S(1)}, u32[]{:S(2)}, u32[]{:S(2)}) %collective-permute-start.17) | collective-permute-done | bytes 114720 | tf_op jit(solution)/shard_map/ppermute | solution.py:314
  81.5 2.2 %collective-permute-start.18 = (f32[112,256]{1,0:T(8,128)S(1)}, f32[112,256]{1,0:T(8,128)S(1)}, u32[]{:S(2)}, u32[]{:S(2)}) collective-permute-start(f32[112,256]{1,0:T(8,128)S(1)} %add.52), channel_id=1, source_target_pairs={{0,16},{2,18},{4,20},{6,22},{8,24},{10,26},{12,28},{14,30},{16,0},... | collective-permute-start | bytes 344072 | tf_op jit(solution)/shard_map/ppermute | solution.py:314
  83.6 3.7 %collective-permute-done.18 = f32[112,256]{1,0:T(8,128)S(1)} collective-permute-done((f32[112,256]{1,0:T(8,128)S(1)}, f32[112,256]{1,0:T(8,128)S(1)}, u32[]{:S(2)}, u32[]{:S(2)}) %collective-permute-start.18) | collective-permute-done | bytes 114720 | tf_op jit(solution)/shard_map/ppermute | solution.py:314
  88.3 2.8 %collective-permute-done.19 = f32[112,256]{1,0:T(8,128)S(1)} collective-permute-done((f32[112,256]{1,0:T(8,128)S(1)}, f32[112,256]{1,0:T(8,128)S(1)}, u32[]{:S(2)}, u32[]{:S(2)}) %collective-permute-start.19) | collective-permute-done | bytes 114720 | tf_op jit(solution)/shard_map/ppermute | solution.py:314
  91.1 4.6 %collective-permute-start.20 = (f32[192,128]{1,0:T(8,128)S(1)}, f32[192,128]{1,0:T(8,128)S(1)}, u32[]{:S(2)}, u32[]{:S(2)}) collective-permute-start(f32[192,128]{1,0:T(8,128)S(1)} %pad_maximum_fusion.3), channel_id=1, source_target_pairs={{0,1},{1,0},{2,3},{3,2},{4,5},{5,4},{6,7},{7,6},{8,9},{9,8},{10,11... | collective-permute-start | bytes 294920 | tf_op jit(solution)/shard_map/ppermute | solution.py:314
  96.7 4.8 %shard_map.87 = (f32[128,128]{1,0:T(8,128)S(1)}, f32[128,128]{1,0:T(8,128)S(1)}, f32[128,128]{1,0:T(8,128)S(1)}) custom-call(s32[1]{0:T(128)} %bitcast.15.refs_6_.number_ref, f32[384,128]{1,0:T(8,128)S(1)} %constant_dynamic-update-slice_fusion.gram_ref), custom_call_target="tpu_custom_call" | custom-call | flops 100000000 | bytes 3072 | tf_op jit(solution)/shard_map/pallas_call | solution.py:291
  101.5 4.2 %shard_map.88 = (f32[128,128]{1,0:T(8,128)S(1)}, f32[128,128]{1,0:T(8,128)S(1)}, f32[128,128]{1,0:T(8,128)S(1)}) custom-call(f32[128,128]{1,0:T(8,128)S(1)} %get-tuple-element.45.refs_0_, f32[128,128]{1,0:T(8,128)S(1)} %get-tuple-element.46.refs_1_, f32[128,128]{1,0:T(8,128)S(1)} %get-tuple-element.47.refs_2_), custom_call_target="tpu_custom_call" | custom-call | flops 100000000 | bytes 1024 | tf_op jit(solution)/shard_map/pallas_call | solution.py:297
  106.5 1.9 %shard_map.89 = (f32[576,256]{1,0:T(8,128)}, f32[256,256]{1,0:T(8,128)S(1)}) custom-call(f32[128,128]{1,0:T(8,128)S(1)} %get-tuple-element.52.refs_0_, f32[128,128]{1,0:T(8,128)S(1)} %get-tuple-element.53.refs_1_, f32[128,128]{1,0:T(8,128)S(1)} %get-tuple-element.54.refs_2_, f32[576,256]{1,0:T(8,128)S(1)} %copy-done.4), custom_call_target="tpu_custom_call" | custom-call | flops 100000000 | bytes 9216 | tf_op jit(solution)/shard_map/pallas_call | solution.py:304
  108.4 1.7 %shard_map.90 = f32[256,256]{1,0:T(8,128)} custom-call(s32[1]{0:T(128)} %bitcast.20.refs_6_.number_ref, f32[256,256]{1,0:T(8,128)S(1)} %pad_maximum_fusion.cross_ref, f32[256,256]{1,0:T(8,128)S(1)} %get-tuple-element.59.inverse_ref), custom_call_target="tpu_custom_call" | custom-call | flops 150994944 | bytes 276480 | tf_op jit(solution)/shard_map/pallas_call | solution.py:513
  (81 shorter events, 25.2 us)
Async XLA Ops:
  3.2 14.7 %collective-permute-start = (bf16[592,256]{1,0:T(8,128)(2,1)}, bf16[592,256]{1,0:T(8,128)(2,1)}, u32[]{:S(2)}, u32[]{:S(2)}) collective-permute-start(bf16[592,256]{1,0:T(8,128)(2,1)} %fusion.1), channel_id=1, source_target_pairs={{0,2},{2,4},{4,6},{6,8},{8,10},{10,12},{12,14},{14,16},{16,18},{18... | collective-permute-start | bytes 909320 | tf_op jit(solution)/shard_map/ppermute | solution.py:27
  5.2 14.6 %collective-permute-start.1 = (bf16[592,256]{1,0:T(8,128)(2,1)}, bf16[592,256]{1,0:T(8,128)(2,1)}, u32[]{:S(2)}, u32[]{:S(2)}) collective-permute-start(bf16[592,256]{1,0:T(8,128)(2,1)} %fusion.1), channel_id=1, source_target_pairs={{0,30},{2,0},{4,2},{6,4},{8,6},{10,8},{12,10},{14,12},{16,14},{18,... | collective-permute-start | bytes 909320 | tf_op jit(solution)/shard_map/ppermute | solution.py:27
  9.2 2.0 %copy-start.1 = (bf16[3,12,192,192]{3,2,1,0:T(8,128)(2,1)S(1)}, bf16[3,12,192,192]{3,2,1,0:T(8,128)(2,1)}, u32[]{:S(2)}) copy-start(bf16[3,12,192,192]{3,2,1,0:T(8,128)(2,1)} %blocks_ref.1) | copy-start | bytes 7962628
  11.2 3.5 %copy-start = (f32[576,256]{1,0:T(8,128)S(1)}, f32[576,256]{1,0:T(8,128)}, u32[]{:S(2)}) copy-start(f32[576,256]{1,0:T(8,128)} %refs_7_.1) | copy-start | bytes 1769476
  11.2 3.5 %copy-start.6 = (s32[3,12]{1,0:T(4,128)S(1)}, s32[3,12]{1,0:T(4,128)}, u32[]{:S(2)}) copy-start(s32[3,12]{1,0:T(4,128)} %refs_0_.5) | copy-start | bytes 436
  11.2 3.5 %copy-start.7 = (s32[3]{0:T(128)S(1)}, s32[3]{0:T(128)}, u32[]{:S(2)}) copy-start(s32[3]{0:T(128)} %refs_1_.5) | copy-start | bytes 40
  11.2 3.5 %copy-start.8 = (f32[2]{0:T(128)S(1)}, f32[2]{0:T(128)}, u32[]{:S(2)}) copy-start(f32[2]{0:T(128)} %refs_6_.5) | copy-start | bytes 28
  20.5 4.1 %collective-permute-start.2 = (bf16[592,256]{1,0:T(8,128)(2,1)}, bf16[592,256]{1,0:T(8,128)(2,1)S(1)}, u32[]{:S(2)}, u32[]{:S(2)}) collective-permute-start(bf16[592,256]{1,0:T(8,128)(2,1)} %collective-permute-done), channel_id=1, source_target_pairs={{0,1},{1,0},{2,3},{3,2},{4,5},{5,4},{6,7},{7,6},{8,9},{9,8},{10,11... | collective-permute-start | bytes 909320 | tf_op jit(solution)/shard_map/ppermute | solution.py:378
  22.1 2.5 %collective-permute-start.3 = (bf16[592,256]{1,0:T(8,128)(2,1)}, bf16[592,256]{1,0:T(8,128)(2,1)S(1)}, u32[]{:S(2)}, u32[]{:S(2)}) collective-permute-start(bf16[592,256]{1,0:T(8,128)(2,1)} %collective-permute-done.1), channel_id=1, source_target_pairs={{0,1},{1,0},{2,3},{3,2},{4,5},{5,4},{6,7},{7,6},{8,9},{9,8},{10,11... | collective-permute-start | bytes 909320 | tf_op jit(solution)/shard_map/ppermute | solution.py:378
  25.8 13.5 %collective-permute-start.4 = (bf16[576,256]{1,0:T(8,128)(2,1)S(1)}, bf16[576,256]{1,0:T(8,128)(2,1)S(1)}, u32[]{:S(2)}, u32[]{:S(2)}) collective-permute-start(bf16[576,256]{1,0:T(8,128)(2,1)S(1)} %get-tuple-element.33), channel_id=1, source_target_pairs={{0,2},{2,4},{4,6},{6,8},{8,10},{10,12},{12,14},{14,16},{16,18},{18... | collective-permute-start | bytes 884744 | tf_op jit(solution)/shard_map/ppermute | solution.py:27
  27.1 14.5 %collective-permute-start.6 = (bf16[576,256]{1,0:T(8,128)(2,1)S(1)}, bf16[576,256]{1,0:T(8,128)(2,1)S(1)}, u32[]{:S(2)}, u32[]{:S(2)}) collective-permute-start(bf16[576,256]{1,0:T(8,128)(2,1)S(1)} %get-tuple-element.33), channel_id=1, source_target_pairs={{0,30},{2,0},{4,2},{6,4},{8,6},{10,8},{12,10},{14,12},{16,14},{18,... | collective-permute-start | bytes 884744 | tf_op jit(solution)/shard_map/ppermute | solution.py:27
  39.3 4.7 %collective-permute-start.5 = (bf16[576,256]{1,0:T(8,128)(2,1)S(1)}, bf16[576,256]{1,0:T(8,128)(2,1)S(1)}, u32[]{:S(2)}, u32[]{:S(2)}) collective-permute-start(bf16[576,256]{1,0:T(8,128)(2,1)S(1)} %collective-permute-done.4), channel_id=1, source_target_pairs={{0,1},{1,0},{2,3},{3,2},{4,5},{5,4},{6,7},{7,6},{8,9},{9,8},{10,11... | collective-permute-start | bytes 884744 | tf_op jit(solution)/shard_map/ppermute | solution.py:378
  41.5 2.5 %collective-permute-start.7 = (bf16[576,256]{1,0:T(8,128)(2,1)S(1)}, bf16[576,256]{1,0:T(8,128)(2,1)S(1)}, u32[]{:S(2)}, u32[]{:S(2)}) collective-permute-start(bf16[576,256]{1,0:T(8,128)(2,1)S(1)} %collective-permute-done.6), channel_id=1, source_target_pairs={{0,1},{1,0},{2,3},{3,2},{4,5},{5,4},{6,7},{7,6},{8,9},{9,8},{10,11... | collective-permute-start | bytes 884744 | tf_op jit(solution)/shard_map/ppermute | solution.py:378
  46.7 5.4 %collective-permute-start.8 = (bf16[576,256]{1,0:T(8,128)(2,1)}, bf16[576,256]{1,0:T(8,128)(2,1)}, u32[]{:S(2)}, u32[]{:S(2)}) collective-permute-start(bf16[576,256]{1,0:T(8,128)(2,1)} %get-tuple-element.35), channel_id=1, source_target_pairs={{0,1},{1,0},{2,3},{3,2},{4,5},{5,4},{6,7},{7,6},{8,9},{9,8},{10,11... | collective-permute-start | bytes 884744 | tf_op jit(solution)/shard_map/ppermute | solution.py:378
  47.1 13.3 %collective-permute-start.11 = (bf16[576,256]{1,0:T(8,128)(2,1)}, bf16[576,256]{1,0:T(8,128)(2,1)}, u32[]{:S(2)}, u32[]{:S(2)}) collective-permute-start(bf16[576,256]{1,0:T(8,128)(2,1)} %get-tuple-element.35), channel_id=1, source_target_pairs={{0,2},{2,4},{4,6},{6,8},{8,10},{10,12},{12,14},{14,16},{16,18},{18... | collective-permute-start | bytes 884744 | tf_op jit(solution)/shard_map/ppermute | solution.py:27
  47.5 15.4 %collective-permute-start.12 = (bf16[576,256]{1,0:T(8,128)(2,1)}, bf16[576,256]{1,0:T(8,128)(2,1)}, u32[]{:S(2)}, u32[]{:S(2)}) collective-permute-start(bf16[576,256]{1,0:T(8,128)(2,1)} %get-tuple-element.35), channel_id=1, source_target_pairs={{0,30},{2,0},{4,2},{6,4},{8,6},{10,8},{12,10},{14,12},{16,14},{18,... | collective-permute-start | bytes 884744 | tf_op jit(solution)/shard_map/ppermute | solution.py:27
  52.2 1.1 copy-start.3
  55.9 0.8 copy-start.9
  58.0 5.9 %collective-permute-start.9 = (f32[192,128]{1,0:T(8,128)}, f32[192,128]{1,0:T(8,128)}, u32[]{:S(2)}, u32[]{:S(2)}) collective-permute-start(f32[192,128]{1,0:T(8,128)} %slice.63), channel_id=1, source_target_pairs={{0,1},{1,0},{2,3},{3,2},{4,5},{5,4},{6,7},{7,6},{8,9},{9,8},{10,11... | collective-permute-start | bytes 294920 | tf_op jit(solution)/shard_map/ppermute | solution.py:314
  60.4 8.5 %collective-permute-start.13 = (bf16[576,256]{1,0:T(8,128)(2,1)}, bf16[576,256]{1,0:T(8,128)(2,1)S(1)}, u32[]{:S(2)}, u32[]{:S(2)}) collective-permute-start(bf16[576,256]{1,0:T(8,128)(2,1)} %collective-permute-done.11), channel_id=1, source_target_pairs={{0,1},{1,0},{2,3},{3,2},{4,5},{5,4},{6,7},{7,6},{8,9},{9,8},{10,11... | collective-permute-start | bytes 884744 | tf_op jit(solution)/shard_map/ppermute | solution.py:378
  62.9 6.0 %collective-permute-start.14 = (bf16[576,256]{1,0:T(8,128)(2,1)}, bf16[576,256]{1,0:T(8,128)(2,1)S(1)}, u32[]{:S(2)}, u32[]{:S(2)}) collective-permute-start(bf16[576,256]{1,0:T(8,128)(2,1)} %collective-permute-done.12), channel_id=1, source_target_pairs={{0,1},{1,0},{2,3},{3,2},{4,5},{5,4},{6,7},{7,6},{8,9},{9,8},{10,11... | collective-permute-start | bytes 884744 | tf_op jit(solution)/shard_map/ppermute | solution.py:378
  64.8 4.0 %collective-permute-start.10 = (f32[96,128]{1,0:T(8,128)S(1)}, f32[96,128]{1,0:T(8,128)S(1)}, u32[]{:S(2)}, u32[]{:S(2)}) collective-permute-start(f32[96,128]{1,0:T(8,128)S(1)} %slice.81), channel_id=1, source_target_pairs={{0,4},{2,6},{4,0},{6,2},{8,12},{10,14},{12,8},{14,10},{16,20},{18,... | collective-permute-start | bytes 147464 | tf_op jit(solution)/shard_map/ppermute | solution.py:314
  66.1 1.1 copy-start.10
  67.1 1.8 %copy-start.4 = (f32[576,256]{1,0:T(8,128)S(1)}, f32[576,256]{1,0:T(8,128)}, u32[]{:S(2)}) copy-start(f32[576,256]{1,0:T(8,128)} %copy-done.2) | copy-start | bytes 1769476
  71.7 1.4 %collective-permute-start.15 = (f32[128,256]{1,0:T(8,128)S(1)}, f32[128,256]{1,0:T(8,128)S(1)}, u32[]{:S(2)}, u32[]{:S(2)}) collective-permute-start(f32[128,256]{1,0:T(8,128)S(1)} %slice.83), channel_id=1, source_target_pairs={{0,1},{1,0},{2,3},{3,2},{4,5},{5,4},{6,7},{7,6},{8,9},{9,8},{10,11... | collective-permute-start | bytes 393224 | tf_op jit(solution)/shard_map/ppermute | solution.py:314
  73.2 4.5 %collective-permute-start.16 = (f32[112,256]{1,0:T(8,128)S(1)}, f32[112,256]{1,0:T(8,128)S(1)}, u32[]{:S(2)}, u32[]{:S(2)}) collective-permute-start(f32[112,256]{1,0:T(8,128)S(1)} %fusion.2), channel_id=1, source_target_pairs={{0,2},{2,0},{4,6},{6,4},{8,10},{10,8},{12,14},{14,12},{16,18},{18,... | collective-permute-start | bytes 344072 | tf_op jit(solution)/shard_map/ppermute | solution.py:314
  77.8 3.7 %collective-permute-start.17 = (f32[112,256]{1,0:T(8,128)S(1)}, f32[112,256]{1,0:T(8,128)S(1)}, u32[]{:S(2)}, u32[]{:S(2)}) collective-permute-start(f32[112,256]{1,0:T(8,128)S(1)} %maximum_add_fusion), channel_id=1, source_target_pairs={{0,8},{2,10},{4,12},{6,14},{8,0},{10,2},{12,4},{14,6},{16,24},{18,... | collective-permute-start | bytes 344072 | tf_op jit(solution)/shard_map/ppermute | solution.py:314
  81.5 5.8 %collective-permute-start.18 = (f32[112,256]{1,0:T(8,128)S(1)}, f32[112,256]{1,0:T(8,128)S(1)}, u32[]{:S(2)}, u32[]{:S(2)}) collective-permute-start(f32[112,256]{1,0:T(8,128)S(1)} %add.52), channel_id=1, source_target_pairs={{0,16},{2,18},{4,20},{6,22},{8,24},{10,26},{12,28},{14,30},{16,0},... | collective-permute-start | bytes 344072 | tf_op jit(solution)/shard_map/ppermute | solution.py:314
  87.4 3.7 %collective-permute-start.19 = (f32[112,256]{1,0:T(8,128)S(1)}, f32[112,256]{1,0:T(8,128)S(1)}, u32[]{:S(2)}, u32[]{:S(2)}) collective-permute-start(f32[112,256]{1,0:T(8,128)S(1)} %add.53), channel_id=1, source_target_pairs={{0,4},{2,6},{4,0},{6,2},{8,12},{10,14},{12,8},{14,10},{16,20},{18,... | collective-permute-start | bytes 344072 | tf_op jit(solution)/shard_map/ppermute | solution.py:314
  91.1 5.6 %collective-permute-start.20 = (f32[192,128]{1,0:T(8,128)S(1)}, f32[192,128]{1,0:T(8,128)S(1)}, u32[]{:S(2)}, u32[]{:S(2)}) collective-permute-start(f32[192,128]{1,0:T(8,128)S(1)} %pad_maximum_fusion.3), channel_id=1, source_target_pairs={{0,1},{1,0},{2,3},{3,2},{4,5},{5,4},{6,7},{7,6},{8,9},{9,8},{10,11... | collective-permute-start | bytes 294920 | tf_op jit(solution)/shard_map/ppermute | solution.py:314
  96.6 9.1 %collective-permute-start.21 = (f32[64,256]{1,0:T(8,128)S(1)}, f32[64,256]{1,0:T(8,128)S(1)}, u32[]{:S(2)}, u32[]{:S(2)}) collective-permute-start(f32[64,256]{1,0:T(8,128)S(1)} %slice_add_fusion.2), channel_id=1, source_target_pairs={{0,2},{2,0},{4,6},{6,4},{8,10},{10,8},{12,14},{14,12},{16,18},{18,... | collective-permute-start | bytes 196616 | tf_op jit(solution)/shard_map/ppermute | solution.py:314
  105.7 2.6 %collective-permute-start.22 = (f32[128,256]{1,0:T(8,128)S(1)}, f32[128,256]{1,0:T(8,128)S(1)}, u32[]{:S(2)}, u32[]{:S(2)}) collective-permute-start(f32[128,256]{1,0:T(8,128)S(1)} %pad_maximum_fusion.1), channel_id=1, source_target_pairs={{0,1},{1,0},{2,3},{3,2},{4,5},{5,4},{6,7},{7,6},{8,9},{9,8},{10,11... | collective-permute-start | bytes 393224 | tf_op jit(solution)/shard_map/ppermute | solution.py:314
  (2 other events, 1.5 us)

commit v16 on v15

--- a/solution.py
+++ b/solution.py
@@ -198,17 +198,23 @@
             inside = (lane >= start) & (lane < start + GROUP)
             forward = jnp.where(inside, jnp.where(lane - start == sub, 1.0, 0.0), rows[step])
             solved = forward
+            scalars = {
+                (row, col): over_rows(pivot_cols[col], row) for row in range(GROUP) for col in range(row + 1)
+            }
             for pivot in range(GROUP):
+                inverse = 1.0 / scalars[pivot, pivot]
+                for row in range(pivot + 1, GROUP):
+                    multiple = scalars[row, pivot] * inverse
+                    for col in range(pivot + 1, row + 1):
+                        scalars[row, col] = scalars[row, col] - multiple * scalars[col, pivot]
                 here = sub == pivot
-                value = over_rows(pivot_cols[pivot], pivot)
-                inverse = 1.0 / value
                 ratio = pivot_cols[pivot] * inverse
                 row = over_rows(forward, pivot)
                 below_row = jnp.where(sub > pivot, forward - ratio * row, forward)
-                forward = jnp.where(here, row * lax.rsqrt(value), below_row)
+                forward = jnp.where(here, row * lax.rsqrt(scalars[pivot, pivot]), below_row)
                 solved = jnp.where(here, row * inverse, solved - ratio * row)
                 for col in range(pivot + 1, GROUP):
-                    top = over_rows(pivot_cols[col], pivot)
+                    top = scalars[col, pivot]
                     pivot_cols[col] = jnp.where(here, top * inverse, pivot_cols[col] - ratio * top)
             own_part = (lane < start + GROUP) | (lane >= end * GROUP)
             reduced.append((forward, jnp.where(own_part, forward, 0.0)))

time: 111 us -> 111 us (level)
  no operation moved by 1% of the time
where the time goes in v16:
time: 111 us; the launch traced here: 110 us
  starting transfers between devices  34.7 us (31%)
  Pallas kernels  29.9 us (27%)
  waiting for transfers between devices  26.8 us (24%)
  local copies, waits for them, and re-layouts  8.52 us (8%)
  blocking collectives  5.87 us (5%)
  other arithmetic  3.69 us (3%)
    ppermute x6, starting transfers between devices, shifted(): return lax.ppermute(value, axis, pairs)  16.2 us
    ppermute x10, waiting for transfers between devices, partner_value(): lax.ppermute(value, axis, [(at, at ^ bit) for at in range(lax.axis_size(a...  15.4 us
    ppermute x10, starting transfers between devices, partner_value(): lax.ppermute(value, axis, [(at, at ^ bit) for at in range(lax.axis_size(a...  12 us
    ppermute x6, waiting for transfers between devices, shifted(): return lax.ppermute(value, axis, pairs)  11.3 us
    pallas_call x5, Pallas kernels, halo_part(): return call(table, bases, held, *pair, total, *scalars, *extra)  8.8 us
    ppermute x7, starting transfers between devices, local(): swapped = lambda value: lax.ppermute(value, 'split', [(0, 1), (1, 0)])  6.52 us
    unnamed x24, local copies, waits for them, and re-layouts  6.46 us
    all_gather x2, blocking collectives, exchange(): groups = [lax.all_gather(operand, 'split', axis=0)]  5.87 us
  transfers between devices with their start and end apart: 23, of which 12 were waited for; matrix products, arithmetic and copies ran while one was open for 2% of the time, Pallas kernels for 20%

profile of v16, /device:TPU:1, one launch (start us, length us, event | category | flops | bytes accessed | tf_op | source)
XLA Modules:
  0.0 110.5 jit_solution(732681100897911496)
XLA Ops:
  3.2 2.0 %collective-permute-start = (bf16[592,256]{1,0:T(8,128)(2,1)}, bf16[592,256]{1,0:T(8,128)(2,1)}, u32[]{:S(2)}, u32[]{:S(2)}) collective-permute-start(bf16[592,256]{1,0:T(8,128)(2,1)} %fusion.1), channel_id=1, source_target_pairs={{0,2},{2,4},{4,6},{6,8},{8,10},{10,12},{12,14},{14,16},{16,18},{18... | collective-permute-start | bytes 909320 | tf_op jit(solution)/shard_map/ppermute | solution.py:27
  5.2 4.0 %collective-permute-start.1 = (bf16[592,256]{1,0:T(8,128)(2,1)}, bf16[592,256]{1,0:T(8,128)(2,1)}, u32[]{:S(2)}, u32[]{:S(2)}) collective-permute-start(bf16[592,256]{1,0:T(8,128)(2,1)} %fusion.1), channel_id=1, source_target_pairs={{0,30},{2,0},{4,2},{6,4},{8,6},{10,8},{12,10},{14,12},{16,14},{18,... | collective-permute-start | bytes 909320 | tf_op jit(solution)/shard_map/ppermute | solution.py:27
  9.2 2.0 %copy-done.1 = bf16[3,12,192,192]{3,2,1,0:T(8,128)(2,1)S(1)} copy-done((bf16[3,12,192,192]{3,2,1,0:T(8,128)(2,1)S(1)}, bf16[3,12,192,192]{3,2,1,0:T(8,128)(2,1)}, u32[]{:S(2)}) %copy-start.1) | copy-done | bytes 2654232
  11.6 3.0 %all-gather = bf16[1184,256]{1,0:T(8,128)(2,1)S(1)} all-gather(bf16[592,256]{1,0:T(8,128)(2,1)} %fusion.1), channel_id=2, replica_groups=mesh['region'=16,'split'=2] {'split'}, dimensions={0}, use_global_device_ids=true | all-gather | bytes 909312 | tf_op jit(solution)/shard_map/all_gather | solution.py:411
  14.7 1.4 %shard_map.78.refs_4_ = f32[576,256]{1,0:T(8,128)S(1)} custom-call(s32[3,12]{1,0:T(4,128)S(1)} %copy-done.6, s32[3]{0:T(128)S(1)} %copy-done.7, s32[2]{0:T(128)S(1)} %broadcast_1_refs_2_.2.refs_2_, bf16[3,12,192,192]{3,2,1,0:T(8,128)(2,1)S(1)} %shard_map.77.refs_3_.refs_1_.refs_2_, bf16[2,592,256]{2,1,0:T(8,128)(2,1)S(1)} %bitcast.22, f32[2]{0:T(128)S(1)} %copy-done.8, ...), custom_call_target="tpu_custom_call" | custom-call | flops 10000000 | bytes 276480 | tf_op jit(solution)/shard_map/pallas_call | solution.py:452
  16.1 1.7 %collective-permute-done = bf16[592,256]{1,0:T(8,128)(2,1)} collective-permute-done((bf16[592,256]{1,0:T(8,128)(2,1)}, bf16[592,256]{1,0:T(8,128)(2,1)}, u32[]{:S(2)}, u32[]{:S(2)}) %collective-permute-start) | collective-permute-done | bytes 303136 | tf_op jit(solution)/shard_map/ppermute | solution.py:27
  20.5 1.6 %collective-permute-start.2 = (bf16[592,256]{1,0:T(8,128)(2,1)}, bf16[592,256]{1,0:T(8,128)(2,1)S(1)}, u32[]{:S(2)}, u32[]{:S(2)}) collective-permute-start(bf16[592,256]{1,0:T(8,128)(2,1)} %collective-permute-done), channel_id=1, source_target_pairs={{0,1},{1,0},{2,3},{3,2},{4,5},{5,4},{6,7},{7,6},{8,9},{9,8},{10,11... | collective-permute-start | bytes 909320 | tf_op jit(solution)/shard_map/ppermute | solution.py:384
  22.2 2.4 %shard_map.79 = (f32[576,256]{1,0:T(8,128)S(1)}, s32[3,13]{1,0:T(4,128)S(1)}) custom-call(s32[3,12]{1,0:T(4,128)S(1)} %copy-done.6, s32[3]{0:T(128)S(1)} %copy-done.7, s32[2,6]{1,0:T(2,128)S(1)} %maximum_convert_fusion.lists_ref, s32[2]{0:T(128)S(1)} %pad_add_fusion.refs_0_.refs_1_.refs_2_, bf16[3,12,192,192]{3,2,1,0:T(8,128)(2,1)S(1)} %shard_map.77.refs_3_.refs_1_.refs_2_, ...), custom_call_target="tpu_custom_call" | custom-call | flops 30000001024 | bytes 276480 | tf_op jit(solution)/shard_map/pallas_call | solution.py:473
  25.8 1.3 %collective-permute-start.4 = (bf16[576,256]{1,0:T(8,128)(2,1)S(1)}, bf16[576,256]{1,0:T(8,128)(2,1)S(1)}, u32[]{:S(2)}, u32[]{:S(2)}) collective-permute-start(bf16[576,256]{1,0:T(8,128)(2,1)S(1)} %get-tuple-element.33), channel_id=1, source_target_pairs={{0,2},{2,4},{4,6},{6,8},{8,10},{10,12},{12,14},{14,16},{16,18},{18... | collective-permute-start | bytes 884744 | tf_op jit(solution)/shard_map/ppermute | solution.py:27
  27.1 3.8 %collective-permute-start.6 = (bf16[576,256]{1,0:T(8,128)(2,1)S(1)}, bf16[576,256]{1,0:T(8,128)(2,1)S(1)}, u32[]{:S(2)}, u32[]{:S(2)}) collective-permute-start(bf16[576,256]{1,0:T(8,128)(2,1)S(1)} %get-tuple-element.33), channel_id=1, source_target_pairs={{0,30},{2,0},{4,2},{6,4},{8,6},{10,8},{12,10},{14,12},{16,14},{18,... | collective-permute-start | bytes 884744 | tf_op jit(solution)/shard_map/ppermute | solution.py:27
  30.9 2.8 %all-gather.1 = bf16[1152,256]{1,0:T(8,128)(2,1)S(1)} all-gather(bf16[576,256]{1,0:T(8,128)(2,1)S(1)} %get-tuple-element.33), channel_id=3, replica_groups=mesh['region'=16,'split'=2] {'split'}, dimensions={0}, use_global_device_ids=true | all-gather | bytes 884736 | tf_op jit(solution)/shard_map/all_gather | solution.py:411
  33.7 1.4 %shard_map.81.refs_5_ = f32[576,256]{1,0:T(8,128)S(1)} custom-call(s32[3,12]{1,0:T(4,128)S(1)} %copy-done.6, s32[3]{0:T(128)S(1)} %copy-done.7, s32[2]{0:T(128)S(1)} %broadcast_1_refs_2_.2.refs_2_, bf16[3,12,192,192]{3,2,1,0:T(8,128)(2,1)S(1)} %shard_map.77.refs_3_.refs_1_.refs_2_, bf16[2,576,256]{2,1,0:T(8,128)(2,1)S(1)} %bitcast.23, f32[2]{0:T(128)S(1)} %copy-done.8, ...), custom_call_target="tpu_custom_call" | custom-call | flops 10000000 | bytes 276480 | tf_op jit(solution)/shard_map/pallas_call | solution.py:452
  35.1 4.2 %collective-permute-done.4 = bf16[576,256]{1,0:T(8,128)(2,1)S(1)} collective-permute-done((bf16[576,256]{1,0:T(8,128)(2,1)S(1)}, bf16[576,256]{1,0:T(8,128)(2,1)S(1)}, u32[]{:S(2)}, u32[]{:S(2)}) %collective-permute-start.4) | collective-permute-done | bytes 294944 | tf_op jit(solution)/shard_map/ppermute | solution.py:27
  39.3 1.3 %collective-permute-start.5 = (bf16[576,256]{1,0:T(8,128)(2,1)S(1)}, bf16[576,256]{1,0:T(8,128)(2,1)S(1)}, u32[]{:S(2)}, u32[]{:S(2)}) collective-permute-start(bf16[576,256]{1,0:T(8,128)(2,1)S(1)} %collective-permute-done.4), channel_id=1, source_target_pairs={{0,1},{1,0},{2,3},{3,2},{4,5},{5,4},{6,7},{7,6},{8,9},{9,8},{10,11... | collective-permute-start | bytes 884744 | tf_op jit(solution)/shard_map/ppermute | solution.py:384
  41.5 1.3 %collective-permute-start.7 = (bf16[576,256]{1,0:T(8,128)(2,1)S(1)}, bf16[576,256]{1,0:T(8,128)(2,1)S(1)}, u32[]{:S(2)}, u32[]{:S(2)}) collective-permute-start(bf16[576,256]{1,0:T(8,128)(2,1)S(1)} %collective-permute-done.6), channel_id=1, source_target_pairs={{0,1},{1,0},{2,3},{3,2},{4,5},{5,4},{6,7},{7,6},{8,9},{9,8},{10,11... | collective-permute-start | bytes 884744 | tf_op jit(solution)/shard_map/ppermute | solution.py:384
  44.0 1.9 %shard_map.83 = (f32[576,256]{1,0:T(8,128)S(1)}, bf16[576,256]{1,0:T(8,128)(2,1)}) custom-call(s32[3,13]{1,0:T(4,128)S(1)} %get-tuple-element.31.refs_0_, s32[2]{0:T(128)S(1)} %pad_add_fusion.refs_0_.refs_1_.refs_2_, bf16[3,12,192,192]{3,2,1,0:T(8,128)(2,1)S(1)} %shard_map.77.refs_3_.refs_1_.refs_2_, bf16[1,576,256]{2,1,0:T(8,128)(2,1)S(1)} %bitcast.30, ...), custom_call_target="tpu_custom_call" | custom-call | flops 30000001024 | bytes 276480 | tf_op jit(solution)/shard_map/pallas_call | solution.py:457
  47.5 4.6 %collective-permute-start.12 = (bf16[576,256]{1,0:T(8,128)(2,1)}, bf16[576,256]{1,0:T(8,128)(2,1)}, u32[]{:S(2)}, u32[]{:S(2)}) collective-permute-start(bf16[576,256]{1,0:T(8,128)(2,1)} %get-tuple-element.35), channel_id=1, source_target_pairs={{0,30},{2,0},{4,2},{6,4},{8,6},{10,8},{12,10},{14,12},{16,14},{18,... | collective-permute-start | bytes 884744 | tf_op jit(solution)/shard_map/ppermute | solution.py:27
  53.2 2.6 %shard_map.84 = (f32[576,256]{1,0:T(8,128)S(1)}, f32[384,128]{1,0:T(8,128)S(1)}) custom-call(s32[3,12]{1,0:T(4,128)S(1)} %copy-done.6, s32[3]{0:T(128)S(1)} %copy-done.7, s32[2]{0:T(128)S(1)} %pad_add_fusion.refs_0_.refs_1_.refs_2_, bf16[3,12,192,192]{3,2,1,0:T(8,128)(2,1)S(1)} %shard_map.77.refs_3_.refs_1_.refs_2_, bf16[1,576,256]{2,1,0:T(8,128)(2,1)} %bitcast.13.refs_4_, ...), custom_call_target="tpu_custom_call" | custom-call | flops 10000000 | bytes 276480 | tf_op jit(solution)/shard_map/pallas_call | solution.py:452
  58.7 1.7 %collective-permute-done.11 = bf16[576,256]{1,0:T(8,128)(2,1)} collective-permute-done((bf16[576,256]{1,0:T(8,128)(2,1)}, bf16[576,256]{1,0:T(8,128)(2,1)}, u32[]{:S(2)}, u32[]{:S(2)}) %collective-permute-start.11) | collective-permute-done | bytes 294944 | tf_op jit(solution)/shard_map/ppermute | solution.py:27
  61.4 1.5 %collective-permute-done.12 = bf16[576,256]{1,0:T(8,128)(2,1)} collective-permute-done((bf16[576,256]{1,0:T(8,128)(2,1)}, bf16[576,256]{1,0:T(8,128)(2,1)}, u32[]{:S(2)}, u32[]{:S(2)}) %collective-permute-start.12) | collective-permute-done | bytes 294944 | tf_op jit(solution)/shard_map/ppermute | solution.py:27
  67.1 1.7 %shard_map.85 = (f32[576,256]{1,0:T(8,128)S(1)}, f32[8,128]{1,0:T(8,128)S(1)}) custom-call(s32[3,13]{1,0:T(4,128)S(1)} %get-tuple-element.31.refs_0_, s32[2]{0:T(128)S(1)} %pad_add_fusion.refs_0_.refs_1_.refs_2_, bf16[3,12,192,192]{3,2,1,0:T(8,128)(2,1)S(1)} %shard_map.77.refs_3_.refs_1_.refs_2_, bf16[1,576,256]{2,1,0:T(8,128)(2,1)} %bitcast.16.refs_3_, ...), custom_call_target="tpu_custom_call" | custom-call | flops 30000001024 | bytes 276480 | tf_op jit(solution)/shard_map/pallas_call | solution.py:457
  68.9 2.8 %shard_map.86 = f32[256,256]{1,0:T(8,128)S(1)} custom-call(s32[3,13]{1,0:T(4,128)S(1)} %get-tuple-element.31.refs_0_, s32[2]{0:T(128)S(1)} %pad_add_fusion.refs_0_.refs_1_.refs_2_, bf16[3,12,192,192]{3,2,1,0:T(8,128)(2,1)S(1)} %shard_map.77.refs_3_.refs_1_.refs_2_, bf16[1,576,256]{2,1,0:T(8,128)(2,1)S(1)} %bitcast.26, bf16[1,576,256]{2,1,0:T(8,128)(2,1)S(1)} %bitcast.27, ...), custom_call_target="tpu_custom_call" | custom-call | flops 30000001024 | bytes 276480 | tf_op jit(solution)/shard_map/pallas_call | solution.py:457
  73.3 4.4 %collective-permute-done.16 = f32[112,256]{1,0:T(8,128)S(1)} collective-permute-done((f32[112,256]{1,0:T(8,128)S(1)}, f32[112,256]{1,0:T(8,128)S(1)}, u32[]{:S(2)}, u32[]{:S(2)}) %collective-permute-start.16) | collective-permute-done | bytes 114720 | tf_op jit(solution)/shard_map/ppermute | solution.py:320
  78.9 2.6 %collective-permute-done.17 = f32[112,256]{1,0:T(8,128)S(1)} collective-permute-done((f32[112,256]{1,0:T(8,128)S(1)}, f32[112,256]{1,0:T(8,128)S(1)}, u32[]{:S(2)}, u32[]{:S(2)}) %collective-permute-start.17) | collective-permute-done | bytes 114720 | tf_op jit(solution)/shard_map/ppermute | solution.py:320
  81.5 2.2 %collective-permute-start.18 = (f32[112,256]{1,0:T(8,128)S(1)}, f32[112,256]{1,0:T(8,128)S(1)}, u32[]{:S(2)}, u32[]{:S(2)}) collective-permute-start(f32[112,256]{1,0:T(8,128)S(1)} %add.52), channel_id=1, source_target_pairs={{0,16},{2,18},{4,20},{6,22},{8,24},{10,26},{12,28},{14,30},{16,0},... | collective-permute-start | bytes 344072 | tf_op jit(solution)/shard_map/ppermute | solution.py:320
  83.6 3.7 %collective-permute-done.18 = f32[112,256]{1,0:T(8,128)S(1)} collective-permute-done((f32[112,256]{1,0:T(8,128)S(1)}, f32[112,256]{1,0:T(8,128)S(1)}, u32[]{:S(2)}, u32[]{:S(2)}) %collective-permute-start.18) | collective-permute-done | bytes 114720 | tf_op jit(solution)/shard_map/ppermute | solution.py:320
  88.3 2.8 %collective-permute-done.19 = f32[112,256]{1,0:T(8,128)S(1)} collective-permute-done((f32[112,256]{1,0:T(8,128)S(1)}, f32[112,256]{1,0:T(8,128)S(1)}, u32[]{:S(2)}, u32[]{:S(2)}) %collective-permute-start.19) | collective-permute-done | bytes 114720 | tf_op jit(solution)/shard_map/ppermute | solution.py:320
  91.1 4.6 %collective-permute-start.20 = (f32[192,128]{1,0:T(8,128)S(1)}, f32[192,128]{1,0:T(8,128)S(1)}, u32[]{:S(2)}, u32[]{:S(2)}) collective-permute-start(f32[192,128]{1,0:T(8,128)S(1)} %pad_maximum_fusion.3), channel_id=1, source_target_pairs={{0,1},{1,0},{2,3},{3,2},{4,5},{5,4},{6,7},{7,6},{8,9},{9,8},{10,11... | collective-permute-start | bytes 294920 | tf_op jit(solution)/shard_map/ppermute | solution.py:320
  96.7 5.0 %shard_map.87 = (f32[128,128]{1,0:T(8,128)S(1)}, f32[128,128]{1,0:T(8,128)S(1)}, f32[128,128]{1,0:T(8,128)S(1)}) custom-call(s32[1]{0:T(128)} %bitcast.15.refs_6_.number_ref, f32[384,128]{1,0:T(8,128)S(1)} %constant_dynamic-update-slice_fusion.gram_ref), custom_call_target="tpu_custom_call" | custom-call | flops 100000000 | bytes 3072 | tf_op jit(solution)/shard_map/pallas_call | solution.py:297
  101.7 4.4 %shard_map.88 = (f32[128,128]{1,0:T(8,128)S(1)}, f32[128,128]{1,0:T(8,128)S(1)}, f32[128,128]{1,0:T(8,128)S(1)}) custom-call(f32[128,128]{1,0:T(8,128)S(1)} %get-tuple-element.45.refs_0_, f32[128,128]{1,0:T(8,128)S(1)} %get-tuple-element.46.refs_1_, f32[128,128]{1,0:T(8,128)S(1)} %get-tuple-element.47.refs_2_), custom_call_target="tpu_custom_call" | custom-call | flops 100000000 | bytes 1024 | tf_op jit(solution)/shard_map/pallas_call | solution.py:303
  106.8 1.9 %shard_map.89 = (f32[576,256]{1,0:T(8,128)}, f32[256,256]{1,0:T(8,128)S(1)}) custom-call(f32[128,128]{1,0:T(8,128)S(1)} %get-tuple-element.52.refs_0_, f32[128,128]{1,0:T(8,128)S(1)} %get-tuple-element.53.refs_1_, f32[128,128]{1,0:T(8,128)S(1)} %get-tuple-element.54.refs_2_, f32[576,256]{1,0:T(8,128)S(1)} %copy-done.4), custom_call_target="tpu_custom_call" | custom-call | flops 100000000 | bytes 9216 | tf_op jit(solution)/shard_map/pallas_call | solution.py:310
  108.8 1.7 %shard_map.90 = f32[256,256]{1,0:T(8,128)} custom-call(s32[1]{0:T(128)} %bitcast.20.refs_6_.number_ref, f32[256,256]{1,0:T(8,128)S(1)} %pad_maximum_fusion.cross_ref, f32[256,256]{1,0:T(8,128)S(1)} %get-tuple-element.59.inverse_ref), custom_call_target="tpu_custom_call" | custom-call | flops 150994944 | bytes 276480 | tf_op jit(solution)/shard_map/pallas_call | solution.py:519
  (81 shorter events, 25.2 us)
Async XLA Ops:
  3.2 14.7 %collective-permute-start = (bf16[592,256]{1,0:T(8,128)(2,1)}, bf16[592,256]{1,0:T(8,128)(2,1)}, u32[]{:S(2)}, u32[]{:S(2)}) collective-permute-start(bf16[592,256]{1,0:T(8,128)(2,1)} %fusion.1), channel_id=1, source_target_pairs={{0,2},{2,4},{4,6},{6,8},{8,10},{10,12},{12,14},{14,16},{16,18},{18... | collective-permute-start | bytes 909320 | tf_op jit(solution)/shard_map/ppermute | solution.py:27
  5.2 14.6 %collective-permute-start.1 = (bf16[592,256]{1,0:T(8,128)(2,1)}, bf16[592,256]{1,0:T(8,128)(2,1)}, u32[]{:S(2)}, u32[]{:S(2)}) collective-permute-start(bf16[592,256]{1,0:T(8,128)(2,1)} %fusion.1), channel_id=1, source_target_pairs={{0,30},{2,0},{4,2},{6,4},{8,6},{10,8},{12,10},{14,12},{16,14},{18,... | collective-permute-start | bytes 909320 | tf_op jit(solution)/shard_map/ppermute | solution.py:27
  9.2 2.0 %copy-start.1 = (bf16[3,12,192,192]{3,2,1,0:T(8,128)(2,1)S(1)}, bf16[3,12,192,192]{3,2,1,0:T(8,128)(2,1)}, u32[]{:S(2)}) copy-start(bf16[3,12,192,192]{3,2,1,0:T(8,128)(2,1)} %blocks_ref.1) | copy-start | bytes 7962628
  11.2 3.5 %copy-start = (f32[576,256]{1,0:T(8,128)S(1)}, f32[576,256]{1,0:T(8,128)}, u32[]{:S(2)}) copy-start(f32[576,256]{1,0:T(8,128)} %refs_7_.1) | copy-start | bytes 1769476
  11.2 3.5 %copy-start.6 = (s32[3,12]{1,0:T(4,128)S(1)}, s32[3,12]{1,0:T(4,128)}, u32[]{:S(2)}) copy-start(s32[3,12]{1,0:T(4,128)} %refs_0_.5) | copy-start | bytes 436
  11.2 3.5 %copy-start.7 = (s32[3]{0:T(128)S(1)}, s32[3]{0:T(128)}, u32[]{:S(2)}) copy-start(s32[3]{0:T(128)} %refs_1_.5) | copy-start | bytes 40
  11.2 3.5 %copy-start.8 = (f32[2]{0:T(128)S(1)}, f32[2]{0:T(128)}, u32[]{:S(2)}) copy-start(f32[2]{0:T(128)} %refs_6_.5) | copy-start | bytes 28
  20.5 4.1 %collective-permute-start.2 = (bf16[592,256]{1,0:T(8,128)(2,1)}, bf16[592,256]{1,0:T(8,128)(2,1)S(1)}, u32[]{:S(2)}, u32[]{:S(2)}) collective-permute-start(bf16[592,256]{1,0:T(8,128)(2,1)} %collective-permute-done), channel_id=1, source_target_pairs={{0,1},{1,0},{2,3},{3,2},{4,5},{5,4},{6,7},{7,6},{8,9},{9,8},{10,11... | collective-permute-start | bytes 909320 | tf_op jit(solution)/shard_map/ppermute | solution.py:384
  22.1 2.5 %collective-permute-start.3 = (bf16[592,256]{1,0:T(8,128)(2,1)}, bf16[592,256]{1,0:T(8,128)(2,1)S(1)}, u32[]{:S(2)}, u32[]{:S(2)}) collective-permute-start(bf16[592,256]{1,0:T(8,128)(2,1)} %collective-permute-done.1), channel_id=1, source_target_pairs={{0,1},{1,0},{2,3},{3,2},{4,5},{5,4},{6,7},{7,6},{8,9},{9,8},{10,11... | collective-permute-start | bytes 909320 | tf_op jit(solution)/shard_map/ppermute | solution.py:384
  25.8 13.5 %collective-permute-start.4 = (bf16[576,256]{1,0:T(8,128)(2,1)S(1)}, bf16[576,256]{1,0:T(8,128)(2,1)S(1)}, u32[]{:S(2)}, u32[]{:S(2)}) collective-permute-start(bf16[576,256]{1,0:T(8,128)(2,1)S(1)} %get-tuple-element.33), channel_id=1, source_target_pairs={{0,2},{2,4},{4,6},{6,8},{8,10},{10,12},{12,14},{14,16},{16,18},{18... | collective-permute-start | bytes 884744 | tf_op jit(solution)/shard_map/ppermute | solution.py:27
  27.1 14.5 %collective-permute-start.6 = (bf16[576,256]{1,0:T(8,128)(2,1)S(1)}, bf16[576,256]{1,0:T(8,128)(2,1)S(1)}, u32[]{:S(2)}, u32[]{:S(2)}) collective-permute-start(bf16[576,256]{1,0:T(8,128)(2,1)S(1)} %get-tuple-element.33), channel_id=1, source_target_pairs={{0,30},{2,0},{4,2},{6,4},{8,6},{10,8},{12,10},{14,12},{16,14},{18,... | collective-permute-start | bytes 884744 | tf_op jit(solution)/shard_map/ppermute | solution.py:27
  39.3 4.7 %collective-permute-start.5 = (bf16[576,256]{1,0:T(8,128)(2,1)S(1)}, bf16[576,256]{1,0:T(8,128)(2,1)S(1)}, u32[]{:S(2)}, u32[]{:S(2)}) collective-permute-start(bf16[576,256]{1,0:T(8,128)(2,1)S(1)} %collective-permute-done.4), channel_id=1, source_target_pairs={{0,1},{1,0},{2,3},{3,2},{4,5},{5,4},{6,7},{7,6},{8,9},{9,8},{10,11... | collective-permute-start | bytes 884744 | tf_op jit(solution)/shard_map/ppermute | solution.py:384
  41.5 2.5 %collective-permute-start.7 = (bf16[576,256]{1,0:T(8,128)(2,1)S(1)}, bf16[576,256]{1,0:T(8,128)(2,1)S(1)}, u32[]{:S(2)}, u32[]{:S(2)}) collective-permute-start(bf16[576,256]{1,0:T(8,128)(2,1)S(1)} %collective-permute-done.6), channel_id=1, source_target_pairs={{0,1},{1,0},{2,3},{3,2},{4,5},{5,4},{6,7},{7,6},{8,9},{9,8},{10,11... | collective-permute-start | bytes 884744 | tf_op jit(solution)/shard_map/ppermute | solution.py:384
  46.7 5.4 %collective-permute-start.8 = (bf16[576,256]{1,0:T(8,128)(2,1)}, bf16[576,256]{1,0:T(8,128)(2,1)}, u32[]{:S(2)}, u32[]{:S(2)}) collective-permute-start(bf16[576,256]{1,0:T(8,128)(2,1)} %get-tuple-element.35), channel_id=1, source_target_pairs={{0,1},{1,0},{2,3},{3,2},{4,5},{5,4},{6,7},{7,6},{8,9},{9,8},{10,11... | collective-permute-start | bytes 884744 | tf_op jit(solution)/shard_map/ppermute | solution.py:384
  47.1 13.3 %collective-permute-start.11 = (bf16[576,256]{1,0:T(8,128)(2,1)}, bf16[576,256]{1,0:T(8,128)(2,1)}, u32[]{:S(2)}, u32[]{:S(2)}) collective-permute-start(bf16[576,256]{1,0:T(8,128)(2,1)} %get-tuple-element.35), channel_id=1, source_target_pairs={{0,2},{2,4},{4,6},{6,8},{8,10},{10,12},{12,14},{14,16},{16,18},{18... | collective-permute-start | bytes 884744 | tf_op jit(solution)/shard_map/ppermute | solution.py:27
  47.5 15.4 %collective-permute-start.12 = (bf16[576,256]{1,0:T(8,128)(2,1)}, bf16[576,256]{1,0:T(8,128)(2,1)}, u32[]{:S(2)}, u32[]{:S(2)}) collective-permute-start(bf16[576,256]{1,0:T(8,128)(2,1)} %get-tuple-element.35), channel_id=1, source_target_pairs={{0,30},{2,0},{4,2},{6,4},{8,6},{10,8},{12,10},{14,12},{16,14},{18,... | collective-permute-start | bytes 884744 | tf_op jit(solution)/shard_map/ppermute | solution.py:27
  52.2 1.1 copy-start.3
  55.9 0.8 copy-start.9
  58.0 5.9 %collective-permute-start.9 = (f32[192,128]{1,0:T(8,128)}, f32[192,128]{1,0:T(8,128)}, u32[]{:S(2)}, u32[]{:S(2)}) collective-permute-start(f32[192,128]{1,0:T(8,128)} %slice.63), channel_id=1, source_target_pairs={{0,1},{1,0},{2,3},{3,2},{4,5},{5,4},{6,7},{7,6},{8,9},{9,8},{10,11... | collective-permute-start | bytes 294920 | tf_op jit(solution)/shard_map/ppermute | solution.py:320
  60.4 8.5 %collective-permute-start.13 = (bf16[576,256]{1,0:T(8,128)(2,1)}, bf16[576,256]{1,0:T(8,128)(2,1)S(1)}, u32[]{:S(2)}, u32[]{:S(2)}) collective-permute-start(bf16[576,256]{1,0:T(8,128)(2,1)} %collective-permute-done.11), channel_id=1, source_target_pairs={{0,1},{1,0},{2,3},{3,2},{4,5},{5,4},{6,7},{7,6},{8,9},{9,8},{10,11... | collective-permute-start | bytes 884744 | tf_op jit(solution)/shard_map/ppermute | solution.py:384
  62.9 6.0 %collective-permute-start.14 = (bf16[576,256]{1,0:T(8,128)(2,1)}, bf16[576,256]{1,0:T(8,128)(2,1)S(1)}, u32[]{:S(2)}, u32[]{:S(2)}) collective-permute-start(bf16[576,256]{1,0:T(8,128)(2,1)} %collective-permute-done.12), channel_id=1, source_target_pairs={{0,1},{1,0},{2,3},{3,2},{4,5},{5,4},{6,7},{7,6},{8,9},{9,8},{10,11... | collective-permute-start | bytes 884744 | tf_op jit(solution)/shard_map/ppermute | solution.py:384
  64.8 4.0 %collective-permute-start.10 = (f32[96,128]{1,0:T(8,128)S(1)}, f32[96,128]{1,0:T(8,128)S(1)}, u32[]{:S(2)}, u32[]{:S(2)}) collective-permute-start(f32[96,128]{1,0:T(8,128)S(1)} %slice.81), channel_id=1, source_target_pairs={{0,4},{2,6},{4,0},{6,2},{8,12},{10,14},{12,8},{14,10},{16,20},{18,... | collective-permute-start | bytes 147464 | tf_op jit(solution)/shard_map/ppermute | solution.py:320
  66.1 1.1 copy-start.10
  67.1 1.8 %copy-start.4 = (f32[576,256]{1,0:T(8,128)S(1)}, f32[576,256]{1,0:T(8,128)}, u32[]{:S(2)}) copy-start(f32[576,256]{1,0:T(8,128)} %copy-done.2) | copy-start | bytes 1769476
  71.7 1.4 %collective-permute-start.15 = (f32[128,256]{1,0:T(8,128)S(1)}, f32[128,256]{1,0:T(8,128)S(1)}, u32[]{:S(2)}, u32[]{:S(2)}) collective-permute-start(f32[128,256]{1,0:T(8,128)S(1)} %slice.83), channel_id=1, source_target_pairs={{0,1},{1,0},{2,3},{3,2},{4,5},{5,4},{6,7},{7,6},{8,9},{9,8},{10,11... | collective-permute-start | bytes 393224 | tf_op jit(solution)/shard_map/ppermute | solution.py:320
  73.2 4.5 %collective-permute-start.16 = (f32[112,256]{1,0:T(8,128)S(1)}, f32[112,256]{1,0:T(8,128)S(1)}, u32[]{:S(2)}, u32[]{:S(2)}) collective-permute-start(f32[112,256]{1,0:T(8,128)S(1)} %fusion.2), channel_id=1, source_target_pairs={{0,2},{2,0},{4,6},{6,4},{8,10},{10,8},{12,14},{14,12},{16,18},{18,... | collective-permute-start | bytes 344072 | tf_op jit(solution)/shard_map/ppermute | solution.py:320
  77.8 3.7 %collective-permute-start.17 = (f32[112,256]{1,0:T(8,128)S(1)}, f32[112,256]{1,0:T(8,128)S(1)}, u32[]{:S(2)}, u32[]{:S(2)}) collective-permute-start(f32[112,256]{1,0:T(8,128)S(1)} %maximum_add_fusion), channel_id=1, source_target_pairs={{0,8},{2,10},{4,12},{6,14},{8,0},{10,2},{12,4},{14,6},{16,24},{18,... | collective-permute-start | bytes 344072 | tf_op jit(solution)/shard_map/ppermute | solution.py:320
  81.5 5.8 %collective-permute-start.18 = (f32[112,256]{1,0:T(8,128)S(1)}, f32[112,256]{1,0:T(8,128)S(1)}, u32[]{:S(2)}, u32[]{:S(2)}) collective-permute-start(f32[112,256]{1,0:T(8,128)S(1)} %add.52), channel_id=1, source_target_pairs={{0,16},{2,18},{4,20},{6,22},{8,24},{10,26},{12,28},{14,30},{16,0},... | collective-permute-start | bytes 344072 | tf_op jit(solution)/shard_map/ppermute | solution.py:320
  87.4 3.7 %collective-permute-start.19 = (f32[112,256]{1,0:T(8,128)S(1)}, f32[112,256]{1,0:T(8,128)S(1)}, u32[]{:S(2)}, u32[]{:S(2)}) collective-permute-start(f32[112,256]{1,0:T(8,128)S(1)} %add.53), channel_id=1, source_target_pairs={{0,4},{2,6},{4,0},{6,2},{8,12},{10,14},{12,8},{14,10},{16,20},{18,... | collective-permute-start | bytes 344072 | tf_op jit(solution)/shard_map/ppermute | solution.py:320
  91.1 5.6 %collective-permute-start.20 = (f32[192,128]{1,0:T(8,128)S(1)}, f32[192,128]{1,0:T(8,128)S(1)}, u32[]{:S(2)}, u32[]{:S(2)}) collective-permute-start(f32[192,128]{1,0:T(8,128)S(1)} %pad_maximum_fusion.3), channel_id=1, source_target_pairs={{0,1},{1,0},{2,3},{3,2},{4,5},{5,4},{6,7},{7,6},{8,9},{9,8},{10,11... | collective-permute-start | bytes 294920 | tf_op jit(solution)/shard_map/ppermute | solution.py:320
  96.6 9.5 %collective-permute-start.21 = (f32[64,256]{1,0:T(8,128)S(1)}, f32[64,256]{1,0:T(8,128)S(1)}, u32[]{:S(2)}, u32[]{:S(2)}) collective-permute-start(f32[64,256]{1,0:T(8,128)S(1)} %slice_add_fusion.2), channel_id=1, source_target_pairs={{0,2},{2,0},{4,6},{6,4},{8,10},{10,8},{12,14},{14,12},{16,18},{18,... | collective-permute-start | bytes 196616 | tf_op jit(solution)/shard_map/ppermute | solution.py:320
  106.1 2.6 %collective-permute-start.22 = (f32[128,256]{1,0:T(8,128)S(1)}, f32[128,256]{1,0:T(8,128)S(1)}, u32[]{:S(2)}, u32[]{:S(2)}) collective-permute-start(f32[128,256]{1,0:T(8,128)S(1)} %pad_maximum_fusion.1), channel_id=1, source_target_pairs={{0,1},{1,0},{2,3},{3,2},{4,5},{5,4},{6,7},{7,6},{8,9},{9,8},{10,11... | collective-permute-start | bytes 393224 | tf_op jit(solution)/shard_map/ppermute | solution.py:320
  (2 other events, 1.5 us)

commit v17 on v16

--- a/solution.py
+++ b/solution.py
@@ -179,6 +179,12 @@
 
 def over_rows(value, row):
     return jnp.broadcast_to(value[row : row + 1, :], value.shape)
+
+
+def refined_reciprocal(value):
+    guess = pl.reciprocal(value, approx=True)
+    guess = guess * (2.0 - value * guess)
+    return guess * (2.0 - value * guess)
 
 
 def eliminate(tile):
@@ -202,7 +208,7 @@
                 (row, col): over_rows(pivot_cols[col], row) for row in range(GROUP) for col in range(row + 1)
             }
             for pivot in range(GROUP):
-                inverse = 1.0 / scalars[pivot, pivot]
+                inverse = refined_reciprocal(scalars[pivot, pivot])
                 for row in range(pivot + 1, GROUP):
                     multiple = scalars[row, pivot] * inverse
                     for col in range(pivot + 1, row + 1):

time: 111 us -> 112 us (level)
  transfers between devices with their start and end apart: 23 -> 23, of which waited for: 12 -> 12; matrix products, arithmetic and copies ran while one was open for 2% -> 2% of each run, Pallas kernels for 20% -> 21%
where the time goes in v17:
time: 112 us; the launch traced here: 111 us
  starting transfers between devices  34.7 us (31%)
  Pallas kernels  30.8 us (28%)
  waiting for transfers between devices  26.8 us (24%)
  local copies, waits for them, and re-layouts  8.52 us (8%)
  blocking collectives  5.87 us (5%)
  other arithmetic  3.69 us (3%)
    ppermute x6, starting transfers between devices, shifted(): return lax.ppermute(value, axis, pairs)  16.2 us
    ppermute x10, waiting for transfers between devices, partner_value(): lax.ppermute(value, axis, [(at, at ^ bit) for at in range(lax.axis_size(a...  15.4 us
    ppermute x10, starting transfers between devices, partner_value(): lax.ppermute(value, axis, [(at, at ^ bit) for at in range(lax.axis_size(a...  12 us
    ppermute x6, waiting for transfers between devices, shifted(): return lax.ppermute(value, axis, pairs)  11.3 us
    pallas_call x5, Pallas kernels, halo_part(): return call(table, bases, held, *pair, total, *scalars, *extra)  8.8 us
    ppermute x7, starting transfers between devices, local(): swapped = lambda value: lax.ppermute(value, 'split', [(0, 1), (1, 0)])  6.52 us
    unnamed x24, local copies, waits for them, and re-layouts  6.46 us
    all_gather x2, blocking collectives, exchange(): groups = [lax.all_gather(operand, 'split', axis=0)]  5.87 us
  transfers between devices with their start and end apart: 23, of which 12 were waited for; matrix products, arithmetic and copies ran while one was open for 2% of the time, Pallas kernels for 21%

profile of v17, /device:TPU:1, one launch (start us, length us, event | category | flops | bytes accessed | tf_op | source)
XLA Modules:
  0.0 111.3 jit_solution(16969475863779935575)
XLA Ops:
  3.2 2.0 %collective-permute-start = (bf16[592,256]{1,0:T(8,128)(2,1)}, bf16[592,256]{1,0:T(8,128)(2,1)}, u32[]{:S(2)}, u32[]{:S(2)}) collective-permute-start(bf16[592,256]{1,0:T(8,128)(2,1)} %fusion.1), channel_id=1, source_target_pairs={{0,2},{2,4},{4,6},{6,8},{8,10},{10,12},{12,14},{14,16},{16,18},{18... | collective-permute-start | bytes 909320 | tf_op jit(solution)/shard_map/ppermute | solution.py:27
  5.2 4.0 %collective-permute-start.1 = (bf16[592,256]{1,0:T(8,128)(2,1)}, bf16[592,256]{1,0:T(8,128)(2,1)}, u32[]{:S(2)}, u32[]{:S(2)}) collective-permute-start(bf16[592,256]{1,0:T(8,128)(2,1)} %fusion.1), channel_id=1, source_target_pairs={{0,30},{2,0},{4,2},{6,4},{8,6},{10,8},{12,10},{14,12},{16,14},{18,... | collective-permute-start | bytes 909320 | tf_op jit(solution)/shard_map/ppermute | solution.py:27
  9.2 2.0 %copy-done.1 = bf16[3,12,192,192]{3,2,1,0:T(8,128)(2,1)S(1)} copy-done((bf16[3,12,192,192]{3,2,1,0:T(8,128)(2,1)S(1)}, bf16[3,12,192,192]{3,2,1,0:T(8,128)(2,1)}, u32[]{:S(2)}) %copy-start.1) | copy-done | bytes 2654232
  11.6 3.0 %all-gather = bf16[1184,256]{1,0:T(8,128)(2,1)S(1)} all-gather(bf16[592,256]{1,0:T(8,128)(2,1)} %fusion.1), channel_id=2, replica_groups=mesh['region'=16,'split'=2] {'split'}, dimensions={0}, use_global_device_ids=true | all-gather | bytes 909312 | tf_op jit(solution)/shard_map/all_gather | solution.py:417
  14.7 1.4 %shard_map.78.refs_4_ = f32[576,256]{1,0:T(8,128)S(1)} custom-call(s32[3,12]{1,0:T(4,128)S(1)} %copy-done.6, s32[3]{0:T(128)S(1)} %copy-done.7, s32[2]{0:T(128)S(1)} %broadcast_1_refs_2_.2.refs_2_, bf16[3,12,192,192]{3,2,1,0:T(8,128)(2,1)S(1)} %shard_map.77.refs_3_.refs_1_.refs_2_, bf16[2,592,256]{2,1,0:T(8,128)(2,1)S(1)} %bitcast.22, f32[2]{0:T(128)S(1)} %copy-done.8, ...), custom_call_target="tpu_custom_call" | custom-call | flops 10000000 | bytes 276480 | tf_op jit(solution)/shard_map/pallas_call | solution.py:458
  16.1 1.7 %collective-permute-done = bf16[592,256]{1,0:T(8,128)(2,1)} collective-permute-done((bf16[592,256]{1,0:T(8,128)(2,1)}, bf16[592,256]{1,0:T(8,128)(2,1)}, u32[]{:S(2)}, u32[]{:S(2)}) %collective-permute-start) | collective-permute-done | bytes 303136 | tf_op jit(solution)/shard_map/ppermute | solution.py:27
  20.5 1.6 %collective-permute-start.2 = (bf16[592,256]{1,0:T(8,128)(2,1)}, bf16[592,256]{1,0:T(8,128)(2,1)S(1)}, u32[]{:S(2)}, u32[]{:S(2)}) collective-permute-start(bf16[592,256]{1,0:T(8,128)(2,1)} %collective-permute-done), channel_id=1, source_target_pairs={{0,1},{1,0},{2,3},{3,2},{4,5},{5,4},{6,7},{7,6},{8,9},{9,8},{10,11... | collective-permute-start | bytes 909320 | tf_op jit(solution)/shard_map/ppermute | solution.py:390
  22.2 2.4 %shard_map.79 = (f32[576,256]{1,0:T(8,128)S(1)}, s32[3,13]{1,0:T(4,128)S(1)}) custom-call(s32[3,12]{1,0:T(4,128)S(1)} %copy-done.6, s32[3]{0:T(128)S(1)} %copy-done.7, s32[2,6]{1,0:T(2,128)S(1)} %maximum_convert_fusion.lists_ref, s32[2]{0:T(128)S(1)} %pad_add_fusion.refs_0_.refs_1_.refs_2_, bf16[3,12,192,192]{3,2,1,0:T(8,128)(2,1)S(1)} %shard_map.77.refs_3_.refs_1_.refs_2_, ...), custom_call_target="tpu_custom_call" | custom-call | flops 30000001024 | bytes 276480 | tf_op jit(solution)/shard_map/pallas_call | solution.py:479
  25.8 1.3 %collective-permute-start.4 = (bf16[576,256]{1,0:T(8,128)(2,1)S(1)}, bf16[576,256]{1,0:T(8,128)(2,1)S(1)}, u32[]{:S(2)}, u32[]{:S(2)}) collective-permute-start(bf16[576,256]{1,0:T(8,128)(2,1)S(1)} %get-tuple-element.33), channel_id=1, source_target_pairs={{0,2},{2,4},{4,6},{6,8},{8,10},{10,12},{12,14},{14,16},{16,18},{18... | collective-permute-start | bytes 884744 | tf_op jit(solution)/shard_map/ppermute | solution.py:27
  27.1 3.8 %collective-permute-start.6 = (bf16[576,256]{1,0:T(8,128)(2,1)S(1)}, bf16[576,256]{1,0:T(8,128)(2,1)S(1)}, u32[]{:S(2)}, u32[]{:S(2)}) collective-permute-start(bf16[576,256]{1,0:T(8,128)(2,1)S(1)} %get-tuple-element.33), channel_id=1, source_target_pairs={{0,30},{2,0},{4,2},{6,4},{8,6},{10,8},{12,10},{14,12},{16,14},{18,... | collective-permute-start | bytes 884744 | tf_op jit(solution)/shard_map/ppermute | solution.py:27
  30.9 2.8 %all-gather.1 = bf16[1152,256]{1,0:T(8,128)(2,1)S(1)} all-gather(bf16[576,256]{1,0:T(8,128)(2,1)S(1)} %get-tuple-element.33), channel_id=3, replica_groups=mesh['region'=16,'split'=2] {'split'}, dimensions={0}, use_global_device_ids=true | all-gather | bytes 884736 | tf_op jit(solution)/shard_map/all_gather | solution.py:417
  33.7 1.4 %shard_map.81.refs_5_ = f32[576,256]{1,0:T(8,128)S(1)} custom-call(s32[3,12]{1,0:T(4,128)S(1)} %copy-done.6, s32[3]{0:T(128)S(1)} %copy-done.7, s32[2]{0:T(128)S(1)} %broadcast_1_refs_2_.2.refs_2_, bf16[3,12,192,192]{3,2,1,0:T(8,128)(2,1)S(1)} %shard_map.77.refs_3_.refs_1_.refs_2_, bf16[2,576,256]{2,1,0:T(8,128)(2,1)S(1)} %bitcast.23, f32[2]{0:T(128)S(1)} %copy-done.8, ...), custom_call_target="tpu_custom_call" | custom-call | flops 10000000 | bytes 276480 | tf_op jit(solution)/shard_map/pallas_call | solution.py:458
  35.1 4.2 %collective-permute-done.4 = bf16[576,256]{1,0:T(8,128)(2,1)S(1)} collective-permute-done((bf16[576,256]{1,0:T(8,128)(2,1)S(1)}, bf16[576,256]{1,0:T(8,128)(2,1)S(1)}, u32[]{:S(2)}, u32[]{:S(2)}) %collective-permute-start.4) | collective-permute-done | bytes 294944 | tf_op jit(solution)/shard_map/ppermute | solution.py:27
  39.3 1.3 %collective-permute-start.5 = (bf16[576,256]{1,0:T(8,128)(2,1)S(1)}, bf16[576,256]{1,0:T(8,128)(2,1)S(1)}, u32[]{:S(2)}, u32[]{:S(2)}) collective-permute-start(bf16[576,256]{1,0:T(8,128)(2,1)S(1)} %collective-permute-done.4), channel_id=1, source_target_pairs={{0,1},{1,0},{2,3},{3,2},{4,5},{5,4},{6,7},{7,6},{8,9},{9,8},{10,11... | collective-permute-start | bytes 884744 | tf_op jit(solution)/shard_map/ppermute | solution.py:390
  41.5 1.3 %collective-permute-start.7 = (bf16[576,256]{1,0:T(8,128)(2,1)S(1)}, bf16[576,256]{1,0:T(8,128)(2,1)S(1)}, u32[]{:S(2)}, u32[]{:S(2)}) collective-permute-start(bf16[576,256]{1,0:T(8,128)(2,1)S(1)} %collective-permute-done.6), channel_id=1, source_target_pairs={{0,1},{1,0},{2,3},{3,2},{4,5},{5,4},{6,7},{7,6},{8,9},{9,8},{10,11... | collective-permute-start | bytes 884744 | tf_op jit(solution)/shard_map/ppermute | solution.py:390
  44.0 1.9 %shard_map.83 = (f32[576,256]{1,0:T(8,128)S(1)}, bf16[576,256]{1,0:T(8,128)(2,1)}) custom-call(s32[3,13]{1,0:T(4,128)S(1)} %get-tuple-element.31.refs_0_, s32[2]{0:T(128)S(1)} %pad_add_fusion.refs_0_.refs_1_.refs_2_, bf16[3,12,192,192]{3,2,1,0:T(8,128)(2,1)S(1)} %shard_map.77.refs_3_.refs_1_.refs_2_, bf16[1,576,256]{2,1,0:T(8,128)(2,1)S(1)} %bitcast.30, ...), custom_call_target="tpu_custom_call" | custom-call | flops 30000001024 | bytes 276480 | tf_op jit(solution)/shard_map/pallas_call | solution.py:463
  47.5 4.6 %collective-permute-start.12 = (bf16[576,256]{1,0:T(8,128)(2,1)}, bf16[576,256]{1,0:T(8,128)(2,1)}, u32[]{:S(2)}, u32[]{:S(2)}) collective-permute-start(bf16[576,256]{1,0:T(8,128)(2,1)} %get-tuple-element.35), channel_id=1, source_target_pairs={{0,30},{2,0},{4,2},{6,4},{8,6},{10,8},{12,10},{14,12},{16,14},{18,... | collective-permute-start | bytes 884744 | tf_op jit(solution)/shard_map/ppermute | solution.py:27
  53.2 2.6 %shard_map.84 = (f32[576,256]{1,0:T(8,128)S(1)}, f32[384,128]{1,0:T(8,128)S(1)}) custom-call(s32[3,12]{1,0:T(4,128)S(1)} %copy-done.6, s32[3]{0:T(128)S(1)} %copy-done.7, s32[2]{0:T(128)S(1)} %pad_add_fusion.refs_0_.refs_1_.refs_2_, bf16[3,12,192,192]{3,2,1,0:T(8,128)(2,1)S(1)} %shard_map.77.refs_3_.refs_1_.refs_2_, bf16[1,576,256]{2,1,0:T(8,128)(2,1)} %bitcast.13.refs_4_, ...), custom_call_target="tpu_custom_call" | custom-call | flops 10000000 | bytes 276480 | tf_op jit(solution)/shard_map/pallas_call | solution.py:458
  58.7 1.7 %collective-permute-done.11 = bf16[576,256]{1,0:T(8,128)(2,1)} collective-permute-done((bf16[576,256]{1,0:T(8,128)(2,1)}, bf16[576,256]{1,0:T(8,128)(2,1)}, u32[]{:S(2)}, u32[]{:S(2)}) %collective-permute-start.11) | collective-permute-done | bytes 294944 | tf_op jit(solution)/shard_map/ppermute | solution.py:27
  61.4 1.5 %collective-permute-done.12 = bf16[576,256]{1,0:T(8,128)(2,1)} collective-permute-done((bf16[576,256]{1,0:T(8,128)(2,1)}, bf16[576,256]{1,0:T(8,128)(2,1)}, u32[]{:S(2)}, u32[]{:S(2)}) %collective-permute-start.12) | collective-permute-done | bytes 294944 | tf_op jit(solution)/shard_map/ppermute | solution.py:27
  67.1 1.7 %shard_map.85 = (f32[576,256]{1,0:T(8,128)S(1)}, f32[8,128]{1,0:T(8,128)S(1)}) custom-call(s32[3,13]{1,0:T(4,128)S(1)} %get-tuple-element.31.refs_0_, s32[2]{0:T(128)S(1)} %pad_add_fusion.refs_0_.refs_1_.refs_2_, bf16[3,12,192,192]{3,2,1,0:T(8,128)(2,1)S(1)} %shard_map.77.refs_3_.refs_1_.refs_2_, bf16[1,576,256]{2,1,0:T(8,128)(2,1)} %bitcast.16.refs_3_, ...), custom_call_target="tpu_custom_call" | custom-call | flops 30000001024 | bytes 276480 | tf_op jit(solution)/shard_map/pallas_call | solution.py:463
  68.9 2.8 %shard_map.86 = f32[256,256]{1,0:T(8,128)S(1)} custom-call(s32[3,13]{1,0:T(4,128)S(1)} %get-tuple-element.31.refs_0_, s32[2]{0:T(128)S(1)} %pad_add_fusion.refs_0_.refs_1_.refs_2_, bf16[3,12,192,192]{3,2,1,0:T(8,128)(2,1)S(1)} %shard_map.77.refs_3_.refs_1_.refs_2_, bf16[1,576,256]{2,1,0:T(8,128)(2,1)S(1)} %bitcast.26, bf16[1,576,256]{2,1,0:T(8,128)(2,1)S(1)} %bitcast.27, ...), custom_call_target="tpu_custom_call" | custom-call | flops 30000001024 | bytes 276480 | tf_op jit(solution)/shard_map/pallas_call | solution.py:463
  73.3 4.4 %collective-permute-done.16 = f32[112,256]{1,0:T(8,128)S(1)} collective-permute-done((f32[112,256]{1,0:T(8,128)S(1)}, f32[112,256]{1,0:T(8,128)S(1)}, u32[]{:S(2)}, u32[]{:S(2)}) %collective-permute-start.16) | collective-permute-done | bytes 114720 | tf_op jit(solution)/shard_map/ppermute | solution.py:326
  78.9 2.6 %collective-permute-done.17 = f32[112,256]{1,0:T(8,128)S(1)} collective-permute-done((f32[112,256]{1,0:T(8,128)S(1)}, f32[112,256]{1,0:T(8,128)S(1)}, u32[]{:S(2)}, u32[]{:S(2)}) %collective-permute-start.17) | collective-permute-done | bytes 114720 | tf_op jit(solution)/shard_map/ppermute | solution.py:326
  81.5 2.2 %collective-permute-start.18 = (f32[112,256]{1,0:T(8,128)S(1)}, f32[112,256]{1,0:T(8,128)S(1)}, u32[]{:S(2)}, u32[]{:S(2)}) collective-permute-start(f32[112,256]{1,0:T(8,128)S(1)} %add.52), channel_id=1, source_target_pairs={{0,16},{2,18},{4,20},{6,22},{8,24},{10,26},{12,28},{14,30},{16,0},... | collective-permute-start | bytes 344072 | tf_op jit(solution)/shard_map/ppermute | solution.py:326
  83.6 3.7 %collective-permute-done.18 = f32[112,256]{1,0:T(8,128)S(1)} collective-permute-done((f32[112,256]{1,0:T(8,128)S(1)}, f32[112,256]{1,0:T(8,128)S(1)}, u32[]{:S(2)}, u32[]{:S(2)}) %collective-permute-start.18) | collective-permute-done | bytes 114720 | tf_op jit(solution)/shard_map/ppermute | solution.py:326
  88.3 2.8 %collective-permute-done.19 = f32[112,256]{1,0:T(8,128)S(1)} collective-permute-done((f32[112,256]{1,0:T(8,128)S(1)}, f32[112,256]{1,0:T(8,128)S(1)}, u32[]{:S(2)}, u32[]{:S(2)}) %collective-permute-start.19) | collective-permute-done | bytes 114720 | tf_op jit(solution)/shard_map/ppermute | solution.py:326
  91.1 4.6 %collective-permute-start.20 = (f32[192,128]{1,0:T(8,128)S(1)}, f32[192,128]{1,0:T(8,128)S(1)}, u32[]{:S(2)}, u32[]{:S(2)}) collective-permute-start(f32[192,128]{1,0:T(8,128)S(1)} %pad_maximum_fusion.3), channel_id=1, source_target_pairs={{0,1},{1,0},{2,3},{3,2},{4,5},{5,4},{6,7},{7,6},{8,9},{9,8},{10,11... | collective-permute-start | bytes 294920 | tf_op jit(solution)/shard_map/ppermute | solution.py:326
  96.7 5.4 %shard_map.87 = (f32[128,128]{1,0:T(8,128)S(1)}, f32[128,128]{1,0:T(8,128)S(1)}, f32[128,128]{1,0:T(8,128)S(1)}) custom-call(s32[1]{0:T(128)} %bitcast.15.refs_6_.number_ref, f32[384,128]{1,0:T(8,128)S(1)} %constant_dynamic-update-slice_fusion.gram_ref), custom_call_target="tpu_custom_call" | custom-call | flops 100000000 | bytes 3072 | tf_op jit(solution)/shard_map/pallas_call | solution.py:303
  102.1 4.8 %shard_map.88 = (f32[128,128]{1,0:T(8,128)S(1)}, f32[128,128]{1,0:T(8,128)S(1)}, f32[128,128]{1,0:T(8,128)S(1)}) custom-call(f32[128,128]{1,0:T(8,128)S(1)} %get-tuple-element.45.refs_0_, f32[128,128]{1,0:T(8,128)S(1)} %get-tuple-element.46.refs_1_, f32[128,128]{1,0:T(8,128)S(1)} %get-tuple-element.47.refs_2_), custom_call_target="tpu_custom_call" | custom-call | flops 100000000 | bytes 1024 | tf_op jit(solution)/shard_map/pallas_call | solution.py:309
  107.7 1.9 %shard_map.89 = (f32[576,256]{1,0:T(8,128)}, f32[256,256]{1,0:T(8,128)S(1)}) custom-call(f32[128,128]{1,0:T(8,128)S(1)} %get-tuple-element.52.refs_0_, f32[128,128]{1,0:T(8,128)S(1)} %get-tuple-element.53.refs_1_, f32[128,128]{1,0:T(8,128)S(1)} %get-tuple-element.54.refs_2_, f32[576,256]{1,0:T(8,128)S(1)} %copy-done.4), custom_call_target="tpu_custom_call" | custom-call | flops 100000000 | bytes 9216 | tf_op jit(solution)/shard_map/pallas_call | solution.py:316
  109.6 1.7 %shard_map.90 = f32[256,256]{1,0:T(8,128)} custom-call(s32[1]{0:T(128)} %bitcast.20.refs_6_.number_ref, f32[256,256]{1,0:T(8,128)S(1)} %pad_maximum_fusion.cross_ref, f32[256,256]{1,0:T(8,128)S(1)} %get-tuple-element.59.inverse_ref), custom_call_target="tpu_custom_call" | custom-call | flops 150994944 | bytes 276480 | tf_op jit(solution)/shard_map/pallas_call | solution.py:525
  (81 shorter events, 25.2 us)
Async XLA Ops:
  3.2 14.7 %collective-permute-start = (bf16[592,256]{1,0:T(8,128)(2,1)}, bf16[592,256]{1,0:T(8,128)(2,1)}, u32[]{:S(2)}, u32[]{:S(2)}) collective-permute-start(bf16[592,256]{1,0:T(8,128)(2,1)} %fusion.1), channel_id=1, source_target_pairs={{0,2},{2,4},{4,6},{6,8},{8,10},{10,12},{12,14},{14,16},{16,18},{18... | collective-permute-start | bytes 909320 | tf_op jit(solution)/shard_map/ppermute | solution.py:27
  5.2 14.6 %collective-permute-start.1 = (bf16[592,256]{1,0:T(8,128)(2,1)}, bf16[592,256]{1,0:T(8,128)(2,1)}, u32[]{:S(2)}, u32[]{:S(2)}) collective-permute-start(bf16[592,256]{1,0:T(8,128)(2,1)} %fusion.1), channel_id=1, source_target_pairs={{0,30},{2,0},{4,2},{6,4},{8,6},{10,8},{12,10},{14,12},{16,14},{18,... | collective-permute-start | bytes 909320 | tf_op jit(solution)/shard_map/ppermute | solution.py:27
  9.2 2.0 %copy-start.1 = (bf16[3,12,192,192]{3,2,1,0:T(8,128)(2,1)S(1)}, bf16[3,12,192,192]{3,2,1,0:T(8,128)(2,1)}, u32[]{:S(2)}) copy-start(bf16[3,12,192,192]{3,2,1,0:T(8,128)(2,1)} %blocks_ref.1) | copy-start | bytes 7962628
  11.2 3.5 %copy-start = (f32[576,256]{1,0:T(8,128)S(1)}, f32[576,256]{1,0:T(8,128)}, u32[]{:S(2)}) copy-start(f32[576,256]{1,0:T(8,128)} %refs_7_.1) | copy-start | bytes 1769476
  11.2 3.5 %copy-start.6 = (s32[3,12]{1,0:T(4,128)S(1)}, s32[3,12]{1,0:T(4,128)}, u32[]{:S(2)}) copy-start(s32[3,12]{1,0:T(4,128)} %refs_0_.5) | copy-start | bytes 436
  11.2 3.5 %copy-start.7 = (s32[3]{0:T(128)S(1)}, s32[3]{0:T(128)}, u32[]{:S(2)}) copy-start(s32[3]{0:T(128)} %refs_1_.5) | copy-start | bytes 40
  11.2 3.5 %copy-start.8 = (f32[2]{0:T(128)S(1)}, f32[2]{0:T(128)}, u32[]{:S(2)}) copy-start(f32[2]{0:T(128)} %refs_6_.5) | copy-start | bytes 28
  20.5 4.1 %collective-permute-start.2 = (bf16[592,256]{1,0:T(8,128)(2,1)}, bf16[592,256]{1,0:T(8,128)(2,1)S(1)}, u32[]{:S(2)}, u32[]{:S(2)}) collective-permute-start(bf16[592,256]{1,0:T(8,128)(2,1)} %collective-permute-done), channel_id=1, source_target_pairs={{0,1},{1,0},{2,3},{3,2},{4,5},{5,4},{6,7},{7,6},{8,9},{9,8},{10,11... | collective-permute-start | bytes 909320 | tf_op jit(solution)/shard_map/ppermute | solution.py:390
  22.1 2.5 %collective-permute-start.3 = (bf16[592,256]{1,0:T(8,128)(2,1)}, bf16[592,256]{1,0:T(8,128)(2,1)S(1)}, u32[]{:S(2)}, u32[]{:S(2)}) collective-permute-start(bf16[592,256]{1,0:T(8,128)(2,1)} %collective-permute-done.1), channel_id=1, source_target_pairs={{0,1},{1,0},{2,3},{3,2},{4,5},{5,4},{6,7},{7,6},{8,9},{9,8},{10,11... | collective-permute-start | bytes 909320 | tf_op jit(solution)/shard_map/ppermute | solution.py:390
  25.8 13.5 %collective-permute-start.4 = (bf16[576,256]{1,0:T(8,128)(2,1)S(1)}, bf16[576,256]{1,0:T(8,128)(2,1)S(1)}, u32[]{:S(2)}, u32[]{:S(2)}) collective-permute-start(bf16[576,256]{1,0:T(8,128)(2,1)S(1)} %get-tuple-element.33), channel_id=1, source_target_pairs={{0,2},{2,4},{4,6},{6,8},{8,10},{10,12},{12,14},{14,16},{16,18},{18... | collective-permute-start | bytes 884744 | tf_op jit(solution)/shard_map/ppermute | solution.py:27
  27.1 14.5 %collective-permute-start.6 = (bf16[576,256]{1,0:T(8,128)(2,1)S(1)}, bf16[576,256]{1,0:T(8,128)(2,1)S(1)}, u32[]{:S(2)}, u32[]{:S(2)}) collective-permute-start(bf16[576,256]{1,0:T(8,128)(2,1)S(1)} %get-tuple-element.33), channel_id=1, source_target_pairs={{0,30},{2,0},{4,2},{6,4},{8,6},{10,8},{12,10},{14,12},{16,14},{18,... | collective-permute-start | bytes 884744 | tf_op jit(solution)/shard_map/ppermute | solution.py:27
  39.3 4.7 %collective-permute-start.5 = (bf16[576,256]{1,0:T(8,128)(2,1)S(1)}, bf16[576,256]{1,0:T(8,128)(2,1)S(1)}, u32[]{:S(2)}, u32[]{:S(2)}) collective-permute-start(bf16[576,256]{1,0:T(8,128)(2,1)S(1)} %collective-permute-done.4), channel_id=1, source_target_pairs={{0,1},{1,0},{2,3},{3,2},{4,5},{5,4},{6,7},{7,6},{8,9},{9,8},{10,11... | collective-permute-start | bytes 884744 | tf_op jit(solution)/shard_map/ppermute | solution.py:390
  41.5 2.5 %collective-permute-start.7 = (bf16[576,256]{1,0:T(8,128)(2,1)S(1)}, bf16[576,256]{1,0:T(8,128)(2,1)S(1)}, u32[]{:S(2)}, u32[]{:S(2)}) collective-permute-start(bf16[576,256]{1,0:T(8,128)(2,1)S(1)} %collective-permute-done.6), channel_id=1, source_target_pairs={{0,1},{1,0},{2,3},{3,2},{4,5},{5,4},{6,7},{7,6},{8,9},{9,8},{10,11... | collective-permute-start | bytes 884744 | tf_op jit(solution)/shard_map/ppermute | solution.py:390
  46.7 5.4 %collective-permute-start.8 = (bf16[576,256]{1,0:T(8,128)(2,1)}, bf16[576,256]{1,0:T(8,128)(2,1)}, u32[]{:S(2)}, u32[]{:S(2)}) collective-permute-start(bf16[576,256]{1,0:T(8,128)(2,1)} %get-tuple-element.35), channel_id=1, source_target_pairs={{0,1},{1,0},{2,3},{3,2},{4,5},{5,4},{6,7},{7,6},{8,9},{9,8},{10,11... | collective-permute-start | bytes 884744 | tf_op jit(solution)/shard_map/ppermute | solution.py:390
  47.1 13.3 %collective-permute-start.11 = (bf16[576,256]{1,0:T(8,128)(2,1)}, bf16[576,256]{1,0:T(8,128)(2,1)}, u32[]{:S(2)}, u32[]{:S(2)}) collective-permute-start(bf16[576,256]{1,0:T(8,128)(2,1)} %get-tuple-element.35), channel_id=1, source_target_pairs={{0,2},{2,4},{4,6},{6,8},{8,10},{10,12},{12,14},{14,16},{16,18},{18... | collective-permute-start | bytes 884744 | tf_op jit(solution)/shard_map/ppermute | solution.py:27
  47.5 15.4 %collective-permute-start.12 = (bf16[576,256]{1,0:T(8,128)(2,1)}, bf16[576,256]{1,0:T(8,128)(2,1)}, u32[]{:S(2)}, u32[]{:S(2)}) collective-permute-start(bf16[576,256]{1,0:T(8,128)(2,1)} %get-tuple-element.35), channel_id=1, source_target_pairs={{0,30},{2,0},{4,2},{6,4},{8,6},{10,8},{12,10},{14,12},{16,14},{18,... | collective-permute-start | bytes 884744 | tf_op jit(solution)/shard_map/ppermute | solution.py:27
  52.2 1.1 copy-start.3
  55.9 0.8 copy-start.9
  58.0 5.9 %collective-permute-start.9 = (f32[192,128]{1,0:T(8,128)}, f32[192,128]{1,0:T(8,128)}, u32[]{:S(2)}, u32[]{:S(2)}) collective-permute-start(f32[192,128]{1,0:T(8,128)} %slice.63), channel_id=1, source_target_pairs={{0,1},{1,0},{2,3},{3,2},{4,5},{5,4},{6,7},{7,6},{8,9},{9,8},{10,11... | collective-permute-start | bytes 294920 | tf_op jit(solution)/shard_map/ppermute | solution.py:326
  60.4 8.5 %collective-permute-start.13 = (bf16[576,256]{1,0:T(8,128)(2,1)}, bf16[576,256]{1,0:T(8,128)(2,1)S(1)}, u32[]{:S(2)}, u32[]{:S(2)}) collective-permute-start(bf16[576,256]{1,0:T(8,128)(2,1)} %collective-permute-done.11), channel_id=1, source_target_pairs={{0,1},{1,0},{2,3},{3,2},{4,5},{5,4},{6,7},{7,6},{8,9},{9,8},{10,11... | collective-permute-start | bytes 884744 | tf_op jit(solution)/shard_map/ppermute | solution.py:390
  62.9 6.0 %collective-permute-start.14 = (bf16[576,256]{1,0:T(8,128)(2,1)}, bf16[576,256]{1,0:T(8,128)(2,1)S(1)}, u32[]{:S(2)}, u32[]{:S(2)}) collective-permute-start(bf16[576,256]{1,0:T(8,128)(2,1)} %collective-permute-done.12), channel_id=1, source_target_pairs={{0,1},{1,0},{2,3},{3,2},{4,5},{5,4},{6,7},{7,6},{8,9},{9,8},{10,11... | collective-permute-start | bytes 884744 | tf_op jit(solution)/shard_map/ppermute | solution.py:390
  64.8 4.0 %collective-permute-start.10 = (f32[96,128]{1,0:T(8,128)S(1)}, f32[96,128]{1,0:T(8,128)S(1)}, u32[]{:S(2)}, u32[]{:S(2)}) collective-permute-start(f32[96,128]{1,0:T(8,128)S(1)} %slice.81), channel_id=1, source_target_pairs={{0,4},{2,6},{4,0},{6,2},{8,12},{10,14},{12,8},{14,10},{16,20},{18,... | collective-permute-start | bytes 147464 | tf_op jit(solution)/shard_map/ppermute | solution.py:326
  66.1 1.1 copy-start.10
  67.1 1.8 %copy-start.4 = (f32[576,256]{1,0:T(8,128)S(1)}, f32[576,256]{1,0:T(8,128)}, u32[]{:S(2)}) copy-start(f32[576,256]{1,0:T(8,128)} %copy-done.2) | copy-start | bytes 1769476
  71.7 1.4 %collective-permute-start.15 = (f32[128,256]{1,0:T(8,128)S(1)}, f32[128,256]{1,0:T(8,128)S(1)}, u32[]{:S(2)}, u32[]{:S(2)}) collective-permute-start(f32[128,256]{1,0:T(8,128)S(1)} %slice.83), channel_id=1, source_target_pairs={{0,1},{1,0},{2,3},{3,2},{4,5},{5,4},{6,7},{7,6},{8,9},{9,8},{10,11... | collective-permute-start | bytes 393224 | tf_op jit(solution)/shard_map/ppermute | solution.py:326
  73.2 4.5 %collective-permute-start.16 = (f32[112,256]{1,0:T(8,128)S(1)}, f32[112,256]{1,0:T(8,128)S(1)}, u32[]{:S(2)}, u32[]{:S(2)}) collective-permute-start(f32[112,256]{1,0:T(8,128)S(1)} %fusion.2), channel_id=1, source_target_pairs={{0,2},{2,0},{4,6},{6,4},{8,10},{10,8},{12,14},{14,12},{16,18},{18,... | collective-permute-start | bytes 344072 | tf_op jit(solution)/shard_map/ppermute | solution.py:326
  77.8 3.7 %collective-permute-start.17 = (f32[112,256]{1,0:T(8,128)S(1)}, f32[112,256]{1,0:T(8,128)S(1)}, u32[]{:S(2)}, u32[]{:S(2)}) collective-permute-start(f32[112,256]{1,0:T(8,128)S(1)} %maximum_add_fusion), channel_id=1, source_target_pairs={{0,8},{2,10},{4,12},{6,14},{8,0},{10,2},{12,4},{14,6},{16,24},{18,... | collective-permute-start | bytes 344072 | tf_op jit(solution)/shard_map/ppermute | solution.py:326
  81.5 5.8 %collective-permute-start.18 = (f32[112,256]{1,0:T(8,128)S(1)}, f32[112,256]{1,0:T(8,128)S(1)}, u32[]{:S(2)}, u32[]{:S(2)}) collective-permute-start(f32[112,256]{1,0:T(8,128)S(1)} %add.52), channel_id=1, source_target_pairs={{0,16},{2,18},{4,20},{6,22},{8,24},{10,26},{12,28},{14,30},{16,0},... | collective-permute-start | bytes 344072 | tf_op jit(solution)/shard_map/ppermute | solution.py:326
  87.4 3.7 %collective-permute-start.19 = (f32[112,256]{1,0:T(8,128)S(1)}, f32[112,256]{1,0:T(8,128)S(1)}, u32[]{:S(2)}, u32[]{:S(2)}) collective-permute-start(f32[112,256]{1,0:T(8,128)S(1)} %add.53), channel_id=1, source_target_pairs={{0,4},{2,6},{4,0},{6,2},{8,12},{10,14},{12,8},{14,10},{16,20},{18,... | collective-permute-start | bytes 344072 | tf_op jit(solution)/shard_map/ppermute | solution.py:326
  91.1 5.6 %collective-permute-start.20 = (f32[192,128]{1,0:T(8,128)S(1)}, f32[192,128]{1,0:T(8,128)S(1)}, u32[]{:S(2)}, u32[]{:S(2)}) collective-permute-start(f32[192,128]{1,0:T(8,128)S(1)} %pad_maximum_fusion.3), channel_id=1, source_target_pairs={{0,1},{1,0},{2,3},{3,2},{4,5},{5,4},{6,7},{7,6},{8,9},{9,8},{10,11... | collective-permute-start | bytes 294920 | tf_op jit(solution)/shard_map/ppermute | solution.py:326
  96.6 10.3 %collective-permute-start.21 = (f32[64,256]{1,0:T(8,128)S(1)}, f32[64,256]{1,0:T(8,128)S(1)}, u32[]{:S(2)}, u32[]{:S(2)}) collective-permute-start(f32[64,256]{1,0:T(8,128)S(1)} %slice_add_fusion.2), channel_id=1, source_target_pairs={{0,2},{2,0},{4,6},{6,4},{8,10},{10,8},{12,14},{14,12},{16,18},{18,... | collective-permute-start | bytes 196616 | tf_op jit(solution)/shard_map/ppermute | solution.py:326
  107.0 2.6 %collective-permute-start.22 = (f32[128,256]{1,0:T(8,128)S(1)}, f32[128,256]{1,0:T(8,128)S(1)}, u32[]{:S(2)}, u32[]{:S(2)}) collective-permute-start(f32[128,256]{1,0:T(8,128)S(1)} %pad_maximum_fusion.1), channel_id=1, source_target_pairs={{0,1},{1,0},{2,3},{3,2},{4,5},{5,4},{6,7},{7,6},{8,9},{9,8},{10,11... | collective-permute-start | bytes 393224 | tf_op jit(solution)/shard_map/ppermute | solution.py:326
  (2 other events, 1.5 us)

commit v18 on v15

--- a/solution.py
+++ b/solution.py
@@ -31,40 +31,39 @@
     return lax.dot_general(left, right, dims, precision=EXACT, preferred_element_type=jnp.float32)
 
 
-def kernel_call(body, out_shape, in_specs, flops, bytes_accessed, slots=None):
+def kernel_call(body, out_shape, in_specs, flops, bytes_accessed, scratch=()):
     return pl.pallas_call(
         body,
         out_shape=out_shape,
         in_specs=in_specs,
         out_specs=jax.tree.map(lambda out: SMEM if out.dtype == jnp.int32 else VMEM, out_shape),
-        scratch_shapes=[] if slots is None else [pltpu.SMEM(slots, jnp.int32)],
+        scratch_shapes=list(scratch),
         compiler_params=pltpu.CompilerParams(vmem_limit_bytes=VMEM_LIMIT),
         cost_estimate=pl.CostEstimate(flops=flops, bytes_accessed=bytes_accessed // 16, transcendentals=0),
     )
 
 
-def fill_slots(slots_ref, cols_ref, live_ref, first, place_of):
+def fill_slots(slots_ref, cols_ref, live_ref):
     rows, stored = cols_ref.shape
     count = slots_ref.shape[1] - 1
     for row in range(rows):
         for index in range(count):
             slots_ref[row, index] = -1
         for at in range(stored):
-            name = cols_ref[row, at] - first
-            inside = (name >= 0) & (name < count) & (at < live_ref[row])
-            slots_ref[row, jnp.where(inside, place_of(jnp.clip(name, 0, count - 1)), count)] = at
-
-
-def accumulate(slots_ref, hessian_ref, operand_ref, base, total):
+            slots_ref[row, jnp.where(at < live_ref[row], cols_ref[row, at], count)] = at
+
+
+def accumulate(slots_ref, hessian_ref, operand_ref, column_of, total):
     rows, _, size, _ = hessian_ref.shape
     shards, shard_rows, _ = operand_ref.shape
     each = shard_rows // size
     for index in range(shards * each):
         start = index % each * size
         block = operand_ref[index // each, start : start + size, :]
+        column = column_of(index)
         parts = []
         for row in range(rows):
-            slot = slots_ref[row, base + index]
+            slot = slots_ref[row, column]
             live = jnp.where(slot >= 0, 1.0, 0.0).astype(jnp.float32)
             stored = hessian_ref[row, jnp.maximum(slot, 0)]
             parts.append(stored * jnp.broadcast_to(live, (size, size)).astype(jnp.bfloat16))
@@ -77,19 +76,26 @@
     pltpu.sync_copy(blocks_ref, out_ref)
 
 
-def near_body(groups, linear, *refs):
-    cols_ref, live_ref, bases_ref, hessian_ref = refs[:4]
-    operands, (*terms, out_ref, slots_ref) = refs[4 : 4 + groups], refs[4 + groups :]
-    fill_slots(slots_ref, cols_ref, live_ref, 0, lambda name: name)
+def near_sum(slots_ref, bases_ref, hessian_ref, operands):
     total = None
     for at, operand_ref in enumerate(operands):
-        total = accumulate(slots_ref, hessian_ref, operand_ref, bases_ref[at], total)
-    out_ref[...] = linear(total, *terms)
+        total = accumulate(slots_ref, hessian_ref, operand_ref, lambda index: bases_ref[at] + index, total)
+    return total
+
+
+def table_body(cols_ref, live_ref, bases_ref, hessian_ref, operand_ref, bounds_ref, vectors_ref, out_ref, slots_ref):
+    fill_slots(slots_ref, cols_ref, live_ref)
+    out_ref[...] = first_terms(near_sum(slots_ref, bases_ref, hessian_ref, [operand_ref]), bounds_ref, vectors_ref)
+
+
+def near_body(groups, linear, slots_ref, bases_ref, hessian_ref, *refs):
+    operands, (*terms, out_ref) = refs[:groups], refs[groups:]
+    out_ref[...] = linear(near_sum(slots_ref, bases_ref, hessian_ref, operands), *terms)
 
 
 def near_gram_body(groups, *refs):
-    *operands, number_ref, two_ref, out_ref, gram_ref, slots_ref = refs
-    near_body(groups, lambda total: total, *operands, out_ref, slots_ref)
+    *operands, number_ref, two_ref, out_ref, gram_ref = refs
+    near_body(groups, lambda total: total, *operands, out_ref)
     gram_part(number_ref, two_ref, gram_ref)
 
 
@@ -103,40 +109,38 @@
     return total - centre * one_ref[...] - (0.5 * half) * vectors_ref[...]
 
 
-def list_place(lists_ref, name):
+def halo_sum(which, slots_ref, lists_ref, bases_ref, hessian_ref, lower_ref, upper_ref, names_ref):
     halo = lists_ref.shape[1]
-    side = jnp.where(name >= halo, 1, 0).astype(jnp.int32)
-    return side * halo + lists_ref[side, name - side * halo]
-
-
-def halo_total(which, slots_ref, bases_ref, hessian_ref, lower_ref, upper_ref, total_ref):
-    halo = (slots_ref.shape[1] - 1) // 2
-    total = accumulate(slots_ref, hessian_ref, lower_ref, bases_ref[which], total_ref[...])
-    return accumulate(slots_ref, hessian_ref, upper_ref, halo + bases_ref[which], total)
-
-
-def table_body(first, which, cols_ref, live_ref, lists_ref, *refs):
-    *operands, out_ref, slots_ref = refs
-    fill_slots(slots_ref, cols_ref, live_ref, first, lambda name: list_place(lists_ref, name))
-    out_ref[...] = halo_total(which, slots_ref, *operands)
+    near = slots_ref.shape[1] - 1 - 2 * halo
+    for side in range(2):
+        for at in range(halo):
+            names_ref[side * halo + lists_ref[side, at]] = near + side * halo + at
+    total = None
+    for side, operand_ref in enumerate((lower_ref, upper_ref)):
+        first = side * halo + bases_ref[which]
+        total = accumulate(slots_ref, hessian_ref, operand_ref, lambda index: names_ref[first + index], total)
+    return total
 
 
 def middle_body(which, *refs):
-    operands, (out_ref, *token_refs) = refs[:6], refs[6:]
-    total = halo_total(which, *operands)
+    operands, (total_ref, out_ref, token_ref, names_ref, held_ref, done_ref) = refs[:6], refs[6:]
+    copy = pltpu.make_async_copy(total_ref, held_ref, done_ref)
+    copy.start()
+    added = halo_sum(which, *operands, names_ref)
+    copy.wait()
+    total = held_ref[...] + added
     out_ref[...] = total
-    for token_ref in token_refs:
-        token_ref[...] = total[:GROUP, :TILE]
+    token_ref[...] = total[:GROUP, :TILE]
 
 
 def interval(bounds_ref):
     return 0.5 * (bounds_ref[0] + bounds_ref[1]), 0.5 * (bounds_ref[1] - bounds_ref[0])
 
 
-def scaled_body(which, factor, *refs):
-    *operands, bounds_ref, out_ref, cast_ref = refs
+def scaled_body(factor, which, *refs):
+    operands, (total_ref, bounds_ref, out_ref, cast_ref, names_ref) = refs[:6], refs[6:]
     _, half = interval(bounds_ref)
-    value = factor * halo_total(which, *operands) / half
+    value = factor * (total_ref[...] + halo_sum(which, *operands, names_ref)) / half
     out_ref[...] = value
     cast_ref[...] = value.astype(jnp.bfloat16)
 
@@ -168,8 +172,8 @@
 
 
 def third_body(which, *refs):
-    *operands, number_ref, two_ref, _, out_ref = refs
-    image = halo_total(which, *operands)
+    operands, (total_ref, number_ref, two_ref, _, out_ref, names_ref) = refs[:6], refs[6:]
+    image = total_ref[...] + halo_sum(which, *operands, names_ref)
     scatter_pieces(number_ref, out_ref, exact_dot(two_ref[...], image, TN))
 
 
@@ -426,7 +430,8 @@
     near, across, *far = axis_bits("region")
     between = other_cores + far
     gram_number, cross_number = device_number([cores, across]), device_number([cores, near])
-    halo_slots = (row_blocks, 2 * halo_blocks + 1)
+    names = [pltpu.SMEM((2 * halo_blocks,), jnp.int32)]
+    table_shape = jax.ShapeDtypeStruct((row_blocks, region_blocks + 2 * halo_blocks + 1), jnp.int32)
 
     covering, free = 3 * 10 ** 10, 10 ** 7
     token = jax.ShapeDtypeStruct((GROUP, TILE), jnp.float32)
@@ -440,43 +445,37 @@
     )(hessian)
 
     def near_total(body, outs, groups, scalars, terms):
-        specs = [SMEM] * 3 + [VMEM] * (1 + len(groups)) + [SMEM] * len(scalars) + [VMEM] * len(terms)
-        call = kernel_call(body, outs, specs, free, traffic, (row_blocks, region_blocks + 1))
+        specs = [SMEM] * 2 + [VMEM] * (1 + len(groups)) + [SMEM] * len(scalars) + [VMEM] * len(terms)
         near_bases = bases if len(groups) > 1 else jnp.zeros_like(bases)
-        return call(block_cols, live_blocks, near_bases, held, *groups, *scalars, *terms)
-
-    def halo_part(body, outs, table, pair, total, scalars=(), extra=()):
-        specs = [SMEM] * 2 + [VMEM] * 4 + [SMEM] * len(scalars) + [VMEM] * len(extra)
-        call = kernel_call(body, outs, specs, covering, traffic)
-        return call(table, bases, held, *pair, total, *scalars, *extra)
-
-    def pairs_of(lower, upper):
+        return kernel_call(body, outs, specs, free, traffic)(table, near_bases, held, *groups, *scalars, *terms)
+
+    def last_part(body, outs, which, pair, total, scalars, extra=()):
+        specs = [SMEM] * 3 + [VMEM] * 4 + [SMEM] * len(scalars) + [VMEM] * len(extra)
+        call = kernel_call(functools.partial(body, which), outs, specs, covering, traffic, names)
+        return call(table, lists, bases, held, *pair, total, *scalars, *extra)
+
+    def before_last(lower, upper, total):
         *pairs, last = zip(gathered(lower), gathered(upper))
-        return pairs, last
-
-    body_of = functools.partial(near_body, len(first_near), first_terms)
-    (total,) = near_total(body_of, (wide,), first_near, (bounds,), (vectors,))
-    pairs, last = pairs_of(first_lower, first_upper)
-    pairs.append(last)
-    body_of = functools.partial(table_body, region_blocks, 0)
-    table_shape = jax.ShapeDtypeStruct(halo_slots, jnp.int32)
-    specs = [SMEM] * 4 + [VMEM] * 4
-    call = kernel_call(body_of, (wide, table_shape), specs, covering, traffic)
-    if len(pairs) == 1:
-        pairs.append(tuple(jnp.zeros_like(part) for part in last))
-    total, table = call(block_cols, live_blocks, lists, bases, held, *pairs[0], total)
-    which = len(pairs) - 1 if paired else 0
-    body_of = functools.partial(scaled_body, which, 1.0)
-    one, one_cast = halo_part(body_of, (wide, narrow), table, pairs[-1], total, (bounds,))
+        after = jnp.zeros(token.shape, token.dtype)
+        for which, pair in enumerate(pairs):
+            specs = [SMEM] * 3 + [VMEM] * 3 + [pl.BlockSpec(memory_space=pl.ANY)]
+            scratch = names + [pltpu.VMEM((rows, modes), jnp.float32), pltpu.SemaphoreType.DMA(())]
+            body_of = functools.partial(middle_body, which)
+            call = kernel_call(body_of, (wide, token), specs, covering, traffic, scratch)
+            total, after = call(table, lists, bases, held, *pair, total)
+        return total, after, len(pairs), last
+
+    specs = [SMEM] * 3 + [VMEM] * 2 + [SMEM, VMEM]
+    call = kernel_call(table_body, (wide, table_shape), specs, free, traffic)
+    total, table = call(block_cols, live_blocks, jnp.zeros_like(bases), held, *first_near, bounds, vectors)
+    total, _, which, last = before_last(first_lower, first_upper, total)
+    one, one_cast = last_part(functools.partial(scaled_body, 1.0), (wide, narrow), which, last, total, (bounds,))
 
     own, lower, upper = exchange(one_cast)
     body_of = functools.partial(near_body, len(own), second_terms)
     (total,) = near_total(body_of, (wide,), own, (bounds,), (one, vectors))
-    pairs, last = pairs_of(lower, upper)
-    for which, pair in enumerate(pairs):
-        (total,) = halo_part(functools.partial(middle_body, which), (wide,), table, pair, total)
-    body_of = functools.partial(scaled_body, len(pairs), 2.0)
-    two, two_cast = halo_part(body_of, (wide, narrow), table, last, total, (bounds,))
+    total, _, which, last = before_last(lower, upper, total)
+    two, two_cast = last_part(functools.partial(scaled_body, 2.0), (wide, narrow), which, last, total, (bounds,))
 
     own, lower, upper = exchange(two_cast, gather=False)
     packed = jax.ShapeDtypeStruct((tile_rows, TILE), jnp.float32)
@@ -484,13 +483,9 @@
     total, gram = near_total(body_of, (wide, packed), own, (gram_number,), (two,))
     for step_of in [halving(*cores), halving(*across)]:
         gram = step_of(gram)()
-    pairs, last = pairs_of(lower, upper)
-    after = jnp.zeros(token.shape, token.dtype)
-    for which, pair in enumerate(pairs):
-        total, after = halo_part(functools.partial(middle_body, which), (wide, token), table, pair, total)
+    total, after, which, last = before_last(lower, upper, total)
     gram, after = tied(gram, after)
-    body_of = functools.partial(third_body, len(pairs))
-    cross = halo_part(body_of, square, table, last, total, (cross_number,), (two, after))
+    cross = last_part(third_body, square, which, last, total, (cross_number,), (two, after))
     cross = halving(*cores)(cross)()
 
     fold = modes // TILE

time: 111 us -> 111 us (level)
  waiting for transfers between devices: 26.8 us -> 25.3 us
    ppermute x6, waiting for transfers between devices: 11.3 us -> 9.75 us  [shifted(): return lax.ppermute(value, axis, pairs)]
    unnamed x24 -> x26, local copies, waits for them, and re-layouts: 6.46 us -> 7.51 us
  transfers between devices with their start and end apart: 23 -> 23, of which waited for: 12 -> 12; matrix products, arithmetic and copies ran while one was open for 2% -> 2% of each run, Pallas kernels for 20% -> 21%
where the time goes in v18:
time: 111 us
  starting transfers between devices  34.8 us (31%)
  Pallas kernels  30.5 us (27%)
  waiting for transfers between devices  25.3 us (23%)
  local copies, waits for them, and re-layouts  9.56 us (9%)
  blocking collectives  5.87 us (5%)
  other arithmetic  3.69 us (3%)
    ppermute x6, starting transfers between devices, shifted(): return lax.ppermute(value, axis, pairs)  16.2 us
    ppermute x10, waiting for transfers between devices, partner_value(): lax.ppermute(value, axis, [(at, at ^ bit) for at in range(lax.axis_size(a...  15.5 us
    ppermute x10, starting transfers between devices, partner_value(): lax.ppermute(value, axis, [(at, at ^ bit) for at in range(lax.axis_size(a...  12.2 us
    ppermute x6, waiting for transfers between devices, shifted(): return lax.ppermute(value, axis, pairs)  9.75 us
    unnamed x26, local copies, waits for them, and re-layouts  7.51 us
    ppermute x7, starting transfers between devices, local(): swapped = lambda value: lax.ppermute(value, 'split', [(0, 1), (1, 0)])  6.38 us
    pallas_call x3, Pallas kernels, before_last(): total, after = call(table, lists, bases, held, *pair, total)  6.27 us
    pallas_call x3, Pallas kernels, last_part(): return call(table, lists, bases, held, *pair, total, *scalars, *extra)  5.96 us
  transfers between devices with their start and end apart: 23, of which 12 were waited for; matrix products, arithmetic and copies ran while one was open for 2% of the time, Pallas kernels for 21%

profile of v18, /device:TPU:1, one launch (start us, length us, event | category | flops | bytes accessed | tf_op | source)
XLA Modules:
  0.0 110.8 jit_solution(14874836022282922050)
XLA Ops:
  3.2 2.0 %collective-permute-start = (bf16[592,256]{1,0:T(8,128)(2,1)}, bf16[592,256]{1,0:T(8,128)(2,1)}, u32[]{:S(2)}, u32[]{:S(2)}) collective-permute-start(bf16[592,256]{1,0:T(8,128)(2,1)} %fusion.1), channel_id=1, source_target_pairs={{0,2},{2,4},{4,6},{6,8},{8,10},{10,12},{12,14},{14,16},{16,18},{18... | collective-permute-start | bytes 909320 | tf_op jit(solution)/shard_map/ppermute | solution.py:27
  5.2 4.0 %collective-permute-start.1 = (bf16[592,256]{1,0:T(8,128)(2,1)}, bf16[592,256]{1,0:T(8,128)(2,1)}, u32[]{:S(2)}, u32[]{:S(2)}) collective-permute-start(bf16[592,256]{1,0:T(8,128)(2,1)} %fusion.1), channel_id=1, source_target_pairs={{0,30},{2,0},{4,2},{6,4},{8,6},{10,8},{12,10},{14,12},{16,14},{18,... | collective-permute-start | bytes 909320 | tf_op jit(solution)/shard_map/ppermute | solution.py:27
  9.2 2.0 %copy-done.2 = bf16[3,12,192,192]{3,2,1,0:T(8,128)(2,1)S(1)} copy-done((bf16[3,12,192,192]{3,2,1,0:T(8,128)(2,1)S(1)}, bf16[3,12,192,192]{3,2,1,0:T(8,128)(2,1)}, u32[]{:S(2)}) %copy-start.2) | copy-done | bytes 2654232
  11.6 3.0 %all-gather = bf16[1184,256]{1,0:T(8,128)(2,1)S(1)} all-gather(bf16[592,256]{1,0:T(8,128)(2,1)} %fusion.1), channel_id=2, replica_groups=mesh['region'=16,'split'=2] {'split'}, dimensions={0}, use_global_device_ids=true | all-gather | bytes 909312 | tf_op jit(solution)/shard_map/all_gather | solution.py:409
  15.7 1.7 %shard_map.78 = (f32[576,256]{1,0:T(8,128)S(1)}, s32[3,19]{1,0:T(4,128)S(1)}) custom-call(s32[3,12]{1,0:T(4,128)S(1)} %copy-done.7, s32[3]{0:T(128)S(1)} %copy-done.9, s32[2]{0:T(128)S(1)} %broadcast_1_bases_ref.2.bases_ref, bf16[3,12,192,192]{3,2,1,0:T(8,128)(2,1)S(1)} %shard_map.77.hessian_ref.refs_3_.refs_2_, bf16[2,592,256]{2,1,0:T(8,128)(2,1)S(1)} %bitcast.22, ...), custom_call_target="tpu_custom_call" | custom-call | flops 10000000 | bytes 276480 | tf_op jit(solution)/shard_map/pallas_call | solution.py:470
  18.5 1.3 %collective-permute-done.1 = bf16[592,256]{1,0:T(8,128)(2,1)} collective-permute-done((bf16[592,256]{1,0:T(8,128)(2,1)}, bf16[592,256]{1,0:T(8,128)(2,1)}, u32[]{:S(2)}, u32[]{:S(2)}) %collective-permute-start.1) | collective-permute-done | bytes 303136 | tf_op jit(solution)/shard_map/ppermute | solution.py:27
  20.5 1.6 %collective-permute-start.2 = (bf16[592,256]{1,0:T(8,128)(2,1)}, bf16[592,256]{1,0:T(8,128)(2,1)S(1)}, u32[]{:S(2)}, u32[]{:S(2)}) collective-permute-start(bf16[592,256]{1,0:T(8,128)(2,1)} %collective-permute-done), channel_id=1, source_target_pairs={{0,1},{1,0},{2,3},{3,2},{4,5},{5,4},{6,7},{7,6},{8,9},{9,8},{10,11... | collective-permute-start | bytes 909320 | tf_op jit(solution)/shard_map/ppermute | solution.py:382
  22.2 2.4 %shard_map.79 = (f32[576,256]{1,0:T(8,128)S(1)}, f32[8,128]{1,0:T(8,128)}) custom-call(s32[3,19]{1,0:T(4,128)S(1)} %get-tuple-element.33.refs_0_.slots_ref, s32[2,6]{1,0:T(2,128)S(1)} %maximum_convert_fusion.refs_1_, s32[2]{0:T(128)S(1)} %pad_add_fusion.refs_2_.refs_1_, bf16[3,12,192,192]{3,2,1,0:T(8,128)(2,1)S(1)} %shard_map.77.hessian_ref.refs_3_.refs_2_, ...), custom_call_target="tpu_custom_call" | custom-call | flops 30000001024 | bytes 276480 | tf_op jit(solution)/shard_map/pallas_call | solution.py:465
  25.8 1.3 %collective-permute-start.4 = (bf16[576,256]{1,0:T(8,128)(2,1)S(1)}, bf16[576,256]{1,0:T(8,128)(2,1)S(1)}, u32[]{:S(2)}, u32[]{:S(2)}) collective-permute-start(bf16[576,256]{1,0:T(8,128)(2,1)S(1)} %get-tuple-element.36), channel_id=1, source_target_pairs={{0,2},{2,4},{4,6},{6,8},{8,10},{10,12},{12,14},{14,16},{16,18},{18... | collective-permute-start | bytes 884744 | tf_op jit(solution)/shard_map/ppermute | solution.py:27
  27.1 3.8 %collective-permute-start.6 = (bf16[576,256]{1,0:T(8,128)(2,1)S(1)}, bf16[576,256]{1,0:T(8,128)(2,1)S(1)}, u32[]{:S(2)}, u32[]{:S(2)}) collective-permute-start(bf16[576,256]{1,0:T(8,128)(2,1)S(1)} %get-tuple-element.36), channel_id=1, source_target_pairs={{0,30},{2,0},{4,2},{6,4},{8,6},{10,8},{12,10},{14,12},{16,14},{18,... | collective-permute-start | bytes 884744 | tf_op jit(solution)/shard_map/ppermute | solution.py:27
  31.0 2.8 %all-gather.1 = bf16[1152,256]{1,0:T(8,128)(2,1)S(1)} all-gather(bf16[576,256]{1,0:T(8,128)(2,1)S(1)} %get-tuple-element.36), channel_id=3, replica_groups=mesh['region'=16,'split'=2] {'split'}, dimensions={0}, use_global_device_ids=true | all-gather | bytes 884736 | tf_op jit(solution)/shard_map/all_gather | solution.py:409
  35.0 4.4 %collective-permute-done.4 = bf16[576,256]{1,0:T(8,128)(2,1)S(1)} collective-permute-done((bf16[576,256]{1,0:T(8,128)(2,1)S(1)}, bf16[576,256]{1,0:T(8,128)(2,1)S(1)}, u32[]{:S(2)}, u32[]{:S(2)}) %collective-permute-start.4) | collective-permute-done | bytes 294944 | tf_op jit(solution)/shard_map/ppermute | solution.py:27
  39.4 1.3 %collective-permute-start.5 = (bf16[576,256]{1,0:T(8,128)(2,1)S(1)}, bf16[576,256]{1,0:T(8,128)(2,1)S(1)}, u32[]{:S(2)}, u32[]{:S(2)}) collective-permute-start(bf16[576,256]{1,0:T(8,128)(2,1)S(1)} %collective-permute-done.4), channel_id=1, source_target_pairs={{0,1},{1,0},{2,3},{3,2},{4,5},{5,4},{6,7},{7,6},{8,9},{9,8},{10,11... | collective-permute-start | bytes 884744 | tf_op jit(solution)/shard_map/ppermute | solution.py:382
  41.6 1.3 %collective-permute-start.7 = (bf16[576,256]{1,0:T(8,128)(2,1)S(1)}, bf16[576,256]{1,0:T(8,128)(2,1)S(1)}, u32[]{:S(2)}, u32[]{:S(2)}) collective-permute-start(bf16[576,256]{1,0:T(8,128)(2,1)S(1)} %collective-permute-done.6), channel_id=1, source_target_pairs={{0,1},{1,0},{2,3},{3,2},{4,5},{5,4},{6,7},{7,6},{8,9},{9,8},{10,11... | collective-permute-start | bytes 884744 | tf_op jit(solution)/shard_map/ppermute | solution.py:382
  42.9 1.9 %shard_map.82 = (f32[576,256]{1,0:T(8,128)S(1)}, f32[8,128]{1,0:T(8,128)}) custom-call(s32[3,19]{1,0:T(4,128)S(1)} %get-tuple-element.33.refs_0_.slots_ref, s32[2,6]{1,0:T(2,128)S(1)} %maximum_convert_fusion.refs_1_, s32[2]{0:T(128)S(1)} %pad_add_fusion.refs_2_.refs_1_, bf16[3,12,192,192]{3,2,1,0:T(8,128)(2,1)S(1)} %shard_map.77.hessian_ref.refs_3_.refs_2_, ...), custom_call_target="tpu_custom_call" | custom-call | flops 30000001024 | bytes 276480 | tf_op jit(solution)/shard_map/pallas_call | solution.py:465
  44.8 1.9 %shard_map.83 = (f32[576,256]{1,0:T(8,128)S(1)}, bf16[576,256]{1,0:T(8,128)(2,1)}) custom-call(s32[3,19]{1,0:T(4,128)S(1)} %get-tuple-element.33.refs_0_.slots_ref, s32[2,6]{1,0:T(2,128)S(1)} %maximum_convert_fusion.refs_1_, s32[2]{0:T(128)S(1)} %pad_add_fusion.refs_2_.refs_1_, bf16[3,12,192,192]{3,2,1,0:T(8,128)(2,1)S(1)} %shard_map.77.hessian_ref.refs_3_.refs_2_, ...), custom_call_target="tpu_custom_call" | custom-call | flops 30000001024 | bytes 276480 | tf_op jit(solution)/shard_map/pallas_call | solution.py:455
  48.1 4.6 %collective-permute-start.12 = (bf16[576,256]{1,0:T(8,128)(2,1)}, bf16[576,256]{1,0:T(8,128)(2,1)}, u32[]{:S(2)}, u32[]{:S(2)}) collective-permute-start(bf16[576,256]{1,0:T(8,128)(2,1)} %get-tuple-element.39), channel_id=1, source_target_pairs={{0,30},{2,0},{4,2},{6,4},{8,6},{10,8},{12,10},{14,12},{16,14},{18,... | collective-permute-start | bytes 884744 | tf_op jit(solution)/shard_map/ppermute | solution.py:27
  53.7 2.5 %shard_map.84 = (f32[576,256]{1,0:T(8,128)S(1)}, f32[384,128]{1,0:T(8,128)S(1)}) custom-call(s32[3,19]{1,0:T(4,128)S(1)} %get-tuple-element.33.refs_0_.slots_ref, s32[2]{0:T(128)S(1)} %pad_add_fusion.refs_2_.refs_1_, bf16[3,12,192,192]{3,2,1,0:T(8,128)(2,1)S(1)} %shard_map.77.hessian_ref.refs_3_.refs_2_, bf16[1,576,256]{2,1,0:T(8,128)(2,1)} %bitcast.13.refs_3_, ...), custom_call_target="tpu_custom_call" | custom-call | flops 10000000 | bytes 276480 | tf_op jit(solution)/shard_map/pallas_call | solution.py:450
  59.4 1.8 %collective-permute-done.11 = bf16[576,256]{1,0:T(8,128)(2,1)} collective-permute-done((bf16[576,256]{1,0:T(8,128)(2,1)}, bf16[576,256]{1,0:T(8,128)(2,1)}, u32[]{:S(2)}, u32[]{:S(2)}) %collective-permute-start.11) | collective-permute-done | bytes 294944 | tf_op jit(solution)/shard_map/ppermute | solution.py:27
  63.0 1.4 %collective-permute-start.14 = (bf16[576,256]{1,0:T(8,128)(2,1)}, bf16[576,256]{1,0:T(8,128)(2,1)S(1)}, u32[]{:S(2)}, u32[]{:S(2)}) collective-permute-start(bf16[576,256]{1,0:T(8,128)(2,1)} %collective-permute-done.12), channel_id=1, source_target_pairs={{0,1},{1,0},{2,3},{3,2},{4,5},{5,4},{6,7},{7,6},{8,9},{9,8},{10,11... | collective-permute-start | bytes 884744 | tf_op jit(solution)/shard_map/ppermute | solution.py:382
  67.6 1.9 %shard_map.85 = (f32[576,256]{1,0:T(8,128)S(1)}, f32[8,128]{1,0:T(8,128)S(1)}) custom-call(s32[3,19]{1,0:T(4,128)S(1)} %get-tuple-element.33.refs_0_.slots_ref, s32[2,6]{1,0:T(2,128)S(1)} %maximum_convert_fusion.refs_1_, s32[2]{0:T(128)S(1)} %pad_add_fusion.refs_2_.refs_1_, bf16[3,12,192,192]{3,2,1,0:T(8,128)(2,1)S(1)} %shard_map.77.hessian_ref.refs_3_.refs_2_, ...), custom_call_target="tpu_custom_call" | custom-call | flops 30000001024 | bytes 276480 | tf_op jit(solution)/shard_map/pallas_call | solution.py:465
  69.6 2.8 %shard_map.86 = f32[256,256]{1,0:T(8,128)S(1)} custom-call(s32[3,19]{1,0:T(4,128)S(1)} %get-tuple-element.33.refs_0_.slots_ref, s32[2,6]{1,0:T(2,128)S(1)} %maximum_convert_fusion.refs_1_, s32[2]{0:T(128)S(1)} %pad_add_fusion.refs_2_.refs_1_, bf16[3,12,192,192]{3,2,1,0:T(8,128)(2,1)S(1)} %shard_map.77.hessian_ref.refs_3_.refs_2_, ...), custom_call_target="tpu_custom_call" | custom-call | flops 30000001024 | bytes 276480 | tf_op jit(solution)/shard_map/pallas_call | solution.py:455
  74.0 4.4 %collective-permute-done.16 = f32[112,256]{1,0:T(8,128)S(1)} collective-permute-done((f32[112,256]{1,0:T(8,128)S(1)}, f32[112,256]{1,0:T(8,128)S(1)}, u32[]{:S(2)}, u32[]{:S(2)}) %collective-permute-start.16) | collective-permute-done | bytes 114720 | tf_op jit(solution)/shard_map/ppermute | solution.py:318
  79.6 2.5 %collective-permute-done.17 = f32[112,256]{1,0:T(8,128)S(1)} collective-permute-done((f32[112,256]{1,0:T(8,128)S(1)}, f32[112,256]{1,0:T(8,128)S(1)}, u32[]{:S(2)}, u32[]{:S(2)}) %collective-permute-start.17) | collective-permute-done | bytes 114720 | tf_op jit(solution)/shard_map/ppermute | solution.py:318
  82.2 2.2 %collective-permute-start.18 = (f32[112,256]{1,0:T(8,128)S(1)}, f32[112,256]{1,0:T(8,128)S(1)}, u32[]{:S(2)}, u32[]{:S(2)}) collective-permute-start(f32[112,256]{1,0:T(8,128)S(1)} %add.52), channel_id=1, source_target_pairs={{0,16},{2,18},{4,20},{6,22},{8,24},{10,26},{12,28},{14,30},{16,0},... | collective-permute-start | bytes 344072 | tf_op jit(solution)/shard_map/ppermute | solution.py:318
  84.4 3.6 %collective-permute-done.18 = f32[112,256]{1,0:T(8,128)S(1)} collective-permute-done((f32[112,256]{1,0:T(8,128)S(1)}, f32[112,256]{1,0:T(8,128)S(1)}, u32[]{:S(2)}, u32[]{:S(2)}) %collective-permute-start.18) | collective-permute-done | bytes 114720 | tf_op jit(solution)/shard_map/ppermute | solution.py:318
  88.8 3.0 %collective-permute-done.19 = f32[112,256]{1,0:T(8,128)S(1)} collective-permute-done((f32[112,256]{1,0:T(8,128)S(1)}, f32[112,256]{1,0:T(8,128)S(1)}, u32[]{:S(2)}, u32[]{:S(2)}) %collective-permute-start.19) | collective-permute-done | bytes 114720 | tf_op jit(solution)/shard_map/ppermute | solution.py:318
  91.8 4.6 %collective-permute-start.20 = (f32[192,128]{1,0:T(8,128)S(1)}, f32[192,128]{1,0:T(8,128)S(1)}, u32[]{:S(2)}, u32[]{:S(2)}) collective-permute-start(f32[192,128]{1,0:T(8,128)S(1)} %pad_maximum_fusion.3), channel_id=1, source_target_pairs={{0,1},{1,0},{2,3},{3,2},{4,5},{5,4},{6,7},{7,6},{8,9},{9,8},{10,11... | collective-permute-start | bytes 294920 | tf_op jit(solution)/shard_map/ppermute | solution.py:318
  97.4 4.8 %shard_map.87 = (f32[128,128]{1,0:T(8,128)S(1)}, f32[128,128]{1,0:T(8,128)S(1)}, f32[128,128]{1,0:T(8,128)S(1)}) custom-call(s32[1]{0:T(128)} %bitcast.15.refs_5_.number_ref, f32[384,128]{1,0:T(8,128)S(1)} %constant_dynamic-update-slice_fusion.gram_ref), custom_call_target="tpu_custom_call" | custom-call | flops 100000000 | bytes 3072 | tf_op jit(solution)/shard_map/pallas_call | solution.py:295
  102.2 4.2 %shard_map.88 = (f32[128,128]{1,0:T(8,128)S(1)}, f32[128,128]{1,0:T(8,128)S(1)}, f32[128,128]{1,0:T(8,128)S(1)}) custom-call(f32[128,128]{1,0:T(8,128)S(1)} %get-tuple-element.49.refs_0_, f32[128,128]{1,0:T(8,128)S(1)} %get-tuple-element.50.refs_1_, f32[128,128]{1,0:T(8,128)S(1)} %get-tuple-element.51.refs_2_), custom_call_target="tpu_custom_call" | custom-call | flops 100000000 | bytes 1024 | tf_op jit(solution)/shard_map/pallas_call | solution.py:301
  107.1 1.9 %shard_map.89 = (f32[576,256]{1,0:T(8,128)}, f32[256,256]{1,0:T(8,128)S(1)}) custom-call(f32[128,128]{1,0:T(8,128)S(1)} %get-tuple-element.56.refs_0_, f32[128,128]{1,0:T(8,128)S(1)} %get-tuple-element.57.refs_1_, f32[128,128]{1,0:T(8,128)S(1)} %get-tuple-element.58.refs_2_, f32[576,256]{1,0:T(8,128)S(1)} %copy-done.5), custom_call_target="tpu_custom_call" | custom-call | flops 100000000 | bytes 9216 | tf_op jit(solution)/shard_map/pallas_call | solution.py:308
  109.0 1.7 %shard_map.90 = f32[256,256]{1,0:T(8,128)} custom-call(s32[1]{0:T(128)} %bitcast.20.refs_7_.number_ref, f32[256,256]{1,0:T(8,128)S(1)} %pad_maximum_fusion.cross_ref, f32[256,256]{1,0:T(8,128)S(1)} %get-tuple-element.63.inverse_ref), custom_call_target="tpu_custom_call" | custom-call | flops 150994944 | bytes 276480 | tf_op jit(solution)/shard_map/pallas_call | solution.py:508
  (83 shorter events, 25.2 us)
Async XLA Ops:
  3.2 14.7 %collective-permute-start = (bf16[592,256]{1,0:T(8,128)(2,1)}, bf16[592,256]{1,0:T(8,128)(2,1)}, u32[]{:S(2)}, u32[]{:S(2)}) collective-permute-start(bf16[592,256]{1,0:T(8,128)(2,1)} %fusion.1), channel_id=1, source_target_pairs={{0,2},{2,4},{4,6},{6,8},{8,10},{10,12},{12,14},{14,16},{16,18},{18... | collective-permute-start | bytes 909320 | tf_op jit(solution)/shard_map/ppermute | solution.py:27
  5.2 14.6 %collective-permute-start.1 = (bf16[592,256]{1,0:T(8,128)(2,1)}, bf16[592,256]{1,0:T(8,128)(2,1)}, u32[]{:S(2)}, u32[]{:S(2)}) collective-permute-start(bf16[592,256]{1,0:T(8,128)(2,1)} %fusion.1), channel_id=1, source_target_pairs={{0,30},{2,0},{4,2},{6,4},{8,6},{10,8},{12,10},{14,12},{16,14},{18,... | collective-permute-start | bytes 909320 | tf_op jit(solution)/shard_map/ppermute | solution.py:27
  9.2 2.0 %copy-start.2 = (bf16[3,12,192,192]{3,2,1,0:T(8,128)(2,1)S(1)}, bf16[3,12,192,192]{3,2,1,0:T(8,128)(2,1)}, u32[]{:S(2)}) copy-start(bf16[3,12,192,192]{3,2,1,0:T(8,128)(2,1)} %blocks_ref.1) | copy-start | bytes 7962628
  11.2 3.5 %copy-start.7 = (s32[3,12]{1,0:T(4,128)S(1)}, s32[3,12]{1,0:T(4,128)}, u32[]{:S(2)}) copy-start(s32[3,12]{1,0:T(4,128)} %cols_ref.1) | copy-start | bytes 436
  11.2 3.5 %copy-start.8 = (f32[2]{0:T(128)S(1)}, f32[2]{0:T(128)}, u32[]{:S(2)}) copy-start(f32[2]{0:T(128)} %refs_7_.3) | copy-start | bytes 28
  11.2 3.5 %copy-start.9 = (s32[3]{0:T(128)S(1)}, s32[3]{0:T(128)}, u32[]{:S(2)}) copy-start(s32[3]{0:T(128)} %live_ref.1) | copy-start | bytes 40
  14.7 1.1 copy-start
  20.5 4.1 %collective-permute-start.2 = (bf16[592,256]{1,0:T(8,128)(2,1)}, bf16[592,256]{1,0:T(8,128)(2,1)S(1)}, u32[]{:S(2)}, u32[]{:S(2)}) collective-permute-start(bf16[592,256]{1,0:T(8,128)(2,1)} %collective-permute-done), channel_id=1, source_target_pairs={{0,1},{1,0},{2,3},{3,2},{4,5},{5,4},{6,7},{7,6},{8,9},{9,8},{10,11... | collective-permute-start | bytes 909320 | tf_op jit(solution)/shard_map/ppermute | solution.py:382
  22.1 2.5 %collective-permute-start.3 = (bf16[592,256]{1,0:T(8,128)(2,1)}, bf16[592,256]{1,0:T(8,128)(2,1)S(1)}, u32[]{:S(2)}, u32[]{:S(2)}) collective-permute-start(bf16[592,256]{1,0:T(8,128)(2,1)} %collective-permute-done.1), channel_id=1, source_target_pairs={{0,1},{1,0},{2,3},{3,2},{4,5},{5,4},{6,7},{7,6},{8,9},{9,8},{10,11... | collective-permute-start | bytes 909320 | tf_op jit(solution)/shard_map/ppermute | solution.py:382
  24.6 9.2 %copy-start.1 = (f32[576,256]{1,0:T(8,128)S(1)}, f32[576,256]{1,0:T(8,128)}, u32[]{:S(2)}) copy-start(f32[576,256]{1,0:T(8,128)} %refs_3_.1) | copy-start | bytes 1769476
  25.8 13.5 %collective-permute-start.4 = (bf16[576,256]{1,0:T(8,128)(2,1)S(1)}, bf16[576,256]{1,0:T(8,128)(2,1)S(1)}, u32[]{:S(2)}, u32[]{:S(2)}) collective-permute-start(bf16[576,256]{1,0:T(8,128)(2,1)S(1)} %get-tuple-element.36), channel_id=1, source_target_pairs={{0,2},{2,4},{4,6},{6,8},{8,10},{10,12},{12,14},{14,16},{16,18},{18... | collective-permute-start | bytes 884744 | tf_op jit(solution)/shard_map/ppermute | solution.py:27
  27.1 14.5 %collective-permute-start.6 = (bf16[576,256]{1,0:T(8,128)(2,1)S(1)}, bf16[576,256]{1,0:T(8,128)(2,1)S(1)}, u32[]{:S(2)}, u32[]{:S(2)}) collective-permute-start(bf16[576,256]{1,0:T(8,128)(2,1)S(1)} %get-tuple-element.36), channel_id=1, source_target_pairs={{0,30},{2,0},{4,2},{6,4},{8,6},{10,8},{12,10},{14,12},{16,14},{18,... | collective-permute-start | bytes 884744 | tf_op jit(solution)/shard_map/ppermute | solution.py:27
  39.4 5.4 %collective-permute-start.5 = (bf16[576,256]{1,0:T(8,128)(2,1)S(1)}, bf16[576,256]{1,0:T(8,128)(2,1)S(1)}, u32[]{:S(2)}, u32[]{:S(2)}) collective-permute-start(bf16[576,256]{1,0:T(8,128)(2,1)S(1)} %collective-permute-done.4), channel_id=1, source_target_pairs={{0,1},{1,0},{2,3},{3,2},{4,5},{5,4},{6,7},{7,6},{8,9},{9,8},{10,11... | collective-permute-start | bytes 884744 | tf_op jit(solution)/shard_map/ppermute | solution.py:382
  41.6 3.2 %collective-permute-start.7 = (bf16[576,256]{1,0:T(8,128)(2,1)S(1)}, bf16[576,256]{1,0:T(8,128)(2,1)S(1)}, u32[]{:S(2)}, u32[]{:S(2)}) collective-permute-start(bf16[576,256]{1,0:T(8,128)(2,1)S(1)} %collective-permute-done.6), channel_id=1, source_target_pairs={{0,1},{1,0},{2,3},{3,2},{4,5},{5,4},{6,7},{7,6},{8,9},{9,8},{10,11... | collective-permute-start | bytes 884744 | tf_op jit(solution)/shard_map/ppermute | solution.py:382
  47.6 5.1 %collective-permute-start.8 = (bf16[576,256]{1,0:T(8,128)(2,1)}, bf16[576,256]{1,0:T(8,128)(2,1)}, u32[]{:S(2)}, u32[]{:S(2)}) collective-permute-start(bf16[576,256]{1,0:T(8,128)(2,1)} %get-tuple-element.39), channel_id=1, source_target_pairs={{0,1},{1,0},{2,3},{3,2},{4,5},{5,4},{6,7},{7,6},{8,9},{9,8},{10,11... | collective-permute-start | bytes 884744 | tf_op jit(solution)/shard_map/ppermute | solution.py:382
  47.6 13.6 %collective-permute-start.11 = (bf16[576,256]{1,0:T(8,128)(2,1)}, bf16[576,256]{1,0:T(8,128)(2,1)}, u32[]{:S(2)}, u32[]{:S(2)}) collective-permute-start(bf16[576,256]{1,0:T(8,128)(2,1)} %get-tuple-element.39), channel_id=1, source_target_pairs={{0,2},{2,4},{4,6},{6,8},{8,10},{10,12},{12,14},{14,16},{16,18},{18... | collective-permute-start | bytes 884744 | tf_op jit(solution)/shard_map/ppermute | solution.py:27
  48.1 14.9 %collective-permute-start.12 = (bf16[576,256]{1,0:T(8,128)(2,1)}, bf16[576,256]{1,0:T(8,128)(2,1)}, u32[]{:S(2)}, u32[]{:S(2)}) collective-permute-start(bf16[576,256]{1,0:T(8,128)(2,1)} %get-tuple-element.39), channel_id=1, source_target_pairs={{0,30},{2,0},{4,2},{6,4},{8,6},{10,8},{12,10},{14,12},{16,14},{18,... | collective-permute-start | bytes 884744 | tf_op jit(solution)/shard_map/ppermute | solution.py:27
  52.7 1.1 copy-start.4
  58.3 6.0 %collective-permute-start.9 = (f32[192,128]{1,0:T(8,128)}, f32[192,128]{1,0:T(8,128)}, u32[]{:S(2)}, u32[]{:S(2)}) collective-permute-start(f32[192,128]{1,0:T(8,128)} %slice.63), channel_id=1, source_target_pairs={{0,1},{1,0},{2,3},{3,2},{4,5},{5,4},{6,7},{7,6},{8,9},{9,8},{10,11... | collective-permute-start | bytes 294920 | tf_op jit(solution)/shard_map/ppermute | solution.py:318
  61.2 8.4 %collective-permute-start.13 = (bf16[576,256]{1,0:T(8,128)(2,1)}, bf16[576,256]{1,0:T(8,128)(2,1)S(1)}, u32[]{:S(2)}, u32[]{:S(2)}) collective-permute-start(bf16[576,256]{1,0:T(8,128)(2,1)} %collective-permute-done.11), channel_id=1, source_target_pairs={{0,1},{1,0},{2,3},{3,2},{4,5},{5,4},{6,7},{7,6},{8,9},{9,8},{10,11... | collective-permute-start | bytes 884744 | tf_op jit(solution)/shard_map/ppermute | solution.py:382
  63.0 6.6 %collective-permute-start.14 = (bf16[576,256]{1,0:T(8,128)(2,1)}, bf16[576,256]{1,0:T(8,128)(2,1)S(1)}, u32[]{:S(2)}, u32[]{:S(2)}) collective-permute-start(bf16[576,256]{1,0:T(8,128)(2,1)} %collective-permute-done.12), channel_id=1, source_target_pairs={{0,1},{1,0},{2,3},{3,2},{4,5},{5,4},{6,7},{7,6},{8,9},{9,8},{10,11... | collective-permute-start | bytes 884744 | tf_op jit(solution)/shard_map/ppermute | solution.py:382
  65.3 4.2 %collective-permute-start.10 = (f32[96,128]{1,0:T(8,128)S(1)}, f32[96,128]{1,0:T(8,128)S(1)}, u32[]{:S(2)}, u32[]{:S(2)}) collective-permute-start(f32[96,128]{1,0:T(8,128)S(1)} %slice.81), channel_id=1, source_target_pairs={{0,4},{2,6},{4,0},{6,2},{8,12},{10,14},{12,8},{14,10},{16,20},{18,... | collective-permute-start | bytes 147464 | tf_op jit(solution)/shard_map/ppermute | solution.py:318
  66.5 1.1 copy-start.11
  67.6 2.0 %copy-start.5 = (f32[576,256]{1,0:T(8,128)S(1)}, f32[576,256]{1,0:T(8,128)}, u32[]{:S(2)}) copy-start(f32[576,256]{1,0:T(8,128)} %copy-done.3) | copy-start | bytes 1769476
  72.4 1.4 %collective-permute-start.15 = (f32[128,256]{1,0:T(8,128)S(1)}, f32[128,256]{1,0:T(8,128)S(1)}, u32[]{:S(2)}, u32[]{:S(2)}) collective-permute-start(f32[128,256]{1,0:T(8,128)S(1)} %slice.83), channel_id=1, source_target_pairs={{0,1},{1,0},{2,3},{3,2},{4,5},{5,4},{6,7},{7,6},{8,9},{9,8},{10,11... | collective-permute-start | bytes 393224 | tf_op jit(solution)/shard_map/ppermute | solution.py:318
  73.9 4.5 %collective-permute-start.16 = (f32[112,256]{1,0:T(8,128)S(1)}, f32[112,256]{1,0:T(8,128)S(1)}, u32[]{:S(2)}, u32[]{:S(2)}) collective-permute-start(f32[112,256]{1,0:T(8,128)S(1)} %fusion.2), channel_id=1, source_target_pairs={{0,2},{2,0},{4,6},{6,4},{8,10},{10,8},{12,14},{14,12},{16,18},{18,... | collective-permute-start | bytes 344072 | tf_op jit(solution)/shard_map/ppermute | solution.py:318
  78.4 3.7 %collective-permute-start.17 = (f32[112,256]{1,0:T(8,128)S(1)}, f32[112,256]{1,0:T(8,128)S(1)}, u32[]{:S(2)}, u32[]{:S(2)}) collective-permute-start(f32[112,256]{1,0:T(8,128)S(1)} %maximum_add_fusion), channel_id=1, source_target_pairs={{0,8},{2,10},{4,12},{6,14},{8,0},{10,2},{12,4},{14,6},{16,24},{18,... | collective-permute-start | bytes 344072 | tf_op jit(solution)/shard_map/ppermute | solution.py:318
  82.2 5.8 %collective-permute-start.18 = (f32[112,256]{1,0:T(8,128)S(1)}, f32[112,256]{1,0:T(8,128)S(1)}, u32[]{:S(2)}, u32[]{:S(2)}) collective-permute-start(f32[112,256]{1,0:T(8,128)S(1)} %add.52), channel_id=1, source_target_pairs={{0,16},{2,18},{4,20},{6,22},{8,24},{10,26},{12,28},{14,30},{16,0},... | collective-permute-start | bytes 344072 | tf_op jit(solution)/shard_map/ppermute | solution.py:318
  88.0 3.7 %collective-permute-start.19 = (f32[112,256]{1,0:T(8,128)S(1)}, f32[112,256]{1,0:T(8,128)S(1)}, u32[]{:S(2)}, u32[]{:S(2)}) collective-permute-start(f32[112,256]{1,0:T(8,128)S(1)} %add.53), channel_id=1, source_target_pairs={{0,4},{2,6},{4,0},{6,2},{8,12},{10,14},{12,8},{14,10},{16,20},{18,... | collective-permute-start | bytes 344072 | tf_op jit(solution)/shard_map/ppermute | solution.py:318
  91.8 5.6 %collective-permute-start.20 = (f32[192,128]{1,0:T(8,128)S(1)}, f32[192,128]{1,0:T(8,128)S(1)}, u32[]{:S(2)}, u32[]{:S(2)}) collective-permute-start(f32[192,128]{1,0:T(8,128)S(1)} %pad_maximum_fusion.3), channel_id=1, source_target_pairs={{0,1},{1,0},{2,3},{3,2},{4,5},{5,4},{6,7},{7,6},{8,9},{9,8},{10,11... | collective-permute-start | bytes 294920 | tf_op jit(solution)/shard_map/ppermute | solution.py:318
  97.3 9.1 %collective-permute-start.21 = (f32[64,256]{1,0:T(8,128)S(1)}, f32[64,256]{1,0:T(8,128)S(1)}, u32[]{:S(2)}, u32[]{:S(2)}) collective-permute-start(f32[64,256]{1,0:T(8,128)S(1)} %slice_add_fusion.2), channel_id=1, source_target_pairs={{0,2},{2,0},{4,6},{6,4},{8,10},{10,8},{12,14},{14,12},{16,18},{18,... | collective-permute-start | bytes 196616 | tf_op jit(solution)/shard_map/ppermute | solution.py:318
  106.4 2.6 %collective-permute-start.22 = (f32[128,256]{1,0:T(8,128)S(1)}, f32[128,256]{1,0:T(8,128)S(1)}, u32[]{:S(2)}, u32[]{:S(2)}) collective-permute-start(f32[128,256]{1,0:T(8,128)S(1)} %pad_maximum_fusion.1), channel_id=1, source_target_pairs={{0,1},{1,0},{2,3},{3,2},{4,5},{5,4},{6,7},{7,6},{8,9},{9,8},{10,11... | collective-permute-start | bytes 393224 | tf_op jit(solution)/shard_map/ppermute | solution.py:318
  (3 other events, 2.3 us)

commit v19 on v18

--- a/solution.py
+++ b/solution.py
@@ -123,12 +123,8 @@
 
 
 def middle_body(which, *refs):
-    operands, (total_ref, out_ref, token_ref, names_ref, held_ref, done_ref) = refs[:6], refs[6:]
-    copy = pltpu.make_async_copy(total_ref, held_ref, done_ref)
-    copy.start()
-    added = halo_sum(which, *operands, names_ref)
-    copy.wait()
-    total = held_ref[...] + added
+    operands, (total_ref, out_ref, token_ref, names_ref) = refs[:6], refs[6:]
+    total = total_ref[...] + halo_sum(which, *operands, names_ref)
     out_ref[...] = total
     token_ref[...] = total[:GROUP, :TILE]
 
@@ -458,10 +454,9 @@
         *pairs, last = zip(gathered(lower), gathered(upper))
         after = jnp.zeros(token.shape, token.dtype)
         for which, pair in enumerate(pairs):
-            specs = [SMEM] * 3 + [VMEM] * 3 + [pl.BlockSpec(memory_space=pl.ANY)]
-            scratch = names + [pltpu.VMEM((rows, modes), jnp.float32), pltpu.SemaphoreType.DMA(())]
+            specs = [SMEM] * 3 + [VMEM] * 4
             body_of = functools.partial(middle_body, which)
-            call = kernel_call(body_of, (wide, token), specs, covering, traffic, scratch)
+            call = kernel_call(body_of, (wide, token), specs, covering, traffic, names)
             total, after = call(table, lists, bases, held, *pair, total)
         return total, after, len(pairs), last
 

time: 111 us -> 111 us (level)
  transfers between devices with their start and end apart: 23 -> 23, of which waited for: 12 -> 12; matrix products, arithmetic and copies ran while one was open for 2% -> 2% of each run, Pallas kernels for 21% -> 20%
where the time goes in v19:
time: 111 us; the launch traced here: 110 us
  starting transfers between devices  35.1 us (32%)
  Pallas kernels  29.8 us (27%)
  waiting for transfers between devices  25.1 us (23%)
  local copies, waits for them, and re-layouts  9.56 us (9%)
  blocking collectives  5.87 us (5%)
  other arithmetic  3.69 us (3%)
    ppermute x6, starting transfers between devices, shifted(): return lax.ppermute(value, axis, pairs)  16.2 us
    ppermute x10, waiting for transfers between devices, partner_value(): lax.ppermute(value, axis, [(at, at ^ bit) for at in range(lax.axis_size(a...  15.3 us
    ppermute x10, starting transfers between devices, partner_value(): lax.ppermute(value, axis, [(at, at ^ bit) for at in range(lax.axis_size(a...  12.5 us
    ppermute x6, waiting for transfers between devices, shifted(): return lax.ppermute(value, axis, pairs)  9.74 us
    unnamed x26, local copies, waits for them, and re-layouts  7.51 us
    ppermute x7, starting transfers between devices, local(): swapped = lambda value: lax.ppermute(value, 'split', [(0, 1), (1, 0)])  6.39 us
    pallas_call x3, Pallas kernels, last_part(): return call(table, lists, bases, held, *pair, total, *scalars, *extra)  5.96 us
    all_gather x2, blocking collectives, exchange(): groups = [lax.all_gather(operand, 'split', axis=0)]  5.87 us
  transfers between devices with their start and end apart: 23, of which 12 were waited for; matrix products, arithmetic and copies ran while one was open for 2% of the time, Pallas kernels for 20%

profile of v19, /device:TPU:1, one launch (start us, length us, event | category | flops | bytes accessed | tf_op | source)
XLA Modules:
  0.0 110.0 jit_solution(17710136356629598946)
XLA Ops:
  3.2 2.0 %collective-permute-start = (bf16[592,256]{1,0:T(8,128)(2,1)}, bf16[592,256]{1,0:T(8,128)(2,1)}, u32[]{:S(2)}, u32[]{:S(2)}) collective-permute-start(bf16[592,256]{1,0:T(8,128)(2,1)} %fusion.1), channel_id=1, source_target_pairs={{0,2},{2,4},{4,6},{6,8},{8,10},{10,12},{12,14},{14,16},{16,18},{18... | collective-permute-start | bytes 909320 | tf_op jit(solution)/shard_map/ppermute | solution.py:27
  5.2 4.0 %collective-permute-start.1 = (bf16[592,256]{1,0:T(8,128)(2,1)}, bf16[592,256]{1,0:T(8,128)(2,1)}, u32[]{:S(2)}, u32[]{:S(2)}) collective-permute-start(bf16[592,256]{1,0:T(8,128)(2,1)} %fusion.1), channel_id=1, source_target_pairs={{0,30},{2,0},{4,2},{6,4},{8,6},{10,8},{12,10},{14,12},{16,14},{18,... | collective-permute-start | bytes 909320 | tf_op jit(solution)/shard_map/ppermute | solution.py:27
  9.2 2.0 %copy-done.2 = bf16[3,12,192,192]{3,2,1,0:T(8,128)(2,1)S(1)} copy-done((bf16[3,12,192,192]{3,2,1,0:T(8,128)(2,1)S(1)}, bf16[3,12,192,192]{3,2,1,0:T(8,128)(2,1)}, u32[]{:S(2)}) %copy-start.2) | copy-done | bytes 2654232
  11.6 3.0 %all-gather = bf16[1184,256]{1,0:T(8,128)(2,1)S(1)} all-gather(bf16[592,256]{1,0:T(8,128)(2,1)} %fusion.1), channel_id=2, replica_groups=mesh['region'=16,'split'=2] {'split'}, dimensions={0}, use_global_device_ids=true | all-gather | bytes 909312 | tf_op jit(solution)/shard_map/all_gather | solution.py:405
  15.7 1.7 %shard_map.78 = (f32[576,256]{1,0:T(8,128)S(1)}, s32[3,19]{1,0:T(4,128)S(1)}) custom-call(s32[3,12]{1,0:T(4,128)S(1)} %copy-done.7, s32[3]{0:T(128)S(1)} %copy-done.9, s32[2]{0:T(128)S(1)} %broadcast_1_bases_ref.2.bases_ref, bf16[3,12,192,192]{3,2,1,0:T(8,128)(2,1)S(1)} %shard_map.77.hessian_ref.refs_3_.refs_2_, bf16[2,592,256]{2,1,0:T(8,128)(2,1)S(1)} %bitcast.22, ...), custom_call_target="tpu_custom_call" | custom-call | flops 10000000 | bytes 276480 | tf_op jit(solution)/shard_map/pallas_call | solution.py:465
  18.5 1.3 %collective-permute-done.1 = bf16[592,256]{1,0:T(8,128)(2,1)} collective-permute-done((bf16[592,256]{1,0:T(8,128)(2,1)}, bf16[592,256]{1,0:T(8,128)(2,1)}, u32[]{:S(2)}, u32[]{:S(2)}) %collective-permute-start.1) | collective-permute-done | bytes 303136 | tf_op jit(solution)/shard_map/ppermute | solution.py:27
  20.5 1.6 %collective-permute-start.2 = (bf16[592,256]{1,0:T(8,128)(2,1)}, bf16[592,256]{1,0:T(8,128)(2,1)S(1)}, u32[]{:S(2)}, u32[]{:S(2)}) collective-permute-start(bf16[592,256]{1,0:T(8,128)(2,1)} %collective-permute-done), channel_id=1, source_target_pairs={{0,1},{1,0},{2,3},{3,2},{4,5},{5,4},{6,7},{7,6},{8,9},{9,8},{10,11... | collective-permute-start | bytes 909320 | tf_op jit(solution)/shard_map/ppermute | solution.py:378
  22.2 2.1 %shard_map.79 = (f32[576,256]{1,0:T(8,128)S(1)}, f32[8,128]{1,0:T(8,128)}) custom-call(s32[3,19]{1,0:T(4,128)S(1)} %get-tuple-element.33.refs_0_.slots_ref, s32[2,6]{1,0:T(2,128)S(1)} %maximum_convert_fusion.refs_1_, s32[2]{0:T(128)S(1)} %pad_add_fusion.refs_2_.refs_1_, bf16[3,12,192,192]{3,2,1,0:T(8,128)(2,1)S(1)} %shard_map.77.hessian_ref.refs_3_.refs_2_, ...), custom_call_target="tpu_custom_call" | custom-call | flops 30000001024 | bytes 276480 | tf_op jit(solution)/shard_map/pallas_call | solution.py:460
  25.6 1.3 %collective-permute-start.4 = (bf16[576,256]{1,0:T(8,128)(2,1)S(1)}, bf16[576,256]{1,0:T(8,128)(2,1)S(1)}, u32[]{:S(2)}, u32[]{:S(2)}) collective-permute-start(bf16[576,256]{1,0:T(8,128)(2,1)S(1)} %get-tuple-element.36), channel_id=1, source_target_pairs={{0,2},{2,4},{4,6},{6,8},{8,10},{10,12},{12,14},{14,16},{16,18},{18... | collective-permute-start | bytes 884744 | tf_op jit(solution)/shard_map/ppermute | solution.py:27
  26.8 3.9 %collective-permute-start.6 = (bf16[576,256]{1,0:T(8,128)(2,1)S(1)}, bf16[576,256]{1,0:T(8,128)(2,1)S(1)}, u32[]{:S(2)}, u32[]{:S(2)}) collective-permute-start(bf16[576,256]{1,0:T(8,128)(2,1)S(1)} %get-tuple-element.36), channel_id=1, source_target_pairs={{0,30},{2,0},{4,2},{6,4},{8,6},{10,8},{12,10},{14,12},{16,14},{18,... | collective-permute-start | bytes 884744 | tf_op jit(solution)/shard_map/ppermute | solution.py:27
  30.7 2.8 %all-gather.1 = bf16[1152,256]{1,0:T(8,128)(2,1)S(1)} all-gather(bf16[576,256]{1,0:T(8,128)(2,1)S(1)} %get-tuple-element.36), channel_id=3, replica_groups=mesh['region'=16,'split'=2] {'split'}, dimensions={0}, use_global_device_ids=true | all-gather | bytes 884736 | tf_op jit(solution)/shard_map/all_gather | solution.py:405
  34.7 4.4 %collective-permute-done.4 = bf16[576,256]{1,0:T(8,128)(2,1)S(1)} collective-permute-done((bf16[576,256]{1,0:T(8,128)(2,1)S(1)}, bf16[576,256]{1,0:T(8,128)(2,1)S(1)}, u32[]{:S(2)}, u32[]{:S(2)}) %collective-permute-start.4) | collective-permute-done | bytes 294944 | tf_op jit(solution)/shard_map/ppermute | solution.py:27
  39.1 1.3 %collective-permute-start.5 = (bf16[576,256]{1,0:T(8,128)(2,1)S(1)}, bf16[576,256]{1,0:T(8,128)(2,1)S(1)}, u32[]{:S(2)}, u32[]{:S(2)}) collective-permute-start(bf16[576,256]{1,0:T(8,128)(2,1)S(1)} %collective-permute-done.4), channel_id=1, source_target_pairs={{0,1},{1,0},{2,3},{3,2},{4,5},{5,4},{6,7},{7,6},{8,9},{9,8},{10,11... | collective-permute-start | bytes 884744 | tf_op jit(solution)/shard_map/ppermute | solution.py:378
  41.3 1.3 %collective-permute-start.7 = (bf16[576,256]{1,0:T(8,128)(2,1)S(1)}, bf16[576,256]{1,0:T(8,128)(2,1)S(1)}, u32[]{:S(2)}, u32[]{:S(2)}) collective-permute-start(bf16[576,256]{1,0:T(8,128)(2,1)S(1)} %collective-permute-done.6), channel_id=1, source_target_pairs={{0,1},{1,0},{2,3},{3,2},{4,5},{5,4},{6,7},{7,6},{8,9},{9,8},{10,11... | collective-permute-start | bytes 884744 | tf_op jit(solution)/shard_map/ppermute | solution.py:378
  42.6 1.6 %shard_map.82 = (f32[576,256]{1,0:T(8,128)S(1)}, f32[8,128]{1,0:T(8,128)}) custom-call(s32[3,19]{1,0:T(4,128)S(1)} %get-tuple-element.33.refs_0_.slots_ref, s32[2,6]{1,0:T(2,128)S(1)} %maximum_convert_fusion.refs_1_, s32[2]{0:T(128)S(1)} %pad_add_fusion.refs_2_.refs_1_, bf16[3,12,192,192]{3,2,1,0:T(8,128)(2,1)S(1)} %shard_map.77.hessian_ref.refs_3_.refs_2_, ...), custom_call_target="tpu_custom_call" | custom-call | flops 30000001024 | bytes 276480 | tf_op jit(solution)/shard_map/pallas_call | solution.py:460
  44.2 2.0 %shard_map.83 = (f32[576,256]{1,0:T(8,128)S(1)}, bf16[576,256]{1,0:T(8,128)(2,1)}) custom-call(s32[3,19]{1,0:T(4,128)S(1)} %get-tuple-element.33.refs_0_.slots_ref, s32[2,6]{1,0:T(2,128)S(1)} %maximum_convert_fusion.refs_1_, s32[2]{0:T(128)S(1)} %pad_add_fusion.refs_2_.refs_1_, bf16[3,12,192,192]{3,2,1,0:T(8,128)(2,1)S(1)} %shard_map.77.hessian_ref.refs_3_.refs_2_, ...), custom_call_target="tpu_custom_call" | custom-call | flops 30000001024 | bytes 276480 | tf_op jit(solution)/shard_map/pallas_call | solution.py:451
  47.5 4.6 %collective-permute-start.12 = (bf16[576,256]{1,0:T(8,128)(2,1)}, bf16[576,256]{1,0:T(8,128)(2,1)}, u32[]{:S(2)}, u32[]{:S(2)}) collective-permute-start(bf16[576,256]{1,0:T(8,128)(2,1)} %get-tuple-element.39), channel_id=1, source_target_pairs={{0,30},{2,0},{4,2},{6,4},{8,6},{10,8},{12,10},{14,12},{16,14},{18,... | collective-permute-start | bytes 884744 | tf_op jit(solution)/shard_map/ppermute | solution.py:27
  53.1 2.5 %shard_map.84 = (f32[576,256]{1,0:T(8,128)S(1)}, f32[384,128]{1,0:T(8,128)S(1)}) custom-call(s32[3,19]{1,0:T(4,128)S(1)} %get-tuple-element.33.refs_0_.slots_ref, s32[2]{0:T(128)S(1)} %pad_add_fusion.refs_2_.refs_1_, bf16[3,12,192,192]{3,2,1,0:T(8,128)(2,1)S(1)} %shard_map.77.hessian_ref.refs_3_.refs_2_, bf16[1,576,256]{2,1,0:T(8,128)(2,1)} %bitcast.13.refs_3_, ...), custom_call_target="tpu_custom_call" | custom-call | flops 10000000 | bytes 276480 | tf_op jit(solution)/shard_map/pallas_call | solution.py:446
  58.8 1.8 %collective-permute-done.11 = bf16[576,256]{1,0:T(8,128)(2,1)} collective-permute-done((bf16[576,256]{1,0:T(8,128)(2,1)}, bf16[576,256]{1,0:T(8,128)(2,1)}, u32[]{:S(2)}, u32[]{:S(2)}) %collective-permute-start.11) | collective-permute-done | bytes 294944 | tf_op jit(solution)/shard_map/ppermute | solution.py:27
  62.4 1.4 %collective-permute-start.14 = (bf16[576,256]{1,0:T(8,128)(2,1)}, bf16[576,256]{1,0:T(8,128)(2,1)S(1)}, u32[]{:S(2)}, u32[]{:S(2)}) collective-permute-start(bf16[576,256]{1,0:T(8,128)(2,1)} %collective-permute-done.12), channel_id=1, source_target_pairs={{0,1},{1,0},{2,3},{3,2},{4,5},{5,4},{6,7},{7,6},{8,9},{9,8},{10,11... | collective-permute-start | bytes 884744 | tf_op jit(solution)/shard_map/ppermute | solution.py:378
  67.0 1.7 %shard_map.85 = (f32[576,256]{1,0:T(8,128)S(1)}, f32[8,128]{1,0:T(8,128)S(1)}) custom-call(s32[3,19]{1,0:T(4,128)S(1)} %get-tuple-element.33.refs_0_.slots_ref, s32[2,6]{1,0:T(2,128)S(1)} %maximum_convert_fusion.refs_1_, s32[2]{0:T(128)S(1)} %pad_add_fusion.refs_2_.refs_1_, bf16[3,12,192,192]{3,2,1,0:T(8,128)(2,1)S(1)} %shard_map.77.hessian_ref.refs_3_.refs_2_, ...), custom_call_target="tpu_custom_call" | custom-call | flops 30000001024 | bytes 276480 | tf_op jit(solution)/shard_map/pallas_call | solution.py:460
  68.8 2.8 %shard_map.86 = f32[256,256]{1,0:T(8,128)S(1)} custom-call(s32[3,19]{1,0:T(4,128)S(1)} %get-tuple-element.33.refs_0_.slots_ref, s32[2,6]{1,0:T(2,128)S(1)} %maximum_convert_fusion.refs_1_, s32[2]{0:T(128)S(1)} %pad_add_fusion.refs_2_.refs_1_, bf16[3,12,192,192]{3,2,1,0:T(8,128)(2,1)S(1)} %shard_map.77.hessian_ref.refs_3_.refs_2_, ...), custom_call_target="tpu_custom_call" | custom-call | flops 30000001024 | bytes 276480 | tf_op jit(solution)/shard_map/pallas_call | solution.py:451
  73.2 4.4 %collective-permute-done.16 = f32[112,256]{1,0:T(8,128)S(1)} collective-permute-done((f32[112,256]{1,0:T(8,128)S(1)}, f32[112,256]{1,0:T(8,128)S(1)}, u32[]{:S(2)}, u32[]{:S(2)}) %collective-permute-start.16) | collective-permute-done | bytes 114720 | tf_op jit(solution)/shard_map/ppermute | solution.py:314
  78.8 2.5 %collective-permute-done.17 = f32[112,256]{1,0:T(8,128)S(1)} collective-permute-done((f32[112,256]{1,0:T(8,128)S(1)}, f32[112,256]{1,0:T(8,128)S(1)}, u32[]{:S(2)}, u32[]{:S(2)}) %collective-permute-start.17) | collective-permute-done | bytes 114720 | tf_op jit(solution)/shard_map/ppermute | solution.py:314
  81.4 2.2 %collective-permute-start.18 = (f32[112,256]{1,0:T(8,128)S(1)}, f32[112,256]{1,0:T(8,128)S(1)}, u32[]{:S(2)}, u32[]{:S(2)}) collective-permute-start(f32[112,256]{1,0:T(8,128)S(1)} %add.52), channel_id=1, source_target_pairs={{0,16},{2,18},{4,20},{6,22},{8,24},{10,26},{12,28},{14,30},{16,0},... | collective-permute-start | bytes 344072 | tf_op jit(solution)/shard_map/ppermute | solution.py:314
  83.6 3.6 %collective-permute-done.18 = f32[112,256]{1,0:T(8,128)S(1)} collective-permute-done((f32[112,256]{1,0:T(8,128)S(1)}, f32[112,256]{1,0:T(8,128)S(1)}, u32[]{:S(2)}, u32[]{:S(2)}) %collective-permute-start.18) | collective-permute-done | bytes 114720 | tf_op jit(solution)/shard_map/ppermute | solution.py:314
  88.2 2.8 %collective-permute-done.19 = f32[112,256]{1,0:T(8,128)S(1)} collective-permute-done((f32[112,256]{1,0:T(8,128)S(1)}, f32[112,256]{1,0:T(8,128)S(1)}, u32[]{:S(2)}, u32[]{:S(2)}) %collective-permute-start.19) | collective-permute-done | bytes 114720 | tf_op jit(solution)/shard_map/ppermute | solution.py:314
  91.0 4.6 %collective-permute-start.20 = (f32[192,128]{1,0:T(8,128)S(1)}, f32[192,128]{1,0:T(8,128)S(1)}, u32[]{:S(2)}, u32[]{:S(2)}) collective-permute-start(f32[192,128]{1,0:T(8,128)S(1)} %pad_maximum_fusion.3), channel_id=1, source_target_pairs={{0,1},{1,0},{2,3},{3,2},{4,5},{5,4},{6,7},{7,6},{8,9},{9,8},{10,11... | collective-permute-start | bytes 294920 | tf_op jit(solution)/shard_map/ppermute | solution.py:314
  96.7 4.8 %shard_map.87 = (f32[128,128]{1,0:T(8,128)S(1)}, f32[128,128]{1,0:T(8,128)S(1)}, f32[128,128]{1,0:T(8,128)S(1)}) custom-call(s32[1]{0:T(128)} %bitcast.15.refs_5_.number_ref, f32[384,128]{1,0:T(8,128)S(1)} %constant_dynamic-update-slice_fusion.gram_ref), custom_call_target="tpu_custom_call" | custom-call | flops 100000000 | bytes 3072 | tf_op jit(solution)/shard_map/pallas_call | solution.py:291
  101.5 4.2 %shard_map.88 = (f32[128,128]{1,0:T(8,128)S(1)}, f32[128,128]{1,0:T(8,128)S(1)}, f32[128,128]{1,0:T(8,128)S(1)}) custom-call(f32[128,128]{1,0:T(8,128)S(1)} %get-tuple-element.49.refs_0_, f32[128,128]{1,0:T(8,128)S(1)} %get-tuple-element.50.refs_1_, f32[128,128]{1,0:T(8,128)S(1)} %get-tuple-element.51.refs_2_), custom_call_target="tpu_custom_call" | custom-call | flops 100000000 | bytes 1024 | tf_op jit(solution)/shard_map/pallas_call | solution.py:297
  106.4 1.9 %shard_map.89 = (f32[576,256]{1,0:T(8,128)}, f32[256,256]{1,0:T(8,128)S(1)}) custom-call(f32[128,128]{1,0:T(8,128)S(1)} %get-tuple-element.56.refs_0_, f32[128,128]{1,0:T(8,128)S(1)} %get-tuple-element.57.refs_1_, f32[128,128]{1,0:T(8,128)S(1)} %get-tuple-element.58.refs_2_, f32[576,256]{1,0:T(8,128)S(1)} %copy-done.5), custom_call_target="tpu_custom_call" | custom-call | flops 100000000 | bytes 9216 | tf_op jit(solution)/shard_map/pallas_call | solution.py:304
  108.3 1.7 %shard_map.90 = f32[256,256]{1,0:T(8,128)} custom-call(s32[1]{0:T(128)} %bitcast.20.refs_7_.number_ref, f32[256,256]{1,0:T(8,128)S(1)} %pad_maximum_fusion.cross_ref, f32[256,256]{1,0:T(8,128)S(1)} %get-tuple-element.63.inverse_ref), custom_call_target="tpu_custom_call" | custom-call | flops 150994944 | bytes 276480 | tf_op jit(solution)/shard_map/pallas_call | solution.py:503
  (83 shorter events, 25.4 us)
Async XLA Ops:
  3.2 14.7 %collective-permute-start = (bf16[592,256]{1,0:T(8,128)(2,1)}, bf16[592,256]{1,0:T(8,128)(2,1)}, u32[]{:S(2)}, u32[]{:S(2)}) collective-permute-start(bf16[592,256]{1,0:T(8,128)(2,1)} %fusion.1), channel_id=1, source_target_pairs={{0,2},{2,4},{4,6},{6,8},{8,10},{10,12},{12,14},{14,16},{16,18},{18... | collective-permute-start | bytes 909320 | tf_op jit(solution)/shard_map/ppermute | solution.py:27
  5.2 14.6 %collective-permute-start.1 = (bf16[592,256]{1,0:T(8,128)(2,1)}, bf16[592,256]{1,0:T(8,128)(2,1)}, u32[]{:S(2)}, u32[]{:S(2)}) collective-permute-start(bf16[592,256]{1,0:T(8,128)(2,1)} %fusion.1), channel_id=1, source_target_pairs={{0,30},{2,0},{4,2},{6,4},{8,6},{10,8},{12,10},{14,12},{16,14},{18,... | collective-permute-start | bytes 909320 | tf_op jit(solution)/shard_map/ppermute | solution.py:27
  9.2 2.0 %copy-start.2 = (bf16[3,12,192,192]{3,2,1,0:T(8,128)(2,1)S(1)}, bf16[3,12,192,192]{3,2,1,0:T(8,128)(2,1)}, u32[]{:S(2)}) copy-start(bf16[3,12,192,192]{3,2,1,0:T(8,128)(2,1)} %blocks_ref.1) | copy-start | bytes 7962628
  11.2 3.5 %copy-start.7 = (s32[3,12]{1,0:T(4,128)S(1)}, s32[3,12]{1,0:T(4,128)}, u32[]{:S(2)}) copy-start(s32[3,12]{1,0:T(4,128)} %cols_ref.1) | copy-start | bytes 436
  11.2 3.5 %copy-start.8 = (f32[2]{0:T(128)S(1)}, f32[2]{0:T(128)}, u32[]{:S(2)}) copy-start(f32[2]{0:T(128)} %refs_7_.3) | copy-start | bytes 28
  11.2 3.5 %copy-start.9 = (s32[3]{0:T(128)S(1)}, s32[3]{0:T(128)}, u32[]{:S(2)}) copy-start(s32[3]{0:T(128)} %live_ref.1) | copy-start | bytes 40
  14.7 1.1 copy-start
  20.5 3.8 %collective-permute-start.2 = (bf16[592,256]{1,0:T(8,128)(2,1)}, bf16[592,256]{1,0:T(8,128)(2,1)S(1)}, u32[]{:S(2)}, u32[]{:S(2)}) collective-permute-start(bf16[592,256]{1,0:T(8,128)(2,1)} %collective-permute-done), channel_id=1, source_target_pairs={{0,1},{1,0},{2,3},{3,2},{4,5},{5,4},{6,7},{7,6},{8,9},{9,8},{10,11... | collective-permute-start | bytes 909320 | tf_op jit(solution)/shard_map/ppermute | solution.py:378
  22.1 2.2 %collective-permute-start.3 = (bf16[592,256]{1,0:T(8,128)(2,1)}, bf16[592,256]{1,0:T(8,128)(2,1)S(1)}, u32[]{:S(2)}, u32[]{:S(2)}) collective-permute-start(bf16[592,256]{1,0:T(8,128)(2,1)} %collective-permute-done.1), channel_id=1, source_target_pairs={{0,1},{1,0},{2,3},{3,2},{4,5},{5,4},{6,7},{7,6},{8,9},{9,8},{10,11... | collective-permute-start | bytes 909320 | tf_op jit(solution)/shard_map/ppermute | solution.py:378
  24.3 9.2 %copy-start.1 = (f32[576,256]{1,0:T(8,128)S(1)}, f32[576,256]{1,0:T(8,128)}, u32[]{:S(2)}) copy-start(f32[576,256]{1,0:T(8,128)} %refs_3_.1) | copy-start | bytes 1769476
  25.6 13.5 %collective-permute-start.4 = (bf16[576,256]{1,0:T(8,128)(2,1)S(1)}, bf16[576,256]{1,0:T(8,128)(2,1)S(1)}, u32[]{:S(2)}, u32[]{:S(2)}) collective-permute-start(bf16[576,256]{1,0:T(8,128)(2,1)S(1)} %get-tuple-element.36), channel_id=1, source_target_pairs={{0,2},{2,4},{4,6},{6,8},{8,10},{10,12},{12,14},{14,16},{16,18},{18... | collective-permute-start | bytes 884744 | tf_op jit(solution)/shard_map/ppermute | solution.py:27
  26.8 14.5 %collective-permute-start.6 = (bf16[576,256]{1,0:T(8,128)(2,1)S(1)}, bf16[576,256]{1,0:T(8,128)(2,1)S(1)}, u32[]{:S(2)}, u32[]{:S(2)}) collective-permute-start(bf16[576,256]{1,0:T(8,128)(2,1)S(1)} %get-tuple-element.36), channel_id=1, source_target_pairs={{0,30},{2,0},{4,2},{6,4},{8,6},{10,8},{12,10},{14,12},{16,14},{18,... | collective-permute-start | bytes 884744 | tf_op jit(solution)/shard_map/ppermute | solution.py:27
  39.1 5.1 %collective-permute-start.5 = (bf16[576,256]{1,0:T(8,128)(2,1)S(1)}, bf16[576,256]{1,0:T(8,128)(2,1)S(1)}, u32[]{:S(2)}, u32[]{:S(2)}) collective-permute-start(bf16[576,256]{1,0:T(8,128)(2,1)S(1)} %collective-permute-done.4), channel_id=1, source_target_pairs={{0,1},{1,0},{2,3},{3,2},{4,5},{5,4},{6,7},{7,6},{8,9},{9,8},{10,11... | collective-permute-start | bytes 884744 | tf_op jit(solution)/shard_map/ppermute | solution.py:378
  41.3 2.9 %collective-permute-start.7 = (bf16[576,256]{1,0:T(8,128)(2,1)S(1)}, bf16[576,256]{1,0:T(8,128)(2,1)S(1)}, u32[]{:S(2)}, u32[]{:S(2)}) collective-permute-start(bf16[576,256]{1,0:T(8,128)(2,1)S(1)} %collective-permute-done.6), channel_id=1, source_target_pairs={{0,1},{1,0},{2,3},{3,2},{4,5},{5,4},{6,7},{7,6},{8,9},{9,8},{10,11... | collective-permute-start | bytes 884744 | tf_op jit(solution)/shard_map/ppermute | solution.py:378
  47.0 5.1 %collective-permute-start.8 = (bf16[576,256]{1,0:T(8,128)(2,1)}, bf16[576,256]{1,0:T(8,128)(2,1)}, u32[]{:S(2)}, u32[]{:S(2)}) collective-permute-start(bf16[576,256]{1,0:T(8,128)(2,1)} %get-tuple-element.39), channel_id=1, source_target_pairs={{0,1},{1,0},{2,3},{3,2},{4,5},{5,4},{6,7},{7,6},{8,9},{9,8},{10,11... | collective-permute-start | bytes 884744 | tf_op jit(solution)/shard_map/ppermute | solution.py:378
  47.0 13.6 %collective-permute-start.11 = (bf16[576,256]{1,0:T(8,128)(2,1)}, bf16[576,256]{1,0:T(8,128)(2,1)}, u32[]{:S(2)}, u32[]{:S(2)}) collective-permute-start(bf16[576,256]{1,0:T(8,128)(2,1)} %get-tuple-element.39), channel_id=1, source_target_pairs={{0,2},{2,4},{4,6},{6,8},{8,10},{10,12},{12,14},{14,16},{16,18},{18... | collective-permute-start | bytes 884744 | tf_op jit(solution)/shard_map/ppermute | solution.py:27
  47.5 14.9 %collective-permute-start.12 = (bf16[576,256]{1,0:T(8,128)(2,1)}, bf16[576,256]{1,0:T(8,128)(2,1)}, u32[]{:S(2)}, u32[]{:S(2)}) collective-permute-start(bf16[576,256]{1,0:T(8,128)(2,1)} %get-tuple-element.39), channel_id=1, source_target_pairs={{0,30},{2,0},{4,2},{6,4},{8,6},{10,8},{12,10},{14,12},{16,14},{18,... | collective-permute-start | bytes 884744 | tf_op jit(solution)/shard_map/ppermute | solution.py:27
  52.1 1.1 copy-start.4
  57.7 6.0 %collective-permute-start.9 = (f32[192,128]{1,0:T(8,128)}, f32[192,128]{1,0:T(8,128)}, u32[]{:S(2)}, u32[]{:S(2)}) collective-permute-start(f32[192,128]{1,0:T(8,128)} %slice.63), channel_id=1, source_target_pairs={{0,1},{1,0},{2,3},{3,2},{4,5},{5,4},{6,7},{7,6},{8,9},{9,8},{10,11... | collective-permute-start | bytes 294920 | tf_op jit(solution)/shard_map/ppermute | solution.py:314
  60.6 8.2 %collective-permute-start.13 = (bf16[576,256]{1,0:T(8,128)(2,1)}, bf16[576,256]{1,0:T(8,128)(2,1)S(1)}, u32[]{:S(2)}, u32[]{:S(2)}) collective-permute-start(bf16[576,256]{1,0:T(8,128)(2,1)} %collective-permute-done.11), channel_id=1, source_target_pairs={{0,1},{1,0},{2,3},{3,2},{4,5},{5,4},{6,7},{7,6},{8,9},{9,8},{10,11... | collective-permute-start | bytes 884744 | tf_op jit(solution)/shard_map/ppermute | solution.py:378
  62.4 6.4 %collective-permute-start.14 = (bf16[576,256]{1,0:T(8,128)(2,1)}, bf16[576,256]{1,0:T(8,128)(2,1)S(1)}, u32[]{:S(2)}, u32[]{:S(2)}) collective-permute-start(bf16[576,256]{1,0:T(8,128)(2,1)} %collective-permute-done.12), channel_id=1, source_target_pairs={{0,1},{1,0},{2,3},{3,2},{4,5},{5,4},{6,7},{7,6},{8,9},{9,8},{10,11... | collective-permute-start | bytes 884744 | tf_op jit(solution)/shard_map/ppermute | solution.py:378
  64.7 4.1 %collective-permute-start.10 = (f32[96,128]{1,0:T(8,128)S(1)}, f32[96,128]{1,0:T(8,128)S(1)}, u32[]{:S(2)}, u32[]{:S(2)}) collective-permute-start(f32[96,128]{1,0:T(8,128)S(1)} %slice.81), channel_id=1, source_target_pairs={{0,4},{2,6},{4,0},{6,2},{8,12},{10,14},{12,8},{14,10},{16,20},{18,... | collective-permute-start | bytes 147464 | tf_op jit(solution)/shard_map/ppermute | solution.py:314
  66.0 1.1 copy-start.11
  67.0 1.8 %copy-start.5 = (f32[576,256]{1,0:T(8,128)S(1)}, f32[576,256]{1,0:T(8,128)}, u32[]{:S(2)}) copy-start(f32[576,256]{1,0:T(8,128)} %copy-done.3) | copy-start | bytes 1769476
  71.6 1.4 %collective-permute-start.15 = (f32[128,256]{1,0:T(8,128)S(1)}, f32[128,256]{1,0:T(8,128)S(1)}, u32[]{:S(2)}, u32[]{:S(2)}) collective-permute-start(f32[128,256]{1,0:T(8,128)S(1)} %slice.83), channel_id=1, source_target_pairs={{0,1},{1,0},{2,3},{3,2},{4,5},{5,4},{6,7},{7,6},{8,9},{9,8},{10,11... | collective-permute-start | bytes 393224 | tf_op jit(solution)/shard_map/ppermute | solution.py:314
  73.1 4.5 %collective-permute-start.16 = (f32[112,256]{1,0:T(8,128)S(1)}, f32[112,256]{1,0:T(8,128)S(1)}, u32[]{:S(2)}, u32[]{:S(2)}) collective-permute-start(f32[112,256]{1,0:T(8,128)S(1)} %fusion.2), channel_id=1, source_target_pairs={{0,2},{2,0},{4,6},{6,4},{8,10},{10,8},{12,14},{14,12},{16,18},{18,... | collective-permute-start | bytes 344072 | tf_op jit(solution)/shard_map/ppermute | solution.py:314
  77.7 3.7 %collective-permute-start.17 = (f32[112,256]{1,0:T(8,128)S(1)}, f32[112,256]{1,0:T(8,128)S(1)}, u32[]{:S(2)}, u32[]{:S(2)}) collective-permute-start(f32[112,256]{1,0:T(8,128)S(1)} %maximum_add_fusion), channel_id=1, source_target_pairs={{0,8},{2,10},{4,12},{6,14},{8,0},{10,2},{12,4},{14,6},{16,24},{18,... | collective-permute-start | bytes 344072 | tf_op jit(solution)/shard_map/ppermute | solution.py:314
  81.4 5.8 %collective-permute-start.18 = (f32[112,256]{1,0:T(8,128)S(1)}, f32[112,256]{1,0:T(8,128)S(1)}, u32[]{:S(2)}, u32[]{:S(2)}) collective-permute-start(f32[112,256]{1,0:T(8,128)S(1)} %add.52), channel_id=1, source_target_pairs={{0,16},{2,18},{4,20},{6,22},{8,24},{10,26},{12,28},{14,30},{16,0},... | collective-permute-start | bytes 344072 | tf_op jit(solution)/shard_map/ppermute | solution.py:314
  87.3 3.7 %collective-permute-start.19 = (f32[112,256]{1,0:T(8,128)S(1)}, f32[112,256]{1,0:T(8,128)S(1)}, u32[]{:S(2)}, u32[]{:S(2)}) collective-permute-start(f32[112,256]{1,0:T(8,128)S(1)} %add.53), channel_id=1, source_target_pairs={{0,4},{2,6},{4,0},{6,2},{8,12},{10,14},{12,8},{14,10},{16,20},{18,... | collective-permute-start | bytes 344072 | tf_op jit(solution)/shard_map/ppermute | solution.py:314
  91.0 5.6 %collective-permute-start.20 = (f32[192,128]{1,0:T(8,128)S(1)}, f32[192,128]{1,0:T(8,128)S(1)}, u32[]{:S(2)}, u32[]{:S(2)}) collective-permute-start(f32[192,128]{1,0:T(8,128)S(1)} %pad_maximum_fusion.3), channel_id=1, source_target_pairs={{0,1},{1,0},{2,3},{3,2},{4,5},{5,4},{6,7},{7,6},{8,9},{9,8},{10,11... | collective-permute-start | bytes 294920 | tf_op jit(solution)/shard_map/ppermute | solution.py:314
  96.6 9.1 %collective-permute-start.21 = (f32[64,256]{1,0:T(8,128)S(1)}, f32[64,256]{1,0:T(8,128)S(1)}, u32[]{:S(2)}, u32[]{:S(2)}) collective-permute-start(f32[64,256]{1,0:T(8,128)S(1)} %slice_add_fusion.2), channel_id=1, source_target_pairs={{0,2},{2,0},{4,6},{6,4},{8,10},{10,8},{12,14},{14,12},{16,18},{18,... | collective-permute-start | bytes 196616 | tf_op jit(solution)/shard_map/ppermute | solution.py:314
  105.7 2.6 %collective-permute-start.22 = (f32[128,256]{1,0:T(8,128)S(1)}, f32[128,256]{1,0:T(8,128)S(1)}, u32[]{:S(2)}, u32[]{:S(2)}) collective-permute-start(f32[128,256]{1,0:T(8,128)S(1)} %pad_maximum_fusion.1), channel_id=1, source_target_pairs={{0,1},{1,0},{2,3},{3,2},{4,5},{5,4},{6,7},{7,6},{8,9},{9,8},{10,11... | collective-permute-start | bytes 393224 | tf_op jit(solution)/shard_map/ppermute | solution.py:314
  (3 other events, 2.3 us)

commit v20 on v19

--- a/solution.py
+++ b/solution.py
@@ -252,8 +252,8 @@
         out_ref[...] = tiles[name]
 
 
-def basis_body(count, *refs):
-    *tile_refs, two_ref, basis_ref, inverse_ref = refs
+def basis_body(count, total_rows, number_ref, cross_ref, *refs):
+    *tile_refs, two_ref, basis_ref, projected_ref = refs
     tiles = {name: ref[...] for name, ref in zip(lower_tiles(count), tile_refs)}
     inverse = {}
     for row in range(count):
@@ -271,16 +271,13 @@
         ],
         0,
     )
-    inverse_ref[...] = whole
+    cross = ordered_pieces(number_ref, cross_ref) / total_rows
+    left = exact_dot(whole, cross)
     basis_ref[...] = exact_dot(two_ref[...], whole, NT)
-
-
-def projected_body(total_rows, number_ref, cross_ref, inverse_ref, projected_ref):
-    cross = ordered_pieces(number_ref, cross_ref) / total_rows
-    projected_ref[...] = exact_dot(exact_dot(inverse_ref[...], cross), inverse_ref[...], NT)
-
-
-def factor_stages(total_rows, count, number, two):
+    projected_ref[...] = exact_dot(left, whole, NT)
+
+
+def factor_stages(total_rows, count, number, two, cross_number):
     rows, modes = two.shape
     tile = jax.ShapeDtypeStruct((TILE, TILE), jnp.float32)
     names = lower_tiles(count)
@@ -298,12 +295,13 @@
 
         return stage
 
-    def finish(state):
+    def finish(state, cross):
         outs = (jax.ShapeDtypeStruct((rows, modes), jnp.float32), jax.ShapeDtypeStruct((modes, modes), jnp.float32))
-        body = functools.partial(basis_body, count)
-        return tuple(kernel_call(body, outs, [VMEM] * (len(names) + 1), work, rows * modes)(*state, two))
-
-    return [first] + [following(at) for at in range(1, count)] + [finish]
+        body = functools.partial(basis_body, count, total_rows)
+        call = kernel_call(body, outs, [SMEM] + [VMEM] * (len(names) + 2), work, rows * modes)
+        return tuple(call(cross_number, cross, *state, two))
+
+    return [first] + [following(at) for at in range(1, count)], finish
 
 
 def tied(left, right):
@@ -495,12 +493,10 @@
     got = partner_value(both, *across)
     gram = joining(*cores)(jnp.concatenate(flat(both[:cut]) + flat(got[:cut]), 0))()
     cross = both[cut:] + got[cut:]
-    stages = factor_stages(float(total_rows), modes // TILE, gram_number, two)
+    stages, finish = factor_stages(float(total_rows), modes // TILE, gram_number, two, cross_number)
     steps = [joining(*near), joining(*cores)]
-    cross, (basis, inverse) = run_beside(cross, steps, gram, stages)
-    body_of = functools.partial(projected_body, float(total_rows))
-    call = kernel_call(body_of, square, [SMEM] + [VMEM] * 2, 2 * square_work, traffic)
-    return basis, call(cross_number, cross, inverse)
+    cross, tiles = run_beside(cross, steps, gram, stages)
+    return finish(tiles, cross)
 
 
 def solution(mesh):

time: 111 us -> 109 us (0.982)
  waiting for transfers between devices: 25.1 us -> 26.8 us
  starting transfers between devices: 35.1 us -> 33.6 us
  Pallas kernels: 29.8 us -> 28.5 us
    ppermute x6, starting transfers between devices: 16.2 us -> 14.3 us  [shifted(): return lax.ppermute(value, axis, pairs)]
    ppermute x6, waiting for transfers between devices: 9.74 us -> 11.4 us  [shifted(): return lax.ppermute(value, axis, pairs)]
    pallas_call x2 -> x1, Pallas kernels: 3.61 us -> 2.33 us  [finish(): return tuple(call(cross_number, cross, *state, two))]
  transfers between devices with their start and end apart: 23 -> 23, of which waited for: 12 -> 12; matrix products, arithmetic and copies ran while one was open for 2% -> 2% of each run, Pallas kernels for 20% -> 19%
where the time goes in v20:
time: 109 us
  starting transfers between devices  33.6 us (31%)
  Pallas kernels  28.5 us (26%)
  waiting for transfers between devices  26.8 us (25%)
  local copies, waits for them, and re-layouts  9.54 us (9%)
  blocking collectives  5.58 us (5%)
  other arithmetic  3.69 us (3%)
    ppermute x10, waiting for transfers between devices, partner_value(): lax.ppermute(value, axis, [(at, at ^ bit) for at in range(lax.axis_size(a...  15.4 us
    ppermute x6, starting transfers between devices, shifted(): return lax.ppermute(value, axis, pairs)  14.3 us
    ppermute x10, starting transfers between devices, partner_value(): lax.ppermute(value, axis, [(at, at ^ bit) for at in range(lax.axis_size(a...  12.5 us
    ppermute x6, waiting for transfers between devices, shifted(): return lax.ppermute(value, axis, pairs)  11.4 us
    unnamed x26, local copies, waits for them, and re-layouts  7.52 us
    ppermute x7, starting transfers between devices, local(): swapped = lambda value: lax.ppermute(value, 'split', [(0, 1), (1, 0)])  6.77 us
    pallas_call x3, Pallas kernels, last_part(): return call(table, lists, bases, held, *pair, total, *scalars, *extra)  5.95 us
    all_gather x2, blocking collectives, exchange(): groups = [lax.all_gather(operand, 'split', axis=0)]  5.58 us
  transfers between devices with their start and end apart: 23, of which 12 were waited for; matrix products, arithmetic and copies ran while one was open for 2% of the time, Pallas kernels for 19%

profile of v20, /device:TPU:1, one launch (start us, length us, event | category | flops | bytes accessed | tf_op | source)
XLA Modules:
  0.0 108.7 jit_solution(14797556426665764620)
XLA Ops:
  3.2 2.0 %collective-permute-start = (bf16[592,256]{1,0:T(8,128)(2,1)}, bf16[592,256]{1,0:T(8,128)(2,1)}, u32[]{:S(2)}, u32[]{:S(2)}) collective-permute-start(bf16[592,256]{1,0:T(8,128)(2,1)} %fusion.1), channel_id=1, source_target_pairs={{0,2},{2,4},{4,6},{6,8},{8,10},{10,12},{12,14},{14,16},{16,18},{18... | collective-permute-start | bytes 909320 | tf_op jit(solution)/shard_map/ppermute | solution.py:27
  5.2 4.0 %collective-permute-start.1 = (bf16[592,256]{1,0:T(8,128)(2,1)}, bf16[592,256]{1,0:T(8,128)(2,1)}, u32[]{:S(2)}, u32[]{:S(2)}) collective-permute-start(bf16[592,256]{1,0:T(8,128)(2,1)} %fusion.1), channel_id=1, source_target_pairs={{0,30},{2,0},{4,2},{6,4},{8,6},{10,8},{12,10},{14,12},{16,14},{18,... | collective-permute-start | bytes 909320 | tf_op jit(solution)/shard_map/ppermute | solution.py:27
  9.2 2.0 %copy-done.2 = bf16[3,12,192,192]{3,2,1,0:T(8,128)(2,1)S(1)} copy-done((bf16[3,12,192,192]{3,2,1,0:T(8,128)(2,1)S(1)}, bf16[3,12,192,192]{3,2,1,0:T(8,128)(2,1)}, u32[]{:S(2)}) %copy-start.2) | copy-done | bytes 2654232
  11.6 3.0 %all-gather = bf16[1184,256]{1,0:T(8,128)(2,1)S(1)} all-gather(bf16[592,256]{1,0:T(8,128)(2,1)} %fusion.1), channel_id=2, replica_groups=mesh['region'=16,'split'=2] {'split'}, dimensions={0}, use_global_device_ids=true | all-gather | bytes 909312 | tf_op jit(solution)/shard_map/all_gather | solution.py:403
  15.7 1.7 %shard_map.78 = (f32[576,256]{1,0:T(8,128)S(1)}, s32[3,19]{1,0:T(4,128)S(1)}) custom-call(s32[3,12]{1,0:T(4,128)S(1)} %copy-done.7, s32[3]{0:T(128)S(1)} %copy-done.9, s32[2]{0:T(128)S(1)} %broadcast_1_bases_ref.2.bases_ref, bf16[3,12,192,192]{3,2,1,0:T(8,128)(2,1)S(1)} %shard_map.77.hessian_ref.refs_3_.refs_2_, bf16[2,592,256]{2,1,0:T(8,128)(2,1)S(1)} %bitcast.22, ...), custom_call_target="tpu_custom_call" | custom-call | flops 10000000 | bytes 276480 | tf_op jit(solution)/shard_map/pallas_call | solution.py:463
  18.5 1.3 %collective-permute-done.1 = bf16[592,256]{1,0:T(8,128)(2,1)} collective-permute-done((bf16[592,256]{1,0:T(8,128)(2,1)}, bf16[592,256]{1,0:T(8,128)(2,1)}, u32[]{:S(2)}, u32[]{:S(2)}) %collective-permute-start.1) | collective-permute-done | bytes 303136 | tf_op jit(solution)/shard_map/ppermute | solution.py:27
  20.5 1.6 %collective-permute-start.2 = (bf16[592,256]{1,0:T(8,128)(2,1)}, bf16[592,256]{1,0:T(8,128)(2,1)S(1)}, u32[]{:S(2)}, u32[]{:S(2)}) collective-permute-start(bf16[592,256]{1,0:T(8,128)(2,1)} %collective-permute-done), channel_id=1, source_target_pairs={{0,1},{1,0},{2,3},{3,2},{4,5},{5,4},{6,7},{7,6},{8,9},{9,8},{10,11... | collective-permute-start | bytes 909320 | tf_op jit(solution)/shard_map/ppermute | solution.py:376
  22.2 2.1 %shard_map.79 = (f32[576,256]{1,0:T(8,128)S(1)}, f32[8,128]{1,0:T(8,128)}) custom-call(s32[3,19]{1,0:T(4,128)S(1)} %get-tuple-element.32.refs_0_.slots_ref, s32[2,6]{1,0:T(2,128)S(1)} %maximum_convert_fusion.refs_1_, s32[2]{0:T(128)S(1)} %pad_add_fusion.refs_2_.refs_1_, bf16[3,12,192,192]{3,2,1,0:T(8,128)(2,1)S(1)} %shard_map.77.hessian_ref.refs_3_.refs_2_, ...), custom_call_target="tpu_custom_call" | custom-call | flops 30000001024 | bytes 276480 | tf_op jit(solution)/shard_map/pallas_call | solution.py:458
  25.5 3.2 %collective-permute-start.6 = (bf16[576,256]{1,0:T(8,128)(2,1)S(1)}, bf16[576,256]{1,0:T(8,128)(2,1)S(1)}, u32[]{:S(2)}, u32[]{:S(2)}) collective-permute-start(bf16[576,256]{1,0:T(8,128)(2,1)S(1)} %get-tuple-element.35), channel_id=1, source_target_pairs={{0,30},{2,0},{4,2},{6,4},{8,6},{10,8},{12,10},{14,12},{16,14},{18,... | collective-permute-start | bytes 884744 | tf_op jit(solution)/shard_map/ppermute | solution.py:27
  28.7 2.5 %all-gather.1 = bf16[1152,256]{1,0:T(8,128)(2,1)S(1)} all-gather(bf16[576,256]{1,0:T(8,128)(2,1)S(1)} %get-tuple-element.35), channel_id=3, replica_groups=mesh['region'=16,'split'=2] {'split'}, dimensions={0}, use_global_device_ids=true | all-gather | bytes 884736 | tf_op jit(solution)/shard_map/all_gather | solution.py:403
  32.5 2.2 %collective-permute-done.6 = bf16[576,256]{1,0:T(8,128)(2,1)S(1)} collective-permute-done((bf16[576,256]{1,0:T(8,128)(2,1)S(1)}, bf16[576,256]{1,0:T(8,128)(2,1)S(1)}, u32[]{:S(2)}, u32[]{:S(2)}) %collective-permute-start.6) | collective-permute-done | bytes 294944 | tf_op jit(solution)/shard_map/ppermute | solution.py:27
  34.7 1.3 %collective-permute-start.7 = (bf16[576,256]{1,0:T(8,128)(2,1)S(1)}, bf16[576,256]{1,0:T(8,128)(2,1)S(1)}, u32[]{:S(2)}, u32[]{:S(2)}) collective-permute-start(bf16[576,256]{1,0:T(8,128)(2,1)S(1)} %collective-permute-done.6), channel_id=1, source_target_pairs={{0,1},{1,0},{2,3},{3,2},{4,5},{5,4},{6,7},{7,6},{8,9},{9,8},{10,11... | collective-permute-start | bytes 884744 | tf_op jit(solution)/shard_map/ppermute | solution.py:376
  36.0 4.2 %collective-permute-done.4 = bf16[576,256]{1,0:T(8,128)(2,1)S(1)} collective-permute-done((bf16[576,256]{1,0:T(8,128)(2,1)S(1)}, bf16[576,256]{1,0:T(8,128)(2,1)S(1)}, u32[]{:S(2)}, u32[]{:S(2)}) %collective-permute-start.4) | collective-permute-done | bytes 294944 | tf_op jit(solution)/shard_map/ppermute | solution.py:27
  40.2 1.7 %collective-permute-start.5 = (bf16[576,256]{1,0:T(8,128)(2,1)S(1)}, bf16[576,256]{1,0:T(8,128)(2,1)S(1)}, u32[]{:S(2)}, u32[]{:S(2)}) collective-permute-start(bf16[576,256]{1,0:T(8,128)(2,1)S(1)} %collective-permute-done.4), channel_id=1, source_target_pairs={{0,1},{1,0},{2,3},{3,2},{4,5},{5,4},{6,7},{7,6},{8,9},{9,8},{10,11... | collective-permute-start | bytes 884744 | tf_op jit(solution)/shard_map/ppermute | solution.py:376
  41.9 1.6 %shard_map.82 = (f32[576,256]{1,0:T(8,128)S(1)}, f32[8,128]{1,0:T(8,128)}) custom-call(s32[3,19]{1,0:T(4,128)S(1)} %get-tuple-element.32.refs_0_.slots_ref, s32[2,6]{1,0:T(2,128)S(1)} %maximum_convert_fusion.refs_1_, s32[2]{0:T(128)S(1)} %pad_add_fusion.refs_2_.refs_1_, bf16[3,12,192,192]{3,2,1,0:T(8,128)(2,1)S(1)} %shard_map.77.hessian_ref.refs_3_.refs_2_, ...), custom_call_target="tpu_custom_call" | custom-call | flops 30000001024 | bytes 276480 | tf_op jit(solution)/shard_map/pallas_call | solution.py:458
  43.5 1.9 %shard_map.83 = (f32[576,256]{1,0:T(8,128)S(1)}, bf16[576,256]{1,0:T(8,128)(2,1)}) custom-call(s32[3,19]{1,0:T(4,128)S(1)} %get-tuple-element.32.refs_0_.slots_ref, s32[2,6]{1,0:T(2,128)S(1)} %maximum_convert_fusion.refs_1_, s32[2]{0:T(128)S(1)} %pad_add_fusion.refs_2_.refs_1_, bf16[3,12,192,192]{3,2,1,0:T(8,128)(2,1)S(1)} %shard_map.77.hessian_ref.refs_3_.refs_2_, ...), custom_call_target="tpu_custom_call" | custom-call | flops 30000001024 | bytes 276480 | tf_op jit(solution)/shard_map/pallas_call | solution.py:449
  47.1 4.2 %collective-permute-start.12 = (bf16[576,256]{1,0:T(8,128)(2,1)}, bf16[576,256]{1,0:T(8,128)(2,1)}, u32[]{:S(2)}, u32[]{:S(2)}) collective-permute-start(bf16[576,256]{1,0:T(8,128)(2,1)} %get-tuple-element.38), channel_id=1, source_target_pairs={{0,30},{2,0},{4,2},{6,4},{8,6},{10,8},{12,10},{14,12},{16,14},{18,... | collective-permute-start | bytes 884744 | tf_op jit(solution)/shard_map/ppermute | solution.py:27
  52.4 2.5 %shard_map.84 = (f32[576,256]{1,0:T(8,128)S(1)}, f32[384,128]{1,0:T(8,128)S(1)}) custom-call(s32[3,19]{1,0:T(4,128)S(1)} %get-tuple-element.32.refs_0_.slots_ref, s32[2]{0:T(128)S(1)} %pad_add_fusion.refs_2_.refs_1_, bf16[3,12,192,192]{3,2,1,0:T(8,128)(2,1)S(1)} %shard_map.77.hessian_ref.refs_3_.refs_2_, bf16[1,576,256]{2,1,0:T(8,128)(2,1)} %bitcast.14.refs_3_, ...), custom_call_target="tpu_custom_call" | custom-call | flops 10000000 | bytes 276480 | tf_op jit(solution)/shard_map/pallas_call | solution.py:444
  58.1 1.6 %collective-permute-done.11 = bf16[576,256]{1,0:T(8,128)(2,1)} collective-permute-done((bf16[576,256]{1,0:T(8,128)(2,1)}, bf16[576,256]{1,0:T(8,128)(2,1)}, u32[]{:S(2)}, u32[]{:S(2)}) %collective-permute-start.11) | collective-permute-done | bytes 294944 | tf_op jit(solution)/shard_map/ppermute | solution.py:27
  59.7 1.3 %collective-permute-start.13 = (bf16[576,256]{1,0:T(8,128)(2,1)}, bf16[576,256]{1,0:T(8,128)(2,1)S(1)}, u32[]{:S(2)}, u32[]{:S(2)}) collective-permute-start(bf16[576,256]{1,0:T(8,128)(2,1)} %collective-permute-done.11), channel_id=1, source_target_pairs={{0,1},{1,0},{2,3},{3,2},{4,5},{5,4},{6,7},{7,6},{8,9},{9,8},{10,11... | collective-permute-start | bytes 884744 | tf_op jit(solution)/shard_map/ppermute | solution.py:376
  61.0 1.7 %collective-permute-done.12 = bf16[576,256]{1,0:T(8,128)(2,1)} collective-permute-done((bf16[576,256]{1,0:T(8,128)(2,1)}, bf16[576,256]{1,0:T(8,128)(2,1)}, u32[]{:S(2)}, u32[]{:S(2)}) %collective-permute-start.12) | collective-permute-done | bytes 294944 | tf_op jit(solution)/shard_map/ppermute | solution.py:27
  66.3 1.7 %shard_map.85 = (f32[576,256]{1,0:T(8,128)S(1)}, f32[8,128]{1,0:T(8,128)S(1)}) custom-call(s32[3,19]{1,0:T(4,128)S(1)} %get-tuple-element.32.refs_0_.slots_ref, s32[2,6]{1,0:T(2,128)S(1)} %maximum_convert_fusion.refs_1_, s32[2]{0:T(128)S(1)} %pad_add_fusion.refs_2_.refs_1_, bf16[3,12,192,192]{3,2,1,0:T(8,128)(2,1)S(1)} %shard_map.77.hessian_ref.refs_3_.refs_2_, ...), custom_call_target="tpu_custom_call" | custom-call | flops 30000001024 | bytes 276480 | tf_op jit(solution)/shard_map/pallas_call | solution.py:458
  68.1 2.8 %shard_map.86 = f32[256,256]{1,0:T(8,128)S(1)} custom-call(s32[3,19]{1,0:T(4,128)S(1)} %get-tuple-element.32.refs_0_.slots_ref, s32[2,6]{1,0:T(2,128)S(1)} %maximum_convert_fusion.refs_1_, s32[2]{0:T(128)S(1)} %pad_add_fusion.refs_2_.refs_1_, bf16[3,12,192,192]{3,2,1,0:T(8,128)(2,1)S(1)} %shard_map.77.hessian_ref.refs_3_.refs_2_, ...), custom_call_target="tpu_custom_call" | custom-call | flops 30000001024 | bytes 276480 | tf_op jit(solution)/shard_map/pallas_call | solution.py:449
  73.1 4.0 %collective-permute-done.16 = f32[112,256]{1,0:T(8,128)S(1)} collective-permute-done((f32[112,256]{1,0:T(8,128)S(1)}, f32[112,256]{1,0:T(8,128)S(1)}, u32[]{:S(2)}, u32[]{:S(2)}) %collective-permute-start.16) | collective-permute-done | bytes 114720 | tf_op jit(solution)/shard_map/ppermute | solution.py:312
  78.1 2.7 %collective-permute-done.17 = f32[112,256]{1,0:T(8,128)S(1)} collective-permute-done((f32[112,256]{1,0:T(8,128)S(1)}, f32[112,256]{1,0:T(8,128)S(1)}, u32[]{:S(2)}, u32[]{:S(2)}) %collective-permute-start.17) | collective-permute-done | bytes 114720 | tf_op jit(solution)/shard_map/ppermute | solution.py:312
  80.9 2.0 %collective-permute-start.18 = (f32[112,256]{1,0:T(8,128)S(1)}, f32[112,256]{1,0:T(8,128)S(1)}, u32[]{:S(2)}, u32[]{:S(2)}) collective-permute-start(f32[112,256]{1,0:T(8,128)S(1)} %add.52), channel_id=1, source_target_pairs={{0,16},{2,18},{4,20},{6,22},{8,24},{10,26},{12,28},{14,30},{16,0},... | collective-permute-start | bytes 344072 | tf_op jit(solution)/shard_map/ppermute | solution.py:312
  82.9 3.8 %collective-permute-done.18 = f32[112,256]{1,0:T(8,128)S(1)} collective-permute-done((f32[112,256]{1,0:T(8,128)S(1)}, f32[112,256]{1,0:T(8,128)S(1)}, u32[]{:S(2)}, u32[]{:S(2)}) %collective-permute-start.18) | collective-permute-done | bytes 114720 | tf_op jit(solution)/shard_map/ppermute | solution.py:312
  87.5 3.0 %collective-permute-done.19 = f32[112,256]{1,0:T(8,128)S(1)} collective-permute-done((f32[112,256]{1,0:T(8,128)S(1)}, f32[112,256]{1,0:T(8,128)S(1)}, u32[]{:S(2)}, u32[]{:S(2)}) %collective-permute-start.19) | collective-permute-done | bytes 114720 | tf_op jit(solution)/shard_map/ppermute | solution.py:312
  90.5 4.7 %collective-permute-start.20 = (f32[192,128]{1,0:T(8,128)S(1)}, f32[192,128]{1,0:T(8,128)S(1)}, u32[]{:S(2)}, u32[]{:S(2)}) collective-permute-start(f32[192,128]{1,0:T(8,128)S(1)} %pad_maximum_fusion.3), channel_id=1, source_target_pairs={{0,1},{1,0},{2,3},{3,2},{4,5},{5,4},{6,7},{7,6},{8,9},{9,8},{10,11... | collective-permute-start | bytes 294920 | tf_op jit(solution)/shard_map/ppermute | solution.py:312
  96.6 4.8 %shard_map.87 = (f32[128,128]{1,0:T(8,128)S(1)}, f32[128,128]{1,0:T(8,128)S(1)}, f32[128,128]{1,0:T(8,128)S(1)}) custom-call(s32[1]{0:T(128)} %bitcast.16.refs_5_.number_ref, f32[384,128]{1,0:T(8,128)S(1)} %constant_dynamic-update-slice_fusion.gram_ref), custom_call_target="tpu_custom_call" | custom-call | flops 100000000 | bytes 3072 | tf_op jit(solution)/shard_map/pallas_call | solution.py:288
  102.1 4.2 %shard_map.88 = (f32[128,128]{1,0:T(8,128)S(1)}, f32[128,128]{1,0:T(8,128)S(1)}, f32[128,128]{1,0:T(8,128)S(1)}) custom-call(f32[128,128]{1,0:T(8,128)S(1)} %get-tuple-element.52.refs_0_, f32[128,128]{1,0:T(8,128)S(1)} %get-tuple-element.53.refs_1_, f32[128,128]{1,0:T(8,128)S(1)} %get-tuple-element.54.refs_2_), custom_call_target="tpu_custom_call" | custom-call | flops 100000000 | bytes 1024 | tf_op jit(solution)/shard_map/pallas_call | solution.py:294
  106.3 2.3 %shard_map.89 = (f32[576,256]{1,0:T(8,128)}, f32[256,256]{1,0:T(8,128)}) custom-call(s32[1]{0:T(128)} %bitcast.refs_7_.number_ref, f32[256,256]{1,0:T(8,128)S(1)} %pad_maximum_fusion.cross_ref, f32[128,128]{1,0:T(8,128)S(1)} %get-tuple-element.59.refs_0_, f32[128,128]{1,0:T(8,128)S(1)} %get-tuple-element.60.refs_1_, ...), custom_call_target="tpu_custom_call" | custom-call | flops 100000000 | bytes 9216 | tf_op jit(solution)/shard_map/pallas_call | solution.py:302
  (82 shorter events, 23.9 us)
Async XLA Ops:
  3.2 14.7 %collective-permute-start = (bf16[592,256]{1,0:T(8,128)(2,1)}, bf16[592,256]{1,0:T(8,128)(2,1)}, u32[]{:S(2)}, u32[]{:S(2)}) collective-permute-start(bf16[592,256]{1,0:T(8,128)(2,1)} %fusion.1), channel_id=1, source_target_pairs={{0,2},{2,4},{4,6},{6,8},{8,10},{10,12},{12,14},{14,16},{16,18},{18... | collective-permute-start | bytes 909320 | tf_op jit(solution)/shard_map/ppermute | solution.py:27
  5.2 14.6 %collective-permute-start.1 = (bf16[592,256]{1,0:T(8,128)(2,1)}, bf16[592,256]{1,0:T(8,128)(2,1)}, u32[]{:S(2)}, u32[]{:S(2)}) collective-permute-start(bf16[592,256]{1,0:T(8,128)(2,1)} %fusion.1), channel_id=1, source_target_pairs={{0,30},{2,0},{4,2},{6,4},{8,6},{10,8},{12,10},{14,12},{16,14},{18,... | collective-permute-start | bytes 909320 | tf_op jit(solution)/shard_map/ppermute | solution.py:27
  9.2 2.0 %copy-start.2 = (bf16[3,12,192,192]{3,2,1,0:T(8,128)(2,1)S(1)}, bf16[3,12,192,192]{3,2,1,0:T(8,128)(2,1)}, u32[]{:S(2)}) copy-start(bf16[3,12,192,192]{3,2,1,0:T(8,128)(2,1)} %blocks_ref.1) | copy-start | bytes 7962628
  11.2 3.5 %copy-start.7 = (s32[3,12]{1,0:T(4,128)S(1)}, s32[3,12]{1,0:T(4,128)}, u32[]{:S(2)}) copy-start(s32[3,12]{1,0:T(4,128)} %cols_ref.1) | copy-start | bytes 436
  11.2 3.5 %copy-start.8 = (f32[2]{0:T(128)S(1)}, f32[2]{0:T(128)}, u32[]{:S(2)}) copy-start(f32[2]{0:T(128)} %refs_7_.3) | copy-start | bytes 28
  11.2 3.5 %copy-start.9 = (s32[3]{0:T(128)S(1)}, s32[3]{0:T(128)}, u32[]{:S(2)}) copy-start(s32[3]{0:T(128)} %live_ref.1) | copy-start | bytes 40
  14.7 1.1 copy-start
  20.5 3.8 %collective-permute-start.2 = (bf16[592,256]{1,0:T(8,128)(2,1)}, bf16[592,256]{1,0:T(8,128)(2,1)S(1)}, u32[]{:S(2)}, u32[]{:S(2)}) collective-permute-start(bf16[592,256]{1,0:T(8,128)(2,1)} %collective-permute-done), channel_id=1, source_target_pairs={{0,1},{1,0},{2,3},{3,2},{4,5},{5,4},{6,7},{7,6},{8,9},{9,8},{10,11... | collective-permute-start | bytes 909320 | tf_op jit(solution)/shard_map/ppermute | solution.py:376
  22.1 2.2 %collective-permute-start.3 = (bf16[592,256]{1,0:T(8,128)(2,1)}, bf16[592,256]{1,0:T(8,128)(2,1)S(1)}, u32[]{:S(2)}, u32[]{:S(2)}) collective-permute-start(bf16[592,256]{1,0:T(8,128)(2,1)} %collective-permute-done.1), channel_id=1, source_target_pairs={{0,1},{1,0},{2,3},{3,2},{4,5},{5,4},{6,7},{7,6},{8,9},{9,8},{10,11... | collective-permute-start | bytes 909320 | tf_op jit(solution)/shard_map/ppermute | solution.py:376
  24.3 7.0 %copy-start.1 = (f32[576,256]{1,0:T(8,128)S(1)}, f32[576,256]{1,0:T(8,128)}, u32[]{:S(2)}) copy-start(f32[576,256]{1,0:T(8,128)} %refs_3_.1) | copy-start | bytes 1769476
  25.5 9.2 %collective-permute-start.6 = (bf16[576,256]{1,0:T(8,128)(2,1)S(1)}, bf16[576,256]{1,0:T(8,128)(2,1)S(1)}, u32[]{:S(2)}, u32[]{:S(2)}) collective-permute-start(bf16[576,256]{1,0:T(8,128)(2,1)S(1)} %get-tuple-element.35), channel_id=1, source_target_pairs={{0,30},{2,0},{4,2},{6,4},{8,6},{10,8},{12,10},{14,12},{16,14},{18,... | collective-permute-start | bytes 884744 | tf_op jit(solution)/shard_map/ppermute | solution.py:27
  28.7 11.4 %collective-permute-start.4 = (bf16[576,256]{1,0:T(8,128)(2,1)S(1)}, bf16[576,256]{1,0:T(8,128)(2,1)S(1)}, u32[]{:S(2)}, u32[]{:S(2)}) collective-permute-start(bf16[576,256]{1,0:T(8,128)(2,1)S(1)} %get-tuple-element.35), channel_id=1, source_target_pairs={{0,2},{2,4},{4,6},{6,8},{8,10},{10,12},{12,14},{14,16},{16,18},{18... | collective-permute-start | bytes 884744 | tf_op jit(solution)/shard_map/ppermute | solution.py:27
  34.7 8.8 %collective-permute-start.7 = (bf16[576,256]{1,0:T(8,128)(2,1)S(1)}, bf16[576,256]{1,0:T(8,128)(2,1)S(1)}, u32[]{:S(2)}, u32[]{:S(2)}) collective-permute-start(bf16[576,256]{1,0:T(8,128)(2,1)S(1)} %collective-permute-done.6), channel_id=1, source_target_pairs={{0,1},{1,0},{2,3},{3,2},{4,5},{5,4},{6,7},{7,6},{8,9},{9,8},{10,11... | collective-permute-start | bytes 884744 | tf_op jit(solution)/shard_map/ppermute | solution.py:376
  40.2 3.4 %collective-permute-start.5 = (bf16[576,256]{1,0:T(8,128)(2,1)S(1)}, bf16[576,256]{1,0:T(8,128)(2,1)S(1)}, u32[]{:S(2)}, u32[]{:S(2)}) collective-permute-start(bf16[576,256]{1,0:T(8,128)(2,1)S(1)} %collective-permute-done.4), channel_id=1, source_target_pairs={{0,1},{1,0},{2,3},{3,2},{4,5},{5,4},{6,7},{7,6},{8,9},{9,8},{10,11... | collective-permute-start | bytes 884744 | tf_op jit(solution)/shard_map/ppermute | solution.py:376
  46.3 5.1 %collective-permute-start.8 = (bf16[576,256]{1,0:T(8,128)(2,1)}, bf16[576,256]{1,0:T(8,128)(2,1)}, u32[]{:S(2)}, u32[]{:S(2)}) collective-permute-start(bf16[576,256]{1,0:T(8,128)(2,1)} %get-tuple-element.38), channel_id=1, source_target_pairs={{0,1},{1,0},{2,3},{3,2},{4,5},{5,4},{6,7},{7,6},{8,9},{9,8},{10,11... | collective-permute-start | bytes 884744 | tf_op jit(solution)/shard_map/ppermute | solution.py:376
  46.3 13.4 %collective-permute-start.11 = (bf16[576,256]{1,0:T(8,128)(2,1)}, bf16[576,256]{1,0:T(8,128)(2,1)}, u32[]{:S(2)}, u32[]{:S(2)}) collective-permute-start(bf16[576,256]{1,0:T(8,128)(2,1)} %get-tuple-element.38), channel_id=1, source_target_pairs={{0,2},{2,4},{4,6},{6,8},{8,10},{10,12},{12,14},{14,16},{16,18},{18... | collective-permute-start | bytes 884744 | tf_op jit(solution)/shard_map/ppermute | solution.py:27
  47.1 15.6 %collective-permute-start.12 = (bf16[576,256]{1,0:T(8,128)(2,1)}, bf16[576,256]{1,0:T(8,128)(2,1)}, u32[]{:S(2)}, u32[]{:S(2)}) collective-permute-start(bf16[576,256]{1,0:T(8,128)(2,1)} %get-tuple-element.38), channel_id=1, source_target_pairs={{0,30},{2,0},{4,2},{6,4},{8,6},{10,8},{12,10},{14,12},{16,14},{18,... | collective-permute-start | bytes 884744 | tf_op jit(solution)/shard_map/ppermute | solution.py:27
  51.3 1.1 copy-start.4
  57.0 6.5 %collective-permute-start.9 = (f32[192,128]{1,0:T(8,128)}, f32[192,128]{1,0:T(8,128)}, u32[]{:S(2)}, u32[]{:S(2)}) collective-permute-start(f32[192,128]{1,0:T(8,128)} %slice.63), channel_id=1, source_target_pairs={{0,1},{1,0},{2,3},{3,2},{4,5},{5,4},{6,7},{7,6},{8,9},{9,8},{10,11... | collective-permute-start | bytes 294920 | tf_op jit(solution)/shard_map/ppermute | solution.py:312
  59.7 8.4 %collective-permute-start.13 = (bf16[576,256]{1,0:T(8,128)(2,1)}, bf16[576,256]{1,0:T(8,128)(2,1)S(1)}, u32[]{:S(2)}, u32[]{:S(2)}) collective-permute-start(bf16[576,256]{1,0:T(8,128)(2,1)} %collective-permute-done.11), channel_id=1, source_target_pairs={{0,1},{1,0},{2,3},{3,2},{4,5},{5,4},{6,7},{7,6},{8,9},{9,8},{10,11... | collective-permute-start | bytes 884744 | tf_op jit(solution)/shard_map/ppermute | solution.py:376
  62.7 5.3 %collective-permute-start.14 = (bf16[576,256]{1,0:T(8,128)(2,1)}, bf16[576,256]{1,0:T(8,128)(2,1)S(1)}, u32[]{:S(2)}, u32[]{:S(2)}) collective-permute-start(bf16[576,256]{1,0:T(8,128)(2,1)} %collective-permute-done.12), channel_id=1, source_target_pairs={{0,1},{1,0},{2,3},{3,2},{4,5},{5,4},{6,7},{7,6},{8,9},{9,8},{10,11... | collective-permute-start | bytes 884744 | tf_op jit(solution)/shard_map/ppermute | solution.py:376
  64.5 3.6 %collective-permute-start.10 = (f32[96,128]{1,0:T(8,128)S(1)}, f32[96,128]{1,0:T(8,128)S(1)}, u32[]{:S(2)}, u32[]{:S(2)}) collective-permute-start(f32[96,128]{1,0:T(8,128)S(1)} %slice.81), channel_id=1, source_target_pairs={{0,4},{2,6},{4,0},{6,2},{8,12},{10,14},{12,8},{14,10},{16,20},{18,... | collective-permute-start | bytes 147464 | tf_op jit(solution)/shard_map/ppermute | solution.py:312
  65.2 1.1 copy-start.11
  66.3 1.8 %copy-start.5 = (f32[576,256]{1,0:T(8,128)S(1)}, f32[576,256]{1,0:T(8,128)}, u32[]{:S(2)}) copy-start(f32[576,256]{1,0:T(8,128)} %copy-done.3) | copy-start | bytes 1769476
  70.9 1.7 %collective-permute-start.15 = (f32[128,256]{1,0:T(8,128)S(1)}, f32[128,256]{1,0:T(8,128)S(1)}, u32[]{:S(2)}, u32[]{:S(2)}) collective-permute-start(f32[128,256]{1,0:T(8,128)S(1)} %slice.83), channel_id=1, source_target_pairs={{0,1},{1,0},{2,3},{3,2},{4,5},{5,4},{6,7},{7,6},{8,9},{9,8},{10,11... | collective-permute-start | bytes 393224 | tf_op jit(solution)/shard_map/ppermute | solution.py:312
  72.7 4.4 %collective-permute-start.16 = (f32[112,256]{1,0:T(8,128)S(1)}, f32[112,256]{1,0:T(8,128)S(1)}, u32[]{:S(2)}, u32[]{:S(2)}) collective-permute-start(f32[112,256]{1,0:T(8,128)S(1)} %fusion.2), channel_id=1, source_target_pairs={{0,2},{2,0},{4,6},{6,4},{8,10},{10,8},{12,14},{14,12},{16,18},{18,... | collective-permute-start | bytes 344072 | tf_op jit(solution)/shard_map/ppermute | solution.py:312
  77.1 3.7 %collective-permute-start.17 = (f32[112,256]{1,0:T(8,128)S(1)}, f32[112,256]{1,0:T(8,128)S(1)}, u32[]{:S(2)}, u32[]{:S(2)}) collective-permute-start(f32[112,256]{1,0:T(8,128)S(1)} %maximum_add_fusion), channel_id=1, source_target_pairs={{0,8},{2,10},{4,12},{6,14},{8,0},{10,2},{12,4},{14,6},{16,24},{18,... | collective-permute-start | bytes 344072 | tf_op jit(solution)/shard_map/ppermute | solution.py:312
  80.9 5.8 %collective-permute-start.18 = (f32[112,256]{1,0:T(8,128)S(1)}, f32[112,256]{1,0:T(8,128)S(1)}, u32[]{:S(2)}, u32[]{:S(2)}) collective-permute-start(f32[112,256]{1,0:T(8,128)S(1)} %add.52), channel_id=1, source_target_pairs={{0,16},{2,18},{4,20},{6,22},{8,24},{10,26},{12,28},{14,30},{16,0},... | collective-permute-start | bytes 344072 | tf_op jit(solution)/shard_map/ppermute | solution.py:312
  86.7 3.7 %collective-permute-start.19 = (f32[112,256]{1,0:T(8,128)S(1)}, f32[112,256]{1,0:T(8,128)S(1)}, u32[]{:S(2)}, u32[]{:S(2)}) collective-permute-start(f32[112,256]{1,0:T(8,128)S(1)} %add.53), channel_id=1, source_target_pairs={{0,4},{2,6},{4,0},{6,2},{8,12},{10,14},{12,8},{14,10},{16,20},{18,... | collective-permute-start | bytes 344072 | tf_op jit(solution)/shard_map/ppermute | solution.py:312
  90.5 5.6 %collective-permute-start.20 = (f32[192,128]{1,0:T(8,128)S(1)}, f32[192,128]{1,0:T(8,128)S(1)}, u32[]{:S(2)}, u32[]{:S(2)}) collective-permute-start(f32[192,128]{1,0:T(8,128)S(1)} %pad_maximum_fusion.3), channel_id=1, source_target_pairs={{0,1},{1,0},{2,3},{3,2},{4,5},{5,4},{6,7},{7,6},{8,9},{9,8},{10,11... | collective-permute-start | bytes 294920 | tf_op jit(solution)/shard_map/ppermute | solution.py:312
  96.1 5.3 %collective-permute-start.21 = (f32[64,256]{1,0:T(8,128)S(1)}, f32[64,256]{1,0:T(8,128)S(1)}, u32[]{:S(2)}, u32[]{:S(2)}) collective-permute-start(f32[64,256]{1,0:T(8,128)S(1)} %slice_add_fusion.2), channel_id=1, source_target_pairs={{0,2},{2,0},{4,6},{6,4},{8,10},{10,8},{12,14},{14,12},{16,18},{18,... | collective-permute-start | bytes 196616 | tf_op jit(solution)/shard_map/ppermute | solution.py:312
  101.4 4.9 %collective-permute-start.22 = (f32[128,256]{1,0:T(8,128)S(1)}, f32[128,256]{1,0:T(8,128)S(1)}, u32[]{:S(2)}, u32[]{:S(2)}) collective-permute-start(f32[128,256]{1,0:T(8,128)S(1)} %pad_maximum_fusion.1), channel_id=1, source_target_pairs={{0,1},{1,0},{2,3},{3,2},{4,5},{5,4},{6,7},{7,6},{8,9},{9,8},{10,11... | collective-permute-start | bytes 393224 | tf_op jit(solution)/shard_map/ppermute | solution.py:312
  (3 other events, 2.3 us)

commit v21 on v20

--- a/solution.py
+++ b/solution.py
@@ -14,7 +14,7 @@
 NT = (((1,), (1,)), ((), ()))
 TN = (((0,), (0,)), ((), ()))
 GROUP = 8
-PANEL = 32
+PANEL = 64
 TILE = 128
 VMEM_LIMIT = 6 * 1024 * 1024
 LIST_ROWS = 16

time: 109 us -> 109 us (level)
  no operation moved by 1% of the time
where the time goes in v21:
time: 109 us
  starting transfers between devices  33.6 us (31%)
  Pallas kernels  28.7 us (26%)
  waiting for transfers between devices  26.8 us (25%)
  local copies, waits for them, and re-layouts  9.54 us (9%)
  blocking collectives  5.58 us (5%)
  other arithmetic  3.69 us (3%)
    ppermute x10, waiting for transfers between devices, partner_value(): lax.ppermute(value, axis, [(at, at ^ bit) for at in range(lax.axis_size(a...  15.4 us
    ppermute x6, starting transfers between devices, shifted(): return lax.ppermute(value, axis, pairs)  14.3 us
    ppermute x10, starting transfers between devices, partner_value(): lax.ppermute(value, axis, [(at, at ^ bit) for at in range(lax.axis_size(a...  12.5 us
    ppermute x6, waiting for transfers between devices, shifted(): return lax.ppermute(value, axis, pairs)  11.4 us
    unnamed x26, local copies, waits for them, and re-layouts  7.52 us
    ppermute x7, starting transfers between devices, local(): swapped = lambda value: lax.ppermute(value, 'split', [(0, 1), (1, 0)])  6.77 us
    pallas_call x3, Pallas kernels, last_part(): return call(table, lists, bases, held, *pair, total, *scalars, *extra)  5.95 us
    all_gather x2, blocking collectives, exchange(): groups = [lax.all_gather(operand, 'split', axis=0)]  5.58 us
  transfers between devices with their start and end apart: 23, of which 12 were waited for; matrix products, arithmetic and copies ran while one was open for 2% of the time, Pallas kernels for 19%

profile of v21, /device:TPU:1, one launch (start us, length us, event | category | flops | bytes accessed | tf_op | source)
XLA Modules:
  0.0 108.9 jit_solution(10610613773173921222)
XLA Ops:
  3.2 2.0 %collective-permute-start = (bf16[592,256]{1,0:T(8,128)(2,1)}, bf16[592,256]{1,0:T(8,128)(2,1)}, u32[]{:S(2)}, u32[]{:S(2)}) collective-permute-start(bf16[592,256]{1,0:T(8,128)(2,1)} %fusion.1), channel_id=1, source_target_pairs={{0,2},{2,4},{4,6},{6,8},{8,10},{10,12},{12,14},{14,16},{16,18},{18... | collective-permute-start | bytes 909320 | tf_op jit(solution)/shard_map/ppermute | solution.py:27
  5.2 4.0 %collective-permute-start.1 = (bf16[592,256]{1,0:T(8,128)(2,1)}, bf16[592,256]{1,0:T(8,128)(2,1)}, u32[]{:S(2)}, u32[]{:S(2)}) collective-permute-start(bf16[592,256]{1,0:T(8,128)(2,1)} %fusion.1), channel_id=1, source_target_pairs={{0,30},{2,0},{4,2},{6,4},{8,6},{10,8},{12,10},{14,12},{16,14},{18,... | collective-permute-start | bytes 909320 | tf_op jit(solution)/shard_map/ppermute | solution.py:27
  9.2 2.0 %copy-done.2 = bf16[3,12,192,192]{3,2,1,0:T(8,128)(2,1)S(1)} copy-done((bf16[3,12,192,192]{3,2,1,0:T(8,128)(2,1)S(1)}, bf16[3,12,192,192]{3,2,1,0:T(8,128)(2,1)}, u32[]{:S(2)}) %copy-start.2) | copy-done | bytes 2654232
  11.6 3.0 %all-gather = bf16[1184,256]{1,0:T(8,128)(2,1)S(1)} all-gather(bf16[592,256]{1,0:T(8,128)(2,1)} %fusion.1), channel_id=2, replica_groups=mesh['region'=16,'split'=2] {'split'}, dimensions={0}, use_global_device_ids=true | all-gather | bytes 909312 | tf_op jit(solution)/shard_map/all_gather | solution.py:403
  15.7 1.7 %shard_map.78 = (f32[576,256]{1,0:T(8,128)S(1)}, s32[3,19]{1,0:T(4,128)S(1)}) custom-call(s32[3,12]{1,0:T(4,128)S(1)} %copy-done.7, s32[3]{0:T(128)S(1)} %copy-done.9, s32[2]{0:T(128)S(1)} %broadcast_1_bases_ref.2.bases_ref, bf16[3,12,192,192]{3,2,1,0:T(8,128)(2,1)S(1)} %shard_map.77.hessian_ref.refs_3_.refs_2_, bf16[2,592,256]{2,1,0:T(8,128)(2,1)S(1)} %bitcast.22, ...), custom_call_target="tpu_custom_call" | custom-call | flops 10000000 | bytes 276480 | tf_op jit(solution)/shard_map/pallas_call | solution.py:463
  18.5 1.3 %collective-permute-done.1 = bf16[592,256]{1,0:T(8,128)(2,1)} collective-permute-done((bf16[592,256]{1,0:T(8,128)(2,1)}, bf16[592,256]{1,0:T(8,128)(2,1)}, u32[]{:S(2)}, u32[]{:S(2)}) %collective-permute-start.1) | collective-permute-done | bytes 303136 | tf_op jit(solution)/shard_map/ppermute | solution.py:27
  20.5 1.6 %collective-permute-start.2 = (bf16[592,256]{1,0:T(8,128)(2,1)}, bf16[592,256]{1,0:T(8,128)(2,1)S(1)}, u32[]{:S(2)}, u32[]{:S(2)}) collective-permute-start(bf16[592,256]{1,0:T(8,128)(2,1)} %collective-permute-done), channel_id=1, source_target_pairs={{0,1},{1,0},{2,3},{3,2},{4,5},{5,4},{6,7},{7,6},{8,9},{9,8},{10,11... | collective-permute-start | bytes 909320 | tf_op jit(solution)/shard_map/ppermute | solution.py:376
  22.2 2.1 %shard_map.79 = (f32[576,256]{1,0:T(8,128)S(1)}, f32[8,128]{1,0:T(8,128)}) custom-call(s32[3,19]{1,0:T(4,128)S(1)} %get-tuple-element.32.refs_0_.slots_ref, s32[2,6]{1,0:T(2,128)S(1)} %maximum_convert_fusion.refs_1_, s32[2]{0:T(128)S(1)} %pad_add_fusion.refs_2_.refs_1_, bf16[3,12,192,192]{3,2,1,0:T(8,128)(2,1)S(1)} %shard_map.77.hessian_ref.refs_3_.refs_2_, ...), custom_call_target="tpu_custom_call" | custom-call | flops 30000001024 | bytes 276480 | tf_op jit(solution)/shard_map/pallas_call | solution.py:458
  25.5 3.2 %collective-permute-start.6 = (bf16[576,256]{1,0:T(8,128)(2,1)S(1)}, bf16[576,256]{1,0:T(8,128)(2,1)S(1)}, u32[]{:S(2)}, u32[]{:S(2)}) collective-permute-start(bf16[576,256]{1,0:T(8,128)(2,1)S(1)} %get-tuple-element.35), channel_id=1, source_target_pairs={{0,30},{2,0},{4,2},{6,4},{8,6},{10,8},{12,10},{14,12},{16,14},{18,... | collective-permute-start | bytes 884744 | tf_op jit(solution)/shard_map/ppermute | solution.py:27
  28.7 2.5 %all-gather.1 = bf16[1152,256]{1,0:T(8,128)(2,1)S(1)} all-gather(bf16[576,256]{1,0:T(8,128)(2,1)S(1)} %get-tuple-element.35), channel_id=3, replica_groups=mesh['region'=16,'split'=2] {'split'}, dimensions={0}, use_global_device_ids=true | all-gather | bytes 884736 | tf_op jit(solution)/shard_map/all_gather | solution.py:403
  32.5 2.2 %collective-permute-done.6 = bf16[576,256]{1,0:T(8,128)(2,1)S(1)} collective-permute-done((bf16[576,256]{1,0:T(8,128)(2,1)S(1)}, bf16[576,256]{1,0:T(8,128)(2,1)S(1)}, u32[]{:S(2)}, u32[]{:S(2)}) %collective-permute-start.6) | collective-permute-done | bytes 294944 | tf_op jit(solution)/shard_map/ppermute | solution.py:27
  34.7 1.3 %collective-permute-start.7 = (bf16[576,256]{1,0:T(8,128)(2,1)S(1)}, bf16[576,256]{1,0:T(8,128)(2,1)S(1)}, u32[]{:S(2)}, u32[]{:S(2)}) collective-permute-start(bf16[576,256]{1,0:T(8,128)(2,1)S(1)} %collective-permute-done.6), channel_id=1, source_target_pairs={{0,1},{1,0},{2,3},{3,2},{4,5},{5,4},{6,7},{7,6},{8,9},{9,8},{10,11... | collective-permute-start | bytes 884744 | tf_op jit(solution)/shard_map/ppermute | solution.py:376
  36.0 4.2 %collective-permute-done.4 = bf16[576,256]{1,0:T(8,128)(2,1)S(1)} collective-permute-done((bf16[576,256]{1,0:T(8,128)(2,1)S(1)}, bf16[576,256]{1,0:T(8,128)(2,1)S(1)}, u32[]{:S(2)}, u32[]{:S(2)}) %collective-permute-start.4) | collective-permute-done | bytes 294944 | tf_op jit(solution)/shard_map/ppermute | solution.py:27
  40.2 1.7 %collective-permute-start.5 = (bf16[576,256]{1,0:T(8,128)(2,1)S(1)}, bf16[576,256]{1,0:T(8,128)(2,1)S(1)}, u32[]{:S(2)}, u32[]{:S(2)}) collective-permute-start(bf16[576,256]{1,0:T(8,128)(2,1)S(1)} %collective-permute-done.4), channel_id=1, source_target_pairs={{0,1},{1,0},{2,3},{3,2},{4,5},{5,4},{6,7},{7,6},{8,9},{9,8},{10,11... | collective-permute-start | bytes 884744 | tf_op jit(solution)/shard_map/ppermute | solution.py:376
  41.9 1.6 %shard_map.82 = (f32[576,256]{1,0:T(8,128)S(1)}, f32[8,128]{1,0:T(8,128)}) custom-call(s32[3,19]{1,0:T(4,128)S(1)} %get-tuple-element.32.refs_0_.slots_ref, s32[2,6]{1,0:T(2,128)S(1)} %maximum_convert_fusion.refs_1_, s32[2]{0:T(128)S(1)} %pad_add_fusion.refs_2_.refs_1_, bf16[3,12,192,192]{3,2,1,0:T(8,128)(2,1)S(1)} %shard_map.77.hessian_ref.refs_3_.refs_2_, ...), custom_call_target="tpu_custom_call" | custom-call | flops 30000001024 | bytes 276480 | tf_op jit(solution)/shard_map/pallas_call | solution.py:458
  43.5 1.9 %shard_map.83 = (f32[576,256]{1,0:T(8,128)S(1)}, bf16[576,256]{1,0:T(8,128)(2,1)}) custom-call(s32[3,19]{1,0:T(4,128)S(1)} %get-tuple-element.32.refs_0_.slots_ref, s32[2,6]{1,0:T(2,128)S(1)} %maximum_convert_fusion.refs_1_, s32[2]{0:T(128)S(1)} %pad_add_fusion.refs_2_.refs_1_, bf16[3,12,192,192]{3,2,1,0:T(8,128)(2,1)S(1)} %shard_map.77.hessian_ref.refs_3_.refs_2_, ...), custom_call_target="tpu_custom_call" | custom-call | flops 30000001024 | bytes 276480 | tf_op jit(solution)/shard_map/pallas_call | solution.py:449
  47.1 4.2 %collective-permute-start.12 = (bf16[576,256]{1,0:T(8,128)(2,1)}, bf16[576,256]{1,0:T(8,128)(2,1)}, u32[]{:S(2)}, u32[]{:S(2)}) collective-permute-start(bf16[576,256]{1,0:T(8,128)(2,1)} %get-tuple-element.38), channel_id=1, source_target_pairs={{0,30},{2,0},{4,2},{6,4},{8,6},{10,8},{12,10},{14,12},{16,14},{18,... | collective-permute-start | bytes 884744 | tf_op jit(solution)/shard_map/ppermute | solution.py:27
  52.4 2.5 %shard_map.84 = (f32[576,256]{1,0:T(8,128)S(1)}, f32[384,128]{1,0:T(8,128)S(1)}) custom-call(s32[3,19]{1,0:T(4,128)S(1)} %get-tuple-element.32.refs_0_.slots_ref, s32[2]{0:T(128)S(1)} %pad_add_fusion.refs_2_.refs_1_, bf16[3,12,192,192]{3,2,1,0:T(8,128)(2,1)S(1)} %shard_map.77.hessian_ref.refs_3_.refs_2_, bf16[1,576,256]{2,1,0:T(8,128)(2,1)} %bitcast.14.refs_3_, ...), custom_call_target="tpu_custom_call" | custom-call | flops 10000000 | bytes 276480 | tf_op jit(solution)/shard_map/pallas_call | solution.py:444
  58.1 1.6 %collective-permute-done.11 = bf16[576,256]{1,0:T(8,128)(2,1)} collective-permute-done((bf16[576,256]{1,0:T(8,128)(2,1)}, bf16[576,256]{1,0:T(8,128)(2,1)}, u32[]{:S(2)}, u32[]{:S(2)}) %collective-permute-start.11) | collective-permute-done | bytes 294944 | tf_op jit(solution)/shard_map/ppermute | solution.py:27
  59.7 1.3 %collective-permute-start.13 = (bf16[576,256]{1,0:T(8,128)(2,1)}, bf16[576,256]{1,0:T(8,128)(2,1)S(1)}, u32[]{:S(2)}, u32[]{:S(2)}) collective-permute-start(bf16[576,256]{1,0:T(8,128)(2,1)} %collective-permute-done.11), channel_id=1, source_target_pairs={{0,1},{1,0},{2,3},{3,2},{4,5},{5,4},{6,7},{7,6},{8,9},{9,8},{10,11... | collective-permute-start | bytes 884744 | tf_op jit(solution)/shard_map/ppermute | solution.py:376
  61.0 1.7 %collective-permute-done.12 = bf16[576,256]{1,0:T(8,128)(2,1)} collective-permute-done((bf16[576,256]{1,0:T(8,128)(2,1)}, bf16[576,256]{1,0:T(8,128)(2,1)}, u32[]{:S(2)}, u32[]{:S(2)}) %collective-permute-start.12) | collective-permute-done | bytes 294944 | tf_op jit(solution)/shard_map/ppermute | solution.py:27
  66.3 1.7 %shard_map.85 = (f32[576,256]{1,0:T(8,128)S(1)}, f32[8,128]{1,0:T(8,128)S(1)}) custom-call(s32[3,19]{1,0:T(4,128)S(1)} %get-tuple-element.32.refs_0_.slots_ref, s32[2,6]{1,0:T(2,128)S(1)} %maximum_convert_fusion.refs_1_, s32[2]{0:T(128)S(1)} %pad_add_fusion.refs_2_.refs_1_, bf16[3,12,192,192]{3,2,1,0:T(8,128)(2,1)S(1)} %shard_map.77.hessian_ref.refs_3_.refs_2_, ...), custom_call_target="tpu_custom_call" | custom-call | flops 30000001024 | bytes 276480 | tf_op jit(solution)/shard_map/pallas_call | solution.py:458
  68.1 2.8 %shard_map.86 = f32[256,256]{1,0:T(8,128)S(1)} custom-call(s32[3,19]{1,0:T(4,128)S(1)} %get-tuple-element.32.refs_0_.slots_ref, s32[2,6]{1,0:T(2,128)S(1)} %maximum_convert_fusion.refs_1_, s32[2]{0:T(128)S(1)} %pad_add_fusion.refs_2_.refs_1_, bf16[3,12,192,192]{3,2,1,0:T(8,128)(2,1)S(1)} %shard_map.77.hessian_ref.refs_3_.refs_2_, ...), custom_call_target="tpu_custom_call" | custom-call | flops 30000001024 | bytes 276480 | tf_op jit(solution)/shard_map/pallas_call | solution.py:449
  73.1 4.0 %collective-permute-done.16 = f32[112,256]{1,0:T(8,128)S(1)} collective-permute-done((f32[112,256]{1,0:T(8,128)S(1)}, f32[112,256]{1,0:T(8,128)S(1)}, u32[]{:S(2)}, u32[]{:S(2)}) %collective-permute-start.16) | collective-permute-done | bytes 114720 | tf_op jit(solution)/shard_map/ppermute | solution.py:312
  78.1 2.7 %collective-permute-done.17 = f32[112,256]{1,0:T(8,128)S(1)} collective-permute-done((f32[112,256]{1,0:T(8,128)S(1)}, f32[112,256]{1,0:T(8,128)S(1)}, u32[]{:S(2)}, u32[]{:S(2)}) %collective-permute-start.17) | collective-permute-done | bytes 114720 | tf_op jit(solution)/shard_map/ppermute | solution.py:312
  80.9 2.0 %collective-permute-start.18 = (f32[112,256]{1,0:T(8,128)S(1)}, f32[112,256]{1,0:T(8,128)S(1)}, u32[]{:S(2)}, u32[]{:S(2)}) collective-permute-start(f32[112,256]{1,0:T(8,128)S(1)} %add.52), channel_id=1, source_target_pairs={{0,16},{2,18},{4,20},{6,22},{8,24},{10,26},{12,28},{14,30},{16,0},... | collective-permute-start | bytes 344072 | tf_op jit(solution)/shard_map/ppermute | solution.py:312
  82.9 3.8 %collective-permute-done.18 = f32[112,256]{1,0:T(8,128)S(1)} collective-permute-done((f32[112,256]{1,0:T(8,128)S(1)}, f32[112,256]{1,0:T(8,128)S(1)}, u32[]{:S(2)}, u32[]{:S(2)}) %collective-permute-start.18) | collective-permute-done | bytes 114720 | tf_op jit(solution)/shard_map/ppermute | solution.py:312
  87.5 3.0 %collective-permute-done.19 = f32[112,256]{1,0:T(8,128)S(1)} collective-permute-done((f32[112,256]{1,0:T(8,128)S(1)}, f32[112,256]{1,0:T(8,128)S(1)}, u32[]{:S(2)}, u32[]{:S(2)}) %collective-permute-start.19) | collective-permute-done | bytes 114720 | tf_op jit(solution)/shard_map/ppermute | solution.py:312
  90.5 4.7 %collective-permute-start.20 = (f32[192,128]{1,0:T(8,128)S(1)}, f32[192,128]{1,0:T(8,128)S(1)}, u32[]{:S(2)}, u32[]{:S(2)}) collective-permute-start(f32[192,128]{1,0:T(8,128)S(1)} %pad_maximum_fusion.3), channel_id=1, source_target_pairs={{0,1},{1,0},{2,3},{3,2},{4,5},{5,4},{6,7},{7,6},{8,9},{9,8},{10,11... | collective-permute-start | bytes 294920 | tf_op jit(solution)/shard_map/ppermute | solution.py:312
  96.6 4.9 %shard_map.87 = (f32[128,128]{1,0:T(8,128)S(1)}, f32[128,128]{1,0:T(8,128)S(1)}, f32[128,128]{1,0:T(8,128)S(1)}) custom-call(s32[1]{0:T(128)} %bitcast.16.refs_5_.number_ref, f32[384,128]{1,0:T(8,128)S(1)} %constant_dynamic-update-slice_fusion.gram_ref), custom_call_target="tpu_custom_call" | custom-call | flops 100000000 | bytes 3072 | tf_op jit(solution)/shard_map/pallas_call | solution.py:288
  102.2 4.3 %shard_map.88 = (f32[128,128]{1,0:T(8,128)S(1)}, f32[128,128]{1,0:T(8,128)S(1)}, f32[128,128]{1,0:T(8,128)S(1)}) custom-call(f32[128,128]{1,0:T(8,128)S(1)} %get-tuple-element.52.refs_0_, f32[128,128]{1,0:T(8,128)S(1)} %get-tuple-element.53.refs_1_, f32[128,128]{1,0:T(8,128)S(1)} %get-tuple-element.54.refs_2_), custom_call_target="tpu_custom_call" | custom-call | flops 100000000 | bytes 1024 | tf_op jit(solution)/shard_map/pallas_call | solution.py:294
  106.5 2.3 %shard_map.89 = (f32[576,256]{1,0:T(8,128)}, f32[256,256]{1,0:T(8,128)}) custom-call(s32[1]{0:T(128)} %bitcast.refs_7_.number_ref, f32[256,256]{1,0:T(8,128)S(1)} %pad_maximum_fusion.cross_ref, f32[128,128]{1,0:T(8,128)S(1)} %get-tuple-element.59.refs_0_, f32[128,128]{1,0:T(8,128)S(1)} %get-tuple-element.60.refs_1_, ...), custom_call_target="tpu_custom_call" | custom-call | flops 100000000 | bytes 9216 | tf_op jit(solution)/shard_map/pallas_call | solution.py:302
  (82 shorter events, 23.9 us)
Async XLA Ops:
  3.2 14.7 %collective-permute-start = (bf16[592,256]{1,0:T(8,128)(2,1)}, bf16[592,256]{1,0:T(8,128)(2,1)}, u32[]{:S(2)}, u32[]{:S(2)}) collective-permute-start(bf16[592,256]{1,0:T(8,128)(2,1)} %fusion.1), channel_id=1, source_target_pairs={{0,2},{2,4},{4,6},{6,8},{8,10},{10,12},{12,14},{14,16},{16,18},{18... | collective-permute-start | bytes 909320 | tf_op jit(solution)/shard_map/ppermute | solution.py:27
  5.2 14.6 %collective-permute-start.1 = (bf16[592,256]{1,0:T(8,128)(2,1)}, bf16[592,256]{1,0:T(8,128)(2,1)}, u32[]{:S(2)}, u32[]{:S(2)}) collective-permute-start(bf16[592,256]{1,0:T(8,128)(2,1)} %fusion.1), channel_id=1, source_target_pairs={{0,30},{2,0},{4,2},{6,4},{8,6},{10,8},{12,10},{14,12},{16,14},{18,... | collective-permute-start | bytes 909320 | tf_op jit(solution)/shard_map/ppermute | solution.py:27
  9.2 2.0 %copy-start.2 = (bf16[3,12,192,192]{3,2,1,0:T(8,128)(2,1)S(1)}, bf16[3,12,192,192]{3,2,1,0:T(8,128)(2,1)}, u32[]{:S(2)}) copy-start(bf16[3,12,192,192]{3,2,1,0:T(8,128)(2,1)} %blocks_ref.1) | copy-start | bytes 7962628
  11.2 3.5 %copy-start.7 = (s32[3,12]{1,0:T(4,128)S(1)}, s32[3,12]{1,0:T(4,128)}, u32[]{:S(2)}) copy-start(s32[3,12]{1,0:T(4,128)} %cols_ref.1) | copy-start | bytes 436
  11.2 3.5 %copy-start.8 = (f32[2]{0:T(128)S(1)}, f32[2]{0:T(128)}, u32[]{:S(2)}) copy-start(f32[2]{0:T(128)} %refs_7_.3) | copy-start | bytes 28
  11.2 3.5 %copy-start.9 = (s32[3]{0:T(128)S(1)}, s32[3]{0:T(128)}, u32[]{:S(2)}) copy-start(s32[3]{0:T(128)} %live_ref.1) | copy-start | bytes 40
  14.7 1.1 copy-start
  20.5 3.8 %collective-permute-start.2 = (bf16[592,256]{1,0:T(8,128)(2,1)}, bf16[592,256]{1,0:T(8,128)(2,1)S(1)}, u32[]{:S(2)}, u32[]{:S(2)}) collective-permute-start(bf16[592,256]{1,0:T(8,128)(2,1)} %collective-permute-done), channel_id=1, source_target_pairs={{0,1},{1,0},{2,3},{3,2},{4,5},{5,4},{6,7},{7,6},{8,9},{9,8},{10,11... | collective-permute-start | bytes 909320 | tf_op jit(solution)/shard_map/ppermute | solution.py:376
  22.1 2.2 %collective-permute-start.3 = (bf16[592,256]{1,0:T(8,128)(2,1)}, bf16[592,256]{1,0:T(8,128)(2,1)S(1)}, u32[]{:S(2)}, u32[]{:S(2)}) collective-permute-start(bf16[592,256]{1,0:T(8,128)(2,1)} %collective-permute-done.1), channel_id=1, source_target_pairs={{0,1},{1,0},{2,3},{3,2},{4,5},{5,4},{6,7},{7,6},{8,9},{9,8},{10,11... | collective-permute-start | bytes 909320 | tf_op jit(solution)/shard_map/ppermute | solution.py:376
  24.3 7.0 %copy-start.1 = (f32[576,256]{1,0:T(8,128)S(1)}, f32[576,256]{1,0:T(8,128)}, u32[]{:S(2)}) copy-start(f32[576,256]{1,0:T(8,128)} %refs_3_.1) | copy-start | bytes 1769476
  25.5 9.2 %collective-permute-start.6 = (bf16[576,256]{1,0:T(8,128)(2,1)S(1)}, bf16[576,256]{1,0:T(8,128)(2,1)S(1)}, u32[]{:S(2)}, u32[]{:S(2)}) collective-permute-start(bf16[576,256]{1,0:T(8,128)(2,1)S(1)} %get-tuple-element.35), channel_id=1, source_target_pairs={{0,30},{2,0},{4,2},{6,4},{8,6},{10,8},{12,10},{14,12},{16,14},{18,... | collective-permute-start | bytes 884744 | tf_op jit(solution)/shard_map/ppermute | solution.py:27
  28.7 11.4 %collective-permute-start.4 = (bf16[576,256]{1,0:T(8,128)(2,1)S(1)}, bf16[576,256]{1,0:T(8,128)(2,1)S(1)}, u32[]{:S(2)}, u32[]{:S(2)}) collective-permute-start(bf16[576,256]{1,0:T(8,128)(2,1)S(1)} %get-tuple-element.35), channel_id=1, source_target_pairs={{0,2},{2,4},{4,6},{6,8},{8,10},{10,12},{12,14},{14,16},{16,18},{18... | collective-permute-start | bytes 884744 | tf_op jit(solution)/shard_map/ppermute | solution.py:27
  34.7 8.8 %collective-permute-start.7 = (bf16[576,256]{1,0:T(8,128)(2,1)S(1)}, bf16[576,256]{1,0:T(8,128)(2,1)S(1)}, u32[]{:S(2)}, u32[]{:S(2)}) collective-permute-start(bf16[576,256]{1,0:T(8,128)(2,1)S(1)} %collective-permute-done.6), channel_id=1, source_target_pairs={{0,1},{1,0},{2,3},{3,2},{4,5},{5,4},{6,7},{7,6},{8,9},{9,8},{10,11... | collective-permute-start | bytes 884744 | tf_op jit(solution)/shard_map/ppermute | solution.py:376
  40.2 3.4 %collective-permute-start.5 = (bf16[576,256]{1,0:T(8,128)(2,1)S(1)}, bf16[576,256]{1,0:T(8,128)(2,1)S(1)}, u32[]{:S(2)}, u32[]{:S(2)}) collective-permute-start(bf16[576,256]{1,0:T(8,128)(2,1)S(1)} %collective-permute-done.4), channel_id=1, source_target_pairs={{0,1},{1,0},{2,3},{3,2},{4,5},{5,4},{6,7},{7,6},{8,9},{9,8},{10,11... | collective-permute-start | bytes 884744 | tf_op jit(solution)/shard_map/ppermute | solution.py:376
  46.3 5.1 %collective-permute-start.8 = (bf16[576,256]{1,0:T(8,128)(2,1)}, bf16[576,256]{1,0:T(8,128)(2,1)}, u32[]{:S(2)}, u32[]{:S(2)}) collective-permute-start(bf16[576,256]{1,0:T(8,128)(2,1)} %get-tuple-element.38), channel_id=1, source_target_pairs={{0,1},{1,0},{2,3},{3,2},{4,5},{5,4},{6,7},{7,6},{8,9},{9,8},{10,11... | collective-permute-start | bytes 884744 | tf_op jit(solution)/shard_map/ppermute | solution.py:376
  46.3 13.4 %collective-permute-start.11 = (bf16[576,256]{1,0:T(8,128)(2,1)}, bf16[576,256]{1,0:T(8,128)(2,1)}, u32[]{:S(2)}, u32[]{:S(2)}) collective-permute-start(bf16[576,256]{1,0:T(8,128)(2,1)} %get-tuple-element.38), channel_id=1, source_target_pairs={{0,2},{2,4},{4,6},{6,8},{8,10},{10,12},{12,14},{14,16},{16,18},{18... | collective-permute-start | bytes 884744 | tf_op jit(solution)/shard_map/ppermute | solution.py:27
  47.1 15.6 %collective-permute-start.12 = (bf16[576,256]{1,0:T(8,128)(2,1)}, bf16[576,256]{1,0:T(8,128)(2,1)}, u32[]{:S(2)}, u32[]{:S(2)}) collective-permute-start(bf16[576,256]{1,0:T(8,128)(2,1)} %get-tuple-element.38), channel_id=1, source_target_pairs={{0,30},{2,0},{4,2},{6,4},{8,6},{10,8},{12,10},{14,12},{16,14},{18,... | collective-permute-start | bytes 884744 | tf_op jit(solution)/shard_map/ppermute | solution.py:27
  51.3 1.1 copy-start.4
  57.0 6.5 %collective-permute-start.9 = (f32[192,128]{1,0:T(8,128)}, f32[192,128]{1,0:T(8,128)}, u32[]{:S(2)}, u32[]{:S(2)}) collective-permute-start(f32[192,128]{1,0:T(8,128)} %slice.63), channel_id=1, source_target_pairs={{0,1},{1,0},{2,3},{3,2},{4,5},{5,4},{6,7},{7,6},{8,9},{9,8},{10,11... | collective-permute-start | bytes 294920 | tf_op jit(solution)/shard_map/ppermute | solution.py:312
  59.7 8.4 %collective-permute-start.13 = (bf16[576,256]{1,0:T(8,128)(2,1)}, bf16[576,256]{1,0:T(8,128)(2,1)S(1)}, u32[]{:S(2)}, u32[]{:S(2)}) collective-permute-start(bf16[576,256]{1,0:T(8,128)(2,1)} %collective-permute-done.11), channel_id=1, source_target_pairs={{0,1},{1,0},{2,3},{3,2},{4,5},{5,4},{6,7},{7,6},{8,9},{9,8},{10,11... | collective-permute-start | bytes 884744 | tf_op jit(solution)/shard_map/ppermute | solution.py:376
  62.7 5.3 %collective-permute-start.14 = (bf16[576,256]{1,0:T(8,128)(2,1)}, bf16[576,256]{1,0:T(8,128)(2,1)S(1)}, u32[]{:S(2)}, u32[]{:S(2)}) collective-permute-start(bf16[576,256]{1,0:T(8,128)(2,1)} %collective-permute-done.12), channel_id=1, source_target_pairs={{0,1},{1,0},{2,3},{3,2},{4,5},{5,4},{6,7},{7,6},{8,9},{9,8},{10,11... | collective-permute-start | bytes 884744 | tf_op jit(solution)/shard_map/ppermute | solution.py:376
  64.5 3.6 %collective-permute-start.10 = (f32[96,128]{1,0:T(8,128)S(1)}, f32[96,128]{1,0:T(8,128)S(1)}, u32[]{:S(2)}, u32[]{:S(2)}) collective-permute-start(f32[96,128]{1,0:T(8,128)S(1)} %slice.81), channel_id=1, source_target_pairs={{0,4},{2,6},{4,0},{6,2},{8,12},{10,14},{12,8},{14,10},{16,20},{18,... | collective-permute-start | bytes 147464 | tf_op jit(solution)/shard_map/ppermute | solution.py:312
  65.2 1.1 copy-start.11
  66.3 1.8 %copy-start.5 = (f32[576,256]{1,0:T(8,128)S(1)}, f32[576,256]{1,0:T(8,128)}, u32[]{:S(2)}) copy-start(f32[576,256]{1,0:T(8,128)} %copy-done.3) | copy-start | bytes 1769476
  70.9 1.7 %collective-permute-start.15 = (f32[128,256]{1,0:T(8,128)S(1)}, f32[128,256]{1,0:T(8,128)S(1)}, u32[]{:S(2)}, u32[]{:S(2)}) collective-permute-start(f32[128,256]{1,0:T(8,128)S(1)} %slice.83), channel_id=1, source_target_pairs={{0,1},{1,0},{2,3},{3,2},{4,5},{5,4},{6,7},{7,6},{8,9},{9,8},{10,11... | collective-permute-start | bytes 393224 | tf_op jit(solution)/shard_map/ppermute | solution.py:312
  72.7 4.4 %collective-permute-start.16 = (f32[112,256]{1,0:T(8,128)S(1)}, f32[112,256]{1,0:T(8,128)S(1)}, u32[]{:S(2)}, u32[]{:S(2)}) collective-permute-start(f32[112,256]{1,0:T(8,128)S(1)} %fusion.2), channel_id=1, source_target_pairs={{0,2},{2,0},{4,6},{6,4},{8,10},{10,8},{12,14},{14,12},{16,18},{18,... | collective-permute-start | bytes 344072 | tf_op jit(solution)/shard_map/ppermute | solution.py:312
  77.1 3.7 %collective-permute-start.17 = (f32[112,256]{1,0:T(8,128)S(1)}, f32[112,256]{1,0:T(8,128)S(1)}, u32[]{:S(2)}, u32[]{:S(2)}) collective-permute-start(f32[112,256]{1,0:T(8,128)S(1)} %maximum_add_fusion), channel_id=1, source_target_pairs={{0,8},{2,10},{4,12},{6,14},{8,0},{10,2},{12,4},{14,6},{16,24},{18,... | collective-permute-start | bytes 344072 | tf_op jit(solution)/shard_map/ppermute | solution.py:312
  80.9 5.8 %collective-permute-start.18 = (f32[112,256]{1,0:T(8,128)S(1)}, f32[112,256]{1,0:T(8,128)S(1)}, u32[]{:S(2)}, u32[]{:S(2)}) collective-permute-start(f32[112,256]{1,0:T(8,128)S(1)} %add.52), channel_id=1, source_target_pairs={{0,16},{2,18},{4,20},{6,22},{8,24},{10,26},{12,28},{14,30},{16,0},... | collective-permute-start | bytes 344072 | tf_op jit(solution)/shard_map/ppermute | solution.py:312
  86.7 3.7 %collective-permute-start.19 = (f32[112,256]{1,0:T(8,128)S(1)}, f32[112,256]{1,0:T(8,128)S(1)}, u32[]{:S(2)}, u32[]{:S(2)}) collective-permute-start(f32[112,256]{1,0:T(8,128)S(1)} %add.53), channel_id=1, source_target_pairs={{0,4},{2,6},{4,0},{6,2},{8,12},{10,14},{12,8},{14,10},{16,20},{18,... | collective-permute-start | bytes 344072 | tf_op jit(solution)/shard_map/ppermute | solution.py:312
  90.5 5.6 %collective-permute-start.20 = (f32[192,128]{1,0:T(8,128)S(1)}, f32[192,128]{1,0:T(8,128)S(1)}, u32[]{:S(2)}, u32[]{:S(2)}) collective-permute-start(f32[192,128]{1,0:T(8,128)S(1)} %pad_maximum_fusion.3), channel_id=1, source_target_pairs={{0,1},{1,0},{2,3},{3,2},{4,5},{5,4},{6,7},{7,6},{8,9},{9,8},{10,11... | collective-permute-start | bytes 294920 | tf_op jit(solution)/shard_map/ppermute | solution.py:312
  96.1 5.4 %collective-permute-start.21 = (f32[64,256]{1,0:T(8,128)S(1)}, f32[64,256]{1,0:T(8,128)S(1)}, u32[]{:S(2)}, u32[]{:S(2)}) collective-permute-start(f32[64,256]{1,0:T(8,128)S(1)} %slice_add_fusion.2), channel_id=1, source_target_pairs={{0,2},{2,0},{4,6},{6,4},{8,10},{10,8},{12,14},{14,12},{16,18},{18,... | collective-permute-start | bytes 196616 | tf_op jit(solution)/shard_map/ppermute | solution.py:312
  101.5 5.0 %collective-permute-start.22 = (f32[128,256]{1,0:T(8,128)S(1)}, f32[128,256]{1,0:T(8,128)S(1)}, u32[]{:S(2)}, u32[]{:S(2)}) collective-permute-start(f32[128,256]{1,0:T(8,128)S(1)} %pad_maximum_fusion.1), channel_id=1, source_target_pairs={{0,1},{1,0},{2,3},{3,2},{4,5},{5,4},{6,7},{7,6},{8,9},{9,8},{10,11... | collective-permute-start | bytes 393224 | tf_op jit(solution)/shard_map/ppermute | solution.py:312
  (3 other events, 2.3 us)
